TPU v7x, 32 devices: a whole 2x2x4 slice. The times are simulated.
32 devices in a mesh: groups: 2 (over y), labels: 4 (over z), dp: 4 (over x, core).
Axes of the slice: x: 2, y: 2, z: 4, core: 2. Of those that a mesh axis runs over, the one named last changes fastest.
Arguments:
- feats: bfloat16 [4096, 768], P(('groups', 'labels', 'dp')), parts along dimension 0, may hold values from -6 to 6
- enc_weight: bfloat16 [768, 768], P('dp'), may hold values from -0.21875 to 0.21875
- label_weight: bfloat16 [32768, 768], P(('groups', 'labels', 'dp')), parts along dimension 0, may hold values from -0.21875 to 0.21875
- owners: int32 [4096, 4], P(('groups', 'labels', 'dp')), parts along dimension 0, may hold values from 0 to 15, all different within a row; in each aligned block of 128 rows (0 to 127, 128 to 255, ...) at most 64 rows name the same one
- blocks: int32 [4096, 4], P(('groups', 'labels', 'dp')), parts along dimension 0, may hold values from 0 to 7
- positives: int32 [4096, 4], P(('groups', 'labels', 'dp')), parts along dimension 0, may hold values from 0 to 255
Outputs:
- grad_feats: bfloat16 [4096, 768], P(('groups', 'labels', 'dp')), parts along dimension 0
- grad_label: bfloat16 [32768, 768], P(('groups', 'labels', 'dp')), parts along dimension 0
- grad_enc: float32 [1536, 768], P(('groups', 'dp')), parts along dimension 0
There are 2 independent parts, one for each index of `groups`. A program takes and returns all parts, laid end to end along the dimension named above; an argument that names none is the same for every part. Nothing has to cross between parts.
Inputs may be any that keep to these rules, and one draw needn't show every extreme that they name: Each query names 4 different owners; among the 128 queries of one device no owner is named by more than 64 queries, a bound that some block reaches.
All inputs are finite; a program needn't handle non-finite values.
Results may differ from a plain program's by a relative error of at most 0.013.
Values may be sent and summed in bfloat16 or wider, within the bound.
No kernel may reach another device: no remote copies, remote signals or barrier semaphores. Data moves between devices by JAX's collectives and lax.ppermute only.
A program may use at most 64 MiB of HBM per device.

v0:
```python
import jax
import jax.numpy as jnp
from jax import lax
from jax.sharding import PartitionSpec as P

BLK = 128


EPSILON = 1e-06
TILE_ROWS = 128


def local(feats, enc_weight, label_weight, owners, blocks, positives):
    n_labels = lax.axis_size("labels")
    n_data = lax.axis_size("dp")
    n_owner = n_labels * n_data
    row_count, feature_width = feats.shape
    pick_count = owners.shape[1]
    labels_here = label_weight.shape[0]
    block_width = BLK
    local_blocks = labels_here // block_width
    capacity = max(2, 2 * row_count * pick_count // n_owner)
    slot_total = n_owner * capacity
    tile_count = slot_total // TILE_ROWS
    item_count = tile_count + local_blocks
    full_weight = lax.all_gather(enc_weight, "dp", axis=0, tiled=True)
    hidden = jnp.dot(feats, full_weight, preferred_element_type=jnp.float32)
    inv_rms = lax.rsqrt(jnp.mean(hidden * hidden, axis=-1, keepdims=True) + EPSILON)
    embedding = (hidden * inv_rms).astype(jnp.bfloat16)
    target_device = owners.reshape(-1)
    onehot = (target_device[:, None] == jnp.arange(n_owner, dtype=jnp.int32)[None, :]).astype(
        jnp.int32
    )
    position_rank = jnp.sum((jnp.cumsum(onehot, axis=0) - onehot) * onehot, axis=1)
    slot_index = target_device * capacity + position_rank
    query_of = jnp.arange(row_count * pick_count, dtype=jnp.int32) // pick_count
    outgoing = (
        jnp.zeros((slot_total, feature_width), jnp.bfloat16).at[slot_index].set(embedding[query_of])
    )
    block_tag = jnp.zeros((slot_total,), jnp.int32).at[slot_index].set(blocks.reshape(-1) + 1)
    wanted = jnp.zeros((slot_total,), jnp.int32).at[slot_index].set(positives.reshape(-1))
    outgoing = outgoing.reshape(n_labels, n_data, capacity, feature_width)
    block_tag = block_tag.reshape(n_labels, n_data, capacity)
    wanted = wanted.reshape(n_labels, n_data, capacity)
    incoming, tag_in, wanted_in = (
        lax.all_to_all(
            lax.all_to_all(outgoing, "labels", split_axis=0, concat_axis=0, tiled=True),
            "dp",
            split_axis=1,
            concat_axis=1,
            tiled=True,
        ),
        lax.all_to_all(
            lax.all_to_all(block_tag, "labels", split_axis=0, concat_axis=0, tiled=True),
            "dp",
            split_axis=1,
            concat_axis=1,
            tiled=True,
        ),
        lax.all_to_all(
            lax.all_to_all(wanted, "labels", split_axis=0, concat_axis=0, tiled=True),
            "dp",
            split_axis=1,
            concat_axis=1,
            tiled=True,
        ),
    )
    flat_in = incoming.reshape(slot_total, feature_width)
    tag_in = tag_in.reshape(slot_total)
    wanted_in = wanted_in.reshape(slot_total)
    sort_key = jnp.where(tag_in == 0, local_blocks + 1, tag_in).astype(jnp.int32)
    order = jnp.argsort(sort_key, stable=True)
    sorted_key = sort_key[order]
    sorted_rows = flat_in[order]
    sorted_wanted = wanted_in[order]
    tile_keys = sorted_key.reshape(tile_count, TILE_ROWS)
    first_tag = tile_keys[:, 0]
    last_tag = jnp.minimum(tile_keys[:, -1], local_blocks)
    tile_span = jnp.maximum(last_tag - first_tag + 1, 0)
    tile_start = jnp.cumsum(tile_span) - tile_span
    tile_end = tile_start + tile_span
    work_total = jnp.sum(tile_span)
    column = jnp.arange(block_width, dtype=jnp.int32)

    def one_item(carry, item):
        tile = jnp.minimum(jnp.sum((tile_end <= item).astype(jnp.int32)), tile_count - 1)
        tag_now = jnp.clip(first_tag[tile] + item - tile_start[tile], 1, local_blocks)
        valid = item < work_total
        row_start = tile * TILE_ROWS
        rows = lax.dynamic_slice_in_dim(sorted_rows, row_start, TILE_ROWS, 0)
        keys = lax.dynamic_slice_in_dim(sorted_key, row_start, TILE_ROWS, 0)
        wants = lax.dynamic_slice_in_dim(sorted_wanted, row_start, TILE_ROWS, 0)
        weight_rows = lax.dynamic_slice_in_dim(
            label_weight, (tag_now - 1) * block_width, block_width, 0
        )
        scores = lax.dot_general(
            rows, weight_rows, (((1,), (1,)), ((), ())), preferred_element_type=jnp.float32
        )
        live = jnp.logical_and(keys == tag_now, valid)
        target = (column[None, :] == wants[:, None]).astype(jnp.float32)
        grad_scores = jnp.where(live[:, None], jax.nn.sigmoid(scores) - target, 0.0).astype(
            jnp.bfloat16
        )
        item_part = jnp.dot(grad_scores, weight_rows, preferred_element_type=jnp.float32)
        label_part = lax.dot_general(
            grad_scores, rows, (((0,), (0,)), ((), ())), preferred_element_type=jnp.float32
        )
        block_slot = jnp.where(valid, tag_now - 1, local_blocks)
        return (carry, (item_part, label_part, tile, block_slot))

    unused, outputs = lax.scan(
        one_item, jnp.zeros((), jnp.int32), jnp.arange(item_count, dtype=jnp.int32)
    )
    item_parts, label_parts, item_tile, item_block = outputs
    tile_select = (item_tile[:, None] == jnp.arange(tile_count, dtype=jnp.int32)[None, :]).astype(
        jnp.float32
    )
    block_select = (
        item_block[:, None] == jnp.arange(local_blocks, dtype=jnp.int32)[None, :]
    ).astype(jnp.float32)
    sorted_grad = jnp.einsum(
        "it,ird->trd", tile_select, item_parts, precision=lax.Precision.HIGHEST
    ).reshape(slot_total, feature_width)
    label_total = jnp.einsum(
        "ib,ird->brd", block_select, label_parts, precision=lax.Precision.HIGHEST
    ).reshape(labels_here, feature_width)
    grad_label = label_total.astype(jnp.bfloat16)
    inverse = jnp.argsort(order)
    item_grad = sorted_grad[inverse].astype(jnp.bfloat16)
    item_back = item_grad.reshape(n_labels, n_data, capacity, feature_width)
    returned = lax.all_to_all(
        lax.all_to_all(item_back, "labels", split_axis=0, concat_axis=0, tiled=True),
        "dp",
        split_axis=1,
        concat_axis=1,
        tiled=True,
    )
    returned = returned.reshape(slot_total, feature_width)
    grad_embedding = jnp.sum(
        returned[slot_index].astype(jnp.float32).reshape(row_count, pick_count, feature_width),
        axis=1,
    )
    projection = jnp.mean(hidden * grad_embedding, axis=-1, keepdims=True)
    grad_hidden = (inv_rms * grad_embedding - hidden * inv_rms**3 * projection).astype(jnp.bfloat16)
    grad_feats = lax.dot_general(
        grad_hidden, full_weight, (((1,), (1,)), ((), ())), preferred_element_type=jnp.float32
    ).astype(jnp.bfloat16)
    share = lax.psum_scatter(
        lax.dot_general(
            feats, grad_hidden, (((0,), (0,)), ((), ())), preferred_element_type=jnp.float32
        ).astype(jnp.bfloat16),
        "dp",
        scatter_dimension=0,
        tiled=True,
    ).astype(jnp.float32)
    grad_enc = lax.psum(share, "labels")
    return (grad_feats, grad_label, grad_enc)


def solution(mesh):
    return jax.shard_map(
        local,
        mesh=mesh,
        in_specs=(
            P(("groups", "labels", "dp"), None),
            P("dp", None),
            P(("groups", "labels", "dp"), None),
            P(("groups", "labels", "dp"), None),
            P(("groups", "labels", "dp"), None),
            P(("groups", "labels", "dp"), None),
        ),
        out_specs=(
            P(("groups", "labels", "dp"), None),
            P(("groups", "labels", "dp"), None),
            P(("groups", "dp"), None),
        ),
        check_vma=False,
    )
```

profile of v0, /device:TPU:0, one launch (start us, length us, event | category | flops | bytes accessed | tf_op | source)
XLA Modules:
  0.0 739.9 jit_solution(4378099923108659013)
XLA Ops:
  51.7 36.4 %all-to-all-done.2 = bf16[4,4,64,768]{3,2,1,0:T(8,128)(2,1)S(1)} async-done(((bf16[4,4,64,768]{3,2,1,0:T(8,128)(2,1)}), bf16[4,4,64,768]{3,2,1,0:T(8,128)(2,1)S(1)}, u32[]{:S(2)}, u32[]{:S(2)}) %all-to-all-start.2) | async-done | bytes 1572896 | tf_op jit(solution)/shard_map/all_to_all | solution.py:47
  124.7 466.3 %while.19 = (s32[]{:T(128)}, f32[16,128,768]{2,0,1:T(8,128)}, f32[16,128,768]{2,0,1:T(8,128)}, s32[16]{0:T(128)S(1)}, s32[16]{0:T(128)S(1)}, /*index=5*/s32[16]{...) while((s32[]{:T(128)}, f32[16,128,768]{2,0,1:T(8,128)}, ...), condition=%wide.region_12.13_spmd.clone, body=%wide.region_10.12_spmd.clone.sunk | while | flops 75628840 | bytes 4819746 | solution.py:111
  134.8 8.7 %dynamic_update_slice.35 = f32[16,128,768]{2,0,1:T(8,128)} dynamic-update-slice(f32[16,128,768]{2,0,1:T(8,128)} %get-tuple-element.392, f32[1,128,768]{2,0,1:T(1,128)S(1)} %copy.104, s32[]{:T(128)} %get-tuple-element.390, s32[]{:T(128)} %constant.94.clone.1..sunk, s32[]{:T(128)} %constant.94.clone.1..sunk) | dynamic-update-slice | bytes 786436 | tf_op jit(solution)/shard_map/while/body/jit(dynamic_update_index_in_dim)/dynamic_update_slice | solution.py:111
  163.9 8.7 %dynamic_update_slice.35 = f32[16,128,768]{2,0,1:T(8,128)} dynamic-update-slice(f32[16,128,768]{2,0,1:T(8,128)} %get-tuple-element.392, f32[1,128,768]{2,0,1:T(1,128)S(1)} %copy.104, s32[]{:T(128)} %get-tuple-element.390, s32[]{:T(128)} %constant.94.clone.1..sunk, s32[]{:T(128)} %constant.94.clone.1..sunk) | dynamic-update-slice | bytes 786436 | tf_op jit(solution)/shard_map/while/body/jit(dynamic_update_index_in_dim)/dynamic_update_slice | solution.py:111
  174.1 8.7 %dynamic_update_slice.34 = f32[16,128,768]{2,0,1:T(8,128)} dynamic-update-slice(f32[16,128,768]{2,0,1:T(8,128)} %get-tuple-element.391, f32[1,128,768]{2,0,1:T(1,128)S(1)} %copy.103, s32[]{:T(128)} %get-tuple-element.390, s32[]{:T(128)} %constant.94.clone.1..sunk, s32[]{:T(128)} %constant.94.clone.1..sunk) | dynamic-update-slice | bytes 786436 | tf_op jit(solution)/shard_map/while/body/jit(dynamic_update_index_in_dim)/dynamic_update_slice | solution.py:111
  193.1 8.7 %dynamic_update_slice.35 = f32[16,128,768]{2,0,1:T(8,128)} dynamic-update-slice(f32[16,128,768]{2,0,1:T(8,128)} %get-tuple-element.392, f32[1,128,768]{2,0,1:T(1,128)S(1)} %copy.104, s32[]{:T(128)} %get-tuple-element.390, s32[]{:T(128)} %constant.94.clone.1..sunk, s32[]{:T(128)} %constant.94.clone.1..sunk) | dynamic-update-slice | bytes 786436 | tf_op jit(solution)/shard_map/while/body/jit(dynamic_update_index_in_dim)/dynamic_update_slice | solution.py:111
  203.3 8.7 %dynamic_update_slice.34 = f32[16,128,768]{2,0,1:T(8,128)} dynamic-update-slice(f32[16,128,768]{2,0,1:T(8,128)} %get-tuple-element.391, f32[1,128,768]{2,0,1:T(1,128)S(1)} %copy.103, s32[]{:T(128)} %get-tuple-element.390, s32[]{:T(128)} %constant.94.clone.1..sunk, s32[]{:T(128)} %constant.94.clone.1..sunk) | dynamic-update-slice | bytes 786436 | tf_op jit(solution)/shard_map/while/body/jit(dynamic_update_index_in_dim)/dynamic_update_slice | solution.py:111
  222.2 8.7 %dynamic_update_slice.35 = f32[16,128,768]{2,0,1:T(8,128)} dynamic-update-slice(f32[16,128,768]{2,0,1:T(8,128)} %get-tuple-element.392, f32[1,128,768]{2,0,1:T(1,128)S(1)} %copy.104, s32[]{:T(128)} %get-tuple-element.390, s32[]{:T(128)} %constant.94.clone.1..sunk, s32[]{:T(128)} %constant.94.clone.1..sunk) | dynamic-update-slice | bytes 786436 | tf_op jit(solution)/shard_map/while/body/jit(dynamic_update_index_in_dim)/dynamic_update_slice | solution.py:111
  251.4 8.7 %dynamic_update_slice.35 = f32[16,128,768]{2,0,1:T(8,128)} dynamic-update-slice(f32[16,128,768]{2,0,1:T(8,128)} %get-tuple-element.392, f32[1,128,768]{2,0,1:T(1,128)S(1)} %copy.104, s32[]{:T(128)} %get-tuple-element.390, s32[]{:T(128)} %constant.94.clone.1..sunk, s32[]{:T(128)} %constant.94.clone.1..sunk) | dynamic-update-slice | bytes 786436 | tf_op jit(solution)/shard_map/while/body/jit(dynamic_update_index_in_dim)/dynamic_update_slice | solution.py:111
  280.5 8.7 %dynamic_update_slice.35 = f32[16,128,768]{2,0,1:T(8,128)} dynamic-update-slice(f32[16,128,768]{2,0,1:T(8,128)} %get-tuple-element.392, f32[1,128,768]{2,0,1:T(1,128)S(1)} %copy.104, s32[]{:T(128)} %get-tuple-element.390, s32[]{:T(128)} %constant.94.clone.1..sunk, s32[]{:T(128)} %constant.94.clone.1..sunk) | dynamic-update-slice | bytes 786436 | tf_op jit(solution)/shard_map/while/body/jit(dynamic_update_index_in_dim)/dynamic_update_slice | solution.py:111
  309.6 8.7 %dynamic_update_slice.35 = f32[16,128,768]{2,0,1:T(8,128)} dynamic-update-slice(f32[16,128,768]{2,0,1:T(8,128)} %get-tuple-element.392, f32[1,128,768]{2,0,1:T(1,128)S(1)} %copy.104, s32[]{:T(128)} %get-tuple-element.390, s32[]{:T(128)} %constant.94.clone.1..sunk, s32[]{:T(128)} %constant.94.clone.1..sunk) | dynamic-update-slice | bytes 786436 | tf_op jit(solution)/shard_map/while/body/jit(dynamic_update_index_in_dim)/dynamic_update_slice | solution.py:111
  338.8 8.7 %dynamic_update_slice.35 = f32[16,128,768]{2,0,1:T(8,128)} dynamic-update-slice(f32[16,128,768]{2,0,1:T(8,128)} %get-tuple-element.392, f32[1,128,768]{2,0,1:T(1,128)S(1)} %copy.104, s32[]{:T(128)} %get-tuple-element.390, s32[]{:T(128)} %constant.94.clone.1..sunk, s32[]{:T(128)} %constant.94.clone.1..sunk) | dynamic-update-slice | bytes 786436 | tf_op jit(solution)/shard_map/while/body/jit(dynamic_update_index_in_dim)/dynamic_update_slice | solution.py:111
  367.9 8.7 %dynamic_update_slice.35 = f32[16,128,768]{2,0,1:T(8,128)} dynamic-update-slice(f32[16,128,768]{2,0,1:T(8,128)} %get-tuple-element.392, f32[1,128,768]{2,0,1:T(1,128)S(1)} %copy.104, s32[]{:T(128)} %get-tuple-element.390, s32[]{:T(128)} %constant.94.clone.1..sunk, s32[]{:T(128)} %constant.94.clone.1..sunk) | dynamic-update-slice | bytes 786436 | tf_op jit(solution)/shard_map/while/body/jit(dynamic_update_index_in_dim)/dynamic_update_slice | solution.py:111
  397.1 8.7 %dynamic_update_slice.35 = f32[16,128,768]{2,0,1:T(8,128)} dynamic-update-slice(f32[16,128,768]{2,0,1:T(8,128)} %get-tuple-element.392, f32[1,128,768]{2,0,1:T(1,128)S(1)} %copy.104, s32[]{:T(128)} %get-tuple-element.390, s32[]{:T(128)} %constant.94.clone.1..sunk, s32[]{:T(128)} %constant.94.clone.1..sunk) | dynamic-update-slice | bytes 786436 | tf_op jit(solution)/shard_map/while/body/jit(dynamic_update_index_in_dim)/dynamic_update_slice | solution.py:111
  426.2 8.7 %dynamic_update_slice.35 = f32[16,128,768]{2,0,1:T(8,128)} dynamic-update-slice(f32[16,128,768]{2,0,1:T(8,128)} %get-tuple-element.392, f32[1,128,768]{2,0,1:T(1,128)S(1)} %copy.104, s32[]{:T(128)} %get-tuple-element.390, s32[]{:T(128)} %constant.94.clone.1..sunk, s32[]{:T(128)} %constant.94.clone.1..sunk) | dynamic-update-slice | bytes 786436 | tf_op jit(solution)/shard_map/while/body/jit(dynamic_update_index_in_dim)/dynamic_update_slice | solution.py:111
  455.3 8.7 %dynamic_update_slice.35 = f32[16,128,768]{2,0,1:T(8,128)} dynamic-update-slice(f32[16,128,768]{2,0,1:T(8,128)} %get-tuple-element.392, f32[1,128,768]{2,0,1:T(1,128)S(1)} %copy.104, s32[]{:T(128)} %get-tuple-element.390, s32[]{:T(128)} %constant.94.clone.1..sunk, s32[]{:T(128)} %constant.94.clone.1..sunk) | dynamic-update-slice | bytes 786436 | tf_op jit(solution)/shard_map/while/body/jit(dynamic_update_index_in_dim)/dynamic_update_slice | solution.py:111
  484.5 8.7 %dynamic_update_slice.35 = f32[16,128,768]{2,0,1:T(8,128)} dynamic-update-slice(f32[16,128,768]{2,0,1:T(8,128)} %get-tuple-element.392, f32[1,128,768]{2,0,1:T(1,128)S(1)} %copy.104, s32[]{:T(128)} %get-tuple-element.390, s32[]{:T(128)} %constant.94.clone.1..sunk, s32[]{:T(128)} %constant.94.clone.1..sunk) | dynamic-update-slice | bytes 786436 | tf_op jit(solution)/shard_map/while/body/jit(dynamic_update_index_in_dim)/dynamic_update_slice | solution.py:111
  513.6 8.7 %dynamic_update_slice.35 = f32[16,128,768]{2,0,1:T(8,128)} dynamic-update-slice(f32[16,128,768]{2,0,1:T(8,128)} %get-tuple-element.392, f32[1,128,768]{2,0,1:T(1,128)S(1)} %copy.104, s32[]{:T(128)} %get-tuple-element.390, s32[]{:T(128)} %constant.94.clone.1..sunk, s32[]{:T(128)} %constant.94.clone.1..sunk) | dynamic-update-slice | bytes 786436 | tf_op jit(solution)/shard_map/while/body/jit(dynamic_update_index_in_dim)/dynamic_update_slice | solution.py:111
  542.8 8.7 %dynamic_update_slice.35 = f32[16,128,768]{2,0,1:T(8,128)} dynamic-update-slice(f32[16,128,768]{2,0,1:T(8,128)} %get-tuple-element.392, f32[1,128,768]{2,0,1:T(1,128)S(1)} %copy.104, s32[]{:T(128)} %get-tuple-element.390, s32[]{:T(128)} %constant.94.clone.1..sunk, s32[]{:T(128)} %constant.94.clone.1..sunk) | dynamic-update-slice | bytes 786436 | tf_op jit(solution)/shard_map/while/body/jit(dynamic_update_index_in_dim)/dynamic_update_slice | solution.py:111
  571.9 8.7 %dynamic_update_slice.35 = f32[16,128,768]{2,0,1:T(8,128)} dynamic-update-slice(f32[16,128,768]{2,0,1:T(8,128)} %get-tuple-element.392, f32[1,128,768]{2,0,1:T(1,128)S(1)} %copy.104, s32[]{:T(128)} %get-tuple-element.390, s32[]{:T(128)} %constant.94.clone.1..sunk, s32[]{:T(128)} %constant.94.clone.1..sunk) | dynamic-update-slice | bytes 786436 | tf_op jit(solution)/shard_map/while/body/jit(dynamic_update_index_in_dim)/dynamic_update_slice | solution.py:111
  600.5 40.1 %all_to_all.40 = bf16[4,4,64,768]{3,2,1,0:T(8,128)(2,1)S(1)} all-to-all(bf16[4,4,64,768]{3,2,1,0:T(8,128)(2,1)S(1)} %bitcast.86), channel_id=1, replica_groups=mesh['groups'=2,'labels'=4,'dp'=4] {'labels'}, dimensions={0} | all-to-all | bytes 3145728 | tf_op jit(solution)/shard_map/all_to_all | solution.py:132
  645.7 19.8 %all-to-all-done.7 = bf16[4,4,64,768]{3,2,0,1:T(8,128)(2,1)S(1)} async-done(((bf16[4,4,64,768]{3,2,0,1:T(8,128)(2,1)}), bf16[4,4,64,768]{3,2,0,1:T(8,128)(2,1)S(1)}, u32[]{:S(2)}, u32[]{:S(2)}) %all-to-all-start.7) | async-done | bytes 1572896 | tf_op jit(solution)/shard_map/all_to_all | solution.py:131
  679.4 15.9 %reduce-scatter.4.cloned.1.call-done = bf16[192,768]{1,0:T(8,128)(2,1)} async-done(((bf16[768,768]{1,0:T(8,128)(2,1)}), bf16[192,768]{1,0:T(8,128)(2,1)}) %reduce-scatter.4.cloned.1.call-update) | async-done | bytes 294928
  696.4 35.5 %all-reduce.1 = f32[192,768]{0,1:T(8,128)S(1)} all-reduce(bf16[192,768]{0,1:T(8,128)(2,1)S(1)} %copy.87), channel_id=1, replica_groups=mesh['groups'=2,'labels'=4,'dp'=4] {'labels'}, use_global_device_ids=true, to_apply=%region_17.18 | all-reduce | flops 147456 | bytes 884736 | tf_op jit(solution)/shard_map/psum | solution.py:156
  (334 shorter events, 358.8 us)
Async XLA Ops:
  7.2 25.8 %copy-start = (bf16[128,768]{1,0:T(8,128)(2,1)S(1)}, bf16[128,768]{1,0:T(8,128)(2,1)}, u32[]{:S(2)}) copy-start(bf16[128,768]{1,0:T(8,128)(2,1)} %param.8) | copy-start | bytes 589828
  7.2 25.8 %all-gather.2.cloned.1.call-start = ((), (), s32[]{:S(2)}) async-start(), calls=%async_computation.9 | async-start | bytes 1474560 | tf_op jit(solution)/shard_map/all_gather | solution.py:26
  15.5 11.9 %all-to-all-start = ((s32[4,1,256]{2,1,0:T(1,128)}), s32[4,1,256]{2,1,0:T(1,128)S(1)}, u32[]{:S(2)}, u32[]{:S(2)}) async-start(s32[4,1,256]{2,1,0:T(1,128)} %reshape.289), calls=%async_computation | async-start | bytes 8192 | tf_op jit(solution)/shard_map/all_to_all | solution.py:54
  27.4 9.2 %all-to-all-start.4 = ((s32[4,1,256]{2,1,0:T(1,128)}), s32[4,1,256]{2,1,0:T(1,128)S(1)}, u32[]{:S(2)}, u32[]{:S(2)}) async-start(s32[4,1,256]{2,1,0:T(1,128)} %reshape.293), calls=%async_computation.4 | async-start | bytes 8192 | tf_op jit(solution)/shard_map/all_to_all | solution.py:61
  34.7 12.0 %copy-start.1 = (f32[128,768]{1,0:T(8,128)}, f32[128,768]{1,0:T(8,128)S(1)}, u32[]{:S(2)}) copy-start(f32[128,768]{1,0:T(8,128)S(1)} %get-tuple-element.283) | copy-start | bytes 1179652
  36.6 10.1 %all-to-all-start.1 = ((s32[4,1,256]{2,1,0:T(1,128)}), s32[4,1,256]{2,1,0:T(1,128)S(1)}, u32[]{:S(2)}, u32[]{:S(2)}) async-start(s32[4,1,256]{2,1,0:T(1,128)} %reshape.291), calls=%async_computation.1 | async-start | bytes 8192 | tf_op jit(solution)/shard_map/all_to_all | solution.py:53
  46.7 41.4 %all-to-all-start.2 = ((bf16[4,4,64,768]{3,2,1,0:T(8,128)(2,1)}), bf16[4,4,64,768]{3,2,1,0:T(8,128)(2,1)S(1)}, u32[]{:S(2)}, u32[]{:S(2)}) async-start(bf16[4,4,64,768]{3,2,1,0:T(8,128)(2,1)} %bitcast.5), calls=%async_computation.2 | async-start | bytes 3145728 | tf_op jit(solution)/shard_map/all_to_all | solution.py:47
  88.1 7.0 all-to-all-start.5
  95.1 24.2 %all-to-all-start.3 = ((bf16[4,4,64,768]{3,2,0,1:T(8,128)(2,1)}), bf16[4,4,64,768]{3,2,0,1:T(8,128)(2,1)S(1)}, u32[]{:S(2)}, u32[]{:S(2)}) async-start(bf16[4,4,64,768]{3,2,0,1:T(8,128)(2,1)} %copy.74), calls=%async_computation.3 | async-start | bytes 3145728 | tf_op jit(solution)/shard_map/all_to_all | solution.py:46
  641.9 23.6 %all-to-all-start.7 = ((bf16[4,4,64,768]{3,2,0,1:T(8,128)(2,1)}), bf16[4,4,64,768]{3,2,0,1:T(8,128)(2,1)S(1)}, u32[]{:S(2)}, u32[]{:S(2)}) async-start(bf16[4,4,64,768]{3,2,0,1:T(8,128)(2,1)} %copy.81), calls=%async_computation.7 | async-start | bytes 3145728 | tf_op jit(solution)/shard_map/all_to_all | solution.py:131
  645.4 49.9 %reduce-scatter.4.cloned.1.call-start = ((), (), s32[]{:S(2)}) async-start(), calls=%async_computation.10 | async-start | bytes 1474560
  668.0 1.0 copy-start.2
  676.5 1.7 copy-start.3
Sparse Core Ops, SparseCore 0:
  9.6 20.1 all-gather.1
  671.4 23.8 reduce-scatter.3
where the time goes:
time: 749 us; the launch traced here: 740 us
  local copies, waits for them, and re-layouts  372 us (50%)
  waiting for transfers between devices  78.6 us (10%)
  blocking collectives  75.6 us (10%)
  matrix products  70 us (9%)
  loops' own time  62.5 us (8%)
  other arithmetic  39.1 us (5%)
  starting transfers between devices  27.6 us (4%)
  between operations  14.4 us (2%)
    dynamic_update_slice x96, local copies, waits for them, and re-layouts, local(): lax.scan(one_item, jnp.zeros((), jnp.int32), jnp.arange(item_count, dtype...  294 us
    another operation x1, loops' own time, local(): lax.scan(one_item, jnp.zeros((), jnp.int32), jnp.arange(item_count, dtype...  62.5 us
    all_to_all x1, blocking collectives, local(): lax.all_to_all(item_back, 'labels', split_axis=0, concat_axis=0, tiled=True)  40.1 us
    all_to_all x1, waiting for transfers between devices, local(): lax.all_to_all(outgoing, 'labels', split_axis=0, concat_axis=0, tiled=True)  36.4 us
    psum x1, blocking collectives, local(): grad_enc = lax.psum(share, 'labels')  35.5 us
    reduce_sum x16, other arithmetic, one_item(): jnp.sum((tile_end <= item).astype(jnp.int32))  21.5 us
    dot_general x16, matrix products, one_item(): lax.dot_general(rows, weight_rows, (((1,), (1,)), ((), ())), preferred_el...  19.9 us
    all_to_all x1, waiting for transfers between devices, local(): lax.all_to_all(lax.all_to_all(item_back, 'labels', split_axis=0, concat_a...  19.8 us
  transfers between devices with their start and end apart: 9, of which 6 were waited for; matrix products, arithmetic and copies ran while one was open for 7% of the time, Pallas kernels for 0%

commit v1 on v0

v1 whole, which is shorter than its diff:
```python
import functools

import jax
import jax.numpy as jnp
from jax import lax
from jax.experimental import pallas as pl
from jax.experimental.pallas import tpu as pltpu
from jax.sharding import PartitionSpec as P

BLK = 128
EPSILON = 1e-06
STEP_ROWS = 512
F32 = jnp.float32
BF16 = jnp.bfloat16


def dot(a, b, da=1, db=0):
    return lax.dot_general(a, b, (((da,), (db,)), ((), ())), preferred_element_type=F32)


def label_kernel(
    me_ref,
    meta_ref,
    feats_ref,
    enc_ref,
    label_ref,
    back_ref,
    grad_label_ref,
    grad_enc_ref,
    label_acc,
    enc_acc,
    *,
    cap,
):
    step = pl.program_id(0)
    me = me_ref[0]
    sources, rows, width = feats_ref.shape
    n_blocks = label_ref.shape[0] // BLK

    hits, codes = [], []
    for s in range(sources):
        named = meta_ref[s, 0] == me
        hits.append(jnp.sum(named.astype(F32), axis=0, keepdims=True))
        code = (meta_ref[s, 1] * 256 + meta_ref[s, 2] + 1).astype(F32)
        codes.append(jnp.sum(jnp.where(named, code, 0.0), axis=0, keepdims=True))
    hit = jnp.concatenate(hits, axis=0)
    row_id = lax.broadcasted_iota(jnp.int32, (rows, rows), 0)
    col_id = lax.broadcasted_iota(jnp.int32, (rows, rows), 1)
    rank = dot(hit.astype(BF16), (row_id < col_id).astype(BF16))
    slot_id = lax.broadcasted_iota(jnp.int32, (cap, rows), 0).astype(F32)

    picks, picked, slot_codes = [], [], []
    for s in range(sources):
        pick = jnp.where((slot_id == rank[s : s + 1]) & (hits[s] > 0.0), 1.0, 0.0)
        slot_codes.append(jnp.sum(pick * codes[s], axis=1, keepdims=True))
        pick = pick.astype(BF16)
        picks.append(pick)
        picked.append(dot(pick, feats_ref[s]).astype(BF16))
    feats = jnp.concatenate(picked, axis=0)
    code = jnp.concatenate(slot_codes, axis=0).astype(jnp.int32) - 1
    slots = feats.shape[0]

    hidden = dot(feats, enc_ref[...])
    inv_rms = lax.rsqrt(jnp.mean(hidden * hidden, axis=-1, keepdims=True) + EPSILON)
    embedding = (hidden * inv_rms).astype(BF16)

    scores = dot(embedding, label_ref[...], 1, 1)
    block = jnp.broadcast_to(code >> 8, (slots, BLK))
    wanted = jnp.broadcast_to(code & 255, (slots, BLK))
    live = block >= 0
    own_scores = jnp.zeros((slots, BLK), F32)
    for b in range(n_blocks):
        own_scores = jnp.where(block == b, scores[:, b * BLK : (b + 1) * BLK], own_scores)
    column = lax.broadcasted_iota(jnp.int32, (slots, BLK), 1)
    target = jnp.where(column == wanted, 1.0, 0.0)
    grad_scores = jnp.where(live, jax.nn.sigmoid(own_scores) - target, 0.0)

    spread = jnp.concatenate(
        [jnp.where(block == b, grad_scores, 0.0).astype(BF16) for b in range(n_blocks)], axis=1
    )
    grad_pair = dot(spread, label_ref[...]).astype(BF16).astype(F32)

    grad_scores_t = grad_scores.T
    block_t = block.T
    spread_t = jnp.concatenate(
        [jnp.where(block_t == b, grad_scores_t, 0.0).astype(BF16) for b in range(n_blocks)], axis=0
    )
    label_part = dot(spread_t, embedding)

    projection = jnp.mean(hidden * grad_pair, axis=-1, keepdims=True)
    grad_hidden = (inv_rms * grad_pair - hidden * (inv_rms**3 * projection)).astype(BF16)
    enc_part = dot(feats, grad_hidden, 0, 0)
    grad_feats = dot(grad_hidden, enc_ref[...], 1, 1).astype(BF16)
    for s in range(sources):
        back_ref[s] = dot(picks[s], grad_feats[s * cap : (s + 1) * cap], 0, 0).astype(BF16)

    @pl.when(step == 0)
    def _():
        label_acc[...] = label_part
        enc_acc[...] = enc_part

    @pl.when(step > 0)
    def _():
        label_acc[...] += label_part
        enc_acc[...] += enc_part

    @pl.when(step == pl.num_programs(0) - 1)
    def _():
        grad_label_ref[...] = label_acc[...].astype(BF16)
        grad_enc_ref[...] = enc_acc[...].astype(BF16)


def label_work(me, meta, feats, enc_weight, label_weight, cap):
    sources, rows, width = feats.shape
    group = max(1, min(sources, STEP_ROWS // cap))
    while sources % group:
        group -= 1
    labels_here = label_weight.shape[0]
    whole = lambda shape: pl.BlockSpec(shape, lambda i: (0,) * len(shape))
    flops = 2 * sources * cap * width * (3 * labels_here + 3 * width + 2 * rows)
    return pl.pallas_call(
        functools.partial(label_kernel, cap=cap),
        grid=(sources // group,),
        in_specs=[
            pl.BlockSpec(memory_space=pltpu.SMEM),
            pl.BlockSpec((group,) + meta.shape[1:], lambda i: (i, 0, 0, 0)),
            pl.BlockSpec((group, rows, width), lambda i: (i, 0, 0)),
            whole(enc_weight.shape),
            whole(label_weight.shape),
        ],
        out_specs=[
            pl.BlockSpec((group, rows, width), lambda i: (i, 0, 0)),
            whole(label_weight.shape),
            whole(enc_weight.shape),
        ],
        out_shape=[
            jax.ShapeDtypeStruct(feats.shape, BF16),
            jax.ShapeDtypeStruct(label_weight.shape, BF16),
            jax.ShapeDtypeStruct(enc_weight.shape, BF16),
        ],
        scratch_shapes=[
            pltpu.VMEM(label_weight.shape, F32),
            pltpu.VMEM(enc_weight.shape, F32),
        ],
        compiler_params=pltpu.CompilerParams(vmem_limit_bytes=56 << 20),
        cost_estimate=pl.CostEstimate(flops=flops, bytes_accessed=12 << 20, transcendentals=0),
        name="label_work",
    )(me, meta, feats, enc_weight, label_weight)


def swap(x):
    x = lax.all_to_all(x, "labels", split_axis=0, concat_axis=0, tiled=True)
    return lax.all_to_all(x, "dp", split_axis=1, concat_axis=1, tiled=True)


def local(feats, enc_weight, label_weight, owners, blocks, positives):
    n_labels = lax.axis_size("labels")
    n_data = lax.axis_size("dp")
    n_owner = n_labels * n_data
    row_count, width = feats.shape
    pick_count = owners.shape[1]
    cap = max(2, 2 * row_count * pick_count // n_owner)
    me = (lax.axis_index("labels") * n_data + lax.axis_index("dp")).astype(jnp.int32)
    full_weight = lax.all_gather(enc_weight, "dp", axis=0, tiled=True)

    if row_count <= n_data * cap:
        meta = jnp.stack([owners.T, blocks.T, positives.T])
        all_feats = lax.all_gather(feats, ("labels", "dp"))
        all_meta = lax.all_gather(meta, ("labels", "dp"))
        back, grad_label, enc_part = label_work(
            me.reshape(1), all_meta, all_feats, full_weight, label_weight, cap
        )
        grad_feats = lax.psum_scatter(back, ("labels", "dp"), scatter_dimension=0)
    else:
        flat = owners.reshape(-1)
        onehot = (flat[:, None] == jnp.arange(n_owner, dtype=jnp.int32)[None, :]).astype(jnp.int32)
        rank = jnp.sum((jnp.cumsum(onehot, axis=0) - onehot) * onehot, axis=1)
        slot = (flat * cap + rank).reshape(row_count, pick_count)
        slot_total = n_owner * cap
        slots = jnp.arange(slot_total, dtype=jnp.int32)
        place = slots[:, None, None] == slot[None]
        pick = jnp.any(place, axis=2).astype(BF16)
        live = jnp.any(place, axis=(1, 2))
        block_of = jnp.sum(jnp.where(place, blocks[None], 0), axis=(1, 2))
        wanted = jnp.sum(jnp.where(place, positives[None], 0), axis=(1, 2))
        owner_of = jnp.where(live, slots // cap, -1)
        out = dot(pick, feats).astype(BF16).reshape(n_labels, n_data, cap, width)
        meta = jnp.stack([owner_of, block_of, wanted], axis=1).reshape(n_labels, n_data, cap, 3)
        tile = 128
        got = swap(out).reshape(slot_total // tile, tile, width)
        got_meta = swap(meta).reshape(slot_total // tile, tile, 3)
        got_meta = got_meta.transpose(0, 2, 1)[:, :, None, :]
        back, grad_label, enc_part = label_work(
            me.reshape(1), got_meta, got, full_weight, label_weight, tile
        )
        back = swap(back.reshape(n_labels, n_data, cap, width)).reshape(slot_total, width)
        grad_feats = dot(pick, back, 0, 0).astype(BF16)

    share = lax.psum_scatter(enc_part, "dp", scatter_dimension=0, tiled=True)
    grad_enc = lax.psum(share.astype(F32), "labels")
    return (grad_feats, grad_label, grad_enc)


def solution(mesh):
    rows = P(("groups", "labels", "dp"), None)
    return jax.shard_map(
        local,
        mesh=mesh,
        in_specs=(rows, P("dp", None), rows, rows, rows, rows),
        out_specs=(rows, rows, P(("groups", "dp"), None)),
        check_vma=False,
    )
```

time: 749 us -> 198 us (0.26); the launches traced: 740 us -> 197 us
  local copies, waits for them, and re-layouts: 372 us -> 0 us
  matrix products: 70 us -> 0 us
  loops' own time: 62.5 us -> 0 us
  other arithmetic: 39.1 us -> 0.72 us
  waiting for transfers between devices: 78.6 us -> 108 us
  starting transfers between devices: 27.6 us -> 0.16 us
  blocking collectives: 75.6 us -> 57.1 us
  Pallas kernels: 0 us -> 17.5 us
    dynamic_update_slice x96 -> x0, local copies, waits for them, and re-layouts: 294 us -> none  [local(): lax.scan(one_item, jnp.zeros((), jnp.int32), jnp.arange(item_count, dtype...]
    dot_general x53 -> x0, matrix products: 70 us -> none  [the longest x16 19.9 us: one_item(): lax.dot_general(rows, weight_rows, (((1,), (1,)), ((), ())), preferred_el...]
    reduce_scatter x0 -> x2, waiting for transfers between devices: none -> 62.8 us  [the longest x1 38.7 us: local(): grad_feats = lax.psum_scatter(back, ('labels', 'dp'), scatter_dimension=0)]
    another operation x1 -> x0, loops' own time: 62.5 us -> none  [local(): lax.scan(one_item, jnp.zeros((), jnp.int32), jnp.arange(item_count, dtype...]
    all_to_all x7 -> x0, waiting for transfers between devices: 62 us -> none  [the longest x1 36.4 us: local(): lax.all_to_all(outgoing, 'labels', split_axis=0, concat_axis=0, tiled=True)]
    all_gather x0 -> x1, waiting for transfers between devices: none -> 43.3 us  [local(): all_feats = lax.all_gather(feats, ('labels', 'dp'))]
    all_to_all x1 -> x0, blocking collectives: 40.1 us -> none  [local(): lax.all_to_all(item_back, 'labels', split_axis=0, concat_axis=0, tiled=True)]
    dynamic_slice x64 -> x0, local copies, waits for them, and re-layouts: 30.8 us -> none  [the longest x16 9.95 us: one_item(): first_tag[tile] + item - tile_start[tile]]
  transfers between devices with their start and end apart: 9 -> 4, of which waited for: 6 -> 3; matrix products, arithmetic and copies ran while one was open for 7% -> 0% of each run, Pallas kernels for 0% -> 0%
where the time goes in v1:
time: 198 us; the launch traced here: 197 us
  waiting for transfers between devices  108 us (55%)
  blocking collectives  57.1 us (29%)
  Pallas kernels  17.5 us (9%)
  between operations  13.8 us (7%)
    all_gather x1, waiting for transfers between devices, local(): all_feats = lax.all_gather(feats, ('labels', 'dp'))  43.3 us
    reduce_scatter x1, waiting for transfers between devices, local(): grad_feats = lax.psum_scatter(back, ('labels', 'dp'), scatter_dimension=0)  38.7 us
    psum x1, blocking collectives, local(): grad_enc = lax.psum(share.astype(F32), 'labels')  32.2 us
    all_gather x1, blocking collectives, local(): all_meta = lax.all_gather(meta, ('labels', 'dp'))  24.9 us
    reduce_scatter x1, waiting for transfers between devices, local(): share = lax.psum_scatter(enc_part, 'dp', scatter_dimension=0, tiled=True)  24.1 us
    pallas_call x1, Pallas kernels, label_work(): pl.pallas_call(functools.partial(label_kernel, cap=cap), grid=(sources //...  17.5 us
  transfers between devices with their start and end apart: 4, of which 3 were waited for; matrix products, arithmetic and copies ran while one was open for 0% of the time, Pallas kernels for 0%

profile of v1, /device:TPU:0, one launch (start us, length us, event | category | flops | bytes accessed | tf_op | source)
XLA Modules:
  0.0 197.3 jit_solution(12628559151446170750)
XLA Ops:
  7.2 0.0 all-gather.5.cloned.1.call-start
  7.2 0.7 all-gather.5.cloned.1.call-update
  7.9 0.0 all-gather.7.cloned.1.call-start
  7.9 0.7 all-gather.7.cloned.1.call-update
  8.6 0.0 reduce-scatter.5.cloned.1.call-start
  8.7 0.7 pad_add_fusion
  9.4 24.9 %all-gather = s32[48,4,128]{2,1,0:T(4,128)} all-gather(s32[3,4,128]{2,1,0:T(4,128)S(1)} %pad_add_fusion), channel_id=2, replica_groups=mesh['groups'=2,'labels'=4,'dp'=4] {'labels','dp'}, dimensions={0}, use_global_device_ids=true | all-gather | bytes 104448 | tf_op jit(solution)/shard_map/all_gather | solution.py:169
  34.3 0.0 all-gather.5.cloned.1.call-done.enc_ref
  34.3 43.3 %all-gather.7.cloned.1.call-done = bf16[2048,768]{1,0:T(8,128)(2,1)} async-done(((bf16[128,768]{1,0:T(8,128)(2,1)}), bf16[2048,768]{1,0:T(8,128)(2,1)}) %all-gather.7.cloned.1.call-update) | async-done | bytes 3145744 | tf_op jit(solution)/shard_map/all_gather | solution.py:168
  77.6 17.5 %label_work.1 = (bf16[16,128,768]{2,1,0:T(8,128)(2,1)}, bf16[1024,768]{1,0:T(8,128)(2,1)}, bf16[768,768]{1,0:T(8,128)(2,1)}) custom-call(s32[1]{0:T(128)} %bitcast.me_ref, s32[16,3,4,128]{3,2,1,0:T(4,128)} %bitcast.13, bf16[16,128,768]{2,1,0:T(8,128)(2,1)} %bitcast.17, bf16[768,768]{1,0:T(8,128)(2,1)} %all-gather.5.cloned.1.call-done.enc_ref, ...), custom_call_target="tpu_custom_call" | custom-call | flops 8858370048 | bytes 12582912 | tf_op jit(solution)/shard_map/label_work/pallas_call | solution.py:121
  95.1 0.0 reduce-scatter.5.cloned.1.call-update
  95.1 0.0 reduce-scatter.3.cloned.1.call-start
  95.2 0.5 reduce-scatter.3.cloned.1.call-update
  95.7 24.1 %reduce-scatter.5.cloned.1.call-done = bf16[192,768]{1,0:T(8,128)(2,1)} async-done(((bf16[768,768]{1,0:T(8,128)(2,1)}), bf16[192,768]{1,0:T(8,128)(2,1)}) %reduce-scatter.5.cloned.1.call-update) | async-done | bytes 294928 | tf_op jit(solution)/shard_map/reduce_scatter | solution.py:199
  119.8 32.2 %all-reduce.1 = f32[192,768]{1,0:T(8,128)} all-reduce(bf16[192,768]{1,0:T(8,128)(2,1)} %reduce-scatter.5.cloned.1.call-done), channel_id=1, replica_groups=mesh['groups'=2,'labels'=4,'dp'=4] {'labels'}, use_global_device_ids=true, to_apply=%region_2.0 | all-reduce | flops 147456 | bytes 884736 | tf_op jit(solution)/shard_map/psum | solution.py:200
  152.1 38.7 %reduce-scatter.3.cloned.1.call-done = bf16[1,128,768]{2,1,0:T(8,128)(2,1)} async-done(((bf16[16,128,768]{2,1,0:T(8,128)(2,1)}), bf16[1,128,768]{2,1,0:T(8,128)(2,1)}) %reduce-scatter.3.cloned.1.call-update) | async-done | bytes 196624 | tf_op jit(solution)/shard_map/reduce_scatter | solution.py:173
Async XLA Ops:
  7.2 27.2 %all-gather.5.cloned.1.call-start = ((), (), s32[]{:S(2)}) async-start(), calls=%async_computation.2 | async-start | bytes 1474560 | tf_op jit(solution)/shard_map/all_gather | solution.py:164
  7.9 69.7 %all-gather.7.cloned.1.call-start = ((), (), s32[]{:S(2)}) async-start(), calls=%async_computation.5 | async-start | bytes 3342336 | tf_op jit(solution)/shard_map/all_gather | solution.py:168
  8.6 111.2 %reduce-scatter.5.cloned.1.call-start = ((), (), s32[]{:S(2)}) async-start(), calls=%async_computation.4 | async-start | bytes 1474560 | tf_op jit(solution)/shard_map/reduce_scatter | solution.py:199
  95.1 95.6 %reduce-scatter.3.cloned.1.call-start = ((), (), s32[]{:S(2)}) async-start(), calls=%async_computation.3 | async-start | bytes 3342336 | tf_op jit(solution)/shard_map/reduce_scatter | solution.py:173
Sparse Core Ops, SparseCore 0:
  9.6 20.5 all-gather.4
  32.4 45.1 all-gather.6
  95.3 24.5 reduce-scatter.4
  124.6 66.1 reduce-scatter.2

commit v2 on v1

v2 whole, which is shorter than its diff:
```python
import functools

import jax
import jax.numpy as jnp
from jax import lax
from jax.experimental import pallas as pl
from jax.experimental.pallas import tpu as pltpu
from jax.sharding import PartitionSpec as P

BLK = 128
EPSILON = 1e-06
STEP_ROWS = 512
META_ROWS = 16
F32 = jnp.float32
BF16 = jnp.bfloat16


def dot(a, b, da=1, db=0):
    return lax.dot_general(a, b, (((da,), (db,)), ((), ())), preferred_element_type=F32)


def label_kernel(where_ref, *refs, cap, sources, n_data, pick_count):
    it = iter(refs)
    take = lambda n: [next(it) for _ in range(n)]
    source_refs = take(sources)
    shard_refs = take(n_data)
    label_ref = next(it)
    back_refs = take(2 * sources // n_data)
    grad_label_ref = next(it)
    share_refs = take(2)
    src, back, enc, label_acc, enc_acc, in_sem, out_sem = it

    me = where_ref[0].astype(F32)
    my_data = where_ref[1]
    rows, width = src.shape[1] - META_ROWS, src.shape[2]
    shard_rows = shard_refs[0].shape[0]
    n_blocks = label_ref.shape[0] // BLK
    group = max(1, min(sources, STEP_ROWS // cap))
    while sources % group:
        group -= 1
    slots = group * cap

    for i in range(sources):
        pltpu.make_async_copy(source_refs[i], src.at[i], in_sem.at[i]).start()

    def shard(m):
        at = jnp.bitwise_xor(my_data, m) * shard_rows
        return pl.ds(pl.multiple_of(at, 16), shard_rows)

    for m in range(n_data):
        enc[shard(m), :] = shard_refs[m][...]
    label_acc[...] = jnp.zeros_like(label_acc)
    enc_acc[...] = jnp.zeros_like(enc_acc)

    row_id = lax.broadcasted_iota(jnp.int32, (rows, rows), 0)
    col_id = lax.broadcasted_iota(jnp.int32, (rows, rows), 1)
    before = (row_id < col_id).astype(BF16)
    slot_id = lax.broadcasted_iota(jnp.int32, (cap, rows), 0).astype(F32)
    column = lax.broadcasted_iota(jnp.int32, (slots, BLK), 1)

    def chunk(g, carry):
        first = g * group
        for s in range(group):
            at = first + s
            pltpu.make_async_copy(src.at[at], src.at[at], in_sem.at[at]).wait()

        hits, codes = [], []
        for s in range(group):
            meta = src[first + s, pl.ds(rows, META_ROWS), 0 : 3 * rows].astype(F32)[:pick_count]
            named = meta[:, :rows] == me
            hits.append(jnp.sum(named.astype(F32), axis=0, keepdims=True))
            code = meta[:, rows : 2 * rows] * 256.0 + meta[:, 2 * rows :] + 1.0
            codes.append(jnp.sum(jnp.where(named, code, 0.0), axis=0, keepdims=True))
        rank = dot(jnp.concatenate(hits, axis=0).astype(BF16), before)

        picks, picked, slot_codes = [], [], []
        for s in range(group):
            pick = jnp.where((slot_id == rank[s : s + 1]) & (hits[s] > 0.0), 1.0, 0.0)
            slot_codes.append(jnp.sum(pick * codes[s], axis=1, keepdims=True))
            pick = pick.astype(BF16)
            picks.append(pick)
            picked.append(dot(pick, src[first + s, pl.ds(0, rows), :]).astype(BF16))
        feats = jnp.concatenate(picked, axis=0)
        code = jnp.concatenate(slot_codes, axis=0).astype(jnp.int32) - 1

        hidden = dot(feats, enc[...])
        inv_rms = lax.rsqrt(jnp.mean(hidden * hidden, axis=-1, keepdims=True) + EPSILON)
        embedding = (hidden * inv_rms).astype(BF16)

        scores = dot(embedding, label_ref[...], 1, 1)
        block = jnp.broadcast_to(code >> 8, (slots, BLK))
        wanted = jnp.broadcast_to(code & 255, (slots, BLK))
        own_scores = jnp.zeros((slots, BLK), F32)
        for b in range(n_blocks):
            own_scores = jnp.where(block == b, scores[:, b * BLK : (b + 1) * BLK], own_scores)
        target = jnp.where(column == wanted, 1.0, 0.0)
        grad_scores = jnp.where(block >= 0, jax.nn.sigmoid(own_scores) - target, 0.0)

        spread = jnp.concatenate(
            [jnp.where(block == b, grad_scores, 0.0).astype(BF16) for b in range(n_blocks)], axis=1
        )
        grad_pair = dot(spread, label_ref[...]).astype(BF16).astype(F32)

        grad_scores_t = grad_scores.T
        block_t = block.T
        spread_t = jnp.concatenate(
            [jnp.where(block_t == b, grad_scores_t, 0.0).astype(BF16) for b in range(n_blocks)],
            axis=0,
        )
        label_acc[...] += dot(spread_t, embedding)

        projection = jnp.mean(hidden * grad_pair, axis=-1, keepdims=True)
        grad_hidden = (inv_rms * grad_pair - hidden * (inv_rms**3 * projection)).astype(BF16)
        enc_acc[...] += dot(feats, grad_hidden, 0, 0)
        grad_feats = dot(grad_hidden, enc[...], 1, 1).astype(BF16)
        for s in range(group):
            part = dot(picks[s], grad_feats[s * cap : (s + 1) * cap], 0, 0)
            back[first + s] = part.astype(BF16)
        return carry

    lax.fori_loop(0, sources // group, chunk, 0)

    copies = []
    for i in range(sources):
        s, m = divmod(i, n_data)
        copy = pltpu.make_async_copy(
            back.at[i], back_refs[2 * s + m % 2].at[m // 2], out_sem.at[i]
        )
        copy.start()
        copies.append(copy)
    grad_label_ref[...] = label_acc[...].astype(BF16)
    for m in range(n_data):
        share_refs[m % 2][m // 2] = enc_acc[shard(m), :].astype(BF16)
    for copy in copies:
        copy.wait()


def label_work(where, blocks, shards, label_weight, cap, pick_count):
    sources, n_data = len(blocks), len(shards)
    block_rows, width = blocks[0].shape
    rows = block_rows - META_ROWS
    labels_here = label_weight.shape[0]
    shard_rows = shards[0].shape[0]
    half = n_data // 2
    hbm = pl.BlockSpec(memory_space=pl.ANY)
    vmem = pl.BlockSpec(memory_space=pltpu.VMEM)
    flops = 2 * sources * cap * width * (3 * labels_here + 3 * width + 2 * rows)
    runs = 2 * sources // n_data
    return pl.pallas_call(
        functools.partial(
            label_kernel, cap=cap, sources=sources, n_data=n_data, pick_count=pick_count
        ),
        in_specs=[pl.BlockSpec(memory_space=pltpu.SMEM)] + [hbm] * sources + [vmem] * (n_data + 1),
        out_specs=[hbm] * runs + [vmem] * 3,
        out_shape=[jax.ShapeDtypeStruct((half, rows, width), BF16)] * runs
        + [jax.ShapeDtypeStruct(label_weight.shape, BF16)]
        + [jax.ShapeDtypeStruct((half, shard_rows, width), BF16)] * 2,
        scratch_shapes=[
            pltpu.VMEM((sources, block_rows, width), BF16),
            pltpu.VMEM((sources, rows, width), BF16),
            pltpu.VMEM((n_data * shard_rows, width), BF16),
            pltpu.VMEM(label_weight.shape, F32),
            pltpu.VMEM((n_data * shard_rows, width), F32),
            pltpu.SemaphoreType.DMA((sources,)),
            pltpu.SemaphoreType.DMA((sources,)),
        ],
        compiler_params=pltpu.CompilerParams(vmem_limit_bytes=56 << 20),
        cost_estimate=pl.CostEstimate(flops=flops, bytes_accessed=12 << 20, transcendentals=0),
        name="label_work",
    )(where, *blocks, *shards, label_weight)


def swap(x):
    x = lax.all_to_all(x, "labels", split_axis=0, concat_axis=0, tiled=True)
    return lax.all_to_all(x, "dp", split_axis=1, concat_axis=1, tiled=True)


def partner(x, axis, mask):
    return lax.ppermute(x, axis, [(i, i ^ mask) for i in range(lax.axis_size(axis))])


def shifted(x, axis, by):
    n = lax.axis_size(axis)
    return lax.ppermute(x, axis, [(i, (i + by) % n) for i in range(n)])


def masks(n):
    return [1 << i for i in range(n.bit_length() - 1)]


def gather_dp(x):
    got = {0: x}
    for mask in reversed(masks(lax.axis_size("dp"))):
        got.update({m | mask: partner(v, "dp", mask) for m, v in list(got.items())})
    return [got[m] for m in range(len(got))]


def add(*terms):
    return sum(t.astype(F32) for t in terms)


def reduce_dp(even, odd):
    got = partner(odd, "dp", 1)
    terms = [[even[i], got[i]] for i in range(even.shape[0])]
    for mask in masks(len(terms)):
        for i in range(len(terms)):
            if i & mask == 0 and i % mask == 0:
                terms[i].append(partner(add(*terms[i | mask]).astype(BF16), "dp", 2 * mask))
    return add(*terms[0])


def with_meta(feats, owner_rows, block_rows, positive_rows):
    meta = jnp.concatenate([owner_rows, block_rows, positive_rows], axis=1).astype(BF16)
    meta = jnp.pad(meta, ((0, META_ROWS - meta.shape[0]), (0, feats.shape[1] - meta.shape[1])))
    return jnp.concatenate([feats, meta], axis=0)


def local(feats, enc_weight, label_weight, owners, blocks, positives):
    n_labels = lax.axis_size("labels")
    n_data = lax.axis_size("dp")
    n_owner = n_labels * n_data
    row_count, width = feats.shape
    pick_count = owners.shape[1]
    cap = max(2, 2 * row_count * pick_count // n_owner)
    my_data = lax.axis_index("dp")
    where = jnp.stack([lax.axis_index("labels") * n_data + my_data, my_data]).astype(jnp.int32)
    shards = gather_dp(enc_weight)

    if row_count <= n_data * cap:
        own = with_meta(feats, owners.T, blocks.T, positives.T)
        sources = []
        for by in range(n_labels):
            sources += gather_dp(own if by == 0 else shifted(own, "labels", by))
        *back, grad_label, even, odd = label_work(
            where, sources, shards, label_weight, cap, pick_count
        )
        total = []
        for by in range(n_labels):
            part = reduce_dp(back[2 * by], back[2 * by + 1])
            total.append(part if by == 0 else shifted(part.astype(BF16), "labels", -by))
        grad_feats = add(*total).astype(BF16)
    else:
        flat = owners.reshape(-1)
        onehot = (flat[:, None] == jnp.arange(n_owner, dtype=jnp.int32)[None, :]).astype(jnp.int32)
        rank = jnp.sum((jnp.cumsum(onehot, axis=0) - onehot) * onehot, axis=1)
        slot = (flat * cap + rank).reshape(row_count, pick_count)
        slot_total = n_owner * cap
        slots = jnp.arange(slot_total, dtype=jnp.int32)
        place = slots[:, None, None] == slot[None]
        pick = jnp.any(place, axis=2).astype(BF16)
        live = jnp.any(place, axis=(1, 2))
        block_of = jnp.sum(jnp.where(place, blocks[None], 0), axis=(1, 2))
        wanted = jnp.sum(jnp.where(place, positives[None], 0), axis=(1, 2))
        owner_of = jnp.where(live, slots // cap, -1)
        out = dot(pick, feats).astype(BF16).reshape(n_labels, n_data, cap, width)
        meta = jnp.stack([owner_of, block_of, wanted], axis=1).reshape(n_labels, n_data, cap, 3)
        tile = 128
        got = swap(out).reshape(slot_total // tile, tile, width)
        got_meta = swap(meta).reshape(slot_total // tile, tile, 3).transpose(0, 2, 1)
        sources = [
            with_meta(got[i], got_meta[i, 0:1], got_meta[i, 1:2], got_meta[i, 2:3])
            for i in range(slot_total // tile)
        ]
        *back, grad_label, even, odd = label_work(where, sources, shards, label_weight, tile, 1)
        back = jnp.stack(back).reshape(-1, 2, n_data // 2, tile, width).transpose(0, 2, 1, 3, 4)
        back = swap(back.reshape(n_labels, n_data, cap, width)).reshape(slot_total, width)
        grad_feats = dot(pick, back, 0, 0).astype(BF16)

    grad_enc = reduce_dp(even, odd)
    for mask in masks(n_labels):
        grad_enc = add(grad_enc, partner(grad_enc.astype(BF16), "labels", mask))
    return (grad_feats, grad_label, grad_enc)


def solution(mesh):
    rows = P(("groups", "labels", "dp"), None)
    return jax.shard_map(
        local,
        mesh=mesh,
        in_specs=(rows, P("dp", None), rows, rows, rows, rows),
        out_specs=(rows, rows, P(("groups", "dp"), None)),
        check_vma=False,
    )
```

time: 198 us -> 122 us (0.62)
  blocking collectives: 57.1 us -> 0 us
  waiting for transfers between devices: 108 us -> 69 us
  starting transfers between devices: 0.16 us -> 24.2 us
  between operations: 13.8 us -> 0.96 us
  other arithmetic: 0.72 us -> 8.38 us
    ppermute x0 -> x33, waiting for transfers between devices: none -> 69 us  [the longest x27 48.3 us: partner(): lax.ppermute(x, axis, [(i, i ^ mask) for i in range(lax.axis_size(axis))])]
    reduce_scatter x2 -> x0, waiting for transfers between devices: 62.8 us -> none  [the longest x1 38.7 us: local(): grad_feats = lax.psum_scatter(back, ('labels', 'dp'), scatter_dimension=0)]
    all_gather x2 -> x0, waiting for transfers between devices: 43.3 us -> none  [the longest x1 43.3 us: local(): all_feats = lax.all_gather(feats, ('labels', 'dp'))]
    psum x1 -> x0, blocking collectives: 32.2 us -> none  [local(): grad_enc = lax.psum(share.astype(F32), 'labels')]
    all_gather x1 -> x0, blocking collectives: 24.9 us -> none  [local(): all_meta = lax.all_gather(meta, ('labels', 'dp'))]
    ppermute x0 -> x33, starting transfers between devices: none -> 24.2 us  [the longest x27 16.4 us: partner(): lax.ppermute(x, axis, [(i, i ^ mask) for i in range(lax.axis_size(axis))])]
    convert_element_type x0 -> x11, other arithmetic: none -> 4.43 us  [the longest x5 3.09 us: reduce_dp(): terms[i].append(partner(add(*terms[i | mask]).astype(BF16), 'dp', 2 * mask))]
  transfers between devices with their start and end apart: 4 -> 33, of which waited for: 3 -> 14; matrix products, arithmetic and copies ran while one was open for 0% -> 4% of each run, Pallas kernels for 0% -> 0%
where the time goes in v2:
time: 122 us; the launch traced here: 121 us
  waiting for transfers between devices  69 us (57%)
  starting transfers between devices  24.2 us (20%)
  Pallas kernels  18.8 us (15%)
  other arithmetic  8.38 us (7%)
    ppermute x27, waiting for transfers between devices, partner(): lax.ppermute(x, axis, [(i, i ^ mask) for i in range(lax.axis_size(axis))])  48.3 us
    ppermute x6, waiting for transfers between devices, shifted(): return lax.ppermute(x, axis, [(i, (i + by) % n) for i in range(n)])  20.7 us
    pallas_call x1, Pallas kernels, label_work(): pl.pallas_call(functools.partial(label_kernel, cap=cap, sources=sources,...  18.8 us
    ppermute x27, starting transfers between devices, partner(): lax.ppermute(x, axis, [(i, i ^ mask) for i in range(lax.axis_size(axis))])  16.4 us
    ppermute x6, starting transfers between devices, shifted(): return lax.ppermute(x, axis, [(i, (i + by) % n) for i in range(n)])  7.83 us
    convert_element_type x5, other arithmetic, reduce_dp(): terms[i].append(partner(add(*terms[i | mask]).astype(BF16), 'dp', 2 * mask))  3.09 us
  transfers between devices with their start and end apart: 33, of which 14 were waited for; matrix products, arithmetic and copies ran while one was open for 4% of the time, Pallas kernels for 0%

profile of v2, /device:TPU:0, one launch (start us, length us, event | category | flops | bytes accessed | tf_op | source)
XLA Modules:
  0.0 121.4 jit_solution(232005443886682278)
XLA Ops:
  3.0 5.1 %collective-permute-start.11 = (bf16[144,768]{1,0:T(8,128)(2,1)S(1)}, bf16[144,768]{1,0:T(8,128)(2,1)S(1)}, u32[]{:S(2)}, u32[]{:S(2)}) collective-permute-start(bf16[144,768]{1,0:T(8,128)(2,1)S(1)} %pad_maximum_fusion.refs_0_), channel_id=1, source_target_pairs={{0,12},{4,0},{8,4},{12,8},{1,13},{5,1},{9,5},{13,9},{2,14},{6,2},{... | collective-permute-start | bytes 663560 | tf_op jit(solution)/shard_map/ppermute | solution.py:184
  8.1 1.0 collective-permute-start.3
  9.1 1.5 %collective-permute-start.1 = (bf16[144,768]{1,0:T(8,128)(2,1)S(1)}, bf16[144,768]{1,0:T(8,128)(2,1)S(1)}, u32[]{:S(2)}, u32[]{:S(2)}) collective-permute-start(bf16[144,768]{1,0:T(8,128)(2,1)S(1)} %pad_maximum_fusion.refs_0_), channel_id=1, source_target_pairs={{0,2},{1,3},{2,0},{3,1},{4,6},{5,7},{6,4},{7,5},{8,10},{9,11},{10,... | collective-permute-start | bytes 663560 | tf_op jit(solution)/shard_map/ppermute | solution.py:179
  10.6 3.4 %collective-permute-done.11.refs_12_ = bf16[144,768]{1,0:T(8,128)(2,1)S(1)} collective-permute-done((bf16[144,768]{1,0:T(8,128)(2,1)S(1)}, bf16[144,768]{1,0:T(8,128)(2,1)S(1)}, u32[]{:S(2)}, u32[]{:S(2)}) %collective-permute-start.11) | collective-permute-done | bytes 221216 | tf_op jit(solution)/shard_map/ppermute | solution.py:184
  14.0 1.5 %collective-permute-start.16 = (bf16[192,768]{1,0:T(8,128)(2,1)}, bf16[192,768]{1,0:T(8,128)(2,1)S(1)}, u32[]{:S(2)}, u32[]{:S(2)}) collective-permute-start(bf16[192,768]{1,0:T(8,128)(2,1)} %refs_16_.1), channel_id=1, source_target_pairs={{0,2},{1,3},{2,0},{3,1},{4,6},{5,7},{6,4},{7,5},{8,10},{9,11},{10,... | collective-permute-start | bytes 884744 | tf_op jit(solution)/shard_map/ppermute | solution.py:179
  15.5 11.4 %collective-permute-done.7.refs_8_ = bf16[144,768]{1,0:T(8,128)(2,1)S(1)} collective-permute-done((bf16[144,768]{1,0:T(8,128)(2,1)S(1)}, bf16[144,768]{1,0:T(8,128)(2,1)S(1)}, u32[]{:S(2)}, u32[]{:S(2)}) %collective-permute-start.7) | collective-permute-done | bytes 221216 | tf_op jit(solution)/shard_map/ppermute | solution.py:184
  26.9 1.6 %collective-permute-start.13 = (bf16[144,768]{1,0:T(8,128)(2,1)S(1)}, bf16[144,768]{1,0:T(8,128)(2,1)S(1)}, u32[]{:S(2)}, u32[]{:S(2)}) collective-permute-start(bf16[144,768]{1,0:T(8,128)(2,1)S(1)} %collective-permute-done.11.refs_12_), channel_id=1, source_target_pairs={{0,2},{1,3},{2,0},{3,1},{4,6},{5,7},{6,4},{7,5},{8,10},{9,11},{10,... | collective-permute-start | bytes 663560 | tf_op jit(solution)/shard_map/ppermute | solution.py:179
  28.6 1.2 %collective-permute-start.9 = (bf16[144,768]{1,0:T(8,128)(2,1)S(1)}, bf16[144,768]{1,0:T(8,128)(2,1)S(1)}, u32[]{:S(2)}, u32[]{:S(2)}) collective-permute-start(bf16[144,768]{1,0:T(8,128)(2,1)S(1)} %collective-permute-done.7.refs_8_), channel_id=1, source_target_pairs={{0,2},{1,3},{2,0},{3,1},{4,6},{5,7},{6,4},{7,5},{8,10},{9,11},{10,... | collective-permute-start | bytes 663560 | tf_op jit(solution)/shard_map/ppermute | solution.py:179
  30.8 4.4 %collective-permute-done.13.refs_14_ = bf16[144,768]{1,0:T(8,128)(2,1)S(1)} collective-permute-done((bf16[144,768]{1,0:T(8,128)(2,1)S(1)}, bf16[144,768]{1,0:T(8,128)(2,1)S(1)}, u32[]{:S(2)}, u32[]{:S(2)}) %collective-permute-start.13) | collective-permute-done | bytes 221216 | tf_op jit(solution)/shard_map/ppermute | solution.py:179
  35.7 4.2 %collective-permute-done.9.refs_10_ = bf16[144,768]{1,0:T(8,128)(2,1)S(1)} collective-permute-done((bf16[144,768]{1,0:T(8,128)(2,1)S(1)}, bf16[144,768]{1,0:T(8,128)(2,1)S(1)}, u32[]{:S(2)}, u32[]{:S(2)}) %collective-permute-start.9) | collective-permute-done | bytes 221216 | tf_op jit(solution)/shard_map/ppermute | solution.py:179
  40.5 3.8 %collective-permute-done.5.refs_6_ = bf16[144,768]{1,0:T(8,128)(2,1)S(1)} collective-permute-done((bf16[144,768]{1,0:T(8,128)(2,1)S(1)}, bf16[144,768]{1,0:T(8,128)(2,1)S(1)}, u32[]{:S(2)}, u32[]{:S(2)}) %collective-permute-start.5) | collective-permute-done | bytes 221216 | tf_op jit(solution)/shard_map/ppermute | solution.py:179
  46.3 18.8 %label_work.1 = (bf16[2,128,768]{2,1,0:T(8,128)(2,1)}, bf16[2,128,768]{2,1,0:T(8,128)(2,1)}, bf16[2,128,768]{2,1,0:T(8,128)(2,1)}, bf16[2,128,768]{2,1,0:T(8,128...) custom-call(s32[2]{0:T(128)} %pad_add_fusion.where_ref, ...), custom_call_target="tpu_custom_call" | custom-call | flops 8858370048 | bytes 12582912 | tf_op jit(solution)/shard_map/label_work/pallas_call | solution.py:149
  67.1 1.0 fusion.9
  68.1 1.6 %collective-permute-start.19 = (bf16[128,768]{1,0:T(8,128)(2,1)S(1)}, bf16[128,768]{1,0:T(8,128)(2,1)S(1)}, u32[]{:S(2)}, u32[]{:S(2)}) collective-permute-start(bf16[128,768]{1,0:T(8,128)(2,1)S(1)} %fusion.9), channel_id=1, source_target_pairs={{0,2},{1,3},{2,0},{3,1},{4,6},{5,7},{6,4},{7,5},{8,10},{9,11},{10,... | collective-permute-start | bytes 589832 | tf_op jit(solution)/shard_map/ppermute | solution.py:179
  69.7 1.0 fusion.10
  72.3 1.6 %collective-permute-start.24 = (bf16[128,768]{1,0:T(8,128)(2,1)S(1)}, bf16[128,768]{1,0:T(8,128)(2,1)S(1)}, u32[]{:S(2)}, u32[]{:S(2)}) collective-permute-start(bf16[128,768]{1,0:T(8,128)(2,1)S(1)} %fusion.11), channel_id=1, source_target_pairs={{0,2},{1,3},{2,0},{3,1},{4,6},{5,7},{6,4},{7,5},{8,10},{9,11},{10,... | collective-permute-start | bytes 589832 | tf_op jit(solution)/shard_map/ppermute | solution.py:179
  74.5 1.6 %collective-permute-start.27 = (bf16[128,768]{1,0:T(8,128)(2,1)S(1)}, bf16[128,768]{1,0:T(8,128)(2,1)S(1)}, u32[]{:S(2)}, u32[]{:S(2)}) collective-permute-start(bf16[128,768]{1,0:T(8,128)(2,1)S(1)} %fusion.12), channel_id=1, source_target_pairs={{0,2},{1,3},{2,0},{3,1},{4,6},{5,7},{6,4},{7,5},{8,10},{9,11},{10,... | collective-permute-start | bytes 589832 | tf_op jit(solution)/shard_map/ppermute | solution.py:179
  76.1 4.0 %collective-permute-done.21 = bf16[128,768]{1,0:T(8,128)(2,1)S(1)} collective-permute-done((bf16[128,768]{1,0:T(8,128)(2,1)S(1)}, bf16[128,768]{1,0:T(8,128)(2,1)S(1)}, u32[]{:S(2)}, u32[]{:S(2)}) %collective-permute-start.21) | collective-permute-done | bytes 196640 | tf_op jit(solution)/shard_map/ppermute | solution.py:179
  80.3 10.4 %collective-permute-done.30 = bf16[192,768]{1,0:T(8,128)(2,1)S(1)} collective-permute-done((bf16[192,768]{1,0:T(8,128)(2,1)S(1)}, bf16[192,768]{1,0:T(8,128)(2,1)S(1)}, u32[]{:S(2)}, u32[]{:S(2)}) %collective-permute-start.30) | collective-permute-done | bytes 294944 | tf_op jit(solution)/shard_map/ppermute | solution.py:179
  92.6 1.6 %collective-permute-done.27 = bf16[128,768]{1,0:T(8,128)(2,1)S(1)} collective-permute-done((bf16[128,768]{1,0:T(8,128)(2,1)S(1)}, bf16[128,768]{1,0:T(8,128)(2,1)S(1)}, u32[]{:S(2)}, u32[]{:S(2)}) %collective-permute-start.27) | collective-permute-done | bytes 196640 | tf_op jit(solution)/shard_map/ppermute | solution.py:179
  95.1 9.1 %collective-permute-done.31 = bf16[192,768]{1,0:T(8,128)(2,1)S(1)} collective-permute-done((bf16[192,768]{1,0:T(8,128)(2,1)S(1)}, bf16[192,768]{1,0:T(8,128)(2,1)S(1)}, u32[]{:S(2)}, u32[]{:S(2)}) %collective-permute-start.31) | collective-permute-done | bytes 294944 | tf_op jit(solution)/shard_map/ppermute | solution.py:179
  104.4 5.9 %collective-permute-done.28 = bf16[128,768]{1,0:T(8,128)(2,1)S(1)} collective-permute-done((bf16[128,768]{1,0:T(8,128)(2,1)S(1)}, bf16[128,768]{1,0:T(8,128)(2,1)S(1)}, u32[]{:S(2)}, u32[]{:S(2)}) %collective-permute-start.28) | collective-permute-done | bytes 196640 | tf_op jit(solution)/shard_map/ppermute | solution.py:184
  111.1 9.3 %collective-permute-done.32 = bf16[192,768]{1,0:T(8,128)(2,1)S(1)} collective-permute-done((bf16[192,768]{1,0:T(8,128)(2,1)S(1)}, bf16[192,768]{1,0:T(8,128)(2,1)S(1)}, u32[]{:S(2)}, u32[]{:S(2)}) %collective-permute-start.32) | collective-permute-done | bytes 294944 | tf_op jit(solution)/shard_map/ppermute | solution.py:179
  120.4 1.0 convert_add_fusion
  (100 shorter events, 14.7 us)
Async XLA Ops:
  3.0 11.0 %collective-permute-start.11 = (bf16[144,768]{1,0:T(8,128)(2,1)S(1)}, bf16[144,768]{1,0:T(8,128)(2,1)S(1)}, u32[]{:S(2)}, u32[]{:S(2)}) collective-permute-start(bf16[144,768]{1,0:T(8,128)(2,1)S(1)} %pad_maximum_fusion.refs_0_), channel_id=1, source_target_pairs={{0,12},{4,0},{8,4},{12,8},{1,13},{5,1},{9,5},{13,9},{2,14},{6,2},{... | collective-permute-start | bytes 663560 | tf_op jit(solution)/shard_map/ppermute | solution.py:184
  8.1 18.8 %collective-permute-start.7 = (bf16[144,768]{1,0:T(8,128)(2,1)S(1)}, bf16[144,768]{1,0:T(8,128)(2,1)S(1)}, u32[]{:S(2)}, u32[]{:S(2)}) collective-permute-start(bf16[144,768]{1,0:T(8,128)(2,1)S(1)} %pad_maximum_fusion.refs_0_), channel_id=1, source_target_pairs={{0,8},{4,12},{8,0},{12,4},{1,9},{5,13},{9,1},{13,5},{2,10},{6,14},... | collective-permute-start | bytes 663560 | tf_op jit(solution)/shard_map/ppermute | solution.py:184
  8.1 18.8 %collective-permute-start.3 = (bf16[144,768]{1,0:T(8,128)(2,1)S(1)}, bf16[144,768]{1,0:T(8,128)(2,1)S(1)}, u32[]{:S(2)}, u32[]{:S(2)}) collective-permute-start(bf16[144,768]{1,0:T(8,128)(2,1)S(1)} %pad_maximum_fusion.refs_0_), channel_id=1, source_target_pairs={{0,4},{4,8},{8,12},{12,0},{1,5},{5,9},{9,13},{13,1},{2,6},{6,10},{... | collective-permute-start | bytes 663560 | tf_op jit(solution)/shard_map/ppermute | solution.py:184
  9.1 19.4 %collective-permute-start.1 = (bf16[144,768]{1,0:T(8,128)(2,1)S(1)}, bf16[144,768]{1,0:T(8,128)(2,1)S(1)}, u32[]{:S(2)}, u32[]{:S(2)}) collective-permute-start(bf16[144,768]{1,0:T(8,128)(2,1)S(1)} %pad_maximum_fusion.refs_0_), channel_id=1, source_target_pairs={{0,2},{1,3},{2,0},{3,1},{4,6},{5,7},{6,4},{7,5},{8,10},{9,11},{10,... | collective-permute-start | bytes 663560 | tf_op jit(solution)/shard_map/ppermute | solution.py:179
  10.6 19.3 %collective-permute-start.15 = (bf16[192,768]{1,0:T(8,128)(2,1)}, bf16[192,768]{1,0:T(8,128)(2,1)S(1)}, u32[]{:S(2)}, u32[]{:S(2)}) collective-permute-start(bf16[192,768]{1,0:T(8,128)(2,1)} %refs_16_.1), channel_id=1, source_target_pairs={{0,1},{1,0},{2,3},{3,2},{4,5},{5,4},{6,7},{7,6},{8,9},{9,8},{10,11... | collective-permute-start | bytes 884744 | tf_op jit(solution)/shard_map/ppermute | solution.py:179
  14.0 15.9 %collective-permute-start.16 = (bf16[192,768]{1,0:T(8,128)(2,1)}, bf16[192,768]{1,0:T(8,128)(2,1)S(1)}, u32[]{:S(2)}, u32[]{:S(2)}) collective-permute-start(bf16[192,768]{1,0:T(8,128)(2,1)} %refs_16_.1), channel_id=1, source_target_pairs={{0,2},{1,3},{2,0},{3,1},{4,6},{5,7},{6,4},{7,5},{8,10},{9,11},{10,... | collective-permute-start | bytes 884744 | tf_op jit(solution)/shard_map/ppermute | solution.py:179
  26.9 8.3 %collective-permute-start.13 = (bf16[144,768]{1,0:T(8,128)(2,1)S(1)}, bf16[144,768]{1,0:T(8,128)(2,1)S(1)}, u32[]{:S(2)}, u32[]{:S(2)}) collective-permute-start(bf16[144,768]{1,0:T(8,128)(2,1)S(1)} %collective-permute-done.11.refs_12_), channel_id=1, source_target_pairs={{0,2},{1,3},{2,0},{3,1},{4,6},{5,7},{6,4},{7,5},{8,10},{9,11},{10,... | collective-permute-start | bytes 663560 | tf_op jit(solution)/shard_map/ppermute | solution.py:179
  28.6 11.3 %collective-permute-start.9 = (bf16[144,768]{1,0:T(8,128)(2,1)S(1)}, bf16[144,768]{1,0:T(8,128)(2,1)S(1)}, u32[]{:S(2)}, u32[]{:S(2)}) collective-permute-start(bf16[144,768]{1,0:T(8,128)(2,1)S(1)} %collective-permute-done.7.refs_8_), channel_id=1, source_target_pairs={{0,2},{1,3},{2,0},{3,1},{4,6},{5,7},{6,4},{7,5},{8,10},{9,11},{10,... | collective-permute-start | bytes 663560 | tf_op jit(solution)/shard_map/ppermute | solution.py:179
  29.9 10.1 %collective-permute-start.8 = (bf16[144,768]{1,0:T(8,128)(2,1)S(1)}, bf16[144,768]{1,0:T(8,128)(2,1)S(1)}, u32[]{:S(2)}, u32[]{:S(2)}) collective-permute-start(bf16[144,768]{1,0:T(8,128)(2,1)S(1)} %collective-permute-done.7.refs_8_), channel_id=1, source_target_pairs={{0,1},{1,0},{2,3},{3,2},{4,5},{5,4},{6,7},{7,6},{8,9},{9,8},{10,11... | collective-permute-start | bytes 663560 | tf_op jit(solution)/shard_map/ppermute | solution.py:179
  29.9 14.3 %collective-permute-start.5 = (bf16[144,768]{1,0:T(8,128)(2,1)S(1)}, bf16[144,768]{1,0:T(8,128)(2,1)S(1)}, u32[]{:S(2)}, u32[]{:S(2)}) collective-permute-start(bf16[144,768]{1,0:T(8,128)(2,1)S(1)} %collective-permute-done.3.refs_4_), channel_id=1, source_target_pairs={{0,2},{1,3},{2,0},{3,1},{4,6},{5,7},{6,4},{7,5},{8,10},{9,11},{10,... | collective-permute-start | bytes 663560 | tf_op jit(solution)/shard_map/ppermute | solution.py:179
  35.2 9.0 %collective-permute-start.4 = (bf16[144,768]{1,0:T(8,128)(2,1)S(1)}, bf16[144,768]{1,0:T(8,128)(2,1)S(1)}, u32[]{:S(2)}, u32[]{:S(2)}) collective-permute-start(bf16[144,768]{1,0:T(8,128)(2,1)S(1)} %collective-permute-done.3.refs_4_), channel_id=1, source_target_pairs={{0,1},{1,0},{2,3},{3,2},{4,5},{5,4},{6,7},{7,6},{8,9},{9,8},{10,11... | collective-permute-start | bytes 663560 | tf_op jit(solution)/shard_map/ppermute | solution.py:179
  35.2 10.1 %collective-permute-start.17 = (bf16[192,768]{1,0:T(8,128)(2,1)S(1)}, bf16[192,768]{1,0:T(8,128)(2,1)S(1)}, u32[]{:S(2)}, u32[]{:S(2)}) collective-permute-start(bf16[192,768]{1,0:T(8,128)(2,1)S(1)} %collective-permute-done.16.refs_18_), channel_id=1, source_target_pairs={{0,1},{1,0},{2,3},{3,2},{4,5},{5,4},{6,7},{7,6},{8,9},{9,8},{10,11... | collective-permute-start | bytes 884744 | tf_op jit(solution)/shard_map/ppermute | solution.py:179
  65.9 8.6 %collective-permute-start.26 = (bf16[2,128,768]{2,1,0:T(8,128)(2,1)}, bf16[2,128,768]{2,1,0:T(8,128)(2,1)S(1)}, u32[]{:S(2)}, u32[]{:S(2)}) collective-permute-start(bf16[2,128,768]{2,1,0:T(8,128)(2,1)} %get-tuple-element.21), channel_id=1, source_target_pairs={{0,1},{1,0},{2,3},{3,2},{4,5},{5,4},{6,7},{7,6},{8,9},{9,8},{10,11... | collective-permute-start | bytes 1179656 | tf_op jit(solution)/shard_map/ppermute | solution.py:179
  66.2 7.6 %collective-permute-start.29 = (bf16[2,192,768]{2,1,0:T(8,128)(2,1)}, bf16[2,192,768]{2,1,0:T(8,128)(2,1)S(1)}, u32[]{:S(2)}, u32[]{:S(2)}) collective-permute-start(bf16[2,192,768]{2,1,0:T(8,128)(2,1)} %get-tuple-element.24), channel_id=1, source_target_pairs={{0,1},{1,0},{2,3},{3,2},{4,5},{5,4},{6,7},{7,6},{8,9},{9,8},{10,11... | collective-permute-start | bytes 1769480 | tf_op jit(solution)/shard_map/ppermute | solution.py:179
  68.1 36.2 %collective-permute-start.19 = (bf16[128,768]{1,0:T(8,128)(2,1)S(1)}, bf16[128,768]{1,0:T(8,128)(2,1)S(1)}, u32[]{:S(2)}, u32[]{:S(2)}) collective-permute-start(bf16[128,768]{1,0:T(8,128)(2,1)S(1)} %fusion.9), channel_id=1, source_target_pairs={{0,2},{1,3},{2,0},{3,1},{4,6},{5,7},{6,4},{7,5},{8,10},{9,11},{10,... | collective-permute-start | bytes 589832 | tf_op jit(solution)/shard_map/ppermute | solution.py:179
  70.7 9.5 %collective-permute-start.21 = (bf16[128,768]{1,0:T(8,128)(2,1)S(1)}, bf16[128,768]{1,0:T(8,128)(2,1)S(1)}, u32[]{:S(2)}, u32[]{:S(2)}) collective-permute-start(bf16[128,768]{1,0:T(8,128)(2,1)S(1)} %fusion.10), channel_id=1, source_target_pairs={{0,2},{1,3},{2,0},{3,1},{4,6},{5,7},{6,4},{7,5},{8,10},{9,11},{10,... | collective-permute-start | bytes 589832 | tf_op jit(solution)/shard_map/ppermute | solution.py:179
  72.3 19.4 %collective-permute-start.24 = (bf16[128,768]{1,0:T(8,128)(2,1)S(1)}, bf16[128,768]{1,0:T(8,128)(2,1)S(1)}, u32[]{:S(2)}, u32[]{:S(2)}) collective-permute-start(bf16[128,768]{1,0:T(8,128)(2,1)S(1)} %fusion.11), channel_id=1, source_target_pairs={{0,2},{1,3},{2,0},{3,1},{4,6},{5,7},{6,4},{7,5},{8,10},{9,11},{10,... | collective-permute-start | bytes 589832 | tf_op jit(solution)/shard_map/ppermute | solution.py:179
  73.9 16.8 %collective-permute-start.30 = (bf16[192,768]{1,0:T(8,128)(2,1)S(1)}, bf16[192,768]{1,0:T(8,128)(2,1)S(1)}, u32[]{:S(2)}, u32[]{:S(2)}) collective-permute-start(bf16[192,768]{1,0:T(8,128)(2,1)S(1)} %fusion.8), channel_id=1, source_target_pairs={{0,2},{1,3},{2,0},{3,1},{4,6},{5,7},{6,4},{7,5},{8,10},{9,11},{10,... | collective-permute-start | bytes 884744 | tf_op jit(solution)/shard_map/ppermute | solution.py:179
  74.5 19.6 %collective-permute-start.27 = (bf16[128,768]{1,0:T(8,128)(2,1)S(1)}, bf16[128,768]{1,0:T(8,128)(2,1)S(1)}, u32[]{:S(2)}, u32[]{:S(2)}) collective-permute-start(bf16[128,768]{1,0:T(8,128)(2,1)S(1)} %fusion.12), channel_id=1, source_target_pairs={{0,2},{1,3},{2,0},{3,1},{4,6},{5,7},{6,4},{7,5},{8,10},{9,11},{10,... | collective-permute-start | bytes 589832 | tf_op jit(solution)/shard_map/ppermute | solution.py:179
  80.2 24.1 %collective-permute-start.22 = (bf16[128,768]{1,0:T(8,128)(2,1)S(1)}, bf16[128,768]{1,0:T(8,128)(2,1)S(1)}, u32[]{:S(2)}, u32[]{:S(2)}) collective-permute-start(bf16[128,768]{1,0:T(8,128)(2,1)S(1)} %fusion.3), channel_id=1, source_target_pairs={{0,12},{4,0},{8,4},{12,8},{1,13},{5,1},{9,5},{13,9},{2,14},{6,2},{... | collective-permute-start | bytes 589832 | tf_op jit(solution)/shard_map/ppermute | solution.py:184
  90.8 13.3 %collective-permute-start.31 = (bf16[192,768]{1,0:T(8,128)(2,1)S(1)}, bf16[192,768]{1,0:T(8,128)(2,1)S(1)}, u32[]{:S(2)}, u32[]{:S(2)}) collective-permute-start(bf16[192,768]{1,0:T(8,128)(2,1)S(1)} %fusion.22), channel_id=1, source_target_pairs={{0,4},{4,0},{8,12},{12,8},{1,5},{5,1},{9,13},{13,9},{2,6},{6,2},{1... | collective-permute-start | bytes 884744 | tf_op jit(solution)/shard_map/ppermute | solution.py:179
  91.7 12.7 %collective-permute-start.25 = (bf16[128,768]{1,0:T(8,128)(2,1)S(1)}, bf16[128,768]{1,0:T(8,128)(2,1)S(1)}, u32[]{:S(2)}, u32[]{:S(2)}) collective-permute-start(bf16[128,768]{1,0:T(8,128)(2,1)S(1)} %fusion.2), channel_id=1, source_target_pairs={{0,8},{4,12},{8,0},{12,4},{1,9},{5,13},{9,1},{13,5},{2,10},{6,14},... | collective-permute-start | bytes 589832 | tf_op jit(solution)/shard_map/ppermute | solution.py:184
  94.3 16.0 %collective-permute-start.28 = (bf16[128,768]{1,0:T(8,128)(2,1)S(1)}, bf16[128,768]{1,0:T(8,128)(2,1)S(1)}, u32[]{:S(2)}, u32[]{:S(2)}) collective-permute-start(bf16[128,768]{1,0:T(8,128)(2,1)S(1)} %fusion.1), channel_id=1, source_target_pairs={{0,4},{4,8},{8,12},{12,0},{1,5},{5,9},{9,13},{13,1},{2,6},{6,10},{... | collective-permute-start | bytes 589832 | tf_op jit(solution)/shard_map/ppermute | solution.py:184
  104.3 16.1 %collective-permute-start.32 = (bf16[192,768]{1,0:T(8,128)(2,1)S(1)}, bf16[192,768]{1,0:T(8,128)(2,1)S(1)}, u32[]{:S(2)}, u32[]{:S(2)}) collective-permute-start(bf16[192,768]{1,0:T(8,128)(2,1)S(1)} %fusion), channel_id=1, source_target_pairs={{0,8},{4,12},{8,0},{12,4},{1,9},{5,13},{9,1},{13,5},{2,10},{6,14},... | collective-permute-start | bytes 884744 | tf_op jit(solution)/shard_map/ppermute | solution.py:179
  (29 other events, 324.8 us)

commit v3 on v2

v3 whole, which is shorter than its diff:
```python
import functools

import jax
import jax.numpy as jnp
from jax import lax
from jax.experimental import pallas as pl
from jax.experimental.pallas import tpu as pltpu
from jax.sharding import PartitionSpec as P

BLK = 128
EPSILON = 1e-06
META_ROWS = 16
F32 = jnp.float32
BF16 = jnp.bfloat16


def dot(a, b, da=1, db=0):
    return lax.dot_general(a, b, (((da,), (db,)), ((), ())), preferred_element_type=F32)


def pair_kernel(where_ref, *refs, cap, pick_count):
    n_data = (len(refs) - 9) // 2
    sources, shards, label_ref = refs[:n_data], refs[n_data : 2 * n_data], refs[2 * n_data]
    even_ref, odd_ref, grad_scores_ref, block_ref, embedding_ref, feats_ref, grad_hidden_ref, enc = (
        refs[2 * n_data + 1 :]
    )
    me = where_ref[0].astype(F32)
    my_data = where_ref[1]
    rows = sources[0].shape[0] - META_ROWS
    shard_rows = shards[0].shape[0]
    n_blocks = label_ref.shape[0] // BLK
    slots = n_data * cap

    for m in range(n_data):
        enc[shard_at(my_data, m, shard_rows), :] = shards[m][...]

    row_id = lax.broadcasted_iota(jnp.int32, (rows, rows), 0)
    col_id = lax.broadcasted_iota(jnp.int32, (rows, rows), 1)
    before = (row_id < col_id).astype(BF16)
    slot_id = lax.broadcasted_iota(jnp.int32, (cap, rows), 0).astype(F32)
    column = lax.broadcasted_iota(jnp.int32, (slots, BLK), 1)

    hits, codes = [], []
    for source in sources:
        meta = source[rows:, 0 : 3 * rows].astype(F32)[:pick_count]
        named = meta[:, :rows] == me
        hits.append(jnp.sum(named.astype(F32), axis=0, keepdims=True))
        code = meta[:, rows : 2 * rows] * 256.0 + meta[:, 2 * rows :] + 1.0
        codes.append(jnp.sum(jnp.where(named, code, 0.0), axis=0, keepdims=True))
    rank = dot(jnp.concatenate(hits, axis=0).astype(BF16), before)

    picks, picked, slot_codes = [], [], []
    for s, source in enumerate(sources):
        pick = jnp.where((slot_id == rank[s : s + 1]) & (hits[s] > 0.0), 1.0, 0.0)
        slot_codes.append(jnp.sum(pick * codes[s], axis=1, keepdims=True))
        pick = pick.astype(BF16)
        picks.append(pick)
        picked.append(dot(pick, source[:rows, :]).astype(BF16))
    feats = jnp.concatenate(picked, axis=0)
    feats_ref[...] = feats
    code = jnp.concatenate(slot_codes, axis=0).astype(jnp.int32) - 1

    hidden = dot(feats, enc[...])
    inv_rms = lax.rsqrt(jnp.mean(hidden * hidden, axis=-1, keepdims=True) + EPSILON)
    embedding = (hidden * inv_rms).astype(BF16)
    embedding_ref[...] = embedding

    scores = dot(embedding, label_ref[...], 1, 1)
    block = jnp.broadcast_to(code >> 8, (slots, BLK))
    block_ref[...] = block
    wanted = jnp.broadcast_to(code & 255, (slots, BLK))
    own_scores = jnp.zeros((slots, BLK), F32)
    for b in range(n_blocks):
        own_scores = jnp.where(block == b, scores[:, b * BLK : (b + 1) * BLK], own_scores)
    target = jnp.where(column == wanted, 1.0, 0.0)
    grad_scores = jnp.where(block >= 0, jax.nn.sigmoid(own_scores) - target, 0.0)
    grad_scores_ref[...] = grad_scores

    spread = jnp.concatenate(
        [jnp.where(block == b, grad_scores, 0.0).astype(BF16) for b in range(n_blocks)], axis=1
    )
    grad_pair = dot(spread, label_ref[...]).astype(BF16).astype(F32)
    projection = jnp.mean(hidden * grad_pair, axis=-1, keepdims=True)
    grad_hidden = (inv_rms * grad_pair - hidden * (inv_rms**3 * projection)).astype(BF16)
    grad_hidden_ref[...] = grad_hidden
    grad_feats = dot(grad_hidden, enc[...], 1, 1).astype(BF16)
    for m in range(n_data):
        part = dot(picks[m], grad_feats[m * cap : (m + 1) * cap], 0, 0)
        (odd_ref if m % 2 else even_ref)[m // 2] = part.astype(BF16)


def enc_kernel(where_ref, *refs):
    runs = (len(refs) - 3) // 2
    even_ref, odd_ref, total = refs[2 * runs :]
    feats = jnp.concatenate([r[...] for r in refs[:runs]], axis=0)
    grad_hidden = jnp.concatenate([r[...] for r in refs[runs : 2 * runs]], axis=0)
    total[...] = dot(feats, grad_hidden, 0, 0)
    half, shard_rows, _ = even_ref.shape
    for m in range(2 * half):
        part = total[shard_at(where_ref[1], m, shard_rows), :]
        (odd_ref if m % 2 else even_ref)[m // 2] = part.astype(BF16)


def grad_label_kernel(*refs):
    runs = (len(refs) - 1) // 3
    grad_scores, blocks, embeddings = refs[:runs], refs[runs : 2 * runs], refs[2 * runs : 3 * runs]
    out_ref = refs[-1]
    grad_scores_t = jnp.concatenate([r[...].T for r in grad_scores], axis=1)
    block_t = jnp.concatenate([r[...].T for r in blocks], axis=1)
    embedding = jnp.concatenate([r[...] for r in embeddings], axis=0)
    for b in range(out_ref.shape[0] // BLK):
        spread_t = jnp.where(block_t == b, grad_scores_t, 0.0).astype(BF16)
        out_ref[b * BLK : (b + 1) * BLK, :] = dot(spread_t, embedding).astype(BF16)


def shard_at(my_data, m, shard_rows):
    at = jnp.bitwise_xor(my_data, m) * shard_rows
    return pl.ds(pl.multiple_of(at, 16), shard_rows)


def call(kernel, name, out_shape, scratch, flops, megabytes, *args):
    smem = pl.BlockSpec(memory_space=pltpu.SMEM)
    vmem = pl.BlockSpec(memory_space=pltpu.VMEM)
    return pl.pallas_call(
        kernel,
        in_specs=[smem if a.ndim == 1 else vmem for a in args],
        out_specs=jax.tree.map(lambda _: vmem, out_shape),
        out_shape=out_shape,
        scratch_shapes=scratch,
        compiler_params=pltpu.CompilerParams(vmem_limit_bytes=24 << 20),
        cost_estimate=pl.CostEstimate(
            flops=flops, bytes_accessed=megabytes << 20, transcendentals=0
        ),
        name=name,
    )(*args)


def pair_work(where, sources, shards, label_weight, cap, pick_count):
    n_data = len(sources)
    rows, width = sources[0].shape[0] - META_ROWS, sources[0].shape[1]
    slots = n_data * cap
    return call(
        functools.partial(pair_kernel, cap=cap, pick_count=pick_count),
        "pair_work",
        [jax.ShapeDtypeStruct((n_data // 2, rows, width), BF16)] * 2
        + [
            jax.ShapeDtypeStruct((slots, BLK), F32),
            jax.ShapeDtypeStruct((slots, BLK), jnp.int32),
        ]
        + [jax.ShapeDtypeStruct((slots, width), BF16)] * 3,
        [pltpu.VMEM((n_data * shards[0].shape[0], width), BF16)],
        2 * slots * width * (2 * label_weight.shape[0] + 2 * width + 2 * rows),
        8,
        where,
        *sources,
        *shards,
        label_weight,
    )


def enc_work(where, feats, grad_hidden, shard, n_data):
    shard_rows, width = shard.shape
    return call(
        enc_kernel,
        "enc_work",
        [jax.ShapeDtypeStruct((n_data // 2, shard_rows, width), BF16)] * 2,
        [pltpu.VMEM((n_data * shard_rows, width), F32)],
        2 * len(feats) * feats[0].shape[0] * width * width,
        4,
        where,
        *feats,
        *grad_hidden,
    )


def grad_label_work(grad_scores, blocks, embeddings, label_weight):
    return call(
        grad_label_kernel,
        "grad_label_work",
        jax.ShapeDtypeStruct(label_weight.shape, BF16),
        [],
        2 * len(blocks) * blocks[0].shape[0] * label_weight.size,
        4,
        *grad_scores,
        *blocks,
        *embeddings,
    )


def swap(x):
    x = lax.all_to_all(x, "labels", split_axis=0, concat_axis=0, tiled=True)
    return lax.all_to_all(x, "dp", split_axis=1, concat_axis=1, tiled=True)


def partner(x, axis, mask):
    return lax.ppermute(x, axis, [(i, i ^ mask) for i in range(lax.axis_size(axis))])


def shifted(x, axis, by):
    n = lax.axis_size(axis)
    return lax.ppermute(x, axis, [(i, (i + by) % n) for i in range(n)])


def masks(n):
    return [1 << i for i in range(n.bit_length() - 1)]


def gather_dp(x):
    got = {0: x}
    for mask in reversed(masks(lax.axis_size("dp"))):
        got.update({m | mask: partner(v, "dp", mask) for m, v in list(got.items())})
    return [got[m] for m in range(len(got))]


def add(*terms):
    return sum(t.astype(F32) for t in terms)


def reduce_dp(even, odd):
    got = partner(odd, "dp", 1)
    terms = [[even[i], got[i]] for i in range(even.shape[0])]
    for mask in masks(len(terms)):
        for i in range(len(terms)):
            if i & mask == 0 and i % mask == 0:
                terms[i].append(partner(add(*terms[i | mask]).astype(BF16), "dp", 2 * mask))
    return add(*terms[0])


def with_meta(feats, owner_rows, block_rows, positive_rows):
    meta = jnp.concatenate([owner_rows, block_rows, positive_rows], axis=1).astype(BF16)
    meta = jnp.pad(meta, ((0, META_ROWS - meta.shape[0]), (0, feats.shape[1] - meta.shape[1])))
    return jnp.concatenate([feats, meta], axis=0)


def local(feats, enc_weight, label_weight, owners, blocks, positives):
    n_labels = lax.axis_size("labels")
    n_data = lax.axis_size("dp")
    n_owner = n_labels * n_data
    row_count, width = feats.shape
    pick_count = owners.shape[1]
    cap = max(2, 2 * row_count * pick_count // n_owner)
    my_data = lax.axis_index("dp")
    where = jnp.stack([lax.axis_index("labels") * n_data + my_data, my_data]).astype(jnp.int32)
    shards = gather_dp(enc_weight)

    if row_count <= n_data * cap:
        own = with_meta(feats, owners.T, blocks.T, positives.T)
        runs = []
        block = own
        for by in range(n_labels):
            if by:
                block = shifted(block, "labels", 1)
            runs.append(gather_dp(block))
        work = [
            pair_work(where, sources, shards, label_weight, cap, pick_count) for sources in runs
        ]
        total = []
        for by in range(n_labels):
            part = reduce_dp(work[by][0], work[by][1])
            total.append(part if by == 0 else shifted(part.astype(BF16), "labels", -by))
        grad_feats = add(*total).astype(BF16)
    else:
        flat = owners.reshape(-1)
        onehot = (flat[:, None] == jnp.arange(n_owner, dtype=jnp.int32)[None, :]).astype(jnp.int32)
        rank = jnp.sum((jnp.cumsum(onehot, axis=0) - onehot) * onehot, axis=1)
        slot = (flat * cap + rank).reshape(row_count, pick_count)
        slot_total = n_owner * cap
        slots = jnp.arange(slot_total, dtype=jnp.int32)
        place = slots[:, None, None] == slot[None]
        pick = jnp.any(place, axis=2).astype(BF16)
        live = jnp.any(place, axis=(1, 2))
        block_of = jnp.sum(jnp.where(place, blocks[None], 0), axis=(1, 2))
        wanted = jnp.sum(jnp.where(place, positives[None], 0), axis=(1, 2))
        owner_of = jnp.where(live, slots // cap, -1)
        out = dot(pick, feats).astype(BF16).reshape(n_labels, n_data, cap, width)
        meta = jnp.stack([owner_of, block_of, wanted], axis=1).reshape(n_labels, n_data, cap, 3)
        tile = 128
        got = swap(out).reshape(slot_total // tile, tile, width)
        got_meta = swap(meta).reshape(slot_total // tile, tile, 3).transpose(0, 2, 1)
        sources = [
            with_meta(got[i], got_meta[i, 0:1], got_meta[i, 1:2], got_meta[i, 2:3])
            for i in range(slot_total // tile)
        ]
        work = [
            pair_work(where, sources[i : i + n_data], shards, label_weight, tile, 1)
            for i in range(0, len(sources), n_data)
        ]
        back = jnp.stack([part for run in work for part in run[:2]])
        back = back.reshape(-1, 2, n_data // 2, tile, width).transpose(0, 2, 1, 3, 4)
        back = swap(back.reshape(n_labels, n_data, cap, width)).reshape(slot_total, width)
        grad_feats = dot(pick, back, 0, 0).astype(BF16)

    _, _, grad_scores, block_of, embedding, picked, grad_hidden = zip(*work)
    even, odd = enc_work(where, picked, grad_hidden, enc_weight, n_data)
    grad_label = grad_label_work(grad_scores, block_of, embedding, label_weight)
    grad_enc = reduce_dp(even, odd)
    for mask in masks(n_labels):
        grad_enc = add(grad_enc, partner(grad_enc.astype(BF16), "labels", mask))
    return (grad_feats, grad_label, grad_enc)


def solution(mesh):
    rows = P(("groups", "labels", "dp"), None)
    return jax.shard_map(
        local,
        mesh=mesh,
        in_specs=(rows, P("dp", None), rows, rows, rows, rows),
        out_specs=(rows, rows, P(("groups", "dp"), None)),
        check_vma=False,
    )
```

time: 122 us -> 104 us (0.85)
  waiting for transfers between devices: 69 us -> 55.3 us
  starting transfers between devices: 24.2 us -> 20 us
  other arithmetic: 8.38 us -> 5 us
  local copies, waits for them, and re-layouts: 0.08 us -> 2.38 us
    ppermute x27, waiting for transfers between devices: 48.3 us -> 31.5 us  [partner(): lax.ppermute(x, axis, [(i, i ^ mask) for i in range(lax.axis_size(axis))])]
    ppermute x6, waiting for transfers between devices: 20.7 us -> 23.8 us  [shifted(): return lax.ppermute(x, axis, [(i, (i + by) % n) for i in range(n)])]
    convert_element_type x5, other arithmetic: 3.09 us -> 0.28 us  [reduce_dp(): terms[i].append(partner(add(*terms[i | mask]).astype(BF16), 'dp', 2 * mask))]
    ppermute x27, starting transfers between devices: 16.4 us -> 13.8 us  [partner(): lax.ppermute(x, axis, [(i, i ^ mask) for i in range(lax.axis_size(axis))])]
    unnamed x40 -> x8, local copies, waits for them, and re-layouts: 0.08 us -> 2.38 us
    ppermute x6, starting transfers between devices: 7.83 us -> 6.25 us  [shifted(): return lax.ppermute(x, axis, [(i, (i + by) % n) for i in range(n)])]
    pallas_call x1 -> x6, Pallas kernels: 18.8 us -> 19.9 us  [call(): pl.pallas_call(kernel, in_specs=[smem if a.ndim == 1 else vmem for a in a...]
  transfers between devices with their start and end apart: 33 -> 33, of which waited for: 14 -> 12; matrix products, arithmetic and copies ran while one was open for 4% -> 2% of each run, Pallas kernels for 0% -> 19%
where the time goes in v3:
time: 104 us; the launch traced here: 103 us
  waiting for transfers between devices  55.3 us (53%)
  starting transfers between devices  20 us (19%)
  Pallas kernels  19.9 us (19%)
  other arithmetic  5 us (5%)
  local copies, waits for them, and re-layouts  2.38 us (2%)
    ppermute x27, waiting for transfers between devices, partner(): lax.ppermute(x, axis, [(i, i ^ mask) for i in range(lax.axis_size(axis))])  31.5 us
    ppermute x6, waiting for transfers between devices, shifted(): return lax.ppermute(x, axis, [(i, (i + by) % n) for i in range(n)])  23.8 us
    pallas_call x6, Pallas kernels, call(): pl.pallas_call(kernel, in_specs=[smem if a.ndim == 1 else vmem for a in a...  19.9 us
    ppermute x27, starting transfers between devices, partner(): lax.ppermute(x, axis, [(i, i ^ mask) for i in range(lax.axis_size(axis))])  13.8 us
    ppermute x6, starting transfers between devices, shifted(): return lax.ppermute(x, axis, [(i, (i + by) % n) for i in range(n)])  6.25 us
    unnamed x8, local copies, waits for them, and re-layouts  2.38 us
  transfers between devices with their start and end apart: 33, of which 12 were waited for; matrix products, arithmetic and copies ran while one was open for 2% of the time, Pallas kernels for 19%

profile of v3, /device:TPU:0, one launch (start us, length us, event | category | flops | bytes accessed | tf_op | source)
XLA Modules:
  0.0 103.4 jit_solution(788747553004882438)
XLA Ops:
  3.0 3.1 %collective-permute-start.8 = (bf16[144,768]{1,0:T(8,128)(2,1)S(1)}, bf16[144,768]{1,0:T(8,128)(2,1)S(1)}, u32[]{:S(2)}, u32[]{:S(2)}) collective-permute-start(bf16[144,768]{1,0:T(8,128)(2,1)S(1)} %pad_maximum_fusion.refs_0_), channel_id=1, source_target_pairs={{0,4},{4,8},{8,12},{12,0},{1,5},{5,9},{9,13},{13,1},{2,6},{6,10},{... | collective-permute-start | bytes 663560 | tf_op jit(solution)/shard_map/ppermute | solution.py:201
  6.1 1.5 %collective-permute-start.4 = (bf16[192,768]{1,0:T(8,128)(2,1)}, bf16[192,768]{1,0:T(8,128)(2,1)S(1)}, u32[]{:S(2)}, u32[]{:S(2)}) collective-permute-start(bf16[192,768]{1,0:T(8,128)(2,1)} %refs_4_.7), channel_id=1, source_target_pairs={{0,2},{1,3},{2,0},{3,1},{4,6},{5,7},{6,4},{7,5},{8,10},{9,11},{10,... | collective-permute-start | bytes 884744 | tf_op jit(solution)/shard_map/ppermute | solution.py:196
  8.1 5.4 %collective-permute-done.8.refs_0_ = bf16[144,768]{1,0:T(8,128)(2,1)S(1)} collective-permute-done((bf16[144,768]{1,0:T(8,128)(2,1)S(1)}, bf16[144,768]{1,0:T(8,128)(2,1)S(1)}, u32[]{:S(2)}, u32[]{:S(2)}) %collective-permute-start.8) | collective-permute-done | bytes 221216 | tf_op jit(solution)/shard_map/ppermute | solution.py:201
  13.5 6.0 %collective-permute-done.1.refs_2_ = bf16[144,768]{1,0:T(8,128)(2,1)S(1)} collective-permute-done((bf16[144,768]{1,0:T(8,128)(2,1)S(1)}, bf16[144,768]{1,0:T(8,128)(2,1)S(1)}, u32[]{:S(2)}, u32[]{:S(2)}) %collective-permute-start.1) | collective-permute-done | bytes 221216 | tf_op jit(solution)/shard_map/ppermute | solution.py:196
  19.5 1.5 %collective-permute-start.10 = (bf16[144,768]{1,0:T(8,128)(2,1)S(1)}, bf16[144,768]{1,0:T(8,128)(2,1)S(1)}, u32[]{:S(2)}, u32[]{:S(2)}) collective-permute-start(bf16[144,768]{1,0:T(8,128)(2,1)S(1)} %collective-permute-done.8.refs_0_), channel_id=1, source_target_pairs={{0,2},{1,3},{2,0},{3,1},{4,6},{5,7},{6,4},{7,5},{8,10},{9,11},{10,... | collective-permute-start | bytes 663560 | tf_op jit(solution)/shard_map/ppermute | solution.py:196
  23.3 2.1 %collective-permute-done.10.refs_2_ = bf16[144,768]{1,0:T(8,128)(2,1)S(1)} collective-permute-done((bf16[144,768]{1,0:T(8,128)(2,1)S(1)}, bf16[144,768]{1,0:T(8,128)(2,1)S(1)}, u32[]{:S(2)}, u32[]{:S(2)}) %collective-permute-start.10) | collective-permute-done | bytes 221216 | tf_op jit(solution)/shard_map/ppermute | solution.py:196
  26.0 4.6 %collective-permute-done.22.refs_0_ = bf16[144,768]{1,0:T(8,128)(2,1)S(1)} collective-permute-done((bf16[144,768]{1,0:T(8,128)(2,1)S(1)}, bf16[144,768]{1,0:T(8,128)(2,1)S(1)}, u32[]{:S(2)}, u32[]{:S(2)}) %collective-permute-start.22) | collective-permute-done | bytes 221216 | tf_op jit(solution)/shard_map/ppermute | solution.py:201
  34.1 3.6 %pair_work.4 = (bf16[2,128,768]{2,1,0:T(8,128)(2,1)S(1)}, bf16[2,128,768]{2,1,0:T(8,128)(2,1)S(1)}, f32[256,128]{1,0:T(8,128)S(1)}, s32[256,128]{1,0:T(8,128)S(1...) custom-call(s32[2]{0:T(128)S(1)} %pad_add_fusion.where_ref, ...), custom_call_target="tpu_custom_call" | custom-call | flops 1509949440 | bytes 8388608 | tf_op jit(solution)/shard_map/pair_work/pallas_call | solution.py:124
  38.4 3.7 %pair_work.5 = (bf16[2,128,768]{2,1,0:T(8,128)(2,1)S(1)}, bf16[2,128,768]{2,1,0:T(8,128)(2,1)S(1)}, f32[256,128]{1,0:T(8,128)S(1)}, s32[256,128]{1,0:T(8,128)S(1...) custom-call(s32[2]{0:T(128)S(1)} %pad_add_fusion.where_ref, ...), custom_call_target="tpu_custom_call" | custom-call | flops 1509949440 | bytes 8388608 | tf_op jit(solution)/shard_map/pair_work/pallas_call | solution.py:124
  42.6 3.6 %pair_work.6 = (bf16[2,128,768]{2,1,0:T(8,128)(2,1)S(1)}, bf16[2,128,768]{2,1,0:T(8,128)(2,1)S(1)}, f32[256,128]{1,0:T(8,128)S(1)}, s32[256,128]{1,0:T(8,128)S(1...) custom-call(s32[2]{0:T(128)S(1)} %pad_add_fusion.where_ref, ...), custom_call_target="tpu_custom_call" | custom-call | flops 1509949440 | bytes 8388608 | tf_op jit(solution)/shard_map/pair_work/pallas_call | solution.py:124
  46.4 3.7 %pair_work.7 = (bf16[2,128,768]{2,1,0:T(8,128)(2,1)S(1)}, bf16[2,128,768]{2,1,0:T(8,128)(2,1)S(1)}, f32[256,128]{1,0:T(8,128)S(1)}, s32[256,128]{1,0:T(8,128)S(1...) custom-call(s32[2]{0:T(128)S(1)} %pad_add_fusion.where_ref, ...), custom_call_target="tpu_custom_call" | custom-call | flops 1509949440 | bytes 8388608 | tf_op jit(solution)/shard_map/pair_work/pallas_call | solution.py:124
  50.1 2.1 %enc_work.1 = (bf16[2,192,768]{2,1,0:T(8,128)(2,1)S(1)}, bf16[2,192,768]{2,1,0:T(8,128)(2,1)S(1)}) custom-call(s32[2]{0:T(128)S(1)} %pad_add_fusion.where_ref, bf16[256,768]{1,0:T(8,128)(2,1)S(1)} %get-tuple-element.53.refs_0_, bf16[256,768]{1,0:T(8,128)(2,1)S(1)} %get-tuple-element.54.refs_1_, bf16[256,768]{1,0:T(8,128)(2,1)S(1)} %get-tuple-element.55.refs_2_, ...), custom_call_target="tpu_custom_call" | custom-call | flops 1207959552 | bytes 4194304 | tf_op jit(solution)/shard_map/enc_work/pallas_call | solution.py:124
  52.7 1.6 %collective-permute-start.13 = (bf16[128,768]{1,0:T(8,128)(2,1)S(1)}, bf16[128,768]{1,0:T(8,128)(2,1)S(1)}, u32[]{:S(2)}, u32[]{:S(2)}) collective-permute-start(bf16[128,768]{1,0:T(8,128)(2,1)S(1)} %fusion.10), channel_id=1, source_target_pairs={{0,2},{1,3},{2,0},{3,1},{4,6},{5,7},{6,4},{7,5},{8,10},{9,11},{10,... | collective-permute-start | bytes 589832 | tf_op jit(solution)/shard_map/ppermute | solution.py:196
  54.9 5.6 %collective-permute-done.13 = bf16[128,768]{1,0:T(8,128)(2,1)S(1)} collective-permute-done((bf16[128,768]{1,0:T(8,128)(2,1)S(1)}, bf16[128,768]{1,0:T(8,128)(2,1)S(1)}, u32[]{:S(2)}, u32[]{:S(2)}) %collective-permute-start.13) | collective-permute-done | bytes 196640 | tf_op jit(solution)/shard_map/ppermute | solution.py:196
  60.6 2.2 %collective-permute-start.14 = (bf16[128,768]{1,0:T(8,128)(2,1)S(1)}, bf16[128,768]{1,0:T(8,128)(2,1)S(1)}, u32[]{:S(2)}, u32[]{:S(2)}) collective-permute-start(bf16[128,768]{1,0:T(8,128)(2,1)S(1)} %fusion.3), channel_id=1, source_target_pairs={{0,12},{4,0},{8,4},{12,8},{1,13},{5,1},{9,5},{13,9},{2,14},{6,2},{... | collective-permute-start | bytes 589832 | tf_op jit(solution)/shard_map/ppermute | solution.py:201
  62.9 1.7 %collective-permute-start.30 = (bf16[192,768]{1,0:T(8,128)(2,1)S(1)}, bf16[192,768]{1,0:T(8,128)(2,1)S(1)}, u32[]{:S(2)}, u32[]{:S(2)}) collective-permute-start(bf16[192,768]{1,0:T(8,128)(2,1)S(1)} %fusion.8), channel_id=1, source_target_pairs={{0,2},{1,3},{2,0},{3,1},{4,6},{5,7},{6,4},{7,5},{8,10},{9,11},{10,... | collective-permute-start | bytes 884744 | tf_op jit(solution)/shard_map/ppermute | solution.py:196
  65.2 1.7 %collective-permute-start.27 = (bf16[128,768]{1,0:T(8,128)(2,1)S(1)}, bf16[128,768]{1,0:T(8,128)(2,1)S(1)}, u32[]{:S(2)}, u32[]{:S(2)}) collective-permute-start(bf16[128,768]{1,0:T(8,128)(2,1)S(1)} %fusion.12), channel_id=1, source_target_pairs={{0,2},{1,3},{2,0},{3,1},{4,6},{5,7},{6,4},{7,5},{8,10},{9,11},{10,... | collective-permute-start | bytes 589832 | tf_op jit(solution)/shard_map/ppermute | solution.py:196
  66.9 6.0 %collective-permute-done.30 = bf16[192,768]{1,0:T(8,128)(2,1)S(1)} collective-permute-done((bf16[192,768]{1,0:T(8,128)(2,1)S(1)}, bf16[192,768]{1,0:T(8,128)(2,1)S(1)}, u32[]{:S(2)}, u32[]{:S(2)}) %collective-permute-start.30) | collective-permute-done | bytes 294944 | tf_op jit(solution)/shard_map/ppermute | solution.py:196
  73.1 4.0 %collective-permute-done.20 = bf16[128,768]{1,0:T(8,128)(2,1)S(1)} collective-permute-done((bf16[128,768]{1,0:T(8,128)(2,1)S(1)}, bf16[128,768]{1,0:T(8,128)(2,1)S(1)}, u32[]{:S(2)}, u32[]{:S(2)}) %collective-permute-start.20) | collective-permute-done | bytes 196640 | tf_op jit(solution)/shard_map/ppermute | solution.py:196
  77.3 1.9 %collective-permute-done.27 = bf16[128,768]{1,0:T(8,128)(2,1)S(1)} collective-permute-done((bf16[128,768]{1,0:T(8,128)(2,1)S(1)}, bf16[128,768]{1,0:T(8,128)(2,1)S(1)}, u32[]{:S(2)}, u32[]{:S(2)}) %collective-permute-start.27) | collective-permute-done | bytes 196640 | tf_op jit(solution)/shard_map/ppermute | solution.py:196
  79.5 2.4 %collective-permute-done.31 = bf16[192,768]{1,0:T(8,128)(2,1)S(1)} collective-permute-done((bf16[192,768]{1,0:T(8,128)(2,1)S(1)}, bf16[192,768]{1,0:T(8,128)(2,1)S(1)}, u32[]{:S(2)}, u32[]{:S(2)}) %collective-permute-start.31) | collective-permute-done | bytes 294944 | tf_op jit(solution)/shard_map/ppermute | solution.py:196
  82.2 3.3 %grad_label_work.1 = bf16[1024,768]{1,0:T(8,128)(2,1)} custom-call(f32[256,128]{1,0:T(8,128)S(1)} %get-tuple-element.41.refs_0_, f32[256,128]{1,0:T(8,128)S(1)} %get-tuple-element.42.refs_1_, f32[256,128]{1,0:T(8,128)S(1)} %get-tuple-element.43.refs_2_, f32[256,128]{1,0:T(8,128)S(1)} %get-tuple-element.44.refs_3_, s32[256,128]{1,0:T(8,128)S(1)} %get-tuple-element.45.refs_4_, ...), custom_call_target="tpu_custom_call" | custom-call | flops 1610612736 | bytes 4194304 | tf_op jit(solution)/shard_map/grad_label_work/pallas_call | solution.py:124
  85.4 12.8 %collective-permute-done.21 = bf16[128,768]{1,0:T(8,128)(2,1)S(1)} collective-permute-done((bf16[128,768]{1,0:T(8,128)(2,1)S(1)}, bf16[128,768]{1,0:T(8,128)(2,1)S(1)}, u32[]{:S(2)}, u32[]{:S(2)}) %collective-permute-start.21) | collective-permute-done | bytes 196640 | tf_op jit(solution)/shard_map/ppermute | solution.py:201
  99.1 3.4 %collective-permute-done.32 = bf16[192,768]{1,0:T(8,128)(2,1)S(1)} collective-permute-done((bf16[192,768]{1,0:T(8,128)(2,1)S(1)}, bf16[192,768]{1,0:T(8,128)(2,1)S(1)}, u32[]{:S(2)}, u32[]{:S(2)}) %collective-permute-start.32) | collective-permute-done | bytes 294944 | tf_op jit(solution)/shard_map/ppermute | solution.py:196
  (73 shorter events, 15.2 us)
Async XLA Ops:
  3.0 10.5 %collective-permute-start.8 = (bf16[144,768]{1,0:T(8,128)(2,1)S(1)}, bf16[144,768]{1,0:T(8,128)(2,1)S(1)}, u32[]{:S(2)}, u32[]{:S(2)}) collective-permute-start(bf16[144,768]{1,0:T(8,128)(2,1)S(1)} %pad_maximum_fusion.refs_0_), channel_id=1, source_target_pairs={{0,4},{4,8},{8,12},{12,0},{1,5},{5,9},{9,13},{13,1},{2,6},{6,10},{... | collective-permute-start | bytes 663560 | tf_op jit(solution)/shard_map/ppermute | solution.py:201
  6.1 16.6 %collective-permute-start.4 = (bf16[192,768]{1,0:T(8,128)(2,1)}, bf16[192,768]{1,0:T(8,128)(2,1)S(1)}, u32[]{:S(2)}, u32[]{:S(2)}) collective-permute-start(bf16[192,768]{1,0:T(8,128)(2,1)} %refs_4_.7), channel_id=1, source_target_pairs={{0,2},{1,3},{2,0},{3,1},{4,6},{5,7},{6,4},{7,5},{8,10},{9,11},{10,... | collective-permute-start | bytes 884744 | tf_op jit(solution)/shard_map/ppermute | solution.py:196
  7.5 11.9 %collective-permute-start.1 = (bf16[144,768]{1,0:T(8,128)(2,1)S(1)}, bf16[144,768]{1,0:T(8,128)(2,1)S(1)}, u32[]{:S(2)}, u32[]{:S(2)}) collective-permute-start(bf16[144,768]{1,0:T(8,128)(2,1)S(1)} %pad_maximum_fusion.refs_0_), channel_id=1, source_target_pairs={{0,2},{1,3},{2,0},{3,1},{4,6},{5,7},{6,4},{7,5},{8,10},{9,11},{10,... | collective-permute-start | bytes 663560 | tf_op jit(solution)/shard_map/ppermute | solution.py:196
  8.1 12.9 %collective-permute-start = (bf16[144,768]{1,0:T(8,128)(2,1)S(1)}, bf16[144,768]{1,0:T(8,128)(2,1)S(1)}, u32[]{:S(2)}, u32[]{:S(2)}) collective-permute-start(bf16[144,768]{1,0:T(8,128)(2,1)S(1)} %pad_maximum_fusion.refs_0_), channel_id=1, source_target_pairs={{0,1},{1,0},{2,3},{3,2},{4,5},{5,4},{6,7},{7,6},{8,9},{9,8},{10,11... | collective-permute-start | bytes 663560 | tf_op jit(solution)/shard_map/ppermute | solution.py:196
  13.5 9.3 %collective-permute-start.3 = (bf16[192,768]{1,0:T(8,128)(2,1)}, bf16[192,768]{1,0:T(8,128)(2,1)S(1)}, u32[]{:S(2)}, u32[]{:S(2)}) collective-permute-start(bf16[192,768]{1,0:T(8,128)(2,1)} %refs_4_.7), channel_id=1, source_target_pairs={{0,1},{1,0},{2,3},{3,2},{4,5},{5,4},{6,7},{7,6},{8,9},{9,8},{10,11... | collective-permute-start | bytes 884744 | tf_op jit(solution)/shard_map/ppermute | solution.py:196
  21.9 8.7 %collective-permute-start.22 = (bf16[144,768]{1,0:T(8,128)(2,1)S(1)}, bf16[144,768]{1,0:T(8,128)(2,1)S(1)}, u32[]{:S(2)}, u32[]{:S(2)}) collective-permute-start(bf16[144,768]{1,0:T(8,128)(2,1)S(1)} %collective-permute-done.15.refs_0_), channel_id=1, source_target_pairs={{0,4},{4,8},{8,12},{12,0},{1,5},{5,9},{9,13},{13,1},{2,6},{6,10},{... | collective-permute-start | bytes 663560 | tf_op jit(solution)/shard_map/ppermute | solution.py:201
  25.5 12.3 %collective-permute-start.9 = (bf16[144,768]{1,0:T(8,128)(2,1)S(1)}, bf16[144,768]{1,0:T(8,128)(2,1)S(1)}, u32[]{:S(2)}, u32[]{:S(2)}) collective-permute-start(bf16[144,768]{1,0:T(8,128)(2,1)S(1)} %collective-permute-done.8.refs_0_), channel_id=1, source_target_pairs={{0,1},{1,0},{2,3},{3,2},{4,5},{5,4},{6,7},{7,6},{8,9},{9,8},{10,11... | collective-permute-start | bytes 663560 | tf_op jit(solution)/shard_map/ppermute | solution.py:196
  25.5 12.5 %collective-permute-start.11 = (bf16[144,768]{1,0:T(8,128)(2,1)S(1)}, bf16[144,768]{1,0:T(8,128)(2,1)S(1)}, u32[]{:S(2)}, u32[]{:S(2)}) collective-permute-start(bf16[144,768]{1,0:T(8,128)(2,1)S(1)} %collective-permute-done.10.refs_2_), channel_id=1, source_target_pairs={{0,1},{1,0},{2,3},{3,2},{4,5},{5,4},{6,7},{7,6},{8,9},{9,8},{10,11... | collective-permute-start | bytes 663560 | tf_op jit(solution)/shard_map/ppermute | solution.py:196
  31.2 10.9 %collective-permute-start.16 = (bf16[144,768]{1,0:T(8,128)(2,1)S(1)}, bf16[144,768]{1,0:T(8,128)(2,1)S(1)}, u32[]{:S(2)}, u32[]{:S(2)}) collective-permute-start(bf16[144,768]{1,0:T(8,128)(2,1)S(1)} %collective-permute-done.15.refs_0_), channel_id=1, source_target_pairs={{0,1},{1,0},{2,3},{3,2},{4,5},{5,4},{6,7},{7,6},{8,9},{9,8},{10,11... | collective-permute-start | bytes 663560 | tf_op jit(solution)/shard_map/ppermute | solution.py:196
  31.3 11.3 %collective-permute-start.18 = (bf16[144,768]{1,0:T(8,128)(2,1)S(1)}, bf16[144,768]{1,0:T(8,128)(2,1)S(1)}, u32[]{:S(2)}, u32[]{:S(2)}) collective-permute-start(bf16[144,768]{1,0:T(8,128)(2,1)S(1)} %collective-permute-done.17.refs_2_), channel_id=1, source_target_pairs={{0,1},{1,0},{2,3},{3,2},{4,5},{5,4},{6,7},{7,6},{8,9},{9,8},{10,11... | collective-permute-start | bytes 663560 | tf_op jit(solution)/shard_map/ppermute | solution.py:196
  37.8 16.5 %collective-permute-start.6 = (bf16[2,128,768]{2,1,0:T(8,128)(2,1)S(1)}, bf16[2,128,768]{2,1,0:T(8,128)(2,1)S(1)}, u32[]{:S(2)}, u32[]{:S(2)}) collective-permute-start(bf16[2,128,768]{2,1,0:T(8,128)(2,1)S(1)} %get-tuple-element.34), channel_id=1, source_target_pairs={{0,1},{1,0},{2,3},{3,2},{4,5},{5,4},{6,7},{7,6},{8,9},{9,8},{10,11... | collective-permute-start | bytes 1179656 | tf_op jit(solution)/shard_map/ppermute | solution.py:196
  42.1 10.5 %collective-permute-start.12 = (bf16[2,128,768]{2,1,0:T(8,128)(2,1)S(1)}, bf16[2,128,768]{2,1,0:T(8,128)(2,1)S(1)}, u32[]{:S(2)}, u32[]{:S(2)}) collective-permute-start(bf16[2,128,768]{2,1,0:T(8,128)(2,1)S(1)} %get-tuple-element.36), channel_id=1, source_target_pairs={{0,1},{1,0},{2,3},{3,2},{4,5},{5,4},{6,7},{7,6},{8,9},{9,8},{10,11... | collective-permute-start | bytes 1179656 | tf_op jit(solution)/shard_map/ppermute | solution.py:196
  46.2 18.4 %collective-permute-start.19 = (bf16[2,128,768]{2,1,0:T(8,128)(2,1)S(1)}, bf16[2,128,768]{2,1,0:T(8,128)(2,1)S(1)}, u32[]{:S(2)}, u32[]{:S(2)}) collective-permute-start(bf16[2,128,768]{2,1,0:T(8,128)(2,1)S(1)} %get-tuple-element.38), channel_id=1, source_target_pairs={{0,1},{1,0},{2,3},{3,2},{4,5},{5,4},{6,7},{7,6},{8,9},{9,8},{10,11... | collective-permute-start | bytes 1179656 | tf_op jit(solution)/shard_map/ppermute | solution.py:196
  52.2 10.6 %collective-permute-start.29 = (bf16[2,192,768]{2,1,0:T(8,128)(2,1)S(1)}, bf16[2,192,768]{2,1,0:T(8,128)(2,1)S(1)}, u32[]{:S(2)}, u32[]{:S(2)}) collective-permute-start(bf16[2,192,768]{2,1,0:T(8,128)(2,1)S(1)} %get-tuple-element.62), channel_id=1, source_target_pairs={{0,1},{1,0},{2,3},{3,2},{4,5},{5,4},{6,7},{7,6},{8,9},{9,8},{10,11... | collective-permute-start | bytes 1769480 | tf_op jit(solution)/shard_map/ppermute | solution.py:196
  54.4 31.1 %collective-permute-start.7 = (bf16[128,768]{1,0:T(8,128)(2,1)S(1)}, bf16[128,768]{1,0:T(8,128)(2,1)S(1)}, u32[]{:S(2)}, u32[]{:S(2)}) collective-permute-start(bf16[128,768]{1,0:T(8,128)(2,1)S(1)} %fusion.9), channel_id=1, source_target_pairs={{0,2},{1,3},{2,0},{3,1},{4,6},{5,7},{6,4},{7,5},{8,10},{9,11},{10,... | collective-permute-start | bytes 589832 | tf_op jit(solution)/shard_map/ppermute | solution.py:196
  54.9 10.2 %collective-permute-start.26 = (bf16[2,128,768]{2,1,0:T(8,128)(2,1)S(1)}, bf16[2,128,768]{2,1,0:T(8,128)(2,1)S(1)}, u32[]{:S(2)}, u32[]{:S(2)}) collective-permute-start(bf16[2,128,768]{2,1,0:T(8,128)(2,1)S(1)} %get-tuple-element.40), channel_id=1, source_target_pairs={{0,1},{1,0},{2,3},{3,2},{4,5},{5,4},{6,7},{7,6},{8,9},{9,8},{10,11... | collective-permute-start | bytes 1179656 | tf_op jit(solution)/shard_map/ppermute | solution.py:196
  60.6 24.8 %collective-permute-start.14 = (bf16[128,768]{1,0:T(8,128)(2,1)S(1)}, bf16[128,768]{1,0:T(8,128)(2,1)S(1)}, u32[]{:S(2)}, u32[]{:S(2)}) collective-permute-start(bf16[128,768]{1,0:T(8,128)(2,1)S(1)} %fusion.3), channel_id=1, source_target_pairs={{0,12},{4,0},{8,4},{12,8},{1,13},{5,1},{9,5},{13,9},{2,14},{6,2},{... | collective-permute-start | bytes 589832 | tf_op jit(solution)/shard_map/ppermute | solution.py:201
  62.9 10.0 %collective-permute-start.30 = (bf16[192,768]{1,0:T(8,128)(2,1)S(1)}, bf16[192,768]{1,0:T(8,128)(2,1)S(1)}, u32[]{:S(2)}, u32[]{:S(2)}) collective-permute-start(bf16[192,768]{1,0:T(8,128)(2,1)S(1)} %fusion.8), channel_id=1, source_target_pairs={{0,2},{1,3},{2,0},{3,1},{4,6},{5,7},{6,4},{7,5},{8,10},{9,11},{10,... | collective-permute-start | bytes 884744 | tf_op jit(solution)/shard_map/ppermute | solution.py:196
  64.7 12.4 %collective-permute-start.20 = (bf16[128,768]{1,0:T(8,128)(2,1)S(1)}, bf16[128,768]{1,0:T(8,128)(2,1)S(1)}, u32[]{:S(2)}, u32[]{:S(2)}) collective-permute-start(bf16[128,768]{1,0:T(8,128)(2,1)S(1)} %fusion.11), channel_id=1, source_target_pairs={{0,2},{1,3},{2,0},{3,1},{4,6},{5,7},{6,4},{7,5},{8,10},{9,11},{10,... | collective-permute-start | bytes 589832 | tf_op jit(solution)/shard_map/ppermute | solution.py:196
  65.2 14.0 %collective-permute-start.27 = (bf16[128,768]{1,0:T(8,128)(2,1)S(1)}, bf16[128,768]{1,0:T(8,128)(2,1)S(1)}, u32[]{:S(2)}, u32[]{:S(2)}) collective-permute-start(bf16[128,768]{1,0:T(8,128)(2,1)S(1)} %fusion.12), channel_id=1, source_target_pairs={{0,2},{1,3},{2,0},{3,1},{4,6},{5,7},{6,4},{7,5},{8,10},{9,11},{10,... | collective-permute-start | bytes 589832 | tf_op jit(solution)/shard_map/ppermute | solution.py:196
  73.0 8.9 %collective-permute-start.31 = (bf16[192,768]{1,0:T(8,128)(2,1)S(1)}, bf16[192,768]{1,0:T(8,128)(2,1)S(1)}, u32[]{:S(2)}, u32[]{:S(2)}) collective-permute-start(bf16[192,768]{1,0:T(8,128)(2,1)S(1)} %fusion.22), channel_id=1, source_target_pairs={{0,4},{4,0},{8,12},{12,8},{1,5},{5,1},{9,13},{13,9},{2,6},{6,2},{1... | collective-permute-start | bytes 884744 | tf_op jit(solution)/shard_map/ppermute | solution.py:196
  77.2 21.0 %collective-permute-start.21 = (bf16[128,768]{1,0:T(8,128)(2,1)S(1)}, bf16[128,768]{1,0:T(8,128)(2,1)S(1)}, u32[]{:S(2)}, u32[]{:S(2)}) collective-permute-start(bf16[128,768]{1,0:T(8,128)(2,1)S(1)} %fusion.2), channel_id=1, source_target_pairs={{0,8},{4,12},{8,0},{12,4},{1,9},{5,13},{9,1},{13,5},{2,10},{6,14},... | collective-permute-start | bytes 589832 | tf_op jit(solution)/shard_map/ppermute | solution.py:201
  79.3 18.9 %collective-permute-start.28 = (bf16[128,768]{1,0:T(8,128)(2,1)S(1)}, bf16[128,768]{1,0:T(8,128)(2,1)S(1)}, u32[]{:S(2)}, u32[]{:S(2)}) collective-permute-start(bf16[128,768]{1,0:T(8,128)(2,1)S(1)} %fusion.1), channel_id=1, source_target_pairs={{0,4},{4,8},{8,12},{12,0},{1,5},{5,9},{9,13},{13,1},{2,6},{6,10},{... | collective-permute-start | bytes 589832 | tf_op jit(solution)/shard_map/ppermute | solution.py:201
  82.1 20.4 %collective-permute-start.32 = (bf16[192,768]{1,0:T(8,128)(2,1)S(1)}, bf16[192,768]{1,0:T(8,128)(2,1)S(1)}, u32[]{:S(2)}, u32[]{:S(2)}) collective-permute-start(bf16[192,768]{1,0:T(8,128)(2,1)S(1)} %fusion), channel_id=1, source_target_pairs={{0,8},{4,12},{8,0},{12,4},{1,9},{5,13},{9,1},{13,5},{2,10},{6,14},... | collective-permute-start | bytes 884744 | tf_op jit(solution)/shard_map/ppermute | solution.py:196
  (13 other events, 79.0 us)

commit v4 on v3

--- a/solution.py
+++ b/solution.py
@@ -9,7 +9,7 @@
 
 BLK = 128
 EPSILON = 1e-06
-META_ROWS = 16
+META_ROWS = 8
 F32 = jnp.float32
 BF16 = jnp.bfloat16
 
@@ -205,10 +205,17 @@
     return [1 << i for i in range(n.bit_length() - 1)]
 
 
-def gather_dp(x):
+def after(x, *others):
+    return lax.optimization_barrier((x, *others))[0]
+
+
+def gather_dp(x, first=None):
     got = {0: x}
     for mask in reversed(masks(lax.axis_size("dp"))):
-        got.update({m | mask: partner(v, "dp", mask) for m, v in list(got.items())})
+        for m, v in list(got.items()):
+            if first is not None and mask == 1 and m:
+                v = after(v, first)
+            got[m | mask] = partner(v, "dp", mask)
     return [got[m] for m in range(len(got))]
 
 
@@ -224,6 +231,18 @@
             if i & mask == 0 and i % mask == 0:
                 terms[i].append(partner(add(*terms[i | mask]).astype(BF16), "dp", 2 * mask))
     return add(*terms[0])
+
+
+def sum_labels(x):
+    half = x.shape[0] // 2
+    odd = lax.axis_index("labels") & 1
+    cut = lambda p: lax.dynamic_slice_in_dim(x, p * half, half, 0)
+    x = add(cut(odd), partner(cut(1 - odd).astype(BF16), "labels", 1)).astype(BF16)
+    for mask in masks(lax.axis_size("labels"))[1:]:
+        x = add(x, partner(x, "labels", mask)).astype(BF16)
+    other = partner(x, "labels", 1)
+    low, high = jnp.where(odd == 0, x, other), jnp.where(odd == 0, other, x)
+    return jnp.concatenate([low, high], axis=0).astype(F32)
 
 
 def with_meta(feats, owner_rows, block_rows, positive_rows):
@@ -245,15 +264,15 @@
 
     if row_count <= n_data * cap:
         own = with_meta(feats, owners.T, blocks.T, positives.T)
-        runs = []
-        block = own
+        rows_of = [own]
+        for _ in range(1, n_labels):
+            rows_of.append(shifted(rows_of[-1], "labels", 1))
+        work = []
         for by in range(n_labels):
-            if by:
-                block = shifted(block, "labels", 1)
-            runs.append(gather_dp(block))
-        work = [
-            pair_work(where, sources, shards, label_weight, cap, pick_count) for sources in runs
-        ]
+            run = gather_dp(rows_of[by], work[-1][0] if work else None)
+            if by + 2 < n_labels:
+                run[0] = after(run[0], rows_of[by + 2])
+            work.append(pair_work(where, run, shards, label_weight, cap, pick_count))
         total = []
         for by in range(n_labels):
             part = reduce_dp(work[by][0], work[by][1])
@@ -292,10 +311,10 @@
 
     _, _, grad_scores, block_of, embedding, picked, grad_hidden = zip(*work)
     even, odd = enc_work(where, picked, grad_hidden, enc_weight, n_data)
+    share = reduce_dp(even, odd)
+    embedding = (after(embedding[0], share),) + embedding[1:]
     grad_label = grad_label_work(grad_scores, block_of, embedding, label_weight)
-    grad_enc = reduce_dp(even, odd)
-    for mask in masks(n_labels):
-        grad_enc = add(grad_enc, partner(grad_enc.astype(BF16), "labels", mask))
+    grad_enc = sum_labels(share)
     return (grad_feats, grad_label, grad_enc)
 
 

time: 104 us -> 109 us (1.048)
  local copies, waits for them, and re-layouts: 2.38 us -> 15.6 us
  waiting for transfers between devices: 55.3 us -> 42.7 us
  other arithmetic: 5 us -> 6.66 us
  starting transfers between devices: 20 us -> 21.3 us
  Pallas kernels: 19.9 us -> 21.1 us
    unnamed x8 -> x74, local copies, waits for them, and re-layouts: 2.38 us -> 15.6 us
    ppermute x6, waiting for transfers between devices: 23.8 us -> 15.7 us  [shifted(): return lax.ppermute(x, axis, [(i, (i + by) % n) for i in range(n)])]
    ppermute x27 -> x28, waiting for transfers between devices: 31.5 us -> 27 us  [partner(): lax.ppermute(x, axis, [(i, i ^ mask) for i in range(lax.axis_size(axis))])]
    ppermute x27 -> x28, starting transfers between devices: 13.8 us -> 15.8 us  [partner(): lax.ppermute(x, axis, [(i, i ^ mask) for i in range(lax.axis_size(axis))])]
    pallas_call x6, Pallas kernels: 19.9 us -> 21.1 us  [call(): pl.pallas_call(kernel, in_specs=[smem if a.ndim == 1 else vmem for a in a...]
  transfers between devices with their start and end apart: 33 -> 34, of which waited for: 12 -> 12; matrix products, arithmetic and copies ran while one was open for 2% -> 5% of each run, Pallas kernels for 19% -> 19%
where the time goes in v4:
time: 109 us
  waiting for transfers between devices  42.7 us (39%)
  starting transfers between devices  21.3 us (20%)
  Pallas kernels  21.1 us (19%)
  local copies, waits for them, and re-layouts  15.6 us (14%)
  other arithmetic  6.66 us (6%)
  between operations  1.17 us (1%)
    ppermute x28, waiting for transfers between devices, partner(): lax.ppermute(x, axis, [(i, i ^ mask) for i in range(lax.axis_size(axis))])  27 us
    pallas_call x6, Pallas kernels, call(): pl.pallas_call(kernel, in_specs=[smem if a.ndim == 1 else vmem for a in a...  21.1 us
    ppermute x28, starting transfers between devices, partner(): lax.ppermute(x, axis, [(i, i ^ mask) for i in range(lax.axis_size(axis))])  15.8 us
    ppermute x6, waiting for transfers between devices, shifted(): return lax.ppermute(x, axis, [(i, (i + by) % n) for i in range(n)])  15.7 us
    unnamed x74, local copies, waits for them, and re-layouts  15.6 us
    ppermute x6, starting transfers between devices, shifted(): return lax.ppermute(x, axis, [(i, (i + by) % n) for i in range(n)])  5.52 us
  transfers between devices with their start and end apart: 34, of which 12 were waited for; matrix products, arithmetic and copies ran while one was open for 5% of the time, Pallas kernels for 19%

profile of v4, /device:TPU:0, one launch (start us, length us, event | category | flops | bytes accessed | tf_op | source)
XLA Modules:
  0.0 108.6 jit_solution(492757391974805464)
XLA Ops:
  0.6 3.0 %collective-permute-start.6 = (bf16[192,768]{1,0:T(8,128)(2,1)}, bf16[192,768]{1,0:T(8,128)(2,1)S(1)}, u32[]{:S(2)}, u32[]{:S(2)}) collective-permute-start(bf16[192,768]{1,0:T(8,128)(2,1)} %refs_4_.7), channel_id=1, source_target_pairs={{0,2},{1,3},{2,0},{3,1},{4,6},{5,7},{6,4},{7,5},{8,10},{9,11},{10,... | collective-permute-start | bytes 884744 | tf_op jit(solution)/shard_map/ppermute | solution.py:196
  6.0 1.6 %collective-permute-start = (bf16[136,768]{1,0:T(8,128)(2,1)S(1)}, bf16[136,768]{1,0:T(8,128)(2,1)S(1)}, u32[]{:S(2)}, u32[]{:S(2)}) collective-permute-start(bf16[136,768]{1,0:T(8,128)(2,1)S(1)} %pad_maximum_fusion.refs_0_), channel_id=1, source_target_pairs={{0,4},{4,8},{8,12},{12,0},{1,5},{5,9},{9,13},{13,1},{2,6},{6,10},{... | collective-permute-start | bytes 626696 | tf_op jit(solution)/shard_map/ppermute | solution.py:201
  8.1 6.4 %collective-permute-done.refs_0_ = bf16[136,768]{1,0:T(8,128)(2,1)S(1)} collective-permute-done((bf16[136,768]{1,0:T(8,128)(2,1)S(1)}, bf16[136,768]{1,0:T(8,128)(2,1)S(1)}, u32[]{:S(2)}, u32[]{:S(2)}) %collective-permute-start) | collective-permute-done | bytes 208928 | tf_op jit(solution)/shard_map/ppermute | solution.py:201
  15.6 6.7 %collective-permute-done.1.refs_0_ = bf16[136,768]{1,0:T(8,128)(2,1)} collective-permute-done((bf16[136,768]{1,0:T(8,128)(2,1)S(1)}, bf16[136,768]{1,0:T(8,128)(2,1)}, u32[]{:S(2)}, u32[]{:S(2)}) %collective-permute-start.1) | collective-permute-done | bytes 208928 | tf_op jit(solution)/shard_map/ppermute | solution.py:201
  23.2 1.4 %copy-done = bf16[1024,768]{1,0:T(8,128)(2,1)S(1)} copy-done((bf16[1024,768]{1,0:T(8,128)(2,1)S(1)}, bf16[1024,768]{1,0:T(8,128)(2,1)}, u32[]{:S(2)}) %copy-start) | copy-done | bytes 1572888
  25.6 3.6 %pair_work.4 = (bf16[2,128,768]{2,1,0:T(8,128)(2,1)S(1)}, bf16[2,128,768]{2,1,0:T(8,128)(2,1)S(1)}, f32[256,128]{1,0:T(8,128)S(1)}, s32[256,128]{1,0:T(8,128)S(1...) custom-call(s32[2]{0:T(128)S(1)} %pad_add_fusion.where_ref, ...), custom_call_target="tpu_custom_call" | custom-call | flops 1509949440 | bytes 8388608 | tf_op jit(solution)/shard_map/pair_work/pallas_call | solution.py:124
  32.7 1.3 %collective-permute-start.18 = (bf16[136,768]{1,0:T(8,128)(2,1)}, bf16[136,768]{1,0:T(8,128)(2,1)}, u32[]{:S(2)}, u32[]{:S(2)}) collective-permute-start(bf16[136,768]{1,0:T(8,128)(2,1)} %collective-permute-done.1.refs_0_), channel_id=1, source_target_pairs={{0,2},{1,3},{2,0},{3,1},{4,6},{5,7},{6,4},{7,5},{8,10},{9,11},{10,... | collective-permute-start | bytes 626696 | tf_op jit(solution)/shard_map/ppermute | solution.py:196
  37.8 3.6 %pair_work.5 = (bf16[2,128,768]{2,1,0:T(8,128)(2,1)S(1)}, bf16[2,128,768]{2,1,0:T(8,128)(2,1)S(1)}, f32[256,128]{1,0:T(8,128)S(1)}, s32[256,128]{1,0:T(8,128)S(1...) custom-call(s32[2]{0:T(128)S(1)} %pad_add_fusion.where_ref, ...), custom_call_target="tpu_custom_call" | custom-call | flops 1509949440 | bytes 8388608 | tf_op jit(solution)/shard_map/pair_work/pallas_call | solution.py:124
  45.8 1.3 %collective-permute-start.24 = (bf16[136,768]{1,0:T(8,128)(2,1)}, bf16[136,768]{1,0:T(8,128)(2,1)}, u32[]{:S(2)}, u32[]{:S(2)}) collective-permute-start(bf16[136,768]{1,0:T(8,128)(2,1)} %collective-permute-done.10.refs_0_), channel_id=1, source_target_pairs={{0,2},{1,3},{2,0},{3,1},{4,6},{5,7},{6,4},{7,5},{8,10},{9,11},{10,... | collective-permute-start | bytes 626696 | tf_op jit(solution)/shard_map/ppermute | solution.py:196
  50.6 4.4 %pair_work.6 = (bf16[2,128,768]{2,1,0:T(8,128)(2,1)S(1)}, bf16[2,128,768]{2,1,0:T(8,128)(2,1)S(1)}, f32[256,128]{1,0:T(8,128)S(1)}, s32[256,128]{1,0:T(8,128)S(1...) custom-call(s32[2]{0:T(128)S(1)} %pad_add_fusion.where_ref, ...), custom_call_target="tpu_custom_call" | custom-call | flops 1509949440 | bytes 8388608 | tf_op jit(solution)/shard_map/pair_work/pallas_call | solution.py:124
  56.6 1.2 %collective-permute-start.15 = (bf16[128,768]{1,0:T(8,128)(2,1)S(1)}, bf16[128,768]{1,0:T(8,128)(2,1)S(1)}, u32[]{:S(2)}, u32[]{:S(2)}) collective-permute-start(bf16[128,768]{1,0:T(8,128)(2,1)S(1)} %fusion.9), channel_id=1, source_target_pairs={{0,2},{1,3},{2,0},{3,1},{4,6},{5,7},{6,4},{7,5},{8,10},{9,11},{10,... | collective-permute-start | bytes 589832 | tf_op jit(solution)/shard_map/ppermute | solution.py:196
  57.8 4.1 %pair_work.7 = (bf16[2,128,768]{2,1,0:T(8,128)(2,1)S(1)}, bf16[2,128,768]{2,1,0:T(8,128)(2,1)S(1)}, f32[256,128]{1,0:T(8,128)S(1)}, s32[256,128]{1,0:T(8,128)S(1...) custom-call(s32[2]{0:T(128)S(1)} %pad_add_fusion.where_ref, ...), custom_call_target="tpu_custom_call" | custom-call | flops 1509949440 | bytes 8388608 | tf_op jit(solution)/shard_map/pair_work/pallas_call | solution.py:124
  62.0 2.1 %enc_work.1 = (bf16[2,192,768]{2,1,0:T(8,128)(2,1)S(1)}, bf16[2,192,768]{2,1,0:T(8,128)(2,1)S(1)}) custom-call(s32[2]{0:T(128)S(1)} %pad_add_fusion.where_ref, bf16[256,768]{1,0:T(8,128)(2,1)S(1)} %copy-done.18, bf16[256,768]{1,0:T(8,128)(2,1)S(1)} %copy-done.22, bf16[256,768]{1,0:T(8,128)(2,1)S(1)} %get-tuple-element.63.refs_2_, ...), custom_call_target="tpu_custom_call" | custom-call | flops 1207959552 | bytes 4194304 | tf_op jit(solution)/shard_map/enc_work/pallas_call | solution.py:124
  66.4 3.7 %collective-permute-start.16 = (bf16[128,768]{1,0:T(8,128)(2,1)S(1)}, bf16[128,768]{1,0:T(8,128)(2,1)S(1)}, u32[]{:S(2)}, u32[]{:S(2)}) collective-permute-start(bf16[128,768]{1,0:T(8,128)(2,1)S(1)} %fusion.2), channel_id=1, source_target_pairs={{0,12},{4,0},{8,4},{12,8},{1,13},{5,1},{9,5},{13,9},{2,14},{6,2},{... | collective-permute-start | bytes 589832 | tf_op jit(solution)/shard_map/ppermute | solution.py:201
  70.1 1.3 %collective-permute-start.21 = (bf16[128,768]{1,0:T(8,128)(2,1)S(1)}, bf16[128,768]{1,0:T(8,128)(2,1)S(1)}, u32[]{:S(2)}, u32[]{:S(2)}) collective-permute-start(bf16[128,768]{1,0:T(8,128)(2,1)S(1)} %fusion.10), channel_id=1, source_target_pairs={{0,2},{1,3},{2,0},{3,1},{4,6},{5,7},{6,4},{7,5},{8,10},{9,11},{10,... | collective-permute-start | bytes 589832 | tf_op jit(solution)/shard_map/ppermute | solution.py:196
  72.4 5.6 %collective-permute-done.21 = bf16[128,768]{1,0:T(8,128)(2,1)S(1)} collective-permute-done((bf16[128,768]{1,0:T(8,128)(2,1)S(1)}, bf16[128,768]{1,0:T(8,128)(2,1)S(1)}, u32[]{:S(2)}, u32[]{:S(2)}) %collective-permute-start.21) | collective-permute-done | bytes 196640 | tf_op jit(solution)/shard_map/ppermute | solution.py:196
  78.2 1.3 %collective-permute-start.27 = (bf16[128,768]{1,0:T(8,128)(2,1)S(1)}, bf16[128,768]{1,0:T(8,128)(2,1)S(1)}, u32[]{:S(2)}, u32[]{:S(2)}) collective-permute-start(bf16[128,768]{1,0:T(8,128)(2,1)S(1)} %fusion.11), channel_id=1, source_target_pairs={{0,2},{1,3},{2,0},{3,1},{4,6},{5,7},{6,4},{7,5},{8,10},{9,11},{10,... | collective-permute-start | bytes 589832 | tf_op jit(solution)/shard_map/ppermute | solution.py:196
  79.5 4.8 %collective-permute-done.30 = bf16[192,768]{1,0:T(8,128)(2,1)S(1)} collective-permute-done((bf16[192,768]{1,0:T(8,128)(2,1)S(1)}, bf16[192,768]{1,0:T(8,128)(2,1)S(1)}, u32[]{:S(2)}, u32[]{:S(2)}) %collective-permute-start.30) | collective-permute-done | bytes 294944 | tf_op jit(solution)/shard_map/ppermute | solution.py:196
  84.6 3.0 %collective-permute-done.27 = bf16[128,768]{1,0:T(8,128)(2,1)S(1)} collective-permute-done((bf16[128,768]{1,0:T(8,128)(2,1)S(1)}, bf16[128,768]{1,0:T(8,128)(2,1)S(1)}, u32[]{:S(2)}, u32[]{:S(2)}) %collective-permute-start.27) | collective-permute-done | bytes 196640 | tf_op jit(solution)/shard_map/ppermute | solution.py:196
  87.7 6.6 %collective-permute-done.31 = bf16[96,768]{1,0:T(8,128)(2,1)S(1)} collective-permute-done((bf16[96,768]{1,0:T(8,128)(2,1)S(1)}, bf16[96,768]{1,0:T(8,128)(2,1)S(1)}, u32[]{:S(2)}, u32[]{:S(2)}) %collective-permute-start.31) | collective-permute-done | bytes 147488 | tf_op jit(solution)/shard_map/ppermute | solution.py:196
  94.4 2.7 %collective-permute-done.28 = bf16[128,768]{1,0:T(8,128)(2,1)S(1)} collective-permute-done((bf16[128,768]{1,0:T(8,128)(2,1)S(1)}, bf16[128,768]{1,0:T(8,128)(2,1)S(1)}, u32[]{:S(2)}, u32[]{:S(2)}) %collective-permute-start.28) | collective-permute-done | bytes 196640 | tf_op jit(solution)/shard_map/ppermute | solution.py:201
  97.9 3.9 %collective-permute-done.32 = bf16[96,768]{1,0:T(8,128)(2,1)S(1)} collective-permute-done((bf16[96,768]{1,0:T(8,128)(2,1)S(1)}, bf16[96,768]{1,0:T(8,128)(2,1)S(1)}, u32[]{:S(2)}, u32[]{:S(2)}) %collective-permute-start.32) | collective-permute-done | bytes 147488 | tf_op jit(solution)/shard_map/ppermute | solution.py:196
  102.0 3.2 %grad_label_work.1 = bf16[1024,768]{1,0:T(8,128)(2,1)} custom-call(f32[256,128]{1,0:T(8,128)S(1)} %copy-done.30, f32[256,128]{1,0:T(8,128)S(1)} %copy-done.34, f32[256,128]{1,0:T(8,128)S(1)} %get-tuple-element.54.refs_2_, f32[256,128]{1,0:T(8,128)S(1)} %get-tuple-element.55.refs_3_, s32[256,128]{1,0:T(8,128)S(1)} %copy-done.32, s32[256,128]{1,0:T(8,128)S(1)} %copy-done.36, ...), custom_call_target="tpu_custom_call" | custom-call | flops 1610612736 | bytes 4194304 | tf_op jit(solution)/shard_map/grad_label_work/pallas_call | solution.py:124
  105.3 2.4 %collective-permute-done.33 = bf16[96,768]{1,0:T(8,128)(2,1)S(1)} collective-permute-done((bf16[96,768]{1,0:T(8,128)(2,1)S(1)}, bf16[96,768]{1,0:T(8,128)(2,1)S(1)}, u32[]{:S(2)}, u32[]{:S(2)}) %collective-permute-start.33) | collective-permute-done | bytes 147488 | tf_op jit(solution)/shard_map/ppermute | solution.py:196
  (144 shorter events, 28.2 us)
Async XLA Ops:
  0.6 13.9 %collective-permute-start.6 = (bf16[192,768]{1,0:T(8,128)(2,1)}, bf16[192,768]{1,0:T(8,128)(2,1)S(1)}, u32[]{:S(2)}, u32[]{:S(2)}) collective-permute-start(bf16[192,768]{1,0:T(8,128)(2,1)} %refs_4_.7), channel_id=1, source_target_pairs={{0,2},{1,3},{2,0},{3,1},{4,6},{5,7},{6,4},{7,5},{8,10},{9,11},{10,... | collective-permute-start | bytes 884744 | tf_op jit(solution)/shard_map/ppermute | solution.py:196
  6.0 8.5 %collective-permute-start = (bf16[136,768]{1,0:T(8,128)(2,1)S(1)}, bf16[136,768]{1,0:T(8,128)(2,1)S(1)}, u32[]{:S(2)}, u32[]{:S(2)}) collective-permute-start(bf16[136,768]{1,0:T(8,128)(2,1)S(1)} %pad_maximum_fusion.refs_0_), channel_id=1, source_target_pairs={{0,4},{4,8},{8,12},{12,0},{1,5},{5,9},{9,13},{13,1},{2,6},{6,10},{... | collective-permute-start | bytes 626696 | tf_op jit(solution)/shard_map/ppermute | solution.py:201
  14.5 8.6 %collective-permute-start.5 = (bf16[192,768]{1,0:T(8,128)(2,1)}, bf16[192,768]{1,0:T(8,128)(2,1)S(1)}, u32[]{:S(2)}, u32[]{:S(2)}) collective-permute-start(bf16[192,768]{1,0:T(8,128)(2,1)} %refs_4_.7), channel_id=1, source_target_pairs={{0,1},{1,0},{2,3},{3,2},{4,5},{5,4},{6,7},{7,6},{8,9},{9,8},{10,11... | collective-permute-start | bytes 884744 | tf_op jit(solution)/shard_map/ppermute | solution.py:196
  14.5 8.6 %collective-permute-start.7 = (bf16[192,768]{1,0:T(8,128)(2,1)S(1)}, bf16[192,768]{1,0:T(8,128)(2,1)S(1)}, u32[]{:S(2)}, u32[]{:S(2)}) collective-permute-start(bf16[192,768]{1,0:T(8,128)(2,1)S(1)} %collective-permute-done.6.refs_6_), channel_id=1, source_target_pairs={{0,1},{1,0},{2,3},{3,2},{4,5},{5,4},{6,7},{7,6},{8,9},{9,8},{10,11... | collective-permute-start | bytes 884744 | tf_op jit(solution)/shard_map/ppermute | solution.py:196
  15.0 8.0 %collective-permute-start.2 = (bf16[136,768]{1,0:T(8,128)(2,1)S(1)}, bf16[136,768]{1,0:T(8,128)(2,1)S(1)}, u32[]{:S(2)}, u32[]{:S(2)}) collective-permute-start(bf16[136,768]{1,0:T(8,128)(2,1)S(1)} %pad_maximum_fusion.refs_0_), channel_id=1, source_target_pairs={{0,1},{1,0},{2,3},{3,2},{4,5},{5,4},{6,7},{7,6},{8,9},{9,8},{10,11... | collective-permute-start | bytes 626696 | tf_op jit(solution)/shard_map/ppermute | solution.py:196
  15.3 7.8 %collective-permute-start.4 = (bf16[136,768]{1,0:T(8,128)(2,1)S(1)}, bf16[136,768]{1,0:T(8,128)(2,1)S(1)}, u32[]{:S(2)}, u32[]{:S(2)}) collective-permute-start(bf16[136,768]{1,0:T(8,128)(2,1)S(1)} %collective-permute-done.3.refs_2_), channel_id=1, source_target_pairs={{0,1},{1,0},{2,3},{3,2},{4,5},{5,4},{6,7},{7,6},{8,9},{9,8},{10,11... | collective-permute-start | bytes 626696 | tf_op jit(solution)/shard_map/ppermute | solution.py:196
  22.2 9.9 %collective-permute-start.12 = (bf16[136,768]{1,0:T(8,128)(2,1)S(1)}, bf16[136,768]{1,0:T(8,128)(2,1)S(1)}, u32[]{:S(2)}, u32[]{:S(2)}) collective-permute-start(bf16[136,768]{1,0:T(8,128)(2,1)S(1)} %collective-permute-done.refs_0_), channel_id=1, source_target_pairs={{0,2},{1,3},{2,0},{3,1},{4,6},{5,7},{6,4},{7,5},{8,10},{9,11},{10,... | collective-permute-start | bytes 626696 | tf_op jit(solution)/shard_map/ppermute | solution.py:196
  23.1 10.9 %collective-permute-start.11 = (bf16[136,768]{1,0:T(8,128)(2,1)S(1)}, bf16[136,768]{1,0:T(8,128)(2,1)S(1)}, u32[]{:S(2)}, u32[]{:S(2)}) collective-permute-start(bf16[136,768]{1,0:T(8,128)(2,1)S(1)} %collective-permute-done.refs_0_), channel_id=1, source_target_pairs={{0,1},{1,0},{2,3},{3,2},{4,5},{5,4},{6,7},{7,6},{8,9},{9,8},{10,11... | collective-permute-start | bytes 626696 | tf_op jit(solution)/shard_map/ppermute | solution.py:196
  23.1 10.9 %collective-permute-start.10 = (bf16[136,768]{1,0:T(8,128)(2,1)}, bf16[136,768]{1,0:T(8,128)(2,1)}, u32[]{:S(2)}, u32[]{:S(2)}) collective-permute-start(bf16[136,768]{1,0:T(8,128)(2,1)} %collective-permute-done.1.refs_0_), channel_id=1, source_target_pairs={{0,4},{4,8},{8,12},{12,0},{1,5},{5,9},{9,13},{13,1},{2,6},{6,10},{... | collective-permute-start | bytes 626696 | tf_op jit(solution)/shard_map/ppermute | solution.py:201
  32.7 12.8 %collective-permute-start.18 = (bf16[136,768]{1,0:T(8,128)(2,1)}, bf16[136,768]{1,0:T(8,128)(2,1)}, u32[]{:S(2)}, u32[]{:S(2)}) collective-permute-start(bf16[136,768]{1,0:T(8,128)(2,1)} %collective-permute-done.1.refs_0_), channel_id=1, source_target_pairs={{0,2},{1,3},{2,0},{3,1},{4,6},{5,7},{6,4},{7,5},{8,10},{9,11},{10,... | collective-permute-start | bytes 626696 | tf_op jit(solution)/shard_map/ppermute | solution.py:196
  45.0 10.5 %collective-permute-start.14 = (bf16[2,128,768]{2,1,0:T(8,128)(2,1)S(1)}, bf16[2,128,768]{2,1,0:T(8,128)(2,1)}, u32[]{:S(2)}, u32[]{:S(2)}) collective-permute-start(bf16[2,128,768]{2,1,0:T(8,128)(2,1)S(1)} %get-tuple-element.45), channel_id=1, source_target_pairs={{0,1},{1,0},{2,3},{3,2},{4,5},{5,4},{6,7},{7,6},{8,9},{9,8},{10,11... | collective-permute-start | bytes 1179656 | tf_op jit(solution)/shard_map/ppermute | solution.py:196
  45.8 9.2 %collective-permute-start.24 = (bf16[136,768]{1,0:T(8,128)(2,1)}, bf16[136,768]{1,0:T(8,128)(2,1)}, u32[]{:S(2)}, u32[]{:S(2)}) collective-permute-start(bf16[136,768]{1,0:T(8,128)(2,1)} %collective-permute-done.10.refs_0_), channel_id=1, source_target_pairs={{0,2},{1,3},{2,0},{3,1},{4,6},{5,7},{6,4},{7,5},{8,10},{9,11},{10,... | collective-permute-start | bytes 626696 | tf_op jit(solution)/shard_map/ppermute | solution.py:196
  47.0 17.2 %collective-permute-start.8 = (bf16[2,128,768]{2,1,0:T(8,128)(2,1)S(1)}, bf16[2,128,768]{2,1,0:T(8,128)(2,1)S(1)}, u32[]{:S(2)}, u32[]{:S(2)}) collective-permute-start(bf16[2,128,768]{2,1,0:T(8,128)(2,1)S(1)} %get-tuple-element.41), channel_id=1, source_target_pairs={{0,1},{1,0},{2,3},{3,2},{4,5},{5,4},{6,7},{7,6},{8,9},{9,8},{10,11... | collective-permute-start | bytes 1179656 | tf_op jit(solution)/shard_map/ppermute | solution.py:196
  47.4 10.4 %collective-permute-start.23 = (bf16[136,768]{1,0:T(8,128)(2,1)}, bf16[136,768]{1,0:T(8,128)(2,1)S(1)}, u32[]{:S(2)}, u32[]{:S(2)}) collective-permute-start(bf16[136,768]{1,0:T(8,128)(2,1)} %collective-permute-done.10.refs_0_), channel_id=1, source_target_pairs={{0,1},{1,0},{2,3},{3,2},{4,5},{5,4},{6,7},{7,6},{8,9},{9,8},{10,11... | collective-permute-start | bytes 626696 | tf_op jit(solution)/shard_map/ppermute | solution.py:196
  55.3 14.8 %collective-permute-start.20 = (bf16[2,128,768]{2,1,0:T(8,128)(2,1)S(1)}, bf16[2,128,768]{2,1,0:T(8,128)(2,1)S(1)}, u32[]{:S(2)}, u32[]{:S(2)}) collective-permute-start(bf16[2,128,768]{2,1,0:T(8,128)(2,1)S(1)} %get-tuple-element.48), channel_id=1, source_target_pairs={{0,1},{1,0},{2,3},{3,2},{4,5},{5,4},{6,7},{7,6},{8,9},{9,8},{10,11... | collective-permute-start | bytes 1179656 | tf_op jit(solution)/shard_map/ppermute | solution.py:196
  56.6 8.8 %collective-permute-start.15 = (bf16[128,768]{1,0:T(8,128)(2,1)S(1)}, bf16[128,768]{1,0:T(8,128)(2,1)S(1)}, u32[]{:S(2)}, u32[]{:S(2)}) collective-permute-start(bf16[128,768]{1,0:T(8,128)(2,1)S(1)} %fusion.9), channel_id=1, source_target_pairs={{0,2},{1,3},{2,0},{3,1},{4,6},{5,7},{6,4},{7,5},{8,10},{9,11},{10,... | collective-permute-start | bytes 589832 | tf_op jit(solution)/shard_map/ppermute | solution.py:196
  64.2 30.2 %collective-permute-start.9 = (bf16[128,768]{1,0:T(8,128)(2,1)S(1)}, bf16[128,768]{1,0:T(8,128)(2,1)S(1)}, u32[]{:S(2)}, u32[]{:S(2)}) collective-permute-start(bf16[128,768]{1,0:T(8,128)(2,1)S(1)} %fusion.8), channel_id=1, source_target_pairs={{0,2},{1,3},{2,0},{3,1},{4,6},{5,7},{6,4},{7,5},{8,10},{9,11},{10,... | collective-permute-start | bytes 589832 | tf_op jit(solution)/shard_map/ppermute | solution.py:196
  65.2 13.0 %collective-permute-start.26 = (bf16[2,128,768]{2,1,0:T(8,128)(2,1)S(1)}, bf16[2,128,768]{2,1,0:T(8,128)(2,1)S(1)}, u32[]{:S(2)}, u32[]{:S(2)}) collective-permute-start(bf16[2,128,768]{2,1,0:T(8,128)(2,1)S(1)} %get-tuple-element.51), channel_id=1, source_target_pairs={{0,1},{1,0},{2,3},{3,2},{4,5},{5,4},{6,7},{7,6},{8,9},{9,8},{10,11... | collective-permute-start | bytes 1179656 | tf_op jit(solution)/shard_map/ppermute | solution.py:196
  66.4 28.0 %collective-permute-start.16 = (bf16[128,768]{1,0:T(8,128)(2,1)S(1)}, bf16[128,768]{1,0:T(8,128)(2,1)S(1)}, u32[]{:S(2)}, u32[]{:S(2)}) collective-permute-start(bf16[128,768]{1,0:T(8,128)(2,1)S(1)} %fusion.2), channel_id=1, source_target_pairs={{0,12},{4,0},{8,4},{12,8},{1,13},{5,1},{9,5},{13,9},{2,14},{6,2},{... | collective-permute-start | bytes 589832 | tf_op jit(solution)/shard_map/ppermute | solution.py:201
  71.6 12.7 %collective-permute-start.30 = (bf16[192,768]{1,0:T(8,128)(2,1)S(1)}, bf16[192,768]{1,0:T(8,128)(2,1)S(1)}, u32[]{:S(2)}, u32[]{:S(2)}) collective-permute-start(bf16[192,768]{1,0:T(8,128)(2,1)S(1)} %fusion.7), channel_id=1, source_target_pairs={{0,2},{1,3},{2,0},{3,1},{4,6},{5,7},{6,4},{7,5},{8,10},{9,11},{10,... | collective-permute-start | bytes 884744 | tf_op jit(solution)/shard_map/ppermute | solution.py:196
  78.1 16.4 %collective-permute-start.22 = (bf16[128,768]{1,0:T(8,128)(2,1)S(1)}, bf16[128,768]{1,0:T(8,128)(2,1)S(1)}, u32[]{:S(2)}, u32[]{:S(2)}) collective-permute-start(bf16[128,768]{1,0:T(8,128)(2,1)S(1)} %fusion.1), channel_id=1, source_target_pairs={{0,8},{4,12},{8,0},{12,4},{1,9},{5,13},{9,1},{13,5},{2,10},{6,14},... | collective-permute-start | bytes 589832 | tf_op jit(solution)/shard_map/ppermute | solution.py:201
  78.2 9.4 %collective-permute-start.27 = (bf16[128,768]{1,0:T(8,128)(2,1)S(1)}, bf16[128,768]{1,0:T(8,128)(2,1)S(1)}, u32[]{:S(2)}, u32[]{:S(2)}) collective-permute-start(bf16[128,768]{1,0:T(8,128)(2,1)S(1)} %fusion.11), channel_id=1, source_target_pairs={{0,2},{1,3},{2,0},{3,1},{4,6},{5,7},{6,4},{7,5},{8,10},{9,11},{10,... | collective-permute-start | bytes 589832 | tf_op jit(solution)/shard_map/ppermute | solution.py:196
  84.5 9.8 %collective-permute-start.31 = (bf16[96,768]{1,0:T(8,128)(2,1)S(1)}, bf16[96,768]{1,0:T(8,128)(2,1)S(1)}, u32[]{:S(2)}, u32[]{:S(2)}) collective-permute-start(bf16[96,768]{1,0:T(8,128)(2,1)S(1)} %dynamic-slice_convert_fusion), channel_id=1, source_target_pairs={{0,4},{4,0},{8,12},{12,8},{1,5},{5,1},{9,13},{13,9},{2,6},{6,2},{1... | collective-permute-start | bytes 442376 | tf_op jit(solution)/shard_map/ppermute | solution.py:196
  87.7 9.4 %collective-permute-start.28 = (bf16[128,768]{1,0:T(8,128)(2,1)S(1)}, bf16[128,768]{1,0:T(8,128)(2,1)S(1)}, u32[]{:S(2)}, u32[]{:S(2)}) collective-permute-start(bf16[128,768]{1,0:T(8,128)(2,1)S(1)} %fusion), channel_id=1, source_target_pairs={{0,4},{4,8},{8,12},{12,0},{1,5},{5,9},{9,13},{13,1},{2,6},{6,10},{... | collective-permute-start | bytes 589832 | tf_op jit(solution)/shard_map/ppermute | solution.py:201
  (47 other events, 289.4 us)

commit v5 on v4

v5 whole, which is shorter than its diff:
```python
import functools

import jax
import jax.numpy as jnp
from jax import lax
from jax.experimental import pallas as pl
from jax.experimental.pallas import tpu as pltpu
from jax.sharding import PartitionSpec as P

BLK = 128
EPSILON = 1e-06
META_ROWS = 8
F32 = jnp.float32
BF16 = jnp.bfloat16


def dot(a, b, da=1, db=0):
    return lax.dot_general(a, b, (((da,), (db,)), ((), ())), preferred_element_type=F32)


def pair_kernel(where_ref, *refs, cap, pick_count, n_data, prior):
    it = iter(refs)
    take = lambda n: [next(it) for _ in range(n)]
    last = prior is not None
    source_in, shard_in, label_in = take(n_data), take(n_data), next(it)
    prior_in = take(2 * prior if last else 0)
    outs = take(9 if last else 7)
    src, enc, label = take(3)
    results = take(9 if last else 7)
    in_sem, out_sem = take(2)
    all_feats, all_grad_hidden, total = take(3) if last else [None] * 3
    even, odd, grad_scores_v, block_v, embedding_v, feats_v, grad_hidden_v = results[:7]

    me = where_ref[0].astype(F32)
    my_data = where_ref[1]
    rows = src.shape[1] - META_ROWS
    shard_rows = shard_in[0].shape[0]
    n_blocks = label.shape[0] // BLK
    slots = n_data * cap

    pairs = [(ref, src.at[m]) for m, ref in enumerate(source_in)]
    pairs += [(ref, enc.at[shard_at(my_data, m, shard_rows)]) for m, ref in enumerate(shard_in)]
    pairs += [(label_in, label)]
    for i in range(len(prior_in) // 2):
        at = pl.ds(i * slots, slots)
        pairs += [(prior_in[i], all_feats.at[at]), (prior_in[prior + i], all_grad_hidden.at[at])]
    fetch = [pltpu.make_async_copy(a, b, in_sem.at[i]) for i, (a, b) in enumerate(pairs)]
    for copy in fetch:
        copy.start()
    store = [pltpu.make_async_copy(a, b, out_sem.at[i]) for i, (a, b) in enumerate(zip(results, outs))]

    row_id = lax.broadcasted_iota(jnp.int32, (rows, rows), 0)
    col_id = lax.broadcasted_iota(jnp.int32, (rows, rows), 1)
    before = (row_id < col_id).astype(BF16)
    slot_id = lax.broadcasted_iota(jnp.int32, (cap, rows), 0).astype(F32)
    column = lax.broadcasted_iota(jnp.int32, (slots, BLK), 1)

    hits, codes = [], []
    for m in range(n_data):
        fetch[m].wait()
        meta = src[m, rows:, 0 : 3 * rows].astype(F32)[:pick_count]
        named = meta[:, :rows] == me
        hits.append(jnp.sum(named.astype(F32), axis=0, keepdims=True))
        code = meta[:, rows : 2 * rows] * 256.0 + meta[:, 2 * rows :] + 1.0
        codes.append(jnp.sum(jnp.where(named, code, 0.0), axis=0, keepdims=True))
    rank = dot(jnp.concatenate(hits, axis=0).astype(BF16), before)

    picks, picked, slot_codes = [], [], []
    for m in range(n_data):
        pick = jnp.where((slot_id == rank[m : m + 1]) & (hits[m] > 0.0), 1.0, 0.0)
        slot_codes.append(jnp.sum(pick * codes[m], axis=1, keepdims=True))
        pick = pick.astype(BF16)
        picks.append(pick)
        picked.append(dot(pick, src[m, :rows, :]).astype(BF16))
    feats = jnp.concatenate(picked, axis=0)
    feats_v[...] = feats
    store[5].start()
    code = jnp.concatenate(slot_codes, axis=0).astype(jnp.int32) - 1

    for m in range(n_data):
        fetch[n_data + m].wait()
    hidden = dot(feats, enc[...])
    inv_rms = lax.rsqrt(jnp.mean(hidden * hidden, axis=-1, keepdims=True) + EPSILON)
    embedding = (hidden * inv_rms).astype(BF16)
    embedding_v[...] = embedding
    store[4].start()

    fetch[2 * n_data].wait()
    scores = dot(embedding, label[...], 1, 1)
    block = jnp.broadcast_to(code >> 8, (slots, BLK))
    block_v[...] = block
    store[3].start()
    wanted = jnp.broadcast_to(code & 255, (slots, BLK))
    own_scores = jnp.zeros((slots, BLK), F32)
    for b in range(n_blocks):
        own_scores = jnp.where(block == b, scores[:, b * BLK : (b + 1) * BLK], own_scores)
    target = jnp.where(column == wanted, 1.0, 0.0)
    grad_scores = jnp.where(block >= 0, jax.nn.sigmoid(own_scores) - target, 0.0)
    grad_scores_v[...] = grad_scores
    store[2].start()

    spread = jnp.concatenate(
        [jnp.where(block == b, grad_scores, 0.0).astype(BF16) for b in range(n_blocks)], axis=1
    )
    grad_pair = dot(spread, label[...]).astype(BF16).astype(F32)
    projection = jnp.mean(hidden * grad_pair, axis=-1, keepdims=True)
    grad_hidden = (inv_rms * grad_pair - hidden * (inv_rms**3 * projection)).astype(BF16)
    grad_hidden_v[...] = grad_hidden
    store[6].start()

    if last:
        at = pl.ds(prior * slots, slots)
        all_feats[at, :] = feats
        all_grad_hidden[at, :] = grad_hidden
        for copy in fetch[2 * n_data + 1 :]:
            copy.wait()
        total[...] = dot(all_feats[...], all_grad_hidden[...], 0, 0)
        for m in range(n_data):
            part = total[shard_at(my_data, m, shard_rows), :]
            results[7 + m % 2][m // 2] = part.astype(BF16)
        store[7].start()
        store[8].start()

    grad_feats = dot(grad_hidden, enc[...], 1, 1).astype(BF16)
    for m in range(n_data):
        part = dot(picks[m], grad_feats[m * cap : (m + 1) * cap], 0, 0)
        results[m % 2][m // 2] = part.astype(BF16)
    store[0].start()
    store[1].start()
    for copy in store:
        copy.wait()


def grad_label_kernel(*refs, runs):
    ins, out_ref, scratch, sem = refs[: 3 * runs], refs[3 * runs], refs[3 * runs + 1 : -1], refs[-1]
    slots = ins[0].shape[0]
    fetch = []
    for i, ref in enumerate(ins):
        target = scratch[i // runs].at[pl.ds(i % runs * slots, slots)]
        fetch.append(pltpu.make_async_copy(ref, target, sem.at[i]))
        fetch[-1].start()
    for copy in fetch:
        copy.wait()
    grad_scores_t, block_t, embedding = scratch[0][...].T, scratch[1][...].T, scratch[2][...]
    for b in range(out_ref.shape[0] // BLK):
        spread_t = jnp.where(block_t == b, grad_scores_t, 0.0).astype(BF16)
        out_ref[b * BLK : (b + 1) * BLK, :] = dot(spread_t, embedding).astype(BF16)


def shard_at(my_data, m, shard_rows):
    at = jnp.bitwise_xor(my_data, m) * shard_rows
    return pl.ds(pl.multiple_of(at, 16), shard_rows)


def call(kernel, name, out_spec, out_shape, scratch, flops, megabytes, *args):
    smem = pl.BlockSpec(memory_space=pltpu.SMEM)
    anywhere = pl.BlockSpec(memory_space=pl.ANY)
    return pl.pallas_call(
        kernel,
        in_specs=[smem if a.ndim == 1 else anywhere for a in args],
        out_specs=jax.tree.map(lambda _: pl.BlockSpec(memory_space=out_spec), out_shape),
        out_shape=out_shape,
        scratch_shapes=scratch,
        compiler_params=pltpu.CompilerParams(vmem_limit_bytes=32 << 20),
        cost_estimate=pl.CostEstimate(
            flops=flops, bytes_accessed=megabytes << 20, transcendentals=0
        ),
        name=name,
    )(*args)


def pair_work(where, sources, shards, label_weight, cap, pick_count, prior=None):
    n_data = len(sources)
    block_rows, width = sources[0].shape
    rows = block_rows - META_ROWS
    slots = n_data * cap
    shard_rows = shards[0].shape[0]
    shapes = [((n_data // 2, rows, width), BF16)] * 2 + [((slots, BLK), F32)]
    shapes += [((slots, BLK), jnp.int32)] + [((slots, width), BF16)] * 3
    scratch, more = [], []
    if prior is not None:
        shapes += [((n_data // 2, shard_rows, width), BF16)] * 2
        more = [run[5] for run in prior] + [run[6] for run in prior]
        scratch = [pltpu.VMEM(((len(prior) + 1) * slots, width), BF16)] * 2
        scratch += [pltpu.VMEM((n_data * shard_rows, width), F32)]
    return call(
        functools.partial(
            pair_kernel,
            cap=cap,
            pick_count=pick_count,
            n_data=n_data,
            prior=None if prior is None else len(prior),
        ),
        "pair_work",
        pl.ANY,
        [jax.ShapeDtypeStruct(*shape) for shape in shapes],
        [
            pltpu.VMEM((n_data, block_rows, width), BF16),
            pltpu.VMEM((n_data * shard_rows, width), BF16),
            pltpu.VMEM(label_weight.shape, BF16),
        ]
        + [pltpu.VMEM(*shape) for shape in shapes]
        + [
            pltpu.SemaphoreType.DMA((2 * n_data + 1 + len(more),)),
            pltpu.SemaphoreType.DMA((len(shapes),)),
        ]
        + scratch,
        2 * slots * width * (2 * label_weight.shape[0] + 2 * width + 2 * rows),
        6,
        where,
        *sources,
        *shards,
        label_weight,
        *more,
    )


def grad_label_work(grad_scores, blocks, embeddings, label_weight):
    runs, slots = len(blocks), blocks[0].shape[0]
    return call(
        functools.partial(grad_label_kernel, runs=runs),
        "grad_label_work",
        pltpu.VMEM,
        jax.ShapeDtypeStruct(label_weight.shape, BF16),
        [
            pltpu.VMEM((runs * slots, BLK), F32),
            pltpu.VMEM((runs * slots, BLK), jnp.int32),
            pltpu.VMEM((runs * slots, label_weight.shape[1]), BF16),
            pltpu.SemaphoreType.DMA((3 * runs,)),
        ],
        2 * runs * slots * label_weight.size,
        4,
        *grad_scores,
        *blocks,
        *embeddings,
    )


def swap(x):
    x = lax.all_to_all(x, "labels", split_axis=0, concat_axis=0, tiled=True)
    return lax.all_to_all(x, "dp", split_axis=1, concat_axis=1, tiled=True)


def partner(x, axis, mask):
    return lax.ppermute(x, axis, [(i, i ^ mask) for i in range(lax.axis_size(axis))])


def masks(n):
    return [1 << i for i in range(n.bit_length() - 1)]


def after(x, *others):
    return lax.optimization_barrier((x, *others))[0]


def gather_dp(x, first=None):
    got = {0: x}
    *far, near = reversed(masks(lax.axis_size("dp")))
    for mask in far:
        got.update({m | mask: partner(v, "dp", mask) for m, v in list(got.items())})
    for m, v in sorted(got.items(), reverse=True):
        if m:
            v = v if first is None else after(v, first)
        elif len(got) > 1:
            v = after(v, got[max(i for i in got if i & near == 0)])
        got[m | near] = partner(v, "dp", near)
    return [got[m] for m in range(len(got))]


def gather_labels(x):
    got = {0: x}
    for mask in reversed(masks(lax.axis_size("labels"))):
        got.update({m | mask: partner(v, "labels", mask) for m, v in list(got.items())})
    return [got[m] for m in range(len(got))]


def add(*terms):
    return sum(t.astype(F32) for t in terms)


def reduce_dp(even, odd):
    got = partner(odd, "dp", 1)
    terms = [[even[i], got[i]] for i in range(even.shape[0])]
    for mask in masks(len(terms)):
        for i in range(len(terms)):
            if i & mask == 0 and i % mask == 0:
                terms[i].append(partner(add(*terms[i | mask]).astype(BF16), "dp", 2 * mask))
    return add(*terms[0])


def sum_labels(x):
    half = x.shape[0] // 2
    odd = lax.axis_index("labels") & 1
    cut = lambda p: lax.dynamic_slice_in_dim(x, p * half, half, 0)
    x = add(cut(odd), partner(cut(1 - odd).astype(BF16), "labels", 1)).astype(BF16)
    for mask in masks(lax.axis_size("labels"))[1:]:
        x = add(x, partner(x, "labels", mask)).astype(BF16)
    other = partner(x, "labels", 1)
    low, high = jnp.where(odd == 0, x, other), jnp.where(odd == 0, other, x)
    return jnp.concatenate([low, high], axis=0).astype(F32)


def reduce_labels(parts):
    terms = [[part] for part in parts]
    for mask in masks(len(terms)):
        for i in range(len(terms)):
            if i & mask == 0 and i % mask == 0:
                terms[i].append(partner(add(*terms[i | mask]).astype(BF16), "labels", mask))
    return add(*terms[0])


def with_meta(feats, owner_rows, block_rows, positive_rows):
    meta = jnp.concatenate([owner_rows, block_rows, positive_rows], axis=1).astype(BF16)
    meta = jnp.pad(meta, ((0, META_ROWS - meta.shape[0]), (0, feats.shape[1] - meta.shape[1])))
    return jnp.concatenate([feats, meta], axis=0)


def local(feats, enc_weight, label_weight, owners, blocks, positives):
    n_labels = lax.axis_size("labels")
    n_data = lax.axis_size("dp")
    n_owner = n_labels * n_data
    row_count, width = feats.shape
    pick_count = owners.shape[1]
    cap = max(2, 2 * row_count * pick_count // n_owner)
    my_data = lax.axis_index("dp")
    where = jnp.stack([lax.axis_index("labels") * n_data + my_data, my_data]).astype(jnp.int32)
    shards = gather_dp(enc_weight)

    if row_count <= n_data * cap:
        own = with_meta(feats, owners.T, blocks.T, positives.T)
        rows_of = gather_labels(own)
        work = []
        for by in range(n_labels):
            run = gather_dp(rows_of[by], work[-1][0] if work else None)
            if by + 1 < n_labels:
                run[0] = after(run[0], *rows_of[by + 1 : by + 3])
            prior = work if by == n_labels - 1 else None
            work.append(pair_work(where, run, shards, label_weight, cap, pick_count, prior))
        grad_feats = reduce_labels([reduce_dp(*run[:2]) for run in work]).astype(BF16)
    else:
        flat = owners.reshape(-1)
        onehot = (flat[:, None] == jnp.arange(n_owner, dtype=jnp.int32)[None, :]).astype(jnp.int32)
        rank = jnp.sum((jnp.cumsum(onehot, axis=0) - onehot) * onehot, axis=1)
        slot = (flat * cap + rank).reshape(row_count, pick_count)
        slot_total = n_owner * cap
        slots = jnp.arange(slot_total, dtype=jnp.int32)
        place = slots[:, None, None] == slot[None]
        pick = jnp.any(place, axis=2).astype(BF16)
        live = jnp.any(place, axis=(1, 2))
        block_of = jnp.sum(jnp.where(place, blocks[None], 0), axis=(1, 2))
        wanted = jnp.sum(jnp.where(place, positives[None], 0), axis=(1, 2))
        owner_of = jnp.where(live, slots // cap, -1)
        out = dot(pick, feats).astype(BF16).reshape(n_labels, n_data, cap, width)
        meta = jnp.stack([owner_of, block_of, wanted], axis=1).reshape(n_labels, n_data, cap, 3)
        tile = 128
        got = swap(out).reshape(slot_total // tile, tile, width)
        got_meta = swap(meta).reshape(slot_total // tile, tile, 3).transpose(0, 2, 1)
        sources = [
            with_meta(got[i], got_meta[i, 0:1], got_meta[i, 1:2], got_meta[i, 2:3])
            for i in range(slot_total // tile)
        ]
        work = []
        for i in range(0, len(sources), n_data):
            prior = work if i + n_data == len(sources) else None
            run = sources[i : i + n_data]
            work.append(pair_work(where, run, shards, label_weight, tile, 1, prior))
        back = jnp.stack([part for run in work for part in run[:2]])
        back = back.reshape(-1, 2, n_data // 2, tile, width).transpose(0, 2, 1, 3, 4)
        back = swap(back.reshape(n_labels, n_data, cap, width)).reshape(slot_total, width)
        grad_feats = dot(pick, back, 0, 0).astype(BF16)

    _, _, grad_scores, block_of, embedding, _, _ = zip(*(run[:7] for run in work))
    share = reduce_dp(*work[-1][7:])
    embedding = (after(embedding[0], share),) + embedding[1:]
    grad_label = grad_label_work(grad_scores, block_of, embedding, label_weight)
    grad_enc = sum_labels(share)
    return (grad_feats, grad_label, grad_enc)


def solution(mesh):
    rows = P(("groups", "labels", "dp"), None)
    return jax.shard_map(
        local,
        mesh=mesh,
        in_specs=(rows, P("dp", None), rows, rows, rows, rows),
        out_specs=(rows, rows, P(("groups", "dp"), None)),
        check_vma=False,
    )
```

time: 109 us -> 134 us (1.23)
  Pallas kernels: 21.1 us -> 36.8 us
  starting transfers between devices: 21.3 us -> 28.6 us
  local copies, waits for them, and re-layouts: 15.6 us -> 22.3 us
  waiting for transfers between devices: 42.7 us -> 38.4 us
    pallas_call x6 -> x5, Pallas kernels: 21.1 us -> 36.8 us  [call(): pl.pallas_call(kernel, in_specs=[smem if a.ndim == 1 else anywhere for a...]
    ppermute x6 -> x0, waiting for transfers between devices: 15.7 us -> none  [shifted(): return lax.ppermute(x, axis, [(i, (i + by) % n) for i in range(n)])]
    ppermute x28 -> x34, starting transfers between devices: 15.8 us -> 28.6 us  [partner(): lax.ppermute(x, axis, [(i, i ^ mask) for i in range(lax.axis_size(axis))])]
    ppermute x28 -> x34, waiting for transfers between devices: 27 us -> 38.4 us  [partner(): lax.ppermute(x, axis, [(i, i ^ mask) for i in range(lax.axis_size(axis))])]
    unnamed x74 -> x84, local copies, waits for them, and re-layouts: 15.6 us -> 22.3 us
    ppermute x6 -> x0, starting transfers between devices: 5.52 us -> none  [shifted(): return lax.ppermute(x, axis, [(i, (i + by) % n) for i in range(n)])]
  transfers between devices with their start and end apart: 34 -> 34, of which waited for: 12 -> 11; matrix products, arithmetic and copies ran while one was open for 5% -> 4% of each run, Pallas kernels for 19% -> 28%
where the time goes in v5:
time: 134 us
  waiting for transfers between devices  38.4 us (29%)
  Pallas kernels  36.8 us (27%)
  starting transfers between devices  28.6 us (21%)
  local copies, waits for them, and re-layouts  22.3 us (17%)
  other arithmetic  6.63 us (5%)
    ppermute x34, waiting for transfers between devices, partner(): lax.ppermute(x, axis, [(i, i ^ mask) for i in range(lax.axis_size(axis))])  38.4 us
    pallas_call x5, Pallas kernels, call(): pl.pallas_call(kernel, in_specs=[smem if a.ndim == 1 else anywhere for a...  36.8 us
    ppermute x34, starting transfers between devices, partner(): lax.ppermute(x, axis, [(i, i ^ mask) for i in range(lax.axis_size(axis))])  28.6 us
    unnamed x84, local copies, waits for them, and re-layouts  22.3 us
  transfers between devices with their start and end apart: 34, of which 11 were waited for; matrix products, arithmetic and copies ran while one was open for 4% of the time, Pallas kernels for 28%

profile of v5, /device:TPU:0, one launch (start us, length us, event | category | flops | bytes accessed | tf_op | source)
XLA Modules:
  0.0 133.8 jit_solution(16703874993457455865)
XLA Ops:
  0.6 3.0 %collective-permute-start.5 = (bf16[192,768]{1,0:T(8,128)(2,1)}, bf16[192,768]{1,0:T(8,128)(2,1)S(1)}, u32[]{:S(2)}, u32[]{:S(2)}) collective-permute-start(bf16[192,768]{1,0:T(8,128)(2,1)} %refs_4_.7), channel_id=1, source_target_pairs={{0,2},{1,3},{2,0},{3,1},{4,6},{5,7},{6,4},{7,5},{8,10},{9,11},{10,... | collective-permute-start | bytes 884744 | tf_op jit(solution)/shard_map/ppermute | solution.py:245
  6.0 1.6 %collective-permute-start = (bf16[136,768]{1,0:T(8,128)(2,1)S(1)}, bf16[136,768]{1,0:T(8,128)(2,1)S(1)}, u32[]{:S(2)}, u32[]{:S(2)}) collective-permute-start(bf16[136,768]{1,0:T(8,128)(2,1)S(1)} %pad_maximum_fusion.refs_0_), channel_id=1, source_target_pairs={{0,4},{4,0},{8,12},{12,8},{1,5},{5,1},{9,13},{13,9},{2,6},{6,2},{1... | collective-permute-start | bytes 626696 | tf_op jit(solution)/shard_map/ppermute | solution.py:245
  8.2 2.6 %collective-permute-start.1 = (bf16[136,768]{1,0:T(8,128)(2,1)S(1)}, bf16[136,768]{1,0:T(8,128)(2,1)}, u32[]{:S(2)}, u32[]{:S(2)}) collective-permute-start(bf16[136,768]{1,0:T(8,128)(2,1)S(1)} %pad_maximum_fusion.refs_0_), channel_id=1, source_target_pairs={{0,8},{4,12},{8,0},{12,4},{1,9},{5,13},{9,1},{13,5},{2,10},{6,14},... | collective-permute-start | bytes 626696 | tf_op jit(solution)/shard_map/ppermute | solution.py:245
  12.2 4.6 %collective-permute-done.refs_0_ = bf16[136,768]{1,0:T(8,128)(2,1)S(1)} collective-permute-done((bf16[136,768]{1,0:T(8,128)(2,1)S(1)}, bf16[136,768]{1,0:T(8,128)(2,1)S(1)}, u32[]{:S(2)}, u32[]{:S(2)}) %collective-permute-start) | collective-permute-done | bytes 208928 | tf_op jit(solution)/shard_map/ppermute | solution.py:245
  17.5 2.3 %collective-permute-done.1.refs_0_ = bf16[136,768]{1,0:T(8,128)(2,1)} collective-permute-done((bf16[136,768]{1,0:T(8,128)(2,1)S(1)}, bf16[136,768]{1,0:T(8,128)(2,1)}, u32[]{:S(2)}, u32[]{:S(2)}) %collective-permute-start.1) | collective-permute-done | bytes 208928 | tf_op jit(solution)/shard_map/ppermute | solution.py:245
  20.5 2.1 %collective-permute-done.11.refs_2_ = bf16[136,768]{1,0:T(8,128)(2,1)S(1)} collective-permute-done((bf16[136,768]{1,0:T(8,128)(2,1)S(1)}, bf16[136,768]{1,0:T(8,128)(2,1)S(1)}, u32[]{:S(2)}, u32[]{:S(2)}) %collective-permute-start.11) | collective-permute-done | bytes 208928 | tf_op jit(solution)/shard_map/ppermute | solution.py:245
  25.5 1.4 %copy-done = bf16[1024,768]{1,0:T(8,128)(2,1)S(1)} copy-done((bf16[1024,768]{1,0:T(8,128)(2,1)S(1)}, bf16[1024,768]{1,0:T(8,128)(2,1)}, u32[]{:S(2)}) %copy-start) | copy-done | bytes 1572888
  32.5 7.1 %pair_work.4 = (bf16[2,128,768]{2,1,0:T(8,128)(2,1)S(1)}, bf16[2,128,768]{2,1,0:T(8,128)(2,1)S(1)}, f32[256,128]{1,0:T(8,128)S(1)}, s32[256,128]{1,0:T(8,128)S(1...) custom-call(s32[2]{0:T(128)S(1)} %pad_add_fusion.where_ref, ...), custom_call_target="tpu_custom_call" | custom-call | flops 1509949440 | bytes 6291456 | tf_op jit(solution)/shard_map/pair_work/pallas_call | solution.py:158
  45.6 7.6 %pair_work.5 = (bf16[2,128,768]{2,1,0:T(8,128)(2,1)S(1)}, bf16[2,128,768]{2,1,0:T(8,128)(2,1)}, f32[256,128]{1,0:T(8,128)S(1)}, s32[256,128]{1,0:T(8,128)S(1)}, ...) custom-call(s32[2]{0:T(128)S(1)} %pad_add_fusion.where_ref, ...), custom_call_target="tpu_custom_call" | custom-call | flops 1509949440 | bytes 6291456 | tf_op jit(solution)/shard_map/pair_work/pallas_call | solution.py:158
  57.8 6.2 %collective-permute-done.22.refs_2_ = bf16[136,768]{1,0:T(8,128)(2,1)} collective-permute-done((bf16[136,768]{1,0:T(8,128)(2,1)}, bf16[136,768]{1,0:T(8,128)(2,1)}, u32[]{:S(2)}, u32[]{:S(2)}) %collective-permute-start.22) | collective-permute-done | bytes 208928 | tf_op jit(solution)/shard_map/ppermute | solution.py:245
  67.8 6.8 %pair_work.6 = (bf16[2,128,768]{2,1,0:T(8,128)(2,1)S(1)}, bf16[2,128,768]{2,1,0:T(8,128)(2,1)S(1)}, f32[256,128]{1,0:T(8,128)S(1)}, s32[256,128]{1,0:T(8,128)S(1...) custom-call(s32[2]{0:T(128)S(1)} %pad_add_fusion.where_ref, ...), custom_call_target="tpu_custom_call" | custom-call | flops 1509949440 | bytes 6291456 | tf_op jit(solution)/shard_map/pair_work/pallas_call | solution.py:158
  77.2 10.1 %pair_work.7 = (bf16[2,128,768]{2,1,0:T(8,128)(2,1)S(1)}, bf16[2,128,768]{2,1,0:T(8,128)(2,1)S(1)}, f32[256,128]{1,0:T(8,128)S(1)}, s32[256,128]{1,0:T(8,128)S(1...) custom-call(s32[2]{0:T(128)S(1)} %pad_add_fusion.where_ref, ...), custom_call_target="tpu_custom_call" | custom-call | flops 1509949440 | bytes 6291456 | tf_op jit(solution)/shard_map/pair_work/pallas_call | solution.py:158
  90.1 2.0 %collective-permute-start.16 = (bf16[128,768]{1,0:T(8,128)(2,1)S(1)}, bf16[128,768]{1,0:T(8,128)(2,1)S(1)}, u32[]{:S(2)}, u32[]{:S(2)}) collective-permute-start(bf16[128,768]{1,0:T(8,128)(2,1)S(1)} %fusion.3), channel_id=1, source_target_pairs={{0,4},{4,0},{8,12},{12,8},{1,5},{5,1},{9,13},{13,9},{2,6},{6,2},{1... | collective-permute-start | bytes 589832 | tf_op jit(solution)/shard_map/ppermute | solution.py:245
  93.3 1.1 collective-permute-start.30
  95.5 4.5 %collective-permute-done.26 = bf16[128,768]{1,0:T(8,128)(2,1)S(1)} collective-permute-done((bf16[128,768]{1,0:T(8,128)(2,1)S(1)}, bf16[128,768]{1,0:T(8,128)(2,1)S(1)}, u32[]{:S(2)}, u32[]{:S(2)}) %collective-permute-start.26) | collective-permute-done | bytes 196640 | tf_op jit(solution)/shard_map/ppermute | solution.py:245
  100.1 2.1 %collective-permute-start.27 = (bf16[128,768]{1,0:T(8,128)(2,1)S(1)}, bf16[128,768]{1,0:T(8,128)(2,1)S(1)}, u32[]{:S(2)}, u32[]{:S(2)}) collective-permute-start(bf16[128,768]{1,0:T(8,128)(2,1)S(1)} %fusion), channel_id=1, source_target_pairs={{0,4},{4,0},{8,12},{12,8},{1,5},{5,1},{9,13},{13,9},{2,6},{6,2},{1... | collective-permute-start | bytes 589832 | tf_op jit(solution)/shard_map/ppermute | solution.py:245
  102.1 4.1 %collective-permute-done.30 = bf16[192,768]{1,0:T(8,128)(2,1)S(1)} collective-permute-done((bf16[192,768]{1,0:T(8,128)(2,1)S(1)}, bf16[192,768]{1,0:T(8,128)(2,1)S(1)}, u32[]{:S(2)}, u32[]{:S(2)}) %collective-permute-start.30) | collective-permute-done | bytes 294944 | tf_op jit(solution)/shard_map/ppermute | solution.py:245
  106.4 2.1 %collective-permute-start.31 = (bf16[96,768]{1,0:T(8,128)(2,1)S(1)}, bf16[96,768]{1,0:T(8,128)(2,1)S(1)}, u32[]{:S(2)}, u32[]{:S(2)}) collective-permute-start(bf16[96,768]{1,0:T(8,128)(2,1)S(1)} %dynamic-slice_convert_fusion), channel_id=1, source_target_pairs={{0,4},{4,0},{8,12},{12,8},{1,5},{5,1},{9,13},{13,9},{2,6},{6,2},{1... | collective-permute-start | bytes 442376 | tf_op jit(solution)/shard_map/ppermute | solution.py:245
  108.5 1.3 collective-permute-done.21
  109.9 2.9 %collective-permute-start.28 = (bf16[128,768]{1,0:T(8,128)(2,1)S(1)}, bf16[128,768]{1,0:T(8,128)(2,1)S(1)}, u32[]{:S(2)}, u32[]{:S(2)}) collective-permute-start(bf16[128,768]{1,0:T(8,128)(2,1)S(1)} %fusion.2), channel_id=1, source_target_pairs={{0,8},{4,12},{8,0},{12,4},{1,9},{5,13},{9,1},{13,5},{2,10},{6,14},... | collective-permute-start | bytes 589832 | tf_op jit(solution)/shard_map/ppermute | solution.py:245
  112.8 2.0 %collective-permute-start.32 = (bf16[96,768]{1,0:T(8,128)(2,1)S(1)}, bf16[96,768]{1,0:T(8,128)(2,1)S(1)}, u32[]{:S(2)}, u32[]{:S(2)}) collective-permute-start(bf16[96,768]{1,0:T(8,128)(2,1)S(1)} %add_convert_fusion.6), channel_id=1, source_target_pairs={{0,8},{4,12},{8,0},{12,4},{1,9},{5,13},{9,1},{13,5},{2,10},{6,14},... | collective-permute-start | bytes 442376 | tf_op jit(solution)/shard_map/ppermute | solution.py:245
  114.9 5.3 %grad_label_work.1 = bf16[1024,768]{1,0:T(8,128)(2,1)} custom-call(f32[256,128]{1,0:T(8,128)S(1)} %copy-done.35, f32[256,128]{1,0:T(8,128)S(1)} %copy-done.39, f32[256,128]{1,0:T(8,128)S(1)} %get-tuple-element.70.refs_2_, f32[256,128]{1,0:T(8,128)S(1)} %get-tuple-element.71.refs_3_, s32[256,128]{1,0:T(8,128)S(1)} %copy-done.37, s32[256,128]{1,0:T(8,128)S(1)} %copy-done.41, ...), custom_call_target="tpu_custom_call" | custom-call | flops 1610612736 | bytes 4194304 | tf_op jit(solution)/shard_map/grad_label_work/pallas_call | solution.py:158
  120.2 7.5 %collective-permute-done.32 = bf16[96,768]{1,0:T(8,128)(2,1)S(1)} collective-permute-done((bf16[96,768]{1,0:T(8,128)(2,1)S(1)}, bf16[96,768]{1,0:T(8,128)(2,1)S(1)}, u32[]{:S(2)}, u32[]{:S(2)}) %collective-permute-start.32) | collective-permute-done | bytes 147488 | tf_op jit(solution)/shard_map/ppermute | solution.py:245
  128.6 4.3 %collective-permute-done.33 = bf16[96,768]{1,0:T(8,128)(2,1)S(1)} collective-permute-done((bf16[96,768]{1,0:T(8,128)(2,1)S(1)}, bf16[96,768]{1,0:T(8,128)(2,1)S(1)}, u32[]{:S(2)}, u32[]{:S(2)}) %collective-permute-start.33) | collective-permute-done | bytes 147488 | tf_op jit(solution)/shard_map/ppermute | solution.py:245
  (153 shorter events, 38.4 us)
Async XLA Ops:
  0.6 11.1 %collective-permute-start.5 = (bf16[192,768]{1,0:T(8,128)(2,1)}, bf16[192,768]{1,0:T(8,128)(2,1)S(1)}, u32[]{:S(2)}, u32[]{:S(2)}) collective-permute-start(bf16[192,768]{1,0:T(8,128)(2,1)} %refs_4_.7), channel_id=1, source_target_pairs={{0,2},{1,3},{2,0},{3,1},{4,6},{5,7},{6,4},{7,5},{8,10},{9,11},{10,... | collective-permute-start | bytes 884744 | tf_op jit(solution)/shard_map/ppermute | solution.py:245
  6.0 10.8 %collective-permute-start = (bf16[136,768]{1,0:T(8,128)(2,1)S(1)}, bf16[136,768]{1,0:T(8,128)(2,1)S(1)}, u32[]{:S(2)}, u32[]{:S(2)}) collective-permute-start(bf16[136,768]{1,0:T(8,128)(2,1)S(1)} %pad_maximum_fusion.refs_0_), channel_id=1, source_target_pairs={{0,4},{4,0},{8,12},{12,8},{1,5},{5,1},{9,13},{13,9},{2,6},{6,2},{1... | collective-permute-start | bytes 626696 | tf_op jit(solution)/shard_map/ppermute | solution.py:245
  7.6 9.2 %collective-permute-start.2 = (bf16[136,768]{1,0:T(8,128)(2,1)S(1)}, bf16[136,768]{1,0:T(8,128)(2,1)S(1)}, u32[]{:S(2)}, u32[]{:S(2)}) collective-permute-start(bf16[136,768]{1,0:T(8,128)(2,1)S(1)} %pad_maximum_fusion.refs_0_), channel_id=1, source_target_pairs={{0,2},{1,3},{2,0},{3,1},{4,6},{5,7},{6,4},{7,5},{8,10},{9,11},{10,... | collective-permute-start | bytes 626696 | tf_op jit(solution)/shard_map/ppermute | solution.py:245
  8.2 11.6 %collective-permute-start.1 = (bf16[136,768]{1,0:T(8,128)(2,1)S(1)}, bf16[136,768]{1,0:T(8,128)(2,1)}, u32[]{:S(2)}, u32[]{:S(2)}) collective-permute-start(bf16[136,768]{1,0:T(8,128)(2,1)S(1)} %pad_maximum_fusion.refs_0_), channel_id=1, source_target_pairs={{0,8},{4,12},{8,0},{12,4},{1,9},{5,13},{9,1},{13,5},{2,10},{6,14},... | collective-permute-start | bytes 626696 | tf_op jit(solution)/shard_map/ppermute | solution.py:245
  11.7 13.0 %collective-permute-start.6 = (bf16[192,768]{1,0:T(8,128)(2,1)}, bf16[192,768]{1,0:T(8,128)(2,1)S(1)}, u32[]{:S(2)}, u32[]{:S(2)}) collective-permute-start(bf16[192,768]{1,0:T(8,128)(2,1)} %refs_4_.7), channel_id=1, source_target_pairs={{0,1},{1,0},{2,3},{3,2},{4,5},{5,4},{6,7},{7,6},{8,9},{9,8},{10,11... | collective-permute-start | bytes 884744 | tf_op jit(solution)/shard_map/ppermute | solution.py:245
  11.7 13.0 %collective-permute-start.7 = (bf16[192,768]{1,0:T(8,128)(2,1)S(1)}, bf16[192,768]{1,0:T(8,128)(2,1)S(1)}, u32[]{:S(2)}, u32[]{:S(2)}) collective-permute-start(bf16[192,768]{1,0:T(8,128)(2,1)S(1)} %collective-permute-done.5.refs_6_), channel_id=1, source_target_pairs={{0,1},{1,0},{2,3},{3,2},{4,5},{5,4},{6,7},{7,6},{8,9},{9,8},{10,11... | collective-permute-start | bytes 884744 | tf_op jit(solution)/shard_map/ppermute | solution.py:245
  22.6 19.6 %collective-permute-start.10 = (bf16[136,768]{1,0:T(8,128)(2,1)}, bf16[136,768]{1,0:T(8,128)(2,1)}, u32[]{:S(2)}, u32[]{:S(2)}) collective-permute-start(bf16[136,768]{1,0:T(8,128)(2,1)} %collective-permute-done.1.refs_0_), channel_id=1, source_target_pairs={{0,4},{4,0},{8,12},{12,8},{1,5},{5,1},{9,13},{13,9},{2,6},{6,2},{1... | collective-permute-start | bytes 626696 | tf_op jit(solution)/shard_map/ppermute | solution.py:245
  23.3 18.8 %collective-permute-start.12 = (bf16[136,768]{1,0:T(8,128)(2,1)S(1)}, bf16[136,768]{1,0:T(8,128)(2,1)S(1)}, u32[]{:S(2)}, u32[]{:S(2)}) collective-permute-start(bf16[136,768]{1,0:T(8,128)(2,1)S(1)} %collective-permute-done.refs_0_), channel_id=1, source_target_pairs={{0,1},{1,0},{2,3},{3,2},{4,5},{5,4},{6,7},{7,6},{8,9},{9,8},{10,11... | collective-permute-start | bytes 626696 | tf_op jit(solution)/shard_map/ppermute | solution.py:245
  41.6 14.8 %collective-permute-start.17 = (bf16[136,768]{1,0:T(8,128)(2,1)}, bf16[136,768]{1,0:T(8,128)(2,1)}, u32[]{:S(2)}, u32[]{:S(2)}) collective-permute-start(bf16[136,768]{1,0:T(8,128)(2,1)} %collective-permute-done.1.refs_0_), channel_id=1, source_target_pairs={{0,2},{1,3},{2,0},{3,1},{4,6},{5,7},{6,4},{7,5},{8,10},{9,11},{10,... | collective-permute-start | bytes 626696 | tf_op jit(solution)/shard_map/ppermute | solution.py:245
  56.0 19.2 %collective-permute-start.14 = (bf16[2,128,768]{2,1,0:T(8,128)(2,1)}, bf16[2,128,768]{2,1,0:T(8,128)(2,1)}, u32[]{:S(2)}, u32[]{:S(2)}) collective-permute-start(bf16[2,128,768]{2,1,0:T(8,128)(2,1)} %get-tuple-element.52), channel_id=1, source_target_pairs={{0,1},{1,0},{2,3},{3,2},{4,5},{5,4},{6,7},{7,6},{8,9},{9,8},{10,11... | collective-permute-start | bytes 1179656 | tf_op jit(solution)/shard_map/ppermute | solution.py:245
  56.4 7.5 %collective-permute-start.22 = (bf16[136,768]{1,0:T(8,128)(2,1)}, bf16[136,768]{1,0:T(8,128)(2,1)}, u32[]{:S(2)}, u32[]{:S(2)}) collective-permute-start(bf16[136,768]{1,0:T(8,128)(2,1)} %collective-permute-done.10.refs_0_), channel_id=1, source_target_pairs={{0,2},{1,3},{2,0},{3,1},{4,6},{5,7},{6,4},{7,5},{8,10},{9,11},{10,... | collective-permute-start | bytes 626696 | tf_op jit(solution)/shard_map/ppermute | solution.py:245
  57.0 6.9 %collective-permute-start.18 = (bf16[136,768]{1,0:T(8,128)(2,1)}, bf16[136,768]{1,0:T(8,128)(2,1)}, u32[]{:S(2)}, u32[]{:S(2)}) collective-permute-start(bf16[136,768]{1,0:T(8,128)(2,1)} %collective-permute-done.1.refs_0_), channel_id=1, source_target_pairs={{0,1},{1,0},{2,3},{3,2},{4,5},{5,4},{6,7},{7,6},{8,9},{9,8},{10,11... | collective-permute-start | bytes 626696 | tf_op jit(solution)/shard_map/ppermute | solution.py:245
  57.2 6.7 %collective-permute-start.19 = (bf16[136,768]{1,0:T(8,128)(2,1)}, bf16[136,768]{1,0:T(8,128)(2,1)}, u32[]{:S(2)}, u32[]{:S(2)}) collective-permute-start(bf16[136,768]{1,0:T(8,128)(2,1)} %collective-permute-done.17.refs_2_), channel_id=1, source_target_pairs={{0,1},{1,0},{2,3},{3,2},{4,5},{5,4},{6,7},{7,6},{8,9},{9,8},{10,11... | collective-permute-start | bytes 626696 | tf_op jit(solution)/shard_map/ppermute | solution.py:245
  57.5 30.4 %collective-permute-start.8 = (bf16[2,128,768]{2,1,0:T(8,128)(2,1)}, bf16[2,128,768]{2,1,0:T(8,128)(2,1)S(1)}, u32[]{:S(2)}, u32[]{:S(2)}) collective-permute-start(bf16[2,128,768]{2,1,0:T(8,128)(2,1)} %copy-done.19), channel_id=1, source_target_pairs={{0,1},{1,0},{2,3},{3,2},{4,5},{5,4},{6,7},{7,6},{8,9},{9,8},{10,11... | collective-permute-start | bytes 1179656 | tf_op jit(solution)/shard_map/ppermute | solution.py:245
  63.9 13.3 %collective-permute-start.23 = (bf16[136,768]{1,0:T(8,128)(2,1)}, bf16[136,768]{1,0:T(8,128)(2,1)S(1)}, u32[]{:S(2)}, u32[]{:S(2)}) collective-permute-start(bf16[136,768]{1,0:T(8,128)(2,1)} %collective-permute-done.10.refs_0_), channel_id=1, source_target_pairs={{0,1},{1,0},{2,3},{3,2},{4,5},{5,4},{6,7},{7,6},{8,9},{9,8},{10,11... | collective-permute-start | bytes 626696 | tf_op jit(solution)/shard_map/ppermute | solution.py:245
  76.2 12.9 %collective-permute-start.15 = (bf16[128,768]{1,0:T(8,128)(2,1)S(1)}, bf16[128,768]{1,0:T(8,128)(2,1)S(1)}, u32[]{:S(2)}, u32[]{:S(2)}) collective-permute-start(bf16[128,768]{1,0:T(8,128)(2,1)S(1)} %fusion.9), channel_id=1, source_target_pairs={{0,2},{1,3},{2,0},{3,1},{4,6},{5,7},{6,4},{7,5},{8,10},{9,11},{10,... | collective-permute-start | bytes 589832 | tf_op jit(solution)/shard_map/ppermute | solution.py:245
  87.9 39.8 %collective-permute-start.9 = (bf16[128,768]{1,0:T(8,128)(2,1)S(1)}, bf16[128,768]{1,0:T(8,128)(2,1)S(1)}, u32[]{:S(2)}, u32[]{:S(2)}) collective-permute-start(bf16[128,768]{1,0:T(8,128)(2,1)S(1)} %fusion.8), channel_id=1, source_target_pairs={{0,2},{1,3},{2,0},{3,1},{4,6},{5,7},{6,4},{7,5},{8,10},{9,11},{10,... | collective-permute-start | bytes 589832 | tf_op jit(solution)/shard_map/ppermute | solution.py:245
  90.1 37.7 %collective-permute-start.16 = (bf16[128,768]{1,0:T(8,128)(2,1)S(1)}, bf16[128,768]{1,0:T(8,128)(2,1)S(1)}, u32[]{:S(2)}, u32[]{:S(2)}) collective-permute-start(bf16[128,768]{1,0:T(8,128)(2,1)S(1)} %fusion.3), channel_id=1, source_target_pairs={{0,4},{4,0},{8,12},{12,8},{1,5},{5,1},{9,13},{13,9},{2,6},{6,2},{1... | collective-permute-start | bytes 589832 | tf_op jit(solution)/shard_map/ppermute | solution.py:245
  92.1 7.8 %collective-permute-start.26 = (bf16[128,768]{1,0:T(8,128)(2,1)S(1)}, bf16[128,768]{1,0:T(8,128)(2,1)S(1)}, u32[]{:S(2)}, u32[]{:S(2)}) collective-permute-start(bf16[128,768]{1,0:T(8,128)(2,1)S(1)} %fusion.11), channel_id=1, source_target_pairs={{0,2},{1,3},{2,0},{3,1},{4,6},{5,7},{6,4},{7,5},{8,10},{9,11},{10,... | collective-permute-start | bytes 589832 | tf_op jit(solution)/shard_map/ppermute | solution.py:245
  93.3 13.0 %collective-permute-start.30 = (bf16[192,768]{1,0:T(8,128)(2,1)S(1)}, bf16[192,768]{1,0:T(8,128)(2,1)S(1)}, u32[]{:S(2)}, u32[]{:S(2)}) collective-permute-start(bf16[192,768]{1,0:T(8,128)(2,1)S(1)} %fusion.7), channel_id=1, source_target_pairs={{0,2},{1,3},{2,0},{3,1},{4,6},{5,7},{6,4},{7,5},{8,10},{9,11},{10,... | collective-permute-start | bytes 884744 | tf_op jit(solution)/shard_map/ppermute | solution.py:245
  94.4 15.3 %collective-permute-start.21 = (bf16[128,768]{1,0:T(8,128)(2,1)S(1)}, bf16[128,768]{1,0:T(8,128)(2,1)S(1)}, u32[]{:S(2)}, u32[]{:S(2)}) collective-permute-start(bf16[128,768]{1,0:T(8,128)(2,1)S(1)} %fusion.10), channel_id=1, source_target_pairs={{0,2},{1,3},{2,0},{3,1},{4,6},{5,7},{6,4},{7,5},{8,10},{9,11},{10,... | collective-permute-start | bytes 589832 | tf_op jit(solution)/shard_map/ppermute | solution.py:245
  100.1 9.7 %collective-permute-start.27 = (bf16[128,768]{1,0:T(8,128)(2,1)S(1)}, bf16[128,768]{1,0:T(8,128)(2,1)S(1)}, u32[]{:S(2)}, u32[]{:S(2)}) collective-permute-start(bf16[128,768]{1,0:T(8,128)(2,1)S(1)} %fusion), channel_id=1, source_target_pairs={{0,4},{4,0},{8,12},{12,8},{1,5},{5,1},{9,13},{13,9},{2,6},{6,2},{1... | collective-permute-start | bytes 589832 | tf_op jit(solution)/shard_map/ppermute | solution.py:245
  109.9 17.9 %collective-permute-start.28 = (bf16[128,768]{1,0:T(8,128)(2,1)S(1)}, bf16[128,768]{1,0:T(8,128)(2,1)S(1)}, u32[]{:S(2)}, u32[]{:S(2)}) collective-permute-start(bf16[128,768]{1,0:T(8,128)(2,1)S(1)} %fusion.2), channel_id=1, source_target_pairs={{0,8},{4,12},{8,0},{12,4},{1,9},{5,13},{9,1},{13,5},{2,10},{6,14},... | collective-permute-start | bytes 589832 | tf_op jit(solution)/shard_map/ppermute | solution.py:245
  112.8 14.8 %collective-permute-start.32 = (bf16[96,768]{1,0:T(8,128)(2,1)S(1)}, bf16[96,768]{1,0:T(8,128)(2,1)S(1)}, u32[]{:S(2)}, u32[]{:S(2)}) collective-permute-start(bf16[96,768]{1,0:T(8,128)(2,1)S(1)} %add_convert_fusion.6), channel_id=1, source_target_pairs={{0,8},{4,12},{8,0},{12,4},{1,9},{5,13},{9,1},{13,5},{2,10},{6,14},... | collective-permute-start | bytes 442376 | tf_op jit(solution)/shard_map/ppermute | solution.py:245
  (52 other events, 284.6 us)

commit v6 on v5

v6 whole, which is shorter than its diff:
```python
import functools

import jax
import jax.numpy as jnp
from jax import lax
from jax.experimental import pallas as pl
from jax.experimental.pallas import tpu as pltpu
from jax.sharding import PartitionSpec as P

BLK = 128
EPSILON = 1e-06
META_ROWS = 8
F32 = jnp.float32
BF16 = jnp.bfloat16


def dot(a, b, da=1, db=0):
    return lax.dot_general(a, b, (((da,), (db,)), ((), ())), preferred_element_type=F32)


def pair_kernel(*refs, cap, pick_count, n_data, prior):
    it = iter(refs)
    take = lambda n: [next(it) for _ in range(n)]
    last = prior is not None
    sources, shards, label = take(n_data), take(n_data), next(it)
    prior_refs = take(2 * prior if last else 0)
    even_ref, odd_ref, grad_scores_ref, block_ref, embedding_ref, feats_ref, grad_hidden_ref = take(7)
    share_refs = take(2 if last else 0)
    enc = next(it)

    my_data = lax.axis_index("dp")
    me = (lax.axis_index("labels") * n_data + my_data).astype(F32)
    rows = sources[0].shape[0] - META_ROWS
    shard_rows = shards[0].shape[0]
    n_blocks = label.shape[0] // BLK
    slots = n_data * cap

    for m in range(n_data):
        enc[shard_at(my_data, m, shard_rows), :] = shards[m][...]

    row_id = lax.broadcasted_iota(jnp.int32, (rows, rows), 0)
    col_id = lax.broadcasted_iota(jnp.int32, (rows, rows), 1)
    before = (row_id < col_id).astype(BF16)
    slot_id = lax.broadcasted_iota(jnp.int32, (cap, rows), 0).astype(F32)
    column = lax.broadcasted_iota(jnp.int32, (slots, BLK), 1)

    hits, codes = [], []
    for source in sources:
        meta = source[rows:, 0 : 3 * rows].astype(F32)[:pick_count]
        named = meta[:, :rows] == me
        hits.append(jnp.sum(named.astype(F32), axis=0, keepdims=True))
        code = meta[:, rows : 2 * rows] * 256.0 + meta[:, 2 * rows :] + 1.0
        codes.append(jnp.sum(jnp.where(named, code, 0.0), axis=0, keepdims=True))
    rank = dot(jnp.concatenate(hits, axis=0).astype(BF16), before)

    picks, picked, slot_codes = [], [], []
    for m, source in enumerate(sources):
        pick = jnp.where((slot_id == rank[m : m + 1]) & (hits[m] > 0.0), 1.0, 0.0)
        slot_codes.append(jnp.sum(pick * codes[m], axis=1, keepdims=True))
        pick = pick.astype(BF16)
        picks.append(pick)
        picked.append(dot(pick, source[:rows, :]).astype(BF16))
    feats = jnp.concatenate(picked, axis=0)
    feats_ref[...] = feats
    code = jnp.concatenate(slot_codes, axis=0).astype(jnp.int32) - 1

    hidden = dot(feats, enc[...])
    inv_rms = lax.rsqrt(jnp.mean(hidden * hidden, axis=-1, keepdims=True) + EPSILON)
    embedding = (hidden * inv_rms).astype(BF16)
    embedding_ref[...] = embedding

    scores = dot(embedding, label[...], 1, 1)
    block = jnp.broadcast_to(code >> 8, (slots, BLK))
    block_ref[...] = block
    wanted = jnp.broadcast_to(code & 255, (slots, BLK))
    own_scores = jnp.zeros((slots, BLK), F32)
    for b in range(n_blocks):
        own_scores = jnp.where(block == b, scores[:, b * BLK : (b + 1) * BLK], own_scores)
    target = jnp.where(column == wanted, 1.0, 0.0)
    grad_scores = jnp.where(block >= 0, jax.nn.sigmoid(own_scores) - target, 0.0)
    grad_scores_ref[...] = grad_scores

    spread = jnp.concatenate(
        [jnp.where(block == b, grad_scores, 0.0).astype(BF16) for b in range(n_blocks)], axis=1
    )
    grad_pair = dot(spread, label[...]).astype(BF16).astype(F32)
    projection = jnp.mean(hidden * grad_pair, axis=-1, keepdims=True)
    grad_hidden = (inv_rms * grad_pair - hidden * (inv_rms**3 * projection)).astype(BF16)
    grad_hidden_ref[...] = grad_hidden

    if last:
        total = next(it)
        all_feats = jnp.concatenate([r[...] for r in prior_refs[:prior]] + [feats], axis=0)
        all_grads = jnp.concatenate([r[...] for r in prior_refs[prior:]] + [grad_hidden], axis=0)
        total[...] = dot(all_feats, all_grads, 0, 0)
        for m in range(n_data):
            part = total[shard_at(my_data, m, shard_rows), :]
            share_refs[m % 2][m // 2] = part.astype(BF16)

    grad_feats = dot(grad_hidden, enc[...], 1, 1).astype(BF16)
    for m in range(n_data):
        part = dot(picks[m], grad_feats[m * cap : (m + 1) * cap], 0, 0)
        (odd_ref if m % 2 else even_ref)[m // 2] = part.astype(BF16)


def grad_label_kernel(*refs):
    runs = (len(refs) - 1) // 3
    grad_scores, blocks, embeddings = refs[:runs], refs[runs : 2 * runs], refs[2 * runs : 3 * runs]
    out_ref = refs[-1]
    grad_scores_t = jnp.concatenate([r[...].T for r in grad_scores], axis=1)
    block_t = jnp.concatenate([r[...].T for r in blocks], axis=1)
    embedding = jnp.concatenate([r[...] for r in embeddings], axis=0)
    for b in range(out_ref.shape[0] // BLK):
        spread_t = jnp.where(block_t == b, grad_scores_t, 0.0).astype(BF16)
        out_ref[b * BLK : (b + 1) * BLK, :] = dot(spread_t, embedding).astype(BF16)


def half_at(mine, half):
    odd = jnp.bitwise_and(lax.axis_index("labels"), 1)
    return pl.ds(pl.multiple_of((odd if mine else 1 - odd) * half, 16), half)


def split_kernel(even_ref, got_ref, *refs):
    *more, keep_ref, send_ref, total = refs
    share = even_ref[0].astype(F32) + got_ref[0].astype(F32)
    for ref in more:
        share = share + ref[...].astype(F32)
    total[...] = share
    half = keep_ref.shape[0]
    keep_ref[...] = total[half_at(True, half), :]
    send_ref[...] = total[half_at(False, half), :].astype(BF16)


def merge_kernel(mine_ref, other_ref, out_ref):
    half = mine_ref.shape[0]
    out_ref[half_at(True, half), :] = mine_ref[...].astype(F32)
    out_ref[half_at(False, half), :] = other_ref[...].astype(F32)


def shard_at(my_data, m, shard_rows):
    at = jnp.bitwise_xor(my_data, m) * shard_rows
    return pl.ds(pl.multiple_of(at, 16), shard_rows)


def call(kernel, name, out_shape, scratch, flops, megabytes, *args):
    vmem = pl.BlockSpec(memory_space=pltpu.VMEM)
    return pl.pallas_call(
        kernel,
        in_specs=[vmem] * len(args),
        out_specs=jax.tree.map(lambda _: vmem, out_shape),
        out_shape=out_shape,
        scratch_shapes=scratch,
        compiler_params=pltpu.CompilerParams(vmem_limit_bytes=24 << 20),
        cost_estimate=pl.CostEstimate(
            flops=flops, bytes_accessed=megabytes << 20, transcendentals=0
        ),
        name=name,
    )(*args)


def pair_work(sources, shards, label_weight, cap, pick_count, prior=None):
    n_data = len(sources)
    block_rows, width = sources[0].shape
    rows = block_rows - META_ROWS
    slots = n_data * cap
    shard_rows = shards[0].shape[0]
    shapes = [((n_data // 2, rows, width), BF16)] * 2 + [((slots, BLK), F32)]
    shapes += [((slots, BLK), jnp.int32)] + [((slots, width), BF16)] * 3
    scratch = [pltpu.VMEM((n_data * shard_rows, width), BF16)]
    more = []
    if prior is not None:
        shapes += [((n_data // 2, shard_rows, width), BF16)] * 2
        more = [run[5] for run in prior] + [run[6] for run in prior]
        scratch += [pltpu.VMEM((n_data * shard_rows, width), F32)]
    return call(
        functools.partial(
            pair_kernel,
            cap=cap,
            pick_count=pick_count,
            n_data=n_data,
            prior=None if prior is None else len(prior),
        ),
        "pair_work",
        [jax.ShapeDtypeStruct(*shape) for shape in shapes],
        scratch,
        2 * slots * width * (2 * label_weight.shape[0] + 2 * width + 2 * rows),
        6,
        *sources,
        *shards,
        label_weight,
        *more,
    )


def grad_label_work(grad_scores, blocks, embeddings, label_weight):
    return call(
        grad_label_kernel,
        "grad_label_work",
        jax.ShapeDtypeStruct(label_weight.shape, BF16),
        [],
        2 * len(blocks) * blocks[0].shape[0] * label_weight.size,
        4,
        *grad_scores,
        *blocks,
        *embeddings,
    )


def swap(x):
    x = lax.all_to_all(x, "labels", split_axis=0, concat_axis=0, tiled=True)
    return lax.all_to_all(x, "dp", split_axis=1, concat_axis=1, tiled=True)


def partner(x, axis, mask):
    return lax.ppermute(x, axis, [(i, i ^ mask) for i in range(lax.axis_size(axis))])


def masks(n):
    return [1 << i for i in range(n.bit_length() - 1)]


def after(x, *others):
    return lax.optimization_barrier((x, *others))[0]


def gather_dp(x, first=None):
    got = {0: x}
    *far, near = reversed(masks(lax.axis_size("dp")))
    for mask in far:
        got.update({m | mask: partner(v, "dp", mask) for m, v in list(got.items())})
    for m, v in sorted(got.items(), reverse=True):
        if m:
            v = v if first is None else after(v, first)
        elif len(got) > 1:
            v = after(v, got[max(i for i in got if i & near == 0)])
        got[m | near] = partner(v, "dp", near)
    return [got[m] for m in range(len(got))]


def gather_labels(x):
    got = {0: x}
    for mask in reversed(masks(lax.axis_size("labels"))):
        got.update({m | mask: partner(v, "labels", mask) for m, v in list(got.items())})
    return [got[m] for m in range(len(got))]


def add(*terms):
    return sum(t.astype(F32) for t in terms)


def dp_terms(even, odd):
    got = partner(odd, "dp", 1)
    terms = [[even[i], got[i]] for i in range(even.shape[0])]
    for mask in masks(len(terms)):
        for i in range(len(terms)):
            if i & mask == 0 and i % mask == 0:
                terms[i].append(partner(add(*terms[i | mask]).astype(BF16), "dp", 2 * mask))
    return got, terms[0]


def reduce_dp(even, odd):
    return add(*dp_terms(even, odd)[1])


def sum_shares(even, odd):
    got, terms = dp_terms(even, odd)
    rows, width = even.shape[1:]
    half = rows // 2
    keep, send = call(
        split_kernel,
        "split_share",
        [jax.ShapeDtypeStruct((half, width), F32), jax.ShapeDtypeStruct((half, width), BF16)],
        [pltpu.VMEM((rows, width), F32)],
        0,
        1,
        even,
        got,
        *terms[2:],
    )
    x = add(keep, partner(send, "labels", 1)).astype(BF16)
    for mask in masks(lax.axis_size("labels"))[1:]:
        x = add(x, partner(x, "labels", mask)).astype(BF16)
    other = partner(x, "labels", 1)
    out = jax.ShapeDtypeStruct((rows, width), F32)
    return keep, call(merge_kernel, "merge_share", out, [], 0, 1, x, other)


def reduce_labels(parts):
    terms = [[part] for part in parts]
    for mask in masks(len(terms)):
        for i in range(len(terms)):
            if i & mask == 0 and i % mask == 0:
                terms[i].append(partner(add(*terms[i | mask]).astype(BF16), "labels", mask))
    return add(*terms[0])


def with_meta(feats, owner_rows, block_rows, positive_rows):
    meta = jnp.concatenate([owner_rows, block_rows, positive_rows], axis=1).astype(BF16)
    meta = jnp.pad(meta, ((0, META_ROWS - meta.shape[0]), (0, feats.shape[1] - meta.shape[1])))
    return jnp.concatenate([feats, meta], axis=0)


def local(feats, enc_weight, label_weight, owners, blocks, positives):
    n_labels = lax.axis_size("labels")
    n_data = lax.axis_size("dp")
    n_owner = n_labels * n_data
    row_count, width = feats.shape
    pick_count = owners.shape[1]
    cap = max(2, 2 * row_count * pick_count // n_owner)
    shards = gather_dp(enc_weight)

    if row_count <= n_data * cap:
        own = with_meta(feats, owners.T, blocks.T, positives.T)
        rows_of = gather_labels(own)
        work = []
        for by in range(n_labels):
            run = gather_dp(rows_of[by], work[-1][0] if work else None)
            if by + 1 < n_labels:
                run[0] = after(run[0], *rows_of[by + 1 : by + 3])
            prior = work if by == n_labels - 1 else None
            work.append(pair_work(run, shards, label_weight, cap, pick_count, prior))
        grad_feats = reduce_labels([reduce_dp(*run[:2]) for run in work]).astype(BF16)
    else:
        flat = owners.reshape(-1)
        onehot = (flat[:, None] == jnp.arange(n_owner, dtype=jnp.int32)[None, :]).astype(jnp.int32)
        rank = jnp.sum((jnp.cumsum(onehot, axis=0) - onehot) * onehot, axis=1)
        slot = (flat * cap + rank).reshape(row_count, pick_count)
        slot_total = n_owner * cap
        slots = jnp.arange(slot_total, dtype=jnp.int32)
        place = slots[:, None, None] == slot[None]
        pick = jnp.any(place, axis=2).astype(BF16)
        live = jnp.any(place, axis=(1, 2))
        block_of = jnp.sum(jnp.where(place, blocks[None], 0), axis=(1, 2))
        wanted = jnp.sum(jnp.where(place, positives[None], 0), axis=(1, 2))
        owner_of = jnp.where(live, slots // cap, -1)
        out = dot(pick, feats).astype(BF16).reshape(n_labels, n_data, cap, width)
        meta = jnp.stack([owner_of, block_of, wanted], axis=1).reshape(n_labels, n_data, cap, 3)
        tile = 128
        got = swap(out).reshape(slot_total // tile, tile, width)
        got_meta = swap(meta).reshape(slot_total // tile, tile, 3).transpose(0, 2, 1)
        sources = [
            with_meta(got[i], got_meta[i, 0:1], got_meta[i, 1:2], got_meta[i, 2:3])
            for i in range(slot_total // tile)
        ]
        work = []
        for i in range(0, len(sources), n_data):
            prior = work if i + n_data == len(sources) else None
            run = sources[i : i + n_data]
            work.append(pair_work(run, shards, label_weight, tile, 1, prior))
        back = jnp.stack([part for run in work for part in run[:2]])
        back = back.reshape(-1, 2, n_data // 2, tile, width).transpose(0, 2, 1, 3, 4)
        back = swap(back.reshape(n_labels, n_data, cap, width)).reshape(slot_total, width)
        grad_feats = dot(pick, back, 0, 0).astype(BF16)

    _, _, grad_scores, block_of, embedding, _, _ = zip(*(run[:7] for run in work))
    keep, grad_enc = sum_shares(*work[-1][7:])
    embedding = (after(embedding[0], keep),) + embedding[1:]
    grad_label = grad_label_work(grad_scores, block_of, embedding, label_weight)
    return (grad_feats, grad_label, grad_enc)


def solution(mesh):
    rows = P(("groups", "labels", "dp"), None)
    return jax.shard_map(
        local,
        mesh=mesh,
        in_specs=(rows, P("dp", None), rows, rows, rows, rows),
        out_specs=(rows, rows, P(("groups", "dp"), None)),
        check_vma=False,
    )
```

time: 134 us -> 96.6 us (0.72)
  local copies, waits for them, and re-layouts: 22.3 us -> 2.37 us
  Pallas kernels: 36.8 us -> 18.2 us
  waiting for transfers between devices: 38.4 us -> 44.5 us
  other arithmetic: 6.63 us -> 3.77 us
  starting transfers between devices: 28.6 us -> 26.8 us
    unnamed x84 -> x8, local copies, waits for them, and re-layouts: 22.3 us -> 2.37 us
    pallas_call x5 -> x7, Pallas kernels: 36.8 us -> 18.2 us  [call(): pl.pallas_call(kernel, in_specs=[vmem] * len(args), out_specs=jax.tree.ma...]
    ppermute x34, waiting for transfers between devices: 38.4 us -> 44.5 us  [partner(): lax.ppermute(x, axis, [(i, i ^ mask) for i in range(lax.axis_size(axis))])]
    ppermute x34, starting transfers between devices: 28.6 us -> 26.8 us  [partner(): lax.ppermute(x, axis, [(i, i ^ mask) for i in range(lax.axis_size(axis))])]
    convert_element_type x8 -> x7, other arithmetic: 2.11 us -> 0.33 us  [the longest x5 0.26 us: dp_terms(): terms[i].append(partner(add(*terms[i | mask]).astype(BF16), 'dp', 2 * mask))]
  transfers between devices with their start and end apart: 34 -> 34, of which waited for: 11 -> 10; matrix products, arithmetic and copies ran while one was open for 4% -> 4% of each run, Pallas kernels for 28% -> 18%
where the time goes in v6:
time: 96.6 us; the launch traced here: 96.4 us
  waiting for transfers between devices  44.5 us (46%)
  starting transfers between devices  26.8 us (28%)
  Pallas kernels  18.2 us (19%)
  other arithmetic  3.77 us (4%)
  local copies, waits for them, and re-layouts  2.37 us (2%)
    ppermute x34, waiting for transfers between devices, partner(): lax.ppermute(x, axis, [(i, i ^ mask) for i in range(lax.axis_size(axis))])  44.5 us
    ppermute x34, starting transfers between devices, partner(): lax.ppermute(x, axis, [(i, i ^ mask) for i in range(lax.axis_size(axis))])  26.8 us
    pallas_call x7, Pallas kernels, call(): pl.pallas_call(kernel, in_specs=[vmem] * len(args), out_specs=jax.tree.ma...  18.2 us
    unnamed x8, local copies, waits for them, and re-layouts  2.37 us
  transfers between devices with their start and end apart: 34, of which 10 were waited for; matrix products, arithmetic and copies ran while one was open for 4% of the time, Pallas kernels for 18%

profile of v6, /device:TPU:0, one launch (start us, length us, event | category | flops | bytes accessed | tf_op | source)
XLA Modules:
  0.0 96.4 jit_solution(2154774896811714137)
XLA Ops:
  0.6 3.0 %collective-permute-start.5 = (bf16[192,768]{1,0:T(8,128)(2,1)}, bf16[192,768]{1,0:T(8,128)(2,1)S(1)}, u32[]{:S(2)}, u32[]{:S(2)}) collective-permute-start(bf16[192,768]{1,0:T(8,128)(2,1)} %refs_4_.7), channel_id=1, source_target_pairs={{0,2},{1,3},{2,0},{3,1},{4,6},{5,7},{6,4},{7,5},{8,10},{9,11},{10,... | collective-permute-start | bytes 884744 | tf_op jit(solution)/shard_map/ppermute | solution.py:215
  6.0 1.6 %collective-permute-start = (bf16[136,768]{1,0:T(8,128)(2,1)S(1)}, bf16[136,768]{1,0:T(8,128)(2,1)S(1)}, u32[]{:S(2)}, u32[]{:S(2)}) collective-permute-start(bf16[136,768]{1,0:T(8,128)(2,1)S(1)} %pad_maximum_fusion.refs_0_), channel_id=1, source_target_pairs={{0,4},{4,0},{8,12},{12,8},{1,5},{5,1},{9,13},{13,9},{2,6},{6,2},{1... | collective-permute-start | bytes 626696 | tf_op jit(solution)/shard_map/ppermute | solution.py:215
  8.2 2.6 %collective-permute-start.1 = (bf16[136,768]{1,0:T(8,128)(2,1)S(1)}, bf16[136,768]{1,0:T(8,128)(2,1)S(1)}, u32[]{:S(2)}, u32[]{:S(2)}) collective-permute-start(bf16[136,768]{1,0:T(8,128)(2,1)S(1)} %pad_maximum_fusion.refs_0_), channel_id=1, source_target_pairs={{0,8},{4,12},{8,0},{12,4},{1,9},{5,13},{9,1},{13,5},{2,10},{6,14},... | collective-permute-start | bytes 626696 | tf_op jit(solution)/shard_map/ppermute | solution.py:215
  12.2 4.6 %collective-permute-done.refs_0_ = bf16[136,768]{1,0:T(8,128)(2,1)S(1)} collective-permute-done((bf16[136,768]{1,0:T(8,128)(2,1)S(1)}, bf16[136,768]{1,0:T(8,128)(2,1)S(1)}, u32[]{:S(2)}, u32[]{:S(2)}) %collective-permute-start) | collective-permute-done | bytes 208928 | tf_op jit(solution)/shard_map/ppermute | solution.py:215
  16.8 2.8 %collective-permute-done.1.refs_0_ = bf16[136,768]{1,0:T(8,128)(2,1)S(1)} collective-permute-done((bf16[136,768]{1,0:T(8,128)(2,1)S(1)}, bf16[136,768]{1,0:T(8,128)(2,1)S(1)}, u32[]{:S(2)}, u32[]{:S(2)}) %collective-permute-start.1) | collective-permute-done | bytes 208928 | tf_op jit(solution)/shard_map/ppermute | solution.py:215
  19.7 2.9 %collective-permute-done.11.refs_2_ = bf16[136,768]{1,0:T(8,128)(2,1)S(1)} collective-permute-done((bf16[136,768]{1,0:T(8,128)(2,1)S(1)}, bf16[136,768]{1,0:T(8,128)(2,1)S(1)}, u32[]{:S(2)}, u32[]{:S(2)}) %collective-permute-start.11) | collective-permute-done | bytes 208928 | tf_op jit(solution)/shard_map/ppermute | solution.py:215
  23.2 1.4 %copy-done = bf16[1024,768]{1,0:T(8,128)(2,1)S(1)} copy-done((bf16[1024,768]{1,0:T(8,128)(2,1)S(1)}, bf16[1024,768]{1,0:T(8,128)(2,1)}, u32[]{:S(2)}) %copy-start) | copy-done | bytes 1572888
  25.5 3.1 %pair_work.4 = (bf16[2,128,768]{2,1,0:T(8,128)(2,1)S(1)}, bf16[2,128,768]{2,1,0:T(8,128)(2,1)S(1)}, f32[256,128]{1,0:T(8,128)S(1)}, s32[256,128]{1,0:T(8,128)S(1...) custom-call(bf16[136,768]{1,0:T(8,128)(2,1)S(1)} %pad_maximum_fusion.refs_0_, ...), custom_call_target="tpu_custom_call" | custom-call | flops 1509949440 | bytes 6291456 | tf_op jit(solution)/shard_map/pair_work/pallas_call | solution.py:147
  29.2 1.6 %collective-permute-start.22 = (bf16[136,768]{1,0:T(8,128)(2,1)S(1)}, bf16[136,768]{1,0:T(8,128)(2,1)S(1)}, u32[]{:S(2)}, u32[]{:S(2)}) collective-permute-start(bf16[136,768]{1,0:T(8,128)(2,1)S(1)} %collective-permute-done.10.refs_0_), channel_id=1, source_target_pairs={{0,2},{1,3},{2,0},{3,1},{4,6},{5,7},{6,4},{7,5},{8,10},{9,11},{10,... | collective-permute-start | bytes 626696 | tf_op jit(solution)/shard_map/ppermute | solution.py:215
  31.0 3.1 %pair_work.5 = (bf16[2,128,768]{2,1,0:T(8,128)(2,1)S(1)}, bf16[2,128,768]{2,1,0:T(8,128)(2,1)S(1)}, f32[256,128]{1,0:T(8,128)S(1)}, s32[256,128]{1,0:T(8,128)S(1...) custom-call(bf16[136,768]{1,0:T(8,128)(2,1)S(1)} %collective-permute-done.refs_0_, ...), custom_call_target="tpu_custom_call" | custom-call | flops 1509949440 | bytes 6291456 | tf_op jit(solution)/shard_map/pair_work/pallas_call | solution.py:147
  34.5 2.2 %collective-permute-done.22.refs_2_ = bf16[136,768]{1,0:T(8,128)(2,1)S(1)} collective-permute-done((bf16[136,768]{1,0:T(8,128)(2,1)S(1)}, bf16[136,768]{1,0:T(8,128)(2,1)S(1)}, u32[]{:S(2)}, u32[]{:S(2)}) %collective-permute-start.22) | collective-permute-done | bytes 208928 | tf_op jit(solution)/shard_map/ppermute | solution.py:215
  37.3 3.1 %pair_work.6 = (bf16[2,128,768]{2,1,0:T(8,128)(2,1)S(1)}, bf16[2,128,768]{2,1,0:T(8,128)(2,1)S(1)}, f32[256,128]{1,0:T(8,128)S(1)}, s32[256,128]{1,0:T(8,128)S(1...) custom-call(bf16[136,768]{1,0:T(8,128)(2,1)S(1)} %collective-permute-done.1.refs_0_, ...), custom_call_target="tpu_custom_call" | custom-call | flops 1509949440 | bytes 6291456 | tf_op jit(solution)/shard_map/pair_work/pallas_call | solution.py:147
  41.0 1.7 %collective-permute-start.9 = (bf16[128,768]{1,0:T(8,128)(2,1)S(1)}, bf16[128,768]{1,0:T(8,128)(2,1)S(1)}, u32[]{:S(2)}, u32[]{:S(2)}) collective-permute-start(bf16[128,768]{1,0:T(8,128)(2,1)S(1)} %fusion.8), channel_id=1, source_target_pairs={{0,2},{1,3},{2,0},{3,1},{4,6},{5,7},{6,4},{7,5},{8,10},{9,11},{10,... | collective-permute-start | bytes 589832 | tf_op jit(solution)/shard_map/ppermute | solution.py:215
  42.7 4.7 %pair_work.7 = (bf16[2,128,768]{2,1,0:T(8,128)(2,1)S(1)}, bf16[2,128,768]{2,1,0:T(8,128)(2,1)S(1)}, f32[256,128]{1,0:T(8,128)S(1)}, s32[256,128]{1,0:T(8,128)S(1...) custom-call(bf16[136,768]{1,0:T(8,128)(2,1)S(1)} %collective-permute, ...), custom_call_target="tpu_custom_call" | custom-call | flops 1509949440 | bytes 6291456 | tf_op jit(solution)/shard_map/pair_work/pallas_call | solution.py:147
  48.9 1.5 %collective-permute-start.21 = (bf16[128,768]{1,0:T(8,128)(2,1)S(1)}, bf16[128,768]{1,0:T(8,128)(2,1)S(1)}, u32[]{:S(2)}, u32[]{:S(2)}) collective-permute-start(bf16[128,768]{1,0:T(8,128)(2,1)S(1)} %fusion.10), channel_id=1, source_target_pairs={{0,2},{1,3},{2,0},{3,1},{4,6},{5,7},{6,4},{7,5},{8,10},{9,11},{10,... | collective-permute-start | bytes 589832 | tf_op jit(solution)/shard_map/ppermute | solution.py:215
  52.6 11.6 %collective-permute-done.26 = bf16[128,768]{1,0:T(8,128)(2,1)S(1)} collective-permute-done((bf16[128,768]{1,0:T(8,128)(2,1)S(1)}, bf16[128,768]{1,0:T(8,128)(2,1)S(1)}, u32[]{:S(2)}, u32[]{:S(2)}) %collective-permute-start.26) | collective-permute-done | bytes 196640 | tf_op jit(solution)/shard_map/ppermute | solution.py:215
  64.3 2.0 %collective-permute-start.27 = (bf16[128,768]{1,0:T(8,128)(2,1)S(1)}, bf16[128,768]{1,0:T(8,128)(2,1)S(1)}, u32[]{:S(2)}, u32[]{:S(2)}) collective-permute-start(bf16[128,768]{1,0:T(8,128)(2,1)S(1)} %fusion), channel_id=1, source_target_pairs={{0,4},{4,0},{8,12},{12,8},{1,5},{5,1},{9,13},{13,9},{2,6},{6,2},{1... | collective-permute-start | bytes 589832 | tf_op jit(solution)/shard_map/ppermute | solution.py:215
  66.5 3.0 %collective-permute-done.30.refs_0_ = bf16[192,768]{1,0:T(8,128)(2,1)S(1)} collective-permute-done((bf16[192,768]{1,0:T(8,128)(2,1)S(1)}, bf16[192,768]{1,0:T(8,128)(2,1)S(1)}, u32[]{:S(2)}, u32[]{:S(2)}) %collective-permute-start.30) | collective-permute-done | bytes 294944 | tf_op jit(solution)/shard_map/ppermute | solution.py:215
  69.8 2.0 %collective-permute-start.31 = (bf16[96,768]{1,0:T(8,128)(2,1)S(1)}, bf16[96,768]{1,0:T(8,128)(2,1)S(1)}, u32[]{:S(2)}, u32[]{:S(2)}) collective-permute-start(bf16[96,768]{1,0:T(8,128)(2,1)S(1)} %get-tuple-element.86), channel_id=1, source_target_pairs={{0,4},{4,0},{8,12},{12,8},{1,5},{5,1},{9,13},{13,9},{2,6},{6,2},{1... | collective-permute-start | bytes 442376 | tf_op jit(solution)/shard_map/ppermute | solution.py:215
  71.9 2.7 %collective-permute-start.28 = (bf16[128,768]{1,0:T(8,128)(2,1)S(1)}, bf16[128,768]{1,0:T(8,128)(2,1)S(1)}, u32[]{:S(2)}, u32[]{:S(2)}) collective-permute-start(bf16[128,768]{1,0:T(8,128)(2,1)S(1)} %fusion.2), channel_id=1, source_target_pairs={{0,8},{4,12},{8,0},{12,4},{1,9},{5,13},{9,1},{13,5},{2,10},{6,14},... | collective-permute-start | bytes 589832 | tf_op jit(solution)/shard_map/ppermute | solution.py:215
  74.6 6.6 %collective-permute-done.31 = bf16[96,768]{1,0:T(8,128)(2,1)S(1)} collective-permute-done((bf16[96,768]{1,0:T(8,128)(2,1)S(1)}, bf16[96,768]{1,0:T(8,128)(2,1)S(1)}, u32[]{:S(2)}, u32[]{:S(2)}) %collective-permute-start.31) | collective-permute-done | bytes 147488 | tf_op jit(solution)/shard_map/ppermute | solution.py:215
  81.7 3.2 %grad_label_work.1 = bf16[1024,768]{1,0:T(8,128)(2,1)} custom-call(f32[256,128]{1,0:T(8,128)S(1)} %get-tuple-element.70.refs_0_, f32[256,128]{1,0:T(8,128)S(1)} %get-tuple-element.71.refs_1_, f32[256,128]{1,0:T(8,128)S(1)} %get-tuple-element.72.refs_2_, f32[256,128]{1,0:T(8,128)S(1)} %get-tuple-element.73.refs_3_, s32[256,128]{1,0:T(8,128)S(1)} %get-tuple-element.74.refs_4_, ...), custom_call_target="tpu_custom_call" | custom-call | flops 1610612736 | bytes 4194304 | tf_op jit(solution)/shard_map/grad_label_work/pallas_call | solution.py:147
  84.8 4.8 %collective-permute-done.32 = bf16[96,768]{1,0:T(8,128)(2,1)S(1)} collective-permute-done((bf16[96,768]{1,0:T(8,128)(2,1)S(1)}, bf16[96,768]{1,0:T(8,128)(2,1)S(1)}, u32[]{:S(2)}, u32[]{:S(2)}) %collective-permute-start.32) | collective-permute-done | bytes 147488 | tf_op jit(solution)/shard_map/ppermute | solution.py:215
  90.6 4.9 %collective-permute-done.33.other_ref = bf16[96,768]{1,0:T(8,128)(2,1)S(1)} collective-permute-done((bf16[96,768]{1,0:T(8,128)(2,1)S(1)}, bf16[96,768]{1,0:T(8,128)(2,1)S(1)}, u32[]{:S(2)}, u32[]{:S(2)}) %collective-permute-start.33) | collective-permute-done | bytes 147488 | tf_op jit(solution)/shard_map/ppermute | solution.py:215
  (74 shorter events, 14.8 us)
Async XLA Ops:
  0.6 11.1 %collective-permute-start.5 = (bf16[192,768]{1,0:T(8,128)(2,1)}, bf16[192,768]{1,0:T(8,128)(2,1)S(1)}, u32[]{:S(2)}, u32[]{:S(2)}) collective-permute-start(bf16[192,768]{1,0:T(8,128)(2,1)} %refs_4_.7), channel_id=1, source_target_pairs={{0,2},{1,3},{2,0},{3,1},{4,6},{5,7},{6,4},{7,5},{8,10},{9,11},{10,... | collective-permute-start | bytes 884744 | tf_op jit(solution)/shard_map/ppermute | solution.py:215
  6.0 10.8 %collective-permute-start = (bf16[136,768]{1,0:T(8,128)(2,1)S(1)}, bf16[136,768]{1,0:T(8,128)(2,1)S(1)}, u32[]{:S(2)}, u32[]{:S(2)}) collective-permute-start(bf16[136,768]{1,0:T(8,128)(2,1)S(1)} %pad_maximum_fusion.refs_0_), channel_id=1, source_target_pairs={{0,4},{4,0},{8,12},{12,8},{1,5},{5,1},{9,13},{13,9},{2,6},{6,2},{1... | collective-permute-start | bytes 626696 | tf_op jit(solution)/shard_map/ppermute | solution.py:215
  7.7 9.2 %collective-permute-start.2 = (bf16[136,768]{1,0:T(8,128)(2,1)S(1)}, bf16[136,768]{1,0:T(8,128)(2,1)S(1)}, u32[]{:S(2)}, u32[]{:S(2)}) collective-permute-start(bf16[136,768]{1,0:T(8,128)(2,1)S(1)} %pad_maximum_fusion.refs_0_), channel_id=1, source_target_pairs={{0,2},{1,3},{2,0},{3,1},{4,6},{5,7},{6,4},{7,5},{8,10},{9,11},{10,... | collective-permute-start | bytes 626696 | tf_op jit(solution)/shard_map/ppermute | solution.py:215
  8.2 11.5 %collective-permute-start.1 = (bf16[136,768]{1,0:T(8,128)(2,1)S(1)}, bf16[136,768]{1,0:T(8,128)(2,1)S(1)}, u32[]{:S(2)}, u32[]{:S(2)}) collective-permute-start(bf16[136,768]{1,0:T(8,128)(2,1)S(1)} %pad_maximum_fusion.refs_0_), channel_id=1, source_target_pairs={{0,8},{4,12},{8,0},{12,4},{1,9},{5,13},{9,1},{13,5},{2,10},{6,14},... | collective-permute-start | bytes 626696 | tf_op jit(solution)/shard_map/ppermute | solution.py:215
  11.7 11.5 %collective-permute-start.6 = (bf16[192,768]{1,0:T(8,128)(2,1)}, bf16[192,768]{1,0:T(8,128)(2,1)S(1)}, u32[]{:S(2)}, u32[]{:S(2)}) collective-permute-start(bf16[192,768]{1,0:T(8,128)(2,1)} %refs_4_.7), channel_id=1, source_target_pairs={{0,1},{1,0},{2,3},{3,2},{4,5},{5,4},{6,7},{7,6},{8,9},{9,8},{10,11... | collective-permute-start | bytes 884744 | tf_op jit(solution)/shard_map/ppermute | solution.py:215
  11.7 11.5 %collective-permute-start.7 = (bf16[192,768]{1,0:T(8,128)(2,1)S(1)}, bf16[192,768]{1,0:T(8,128)(2,1)S(1)}, u32[]{:S(2)}, u32[]{:S(2)}) collective-permute-start(bf16[192,768]{1,0:T(8,128)(2,1)S(1)} %collective-permute-done.5.refs_6_), channel_id=1, source_target_pairs={{0,1},{1,0},{2,3},{3,2},{4,5},{5,4},{6,7},{7,6},{8,9},{9,8},{10,11... | collective-permute-start | bytes 884744 | tf_op jit(solution)/shard_map/ppermute | solution.py:215
  22.6 6.5 %collective-permute-start.17 = (bf16[136,768]{1,0:T(8,128)(2,1)S(1)}, bf16[136,768]{1,0:T(8,128)(2,1)S(1)}, u32[]{:S(2)}, u32[]{:S(2)}) collective-permute-start(bf16[136,768]{1,0:T(8,128)(2,1)S(1)} %collective-permute-done.1.refs_0_), channel_id=1, source_target_pairs={{0,2},{1,3},{2,0},{3,1},{4,6},{5,7},{6,4},{7,5},{8,10},{9,11},{10,... | collective-permute-start | bytes 626696 | tf_op jit(solution)/shard_map/ppermute | solution.py:215
  22.6 6.6 %collective-permute-start.10 = (bf16[136,768]{1,0:T(8,128)(2,1)S(1)}, bf16[136,768]{1,0:T(8,128)(2,1)S(1)}, u32[]{:S(2)}, u32[]{:S(2)}) collective-permute-start(bf16[136,768]{1,0:T(8,128)(2,1)S(1)} %collective-permute-done.1.refs_0_), channel_id=1, source_target_pairs={{0,4},{4,0},{8,12},{12,8},{1,5},{5,1},{9,13},{13,9},{2,6},{6,2},{1... | collective-permute-start | bytes 626696 | tf_op jit(solution)/shard_map/ppermute | solution.py:215
  23.1 7.9 %collective-permute-start.12 = (bf16[136,768]{1,0:T(8,128)(2,1)S(1)}, bf16[136,768]{1,0:T(8,128)(2,1)S(1)}, u32[]{:S(2)}, u32[]{:S(2)}) collective-permute-start(bf16[136,768]{1,0:T(8,128)(2,1)S(1)} %collective-permute-done.refs_0_), channel_id=1, source_target_pairs={{0,1},{1,0},{2,3},{3,2},{4,5},{5,4},{6,7},{7,6},{8,9},{9,8},{10,11... | collective-permute-start | bytes 626696 | tf_op jit(solution)/shard_map/ppermute | solution.py:215
  29.2 8.1 %collective-permute-start.18 = (bf16[136,768]{1,0:T(8,128)(2,1)S(1)}, bf16[136,768]{1,0:T(8,128)(2,1)S(1)}, u32[]{:S(2)}, u32[]{:S(2)}) collective-permute-start(bf16[136,768]{1,0:T(8,128)(2,1)S(1)} %collective-permute-done.1.refs_0_), channel_id=1, source_target_pairs={{0,1},{1,0},{2,3},{3,2},{4,5},{5,4},{6,7},{7,6},{8,9},{9,8},{10,11... | collective-permute-start | bytes 626696 | tf_op jit(solution)/shard_map/ppermute | solution.py:215
  29.2 7.5 %collective-permute-start.22 = (bf16[136,768]{1,0:T(8,128)(2,1)S(1)}, bf16[136,768]{1,0:T(8,128)(2,1)S(1)}, u32[]{:S(2)}, u32[]{:S(2)}) collective-permute-start(bf16[136,768]{1,0:T(8,128)(2,1)S(1)} %collective-permute-done.10.refs_0_), channel_id=1, source_target_pairs={{0,2},{1,3},{2,0},{3,1},{4,6},{5,7},{6,4},{7,5},{8,10},{9,11},{10,... | collective-permute-start | bytes 626696 | tf_op jit(solution)/shard_map/ppermute | solution.py:215
  30.9 10.1 %collective-permute-start.8 = (bf16[2,128,768]{2,1,0:T(8,128)(2,1)S(1)}, bf16[2,128,768]{2,1,0:T(8,128)(2,1)S(1)}, u32[]{:S(2)}, u32[]{:S(2)}) collective-permute-start(bf16[2,128,768]{2,1,0:T(8,128)(2,1)S(1)} %get-tuple-element.49), channel_id=1, source_target_pairs={{0,1},{1,0},{2,3},{3,2},{4,5},{5,4},{6,7},{7,6},{8,9},{9,8},{10,11... | collective-permute-start | bytes 1179656 | tf_op jit(solution)/shard_map/ppermute | solution.py:215
  36.8 11.1 %collective-permute-start.14 = (bf16[2,128,768]{2,1,0:T(8,128)(2,1)S(1)}, bf16[2,128,768]{2,1,0:T(8,128)(2,1)S(1)}, u32[]{:S(2)}, u32[]{:S(2)}) collective-permute-start(bf16[2,128,768]{2,1,0:T(8,128)(2,1)S(1)} %get-tuple-element.54), channel_id=1, source_target_pairs={{0,1},{1,0},{2,3},{3,2},{4,5},{5,4},{6,7},{7,6},{8,9},{9,8},{10,11... | collective-permute-start | bytes 1179656 | tf_op jit(solution)/shard_map/ppermute | solution.py:215
  40.4 8.4 %collective-permute-start.20 = (bf16[2,128,768]{2,1,0:T(8,128)(2,1)S(1)}, bf16[2,128,768]{2,1,0:T(8,128)(2,1)S(1)}, u32[]{:S(2)}, u32[]{:S(2)}) collective-permute-start(bf16[2,128,768]{2,1,0:T(8,128)(2,1)S(1)} %get-tuple-element.59), channel_id=1, source_target_pairs={{0,1},{1,0},{2,3},{3,2},{4,5},{5,4},{6,7},{7,6},{8,9},{9,8},{10,11... | collective-permute-start | bytes 1179656 | tf_op jit(solution)/shard_map/ppermute | solution.py:215
  41.0 48.8 %collective-permute-start.9 = (bf16[128,768]{1,0:T(8,128)(2,1)S(1)}, bf16[128,768]{1,0:T(8,128)(2,1)S(1)}, u32[]{:S(2)}, u32[]{:S(2)}) collective-permute-start(bf16[128,768]{1,0:T(8,128)(2,1)S(1)} %fusion.8), channel_id=1, source_target_pairs={{0,2},{1,3},{2,0},{3,1},{4,6},{5,7},{6,4},{7,5},{8,10},{9,11},{10,... | collective-permute-start | bytes 589832 | tf_op jit(solution)/shard_map/ppermute | solution.py:215
  48.0 18.4 %collective-permute-start.15 = (bf16[128,768]{1,0:T(8,128)(2,1)S(1)}, bf16[128,768]{1,0:T(8,128)(2,1)S(1)}, u32[]{:S(2)}, u32[]{:S(2)}) collective-permute-start(bf16[128,768]{1,0:T(8,128)(2,1)S(1)} %fusion.9), channel_id=1, source_target_pairs={{0,2},{1,3},{2,0},{3,1},{4,6},{5,7},{6,4},{7,5},{8,10},{9,11},{10,... | collective-permute-start | bytes 589832 | tf_op jit(solution)/shard_map/ppermute | solution.py:215
  48.9 22.9 %collective-permute-start.21 = (bf16[128,768]{1,0:T(8,128)(2,1)S(1)}, bf16[128,768]{1,0:T(8,128)(2,1)S(1)}, u32[]{:S(2)}, u32[]{:S(2)}) collective-permute-start(bf16[128,768]{1,0:T(8,128)(2,1)S(1)} %fusion.10), channel_id=1, source_target_pairs={{0,2},{1,3},{2,0},{3,1},{4,6},{5,7},{6,4},{7,5},{8,10},{9,11},{10,... | collective-permute-start | bytes 589832 | tf_op jit(solution)/shard_map/ppermute | solution.py:215
  50.4 13.8 %collective-permute-start.26 = (bf16[128,768]{1,0:T(8,128)(2,1)S(1)}, bf16[128,768]{1,0:T(8,128)(2,1)S(1)}, u32[]{:S(2)}, u32[]{:S(2)}) collective-permute-start(bf16[128,768]{1,0:T(8,128)(2,1)S(1)} %fusion.11), channel_id=1, source_target_pairs={{0,2},{1,3},{2,0},{3,1},{4,6},{5,7},{6,4},{7,5},{8,10},{9,11},{10,... | collective-permute-start | bytes 589832 | tf_op jit(solution)/shard_map/ppermute | solution.py:215
  51.4 18.2 %collective-permute-start.30 = (bf16[192,768]{1,0:T(8,128)(2,1)S(1)}, bf16[192,768]{1,0:T(8,128)(2,1)S(1)}, u32[]{:S(2)}, u32[]{:S(2)}) collective-permute-start(bf16[192,768]{1,0:T(8,128)(2,1)S(1)} %fusion.7), channel_id=1, source_target_pairs={{0,2},{1,3},{2,0},{3,1},{4,6},{5,7},{6,4},{7,5},{8,10},{9,11},{10,... | collective-permute-start | bytes 884744 | tf_op jit(solution)/shard_map/ppermute | solution.py:215
  64.3 7.5 %collective-permute-start.27 = (bf16[128,768]{1,0:T(8,128)(2,1)S(1)}, bf16[128,768]{1,0:T(8,128)(2,1)S(1)}, u32[]{:S(2)}, u32[]{:S(2)}) collective-permute-start(bf16[128,768]{1,0:T(8,128)(2,1)S(1)} %fusion), channel_id=1, source_target_pairs={{0,4},{4,0},{8,12},{12,8},{1,5},{5,1},{9,13},{13,9},{2,6},{6,2},{1... | collective-permute-start | bytes 589832 | tf_op jit(solution)/shard_map/ppermute | solution.py:215
  66.4 23.4 %collective-permute-start.16 = (bf16[128,768]{1,0:T(8,128)(2,1)S(1)}, bf16[128,768]{1,0:T(8,128)(2,1)S(1)}, u32[]{:S(2)}, u32[]{:S(2)}) collective-permute-start(bf16[128,768]{1,0:T(8,128)(2,1)S(1)} %fusion.3), channel_id=1, source_target_pairs={{0,4},{4,0},{8,12},{12,8},{1,5},{5,1},{9,13},{13,9},{2,6},{6,2},{1... | collective-permute-start | bytes 589832 | tf_op jit(solution)/shard_map/ppermute | solution.py:215
  69.8 11.4 %collective-permute-start.31 = (bf16[96,768]{1,0:T(8,128)(2,1)S(1)}, bf16[96,768]{1,0:T(8,128)(2,1)S(1)}, u32[]{:S(2)}, u32[]{:S(2)}) collective-permute-start(bf16[96,768]{1,0:T(8,128)(2,1)S(1)} %get-tuple-element.86), channel_id=1, source_target_pairs={{0,4},{4,0},{8,12},{12,8},{1,5},{5,1},{9,13},{13,9},{2,6},{6,2},{1... | collective-permute-start | bytes 442376 | tf_op jit(solution)/shard_map/ppermute | solution.py:215
  71.9 17.9 %collective-permute-start.28 = (bf16[128,768]{1,0:T(8,128)(2,1)S(1)}, bf16[128,768]{1,0:T(8,128)(2,1)S(1)}, u32[]{:S(2)}, u32[]{:S(2)}) collective-permute-start(bf16[128,768]{1,0:T(8,128)(2,1)S(1)} %fusion.2), channel_id=1, source_target_pairs={{0,8},{4,12},{8,0},{12,4},{1,9},{5,13},{9,1},{13,5},{2,10},{6,14},... | collective-permute-start | bytes 589832 | tf_op jit(solution)/shard_map/ppermute | solution.py:215
  81.2 8.5 %collective-permute-start.32 = (bf16[96,768]{1,0:T(8,128)(2,1)S(1)}, bf16[96,768]{1,0:T(8,128)(2,1)S(1)}, u32[]{:S(2)}, u32[]{:S(2)}) collective-permute-start(bf16[96,768]{1,0:T(8,128)(2,1)S(1)} %add_convert_fusion.6), channel_id=1, source_target_pairs={{0,8},{4,12},{8,0},{12,4},{1,9},{5,13},{9,1},{13,5},{2,10},{6,14},... | collective-permute-start | bytes 442376 | tf_op jit(solution)/shard_map/ppermute | solution.py:215
  (14 other events, 75.4 us)

commit v7 on v6

--- a/solution.py
+++ b/solution.py
@@ -18,24 +18,24 @@
     return lax.dot_general(a, b, (((da,), (db,)), ((), ())), preferred_element_type=F32)
 
 
-def pair_kernel(*refs, cap, pick_count, n_data, prior):
+def pair_kernel(*refs, cap, pick_count, n_data, first, prior):
     it = iter(refs)
     take = lambda n: [next(it) for _ in range(n)]
     last = prior is not None
-    sources, shards, label = take(n_data), take(n_data), next(it)
+    sources, shards, label = take(n_data), take(n_data if first else 1), next(it)
     prior_refs = take(2 * prior if last else 0)
     even_ref, odd_ref, grad_scores_ref, block_ref, embedding_ref, feats_ref, grad_hidden_ref = take(7)
+    enc = next(it) if first else shards[0]
     share_refs = take(2 if last else 0)
-    enc = next(it)
 
     my_data = lax.axis_index("dp")
     me = (lax.axis_index("labels") * n_data + my_data).astype(F32)
     rows = sources[0].shape[0] - META_ROWS
-    shard_rows = shards[0].shape[0]
+    shard_rows = enc.shape[0] // n_data
     n_blocks = label.shape[0] // BLK
     slots = n_data * cap
 
-    for m in range(n_data):
+    for m in range(n_data if first else 0):
         enc[shard_at(my_data, m, shard_rows), :] = shards[m][...]
 
     row_id = lax.broadcasted_iota(jnp.int32, (rows, rows), 0)
@@ -113,6 +113,21 @@
     for b in range(out_ref.shape[0] // BLK):
         spread_t = jnp.where(block_t == b, grad_scores_t, 0.0).astype(BF16)
         out_ref[b * BLK : (b + 1) * BLK, :] = dot(spread_t, embedding).astype(BF16)
+
+
+def own_block_kernel(feats_ref, owners_ref, blocks_ref, positives_ref, out_ref):
+    rows, width = feats_ref.shape
+    out_ref[:rows, :] = feats_ref[...]
+    meta = [r[...].astype(F32) for r in (owners_ref, blocks_ref, positives_ref)]
+    meta += [jnp.zeros((meta[0].shape[0], width - 3 * rows), F32)]
+    meta = jnp.concatenate(meta, axis=1)
+    rest = jnp.zeros((META_ROWS - meta.shape[0], width), F32)
+    out_ref[rows:, :] = jnp.concatenate([meta, rest], axis=0).astype(BF16)
+
+
+def load_kernel(label_ref, shard_ref, label_out, shard_out):
+    label_out[...] = label_ref[...]
+    shard_out[...] = shard_ref[...]
 
 
 def half_at(mine, half):
@@ -158,27 +173,32 @@
     )(*args)
 
 
-def pair_work(sources, shards, label_weight, cap, pick_count, prior=None):
+def pair_work(sources, shards, label_weight, cap, pick_count, before, last):
     n_data = len(sources)
     block_rows, width = sources[0].shape
     rows = block_rows - META_ROWS
     slots = n_data * cap
     shard_rows = shards[0].shape[0]
+    full = (n_data * shard_rows, width)
     shapes = [((n_data // 2, rows, width), BF16)] * 2 + [((slots, BLK), F32)]
     shapes += [((slots, BLK), jnp.int32)] + [((slots, width), BF16)] * 3
-    scratch = [pltpu.VMEM((n_data * shard_rows, width), BF16)]
-    more = []
-    if prior is not None:
+    scratch, more = [], []
+    if before:
+        shards = before[0][7:8]
+    else:
+        shapes += [(full, BF16)]
+    if last:
         shapes += [((n_data // 2, shard_rows, width), BF16)] * 2
-        more = [run[5] for run in prior] + [run[6] for run in prior]
-        scratch += [pltpu.VMEM((n_data * shard_rows, width), F32)]
+        more = [run[5] for run in before] + [run[6] for run in before]
+        scratch = [pltpu.VMEM(full, F32)]
     return call(
         functools.partial(
             pair_kernel,
             cap=cap,
             pick_count=pick_count,
             n_data=n_data,
-            prior=None if prior is None else len(prior),
+            first=not before,
+            prior=len(before) if last else None,
         ),
         "pair_work",
         [jax.ShapeDtypeStruct(*shape) for shape in shapes],
@@ -223,18 +243,16 @@
     return lax.optimization_barrier((x, *others))[0]
 
 
-def gather_dp(x, first=None):
+def gather_far(x):
     got = {0: x}
-    *far, near = reversed(masks(lax.axis_size("dp")))
-    for mask in far:
+    for mask in reversed(masks(lax.axis_size("dp"))[1:]):
         got.update({m | mask: partner(v, "dp", mask) for m, v in list(got.items())})
-    for m, v in sorted(got.items(), reverse=True):
-        if m:
-            v = v if first is None else after(v, first)
-        elif len(got) > 1:
-            v = after(v, got[max(i for i in got if i & near == 0)])
-        got[m | near] = partner(v, "dp", near)
-    return [got[m] for m in range(len(got))]
+    return [got[m] for m in sorted(got)]
+
+
+def gather_near(far, *first):
+    near = [partner(after(v, *first, *far[1:]), "dp", 1) for v in far]
+    return [v for pair in zip(far, near) for v in pair]
 
 
 def gather_labels(x):
@@ -256,10 +274,6 @@
             if i & mask == 0 and i % mask == 0:
                 terms[i].append(partner(add(*terms[i | mask]).astype(BF16), "dp", 2 * mask))
     return got, terms[0]
-
-
-def reduce_dp(even, odd):
-    return add(*dp_terms(even, odd)[1])
 
 
 def sum_shares(even, odd):
@@ -285,13 +299,29 @@
     return keep, call(merge_kernel, "merge_share", out, [], 0, 1, x, other)
 
 
-def reduce_labels(parts):
-    terms = [[part] for part in parts]
-    for mask in masks(len(terms)):
-        for i in range(len(terms)):
-            if i & mask == 0 and i % mask == 0:
-                terms[i].append(partner(add(*terms[i | mask]).astype(BF16), "labels", mask))
-    return add(*terms[0])
+def both_cores(run):
+    return [run[0], partner(run[1], "dp", 1)]
+
+
+def reduce_runs(terms):
+    n = len(terms)
+    held = ()
+    for i in reversed(range(0, n, 2)):
+        sent = after(add(*terms[i + 1]).astype(BF16), *held)
+        held = (partner(sent, "labels", 1),)
+        terms[i].append(*held)
+    sums = {}
+    for i in range(0, n, 2):
+        parts = [[t[h] for t in terms[i]] for h in range(terms[i][0].shape[0])]
+        for mask in masks(len(parts)):
+            for h in range(0, len(parts), 2 * mask):
+                sent = add(*parts[h + mask]).astype(BF16)
+                parts[h].append(partner(sent, "dp", 2 * mask))
+        sums[i] = parts[0]
+    for mask in masks(n)[1:]:
+        for i in range(0, n, 2 * mask):
+            sums[i].append(partner(add(*sums[i + mask]).astype(BF16), "labels", mask))
+    return add(*sums[0]).astype(BF16)
 
 
 def with_meta(feats, owner_rows, block_rows, positive_rows):
@@ -307,19 +337,44 @@
     row_count, width = feats.shape
     pick_count = owners.shape[1]
     cap = max(2, 2 * row_count * pick_count // n_owner)
-    shards = gather_dp(enc_weight)
 
     if row_count <= n_data * cap:
-        own = with_meta(feats, owners.T, blocks.T, positives.T)
-        rows_of = gather_labels(own)
-        work = []
+        own = call(
+            own_block_kernel,
+            "own_block",
+            jax.ShapeDtypeStruct((row_count + META_ROWS, width), BF16),
+            [],
+            0,
+            1,
+            feats,
+            owners.T,
+            blocks.T,
+            positives.T,
+        )
+        near = gather_labels(own)
+        far = [gather_far(block) for block in near]
+        shards = gather_near(gather_far(after(enc_weight, own)))
+        label_weight, shards[0] = call(
+            load_kernel,
+            "load",
+            [jax.ShapeDtypeStruct(x.shape, BF16) for x in (label_weight, enc_weight)],
+            [],
+            0,
+            4,
+            after(label_weight, near[1]),
+            enc_weight,
+        )
+        waits = {0: [near[-1]] + [x for blocks in far[1:-1] for x in blocks[1:]], 1: far[-1][1:]}
+        work, terms = [], []
         for by in range(n_labels):
-            run = gather_dp(rows_of[by], work[-1][0] if work else None)
-            if by + 1 < n_labels:
-                run[0] = after(run[0], *rows_of[by + 1 : by + 3])
-            prior = work if by == n_labels - 1 else None
-            work.append(pair_work(run, shards, label_weight, cap, pick_count, prior))
-        grad_feats = reduce_labels([reduce_dp(*run[:2]) for run in work]).astype(BF16)
+            run = gather_near(far[by])
+            run[0] = after(run[0], *waits.get(by, []))
+            run_work = pair_work(
+                run, shards, label_weight, cap, pick_count, work, by == n_labels - 1
+            )
+            work.append(run_work)
+            terms.append(both_cores(run_work))
+        grad_feats = reduce_runs(terms)
     else:
         flat = owners.reshape(-1)
         onehot = (flat[:, None] == jnp.arange(n_owner, dtype=jnp.int32)[None, :]).astype(jnp.int32)
@@ -333,6 +388,7 @@
         block_of = jnp.sum(jnp.where(place, blocks[None], 0), axis=(1, 2))
         wanted = jnp.sum(jnp.where(place, positives[None], 0), axis=(1, 2))
         owner_of = jnp.where(live, slots // cap, -1)
+        shards = gather_near(gather_far(enc_weight))
         out = dot(pick, feats).astype(BF16).reshape(n_labels, n_data, cap, width)
         meta = jnp.stack([owner_of, block_of, wanted], axis=1).reshape(n_labels, n_data, cap, 3)
         tile = 128
@@ -344,16 +400,16 @@
         ]
         work = []
         for i in range(0, len(sources), n_data):
-            prior = work if i + n_data == len(sources) else None
+            last = i + n_data == len(sources)
             run = sources[i : i + n_data]
-            work.append(pair_work(run, shards, label_weight, tile, 1, prior))
+            work.append(pair_work(run, shards, label_weight, tile, 1, work, last))
         back = jnp.stack([part for run in work for part in run[:2]])
         back = back.reshape(-1, 2, n_data // 2, tile, width).transpose(0, 2, 1, 3, 4)
         back = swap(back.reshape(n_labels, n_data, cap, width)).reshape(slot_total, width)
         grad_feats = dot(pick, back, 0, 0).astype(BF16)
 
     _, _, grad_scores, block_of, embedding, _, _ = zip(*(run[:7] for run in work))
-    keep, grad_enc = sum_shares(*work[-1][7:])
+    keep, grad_enc = sum_shares(*work[-1][-2:])
     embedding = (after(embedding[0], keep),) + embedding[1:]
     grad_label = grad_label_work(grad_scores, block_of, embedding, label_weight)
     return (grad_feats, grad_label, grad_enc)

time: 96.6 us -> 99.1 us (1.026)
  local copies, waits for them, and re-layouts: 2.37 us -> 5.33 us
  other arithmetic: 3.77 us -> 1.38 us
  waiting for transfers between devices: 44.5 us -> 45.6 us
    unnamed x8 -> x12, local copies, waits for them, and re-layouts: 2.37 us -> 5.33 us
    transpose x2 -> x0, other arithmetic: 1.39 us -> none  [local(): own = with_meta(feats, owners.T, blocks.T, positives.T)]
    ppermute x34 -> x32, waiting for transfers between devices: 44.5 us -> 45.6 us  [partner(): lax.ppermute(x, axis, [(i, i ^ mask) for i in range(lax.axis_size(axis))])]
    concatenate x2 -> x0, other arithmetic: 1 us -> none  [the longest x1 0.99 us: with_meta(): return jnp.concatenate([feats, meta], axis=0)]
    ppermute x34 -> x32, starting transfers between devices: 26.8 us -> 27.4 us  [partner(): lax.ppermute(x, axis, [(i, i ^ mask) for i in range(lax.axis_size(axis))])]
    pallas_call x7 -> x9, Pallas kernels: 18.2 us -> 18.1 us  [call(): pl.pallas_call(kernel, in_specs=[vmem] * len(args), out_specs=jax.tree.ma...]
  transfers between devices with their start and end apart: 34 -> 32, of which waited for: 10 -> 11; matrix products, arithmetic and copies ran while one was open for 4% -> 1% of each run, Pallas kernels for 18% -> 14%
where the time goes in v7:
time: 99.1 us; the launch traced here: 98.8 us
  waiting for transfers between devices  45.6 us (46%)
  starting transfers between devices  27.4 us (28%)
  Pallas kernels  18.1 us (18%)
  local copies, waits for them, and re-layouts  5.33 us (5%)
  other arithmetic  1.38 us (1%)
    ppermute x32, waiting for transfers between devices, partner(): lax.ppermute(x, axis, [(i, i ^ mask) for i in range(lax.axis_size(axis))])  45.6 us
    ppermute x32, starting transfers between devices, partner(): lax.ppermute(x, axis, [(i, i ^ mask) for i in range(lax.axis_size(axis))])  27.4 us
    pallas_call x9, Pallas kernels, call(): pl.pallas_call(kernel, in_specs=[vmem] * len(args), out_specs=jax.tree.ma...  18.1 us
    unnamed x12, local copies, waits for them, and re-layouts  5.33 us
  transfers between devices with their start and end apart: 32, of which 11 were waited for; matrix products, arithmetic and copies ran while one was open for 1% of the time, Pallas kernels for 14%

profile of v7, /device:TPU:0, one launch (start us, length us, event | category | flops | bytes accessed | tf_op | source)
XLA Modules:
  0.0 98.8 jit_solution(13892286541569886343)
XLA Ops:
  3.6 3.0 %collective-permute-start.5 = (bf16[136,768]{1,0:T(8,128)(2,1)S(1)}, bf16[136,768]{1,0:T(8,128)(2,1)S(1)}, u32[]{:S(2)}, u32[]{:S(2)}) collective-permute-start(bf16[136,768]{1,0:T(8,128)(2,1)S(1)} %own_block.1.refs_0_), channel_id=1, source_target_pairs={{0,2},{1,3},{2,0},{3,1},{4,6},{5,7},{6,4},{7,5},{8,10},{9,11},{10,... | collective-permute-start | bytes 626696 | tf_op jit(solution)/shard_map/ppermute | solution.py:235
  6.6 2.6 %collective-permute-start = (bf16[136,768]{1,0:T(8,128)(2,1)S(1)}, bf16[136,768]{1,0:T(8,128)(2,1)S(1)}, u32[]{:S(2)}, u32[]{:S(2)}) collective-permute-start(bf16[136,768]{1,0:T(8,128)(2,1)S(1)} %own_block.1.refs_0_), channel_id=1, source_target_pairs={{0,8},{4,12},{8,0},{12,4},{1,9},{5,13},{9,1},{13,5},{2,10},{6,14},... | collective-permute-start | bytes 626696 | tf_op jit(solution)/shard_map/ppermute | solution.py:235
  9.8 1.6 %collective-permute-start.2 = (bf16[136,768]{1,0:T(8,128)(2,1)S(1)}, bf16[136,768]{1,0:T(8,128)(2,1)S(1)}, u32[]{:S(2)}, u32[]{:S(2)}) collective-permute-start(bf16[136,768]{1,0:T(8,128)(2,1)S(1)} %own_block.1.refs_0_), channel_id=1, source_target_pairs={{0,4},{4,0},{8,12},{12,8},{1,5},{5,1},{9,13},{13,9},{2,6},{6,2},{1... | collective-permute-start | bytes 626696 | tf_op jit(solution)/shard_map/ppermute | solution.py:235
  12.2 6.5 %collective-permute-done.refs_0_ = bf16[136,768]{1,0:T(8,128)(2,1)S(1)} collective-permute-done((bf16[136,768]{1,0:T(8,128)(2,1)S(1)}, bf16[136,768]{1,0:T(8,128)(2,1)S(1)}, u32[]{:S(2)}, u32[]{:S(2)}) %collective-permute-start) | collective-permute-done | bytes 208928 | tf_op jit(solution)/shard_map/ppermute | solution.py:235
  20.5 4.2 %collective-permute-done.4.refs_2_ = bf16[136,768]{1,0:T(8,128)(2,1)S(1)} collective-permute-done((bf16[136,768]{1,0:T(8,128)(2,1)S(1)}, bf16[136,768]{1,0:T(8,128)(2,1)S(1)}, u32[]{:S(2)}, u32[]{:S(2)}) %collective-permute-start.4) | collective-permute-done | bytes 208928 | tf_op jit(solution)/shard_map/ppermute | solution.py:235
  25.2 1.7 %collective-permute-done.1.refs_0_ = bf16[136,768]{1,0:T(8,128)(2,1)S(1)} collective-permute-done((bf16[136,768]{1,0:T(8,128)(2,1)S(1)}, bf16[136,768]{1,0:T(8,128)(2,1)S(1)}, u32[]{:S(2)}, u32[]{:S(2)}) %collective-permute-start.1) | collective-permute-done | bytes 208928 | tf_op jit(solution)/shard_map/ppermute | solution.py:235
  26.8 1.5 %collective-permute-start.12 = (bf16[136,768]{1,0:T(8,128)(2,1)S(1)}, bf16[136,768]{1,0:T(8,128)(2,1)S(1)}, u32[]{:S(2)}, u32[]{:S(2)}) collective-permute-start(bf16[136,768]{1,0:T(8,128)(2,1)S(1)} %collective-permute-done.1.refs_0_), channel_id=1, source_target_pairs={{0,2},{1,3},{2,0},{3,1},{4,6},{5,7},{6,4},{7,5},{8,10},{9,11},{10,... | collective-permute-start | bytes 626696 | tf_op jit(solution)/shard_map/ppermute | solution.py:235
  28.4 4.0 %collective-permute-done.3.refs_2_ = bf16[136,768]{1,0:T(8,128)(2,1)S(1)} collective-permute-done((bf16[136,768]{1,0:T(8,128)(2,1)S(1)}, bf16[136,768]{1,0:T(8,128)(2,1)S(1)}, u32[]{:S(2)}, u32[]{:S(2)}) %collective-permute-start.3) | collective-permute-done | bytes 208928 | tf_op jit(solution)/shard_map/ppermute | solution.py:235
  32.3 1.4 %copy-done = bf16[1024,768]{1,0:T(8,128)(2,1)S(1)} copy-done((bf16[1024,768]{1,0:T(8,128)(2,1)S(1)}, bf16[1024,768]{1,0:T(8,128)(2,1)}, u32[]{:S(2)}) %copy-start) | copy-done | bytes 1572888
  35.5 3.1 %pair_work.4 = (bf16[2,128,768]{2,1,0:T(8,128)(2,1)S(1)}, bf16[2,128,768]{2,1,0:T(8,128)(2,1)S(1)}, f32[256,128]{1,0:T(8,128)S(1)}, s32[256,128]{1,0:T(8,128)S(1...) custom-call(bf16[136,768]{1,0:T(8,128)(2,1)S(1)} %own_block.1.refs_0, ...), custom_call_target="tpu_custom_call" | custom-call | flops 1509949440 | bytes 6291456 | tf_op jit(solution)/shard_map/pair_work/pallas_call | solution.py:162
  39.2 3.0 %pair_work.6 = (bf16[2,128,768]{2,1,0:T(8,128)(2,1)S(1)}, bf16[2,128,768]{2,1,0:T(8,128)(2,1)S(1)}, f32[256,128]{1,0:T(8,128)S(1)}, s32[256,128]{1,0:T(8,128)S(1...) custom-call(bf16[136,768]{1,0:T(8,128)(2,1)S(1)} %collective-permute-done.refs_0_, ...), custom_call_target="tpu_custom_call" | custom-call | flops 1509949440 | bytes 6291456 | tf_op jit(solution)/shard_map/pair_work/pallas_call | solution.py:162
  42.2 3.0 %pair_work.5 = (bf16[2,128,768]{2,1,0:T(8,128)(2,1)S(1)}, bf16[2,128,768]{2,1,0:T(8,128)(2,1)S(1)}, f32[256,128]{1,0:T(8,128)S(1)}, s32[256,128]{1,0:T(8,128)S(1...) custom-call(bf16[136,768]{1,0:T(8,128)(2,1)S(1)} %collective-permute-done.2.refs_0_, ...), custom_call_target="tpu_custom_call" | custom-call | flops 1509949440 | bytes 6291456 | tf_op jit(solution)/shard_map/pair_work/pallas_call | solution.py:162
  45.3 4.6 %pair_work.7 = (bf16[2,128,768]{2,1,0:T(8,128)(2,1)S(1)}, bf16[2,128,768]{2,1,0:T(8,128)(2,1)S(1)}, f32[256,128]{1,0:T(8,128)S(1)}, s32[256,128]{1,0:T(8,128)S(1...) custom-call(bf16[136,768]{1,0:T(8,128)(2,1)S(1)} %collective-permute, ...), custom_call_target="tpu_custom_call" | custom-call | flops 1509949440 | bytes 6291456 | tf_op jit(solution)/shard_map/pair_work/pallas_call | solution.py:162
  51.8 2.2 %collective-permute-start.21 = (bf16[2,128,768]{2,1,0:T(8,128)(2,1)S(1)}, bf16[2,128,768]{2,1,0:T(8,128)(2,1)S(1)}, u32[]{:S(2)}, u32[]{:S(2)}) collective-permute-start(bf16[2,128,768]{2,1,0:T(8,128)(2,1)S(1)} %add_convert_fusion), channel_id=1, source_target_pairs={{0,4},{4,0},{8,12},{12,8},{1,5},{5,1},{9,13},{13,9},{2,6},{6,2},{1... | collective-permute-start | bytes 1179656 | tf_op jit(solution)/shard_map/ppermute | solution.py:235
  55.3 8.3 %collective-permute-done.21 = bf16[2,128,768]{2,1,0:T(8,128)(2,1)S(1)} collective-permute-done((bf16[2,128,768]{2,1,0:T(8,128)(2,1)S(1)}, bf16[2,128,768]{2,1,0:T(8,128)(2,1)S(1)}, u32[]{:S(2)}, u32[]{:S(2)}) %collective-permute-start.21) | collective-permute-done | bytes 393248 | tf_op jit(solution)/shard_map/ppermute | solution.py:235
  64.8 1.8 %collective-permute-start.22 = (bf16[2,128,768]{2,1,0:T(8,128)(2,1)S(1)}, bf16[2,128,768]{2,1,0:T(8,128)(2,1)S(1)}, u32[]{:S(2)}, u32[]{:S(2)}) collective-permute-start(bf16[2,128,768]{2,1,0:T(8,128)(2,1)S(1)} %add_convert_fusion.1), channel_id=1, source_target_pairs={{0,4},{4,0},{8,12},{12,8},{1,5},{5,1},{9,13},{13,9},{2,6},{6,2},{1... | collective-permute-start | bytes 1179656 | tf_op jit(solution)/shard_map/ppermute | solution.py:235
  67.1 3.5 %collective-permute-done.25 = bf16[128,768]{1,0:T(8,128)(2,1)S(1)} collective-permute-done((bf16[128,768]{1,0:T(8,128)(2,1)S(1)}, bf16[128,768]{1,0:T(8,128)(2,1)S(1)}, u32[]{:S(2)}, u32[]{:S(2)}) %collective-permute-start.25) | collective-permute-done | bytes 196640 | tf_op jit(solution)/shard_map/ppermute | solution.py:235
  70.7 3.4 %collective-permute-start.26 = (bf16[128,768]{1,0:T(8,128)(2,1)S(1)}, bf16[128,768]{1,0:T(8,128)(2,1)S(1)}, u32[]{:S(2)}, u32[]{:S(2)}) collective-permute-start(bf16[128,768]{1,0:T(8,128)(2,1)S(1)} %fusion), channel_id=1, source_target_pairs={{0,8},{4,12},{8,0},{12,4},{1,9},{5,13},{9,1},{13,5},{2,10},{6,14},... | collective-permute-start | bytes 589832 | tf_op jit(solution)/shard_map/ppermute | solution.py:235
  74.2 8.6 %collective-permute-done.29 = bf16[96,768]{1,0:T(8,128)(2,1)S(1)} collective-permute-done((bf16[96,768]{1,0:T(8,128)(2,1)S(1)}, bf16[96,768]{1,0:T(8,128)(2,1)S(1)}, u32[]{:S(2)}, u32[]{:S(2)}) %collective-permute-start.29) | collective-permute-done | bytes 147488 | tf_op jit(solution)/shard_map/ppermute | solution.py:235
  82.8 2.5 %collective-permute-start.30 = (bf16[96,768]{1,0:T(8,128)(2,1)S(1)}, bf16[96,768]{1,0:T(8,128)(2,1)S(1)}, u32[]{:S(2)}, u32[]{:S(2)}) collective-permute-start(bf16[96,768]{1,0:T(8,128)(2,1)S(1)} %add_convert_fusion.6), channel_id=1, source_target_pairs={{0,8},{4,12},{8,0},{12,4},{1,9},{5,13},{9,1},{13,5},{2,10},{6,14},... | collective-permute-start | bytes 442376 | tf_op jit(solution)/shard_map/ppermute | solution.py:235
  85.3 1.4 %collective-permute-start.23 = (bf16[128,768]{1,0:T(8,128)(2,1)S(1)}, bf16[128,768]{1,0:T(8,128)(2,1)S(1)}, u32[]{:S(2)}, u32[]{:S(2)}) collective-permute-start(bf16[128,768]{1,0:T(8,128)(2,1)S(1)} %fusion.4), channel_id=1, source_target_pairs={{0,2},{1,3},{2,0},{3,1},{4,6},{5,7},{6,4},{7,5},{8,10},{9,11},{10,... | collective-permute-start | bytes 589832 | tf_op jit(solution)/shard_map/ppermute | solution.py:235
  86.7 5.1 %collective-permute-done.30 = bf16[96,768]{1,0:T(8,128)(2,1)S(1)} collective-permute-done((bf16[96,768]{1,0:T(8,128)(2,1)S(1)}, bf16[96,768]{1,0:T(8,128)(2,1)S(1)}, u32[]{:S(2)}, u32[]{:S(2)}) %collective-permute-start.30) | collective-permute-done | bytes 147488 | tf_op jit(solution)/shard_map/ppermute | solution.py:235
  92.0 3.2 %grad_label_work.1 = bf16[1024,768]{1,0:T(8,128)(2,1)} custom-call(f32[256,128]{1,0:T(8,128)S(1)} %get-tuple-element.84.refs_0_, f32[256,128]{1,0:T(8,128)S(1)} %get-tuple-element.85.refs_1_, f32[256,128]{1,0:T(8,128)S(1)} %get-tuple-element.86.refs_2_, f32[256,128]{1,0:T(8,128)S(1)} %get-tuple-element.87.refs_3_, s32[256,128]{1,0:T(8,128)S(1)} %get-tuple-element.88.refs_4_, ...), custom_call_target="tpu_custom_call" | custom-call | flops 1610612736 | bytes 4194304 | tf_op jit(solution)/shard_map/grad_label_work/pallas_call | solution.py:162
  95.2 2.0 %collective-permute-done.31.other_ref = bf16[96,768]{1,0:T(8,128)(2,1)S(1)} collective-permute-done((bf16[96,768]{1,0:T(8,128)(2,1)S(1)}, bf16[96,768]{1,0:T(8,128)(2,1)S(1)}, u32[]{:S(2)}, u32[]{:S(2)}) %collective-permute-start.31) | collective-permute-done | bytes 147488 | tf_op jit(solution)/shard_map/ppermute | solution.py:235
  (70 shorter events, 15.6 us)
Async XLA Ops:
  3.6 8.6 %collective-permute-start.5 = (bf16[136,768]{1,0:T(8,128)(2,1)S(1)}, bf16[136,768]{1,0:T(8,128)(2,1)S(1)}, u32[]{:S(2)}, u32[]{:S(2)}) collective-permute-start(bf16[136,768]{1,0:T(8,128)(2,1)S(1)} %own_block.1.refs_0_), channel_id=1, source_target_pairs={{0,2},{1,3},{2,0},{3,1},{4,6},{5,7},{6,4},{7,5},{8,10},{9,11},{10,... | collective-permute-start | bytes 626696 | tf_op jit(solution)/shard_map/ppermute | solution.py:235
  6.6 12.1 %collective-permute-start = (bf16[136,768]{1,0:T(8,128)(2,1)S(1)}, bf16[136,768]{1,0:T(8,128)(2,1)S(1)}, u32[]{:S(2)}, u32[]{:S(2)}) collective-permute-start(bf16[136,768]{1,0:T(8,128)(2,1)S(1)} %own_block.1.refs_0_), channel_id=1, source_target_pairs={{0,8},{4,12},{8,0},{12,4},{1,9},{5,13},{9,1},{13,5},{2,10},{6,14},... | collective-permute-start | bytes 626696 | tf_op jit(solution)/shard_map/ppermute | solution.py:235
  9.2 10.0 %collective-permute-start.8 = (bf16[192,768]{1,0:T(8,128)(2,1)}, bf16[192,768]{1,0:T(8,128)(2,1)S(1)}, u32[]{:S(2)}, u32[]{:S(2)}) collective-permute-start(bf16[192,768]{1,0:T(8,128)(2,1)} %shard_ref.1), channel_id=1, source_target_pairs={{0,2},{1,3},{2,0},{3,1},{4,6},{5,7},{6,4},{7,5},{8,10},{9,11},{10,... | collective-permute-start | bytes 884744 | tf_op jit(solution)/shard_map/ppermute | solution.py:235
  9.8 10.0 %collective-permute-start.2 = (bf16[136,768]{1,0:T(8,128)(2,1)S(1)}, bf16[136,768]{1,0:T(8,128)(2,1)S(1)}, u32[]{:S(2)}, u32[]{:S(2)}) collective-permute-start(bf16[136,768]{1,0:T(8,128)(2,1)S(1)} %own_block.1.refs_0_), channel_id=1, source_target_pairs={{0,4},{4,0},{8,12},{12,8},{1,5},{5,1},{9,13},{13,9},{2,6},{6,2},{1... | collective-permute-start | bytes 626696 | tf_op jit(solution)/shard_map/ppermute | solution.py:235
  12.2 8.2 %collective-permute-start.6 = (bf16[136,768]{1,0:T(8,128)(2,1)S(1)}, bf16[136,768]{1,0:T(8,128)(2,1)S(1)}, u32[]{:S(2)}, u32[]{:S(2)}) collective-permute-start(bf16[136,768]{1,0:T(8,128)(2,1)S(1)} %own_block.1.refs_0_), channel_id=1, source_target_pairs={{0,1},{1,0},{2,3},{3,2},{4,5},{5,4},{6,7},{7,6},{8,9},{9,8},{10,11... | collective-permute-start | bytes 626696 | tf_op jit(solution)/shard_map/ppermute | solution.py:235
  19.2 15.6 %collective-permute-start.9 = (bf16[192,768]{1,0:T(8,128)(2,1)}, bf16[192,768]{1,0:T(8,128)(2,1)S(1)}, u32[]{:S(2)}, u32[]{:S(2)}) collective-permute-start(bf16[192,768]{1,0:T(8,128)(2,1)} %shard_ref.1), channel_id=1, source_target_pairs={{0,1},{1,0},{2,3},{3,2},{4,5},{5,4},{6,7},{7,6},{8,9},{9,8},{10,11... | collective-permute-start | bytes 884744 | tf_op jit(solution)/shard_map/ppermute | solution.py:235
  19.2 16.2 %collective-permute-start.10 = (bf16[192,768]{1,0:T(8,128)(2,1)S(1)}, bf16[192,768]{1,0:T(8,128)(2,1)S(1)}, u32[]{:S(2)}, u32[]{:S(2)}) collective-permute-start(bf16[192,768]{1,0:T(8,128)(2,1)S(1)} %collective-permute-done.8.refs_6_), channel_id=1, source_target_pairs={{0,1},{1,0},{2,3},{3,2},{4,5},{5,4},{6,7},{7,6},{8,9},{9,8},{10,11... | collective-permute-start | bytes 884744 | tf_op jit(solution)/shard_map/ppermute | solution.py:235
  19.7 7.1 %collective-permute-start.1 = (bf16[136,768]{1,0:T(8,128)(2,1)S(1)}, bf16[136,768]{1,0:T(8,128)(2,1)S(1)}, u32[]{:S(2)}, u32[]{:S(2)}) collective-permute-start(bf16[136,768]{1,0:T(8,128)(2,1)S(1)} %collective-permute-done.refs_0_), channel_id=1, source_target_pairs={{0,4},{4,0},{8,12},{12,8},{1,5},{5,1},{9,13},{13,9},{2,6},{6,2},{1... | collective-permute-start | bytes 626696 | tf_op jit(solution)/shard_map/ppermute | solution.py:235
  20.5 7.9 %collective-permute-start.7 = (bf16[136,768]{1,0:T(8,128)(2,1)S(1)}, bf16[136,768]{1,0:T(8,128)(2,1)S(1)}, u32[]{:S(2)}, u32[]{:S(2)}) collective-permute-start(bf16[136,768]{1,0:T(8,128)(2,1)S(1)} %collective-permute-done.5.refs_2_), channel_id=1, source_target_pairs={{0,1},{1,0},{2,3},{3,2},{4,5},{5,4},{6,7},{7,6},{8,9},{9,8},{10,11... | collective-permute-start | bytes 626696 | tf_op jit(solution)/shard_map/ppermute | solution.py:235
  24.6 7.7 %collective-permute-start.3 = (bf16[136,768]{1,0:T(8,128)(2,1)S(1)}, bf16[136,768]{1,0:T(8,128)(2,1)S(1)}, u32[]{:S(2)}, u32[]{:S(2)}) collective-permute-start(bf16[136,768]{1,0:T(8,128)(2,1)S(1)} %collective-permute-done.2.refs_0_), channel_id=1, source_target_pairs={{0,2},{1,3},{2,0},{3,1},{4,6},{5,7},{6,4},{7,5},{8,10},{9,11},{10,... | collective-permute-start | bytes 626696 | tf_op jit(solution)/shard_map/ppermute | solution.py:235
  26.8 11.8 %collective-permute-start.12 = (bf16[136,768]{1,0:T(8,128)(2,1)S(1)}, bf16[136,768]{1,0:T(8,128)(2,1)S(1)}, u32[]{:S(2)}, u32[]{:S(2)}) collective-permute-start(bf16[136,768]{1,0:T(8,128)(2,1)S(1)} %collective-permute-done.1.refs_0_), channel_id=1, source_target_pairs={{0,2},{1,3},{2,0},{3,1},{4,6},{5,7},{6,4},{7,5},{8,10},{9,11},{10,... | collective-permute-start | bytes 626696 | tf_op jit(solution)/shard_map/ppermute | solution.py:235
  28.4 10.7 %collective-permute-start.18 = (bf16[136,768]{1,0:T(8,128)(2,1)S(1)}, bf16[136,768]{1,0:T(8,128)(2,1)S(1)}, u32[]{:S(2)}, u32[]{:S(2)}) collective-permute-start(bf16[136,768]{1,0:T(8,128)(2,1)S(1)} %collective-permute-done.refs_0_), channel_id=1, source_target_pairs={{0,1},{1,0},{2,3},{3,2},{4,5},{5,4},{6,7},{7,6},{8,9},{9,8},{10,11... | collective-permute-start | bytes 626696 | tf_op jit(solution)/shard_map/ppermute | solution.py:235
  32.3 6.9 %collective-permute-start.19 = (bf16[136,768]{1,0:T(8,128)(2,1)S(1)}, bf16[136,768]{1,0:T(8,128)(2,1)S(1)}, u32[]{:S(2)}, u32[]{:S(2)}) collective-permute-start(bf16[136,768]{1,0:T(8,128)(2,1)S(1)} %collective-permute-done.4.refs_2_), channel_id=1, source_target_pairs={{0,1},{1,0},{2,3},{3,2},{4,5},{5,4},{6,7},{7,6},{8,9},{9,8},{10,11... | collective-permute-start | bytes 626696 | tf_op jit(solution)/shard_map/ppermute | solution.py:235
  34.9 7.4 %collective-permute-start.13 = (bf16[136,768]{1,0:T(8,128)(2,1)S(1)}, bf16[136,768]{1,0:T(8,128)(2,1)S(1)}, u32[]{:S(2)}, u32[]{:S(2)}) collective-permute-start(bf16[136,768]{1,0:T(8,128)(2,1)S(1)} %collective-permute-done.2.refs_0_), channel_id=1, source_target_pairs={{0,1},{1,0},{2,3},{3,2},{4,5},{5,4},{6,7},{7,6},{8,9},{9,8},{10,11... | collective-permute-start | bytes 626696 | tf_op jit(solution)/shard_map/ppermute | solution.py:235
  35.4 6.8 %collective-permute-start.14 = (bf16[136,768]{1,0:T(8,128)(2,1)S(1)}, bf16[136,768]{1,0:T(8,128)(2,1)S(1)}, u32[]{:S(2)}, u32[]{:S(2)}) collective-permute-start(bf16[136,768]{1,0:T(8,128)(2,1)S(1)} %collective-permute-done.3.refs_2_), channel_id=1, source_target_pairs={{0,1},{1,0},{2,3},{3,2},{4,5},{5,4},{6,7},{7,6},{8,9},{9,8},{10,11... | collective-permute-start | bytes 626696 | tf_op jit(solution)/shard_map/ppermute | solution.py:235
  51.8 11.9 %collective-permute-start.21 = (bf16[2,128,768]{2,1,0:T(8,128)(2,1)S(1)}, bf16[2,128,768]{2,1,0:T(8,128)(2,1)S(1)}, u32[]{:S(2)}, u32[]{:S(2)}) collective-permute-start(bf16[2,128,768]{2,1,0:T(8,128)(2,1)S(1)} %add_convert_fusion), channel_id=1, source_target_pairs={{0,4},{4,0},{8,12},{12,8},{1,5},{5,1},{9,13},{13,9},{2,6},{6,2},{1... | collective-permute-start | bytes 1179656 | tf_op jit(solution)/shard_map/ppermute | solution.py:235
  54.1 31.2 %collective-permute-start.11 = (bf16[2,128,768]{2,1,0:T(8,128)(2,1)S(1)}, bf16[2,128,768]{2,1,0:T(8,128)(2,1)S(1)}, u32[]{:S(2)}, u32[]{:S(2)}) collective-permute-start(bf16[2,128,768]{2,1,0:T(8,128)(2,1)S(1)} %get-tuple-element.62), channel_id=1, source_target_pairs={{0,1},{1,0},{2,3},{3,2},{4,5},{5,4},{6,7},{7,6},{8,9},{9,8},{10,11... | collective-permute-start | bytes 1179656 | tf_op jit(solution)/shard_map/ppermute | solution.py:235
  54.1 10.5 %collective-permute-start.15 = (bf16[2,128,768]{2,1,0:T(8,128)(2,1)S(1)}, bf16[2,128,768]{2,1,0:T(8,128)(2,1)S(1)}, u32[]{:S(2)}, u32[]{:S(2)}) collective-permute-start(bf16[2,128,768]{2,1,0:T(8,128)(2,1)S(1)} %get-tuple-element.68), channel_id=1, source_target_pairs={{0,1},{1,0},{2,3},{3,2},{4,5},{5,4},{6,7},{7,6},{8,9},{9,8},{10,11... | collective-permute-start | bytes 1179656 | tf_op jit(solution)/shard_map/ppermute | solution.py:235
  54.6 11.9 %collective-permute-start.28 = (bf16[192,768]{1,0:T(8,128)(2,1)S(1)}, bf16[192,768]{1,0:T(8,128)(2,1)S(1)}, u32[]{:S(2)}, u32[]{:S(2)}) collective-permute-start(bf16[192,768]{1,0:T(8,128)(2,1)S(1)} %fusion.3), channel_id=1, source_target_pairs={{0,2},{1,3},{2,0},{3,1},{4,6},{5,7},{6,4},{7,5},{8,10},{9,11},{10,... | collective-permute-start | bytes 884744 | tf_op jit(solution)/shard_map/ppermute | solution.py:235
  64.8 20.5 %collective-permute-start.22 = (bf16[2,128,768]{2,1,0:T(8,128)(2,1)S(1)}, bf16[2,128,768]{2,1,0:T(8,128)(2,1)S(1)}, u32[]{:S(2)}, u32[]{:S(2)}) collective-permute-start(bf16[2,128,768]{2,1,0:T(8,128)(2,1)S(1)} %add_convert_fusion.1), channel_id=1, source_target_pairs={{0,4},{4,0},{8,12},{12,8},{1,5},{5,1},{9,13},{13,9},{2,6},{6,2},{1... | collective-permute-start | bytes 1179656 | tf_op jit(solution)/shard_map/ppermute | solution.py:235
  66.8 16.0 %collective-permute-start.29 = (bf16[96,768]{1,0:T(8,128)(2,1)S(1)}, bf16[96,768]{1,0:T(8,128)(2,1)S(1)}, u32[]{:S(2)}, u32[]{:S(2)}) collective-permute-start(bf16[96,768]{1,0:T(8,128)(2,1)S(1)} %get-tuple-element.100), channel_id=1, source_target_pairs={{0,4},{4,0},{8,12},{12,8},{1,5},{5,1},{9,13},{13,9},{2,6},{6,2},{1... | collective-permute-start | bytes 442376 | tf_op jit(solution)/shard_map/ppermute | solution.py:235
  70.7 27.3 %collective-permute-start.26 = (bf16[128,768]{1,0:T(8,128)(2,1)S(1)}, bf16[128,768]{1,0:T(8,128)(2,1)S(1)}, u32[]{:S(2)}, u32[]{:S(2)}) collective-permute-start(bf16[128,768]{1,0:T(8,128)(2,1)S(1)} %fusion), channel_id=1, source_target_pairs={{0,8},{4,12},{8,0},{12,4},{1,9},{5,13},{9,1},{13,5},{2,10},{6,14},... | collective-permute-start | bytes 589832 | tf_op jit(solution)/shard_map/ppermute | solution.py:235
  82.8 9.1 %collective-permute-start.30 = (bf16[96,768]{1,0:T(8,128)(2,1)S(1)}, bf16[96,768]{1,0:T(8,128)(2,1)S(1)}, u32[]{:S(2)}, u32[]{:S(2)}) collective-permute-start(bf16[96,768]{1,0:T(8,128)(2,1)S(1)} %add_convert_fusion.6), channel_id=1, source_target_pairs={{0,8},{4,12},{8,0},{12,4},{1,9},{5,13},{9,1},{13,5},{2,10},{6,14},... | collective-permute-start | bytes 442376 | tf_op jit(solution)/shard_map/ppermute | solution.py:235
  85.3 12.7 %collective-permute-start.23 = (bf16[128,768]{1,0:T(8,128)(2,1)S(1)}, bf16[128,768]{1,0:T(8,128)(2,1)S(1)}, u32[]{:S(2)}, u32[]{:S(2)}) collective-permute-start(bf16[128,768]{1,0:T(8,128)(2,1)S(1)} %fusion.4), channel_id=1, source_target_pairs={{0,2},{1,3},{2,0},{3,1},{4,6},{5,7},{6,4},{7,5},{8,10},{9,11},{10,... | collective-permute-start | bytes 589832 | tf_op jit(solution)/shard_map/ppermute | solution.py:235
  (14 other events, 46.8 us)

commit v8 on v7

v8 whole, which is shorter than its diff:
```python
import functools

import jax
import jax.numpy as jnp
from jax import lax
from jax.experimental import pallas as pl
from jax.experimental.pallas import tpu as pltpu
from jax.sharding import PartitionSpec as P

BLK = 128
EPSILON = 1e-06
META_ROWS = 8
TILE = 128
F32 = jnp.float32
BF16 = jnp.bfloat16
VMEM = pl.BlockSpec(memory_space=pltpu.VMEM)
HBM = pl.BlockSpec(memory_space=pltpu.HBM)


def dot(a, b, da=1, db=0):
    return lax.dot_general(a, b, (((da,), (db,)), ((), ())), preferred_element_type=F32)


def shard_at(m, shard_rows):
    at = jnp.bitwise_xor(lax.axis_index("dp"), m) * shard_rows
    return pl.ds(pl.multiple_of(at, 16), shard_rows)


def pair_kernel(*refs, cap, pick_count, n_sources, n_sets, n_data, first, last):
    it = iter(refs)
    take = lambda n: [next(it) for _ in range(n)]
    sources, labels = take(n_sources), take(n_sets)
    shards = take(n_data if first else 0)
    enc, total_in = (None, None) if first else take(2)
    backs, grad_scores_ref, block_ref, embedding_ref = take(n_sources // 2), *take(3)
    enc = next(it) if first else enc
    shares = take(2 if last else 0)
    total_ref = next(it)

    n_owner_data = lax.axis_size("dp")
    me = lax.axis_index("labels") * n_owner_data + lax.axis_index("dp")
    rows = sources[0].shape[0] - META_ROWS
    shard_rows = enc.shape[0] // n_data
    n_blocks = labels[0].shape[0] // BLK
    part = n_sources * cap
    slots = n_sets * part

    for m, shard in enumerate(shards):
        enc[shard_at(m, shard_rows), :] = shard[...]

    row_id = lax.broadcasted_iota(jnp.int32, (rows, rows), 0)
    col_id = lax.broadcasted_iota(jnp.int32, (rows, rows), 1)
    before = (row_id < col_id).astype(BF16)
    slot_id = lax.broadcasted_iota(jnp.int32, (cap, rows), 0).astype(F32)
    column = lax.broadcasted_iota(jnp.int32, (slots, BLK), 1)

    hits, codes = [], []
    for source in sources:
        meta = source[rows:, 0 : 3 * rows].astype(F32)[:pick_count]
        code = meta[:, rows : 2 * rows] * 256.0 + meta[:, 2 * rows :] + 1.0
        for j in range(n_sets):
            named = meta[:, :rows] == jnp.bitwise_xor(me, j).astype(F32)
            hits.append(jnp.sum(named.astype(F32), axis=0, keepdims=True))
            codes.append(jnp.sum(jnp.where(named, code, 0.0), axis=0, keepdims=True))
    rank = dot(jnp.concatenate(hits, axis=0).astype(BF16), before)

    picks, picked, slot_codes = [], {}, {}
    for s, source in enumerate(sources):
        pick = []
        for j in range(n_sets):
            i = s * n_sets + j
            pick.append(jnp.where((slot_id == rank[i : i + 1]) & (hits[i] > 0.0), 1.0, 0.0))
            slot_codes[j, s] = jnp.sum(pick[j] * codes[i], axis=1, keepdims=True)
        picks.append(jnp.concatenate(pick, axis=0).astype(BF16))
        found = dot(picks[s], source[:rows, :]).astype(BF16)
        for j in range(n_sets):
            picked[j, s] = found[j * cap : (j + 1) * cap]
    order = [(j, s) for j in range(n_sets) for s in range(n_sources)]
    feats = jnp.concatenate([picked[i] for i in order], axis=0)
    code = jnp.concatenate([slot_codes[i] for i in order], axis=0).astype(jnp.int32) - 1

    hidden = dot(feats, enc[...])
    inv_rms = lax.rsqrt(jnp.mean(hidden * hidden, axis=-1, keepdims=True) + EPSILON)
    embedding = (hidden * inv_rms).astype(BF16)
    embedding_ref[...] = embedding

    block = jnp.broadcast_to(code >> 8, (slots, BLK))
    block_ref[...] = block
    wanted = jnp.broadcast_to(code & 255, (slots, BLK))
    target = jnp.where(column == wanted, 1.0, 0.0)
    grad_pairs = []
    for j in range(n_sets):
        at = slice(j * part, (j + 1) * part)
        scores = dot(embedding[at], labels[j][...], 1, 1)
        mine = block[at]
        own_scores = jnp.zeros((part, BLK), F32)
        for b in range(n_blocks):
            own_scores = jnp.where(mine == b, scores[:, b * BLK : (b + 1) * BLK], own_scores)
        grad_scores = jnp.where(mine >= 0, jax.nn.sigmoid(own_scores) - target[at], 0.0)
        grad_scores_ref[at, :] = grad_scores
        spread = jnp.concatenate(
            [jnp.where(mine == b, grad_scores, 0.0).astype(BF16) for b in range(n_blocks)], axis=1
        )
        grad_pairs.append(dot(spread, labels[j][...]))
    grad_pair = jnp.concatenate(grad_pairs, axis=0).astype(BF16).astype(F32)

    projection = jnp.mean(hidden * grad_pair, axis=-1, keepdims=True)
    grad_hidden = (inv_rms * grad_pair - hidden * (inv_rms**3 * projection)).astype(BF16)
    total = dot(feats, grad_hidden, 0, 0)
    total_ref[...] = total if first else total + total_in[...]
    for m in range(n_data if last else 0):
        shares[m % 2][m // 2] = total_ref[shard_at(m, shard_rows), :].astype(BF16)

    grad_feats = dot(grad_hidden, enc[...], 1, 1).astype(BF16)
    for s in range(n_sources):
        parts = [
            grad_feats[(j * n_sources + s) * cap : (j * n_sources + s + 1) * cap]
            for j in range(n_sets)
        ]
        back = dot(picks[s], jnp.concatenate(parts, axis=0), 0, 0)
        backs[s // 2][s % 2] = back.astype(BF16)


def grad_label_kernel(*refs, calls, n_sets, j):
    grad_scores, blocks, embeddings = refs[:calls], refs[calls : 2 * calls], refs[2 * calls : 3 * calls]
    more, out_ref = refs[3 * calls : -1], refs[-1]
    part = blocks[0].shape[0] // n_sets
    at = slice(j * part, (j + 1) * part)
    grad_scores_t = jnp.concatenate([r[at, :].T for r in grad_scores], axis=1)
    block_t = jnp.concatenate([r[at, :].T for r in blocks], axis=1)
    embedding = jnp.concatenate([r[at, :] for r in embeddings], axis=0)
    for b in range(out_ref.shape[0] // BLK):
        rows = slice(b * BLK, (b + 1) * BLK)
        spread_t = jnp.where(block_t == b, grad_scores_t, 0.0).astype(BF16)
        total = dot(spread_t, embedding)
        for ref in more:
            total = total + ref[rows, :].astype(F32)
        out_ref[rows, :] = total.astype(BF16)


def own_block_kernel(feats_ref, owners_ref, blocks_ref, positives_ref, out_ref, ints, sem):
    rows, width = feats_ref.shape
    feats = pltpu.make_async_copy(feats_ref, out_ref.at[pl.ds(0, rows)], sem.at[0])
    feats.start()
    copies = []
    for i, ref in enumerate((owners_ref, blocks_ref, positives_ref)):
        copies.append(pltpu.make_async_copy(ref, ints.at[i], sem.at[i + 1]))
        copies[i].start()
    for copy in copies:
        copy.wait()
    meta = [ints[i].astype(F32) for i in range(3)]
    meta += [jnp.zeros((meta[0].shape[0], width - 3 * rows), F32)]
    meta = jnp.concatenate(meta, axis=1)
    rest = jnp.zeros((META_ROWS - meta.shape[0], width), F32)
    out_ref[rows:, :] = jnp.concatenate([meta, rest], axis=0).astype(BF16)
    feats.wait()


def load_kernel(label_ref, shard_ref, label_out, shard_out, sem):
    copies = [pltpu.make_async_copy(shard_ref, shard_out, sem.at[0])]
    pieces = sem.shape[0] - 1
    rows = label_ref.shape[0] // pieces
    for i in range(pieces):
        at = pl.ds(i * rows, rows)
        copies.append(pltpu.make_async_copy(label_ref.at[at], label_out.at[at], sem.at[i + 1]))
    for copy in copies:
        copy.start()
    for copy in copies:
        copy.wait()


def half_at(mine, half):
    odd = jnp.bitwise_and(lax.axis_index("labels"), 1)
    return pl.ds(pl.multiple_of((odd if mine else 1 - odd) * half, 16), half)


def split_kernel(even_ref, got_ref, *refs):
    *more, keep_ref, send_ref, total = refs
    share = even_ref[0].astype(F32) + got_ref[0].astype(F32)
    for ref in more:
        share = share + ref[...].astype(F32)
    total[...] = share
    half = keep_ref.shape[0]
    keep_ref[...] = total[half_at(True, half), :]
    send_ref[...] = total[half_at(False, half), :].astype(BF16)


def merge_kernel(mine_ref, other_ref, out_ref):
    half = mine_ref.shape[0]
    out_ref[half_at(True, half), :] = mine_ref[...].astype(F32)
    out_ref[half_at(False, half), :] = other_ref[...].astype(F32)


def call(kernel, name, out_shape, scratch, flops, megabytes, *args, space=VMEM, limit=24):
    return pl.pallas_call(
        kernel,
        in_specs=[space] * len(args),
        out_specs=jax.tree.map(lambda _: VMEM, out_shape),
        out_shape=out_shape,
        scratch_shapes=scratch,
        compiler_params=pltpu.CompilerParams(vmem_limit_bytes=limit << 20),
        cost_estimate=pl.CostEstimate(
            flops=flops, bytes_accessed=megabytes << 20, transcendentals=0
        ),
        name=name,
    )(*args)


def shaped(shape, dtype=BF16):
    return jax.ShapeDtypeStruct(shape, dtype)


def pair_work(sources, labels, shards, cap, pick_count, before, last):
    n_data, n_sets = len(shards), len(labels)
    block_rows, width = sources[0].shape
    rows = block_rows - META_ROWS
    slots = n_sets * len(sources) * cap
    shard_rows = shards[0].shape[0]
    full = (n_data * shard_rows, width)
    backs = len(sources) // 2
    shapes = [shaped((2, rows, width))] * backs
    shapes += [shaped((slots, BLK), F32), shaped((slots, BLK), jnp.int32), shaped((slots, width))]
    more = [before["enc"], before["total"]] if before else shards
    scratch = []
    if not before:
        shapes += [shaped(full)]
    if last:
        shapes += [shaped((n_data // 2, shard_rows, width))] * 2
        scratch = [pltpu.VMEM(full, F32)]
    else:
        shapes += [shaped(full, F32)]
    out = call(
        functools.partial(
            pair_kernel,
            cap=cap,
            pick_count=pick_count,
            n_sources=len(sources),
            n_sets=n_sets,
            n_data=n_data,
            first=not before,
            last=last,
        ),
        "pair_work",
        shapes,
        scratch,
        2 * slots * width * (2 * labels[0].shape[0] + 3 * width + 2 * rows),
        8,
        *sources,
        *labels,
        *more,
    )
    result = {"back": out[:backs], "slots": list(out[backs : backs + 3])}
    rest = list(out[backs + 3 :])
    result["enc"] = before["enc"] if before else rest.pop(0)
    result["shares" if last else "total"] = rest if last else rest[0]
    return result


def grad_label_work(works, n_sets, j, labels_shape, *more):
    slots = list(zip(*(work["slots"] for work in works)))
    return call(
        functools.partial(grad_label_kernel, calls=len(works), n_sets=n_sets, j=j),
        "grad_label_work",
        shaped(labels_shape),
        [],
        2 * sum(x.shape[0] for x in slots[0]) // n_sets * labels_shape[0] * labels_shape[1],
        4,
        *slots[0],
        *slots[1],
        *slots[2],
        *more,
    )


def swap(x):
    x = lax.all_to_all(x, "labels", split_axis=0, concat_axis=0, tiled=True)
    return lax.all_to_all(x, "dp", split_axis=1, concat_axis=1, tiled=True)


def partner(x, axis, mask):
    return lax.ppermute(x, axis, [(i, i ^ mask) for i in range(lax.axis_size(axis))])


def masks(n):
    return [1 << i for i in range(n.bit_length() - 1)]


def after(x, *others):
    return lax.optimization_barrier((x, *others))[0]


def gather_far(x):
    got = {0: x}
    for mask in reversed(masks(lax.axis_size("dp"))[1:]):
        got.update({m | mask: partner(v, "dp", mask) for m, v in list(got.items())})
    return [got[m] for m in sorted(got)]


def gather_near(far):
    near = [partner(after(v, *far[1:]), "dp", 1) for v in far]
    return [v for pair in zip(far, near) for v in pair]


def gather_labels(x):
    got = {0: x}
    for mask in reversed(masks(lax.axis_size("labels"))):
        got.update({m | mask: partner(v, "labels", mask) for m, v in list(got.items())})
    return [got[m] for m in range(len(got))]


def add(*terms):
    return sum(t.astype(F32) for t in terms)


def dp_terms(even, odd):
    got = sent = partner(odd, "dp", 1)
    terms = [[even[i], got[i]] for i in range(even.shape[0])]
    for mask in masks(len(terms)):
        for i in range(len(terms)):
            if i & mask == 0 and i % mask == 0:
                sent = add(*terms[i | mask]).astype(BF16)
                terms[i].append(partner(sent, "dp", 2 * mask))
    return got, terms[0], sent


def sum_shares(even, odd):
    got, terms, sent = dp_terms(even, odd)
    rows, width = even.shape[1:]
    half = rows // 2
    keep, send = call(
        split_kernel,
        "split_share",
        [shaped((half, width), F32), shaped((half, width))],
        [pltpu.VMEM((rows, width), F32)],
        0,
        1,
        even,
        got,
        *terms[2:],
    )
    x = add(keep, partner(send, "labels", 1)).astype(BF16)
    for mask in masks(lax.axis_size("labels"))[1:]:
        x = add(x, partner(x, "labels", mask)).astype(BF16)
    other = partner(x, "labels", 1)
    total = call(merge_kernel, "merge_share", shaped((rows, width), F32), [], 0, 1, x, other)
    return sent, keep, total


def reduce_runs(runs, hold):
    n = len(runs)
    sums = {}
    for i in range(0, n, 2):
        got = partner(runs[i + 1] if i else after(runs[i + 1], hold), "labels", 1)
        parts = [[runs[i][h], got[h]] for h in range(got.shape[0])]
        for mask in masks(len(parts)):
            for h in range(0, len(parts), 2 * mask):
                sent = add(*parts[h + mask]).astype(BF16)
                parts[h].append(partner(sent, "dp", 2 * mask))
        sums[i] = parts[0]
    for mask in masks(n)[1:]:
        for i in range(0, n, 2 * mask):
            sums[i].append(partner(add(*sums[i + mask]).astype(BF16), "labels", mask))
    return add(*sums[0]).astype(BF16)


def with_meta(feats, owner_rows, block_rows, positive_rows):
    meta = jnp.concatenate([owner_rows, block_rows, positive_rows], axis=1).astype(BF16)
    meta = jnp.pad(meta, ((0, META_ROWS - meta.shape[0]), (0, feats.shape[1] - meta.shape[1])))
    return jnp.concatenate([feats, meta], axis=0)


def local(feats, enc_weight, label_weight, owners, blocks, positives):
    n_labels = lax.axis_size("labels")
    n_data = lax.axis_size("dp")
    n_owner = n_labels * n_data
    row_count, width = feats.shape
    pick_count = owners.shape[1]
    cap = max(2, 2 * row_count * pick_count // n_owner)

    if row_count <= n_data * cap:
        own = call(
            own_block_kernel,
            "own_block",
            shaped((row_count + META_ROWS, width)),
            [
                pltpu.VMEM((3, pick_count, row_count), jnp.int32),
                pltpu.SemaphoreType.DMA((4,)),
            ],
            0,
            1,
            feats,
            owners.T,
            blocks.T,
            positives.T,
            space=HBM,
            limit=60,
        )
        near = gather_labels(own)
        far = [gather_far(block) for block in near]
        labels = [label_weight, partner(label_weight, "dp", 1)]
        shards = gather_near(gather_far(after(enc_weight, own)))
        labels[0], shards[0] = call(
            load_kernel,
            "load",
            [shaped(label_weight.shape), shaped(enc_weight.shape)],
            [pltpu.SemaphoreType.DMA((9,))],
            0,
            4,
            after(label_weight, near[1]),
            enc_weight,
            space=HBM,
        )
        works = []
        for by in range(0, n_labels, 2):
            sources = far[by] + far[by + 1]
            if by == 0:
                sources[0] = after(sources[0], near[3 % n_labels])
            before = works[-1] if works else None
            last = by + 2 >= n_labels
            works.append(pair_work(sources, labels, shards, cap, pick_count, before, last))
        sent, keep, grad_enc = sum_shares(*works[-1]["shares"])
        grad_feats = reduce_runs([back for work in works for back in work["back"]], keep)
        works[0]["slots"][2] = after(works[0]["slots"][2], sent)
        other = grad_label_work(works, 2, 1, label_weight.shape)
        other = partner(other, "dp", 1)
        grad_label = grad_label_work(works, 2, 0, label_weight.shape, other)
    else:
        shards = gather_near(gather_far(enc_weight))
        flat = owners.reshape(-1)
        onehot = (flat[:, None] == jnp.arange(n_owner, dtype=jnp.int32)[None, :]).astype(jnp.int32)
        rank = jnp.sum((jnp.cumsum(onehot, axis=0) - onehot) * onehot, axis=1)
        slot = (flat * cap + rank).reshape(row_count, pick_count)
        slot_total = n_owner * cap
        slots = jnp.arange(slot_total, dtype=jnp.int32)
        place = slots[:, None, None] == slot[None]
        pick = jnp.any(place, axis=2).astype(BF16)
        live = jnp.any(place, axis=(1, 2))
        block_of = jnp.sum(jnp.where(place, blocks[None], 0), axis=(1, 2))
        wanted = jnp.sum(jnp.where(place, positives[None], 0), axis=(1, 2))
        owner_of = jnp.where(live, slots // cap, -1)
        out = dot(pick, feats).astype(BF16).reshape(n_labels, n_data, cap, width)
        meta = jnp.stack([owner_of, block_of, wanted], axis=1).reshape(n_labels, n_data, cap, 3)
        tiles = slot_total // TILE
        got = swap(out).reshape(tiles, TILE, width)
        got_meta = swap(meta).reshape(tiles, TILE, 3).transpose(0, 2, 1)
        sources = [
            with_meta(got[i], got_meta[i, 0:1], got_meta[i, 1:2], got_meta[i, 2:3])
            for i in range(tiles)
        ]
        works = []
        for i in range(0, tiles, 4):
            before = works[-1] if works else None
            last = i + 4 >= tiles
            works.append(pair_work(sources[i : i + 4], [label_weight], shards, TILE, 1, before, last))
        back = jnp.concatenate([back for work in works for back in work["back"]], axis=0)
        back = swap(back.reshape(n_labels, n_data, cap, width)).reshape(slot_total, width)
        grad_feats = dot(pick, back, 0, 0).astype(BF16)
        _, _, grad_enc = sum_shares(*works[-1]["shares"])
        grad_label = grad_label_work(works, 1, 0, label_weight.shape)

    return (grad_feats, grad_label, grad_enc)


def solution(mesh):
    rows = P(("groups", "labels", "dp"), None)
    return jax.shard_map(
        local,
        mesh=mesh,
        in_specs=(rows, P("dp", None), rows, rows, rows, rows),
        out_specs=(rows, rows, P(("groups", "dp"), None)),
        check_vma=False,
    )
```

time: 99.1 us -> 91.5 us (0.923)
  waiting for transfers between devices: 45.6 us -> 38.4 us
  Pallas kernels: 18.1 us -> 22 us
  local copies, waits for them, and re-layouts: 5.33 us -> 2.37 us
    ppermute x32 -> x22, waiting for transfers between devices: 45.6 us -> 38.4 us  [partner(): lax.ppermute(x, axis, [(i, i ^ mask) for i in range(lax.axis_size(axis))])]
    pallas_call x9 -> x8, Pallas kernels: 18.1 us -> 22 us  [call(): pl.pallas_call(kernel, in_specs=[space] * len(args), out_specs=jax.tree.m...]
    unnamed x12 -> x6, local copies, waits for them, and re-layouts: 5.33 us -> 2.37 us
    ppermute x32 -> x22, starting transfers between devices: 27.4 us -> 26.7 us  [partner(): lax.ppermute(x, axis, [(i, i ^ mask) for i in range(lax.axis_size(axis))])]
  transfers between devices with their start and end apart: 32 -> 22, of which waited for: 11 -> 9; matrix products, arithmetic and copies ran while one was open for 1% -> 1% of each run, Pallas kernels for 14% -> 14%
where the time goes in v8:
time: 91.5 us; the launch traced here: 91.2 us
  waiting for transfers between devices  38.4 us (42%)
  starting transfers between devices  26.7 us (29%)
  Pallas kernels  22 us (24%)
  local copies, waits for them, and re-layouts  2.37 us (3%)
  other arithmetic  1.08 us (1%)
    ppermute x22, waiting for transfers between devices, partner(): lax.ppermute(x, axis, [(i, i ^ mask) for i in range(lax.axis_size(axis))])  38.4 us
    ppermute x22, starting transfers between devices, partner(): lax.ppermute(x, axis, [(i, i ^ mask) for i in range(lax.axis_size(axis))])  26.7 us
    pallas_call x8, Pallas kernels, call(): pl.pallas_call(kernel, in_specs=[space] * len(args), out_specs=jax.tree.m...  22 us
    unnamed x6, local copies, waits for them, and re-layouts  2.37 us
  transfers between devices with their start and end apart: 22, of which 9 were waited for; matrix products, arithmetic and copies ran while one was open for 1% of the time, Pallas kernels for 14%

profile of v8, /device:TPU:0, one launch (start us, length us, event | category | flops | bytes accessed | tf_op | source)
XLA Modules:
  0.0 91.2 jit_solution(13348090881748086091)
XLA Ops:
  1.1 1.6 %own_block.1.refs_0_ = bf16[136,768]{1,0:T(8,128)(2,1)} custom-call(bf16[128,768]{1,0:T(8,128)(2,1)} %feats_ref.1, s32[4,128]{1,0:T(4,128)} %bitcast.19, s32[4,128]{1,0:T(4,128)} %bitcast.20, s32[4,128]{1,0:T(4,128)} %bitcast.21), custom_call_target="tpu_custom_call" | custom-call | bytes 1048576 | tf_op jit(solution)/shard_map/own_block/pallas_call | solution.py:195
  2.8 3.7 %collective-permute-start = (bf16[136,768]{1,0:T(8,128)(2,1)}, bf16[136,768]{1,0:T(8,128)(2,1)S(1)}, u32[]{:S(2)}, u32[]{:S(2)}) collective-permute-start(bf16[136,768]{1,0:T(8,128)(2,1)} %own_block.1.refs_0_), channel_id=1, source_target_pairs={{0,8},{4,12},{8,0},{12,4},{1,9},{5,13},{9,1},{13,5},{2,10},{6,14},... | collective-permute-start | bytes 626696 | tf_op jit(solution)/shard_map/ppermute | solution.py:281
  6.5 1.5 %collective-permute-start.6 = (bf16[192,768]{1,0:T(8,128)(2,1)}, bf16[192,768]{1,0:T(8,128)(2,1)S(1)}, u32[]{:S(2)}, u32[]{:S(2)}) collective-permute-start(bf16[192,768]{1,0:T(8,128)(2,1)} %shard_ref.1), channel_id=1, source_target_pairs={{0,2},{1,3},{2,0},{3,1},{4,6},{5,7},{6,4},{7,5},{8,10},{9,11},{10,... | collective-permute-start | bytes 884744 | tf_op jit(solution)/shard_map/ppermute | solution.py:281
  8.0 1.6 %collective-permute-start.3 = (bf16[136,768]{1,0:T(8,128)(2,1)}, bf16[136,768]{1,0:T(8,128)(2,1)S(1)}, u32[]{:S(2)}, u32[]{:S(2)}) collective-permute-start(bf16[136,768]{1,0:T(8,128)(2,1)} %own_block.1.refs_0_), channel_id=1, source_target_pairs={{0,4},{4,0},{8,12},{12,8},{1,5},{5,1},{9,13},{13,9},{2,6},{6,2},{1... | collective-permute-start | bytes 626696 | tf_op jit(solution)/shard_map/ppermute | solution.py:281
  9.5 7.5 %collective-permute-done.refs_0_ = bf16[136,768]{1,0:T(8,128)(2,1)S(1)} collective-permute-done((bf16[136,768]{1,0:T(8,128)(2,1)}, bf16[136,768]{1,0:T(8,128)(2,1)S(1)}, u32[]{:S(2)}, u32[]{:S(2)}) %collective-permute-start) | collective-permute-done | bytes 208928 | tf_op jit(solution)/shard_map/ppermute | solution.py:281
  18.5 1.3 %collective-permute-start.2 = (bf16[136,768]{1,0:T(8,128)(2,1)}, bf16[136,768]{1,0:T(8,128)(2,1)S(1)}, u32[]{:S(2)}, u32[]{:S(2)}) collective-permute-start(bf16[136,768]{1,0:T(8,128)(2,1)} %own_block.1.refs_0_), channel_id=1, source_target_pairs={{0,2},{1,3},{2,0},{3,1},{4,6},{5,7},{6,4},{7,5},{8,10},{9,11},{10,... | collective-permute-start | bytes 626696 | tf_op jit(solution)/shard_map/ppermute | solution.py:281
  19.8 4.2 %collective-permute-done.1.refs_2_ = bf16[136,768]{1,0:T(8,128)(2,1)S(1)} collective-permute-done((bf16[136,768]{1,0:T(8,128)(2,1)S(1)}, bf16[136,768]{1,0:T(8,128)(2,1)S(1)}, u32[]{:S(2)}, u32[]{:S(2)}) %collective-permute-start.1) | collective-permute-done | bytes 208928 | tf_op jit(solution)/shard_map/ppermute | solution.py:281
  24.0 1.3 %collective-permute-start.4 = (bf16[136,768]{1,0:T(8,128)(2,1)S(1)}, bf16[136,768]{1,0:T(8,128)(2,1)S(1)}, u32[]{:S(2)}, u32[]{:S(2)}) collective-permute-start(bf16[136,768]{1,0:T(8,128)(2,1)S(1)} %collective-permute-done.3.refs_2_), channel_id=1, source_target_pairs={{0,2},{1,3},{2,0},{3,1},{4,6},{5,7},{6,4},{7,5},{8,10},{9,11},{10,... | collective-permute-start | bytes 626696 | tf_op jit(solution)/shard_map/ppermute | solution.py:281
  25.3 1.4 %copy-done = bf16[1024,768]{1,0:T(8,128)(2,1)S(1)} copy-done((bf16[1024,768]{1,0:T(8,128)(2,1)S(1)}, bf16[1024,768]{1,0:T(8,128)(2,1)}, u32[]{:S(2)}) %copy-start) | copy-done | bytes 1572888
  27.7 2.2 %load.1 = (bf16[1024,768]{1,0:T(8,128)(2,1)S(1)}, bf16[192,768]{1,0:T(8,128)(2,1)S(1)}) custom-call(bf16[1024,768]{1,0:T(8,128)(2,1)S(1)} %copy-done, bf16[192,768]{1,0:T(8,128)(2,1)S(1)} %copy-done.1), custom_call_target="tpu_custom_call" | custom-call | bytes 4194304 | tf_op jit(solution)/shard_map/load/pallas_call | solution.py:195
  30.7 1.3 %collective-permute-start.10 = (bf16[136,768]{1,0:T(8,128)(2,1)S(1)}, bf16[136,768]{1,0:T(8,128)(2,1)S(1)}, u32[]{:S(2)}, u32[]{:S(2)}) collective-permute-start(bf16[136,768]{1,0:T(8,128)(2,1)S(1)} %collective-permute-done.1.refs_2_), channel_id=1, source_target_pairs={{0,2},{1,3},{2,0},{3,1},{4,6},{5,7},{6,4},{7,5},{8,10},{9,11},{10,... | collective-permute-start | bytes 626696 | tf_op jit(solution)/shard_map/ppermute | solution.py:281
  32.0 6.8 %pair_work.2 = (bf16[2,128,768]{2,1,0:T(8,128)(2,1)S(1)}, bf16[2,128,768]{2,1,0:T(8,128)(2,1)S(1)}, f32[512,128]{1,0:T(8,128)S(1)}, s32[512,128]{1,0:T(8,128)S(1...) custom-call(bf16[136,768]{1,0:T(8,128)(2,1)S(1)} %copy-done.2, ...), custom_call_target="tpu_custom_call" | custom-call | flops 3623878656 | bytes 8388608 | tf_op jit(solution)/shard_map/pair_work/pallas_call | solution.py:195
  38.8 1.2 %collective-permute-done.10.refs_3_ = bf16[136,768]{1,0:T(8,128)(2,1)S(1)} collective-permute-done((bf16[136,768]{1,0:T(8,128)(2,1)S(1)}, bf16[136,768]{1,0:T(8,128)(2,1)S(1)}, u32[]{:S(2)}, u32[]{:S(2)}) %collective-permute-start.10) | collective-permute-done | bytes 208928 | tf_op jit(solution)/shard_map/ppermute | solution.py:281
  40.0 7.0 %pair_work.3 = (bf16[2,128,768]{2,1,0:T(8,128)(2,1)S(1)}, bf16[2,128,768]{2,1,0:T(8,128)(2,1)S(1)}, f32[512,128]{1,0:T(8,128)S(1)}, s32[512,128]{1,0:T(8,128)S(1...) custom-call(bf16[136,768]{1,0:T(8,128)(2,1)S(1)} %collective-permute-done.refs_0, ...), custom_call_target="tpu_custom_call" | custom-call | flops 3623878656 | bytes 8388608 | tf_op jit(solution)/shard_map/pair_work/pallas_call | solution.py:195
  47.1 1.6 %collective-permute-start.15 = (bf16[2,128,768]{2,1,0:T(8,128)(2,1)S(1)}, bf16[2,128,768]{2,1,0:T(8,128)(2,1)S(1)}, u32[]{:S(2)}, u32[]{:S(2)}) collective-permute-start(bf16[2,128,768]{2,1,0:T(8,128)(2,1)S(1)} %get-tuple-element.44), channel_id=1, source_target_pairs={{0,4},{4,0},{8,12},{12,8},{1,5},{5,1},{9,13},{13,9},{2,6},{6,2},{1... | collective-permute-start | bytes 1179656 | tf_op jit(solution)/shard_map/ppermute | solution.py:281
  51.3 7.3 %collective-permute-done.15 = bf16[2,128,768]{2,1,0:T(8,128)(2,1)S(1)} collective-permute-done((bf16[2,128,768]{2,1,0:T(8,128)(2,1)S(1)}, bf16[2,128,768]{2,1,0:T(8,128)(2,1)S(1)}, u32[]{:S(2)}, u32[]{:S(2)}) %collective-permute-start.15) | collective-permute-done | bytes 393248 | tf_op jit(solution)/shard_map/ppermute | solution.py:281
  59.9 1.3 %collective-permute-start.19 = (bf16[96,768]{1,0:T(8,128)(2,1)S(1)}, bf16[96,768]{1,0:T(8,128)(2,1)S(1)}, u32[]{:S(2)}, u32[]{:S(2)}) collective-permute-start(bf16[96,768]{1,0:T(8,128)(2,1)S(1)} %get-tuple-element.52), channel_id=1, source_target_pairs={{0,4},{4,0},{8,12},{12,8},{1,5},{5,1},{9,13},{13,9},{2,6},{6,2},{1... | collective-permute-start | bytes 442376 | tf_op jit(solution)/shard_map/ppermute | solution.py:281
  62.0 3.3 %collective-permute-done.16 = bf16[128,768]{1,0:T(8,128)(2,1)S(1)} collective-permute-done((bf16[128,768]{1,0:T(8,128)(2,1)S(1)}, bf16[128,768]{1,0:T(8,128)(2,1)S(1)}, u32[]{:S(2)}, u32[]{:S(2)}) %collective-permute-start.16) | collective-permute-done | bytes 196640 | tf_op jit(solution)/shard_map/ppermute | solution.py:281
  65.3 3.5 %collective-permute-start.17 = (bf16[128,768]{1,0:T(8,128)(2,1)S(1)}, bf16[128,768]{1,0:T(8,128)(2,1)S(1)}, u32[]{:S(2)}, u32[]{:S(2)}) collective-permute-start(bf16[128,768]{1,0:T(8,128)(2,1)S(1)} %fusion), channel_id=1, source_target_pairs={{0,8},{4,12},{8,0},{12,4},{1,9},{5,13},{9,1},{13,5},{2,10},{6,14},... | collective-permute-start | bytes 589832 | tf_op jit(solution)/shard_map/ppermute | solution.py:281
  69.9 11.0 %collective-permute-done.13 = bf16[2,128,768]{2,1,0:T(8,128)(2,1)S(1)} collective-permute-done((bf16[2,128,768]{2,1,0:T(8,128)(2,1)S(1)}, bf16[2,128,768]{2,1,0:T(8,128)(2,1)S(1)}, u32[]{:S(2)}, u32[]{:S(2)}) %collective-permute-start.13) | collective-permute-done | bytes 393248 | tf_op jit(solution)/shard_map/ppermute | solution.py:281
  80.9 1.2 %collective-permute-start.14 = (bf16[128,768]{1,0:T(8,128)(2,1)S(1)}, bf16[128,768]{1,0:T(8,128)(2,1)S(1)}, u32[]{:S(2)}, u32[]{:S(2)}) collective-permute-start(bf16[128,768]{1,0:T(8,128)(2,1)S(1)} %fusion.4), channel_id=1, source_target_pairs={{0,2},{1,3},{2,0},{3,1},{4,6},{5,7},{6,4},{7,5},{8,10},{9,11},{10,... | collective-permute-start | bytes 589832 | tf_op jit(solution)/shard_map/ppermute | solution.py:281
  82.2 1.9 %collective-permute-start.21 = (bf16[96,768]{1,0:T(8,128)(2,1)S(1)}, bf16[96,768]{1,0:T(8,128)(2,1)S(1)}, u32[]{:S(2)}, u32[]{:S(2)}) collective-permute-start(bf16[96,768]{1,0:T(8,128)(2,1)S(1)} %add_convert_fusion.3.mine_ref), channel_id=1, source_target_pairs={{0,4},{4,0},{8,12},{12,8},{1,5},{5,1},{9,13},{13,9},{2,6},{6,2},{1... | collective-permute-start | bytes 442376 | tf_op jit(solution)/shard_map/ppermute | solution.py:281
  84.0 3.4 %collective-permute-done.21.other_ref = bf16[96,768]{1,0:T(8,128)(2,1)S(1)} collective-permute-done((bf16[96,768]{1,0:T(8,128)(2,1)S(1)}, bf16[96,768]{1,0:T(8,128)(2,1)S(1)}, u32[]{:S(2)}, u32[]{:S(2)}) %collective-permute-start.21) | collective-permute-done | bytes 147488 | tf_op jit(solution)/shard_map/ppermute | solution.py:281
  89.0 2.2 %grad_label_work.3 = bf16[1024,768]{1,0:T(8,128)(2,1)} custom-call(f32[512,128]{1,0:T(8,128)S(1)} %get-tuple-element.45.refs_0_, f32[512,128]{1,0:T(8,128)S(1)} %get-tuple-element.46.refs_1_, s32[512,128]{1,0:T(8,128)S(1)} %get-tuple-element.47.refs_2_, s32[512,128]{1,0:T(8,128)S(1)} %get-tuple-element.48.refs_3_, ...), custom_call_target="tpu_custom_call" | custom-call | flops 805306368 | bytes 4194304 | tf_op jit(solution)/shard_map/grad_label_work/pallas_call | solution.py:195
  (41 shorter events, 11.1 us)
Async XLA Ops:
  0.6 31.4 %collective-permute-start.5 = (bf16[1024,768]{1,0:T(8,128)(2,1)}, bf16[1024,768]{1,0:T(8,128)(2,1)}, u32[]{:S(2)}, u32[]{:S(2)}) collective-permute-start(bf16[1024,768]{1,0:T(8,128)(2,1)} %label_ref), channel_id=1, source_target_pairs={{0,1},{1,0},{2,3},{3,2},{4,5},{5,4},{6,7},{7,6},{8,9},{9,8},{10,11... | collective-permute-start | bytes 4718600 | tf_op jit(solution)/shard_map/ppermute | solution.py:281
  2.8 14.3 %collective-permute-start = (bf16[136,768]{1,0:T(8,128)(2,1)}, bf16[136,768]{1,0:T(8,128)(2,1)S(1)}, u32[]{:S(2)}, u32[]{:S(2)}) collective-permute-start(bf16[136,768]{1,0:T(8,128)(2,1)} %own_block.1.refs_0_), channel_id=1, source_target_pairs={{0,8},{4,12},{8,0},{12,4},{1,9},{5,13},{9,1},{13,5},{2,10},{6,14},... | collective-permute-start | bytes 626696 | tf_op jit(solution)/shard_map/ppermute | solution.py:281
  6.5 11.4 %collective-permute-start.6 = (bf16[192,768]{1,0:T(8,128)(2,1)}, bf16[192,768]{1,0:T(8,128)(2,1)S(1)}, u32[]{:S(2)}, u32[]{:S(2)}) collective-permute-start(bf16[192,768]{1,0:T(8,128)(2,1)} %shard_ref.1), channel_id=1, source_target_pairs={{0,2},{1,3},{2,0},{3,1},{4,6},{5,7},{6,4},{7,5},{8,10},{9,11},{10,... | collective-permute-start | bytes 884744 | tf_op jit(solution)/shard_map/ppermute | solution.py:281
  8.0 10.5 %collective-permute-start.3 = (bf16[136,768]{1,0:T(8,128)(2,1)}, bf16[136,768]{1,0:T(8,128)(2,1)S(1)}, u32[]{:S(2)}, u32[]{:S(2)}) collective-permute-start(bf16[136,768]{1,0:T(8,128)(2,1)} %own_block.1.refs_0_), channel_id=1, source_target_pairs={{0,4},{4,0},{8,12},{12,8},{1,5},{5,1},{9,13},{13,9},{2,6},{6,2},{1... | collective-permute-start | bytes 626696 | tf_op jit(solution)/shard_map/ppermute | solution.py:281
  17.1 6.9 %collective-permute-start.1 = (bf16[136,768]{1,0:T(8,128)(2,1)S(1)}, bf16[136,768]{1,0:T(8,128)(2,1)S(1)}, u32[]{:S(2)}, u32[]{:S(2)}) collective-permute-start(bf16[136,768]{1,0:T(8,128)(2,1)S(1)} %collective-permute-done.refs_0_), channel_id=1, source_target_pairs={{0,4},{4,0},{8,12},{12,8},{1,5},{5,1},{9,13},{13,9},{2,6},{6,2},{1... | collective-permute-start | bytes 626696 | tf_op jit(solution)/shard_map/ppermute | solution.py:281
  17.8 14.2 %collective-permute-start.7 = (bf16[192,768]{1,0:T(8,128)(2,1)}, bf16[192,768]{1,0:T(8,128)(2,1)S(1)}, u32[]{:S(2)}, u32[]{:S(2)}) collective-permute-start(bf16[192,768]{1,0:T(8,128)(2,1)} %shard_ref.1), channel_id=1, source_target_pairs={{0,1},{1,0},{2,3},{3,2},{4,5},{5,4},{6,7},{7,6},{8,9},{9,8},{10,11... | collective-permute-start | bytes 884744 | tf_op jit(solution)/shard_map/ppermute | solution.py:281
  17.9 14.2 %collective-permute-start.8 = (bf16[192,768]{1,0:T(8,128)(2,1)S(1)}, bf16[192,768]{1,0:T(8,128)(2,1)S(1)}, u32[]{:S(2)}, u32[]{:S(2)}) collective-permute-start(bf16[192,768]{1,0:T(8,128)(2,1)S(1)} %collective-permute-done.6.refs_8_), channel_id=1, source_target_pairs={{0,1},{1,0},{2,3},{3,2},{4,5},{5,4},{6,7},{7,6},{8,9},{9,8},{10,11... | collective-permute-start | bytes 884744 | tf_op jit(solution)/shard_map/ppermute | solution.py:281
  18.5 11.4 %collective-permute-start.2 = (bf16[136,768]{1,0:T(8,128)(2,1)}, bf16[136,768]{1,0:T(8,128)(2,1)S(1)}, u32[]{:S(2)}, u32[]{:S(2)}) collective-permute-start(bf16[136,768]{1,0:T(8,128)(2,1)} %own_block.1.refs_0_), channel_id=1, source_target_pairs={{0,2},{1,3},{2,0},{3,1},{4,6},{5,7},{6,4},{7,5},{8,10},{9,11},{10,... | collective-permute-start | bytes 626696 | tf_op jit(solution)/shard_map/ppermute | solution.py:281
  24.0 6.7 %collective-permute-start.4 = (bf16[136,768]{1,0:T(8,128)(2,1)S(1)}, bf16[136,768]{1,0:T(8,128)(2,1)S(1)}, u32[]{:S(2)}, u32[]{:S(2)}) collective-permute-start(bf16[136,768]{1,0:T(8,128)(2,1)S(1)} %collective-permute-done.3.refs_2_), channel_id=1, source_target_pairs={{0,2},{1,3},{2,0},{3,1},{4,6},{5,7},{6,4},{7,5},{8,10},{9,11},{10,... | collective-permute-start | bytes 626696 | tf_op jit(solution)/shard_map/ppermute | solution.py:281
  25.3 1.4 %copy-start = (bf16[1024,768]{1,0:T(8,128)(2,1)S(1)}, bf16[1024,768]{1,0:T(8,128)(2,1)}, u32[]{:S(2)}) copy-start(bf16[1024,768]{1,0:T(8,128)(2,1)} %label_ref) | copy-start | bytes 4718596
  27.7 4.3 %copy-start.2 = (bf16[136,768]{1,0:T(8,128)(2,1)S(1)}, bf16[136,768]{1,0:T(8,128)(2,1)}, u32[]{:S(2)}) copy-start(bf16[136,768]{1,0:T(8,128)(2,1)} %own_block.1.refs_0_) | copy-start | bytes 626692
  29.9 8.9 %collective-permute-start.9 = (bf16[136,768]{1,0:T(8,128)(2,1)S(1)}, bf16[136,768]{1,0:T(8,128)(2,1)S(1)}, u32[]{:S(2)}, u32[]{:S(2)}) collective-permute-start(bf16[136,768]{1,0:T(8,128)(2,1)S(1)} %collective-permute-done.refs_0_), channel_id=1, source_target_pairs={{0,2},{1,3},{2,0},{3,1},{4,6},{5,7},{6,4},{7,5},{8,10},{9,11},{10,... | collective-permute-start | bytes 626696 | tf_op jit(solution)/shard_map/ppermute | solution.py:281
  30.7 9.3 %collective-permute-start.10 = (bf16[136,768]{1,0:T(8,128)(2,1)S(1)}, bf16[136,768]{1,0:T(8,128)(2,1)S(1)}, u32[]{:S(2)}, u32[]{:S(2)}) collective-permute-start(bf16[136,768]{1,0:T(8,128)(2,1)S(1)} %collective-permute-done.1.refs_2_), channel_id=1, source_target_pairs={{0,2},{1,3},{2,0},{3,1},{4,6},{5,7},{6,4},{7,5},{8,10},{9,11},{10,... | collective-permute-start | bytes 626696 | tf_op jit(solution)/shard_map/ppermute | solution.py:281
  47.0 2.1 %collective-permute-start.11 = (bf16[2,192,768]{2,1,0:T(8,128)(2,1)S(1)}, bf16[2,192,768]{2,1,0:T(8,128)(2,1)S(1)}, u32[]{:S(2)}, u32[]{:S(2)}) collective-permute-start(bf16[2,192,768]{2,1,0:T(8,128)(2,1)S(1)} %get-tuple-element.40), channel_id=1, source_target_pairs={{0,1},{1,0},{2,3},{3,2},{4,5},{5,4},{6,7},{7,6},{8,9},{9,8},{10,11... | collective-permute-start | bytes 1769480 | tf_op jit(solution)/shard_map/ppermute | solution.py:281
  47.1 11.5 %collective-permute-start.15 = (bf16[2,128,768]{2,1,0:T(8,128)(2,1)S(1)}, bf16[2,128,768]{2,1,0:T(8,128)(2,1)S(1)}, u32[]{:S(2)}, u32[]{:S(2)}) collective-permute-start(bf16[2,128,768]{2,1,0:T(8,128)(2,1)S(1)} %get-tuple-element.44), channel_id=1, source_target_pairs={{0,4},{4,0},{8,12},{12,8},{1,5},{5,1},{9,13},{13,9},{2,6},{6,2},{1... | collective-permute-start | bytes 1179656 | tf_op jit(solution)/shard_map/ppermute | solution.py:281
  49.2 10.5 %collective-permute-start.12 = (bf16[192,768]{1,0:T(8,128)(2,1)S(1)}, bf16[192,768]{1,0:T(8,128)(2,1)S(1)}, u32[]{:S(2)}, u32[]{:S(2)}) collective-permute-start(bf16[192,768]{1,0:T(8,128)(2,1)S(1)} %fusion.3), channel_id=1, source_target_pairs={{0,2},{1,3},{2,0},{3,1},{4,6},{5,7},{6,4},{7,5},{8,10},{9,11},{10,... | collective-permute-start | bytes 884744 | tf_op jit(solution)/shard_map/ppermute | solution.py:281
  51.2 37.8 %collective-permute-start.18 = (bf16[1024,768]{1,0:T(8,128)(2,1)S(1)}, bf16[1024,768]{1,0:T(8,128)(2,1)S(1)}, u32[]{:S(2)}, u32[]{:S(2)}) collective-permute-start(bf16[1024,768]{1,0:T(8,128)(2,1)S(1)} %grad_label_work.2), channel_id=1, source_target_pairs={{0,1},{1,0},{2,3},{3,2},{4,5},{5,4},{6,7},{7,6},{8,9},{9,8},{10,11... | collective-permute-start | bytes 4718600 | tf_op jit(solution)/shard_map/ppermute | solution.py:281
  58.7 6.5 %collective-permute-start.16 = (bf16[128,768]{1,0:T(8,128)(2,1)S(1)}, bf16[128,768]{1,0:T(8,128)(2,1)S(1)}, u32[]{:S(2)}, u32[]{:S(2)}) collective-permute-start(bf16[128,768]{1,0:T(8,128)(2,1)S(1)} %fusion.5), channel_id=1, source_target_pairs={{0,2},{1,3},{2,0},{3,1},{4,6},{5,7},{6,4},{7,5},{8,10},{9,11},{10,... | collective-permute-start | bytes 589832 | tf_op jit(solution)/shard_map/ppermute | solution.py:281
  59.9 8.9 %collective-permute-start.19 = (bf16[96,768]{1,0:T(8,128)(2,1)S(1)}, bf16[96,768]{1,0:T(8,128)(2,1)S(1)}, u32[]{:S(2)}, u32[]{:S(2)}) collective-permute-start(bf16[96,768]{1,0:T(8,128)(2,1)S(1)} %get-tuple-element.52), channel_id=1, source_target_pairs={{0,4},{4,0},{8,12},{12,8},{1,5},{5,1},{9,13},{13,9},{2,6},{6,2},{1... | collective-permute-start | bytes 442376 | tf_op jit(solution)/shard_map/ppermute | solution.py:281
  61.2 19.7 %collective-permute-start.13 = (bf16[2,128,768]{2,1,0:T(8,128)(2,1)S(1)}, bf16[2,128,768]{2,1,0:T(8,128)(2,1)S(1)}, u32[]{:S(2)}, u32[]{:S(2)}) collective-permute-start(bf16[2,128,768]{2,1,0:T(8,128)(2,1)S(1)} %get-tuple-element.42), channel_id=1, source_target_pairs={{0,4},{4,0},{8,12},{12,8},{1,5},{5,1},{9,13},{13,9},{2,6},{6,2},{1... | collective-permute-start | bytes 1179656 | tf_op jit(solution)/shard_map/ppermute | solution.py:281
  65.3 22.9 %collective-permute-start.17 = (bf16[128,768]{1,0:T(8,128)(2,1)S(1)}, bf16[128,768]{1,0:T(8,128)(2,1)S(1)}, u32[]{:S(2)}, u32[]{:S(2)}) collective-permute-start(bf16[128,768]{1,0:T(8,128)(2,1)S(1)} %fusion), channel_id=1, source_target_pairs={{0,8},{4,12},{8,0},{12,4},{1,9},{5,13},{9,1},{13,5},{2,10},{6,14},... | collective-permute-start | bytes 589832 | tf_op jit(solution)/shard_map/ppermute | solution.py:281
  68.8 13.3 %collective-permute-start.20 = (bf16[96,768]{1,0:T(8,128)(2,1)S(1)}, bf16[96,768]{1,0:T(8,128)(2,1)S(1)}, u32[]{:S(2)}, u32[]{:S(2)}) collective-permute-start(bf16[96,768]{1,0:T(8,128)(2,1)S(1)} %add_convert_fusion.4), channel_id=1, source_target_pairs={{0,8},{4,12},{8,0},{12,4},{1,9},{5,13},{9,1},{13,5},{2,10},{6,14},... | collective-permute-start | bytes 442376 | tf_op jit(solution)/shard_map/ppermute | solution.py:281
  80.9 7.3 %collective-permute-start.14 = (bf16[128,768]{1,0:T(8,128)(2,1)S(1)}, bf16[128,768]{1,0:T(8,128)(2,1)S(1)}, u32[]{:S(2)}, u32[]{:S(2)}) collective-permute-start(bf16[128,768]{1,0:T(8,128)(2,1)S(1)} %fusion.4), channel_id=1, source_target_pairs={{0,2},{1,3},{2,0},{3,1},{4,6},{5,7},{6,4},{7,5},{8,10},{9,11},{10,... | collective-permute-start | bytes 589832 | tf_op jit(solution)/shard_map/ppermute | solution.py:281
  82.2 5.2 %collective-permute-start.21 = (bf16[96,768]{1,0:T(8,128)(2,1)S(1)}, bf16[96,768]{1,0:T(8,128)(2,1)S(1)}, u32[]{:S(2)}, u32[]{:S(2)}) collective-permute-start(bf16[96,768]{1,0:T(8,128)(2,1)S(1)} %add_convert_fusion.3.mine_ref), channel_id=1, source_target_pairs={{0,4},{4,0},{8,12},{12,8},{1,5},{5,1},{9,13},{13,9},{2,6},{6,2},{1... | collective-permute-start | bytes 442376 | tf_op jit(solution)/shard_map/ppermute | solution.py:281
  (1 other events, 1.0 us)

commit v9 on v8

--- a/solution.py
+++ b/solution.py
@@ -156,17 +156,9 @@
     feats.wait()
 
 
-def load_kernel(label_ref, shard_ref, label_out, shard_out, sem):
-    copies = [pltpu.make_async_copy(shard_ref, shard_out, sem.at[0])]
-    pieces = sem.shape[0] - 1
-    rows = label_ref.shape[0] // pieces
-    for i in range(pieces):
-        at = pl.ds(i * rows, rows)
-        copies.append(pltpu.make_async_copy(label_ref.at[at], label_out.at[at], sem.at[i + 1]))
-    for copy in copies:
-        copy.start()
-    for copy in copies:
-        copy.wait()
+def load_kernel(label_ref, shard_ref, label_out, shard_out):
+    label_out[...] = label_ref[...]
+    shard_out[...] = shard_ref[...]
 
 
 def half_at(mine, half):
@@ -296,15 +288,16 @@
     return [got[m] for m in sorted(got)]
 
 
-def gather_near(far):
-    near = [partner(after(v, *far[1:]), "dp", 1) for v in far]
+def gather_near(far, *first):
+    near = [partner(after(v, *far[1:], *first), "dp", 1) for v in far]
     return [v for pair in zip(far, near) for v in pair]
 
 
-def gather_labels(x):
+def gather_labels(x, first):
     got = {0: x}
     for mask in reversed(masks(lax.axis_size("labels"))):
-        got.update({m | mask: partner(v, "labels", mask) for m, v in list(got.items())})
+        for m, v in list(got.items()):
+            got[m | mask] = partner(after(v, first) if m else v, "labels", mask)
     return [got[m] for m in range(len(got))]
 
 
@@ -339,24 +332,33 @@
         *terms[2:],
     )
     x = add(keep, partner(send, "labels", 1)).astype(BF16)
+    first = x
     for mask in masks(lax.axis_size("labels"))[1:]:
         x = add(x, partner(x, "labels", mask)).astype(BF16)
+    return sent, first, x
+
+
+def join_halves(x, *first):
     other = partner(x, "labels", 1)
-    total = call(merge_kernel, "merge_share", shaped((rows, width), F32), [], 0, 1, x, other)
-    return sent, keep, total
-
-
-def reduce_runs(runs, hold):
+    out = shaped((2 * x.shape[0], x.shape[1]), F32)
+    return call(merge_kernel, "merge_share", out, [], 0, 1, after(x, *first), other)
+
+
+def reduce_runs(runs):
     n = len(runs)
+    gots = []
+    for i in reversed(range(0, n, 2)):
+        gots.append(partner(after(runs[i + 1], *gots[-1:]), "labels", 1))
     sums = {}
-    for i in range(0, n, 2):
-        got = partner(runs[i + 1] if i else after(runs[i + 1], hold), "labels", 1)
+    held = []
+    for i, got in zip(reversed(range(0, n, 2)), gots):
         parts = [[runs[i][h], got[h]] for h in range(got.shape[0])]
         for mask in masks(len(parts)):
             for h in range(0, len(parts), 2 * mask):
-                sent = add(*parts[h + mask]).astype(BF16)
+                sent = after(add(*parts[h + mask]).astype(BF16), *held)
                 parts[h].append(partner(sent, "dp", 2 * mask))
         sums[i] = parts[0]
+        held = parts[0][-1:]
     for mask in masks(n)[1:]:
         for i in range(0, n, 2 * mask):
             sums[i].append(partner(add(*sums[i + mask]).astype(BF16), "labels", mask))
@@ -395,35 +397,44 @@
             space=HBM,
             limit=60,
         )
-        near = gather_labels(own)
-        far = [gather_far(block) for block in near]
         labels = [label_weight, partner(label_weight, "dp", 1)]
-        shards = gather_near(gather_far(after(enc_weight, own)))
-        labels[0], shards[0] = call(
+        labels[0], own_shard = call(
             load_kernel,
             "load",
             [shaped(label_weight.shape), shaped(enc_weight.shape)],
-            [pltpu.SemaphoreType.DMA((9,))],
+            [],
             0,
             4,
-            after(label_weight, near[1]),
+            after(label_weight, labels[1]),
             enc_weight,
-            space=HBM,
         )
-        works = []
-        for by in range(0, n_labels, 2):
-            sources = far[by] + far[by + 1]
+        near = gather_labels(own, labels[0])
+        far, works = [], []
+        for by in range(n_labels):
+            last = by == n_labels - 1
+            held = far[0][1:] if by else []
+            if last and works:
+                held = held + far[-1][1:] + works[0]["slots"][:1]
+            far.append(gather_far(after(near[by], *held)))
             if by == 0:
-                sources[0] = after(sources[0], near[3 % n_labels])
-            before = works[-1] if works else None
-            last = by + 2 >= n_labels
-            works.append(pair_work(sources, labels, shards, cap, pick_count, before, last))
-        sent, keep, grad_enc = sum_shares(*works[-1]["shares"])
-        grad_feats = reduce_runs([back for work in works for back in work["back"]], keep)
+                shards = gather_near(
+                    gather_far(after(enc_weight, own)), *far[0][1:], *near[1:3], labels[0]
+                )
+                shards[0] = own_shard
+                far[0][0] = after(far[0][0], near[2 % n_labels])
+            if by == 0 or last:
+                for run in range(len(works), by + 1):
+                    sources = [near[run] if run else far[0][0]] + far[run][1:]
+                    before = works[-1] if works else None
+                    final = run == n_labels - 1
+                    works.append(pair_work(sources, labels, shards, cap, pick_count, before, final))
+        sent, first, share = sum_shares(*works[-1]["shares"])
+        grad_feats = reduce_runs([back for work in works for back in work["back"]])
         works[0]["slots"][2] = after(works[0]["slots"][2], sent)
-        other = grad_label_work(works, 2, 1, label_weight.shape)
-        other = partner(other, "dp", 1)
+        other = partner(grad_label_work(works, 2, 1, label_weight.shape), "dp", 1)
+        works[0]["slots"][2] = after(works[0]["slots"][2], first)
         grad_label = grad_label_work(works, 2, 0, label_weight.shape, other)
+        grad_enc = join_halves(share, grad_label, grad_feats)
     else:
         shards = gather_near(gather_far(enc_weight))
         flat = owners.reshape(-1)
@@ -455,8 +466,9 @@
         back = jnp.concatenate([back for work in works for back in work["back"]], axis=0)
         back = swap(back.reshape(n_labels, n_data, cap, width)).reshape(slot_total, width)
         grad_feats = dot(pick, back, 0, 0).astype(BF16)
-        _, _, grad_enc = sum_shares(*works[-1]["shares"])
+        _, _, share = sum_shares(*works[-1]["shares"])
         grad_label = grad_label_work(works, 1, 0, label_weight.shape)
+        grad_enc = join_halves(share, grad_label, grad_feats)
 
     return (grad_feats, grad_label, grad_enc)
 

time: 91.5 us -> 89.5 us (0.978)
  starting transfers between devices: 26.7 us -> 24.3 us
    ppermute x22, starting transfers between devices: 26.7 us -> 24.3 us  [partner(): lax.ppermute(x, axis, [(i, i ^ mask) for i in range(lax.axis_size(axis))])]
    pallas_call x8 -> x10, Pallas kernels: 22 us -> 22.4 us  [call(): pl.pallas_call(kernel, in_specs=[space] * len(args), out_specs=jax.tree.m...]
  transfers between devices with their start and end apart: 22 -> 22, of which waited for: 9 -> 12; matrix products, arithmetic and copies ran while one was open for 1% -> 1% of each run, Pallas kernels for 14% -> 20%
where the time goes in v9:
time: 89.5 us; the launch traced here: 89.3 us
  waiting for transfers between devices  38.3 us (43%)
  starting transfers between devices  24.3 us (27%)
  Pallas kernels  22.4 us (25%)
  local copies, waits for them, and re-layouts  2.37 us (3%)
  other arithmetic  1.09 us (1%)
    ppermute x22, waiting for transfers between devices, partner(): lax.ppermute(x, axis, [(i, i ^ mask) for i in range(lax.axis_size(axis))])  38.3 us
    ppermute x22, starting transfers between devices, partner(): lax.ppermute(x, axis, [(i, i ^ mask) for i in range(lax.axis_size(axis))])  24.3 us
    pallas_call x10, Pallas kernels, call(): pl.pallas_call(kernel, in_specs=[space] * len(args), out_specs=jax.tree.m...  22.4 us
    unnamed x6, local copies, waits for them, and re-layouts  2.37 us
  transfers between devices with their start and end apart: 22, of which 12 were waited for; matrix products, arithmetic and copies ran while one was open for 1% of the time, Pallas kernels for 20%

profile of v9, /device:TPU:0, one launch (start us, length us, event | category | flops | bytes accessed | tf_op | source)
XLA Modules:
  0.0 89.3 jit_solution(14649014336700939903)
XLA Ops:
  1.1 1.6 %own_block.1.refs_0_ = bf16[136,768]{1,0:T(8,128)(2,1)} custom-call(bf16[128,768]{1,0:T(8,128)(2,1)} %feats_ref.1, s32[4,128]{1,0:T(4,128)} %bitcast.19, s32[4,128]{1,0:T(4,128)} %bitcast.20, s32[4,128]{1,0:T(4,128)} %bitcast.21), custom_call_target="tpu_custom_call" | custom-call | bytes 1048576 | tf_op jit(solution)/shard_map/own_block/pallas_call | solution.py:187
  2.8 2.6 %collective-permute-start.3 = (bf16[192,768]{1,0:T(8,128)(2,1)}, bf16[192,768]{1,0:T(8,128)(2,1)S(1)}, u32[]{:S(2)}, u32[]{:S(2)}) collective-permute-start(bf16[192,768]{1,0:T(8,128)(2,1)} %shard_ref.1), channel_id=1, source_target_pairs={{0,2},{1,3},{2,0},{3,1},{4,6},{5,7},{6,4},{7,5},{8,10},{9,11},{10,... | collective-permute-start | bytes 884744 | tf_op jit(solution)/shard_map/ppermute | solution.py:273
  5.4 3.0 %collective-permute-start = (bf16[136,768]{1,0:T(8,128)(2,1)}, bf16[136,768]{1,0:T(8,128)(2,1)S(1)}, u32[]{:S(2)}, u32[]{:S(2)}) collective-permute-start(bf16[136,768]{1,0:T(8,128)(2,1)} %own_block.1.refs_0_), channel_id=1, source_target_pairs={{0,8},{4,12},{8,0},{12,4},{1,9},{5,13},{9,1},{13,5},{2,10},{6,14},... | collective-permute-start | bytes 626696 | tf_op jit(solution)/shard_map/ppermute | solution.py:273
  8.5 1.6 %collective-permute-start.4 = (bf16[136,768]{1,0:T(8,128)(2,1)}, bf16[136,768]{1,0:T(8,128)(2,1)S(1)}, u32[]{:S(2)}, u32[]{:S(2)}) collective-permute-start(bf16[136,768]{1,0:T(8,128)(2,1)} %own_block.1.refs_0_), channel_id=1, source_target_pairs={{0,4},{4,0},{8,12},{12,8},{1,5},{5,1},{9,13},{13,9},{2,6},{6,2},{1... | collective-permute-start | bytes 626696 | tf_op jit(solution)/shard_map/ppermute | solution.py:273
  10.1 1.4 %copy-done = bf16[1024,768]{1,0:T(8,128)(2,1)S(1)} copy-done((bf16[1024,768]{1,0:T(8,128)(2,1)S(1)}, bf16[1024,768]{1,0:T(8,128)(2,1)}, u32[]{:S(2)}) %copy-start) | copy-done | bytes 1572888
  12.6 5.2 %collective-permute-done.1.refs_1_ = bf16[136,768]{1,0:T(8,128)(2,1)S(1)} collective-permute-done((bf16[136,768]{1,0:T(8,128)(2,1)}, bf16[136,768]{1,0:T(8,128)(2,1)S(1)}, u32[]{:S(2)}, u32[]{:S(2)}) %collective-permute-start.1) | collective-permute-done | bytes 208928 | tf_op jit(solution)/shard_map/ppermute | solution.py:273
  19.3 1.5 %collective-permute-start.9 = (bf16[136,768]{1,0:T(8,128)(2,1)S(1)}, bf16[136,768]{1,0:T(8,128)(2,1)S(1)}, u32[]{:S(2)}, u32[]{:S(2)}) collective-permute-start(bf16[136,768]{1,0:T(8,128)(2,1)S(1)} %collective-permute-done.refs_0_), channel_id=1, source_target_pairs={{0,2},{1,3},{2,0},{3,1},{4,6},{5,7},{6,4},{7,5},{8,10},{9,11},{10,... | collective-permute-start | bytes 626696 | tf_op jit(solution)/shard_map/ppermute | solution.py:273
  20.8 1.4 %collective-permute-start.8 = (bf16[136,768]{1,0:T(8,128)(2,1)S(1)}, bf16[136,768]{1,0:T(8,128)(2,1)S(1)}, u32[]{:S(2)}, u32[]{:S(2)}) collective-permute-start(bf16[136,768]{1,0:T(8,128)(2,1)S(1)} %collective-permute-done.refs_0_), channel_id=1, source_target_pairs={{0,4},{4,0},{8,12},{12,8},{1,5},{5,1},{9,13},{13,9},{2,6},{6,2},{1... | collective-permute-start | bytes 626696 | tf_op jit(solution)/shard_map/ppermute | solution.py:273
  22.8 3.9 %pair_work.4 = (bf16[2,128,768]{2,1,0:T(8,128)(2,1)S(1)}, f32[256,128]{1,0:T(8,128)S(1)}, s32[256,128]{1,0:T(8,128)S(1)}, bf16[256,768]{1,0:T(8,128)(2,1)S(1)}, ...) custom-call(bf16[136,768]{1,0:T(8,128)(2,1)S(1)} %copy-done.2, bf16[136,768]{1,0:T(8,128)(2,1)S(1)} %collective-permute-done.1.refs_1_, ...), custom_call_target="tpu_custom_call" | custom-call | flops 1811939328 | bytes 8388608 | tf_op jit(solution)/shard_map/pair_work/pallas_call | solution.py:187
  28.8 2.9 %collective-permute-done.7.refs_1_ = bf16[136,768]{1,0:T(8,128)(2,1)S(1)} collective-permute-done((bf16[136,768]{1,0:T(8,128)(2,1)S(1)}, bf16[136,768]{1,0:T(8,128)(2,1)S(1)}, u32[]{:S(2)}, u32[]{:S(2)}) %collective-permute-start.7) | collective-permute-done | bytes 208928 | tf_op jit(solution)/shard_map/ppermute | solution.py:273
  31.8 3.9 %pair_work.5 = (bf16[2,128,768]{2,1,0:T(8,128)(2,1)S(1)}, f32[256,128]{1,0:T(8,128)S(1)}, s32[256,128]{1,0:T(8,128)S(1)}, bf16[256,768]{1,0:T(8,128)(2,1)S(1)}, f32[768,768]{1,0:T(8,128)S(1)}) custom-call(bf16[136,768]{1,0:T(8,128)(2,1)S(1)} %collective-permute-done.4.refs_0_, bf16[136,768]{1,0:T(8,128)(2,1)S(1)} %collective-permute-done.7.refs_1_, ...), custom_call_target="tpu_custom_call" | custom-call | flops 1811939328 | bytes 8388608 | tf_op jit(solution)/shard_map/pair_work/pallas_call | solution.py:187
  35.7 3.9 %pair_work.6 = (bf16[2,128,768]{2,1,0:T(8,128)(2,1)S(1)}, f32[256,128]{1,0:T(8,128)S(1)}, s32[256,128]{1,0:T(8,128)S(1)}, bf16[256,768]{1,0:T(8,128)(2,1)S(1)}, f32[768,768]{1,0:T(8,128)S(1)}) custom-call(bf16[136,768]{1,0:T(8,128)(2,1)S(1)} %collective-permute-done.refs_0_, bf16[136,768]{1,0:T(8,128)(2,1)S(1)} %collective-permute-done.9.refs_1_, ...), custom_call_target="tpu_custom_call" | custom-call | flops 1811939328 | bytes 8388608 | tf_op jit(solution)/shard_map/pair_work/pallas_call | solution.py:187
  39.6 4.1 %pair_work.7 = (bf16[2,128,768]{2,1,0:T(8,128)(2,1)S(1)}, f32[256,128]{1,0:T(8,128)S(1)}, s32[256,128]{1,0:T(8,128)S(1)}, bf16[256,768]{1,0:T(8,128)(2,1)S(1)}, ...) custom-call(bf16[136,768]{1,0:T(8,128)(2,1)S(1)} %collective-permute-done.8.refs_0_, ...), custom_call_target="tpu_custom_call" | custom-call | flops 1811939328 | bytes 8388608 | tf_op jit(solution)/shard_map/pair_work/pallas_call | solution.py:187
  43.8 1.6 %collective-permute-start.11 = (bf16[2,128,768]{2,1,0:T(8,128)(2,1)S(1)}, bf16[2,128,768]{2,1,0:T(8,128)(2,1)S(1)}, u32[]{:S(2)}, u32[]{:S(2)}) collective-permute-start(bf16[2,128,768]{2,1,0:T(8,128)(2,1)S(1)} %get-tuple-element.61), channel_id=1, source_target_pairs={{0,4},{4,0},{8,12},{12,8},{1,5},{5,1},{9,13},{13,9},{2,6},{6,2},{1... | collective-permute-start | bytes 1179656 | tf_op jit(solution)/shard_map/ppermute | solution.py:273
  45.9 1.6 %collective-permute-start.17 = (bf16[192,768]{1,0:T(8,128)(2,1)S(1)}, bf16[192,768]{1,0:T(8,128)(2,1)S(1)}, u32[]{:S(2)}, u32[]{:S(2)}) collective-permute-start(bf16[192,768]{1,0:T(8,128)(2,1)S(1)} %fusion.3), channel_id=1, source_target_pairs={{0,2},{1,3},{2,0},{3,1},{4,6},{5,7},{6,4},{7,5},{8,10},{9,11},{10,... | collective-permute-start | bytes 884744 | tf_op jit(solution)/shard_map/ppermute | solution.py:273
  48.9 6.4 %collective-permute-done.11 = bf16[2,128,768]{2,1,0:T(8,128)(2,1)S(1)} collective-permute-done((bf16[2,128,768]{2,1,0:T(8,128)(2,1)S(1)}, bf16[2,128,768]{2,1,0:T(8,128)(2,1)S(1)}, u32[]{:S(2)}, u32[]{:S(2)}) %collective-permute-start.11) | collective-permute-done | bytes 393248 | tf_op jit(solution)/shard_map/ppermute | solution.py:273
  55.4 1.6 %collective-permute-start.13 = (bf16[128,768]{1,0:T(8,128)(2,1)S(1)}, bf16[128,768]{1,0:T(8,128)(2,1)S(1)}, u32[]{:S(2)}, u32[]{:S(2)}) collective-permute-start(bf16[128,768]{1,0:T(8,128)(2,1)S(1)} %fusion.5), channel_id=1, source_target_pairs={{0,2},{1,3},{2,0},{3,1},{4,6},{5,7},{6,4},{7,5},{8,10},{9,11},{10,... | collective-permute-start | bytes 589832 | tf_op jit(solution)/shard_map/ppermute | solution.py:273
  57.0 1.4 %collective-permute-start.12 = (bf16[2,128,768]{2,1,0:T(8,128)(2,1)S(1)}, bf16[2,128,768]{2,1,0:T(8,128)(2,1)S(1)}, u32[]{:S(2)}, u32[]{:S(2)}) collective-permute-start(bf16[2,128,768]{2,1,0:T(8,128)(2,1)S(1)} %get-tuple-element.62), channel_id=1, source_target_pairs={{0,4},{4,0},{8,12},{12,8},{1,5},{5,1},{9,13},{13,9},{2,6},{6,2},{1... | collective-permute-start | bytes 1179656 | tf_op jit(solution)/shard_map/ppermute | solution.py:273
  59.3 2.6 %collective-permute-done.13 = bf16[128,768]{1,0:T(8,128)(2,1)S(1)} collective-permute-done((bf16[128,768]{1,0:T(8,128)(2,1)S(1)}, bf16[128,768]{1,0:T(8,128)(2,1)S(1)}, u32[]{:S(2)}, u32[]{:S(2)}) %collective-permute-start.13) | collective-permute-done | bytes 196640 | tf_op jit(solution)/shard_map/ppermute | solution.py:273
  62.0 2.3 %collective-permute-start.15 = (bf16[128,768]{1,0:T(8,128)(2,1)S(1)}, bf16[128,768]{1,0:T(8,128)(2,1)S(1)}, u32[]{:S(2)}, u32[]{:S(2)}) collective-permute-start(bf16[128,768]{1,0:T(8,128)(2,1)S(1)} %fusion), channel_id=1, source_target_pairs={{0,8},{4,12},{8,0},{12,4},{1,9},{5,13},{9,1},{13,5},{2,10},{6,14},... | collective-permute-start | bytes 589832 | tf_op jit(solution)/shard_map/ppermute | solution.py:273
  64.3 10.5 %collective-permute-done.18 = bf16[96,768]{1,0:T(8,128)(2,1)S(1)} collective-permute-done((bf16[96,768]{1,0:T(8,128)(2,1)S(1)}, bf16[96,768]{1,0:T(8,128)(2,1)S(1)}, u32[]{:S(2)}, u32[]{:S(2)}) %collective-permute-start.18) | collective-permute-done | bytes 147488 | tf_op jit(solution)/shard_map/ppermute | solution.py:273
  76.8 6.4 %collective-permute-done.20 = bf16[96,768]{1,0:T(8,128)(2,1)S(1)} collective-permute-done((bf16[96,768]{1,0:T(8,128)(2,1)S(1)}, bf16[96,768]{1,0:T(8,128)(2,1)S(1)}, u32[]{:S(2)}, u32[]{:S(2)}) %collective-permute-start.20) | collective-permute-done | bytes 147488 | tf_op jit(solution)/shard_map/ppermute | solution.py:273
  84.1 2.4 %grad_label_work.3 = bf16[1024,768]{1,0:T(8,128)(2,1)} custom-call(f32[256,128]{1,0:T(8,128)S(1)} %get-tuple-element.57.refs_0_, f32[256,128]{1,0:T(8,128)S(1)} %get-tuple-element.65.refs_1_, f32[256,128]{1,0:T(8,128)S(1)} %get-tuple-element.66.refs_2_, f32[256,128]{1,0:T(8,128)S(1)} %get-tuple-element.67.refs_3_, s32[256,128]{1,0:T(8,128)S(1)} %get-tuple-element.68.refs_4_, ...), custom_call_target="tpu_custom_call" | custom-call | flops 805306368 | bytes 4194304 | tf_op jit(solution)/shard_map/grad_label_work/pallas_call | solution.py:187
  86.4 2.0 %collective-permute-done.21.other_ref = bf16[96,768]{1,0:T(8,128)(2,1)S(1)} collective-permute-done((bf16[96,768]{1,0:T(8,128)(2,1)S(1)}, bf16[96,768]{1,0:T(8,128)(2,1)S(1)}, u32[]{:S(2)}, u32[]{:S(2)}) %collective-permute-start.21) | collective-permute-done | bytes 147488 | tf_op jit(solution)/shard_map/ppermute | solution.py:273
  (43 shorter events, 12.6 us)
Async XLA Ops:
  0.6 9.4 %collective-permute-start.2 = (bf16[1024,768]{1,0:T(8,128)(2,1)}, bf16[1024,768]{1,0:T(8,128)(2,1)S(1)}, u32[]{:S(2)}, u32[]{:S(2)}) collective-permute-start(bf16[1024,768]{1,0:T(8,128)(2,1)} %label_ref), channel_id=1, source_target_pairs={{0,1},{1,0},{2,3},{3,2},{4,5},{5,4},{6,7},{7,6},{8,9},{9,8},{10,11... | collective-permute-start | bytes 4718600 | tf_op jit(solution)/shard_map/ppermute | solution.py:273
  2.8 16.0 %collective-permute-start.3 = (bf16[192,768]{1,0:T(8,128)(2,1)}, bf16[192,768]{1,0:T(8,128)(2,1)S(1)}, u32[]{:S(2)}, u32[]{:S(2)}) collective-permute-start(bf16[192,768]{1,0:T(8,128)(2,1)} %shard_ref.1), channel_id=1, source_target_pairs={{0,2},{1,3},{2,0},{3,1},{4,6},{5,7},{6,4},{7,5},{8,10},{9,11},{10,... | collective-permute-start | bytes 884744 | tf_op jit(solution)/shard_map/ppermute | solution.py:273
  5.4 12.4 %collective-permute-start.1 = (bf16[136,768]{1,0:T(8,128)(2,1)}, bf16[136,768]{1,0:T(8,128)(2,1)S(1)}, u32[]{:S(2)}, u32[]{:S(2)}) collective-permute-start(bf16[136,768]{1,0:T(8,128)(2,1)} %own_block.1.refs_0_), channel_id=1, source_target_pairs={{0,2},{1,3},{2,0},{3,1},{4,6},{5,7},{6,4},{7,5},{8,10},{9,11},{10,... | collective-permute-start | bytes 626696 | tf_op jit(solution)/shard_map/ppermute | solution.py:273
  5.4 13.1 %collective-permute-start = (bf16[136,768]{1,0:T(8,128)(2,1)}, bf16[136,768]{1,0:T(8,128)(2,1)S(1)}, u32[]{:S(2)}, u32[]{:S(2)}) collective-permute-start(bf16[136,768]{1,0:T(8,128)(2,1)} %own_block.1.refs_0_), channel_id=1, source_target_pairs={{0,8},{4,12},{8,0},{12,4},{1,9},{5,13},{9,1},{13,5},{2,10},{6,14},... | collective-permute-start | bytes 626696 | tf_op jit(solution)/shard_map/ppermute | solution.py:273
  8.5 10.3 %collective-permute-start.4 = (bf16[136,768]{1,0:T(8,128)(2,1)}, bf16[136,768]{1,0:T(8,128)(2,1)S(1)}, u32[]{:S(2)}, u32[]{:S(2)}) collective-permute-start(bf16[136,768]{1,0:T(8,128)(2,1)} %own_block.1.refs_0_), channel_id=1, source_target_pairs={{0,4},{4,0},{8,12},{12,8},{1,5},{5,1},{9,13},{13,9},{2,6},{6,2},{1... | collective-permute-start | bytes 626696 | tf_op jit(solution)/shard_map/ppermute | solution.py:273
  10.1 1.4 %copy-start = (bf16[1024,768]{1,0:T(8,128)(2,1)S(1)}, bf16[1024,768]{1,0:T(8,128)(2,1)}, u32[]{:S(2)}) copy-start(bf16[1024,768]{1,0:T(8,128)(2,1)} %label_ref) | copy-start | bytes 4718596
  12.4 10.3 %copy-start.2 = (bf16[136,768]{1,0:T(8,128)(2,1)S(1)}, bf16[136,768]{1,0:T(8,128)(2,1)}, u32[]{:S(2)}) copy-start(bf16[136,768]{1,0:T(8,128)(2,1)} %own_block.1.refs_0_) | copy-start | bytes 626692
  18.8 4.0 %collective-permute-start.5 = (bf16[192,768]{1,0:T(8,128)(2,1)S(1)}, bf16[192,768]{1,0:T(8,128)(2,1)S(1)}, u32[]{:S(2)}, u32[]{:S(2)}) collective-permute-start(bf16[192,768]{1,0:T(8,128)(2,1)S(1)} %copy-done.1), channel_id=1, source_target_pairs={{0,1},{1,0},{2,3},{3,2},{4,5},{5,4},{6,7},{7,6},{8,9},{9,8},{10,11... | collective-permute-start | bytes 884744 | tf_op jit(solution)/shard_map/ppermute | solution.py:273
  18.8 4.0 %collective-permute-start.6 = (bf16[192,768]{1,0:T(8,128)(2,1)S(1)}, bf16[192,768]{1,0:T(8,128)(2,1)S(1)}, u32[]{:S(2)}, u32[]{:S(2)}) collective-permute-start(bf16[192,768]{1,0:T(8,128)(2,1)S(1)} %collective-permute-done.3.refs_6_), channel_id=1, source_target_pairs={{0,1},{1,0},{2,3},{3,2},{4,5},{5,4},{6,7},{7,6},{8,9},{9,8},{10,11... | collective-permute-start | bytes 884744 | tf_op jit(solution)/shard_map/ppermute | solution.py:273
  19.3 8.0 %collective-permute-start.9 = (bf16[136,768]{1,0:T(8,128)(2,1)S(1)}, bf16[136,768]{1,0:T(8,128)(2,1)S(1)}, u32[]{:S(2)}, u32[]{:S(2)}) collective-permute-start(bf16[136,768]{1,0:T(8,128)(2,1)S(1)} %collective-permute-done.refs_0_), channel_id=1, source_target_pairs={{0,2},{1,3},{2,0},{3,1},{4,6},{5,7},{6,4},{7,5},{8,10},{9,11},{10,... | collective-permute-start | bytes 626696 | tf_op jit(solution)/shard_map/ppermute | solution.py:273
  20.8 6.8 %collective-permute-start.8 = (bf16[136,768]{1,0:T(8,128)(2,1)S(1)}, bf16[136,768]{1,0:T(8,128)(2,1)S(1)}, u32[]{:S(2)}, u32[]{:S(2)}) collective-permute-start(bf16[136,768]{1,0:T(8,128)(2,1)S(1)} %collective-permute-done.refs_0_), channel_id=1, source_target_pairs={{0,4},{4,0},{8,12},{12,8},{1,5},{5,1},{9,13},{13,9},{2,6},{6,2},{1... | collective-permute-start | bytes 626696 | tf_op jit(solution)/shard_map/ppermute | solution.py:273
  22.2 9.5 %collective-permute-start.7 = (bf16[136,768]{1,0:T(8,128)(2,1)S(1)}, bf16[136,768]{1,0:T(8,128)(2,1)S(1)}, u32[]{:S(2)}, u32[]{:S(2)}) collective-permute-start(bf16[136,768]{1,0:T(8,128)(2,1)S(1)} %collective-permute-done.4.refs_0_), channel_id=1, source_target_pairs={{0,2},{1,3},{2,0},{3,1},{4,6},{5,7},{6,4},{7,5},{8,10},{9,11},{10,... | collective-permute-start | bytes 626696 | tf_op jit(solution)/shard_map/ppermute | solution.py:273
  27.6 12.0 %collective-permute-start.10 = (bf16[136,768]{1,0:T(8,128)(2,1)S(1)}, bf16[136,768]{1,0:T(8,128)(2,1)S(1)}, u32[]{:S(2)}, u32[]{:S(2)}) collective-permute-start(bf16[136,768]{1,0:T(8,128)(2,1)S(1)} %collective-permute-done.8.refs_0_), channel_id=1, source_target_pairs={{0,2},{1,3},{2,0},{3,1},{4,6},{5,7},{6,4},{7,5},{8,10},{9,11},{10,... | collective-permute-start | bytes 626696 | tf_op jit(solution)/shard_map/ppermute | solution.py:273
  43.7 2.1 %collective-permute-start.16 = (bf16[2,192,768]{2,1,0:T(8,128)(2,1)S(1)}, bf16[2,192,768]{2,1,0:T(8,128)(2,1)S(1)}, u32[]{:S(2)}, u32[]{:S(2)}) collective-permute-start(bf16[2,192,768]{2,1,0:T(8,128)(2,1)S(1)} %get-tuple-element.74), channel_id=1, source_target_pairs={{0,1},{1,0},{2,3},{3,2},{4,5},{5,4},{6,7},{7,6},{8,9},{9,8},{10,11... | collective-permute-start | bytes 1769480 | tf_op jit(solution)/shard_map/ppermute | solution.py:273
  43.8 11.5 %collective-permute-start.11 = (bf16[2,128,768]{2,1,0:T(8,128)(2,1)S(1)}, bf16[2,128,768]{2,1,0:T(8,128)(2,1)S(1)}, u32[]{:S(2)}, u32[]{:S(2)}) collective-permute-start(bf16[2,128,768]{2,1,0:T(8,128)(2,1)S(1)} %get-tuple-element.61), channel_id=1, source_target_pairs={{0,4},{4,0},{8,12},{12,8},{1,5},{5,1},{9,13},{13,9},{2,6},{6,2},{1... | collective-permute-start | bytes 1179656 | tf_op jit(solution)/shard_map/ppermute | solution.py:273
  45.9 12.6 %collective-permute-start.17 = (bf16[192,768]{1,0:T(8,128)(2,1)S(1)}, bf16[192,768]{1,0:T(8,128)(2,1)S(1)}, u32[]{:S(2)}, u32[]{:S(2)}) collective-permute-start(bf16[192,768]{1,0:T(8,128)(2,1)S(1)} %fusion.3), channel_id=1, source_target_pairs={{0,2},{1,3},{2,0},{3,1},{4,6},{5,7},{6,4},{7,5},{8,10},{9,11},{10,... | collective-permute-start | bytes 884744 | tf_op jit(solution)/shard_map/ppermute | solution.py:273
  48.9 35.2 %collective-permute-start.19 = (bf16[1024,768]{1,0:T(8,128)(2,1)S(1)}, bf16[1024,768]{1,0:T(8,128)(2,1)S(1)}, u32[]{:S(2)}, u32[]{:S(2)}) collective-permute-start(bf16[1024,768]{1,0:T(8,128)(2,1)S(1)} %grad_label_work.2), channel_id=1, source_target_pairs={{0,1},{1,0},{2,3},{3,2},{4,5},{5,4},{6,7},{7,6},{8,9},{9,8},{10,11... | collective-permute-start | bytes 4718600 | tf_op jit(solution)/shard_map/ppermute | solution.py:273
  55.4 6.5 %collective-permute-start.13 = (bf16[128,768]{1,0:T(8,128)(2,1)S(1)}, bf16[128,768]{1,0:T(8,128)(2,1)S(1)}, u32[]{:S(2)}, u32[]{:S(2)}) collective-permute-start(bf16[128,768]{1,0:T(8,128)(2,1)S(1)} %fusion.5), channel_id=1, source_target_pairs={{0,2},{1,3},{2,0},{3,1},{4,6},{5,7},{6,4},{7,5},{8,10},{9,11},{10,... | collective-permute-start | bytes 589832 | tf_op jit(solution)/shard_map/ppermute | solution.py:273
  57.0 19.2 %collective-permute-start.12 = (bf16[2,128,768]{2,1,0:T(8,128)(2,1)S(1)}, bf16[2,128,768]{2,1,0:T(8,128)(2,1)S(1)}, u32[]{:S(2)}, u32[]{:S(2)}) collective-permute-start(bf16[2,128,768]{2,1,0:T(8,128)(2,1)S(1)} %get-tuple-element.62), channel_id=1, source_target_pairs={{0,4},{4,0},{8,12},{12,8},{1,5},{5,1},{9,13},{13,9},{2,6},{6,2},{1... | collective-permute-start | bytes 1179656 | tf_op jit(solution)/shard_map/ppermute | solution.py:273
  58.7 16.1 %collective-permute-start.18 = (bf16[96,768]{1,0:T(8,128)(2,1)S(1)}, bf16[96,768]{1,0:T(8,128)(2,1)S(1)}, u32[]{:S(2)}, u32[]{:S(2)}) collective-permute-start(bf16[96,768]{1,0:T(8,128)(2,1)S(1)} %get-tuple-element.77), channel_id=1, source_target_pairs={{0,4},{4,0},{8,12},{12,8},{1,5},{5,1},{9,13},{13,9},{2,6},{6,2},{1... | collective-permute-start | bytes 442376 | tf_op jit(solution)/shard_map/ppermute | solution.py:273
  62.0 21.3 %collective-permute-start.15 = (bf16[128,768]{1,0:T(8,128)(2,1)S(1)}, bf16[128,768]{1,0:T(8,128)(2,1)S(1)}, u32[]{:S(2)}, u32[]{:S(2)}) collective-permute-start(bf16[128,768]{1,0:T(8,128)(2,1)S(1)} %fusion), channel_id=1, source_target_pairs={{0,8},{4,12},{8,0},{12,4},{1,9},{5,13},{9,1},{13,5},{2,10},{6,14},... | collective-permute-start | bytes 589832 | tf_op jit(solution)/shard_map/ppermute | solution.py:273
  74.8 8.3 %collective-permute-start.20 = (bf16[96,768]{1,0:T(8,128)(2,1)S(1)}, bf16[96,768]{1,0:T(8,128)(2,1)S(1)}, u32[]{:S(2)}, u32[]{:S(2)}) collective-permute-start(bf16[96,768]{1,0:T(8,128)(2,1)S(1)} %add_convert_fusion.4), channel_id=1, source_target_pairs={{0,8},{4,12},{8,0},{12,4},{1,9},{5,13},{9,1},{13,5},{2,10},{6,14},... | collective-permute-start | bytes 442376 | tf_op jit(solution)/shard_map/ppermute | solution.py:273
  76.2 7.1 %collective-permute-start.14 = (bf16[128,768]{1,0:T(8,128)(2,1)S(1)}, bf16[128,768]{1,0:T(8,128)(2,1)S(1)}, u32[]{:S(2)}, u32[]{:S(2)}) collective-permute-start(bf16[128,768]{1,0:T(8,128)(2,1)S(1)} %fusion.4), channel_id=1, source_target_pairs={{0,2},{1,3},{2,0},{3,1},{4,6},{5,7},{6,4},{7,5},{8,10},{9,11},{10,... | collective-permute-start | bytes 589832 | tf_op jit(solution)/shard_map/ppermute | solution.py:273
  83.2 5.2 %collective-permute-start.21 = (bf16[96,768]{1,0:T(8,128)(2,1)S(1)}, bf16[96,768]{1,0:T(8,128)(2,1)S(1)}, u32[]{:S(2)}, u32[]{:S(2)}) collective-permute-start(bf16[96,768]{1,0:T(8,128)(2,1)S(1)} %add_convert_fusion.3.mine_ref), channel_id=1, source_target_pairs={{0,4},{4,0},{8,12},{12,8},{1,5},{5,1},{9,13},{13,9},{2,6},{6,2},{1... | collective-permute-start | bytes 442376 | tf_op jit(solution)/shard_map/ppermute | solution.py:273
  (1 other events, 1.0 us)

commit v10 on v9

--- a/solution.py
+++ b/solution.py
@@ -32,7 +32,7 @@
     sources, labels = take(n_sources), take(n_sets)
     shards = take(n_data if first else 0)
     enc, total_in = (None, None) if first else take(2)
-    backs, grad_scores_ref, block_ref, embedding_ref = take(n_sources // 2), *take(3)
+    backs, grad_scores_ref, block_ref, embedding_ref = take(n_sources), *take(3)
     enc = next(it) if first else enc
     shares = take(2 if last else 0)
     total_ref = next(it)
@@ -117,8 +117,7 @@
             grad_feats[(j * n_sources + s) * cap : (j * n_sources + s + 1) * cap]
             for j in range(n_sets)
         ]
-        back = dot(picks[s], jnp.concatenate(parts, axis=0), 0, 0)
-        backs[s // 2][s % 2] = back.astype(BF16)
+        backs[s][...] = dot(picks[s], jnp.concatenate(parts, axis=0), 0, 0).astype(BF16)
 
 
 def grad_label_kernel(*refs, calls, n_sets, j):
@@ -209,8 +208,8 @@
     slots = n_sets * len(sources) * cap
     shard_rows = shards[0].shape[0]
     full = (n_data * shard_rows, width)
-    backs = len(sources) // 2
-    shapes = [shaped((2, rows, width))] * backs
+    backs = len(sources)
+    shapes = [shaped((rows, width))] * backs
     shapes += [shaped((slots, BLK), F32), shaped((slots, BLK), jnp.int32), shaped((slots, width))]
     more = [before["enc"], before["total"]] if before else shards
     scratch = []
@@ -241,7 +240,7 @@
         *labels,
         *more,
     )
-    result = {"back": out[:backs], "slots": list(out[backs : backs + 3])}
+    result = {"back": list(out[:backs]), "slots": list(out[backs : backs + 3])}
     rest = list(out[backs + 3 :])
     result["enc"] = before["enc"] if before else rest.pop(0)
     result["shares" if last else "total"] = rest if last else rest[0]
@@ -306,18 +305,17 @@
 
 
 def dp_terms(even, odd):
-    got = sent = partner(odd, "dp", 1)
+    got = partner(odd, "dp", 1)
     terms = [[even[i], got[i]] for i in range(even.shape[0])]
     for mask in masks(len(terms)):
         for i in range(len(terms)):
             if i & mask == 0 and i % mask == 0:
-                sent = add(*terms[i | mask]).astype(BF16)
-                terms[i].append(partner(sent, "dp", 2 * mask))
-    return got, terms[0], sent
-
-
-def sum_shares(even, odd):
-    got, terms, sent = dp_terms(even, odd)
+                terms[i].append(partner(add(*terms[i | mask]).astype(BF16), "dp", 2 * mask))
+    return got, terms[0]
+
+
+def sum_shares(even, odd, *first):
+    got, terms = dp_terms(even, odd)
     rows, width = even.shape[1:]
     half = rows // 2
     keep, send = call(
@@ -328,14 +326,14 @@
         0,
         1,
         even,
-        got,
+        after(got, *first),
         *terms[2:],
     )
     x = add(keep, partner(send, "labels", 1)).astype(BF16)
     first = x
     for mask in masks(lax.axis_size("labels"))[1:]:
         x = add(x, partner(x, "labels", mask)).astype(BF16)
-    return sent, first, x
+    return keep, first, x
 
 
 def join_halves(x, *first):
@@ -344,15 +342,16 @@
     return call(merge_kernel, "merge_share", out, [], 0, 1, after(x, *first), other)
 
 
-def reduce_runs(runs):
+def reduce_runs(runs, got_last, keep, first):
     n = len(runs)
-    gots = []
+    sums = {}
+    held = [keep]
     for i in reversed(range(0, n, 2)):
-        gots.append(partner(after(runs[i + 1], *gots[-1:]), "labels", 1))
-    sums = {}
-    held = []
-    for i, got in zip(reversed(range(0, n, 2)), gots):
-        parts = [[runs[i][h], got[h]] for h in range(got.shape[0])]
+        got = got_last
+        if i + 2 < n:
+            holds = [[first]] + [held] * (len(runs[i]) - 1)
+            got = [partner(after(x, *hold), "labels", 1) for x, hold in zip(runs[i + 1], holds)]
+        parts = [[part, got[h]] for h, part in enumerate(runs[i])]
         for mask in masks(len(parts)):
             for h in range(0, len(parts), 2 * mask):
                 sent = after(add(*parts[h + mask]).astype(BF16), *held)
@@ -361,7 +360,8 @@
         held = parts[0][-1:]
     for mask in masks(n)[1:]:
         for i in range(0, n, 2 * mask):
-            sums[i].append(partner(add(*sums[i + mask]).astype(BF16), "labels", mask))
+            sent = after(add(*sums[i + mask]).astype(BF16), first)
+            sums[i].append(partner(sent, "labels", mask))
     return add(*sums[0]).astype(BF16)
 
 
@@ -409,30 +409,28 @@
             enc_weight,
         )
         near = gather_labels(own, labels[0])
-        far, works = [], []
-        for by in range(n_labels):
-            last = by == n_labels - 1
-            held = far[0][1:] if by else []
-            if last and works:
-                held = held + far[-1][1:] + works[0]["slots"][:1]
-            far.append(gather_far(after(near[by], *held)))
-            if by == 0:
-                shards = gather_near(
-                    gather_far(after(enc_weight, own)), *far[0][1:], *near[1:3], labels[0]
-                )
-                shards[0] = own_shard
-                far[0][0] = after(far[0][0], near[2 % n_labels])
-            if by == 0 or last:
-                for run in range(len(works), by + 1):
-                    sources = [near[run] if run else far[0][0]] + far[run][1:]
-                    before = works[-1] if works else None
-                    final = run == n_labels - 1
-                    works.append(pair_work(sources, labels, shards, cap, pick_count, before, final))
-        sent, first, share = sum_shares(*works[-1]["shares"])
-        grad_feats = reduce_runs([back for work in works for back in work["back"]])
-        works[0]["slots"][2] = after(works[0]["slots"][2], sent)
+        far = {0: gather_far(near[0])}
+        shards = gather_near(gather_far(enc_weight), *far[0][1:], *near[1:3], labels[0])
+        shards[0] = own_shard
+        works, backs = [], {}
+        for run in [*range(0, n_labels, 2), *range(1, n_labels, 2)]:
+            last = run == n_labels - 1
+            if last:
+                far[run] = gather_far(after(near[run], *far[run - 1][1:]))
+            elif run % 2:
+                sent = [after(x, works[0]["slots"][0]) for x in far[run - 1][1:]]
+                far[run] = near[run : run + 1] + [partner(x, "labels", 1) for x in sent]
+            elif run:
+                far[run] = gather_far(after(near[run], *far[0][1:]))
+            sources = [after(near[run], *([] if run else near[1:3]))] + far[run][1:]
+            before = works[-1] if works else None
+            works.append(pair_work(sources, labels, shards, cap, pick_count, before, last))
+            backs[run] = works[-1]["back"]
+        got_last = [partner(x, "labels", 1) for x in works[-1]["back"]]
+        keep, first, share = sum_shares(*works[-1]["shares"], *got_last[1:])
+        grad_feats = reduce_runs(backs, got_last, keep, first)
+        works[0]["slots"][2] = after(works[0]["slots"][2], *got_last[1:])
         other = partner(grad_label_work(works, 2, 1, label_weight.shape), "dp", 1)
-        works[0]["slots"][2] = after(works[0]["slots"][2], first)
         grad_label = grad_label_work(works, 2, 0, label_weight.shape, other)
         grad_enc = join_halves(share, grad_label, grad_feats)
     else:
@@ -466,7 +464,7 @@
         back = jnp.concatenate([back for work in works for back in work["back"]], axis=0)
         back = swap(back.reshape(n_labels, n_data, cap, width)).reshape(slot_total, width)
         grad_feats = dot(pick, back, 0, 0).astype(BF16)
-        _, _, share = sum_shares(*works[-1]["shares"])
+        *_, share = sum_shares(*works[-1]["shares"])
         grad_label = grad_label_work(works, 1, 0, label_weight.shape)
         grad_enc = join_halves(share, grad_label, grad_feats)
 

time: 89.5 us -> 90 us (level)
  waiting for transfers between devices: 38.3 us -> 40.6 us
  starting transfers between devices: 24.3 us -> 22.6 us
    ppermute x22 -> x24, waiting for transfers between devices: 38.3 us -> 40.6 us  [partner(): lax.ppermute(x, axis, [(i, i ^ mask) for i in range(lax.axis_size(axis))])]
    ppermute x22 -> x24, starting transfers between devices: 24.3 us -> 22.6 us  [partner(): lax.ppermute(x, axis, [(i, i ^ mask) for i in range(lax.axis_size(axis))])]
  transfers between devices with their start and end apart: 22 -> 24, of which waited for: 12 -> 11; matrix products, arithmetic and copies ran while one was open for 1% -> 1% of each run, Pallas kernels for 20% -> 19%
where the time goes in v10:
time: 90 us; the launch traced here: 89.8 us
  waiting for transfers between devices  40.6 us (45%)
  starting transfers between devices  22.6 us (25%)
  Pallas kernels  22.3 us (25%)
  local copies, waits for them, and re-layouts  2.37 us (3%)
  other arithmetic  1.1 us (1%)
    ppermute x24, waiting for transfers between devices, partner(): lax.ppermute(x, axis, [(i, i ^ mask) for i in range(lax.axis_size(axis))])  40.6 us
    ppermute x24, starting transfers between devices, partner(): lax.ppermute(x, axis, [(i, i ^ mask) for i in range(lax.axis_size(axis))])  22.6 us
    pallas_call x10, Pallas kernels, call(): pl.pallas_call(kernel, in_specs=[space] * len(args), out_specs=jax.tree.m...  22.3 us
    unnamed x6, local copies, waits for them, and re-layouts  2.37 us
  transfers between devices with their start and end apart: 24, of which 11 were waited for; matrix products, arithmetic and copies ran while one was open for 1% of the time, Pallas kernels for 19%

profile of v10, /device:TPU:0, one launch (start us, length us, event | category | flops | bytes accessed | tf_op | source)
XLA Modules:
  0.0 89.8 jit_solution(5438099602338531484)
XLA Ops:
  1.1 2.6 %collective-permute-start.4 = (bf16[192,768]{1,0:T(8,128)(2,1)}, bf16[192,768]{1,0:T(8,128)(2,1)S(1)}, u32[]{:S(2)}, u32[]{:S(2)}) collective-permute-start(bf16[192,768]{1,0:T(8,128)(2,1)} %shard_ref.1), channel_id=1, source_target_pairs={{0,2},{1,3},{2,0},{3,1},{4,6},{5,7},{6,4},{7,5},{8,10},{9,11},{10,... | collective-permute-start | bytes 884744 | tf_op jit(solution)/shard_map/ppermute | solution.py:272
  3.7 1.6 %own_block.1.refs_0_ = bf16[136,768]{1,0:T(8,128)(2,1)} custom-call(bf16[128,768]{1,0:T(8,128)(2,1)} %feats_ref.1, s32[4,128]{1,0:T(4,128)} %bitcast.5, s32[4,128]{1,0:T(4,128)} %bitcast.6, s32[4,128]{1,0:T(4,128)} %bitcast.7), custom_call_target="tpu_custom_call" | custom-call | bytes 1048576 | tf_op jit(solution)/shard_map/own_block/pallas_call | solution.py:186
  5.4 3.1 %collective-permute-start.1 = (bf16[136,768]{1,0:T(8,128)(2,1)}, bf16[136,768]{1,0:T(8,128)(2,1)S(1)}, u32[]{:S(2)}, u32[]{:S(2)}) collective-permute-start(bf16[136,768]{1,0:T(8,128)(2,1)} %own_block.1.refs_0_), channel_id=1, source_target_pairs={{0,8},{4,12},{8,0},{12,4},{1,9},{5,13},{9,1},{13,5},{2,10},{6,14},... | collective-permute-start | bytes 626696 | tf_op jit(solution)/shard_map/ppermute | solution.py:272
  8.6 1.6 %collective-permute-start = (bf16[136,768]{1,0:T(8,128)(2,1)}, bf16[136,768]{1,0:T(8,128)(2,1)S(1)}, u32[]{:S(2)}, u32[]{:S(2)}) collective-permute-start(bf16[136,768]{1,0:T(8,128)(2,1)} %own_block.1.refs_0_), channel_id=1, source_target_pairs={{0,4},{4,0},{8,12},{12,8},{1,5},{5,1},{9,13},{13,9},{2,6},{6,2},{1... | collective-permute-start | bytes 626696 | tf_op jit(solution)/shard_map/ppermute | solution.py:272
  10.1 1.4 %copy-done = bf16[1024,768]{1,0:T(8,128)(2,1)S(1)} copy-done((bf16[1024,768]{1,0:T(8,128)(2,1)S(1)}, bf16[1024,768]{1,0:T(8,128)(2,1)}, u32[]{:S(2)}) %copy-start) | copy-done | bytes 1572888
  12.6 3.4 %collective-permute-done.2.refs_1_ = bf16[136,768]{1,0:T(8,128)(2,1)S(1)} collective-permute-done((bf16[136,768]{1,0:T(8,128)(2,1)}, bf16[136,768]{1,0:T(8,128)(2,1)S(1)}, u32[]{:S(2)}, u32[]{:S(2)}) %collective-permute-start.2) | collective-permute-done | bytes 208928 | tf_op jit(solution)/shard_map/ppermute | solution.py:272
  16.0 2.6 %collective-permute-done.1.refs_0_ = bf16[136,768]{1,0:T(8,128)(2,1)S(1)} collective-permute-done((bf16[136,768]{1,0:T(8,128)(2,1)}, bf16[136,768]{1,0:T(8,128)(2,1)S(1)}, u32[]{:S(2)}, u32[]{:S(2)}) %collective-permute-start.1) | collective-permute-done | bytes 208928 | tf_op jit(solution)/shard_map/ppermute | solution.py:272
  19.3 1.5 %collective-permute-start.8 = (bf16[136,768]{1,0:T(8,128)(2,1)S(1)}, bf16[136,768]{1,0:T(8,128)(2,1)S(1)}, u32[]{:S(2)}, u32[]{:S(2)}) collective-permute-start(bf16[136,768]{1,0:T(8,128)(2,1)S(1)} %collective-permute-done.1.refs_0_), channel_id=1, source_target_pairs={{0,2},{1,3},{2,0},{3,1},{4,6},{5,7},{6,4},{7,5},{8,10},{9,11},{10,... | collective-permute-start | bytes 626696 | tf_op jit(solution)/shard_map/ppermute | solution.py:272
  20.8 1.4 %collective-permute-start.9 = (bf16[136,768]{1,0:T(8,128)(2,1)S(1)}, bf16[136,768]{1,0:T(8,128)(2,1)S(1)}, u32[]{:S(2)}, u32[]{:S(2)}) collective-permute-start(bf16[136,768]{1,0:T(8,128)(2,1)S(1)} %collective-permute-done.1.refs_0_), channel_id=1, source_target_pairs={{0,4},{4,0},{8,12},{12,8},{1,5},{5,1},{9,13},{13,9},{2,6},{6,2},{1... | collective-permute-start | bytes 626696 | tf_op jit(solution)/shard_map/ppermute | solution.py:272
  22.3 3.9 %pair_work.4 = (bf16[128,768]{1,0:T(8,128)(2,1)S(1)}, bf16[128,768]{1,0:T(8,128)(2,1)S(1)}, f32[256,128]{1,0:T(8,128)S(1)}, s32[256,128]{1,0:T(8,128)S(1)}, bf16...) custom-call(bf16[136,768]{1,0:T(8,128)(2,1)S(1)} %copy-done.2, ...), custom_call_target="tpu_custom_call" | custom-call | flops 1811939328 | bytes 8388608 | tf_op jit(solution)/shard_map/pair_work/pallas_call | solution.py:186
  28.1 3.9 %pair_work.5 = (bf16[128,768]{1,0:T(8,128)(2,1)S(1)}, bf16[128,768]{1,0:T(8,128)(2,1)S(1)}, f32[256,128]{1,0:T(8,128)S(1)}, s32[256,128]{1,0:T(8,128)S(1)}, bf16...) custom-call(bf16[136,768]{1,0:T(8,128)(2,1)S(1)} %collective-permute-done.1.refs_0_, ...), custom_call_target="tpu_custom_call" | custom-call | flops 1811939328 | bytes 8388608 | tf_op jit(solution)/shard_map/pair_work/pallas_call | solution.py:186
  32.8 3.9 %pair_work.6 = (bf16[128,768]{1,0:T(8,128)(2,1)S(1)}, bf16[128,768]{1,0:T(8,128)(2,1)S(1)}, f32[256,128]{1,0:T(8,128)S(1)}, s32[256,128]{1,0:T(8,128)S(1)}, bf16...) custom-call(bf16[136,768]{1,0:T(8,128)(2,1)S(1)} %collective-permute-done.refs_0_, ...), custom_call_target="tpu_custom_call" | custom-call | flops 1811939328 | bytes 8388608 | tf_op jit(solution)/shard_map/pair_work/pallas_call | solution.py:186
  36.7 4.1 %pair_work.7 = (bf16[128,768]{1,0:T(8,128)(2,1)S(1)}, bf16[128,768]{1,0:T(8,128)(2,1)S(1)}, f32[256,128]{1,0:T(8,128)S(1)}, s32[256,128]{1,0:T(8,128)S(1)}, bf16...) custom-call(bf16[136,768]{1,0:T(8,128)(2,1)S(1)} %collective-permute-done.9.refs_0_, ...), custom_call_target="tpu_custom_call" | custom-call | flops 1811939328 | bytes 8388608 | tf_op jit(solution)/shard_map/pair_work/pallas_call | solution.py:186
  41.7 1.2 %collective-permute-done.11.got_ref = bf16[2,192,768]{2,1,0:T(8,128)(2,1)S(1)} collective-permute-done((bf16[2,192,768]{2,1,0:T(8,128)(2,1)S(1)}, bf16[2,192,768]{2,1,0:T(8,128)(2,1)S(1)}, u32[]{:S(2)}, u32[]{:S(2)}) %collective-permute-start.11) | collective-permute-done | bytes 589856 | tf_op jit(solution)/shard_map/ppermute | solution.py:272
  43.8 4.4 %collective-permute-done.12 = bf16[128,768]{1,0:T(8,128)(2,1)S(1)} collective-permute-done((bf16[128,768]{1,0:T(8,128)(2,1)S(1)}, bf16[128,768]{1,0:T(8,128)(2,1)S(1)}, u32[]{:S(2)}, u32[]{:S(2)}) %collective-permute-start.12) | collective-permute-done | bytes 196640 | tf_op jit(solution)/shard_map/ppermute | solution.py:272
  48.2 1.2 %grad_label_work.2 = bf16[1024,768]{1,0:T(8,128)(2,1)S(1)} custom-call(f32[256,128]{1,0:T(8,128)S(1)} %get-tuple-element.56.refs_0_, f32[256,128]{1,0:T(8,128)S(1)} %get-tuple-element.82.refs_1_, f32[256,128]{1,0:T(8,128)S(1)} %get-tuple-element.83.refs_2_, f32[256,128]{1,0:T(8,128)S(1)} %get-tuple-element.84.refs_3_, ...), custom_call_target="tpu_custom_call" | custom-call | flops 805306368 | bytes 4194304 | tf_op jit(solution)/shard_map/grad_label_work/pallas_call | solution.py:186
  50.3 1.8 %collective-permute-done.13.refs_0_ = bf16[192,768]{1,0:T(8,128)(2,1)S(1)} collective-permute-done((bf16[192,768]{1,0:T(8,128)(2,1)S(1)}, bf16[192,768]{1,0:T(8,128)(2,1)S(1)}, u32[]{:S(2)}, u32[]{:S(2)}) %collective-permute-start.13) | collective-permute-done | bytes 294944 | tf_op jit(solution)/shard_map/ppermute | solution.py:272
  53.2 1.5 %collective-permute-start.16 = (bf16[128,768]{1,0:T(8,128)(2,1)S(1)}, bf16[128,768]{1,0:T(8,128)(2,1)S(1)}, u32[]{:S(2)}, u32[]{:S(2)}) collective-permute-start(bf16[128,768]{1,0:T(8,128)(2,1)S(1)} %add_convert_fusion.4), channel_id=1, source_target_pairs={{0,2},{1,3},{2,0},{3,1},{4,6},{5,7},{6,4},{7,5},{8,10},{9,11},{10,... | collective-permute-start | bytes 589832 | tf_op jit(solution)/shard_map/ppermute | solution.py:272
  54.7 5.3 %collective-permute-done.14 = bf16[96,768]{1,0:T(8,128)(2,1)S(1)} collective-permute-done((bf16[96,768]{1,0:T(8,128)(2,1)S(1)}, bf16[96,768]{1,0:T(8,128)(2,1)S(1)}, u32[]{:S(2)}, u32[]{:S(2)}) %collective-permute-start.14) | collective-permute-done | bytes 147488 | tf_op jit(solution)/shard_map/ppermute | solution.py:272
  60.0 2.4 %collective-permute-start.22 = (bf16[96,768]{1,0:T(8,128)(2,1)S(1)}, bf16[96,768]{1,0:T(8,128)(2,1)S(1)}, u32[]{:S(2)}, u32[]{:S(2)}) collective-permute-start(bf16[96,768]{1,0:T(8,128)(2,1)S(1)} %add_convert_fusion.6), channel_id=1, source_target_pairs={{0,8},{4,12},{8,0},{12,4},{1,9},{5,13},{9,1},{13,5},{2,10},{6,14},... | collective-permute-start | bytes 442376 | tf_op jit(solution)/shard_map/ppermute | solution.py:272
  63.2 1.3 %collective-permute-start.17 = (bf16[128,768]{1,0:T(8,128)(2,1)S(1)}, bf16[128,768]{1,0:T(8,128)(2,1)S(1)}, u32[]{:S(2)}, u32[]{:S(2)}) collective-permute-start(bf16[128,768]{1,0:T(8,128)(2,1)S(1)} %get-tuple-element.77), channel_id=1, source_target_pairs={{0,4},{4,0},{8,12},{12,8},{1,5},{5,1},{9,13},{13,9},{2,6},{6,2},{1... | collective-permute-start | bytes 589832 | tf_op jit(solution)/shard_map/ppermute | solution.py:272
  65.2 14.8 %collective-permute-done.17 = bf16[128,768]{1,0:T(8,128)(2,1)S(1)} collective-permute-done((bf16[128,768]{1,0:T(8,128)(2,1)S(1)}, bf16[128,768]{1,0:T(8,128)(2,1)S(1)}, u32[]{:S(2)}, u32[]{:S(2)}) %collective-permute-start.17) | collective-permute-done | bytes 196640 | tf_op jit(solution)/shard_map/ppermute | solution.py:272
  80.3 5.5 %collective-permute-done.18 = bf16[128,768]{1,0:T(8,128)(2,1)S(1)} collective-permute-done((bf16[128,768]{1,0:T(8,128)(2,1)S(1)}, bf16[128,768]{1,0:T(8,128)(2,1)S(1)}, u32[]{:S(2)}, u32[]{:S(2)}) %collective-permute-start.18) | collective-permute-done | bytes 196640 | tf_op jit(solution)/shard_map/ppermute | solution.py:272
  86.5 2.4 %grad_label_work.3 = bf16[1024,768]{1,0:T(8,128)(2,1)} custom-call(f32[256,128]{1,0:T(8,128)S(1)} %get-tuple-element.56.refs_0_, f32[256,128]{1,0:T(8,128)S(1)} %get-tuple-element.82.refs_1_, f32[256,128]{1,0:T(8,128)S(1)} %get-tuple-element.83.refs_2_, f32[256,128]{1,0:T(8,128)S(1)} %get-tuple-element.84.refs_3_, s32[256,128]{1,0:T(8,128)S(1)} %get-tuple-element.85.refs_4_, ...), custom_call_target="tpu_custom_call" | custom-call | flops 805306368 | bytes 4194304 | tf_op jit(solution)/shard_map/grad_label_work/pallas_call | solution.py:186
  (47 shorter events, 12.2 us)
Async XLA Ops:
  0.6 9.5 %collective-permute-start.3 = (bf16[1024,768]{1,0:T(8,128)(2,1)}, bf16[1024,768]{1,0:T(8,128)(2,1)S(1)}, u32[]{:S(2)}, u32[]{:S(2)}) collective-permute-start(bf16[1024,768]{1,0:T(8,128)(2,1)} %label_ref), channel_id=1, source_target_pairs={{0,1},{1,0},{2,3},{3,2},{4,5},{5,4},{6,7},{7,6},{8,9},{9,8},{10,11... | collective-permute-start | bytes 4718600 | tf_op jit(solution)/shard_map/ppermute | solution.py:272
  1.1 17.6 %collective-permute-start.4 = (bf16[192,768]{1,0:T(8,128)(2,1)}, bf16[192,768]{1,0:T(8,128)(2,1)S(1)}, u32[]{:S(2)}, u32[]{:S(2)}) collective-permute-start(bf16[192,768]{1,0:T(8,128)(2,1)} %shard_ref.1), channel_id=1, source_target_pairs={{0,2},{1,3},{2,0},{3,1},{4,6},{5,7},{6,4},{7,5},{8,10},{9,11},{10,... | collective-permute-start | bytes 884744 | tf_op jit(solution)/shard_map/ppermute | solution.py:272
  5.4 10.6 %collective-permute-start.2 = (bf16[136,768]{1,0:T(8,128)(2,1)}, bf16[136,768]{1,0:T(8,128)(2,1)S(1)}, u32[]{:S(2)}, u32[]{:S(2)}) collective-permute-start(bf16[136,768]{1,0:T(8,128)(2,1)} %own_block.1.refs_0_), channel_id=1, source_target_pairs={{0,2},{1,3},{2,0},{3,1},{4,6},{5,7},{6,4},{7,5},{8,10},{9,11},{10,... | collective-permute-start | bytes 626696 | tf_op jit(solution)/shard_map/ppermute | solution.py:272
  5.4 13.1 %collective-permute-start.1 = (bf16[136,768]{1,0:T(8,128)(2,1)}, bf16[136,768]{1,0:T(8,128)(2,1)S(1)}, u32[]{:S(2)}, u32[]{:S(2)}) collective-permute-start(bf16[136,768]{1,0:T(8,128)(2,1)} %own_block.1.refs_0_), channel_id=1, source_target_pairs={{0,8},{4,12},{8,0},{12,4},{1,9},{5,13},{9,1},{13,5},{2,10},{6,14},... | collective-permute-start | bytes 626696 | tf_op jit(solution)/shard_map/ppermute | solution.py:272
  8.6 10.2 %collective-permute-start = (bf16[136,768]{1,0:T(8,128)(2,1)}, bf16[136,768]{1,0:T(8,128)(2,1)S(1)}, u32[]{:S(2)}, u32[]{:S(2)}) collective-permute-start(bf16[136,768]{1,0:T(8,128)(2,1)} %own_block.1.refs_0_), channel_id=1, source_target_pairs={{0,4},{4,0},{8,12},{12,8},{1,5},{5,1},{9,13},{13,9},{2,6},{6,2},{1... | collective-permute-start | bytes 626696 | tf_op jit(solution)/shard_map/ppermute | solution.py:272
  18.8 3.5 %collective-permute-start.5 = (bf16[192,768]{1,0:T(8,128)(2,1)S(1)}, bf16[192,768]{1,0:T(8,128)(2,1)S(1)}, u32[]{:S(2)}, u32[]{:S(2)}) collective-permute-start(bf16[192,768]{1,0:T(8,128)(2,1)S(1)} %copy-done.1), channel_id=1, source_target_pairs={{0,1},{1,0},{2,3},{3,2},{4,5},{5,4},{6,7},{7,6},{8,9},{9,8},{10,11... | collective-permute-start | bytes 884744 | tf_op jit(solution)/shard_map/ppermute | solution.py:272
  18.8 3.5 %collective-permute-start.6 = (bf16[192,768]{1,0:T(8,128)(2,1)S(1)}, bf16[192,768]{1,0:T(8,128)(2,1)S(1)}, u32[]{:S(2)}, u32[]{:S(2)}) collective-permute-start(bf16[192,768]{1,0:T(8,128)(2,1)S(1)} %collective-permute-done.4.refs_6_), channel_id=1, source_target_pairs={{0,1},{1,0},{2,3},{3,2},{4,5},{5,4},{6,7},{7,6},{8,9},{9,8},{10,11... | collective-permute-start | bytes 884744 | tf_op jit(solution)/shard_map/ppermute | solution.py:272
  19.3 7.6 %collective-permute-start.8 = (bf16[136,768]{1,0:T(8,128)(2,1)S(1)}, bf16[136,768]{1,0:T(8,128)(2,1)S(1)}, u32[]{:S(2)}, u32[]{:S(2)}) collective-permute-start(bf16[136,768]{1,0:T(8,128)(2,1)S(1)} %collective-permute-done.1.refs_0_), channel_id=1, source_target_pairs={{0,2},{1,3},{2,0},{3,1},{4,6},{5,7},{6,4},{7,5},{8,10},{9,11},{10,... | collective-permute-start | bytes 626696 | tf_op jit(solution)/shard_map/ppermute | solution.py:272
  20.8 6.8 %collective-permute-start.9 = (bf16[136,768]{1,0:T(8,128)(2,1)S(1)}, bf16[136,768]{1,0:T(8,128)(2,1)S(1)}, u32[]{:S(2)}, u32[]{:S(2)}) collective-permute-start(bf16[136,768]{1,0:T(8,128)(2,1)S(1)} %collective-permute-done.1.refs_0_), channel_id=1, source_target_pairs={{0,4},{4,0},{8,12},{12,8},{1,5},{5,1},{9,13},{13,9},{2,6},{6,2},{1... | collective-permute-start | bytes 626696 | tf_op jit(solution)/shard_map/ppermute | solution.py:272
  26.2 6.6 %collective-permute-start.7 = (bf16[136,768]{1,0:T(8,128)(2,1)S(1)}, bf16[136,768]{1,0:T(8,128)(2,1)S(1)}, u32[]{:S(2)}, u32[]{:S(2)}) collective-permute-start(bf16[136,768]{1,0:T(8,128)(2,1)S(1)} %collective-permute-done.2.refs_1_), channel_id=1, source_target_pairs={{0,4},{4,0},{8,12},{12,8},{1,5},{5,1},{9,13},{13,9},{2,6},{6,2},{1... | collective-permute-start | bytes 626696 | tf_op jit(solution)/shard_map/ppermute | solution.py:272
  27.6 9.1 %collective-permute-start.10 = (bf16[136,768]{1,0:T(8,128)(2,1)S(1)}, bf16[136,768]{1,0:T(8,128)(2,1)S(1)}, u32[]{:S(2)}, u32[]{:S(2)}) collective-permute-start(bf16[136,768]{1,0:T(8,128)(2,1)S(1)} %collective-permute-done.9.refs_0_), channel_id=1, source_target_pairs={{0,2},{1,3},{2,0},{3,1},{4,6},{5,7},{6,4},{7,5},{8,10},{9,11},{10,... | collective-permute-start | bytes 626696 | tf_op jit(solution)/shard_map/ppermute | solution.py:272
  40.8 2.1 %collective-permute-start.11 = (bf16[2,192,768]{2,1,0:T(8,128)(2,1)S(1)}, bf16[2,192,768]{2,1,0:T(8,128)(2,1)S(1)}, u32[]{:S(2)}, u32[]{:S(2)}) collective-permute-start(bf16[2,192,768]{2,1,0:T(8,128)(2,1)S(1)} %get-tuple-element.67), channel_id=1, source_target_pairs={{0,1},{1,0},{2,3},{3,2},{4,5},{5,4},{6,7},{7,6},{8,9},{9,8},{10,11... | collective-permute-start | bytes 1769480 | tf_op jit(solution)/shard_map/ppermute | solution.py:272
  40.9 7.3 %collective-permute-start.12 = (bf16[128,768]{1,0:T(8,128)(2,1)S(1)}, bf16[128,768]{1,0:T(8,128)(2,1)S(1)}, u32[]{:S(2)}, u32[]{:S(2)}) collective-permute-start(bf16[128,768]{1,0:T(8,128)(2,1)S(1)} %get-tuple-element.68), channel_id=1, source_target_pairs={{0,4},{4,0},{8,12},{12,8},{1,5},{5,1},{9,13},{13,9},{2,6},{6,2},{1... | collective-permute-start | bytes 589832 | tf_op jit(solution)/shard_map/ppermute | solution.py:272
  43.0 9.1 %collective-permute-start.13 = (bf16[192,768]{1,0:T(8,128)(2,1)S(1)}, bf16[192,768]{1,0:T(8,128)(2,1)S(1)}, u32[]{:S(2)}, u32[]{:S(2)}) collective-permute-start(bf16[192,768]{1,0:T(8,128)(2,1)S(1)} %fusion), channel_id=1, source_target_pairs={{0,2},{1,3},{2,0},{3,1},{4,6},{5,7},{6,4},{7,5},{8,10},{9,11},{10,... | collective-permute-start | bytes 884744 | tf_op jit(solution)/shard_map/ppermute | solution.py:272
  49.4 37.1 %collective-permute-start.21 = (bf16[1024,768]{1,0:T(8,128)(2,1)S(1)}, bf16[1024,768]{1,0:T(8,128)(2,1)S(1)}, u32[]{:S(2)}, u32[]{:S(2)}) collective-permute-start(bf16[1024,768]{1,0:T(8,128)(2,1)S(1)} %grad_label_work.2), channel_id=1, source_target_pairs={{0,1},{1,0},{2,3},{3,2},{4,5},{5,4},{6,7},{7,6},{8,9},{9,8},{10,11... | collective-permute-start | bytes 4718600 | tf_op jit(solution)/shard_map/ppermute | solution.py:272
  49.5 15.0 %collective-permute-start.19 = (bf16[128,768]{1,0:T(8,128)(2,1)S(1)}, bf16[128,768]{1,0:T(8,128)(2,1)S(1)}, u32[]{:S(2)}, u32[]{:S(2)}) collective-permute-start(bf16[128,768]{1,0:T(8,128)(2,1)S(1)} %get-tuple-element.80), channel_id=1, source_target_pairs={{0,4},{4,0},{8,12},{12,8},{1,5},{5,1},{9,13},{13,9},{2,6},{6,2},{1... | collective-permute-start | bytes 589832 | tf_op jit(solution)/shard_map/ppermute | solution.py:272
  52.3 7.7 %collective-permute-start.14 = (bf16[96,768]{1,0:T(8,128)(2,1)S(1)}, bf16[96,768]{1,0:T(8,128)(2,1)S(1)}, u32[]{:S(2)}, u32[]{:S(2)}) collective-permute-start(bf16[96,768]{1,0:T(8,128)(2,1)S(1)} %get-tuple-element.71), channel_id=1, source_target_pairs={{0,4},{4,0},{8,12},{12,8},{1,5},{5,1},{9,13},{13,9},{2,6},{6,2},{1... | collective-permute-start | bytes 442376 | tf_op jit(solution)/shard_map/ppermute | solution.py:272
  53.2 10.1 %collective-permute-start.16 = (bf16[128,768]{1,0:T(8,128)(2,1)S(1)}, bf16[128,768]{1,0:T(8,128)(2,1)S(1)}, u32[]{:S(2)}, u32[]{:S(2)}) collective-permute-start(bf16[128,768]{1,0:T(8,128)(2,1)S(1)} %add_convert_fusion.4), channel_id=1, source_target_pairs={{0,2},{1,3},{2,0},{3,1},{4,6},{5,7},{6,4},{7,5},{8,10},{9,11},{10,... | collective-permute-start | bytes 589832 | tf_op jit(solution)/shard_map/ppermute | solution.py:272
  60.0 20.1 %collective-permute-start.22 = (bf16[96,768]{1,0:T(8,128)(2,1)S(1)}, bf16[96,768]{1,0:T(8,128)(2,1)S(1)}, u32[]{:S(2)}, u32[]{:S(2)}) collective-permute-start(bf16[96,768]{1,0:T(8,128)(2,1)S(1)} %add_convert_fusion.6), channel_id=1, source_target_pairs={{0,8},{4,12},{8,0},{12,4},{1,9},{5,13},{9,1},{13,5},{2,10},{6,14},... | collective-permute-start | bytes 442376 | tf_op jit(solution)/shard_map/ppermute | solution.py:272
  62.5 17.8 %collective-permute-start.15 = (bf16[128,768]{1,0:T(8,128)(2,1)S(1)}, bf16[128,768]{1,0:T(8,128)(2,1)S(1)}, u32[]{:S(2)}, u32[]{:S(2)}) collective-permute-start(bf16[128,768]{1,0:T(8,128)(2,1)S(1)} %get-tuple-element.72), channel_id=1, source_target_pairs={{0,4},{4,0},{8,12},{12,8},{1,5},{5,1},{9,13},{13,9},{2,6},{6,2},{1... | collective-permute-start | bytes 589832 | tf_op jit(solution)/shard_map/ppermute | solution.py:272
  63.2 16.7 %collective-permute-start.17 = (bf16[128,768]{1,0:T(8,128)(2,1)S(1)}, bf16[128,768]{1,0:T(8,128)(2,1)S(1)}, u32[]{:S(2)}, u32[]{:S(2)}) collective-permute-start(bf16[128,768]{1,0:T(8,128)(2,1)S(1)} %get-tuple-element.77), channel_id=1, source_target_pairs={{0,4},{4,0},{8,12},{12,8},{1,5},{5,1},{9,13},{13,9},{2,6},{6,2},{1... | collective-permute-start | bytes 589832 | tf_op jit(solution)/shard_map/ppermute | solution.py:272
  64.6 15.7 %collective-permute-start.20 = (bf16[128,768]{1,0:T(8,128)(2,1)S(1)}, bf16[128,768]{1,0:T(8,128)(2,1)S(1)}, u32[]{:S(2)}, u32[]{:S(2)}) collective-permute-start(bf16[128,768]{1,0:T(8,128)(2,1)S(1)} %add_convert_fusion.2), channel_id=1, source_target_pairs={{0,8},{4,12},{8,0},{12,4},{1,9},{5,13},{9,1},{13,5},{2,10},{6,14},... | collective-permute-start | bytes 589832 | tf_op jit(solution)/shard_map/ppermute | solution.py:272
  80.0 5.7 %collective-permute-start.18 = (bf16[128,768]{1,0:T(8,128)(2,1)S(1)}, bf16[128,768]{1,0:T(8,128)(2,1)S(1)}, u32[]{:S(2)}, u32[]{:S(2)}) collective-permute-start(bf16[128,768]{1,0:T(8,128)(2,1)S(1)} %add_convert_fusion.3), channel_id=1, source_target_pairs={{0,2},{1,3},{2,0},{3,1},{4,6},{5,7},{6,4},{7,5},{8,10},{9,11},{10,... | collective-permute-start | bytes 589832 | tf_op jit(solution)/shard_map/ppermute | solution.py:272
  80.2 8.8 %collective-permute-start.23 = (bf16[96,768]{1,0:T(8,128)(2,1)S(1)}, bf16[96,768]{1,0:T(8,128)(2,1)S(1)}, u32[]{:S(2)}, u32[]{:S(2)}) collective-permute-start(bf16[96,768]{1,0:T(8,128)(2,1)S(1)} %add_convert_fusion.5.mine_ref), channel_id=1, source_target_pairs={{0,4},{4,0},{8,12},{12,8},{1,5},{5,1},{9,13},{13,9},{2,6},{6,2},{1... | collective-permute-start | bytes 442376 | tf_op jit(solution)/shard_map/ppermute | solution.py:272
  (3 other events, 12.1 us)

commit v11 on v10

--- a/solution.py
+++ b/solution.py
@@ -343,26 +343,25 @@
 
 
 def reduce_runs(runs, got_last, keep, first):
-    n = len(runs)
-    sums = {}
-    held = [keep]
-    for i in reversed(range(0, n, 2)):
-        got = got_last
-        if i + 2 < n:
-            holds = [[first]] + [held] * (len(runs[i]) - 1)
-            got = [partner(after(x, *hold), "labels", 1) for x, hold in zip(runs[i + 1], holds)]
-        parts = [[part, got[h]] for h, part in enumerate(runs[i])]
+    def over_dp(parts, *hold):
+        parts = [list(part) for part in parts]
         for mask in masks(len(parts)):
             for h in range(0, len(parts), 2 * mask):
-                sent = after(add(*parts[h + mask]).astype(BF16), *held)
+                sent = after(add(*parts[h + mask]).astype(BF16), *hold)
                 parts[h].append(partner(sent, "dp", 2 * mask))
-        sums[i] = parts[0]
-        held = parts[0][-1:]
+        return parts[0]
+
+    n = len(runs)
+    sums = {n - 2: over_dp(list(zip(runs[n - 2], got_last)), keep)}
+    held = sums[n - 2][-1:]
+    for i in reversed(range(0, n - 2, 2)):
+        near = after(add(*over_dp([[x] for x in runs[i + 1]], *held)).astype(BF16), first)
+        sums[i] = over_dp([[x] for x in runs[i]], *held) + [partner(near, "labels", 1)]
     for mask in masks(n)[1:]:
         for i in range(0, n, 2 * mask):
             sent = after(add(*sums[i + mask]).astype(BF16), first)
             sums[i].append(partner(sent, "labels", mask))
-    return add(*sums[0]).astype(BF16)
+    return sums[0]
 
 
 def with_meta(feats, owner_rows, block_rows, positive_rows):
@@ -428,10 +427,11 @@
             backs[run] = works[-1]["back"]
         got_last = [partner(x, "labels", 1) for x in works[-1]["back"]]
         keep, first, share = sum_shares(*works[-1]["shares"], *got_last[1:])
-        grad_feats = reduce_runs(backs, got_last, keep, first)
+        terms = reduce_runs(backs, got_last, keep, first)
         works[0]["slots"][2] = after(works[0]["slots"][2], *got_last[1:])
         other = partner(grad_label_work(works, 2, 1, label_weight.shape), "dp", 1)
         grad_label = grad_label_work(works, 2, 0, label_weight.shape, other)
+        grad_feats = add(after(terms[0], grad_label), *terms[1:]).astype(BF16)
         grad_enc = join_halves(share, grad_label, grad_feats)
     else:
         shards = gather_near(gather_far(enc_weight))

time: 90 us -> 88.1 us (0.979)
  waiting for transfers between devices: 40.6 us -> 36.5 us
  starting transfers between devices: 22.6 us -> 25.3 us
    ppermute x24, waiting for transfers between devices: 40.6 us -> 36.5 us  [partner(): lax.ppermute(x, axis, [(i, i ^ mask) for i in range(lax.axis_size(axis))])]
    ppermute x24, starting transfers between devices: 22.6 us -> 25.3 us  [partner(): lax.ppermute(x, axis, [(i, i ^ mask) for i in range(lax.axis_size(axis))])]
  transfers between devices with their start and end apart: 24 -> 24, of which waited for: 11 -> 13; matrix products, arithmetic and copies ran while one was open for 1% -> 1% of each run, Pallas kernels for 19% -> 19%
where the time goes in v11:
time: 88.1 us; the launch traced here: 87.9 us
  waiting for transfers between devices  36.5 us (41%)
  starting transfers between devices  25.3 us (29%)
  Pallas kernels  21.9 us (25%)
  local copies, waits for them, and re-layouts  2.37 us (3%)
  other arithmetic  1.09 us (1%)
    ppermute x24, waiting for transfers between devices, partner(): lax.ppermute(x, axis, [(i, i ^ mask) for i in range(lax.axis_size(axis))])  36.5 us
    ppermute x24, starting transfers between devices, partner(): lax.ppermute(x, axis, [(i, i ^ mask) for i in range(lax.axis_size(axis))])  25.3 us
    pallas_call x10, Pallas kernels, call(): pl.pallas_call(kernel, in_specs=[space] * len(args), out_specs=jax.tree.m...  21.9 us
    unnamed x6, local copies, waits for them, and re-layouts  2.37 us
  transfers between devices with their start and end apart: 24, of which 13 were waited for; matrix products, arithmetic and copies ran while one was open for 1% of the time, Pallas kernels for 19%

profile of v11, /device:TPU:0, one launch (start us, length us, event | category | flops | bytes accessed | tf_op | source)
XLA Modules:
  0.0 87.9 jit_solution(2872934302431627563)
XLA Ops:
  1.1 2.6 %collective-permute-start.4 = (bf16[192,768]{1,0:T(8,128)(2,1)}, bf16[192,768]{1,0:T(8,128)(2,1)S(1)}, u32[]{:S(2)}, u32[]{:S(2)}) collective-permute-start(bf16[192,768]{1,0:T(8,128)(2,1)} %shard_ref.1), channel_id=1, source_target_pairs={{0,2},{1,3},{2,0},{3,1},{4,6},{5,7},{6,4},{7,5},{8,10},{9,11},{10,... | collective-permute-start | bytes 884744 | tf_op jit(solution)/shard_map/ppermute | solution.py:272
  3.7 1.6 %own_block.1.refs_0_ = bf16[136,768]{1,0:T(8,128)(2,1)} custom-call(bf16[128,768]{1,0:T(8,128)(2,1)} %feats_ref.1, s32[4,128]{1,0:T(4,128)} %bitcast.5, s32[4,128]{1,0:T(4,128)} %bitcast.6, s32[4,128]{1,0:T(4,128)} %bitcast.7), custom_call_target="tpu_custom_call" | custom-call | bytes 1048576 | tf_op jit(solution)/shard_map/own_block/pallas_call | solution.py:186
  5.4 3.1 %collective-permute-start.1 = (bf16[136,768]{1,0:T(8,128)(2,1)}, bf16[136,768]{1,0:T(8,128)(2,1)S(1)}, u32[]{:S(2)}, u32[]{:S(2)}) collective-permute-start(bf16[136,768]{1,0:T(8,128)(2,1)} %own_block.1.refs_0_), channel_id=1, source_target_pairs={{0,8},{4,12},{8,0},{12,4},{1,9},{5,13},{9,1},{13,5},{2,10},{6,14},... | collective-permute-start | bytes 626696 | tf_op jit(solution)/shard_map/ppermute | solution.py:272
  8.6 1.6 %collective-permute-start = (bf16[136,768]{1,0:T(8,128)(2,1)}, bf16[136,768]{1,0:T(8,128)(2,1)S(1)}, u32[]{:S(2)}, u32[]{:S(2)}) collective-permute-start(bf16[136,768]{1,0:T(8,128)(2,1)} %own_block.1.refs_0_), channel_id=1, source_target_pairs={{0,4},{4,0},{8,12},{12,8},{1,5},{5,1},{9,13},{13,9},{2,6},{6,2},{1... | collective-permute-start | bytes 626696 | tf_op jit(solution)/shard_map/ppermute | solution.py:272
  12.6 3.4 %collective-permute-done.2.refs_1_ = bf16[136,768]{1,0:T(8,128)(2,1)S(1)} collective-permute-done((bf16[136,768]{1,0:T(8,128)(2,1)}, bf16[136,768]{1,0:T(8,128)(2,1)S(1)}, u32[]{:S(2)}, u32[]{:S(2)}) %collective-permute-start.2) | collective-permute-done | bytes 208928 | tf_op jit(solution)/shard_map/ppermute | solution.py:272
  16.0 2.6 %collective-permute-done.1.refs_0_ = bf16[136,768]{1,0:T(8,128)(2,1)S(1)} collective-permute-done((bf16[136,768]{1,0:T(8,128)(2,1)}, bf16[136,768]{1,0:T(8,128)(2,1)S(1)}, u32[]{:S(2)}, u32[]{:S(2)}) %collective-permute-start.1) | collective-permute-done | bytes 208928 | tf_op jit(solution)/shard_map/ppermute | solution.py:272
  19.3 1.5 %collective-permute-start.7 = (bf16[136,768]{1,0:T(8,128)(2,1)S(1)}, bf16[136,768]{1,0:T(8,128)(2,1)S(1)}, u32[]{:S(2)}, u32[]{:S(2)}) collective-permute-start(bf16[136,768]{1,0:T(8,128)(2,1)S(1)} %collective-permute-done.1.refs_0_), channel_id=1, source_target_pairs={{0,2},{1,3},{2,0},{3,1},{4,6},{5,7},{6,4},{7,5},{8,10},{9,11},{10,... | collective-permute-start | bytes 626696 | tf_op jit(solution)/shard_map/ppermute | solution.py:272
  20.8 1.4 %collective-permute-start.9 = (bf16[136,768]{1,0:T(8,128)(2,1)S(1)}, bf16[136,768]{1,0:T(8,128)(2,1)S(1)}, u32[]{:S(2)}, u32[]{:S(2)}) collective-permute-start(bf16[136,768]{1,0:T(8,128)(2,1)S(1)} %collective-permute-done.1.refs_0_), channel_id=1, source_target_pairs={{0,4},{4,0},{8,12},{12,8},{1,5},{5,1},{9,13},{13,9},{2,6},{6,2},{1... | collective-permute-start | bytes 626696 | tf_op jit(solution)/shard_map/ppermute | solution.py:272
  22.3 3.9 %pair_work.4 = (bf16[128,768]{1,0:T(8,128)(2,1)S(1)}, bf16[128,768]{1,0:T(8,128)(2,1)S(1)}, f32[256,128]{1,0:T(8,128)S(1)}, s32[256,128]{1,0:T(8,128)S(1)}, bf16...) custom-call(bf16[136,768]{1,0:T(8,128)(2,1)S(1)} %copy-done.2, ...), custom_call_target="tpu_custom_call" | custom-call | flops 1811939328 | bytes 8388608 | tf_op jit(solution)/shard_map/pair_work/pallas_call | solution.py:186
  28.1 3.8 %pair_work.5 = (bf16[128,768]{1,0:T(8,128)(2,1)S(1)}, bf16[128,768]{1,0:T(8,128)(2,1)S(1)}, f32[256,128]{1,0:T(8,128)S(1)}, s32[256,128]{1,0:T(8,128)S(1)}, bf16...) custom-call(bf16[136,768]{1,0:T(8,128)(2,1)S(1)} %collective-permute-done.1.refs_0_, ...), custom_call_target="tpu_custom_call" | custom-call | flops 1811939328 | bytes 8388608 | tf_op jit(solution)/shard_map/pair_work/pallas_call | solution.py:186
  32.7 3.8 %pair_work.6 = (bf16[128,768]{1,0:T(8,128)(2,1)S(1)}, bf16[128,768]{1,0:T(8,128)(2,1)S(1)}, f32[256,128]{1,0:T(8,128)S(1)}, s32[256,128]{1,0:T(8,128)S(1)}, bf16...) custom-call(bf16[136,768]{1,0:T(8,128)(2,1)S(1)} %collective-permute-done.refs_0_, ...), custom_call_target="tpu_custom_call" | custom-call | flops 1811939328 | bytes 8388608 | tf_op jit(solution)/shard_map/pair_work/pallas_call | solution.py:186
  36.6 4.0 %pair_work.7 = (bf16[128,768]{1,0:T(8,128)(2,1)S(1)}, bf16[128,768]{1,0:T(8,128)(2,1)S(1)}, f32[256,128]{1,0:T(8,128)S(1)}, s32[256,128]{1,0:T(8,128)S(1)}, bf16...) custom-call(bf16[136,768]{1,0:T(8,128)(2,1)S(1)} %collective-permute-done.9.refs_0_, ...), custom_call_target="tpu_custom_call" | custom-call | flops 1811939328 | bytes 8388608 | tf_op jit(solution)/shard_map/pair_work/pallas_call | solution.py:186
  41.6 6.5 %collective-permute-done.11 = bf16[128,768]{1,0:T(8,128)(2,1)S(1)} collective-permute-done((bf16[128,768]{1,0:T(8,128)(2,1)S(1)}, bf16[128,768]{1,0:T(8,128)(2,1)S(1)}, u32[]{:S(2)}, u32[]{:S(2)}) %collective-permute-start.11) | collective-permute-done | bytes 196640 | tf_op jit(solution)/shard_map/ppermute | solution.py:272
  50.3 1.5 %collective-permute-start.20 = (bf16[128,768]{1,0:T(8,128)(2,1)S(1)}, bf16[128,768]{1,0:T(8,128)(2,1)S(1)}, u32[]{:S(2)}, u32[]{:S(2)}) collective-permute-start(bf16[128,768]{1,0:T(8,128)(2,1)S(1)} %get-tuple-element.94), channel_id=1, source_target_pairs={{0,4},{4,0},{8,12},{12,8},{1,5},{5,1},{9,13},{13,9},{2,6},{6,2},{1... | collective-permute-start | bytes 589832 | tf_op jit(solution)/shard_map/ppermute | solution.py:272
  51.8 7.1 %collective-permute-done.14.refs_0_ = bf16[192,768]{1,0:T(8,128)(2,1)S(1)} collective-permute-done((bf16[192,768]{1,0:T(8,128)(2,1)S(1)}, bf16[192,768]{1,0:T(8,128)(2,1)S(1)}, u32[]{:S(2)}, u32[]{:S(2)}) %collective-permute-start.14) | collective-permute-done | bytes 294944 | tf_op jit(solution)/shard_map/ppermute | solution.py:272
  60.0 1.5 %collective-permute-start.15 = (bf16[128,768]{1,0:T(8,128)(2,1)S(1)}, bf16[128,768]{1,0:T(8,128)(2,1)S(1)}, u32[]{:S(2)}, u32[]{:S(2)}) collective-permute-start(bf16[128,768]{1,0:T(8,128)(2,1)S(1)} %add_convert_fusion.4), channel_id=1, source_target_pairs={{0,2},{1,3},{2,0},{3,1},{4,6},{5,7},{6,4},{7,5},{8,10},{9,11},{10,... | collective-permute-start | bytes 589832 | tf_op jit(solution)/shard_map/ppermute | solution.py:272
  61.6 3.1 %collective-permute-done.18 = bf16[96,768]{1,0:T(8,128)(2,1)S(1)} collective-permute-done((bf16[96,768]{1,0:T(8,128)(2,1)S(1)}, bf16[96,768]{1,0:T(8,128)(2,1)S(1)}, u32[]{:S(2)}, u32[]{:S(2)}) %collective-permute-start.18) | collective-permute-done | bytes 147488 | tf_op jit(solution)/shard_map/ppermute | solution.py:272
  64.7 2.5 %collective-permute-start.22 = (bf16[96,768]{1,0:T(8,128)(2,1)S(1)}, bf16[96,768]{1,0:T(8,128)(2,1)S(1)}, u32[]{:S(2)}, u32[]{:S(2)}) collective-permute-start(bf16[96,768]{1,0:T(8,128)(2,1)S(1)} %add_convert_fusion.6), channel_id=1, source_target_pairs={{0,8},{4,12},{8,0},{12,4},{1,9},{5,13},{9,1},{13,5},{2,10},{6,14},... | collective-permute-start | bytes 442376 | tf_op jit(solution)/shard_map/ppermute | solution.py:272
  67.9 1.4 %collective-permute-start.16 = (bf16[128,768]{1,0:T(8,128)(2,1)S(1)}, bf16[128,768]{1,0:T(8,128)(2,1)S(1)}, u32[]{:S(2)}, u32[]{:S(2)}) collective-permute-start(bf16[128,768]{1,0:T(8,128)(2,1)S(1)} %get-tuple-element.87), channel_id=1, source_target_pairs={{0,2},{1,3},{2,0},{3,1},{4,6},{5,7},{6,4},{7,5},{8,10},{9,11},{10,... | collective-permute-start | bytes 589832 | tf_op jit(solution)/shard_map/ppermute | solution.py:272
  69.3 1.6 %collective-permute-start.21 = (bf16[128,768]{1,0:T(8,128)(2,1)S(1)}, bf16[128,768]{1,0:T(8,128)(2,1)S(1)}, u32[]{:S(2)}, u32[]{:S(2)}) collective-permute-start(bf16[128,768]{1,0:T(8,128)(2,1)S(1)} %add_convert_fusion.2), channel_id=1, source_target_pairs={{0,8},{4,12},{8,0},{12,4},{1,9},{5,13},{9,1},{13,5},{2,10},{6,14},... | collective-permute-start | bytes 589832 | tf_op jit(solution)/shard_map/ppermute | solution.py:272
  70.9 3.7 %collective-permute-done.17 = bf16[128,768]{1,0:T(8,128)(2,1)S(1)} collective-permute-done((bf16[128,768]{1,0:T(8,128)(2,1)S(1)}, bf16[128,768]{1,0:T(8,128)(2,1)S(1)}, u32[]{:S(2)}, u32[]{:S(2)}) %collective-permute-start.17) | collective-permute-done | bytes 196640 | tf_op jit(solution)/shard_map/ppermute | solution.py:272
  75.5 2.7 %collective-permute-done.22 = bf16[96,768]{1,0:T(8,128)(2,1)S(1)} collective-permute-done((bf16[96,768]{1,0:T(8,128)(2,1)S(1)}, bf16[96,768]{1,0:T(8,128)(2,1)S(1)}, u32[]{:S(2)}, u32[]{:S(2)}) %collective-permute-start.22) | collective-permute-done | bytes 147488 | tf_op jit(solution)/shard_map/ppermute | solution.py:272
  78.4 2.2 %grad_label_work.3 = bf16[1024,768]{1,0:T(8,128)(2,1)} custom-call(f32[256,128]{1,0:T(8,128)S(1)} %get-tuple-element.57.refs_0_, f32[256,128]{1,0:T(8,128)S(1)} %get-tuple-element.61.refs_1_, f32[256,128]{1,0:T(8,128)S(1)} %get-tuple-element.64.refs_2_, f32[256,128]{1,0:T(8,128)S(1)} %get-tuple-element.68.refs_3_, s32[256,128]{1,0:T(8,128)S(1)} %get-tuple-element.69.refs_4_, ...), custom_call_target="tpu_custom_call" | custom-call | flops 805306368 | bytes 4194304 | tf_op jit(solution)/shard_map/grad_label_work/pallas_call | solution.py:186
  81.9 3.6 %collective-permute-done.19 = bf16[128,768]{1,0:T(8,128)(2,1)S(1)} collective-permute-done((bf16[128,768]{1,0:T(8,128)(2,1)S(1)}, bf16[128,768]{1,0:T(8,128)(2,1)S(1)}, u32[]{:S(2)}, u32[]{:S(2)}) %collective-permute-start.19) | collective-permute-done | bytes 196640 | tf_op jit(solution)/shard_map/ppermute | solution.py:272
  (47 shorter events, 16.3 us)
Async XLA Ops:
  0.6 9.5 %collective-permute-start.3 = (bf16[1024,768]{1,0:T(8,128)(2,1)}, bf16[1024,768]{1,0:T(8,128)(2,1)S(1)}, u32[]{:S(2)}, u32[]{:S(2)}) collective-permute-start(bf16[1024,768]{1,0:T(8,128)(2,1)} %label_ref), channel_id=1, source_target_pairs={{0,1},{1,0},{2,3},{3,2},{4,5},{5,4},{6,7},{7,6},{8,9},{9,8},{10,11... | collective-permute-start | bytes 4718600 | tf_op jit(solution)/shard_map/ppermute | solution.py:272
  1.1 17.6 %collective-permute-start.4 = (bf16[192,768]{1,0:T(8,128)(2,1)}, bf16[192,768]{1,0:T(8,128)(2,1)S(1)}, u32[]{:S(2)}, u32[]{:S(2)}) collective-permute-start(bf16[192,768]{1,0:T(8,128)(2,1)} %shard_ref.1), channel_id=1, source_target_pairs={{0,2},{1,3},{2,0},{3,1},{4,6},{5,7},{6,4},{7,5},{8,10},{9,11},{10,... | collective-permute-start | bytes 884744 | tf_op jit(solution)/shard_map/ppermute | solution.py:272
  5.4 10.6 %collective-permute-start.2 = (bf16[136,768]{1,0:T(8,128)(2,1)}, bf16[136,768]{1,0:T(8,128)(2,1)S(1)}, u32[]{:S(2)}, u32[]{:S(2)}) collective-permute-start(bf16[136,768]{1,0:T(8,128)(2,1)} %own_block.1.refs_0_), channel_id=1, source_target_pairs={{0,2},{1,3},{2,0},{3,1},{4,6},{5,7},{6,4},{7,5},{8,10},{9,11},{10,... | collective-permute-start | bytes 626696 | tf_op jit(solution)/shard_map/ppermute | solution.py:272
  5.4 13.1 %collective-permute-start.1 = (bf16[136,768]{1,0:T(8,128)(2,1)}, bf16[136,768]{1,0:T(8,128)(2,1)S(1)}, u32[]{:S(2)}, u32[]{:S(2)}) collective-permute-start(bf16[136,768]{1,0:T(8,128)(2,1)} %own_block.1.refs_0_), channel_id=1, source_target_pairs={{0,8},{4,12},{8,0},{12,4},{1,9},{5,13},{9,1},{13,5},{2,10},{6,14},... | collective-permute-start | bytes 626696 | tf_op jit(solution)/shard_map/ppermute | solution.py:272
  8.6 10.2 %collective-permute-start = (bf16[136,768]{1,0:T(8,128)(2,1)}, bf16[136,768]{1,0:T(8,128)(2,1)S(1)}, u32[]{:S(2)}, u32[]{:S(2)}) collective-permute-start(bf16[136,768]{1,0:T(8,128)(2,1)} %own_block.1.refs_0_), channel_id=1, source_target_pairs={{0,4},{4,0},{8,12},{12,8},{1,5},{5,1},{9,13},{13,9},{2,6},{6,2},{1... | collective-permute-start | bytes 626696 | tf_op jit(solution)/shard_map/ppermute | solution.py:272
  18.8 3.5 %collective-permute-start.5 = (bf16[192,768]{1,0:T(8,128)(2,1)S(1)}, bf16[192,768]{1,0:T(8,128)(2,1)S(1)}, u32[]{:S(2)}, u32[]{:S(2)}) collective-permute-start(bf16[192,768]{1,0:T(8,128)(2,1)S(1)} %copy-done.1), channel_id=1, source_target_pairs={{0,1},{1,0},{2,3},{3,2},{4,5},{5,4},{6,7},{7,6},{8,9},{9,8},{10,11... | collective-permute-start | bytes 884744 | tf_op jit(solution)/shard_map/ppermute | solution.py:272
  18.8 3.5 %collective-permute-start.6 = (bf16[192,768]{1,0:T(8,128)(2,1)S(1)}, bf16[192,768]{1,0:T(8,128)(2,1)S(1)}, u32[]{:S(2)}, u32[]{:S(2)}) collective-permute-start(bf16[192,768]{1,0:T(8,128)(2,1)S(1)} %collective-permute-done.4.refs_6_), channel_id=1, source_target_pairs={{0,1},{1,0},{2,3},{3,2},{4,5},{5,4},{6,7},{7,6},{8,9},{9,8},{10,11... | collective-permute-start | bytes 884744 | tf_op jit(solution)/shard_map/ppermute | solution.py:272
  19.3 7.5 %collective-permute-start.7 = (bf16[136,768]{1,0:T(8,128)(2,1)S(1)}, bf16[136,768]{1,0:T(8,128)(2,1)S(1)}, u32[]{:S(2)}, u32[]{:S(2)}) collective-permute-start(bf16[136,768]{1,0:T(8,128)(2,1)S(1)} %collective-permute-done.1.refs_0_), channel_id=1, source_target_pairs={{0,2},{1,3},{2,0},{3,1},{4,6},{5,7},{6,4},{7,5},{8,10},{9,11},{10,... | collective-permute-start | bytes 626696 | tf_op jit(solution)/shard_map/ppermute | solution.py:272
  20.8 6.8 %collective-permute-start.9 = (bf16[136,768]{1,0:T(8,128)(2,1)S(1)}, bf16[136,768]{1,0:T(8,128)(2,1)S(1)}, u32[]{:S(2)}, u32[]{:S(2)}) collective-permute-start(bf16[136,768]{1,0:T(8,128)(2,1)S(1)} %collective-permute-done.1.refs_0_), channel_id=1, source_target_pairs={{0,4},{4,0},{8,12},{12,8},{1,5},{5,1},{9,13},{13,9},{2,6},{6,2},{1... | collective-permute-start | bytes 626696 | tf_op jit(solution)/shard_map/ppermute | solution.py:272
  26.1 6.6 %collective-permute-start.8 = (bf16[136,768]{1,0:T(8,128)(2,1)S(1)}, bf16[136,768]{1,0:T(8,128)(2,1)S(1)}, u32[]{:S(2)}, u32[]{:S(2)}) collective-permute-start(bf16[136,768]{1,0:T(8,128)(2,1)S(1)} %collective-permute-done.2.refs_1_), channel_id=1, source_target_pairs={{0,4},{4,0},{8,12},{12,8},{1,5},{5,1},{9,13},{13,9},{2,6},{6,2},{1... | collective-permute-start | bytes 626696 | tf_op jit(solution)/shard_map/ppermute | solution.py:272
  27.6 9.0 %collective-permute-start.10 = (bf16[136,768]{1,0:T(8,128)(2,1)S(1)}, bf16[136,768]{1,0:T(8,128)(2,1)S(1)}, u32[]{:S(2)}, u32[]{:S(2)}) collective-permute-start(bf16[136,768]{1,0:T(8,128)(2,1)S(1)} %collective-permute-done.9.refs_0_), channel_id=1, source_target_pairs={{0,2},{1,3},{2,0},{3,1},{4,6},{5,7},{6,4},{7,5},{8,10},{9,11},{10,... | collective-permute-start | bytes 626696 | tf_op jit(solution)/shard_map/ppermute | solution.py:272
  40.6 8.8 %collective-permute-start.13 = (bf16[2,192,768]{2,1,0:T(8,128)(2,1)S(1)}, bf16[2,192,768]{2,1,0:T(8,128)(2,1)S(1)}, u32[]{:S(2)}, u32[]{:S(2)}) collective-permute-start(bf16[2,192,768]{2,1,0:T(8,128)(2,1)S(1)} %get-tuple-element.83), channel_id=1, source_target_pairs={{0,1},{1,0},{2,3},{3,2},{4,5},{5,4},{6,7},{7,6},{8,9},{9,8},{10,11... | collective-permute-start | bytes 1769480 | tf_op jit(solution)/shard_map/ppermute | solution.py:272
  40.7 7.3 %collective-permute-start.11 = (bf16[128,768]{1,0:T(8,128)(2,1)S(1)}, bf16[128,768]{1,0:T(8,128)(2,1)S(1)}, u32[]{:S(2)}, u32[]{:S(2)}) collective-permute-start(bf16[128,768]{1,0:T(8,128)(2,1)S(1)} %get-tuple-element.74), channel_id=1, source_target_pairs={{0,4},{4,0},{8,12},{12,8},{1,5},{5,1},{9,13},{13,9},{2,6},{6,2},{1... | collective-permute-start | bytes 589832 | tf_op jit(solution)/shard_map/ppermute | solution.py:272
  49.3 29.1 %collective-permute-start.12 = (bf16[1024,768]{1,0:T(8,128)(2,1)S(1)}, bf16[1024,768]{1,0:T(8,128)(2,1)S(1)}, u32[]{:S(2)}, u32[]{:S(2)}) collective-permute-start(bf16[1024,768]{1,0:T(8,128)(2,1)S(1)} %grad_label_work.2), channel_id=1, source_target_pairs={{0,1},{1,0},{2,3},{3,2},{4,5},{5,4},{6,7},{7,6},{8,9},{9,8},{10,11... | collective-permute-start | bytes 4718600 | tf_op jit(solution)/shard_map/ppermute | solution.py:272
  49.5 9.5 %collective-permute-start.14 = (bf16[192,768]{1,0:T(8,128)(2,1)S(1)}, bf16[192,768]{1,0:T(8,128)(2,1)S(1)}, u32[]{:S(2)}, u32[]{:S(2)}) collective-permute-start(bf16[192,768]{1,0:T(8,128)(2,1)S(1)} %fusion), channel_id=1, source_target_pairs={{0,2},{1,3},{2,0},{3,1},{4,6},{5,7},{6,4},{7,5},{8,10},{9,11},{10,... | collective-permute-start | bytes 884744 | tf_op jit(solution)/shard_map/ppermute | solution.py:272
  50.3 17.5 %collective-permute-start.20 = (bf16[128,768]{1,0:T(8,128)(2,1)S(1)}, bf16[128,768]{1,0:T(8,128)(2,1)S(1)}, u32[]{:S(2)}, u32[]{:S(2)}) collective-permute-start(bf16[128,768]{1,0:T(8,128)(2,1)S(1)} %get-tuple-element.94), channel_id=1, source_target_pairs={{0,4},{4,0},{8,12},{12,8},{1,5},{5,1},{9,13},{13,9},{2,6},{6,2},{1... | collective-permute-start | bytes 589832 | tf_op jit(solution)/shard_map/ppermute | solution.py:272
  59.1 5.5 %collective-permute-start.18 = (bf16[96,768]{1,0:T(8,128)(2,1)S(1)}, bf16[96,768]{1,0:T(8,128)(2,1)S(1)}, u32[]{:S(2)}, u32[]{:S(2)}) collective-permute-start(bf16[96,768]{1,0:T(8,128)(2,1)S(1)} %get-tuple-element.91), channel_id=1, source_target_pairs={{0,4},{4,0},{8,12},{12,8},{1,5},{5,1},{9,13},{13,9},{2,6},{6,2},{1... | collective-permute-start | bytes 442376 | tf_op jit(solution)/shard_map/ppermute | solution.py:272
  60.0 7.1 %collective-permute-start.15 = (bf16[128,768]{1,0:T(8,128)(2,1)S(1)}, bf16[128,768]{1,0:T(8,128)(2,1)S(1)}, u32[]{:S(2)}, u32[]{:S(2)}) collective-permute-start(bf16[128,768]{1,0:T(8,128)(2,1)S(1)} %add_convert_fusion.4), channel_id=1, source_target_pairs={{0,2},{1,3},{2,0},{3,1},{4,6},{5,7},{6,4},{7,5},{8,10},{9,11},{10,... | collective-permute-start | bytes 589832 | tf_op jit(solution)/shard_map/ppermute | solution.py:272
  64.7 13.5 %collective-permute-start.22 = (bf16[96,768]{1,0:T(8,128)(2,1)S(1)}, bf16[96,768]{1,0:T(8,128)(2,1)S(1)}, u32[]{:S(2)}, u32[]{:S(2)}) collective-permute-start(bf16[96,768]{1,0:T(8,128)(2,1)S(1)} %add_convert_fusion.6), channel_id=1, source_target_pairs={{0,8},{4,12},{8,0},{12,4},{1,9},{5,13},{9,1},{13,5},{2,10},{6,14},... | collective-permute-start | bytes 442376 | tf_op jit(solution)/shard_map/ppermute | solution.py:272
  67.2 7.4 %collective-permute-start.17 = (bf16[128,768]{1,0:T(8,128)(2,1)S(1)}, bf16[128,768]{1,0:T(8,128)(2,1)S(1)}, u32[]{:S(2)}, u32[]{:S(2)}) collective-permute-start(bf16[128,768]{1,0:T(8,128)(2,1)S(1)} %get-tuple-element.90), channel_id=1, source_target_pairs={{0,2},{1,3},{2,0},{3,1},{4,6},{5,7},{6,4},{7,5},{8,10},{9,11},{10,... | collective-permute-start | bytes 589832 | tf_op jit(solution)/shard_map/ppermute | solution.py:272
  67.9 12.7 %collective-permute-start.16 = (bf16[128,768]{1,0:T(8,128)(2,1)S(1)}, bf16[128,768]{1,0:T(8,128)(2,1)S(1)}, u32[]{:S(2)}, u32[]{:S(2)}) collective-permute-start(bf16[128,768]{1,0:T(8,128)(2,1)S(1)} %get-tuple-element.87), channel_id=1, source_target_pairs={{0,2},{1,3},{2,0},{3,1},{4,6},{5,7},{6,4},{7,5},{8,10},{9,11},{10,... | collective-permute-start | bytes 589832 | tf_op jit(solution)/shard_map/ppermute | solution.py:272
  69.3 12.5 %collective-permute-start.21 = (bf16[128,768]{1,0:T(8,128)(2,1)S(1)}, bf16[128,768]{1,0:T(8,128)(2,1)S(1)}, u32[]{:S(2)}, u32[]{:S(2)}) collective-permute-start(bf16[128,768]{1,0:T(8,128)(2,1)S(1)} %add_convert_fusion.2), channel_id=1, source_target_pairs={{0,8},{4,12},{8,0},{12,4},{1,9},{5,13},{9,1},{13,5},{2,10},{6,14},... | collective-permute-start | bytes 589832 | tf_op jit(solution)/shard_map/ppermute | solution.py:272
  74.7 10.8 %collective-permute-start.19 = (bf16[128,768]{1,0:T(8,128)(2,1)S(1)}, bf16[128,768]{1,0:T(8,128)(2,1)S(1)}, u32[]{:S(2)}, u32[]{:S(2)}) collective-permute-start(bf16[128,768]{1,0:T(8,128)(2,1)S(1)} %add_convert_fusion.3), channel_id=1, source_target_pairs={{0,4},{4,0},{8,12},{12,8},{1,5},{5,1},{9,13},{13,9},{2,6},{6,2},{1... | collective-permute-start | bytes 589832 | tf_op jit(solution)/shard_map/ppermute | solution.py:272
  78.3 8.8 %collective-permute-start.23 = (bf16[96,768]{1,0:T(8,128)(2,1)S(1)}, bf16[96,768]{1,0:T(8,128)(2,1)S(1)}, u32[]{:S(2)}, u32[]{:S(2)}) collective-permute-start(bf16[96,768]{1,0:T(8,128)(2,1)S(1)} %add_convert_fusion.5.mine_ref), channel_id=1, source_target_pairs={{0,4},{4,0},{8,12},{12,8},{1,5},{5,1},{9,13},{13,9},{2,6},{6,2},{1... | collective-permute-start | bytes 442376 | tf_op jit(solution)/shard_map/ppermute | solution.py:272
  (3 other events, 12.1 us)

commit v12 on v11

--- a/solution.py
+++ b/solution.py
@@ -355,7 +355,7 @@
     sums = {n - 2: over_dp(list(zip(runs[n - 2], got_last)), keep)}
     held = sums[n - 2][-1:]
     for i in reversed(range(0, n - 2, 2)):
-        near = after(add(*over_dp([[x] for x in runs[i + 1]], *held)).astype(BF16), first)
+        near = after(add(*over_dp([[x] for x in runs[i + 1]], keep)).astype(BF16), first)
         sums[i] = over_dp([[x] for x in runs[i]], *held) + [partner(near, "labels", 1)]
     for mask in masks(n)[1:]:
         for i in range(0, n, 2 * mask):
@@ -431,7 +431,7 @@
         works[0]["slots"][2] = after(works[0]["slots"][2], *got_last[1:])
         other = partner(grad_label_work(works, 2, 1, label_weight.shape), "dp", 1)
         grad_label = grad_label_work(works, 2, 0, label_weight.shape, other)
-        grad_feats = add(after(terms[0], grad_label), *terms[1:]).astype(BF16)
+        grad_feats = add(*terms).astype(BF16)
         grad_enc = join_halves(share, grad_label, grad_feats)
     else:
         shards = gather_near(gather_far(enc_weight))

time: 88.1 us -> 82.3 us (0.934)
  waiting for transfers between devices: 36.5 us -> 31.9 us
  starting transfers between devices: 25.3 us -> 23.8 us
    ppermute x24, waiting for transfers between devices: 36.5 us -> 31.9 us  [partner(): lax.ppermute(x, axis, [(i, i ^ mask) for i in range(lax.axis_size(axis))])]
    ppermute x24, starting transfers between devices: 25.3 us -> 23.8 us  [partner(): lax.ppermute(x, axis, [(i, i ^ mask) for i in range(lax.axis_size(axis))])]
  transfers between devices with their start and end apart: 24 -> 24, of which waited for: 13 -> 11; matrix products, arithmetic and copies ran while one was open for 1% -> 1% of each run, Pallas kernels for 19% -> 21%
where the time goes in v12:
time: 82.3 us; the launch traced here: 82.1 us
  waiting for transfers between devices  31.9 us (39%)
  starting transfers between devices  23.8 us (29%)
  Pallas kernels  22.2 us (27%)
  local copies, waits for them, and re-layouts  2.37 us (3%)
  other arithmetic  1.12 us (1%)
    ppermute x24, waiting for transfers between devices, partner(): lax.ppermute(x, axis, [(i, i ^ mask) for i in range(lax.axis_size(axis))])  31.9 us
    ppermute x24, starting transfers between devices, partner(): lax.ppermute(x, axis, [(i, i ^ mask) for i in range(lax.axis_size(axis))])  23.8 us
    pallas_call x10, Pallas kernels, call(): pl.pallas_call(kernel, in_specs=[space] * len(args), out_specs=jax.tree.m...  22.2 us
    unnamed x6, local copies, waits for them, and re-layouts  2.37 us
  transfers between devices with their start and end apart: 24, of which 11 were waited for; matrix products, arithmetic and copies ran while one was open for 1% of the time, Pallas kernels for 21%

profile of v12, /device:TPU:0, one launch (start us, length us, event | category | flops | bytes accessed | tf_op | source)
XLA Modules:
  0.0 82.1 jit_solution(5808112442085882035)
XLA Ops:
  1.1 2.6 %collective-permute-start.4 = (bf16[192,768]{1,0:T(8,128)(2,1)}, bf16[192,768]{1,0:T(8,128)(2,1)S(1)}, u32[]{:S(2)}, u32[]{:S(2)}) collective-permute-start(bf16[192,768]{1,0:T(8,128)(2,1)} %shard_ref.1), channel_id=1, source_target_pairs={{0,2},{1,3},{2,0},{3,1},{4,6},{5,7},{6,4},{7,5},{8,10},{9,11},{10,... | collective-permute-start | bytes 884744 | tf_op jit(solution)/shard_map/ppermute | solution.py:272
  3.7 1.6 %own_block.1.refs_0_ = bf16[136,768]{1,0:T(8,128)(2,1)} custom-call(bf16[128,768]{1,0:T(8,128)(2,1)} %feats_ref.1, s32[4,128]{1,0:T(4,128)} %bitcast.5, s32[4,128]{1,0:T(4,128)} %bitcast.6, s32[4,128]{1,0:T(4,128)} %bitcast.7), custom_call_target="tpu_custom_call" | custom-call | bytes 1048576 | tf_op jit(solution)/shard_map/own_block/pallas_call | solution.py:186
  5.4 3.1 %collective-permute-start.1 = (bf16[136,768]{1,0:T(8,128)(2,1)}, bf16[136,768]{1,0:T(8,128)(2,1)S(1)}, u32[]{:S(2)}, u32[]{:S(2)}) collective-permute-start(bf16[136,768]{1,0:T(8,128)(2,1)} %own_block.1.refs_0_), channel_id=1, source_target_pairs={{0,8},{4,12},{8,0},{12,4},{1,9},{5,13},{9,1},{13,5},{2,10},{6,14},... | collective-permute-start | bytes 626696 | tf_op jit(solution)/shard_map/ppermute | solution.py:272
  8.6 1.6 %collective-permute-start = (bf16[136,768]{1,0:T(8,128)(2,1)}, bf16[136,768]{1,0:T(8,128)(2,1)S(1)}, u32[]{:S(2)}, u32[]{:S(2)}) collective-permute-start(bf16[136,768]{1,0:T(8,128)(2,1)} %own_block.1.refs_0_), channel_id=1, source_target_pairs={{0,4},{4,0},{8,12},{12,8},{1,5},{5,1},{9,13},{13,9},{2,6},{6,2},{1... | collective-permute-start | bytes 626696 | tf_op jit(solution)/shard_map/ppermute | solution.py:272
  10.1 1.4 %copy-done = bf16[1024,768]{1,0:T(8,128)(2,1)S(1)} copy-done((bf16[1024,768]{1,0:T(8,128)(2,1)S(1)}, bf16[1024,768]{1,0:T(8,128)(2,1)}, u32[]{:S(2)}) %copy-start) | copy-done | bytes 1572888
  12.6 3.4 %collective-permute-done.2.refs_1_ = bf16[136,768]{1,0:T(8,128)(2,1)S(1)} collective-permute-done((bf16[136,768]{1,0:T(8,128)(2,1)}, bf16[136,768]{1,0:T(8,128)(2,1)S(1)}, u32[]{:S(2)}, u32[]{:S(2)}) %collective-permute-start.2) | collective-permute-done | bytes 208928 | tf_op jit(solution)/shard_map/ppermute | solution.py:272
  16.0 2.6 %collective-permute-done.1.refs_0_ = bf16[136,768]{1,0:T(8,128)(2,1)S(1)} collective-permute-done((bf16[136,768]{1,0:T(8,128)(2,1)}, bf16[136,768]{1,0:T(8,128)(2,1)S(1)}, u32[]{:S(2)}, u32[]{:S(2)}) %collective-permute-start.1) | collective-permute-done | bytes 208928 | tf_op jit(solution)/shard_map/ppermute | solution.py:272
  19.3 1.5 %collective-permute-start.7 = (bf16[136,768]{1,0:T(8,128)(2,1)S(1)}, bf16[136,768]{1,0:T(8,128)(2,1)S(1)}, u32[]{:S(2)}, u32[]{:S(2)}) collective-permute-start(bf16[136,768]{1,0:T(8,128)(2,1)S(1)} %collective-permute-done.1.refs_0_), channel_id=1, source_target_pairs={{0,2},{1,3},{2,0},{3,1},{4,6},{5,7},{6,4},{7,5},{8,10},{9,11},{10,... | collective-permute-start | bytes 626696 | tf_op jit(solution)/shard_map/ppermute | solution.py:272
  20.8 1.4 %collective-permute-start.8 = (bf16[136,768]{1,0:T(8,128)(2,1)S(1)}, bf16[136,768]{1,0:T(8,128)(2,1)S(1)}, u32[]{:S(2)}, u32[]{:S(2)}) collective-permute-start(bf16[136,768]{1,0:T(8,128)(2,1)S(1)} %collective-permute-done.1.refs_0_), channel_id=1, source_target_pairs={{0,4},{4,0},{8,12},{12,8},{1,5},{5,1},{9,13},{13,9},{2,6},{6,2},{1... | collective-permute-start | bytes 626696 | tf_op jit(solution)/shard_map/ppermute | solution.py:272
  22.3 3.9 %pair_work.4 = (bf16[128,768]{1,0:T(8,128)(2,1)S(1)}, bf16[128,768]{1,0:T(8,128)(2,1)S(1)}, f32[256,128]{1,0:T(8,128)S(1)}, s32[256,128]{1,0:T(8,128)S(1)}, bf16...) custom-call(bf16[136,768]{1,0:T(8,128)(2,1)S(1)} %copy-done.2, ...), custom_call_target="tpu_custom_call" | custom-call | flops 1811939328 | bytes 8388608 | tf_op jit(solution)/shard_map/pair_work/pallas_call | solution.py:186
  28.1 3.9 %pair_work.5 = (bf16[128,768]{1,0:T(8,128)(2,1)S(1)}, bf16[128,768]{1,0:T(8,128)(2,1)S(1)}, f32[256,128]{1,0:T(8,128)S(1)}, s32[256,128]{1,0:T(8,128)S(1)}, bf16...) custom-call(bf16[136,768]{1,0:T(8,128)(2,1)S(1)} %collective-permute-done.1.refs_0_, ...), custom_call_target="tpu_custom_call" | custom-call | flops 1811939328 | bytes 8388608 | tf_op jit(solution)/shard_map/pair_work/pallas_call | solution.py:186
  32.8 3.9 %pair_work.6 = (bf16[128,768]{1,0:T(8,128)(2,1)S(1)}, bf16[128,768]{1,0:T(8,128)(2,1)S(1)}, f32[256,128]{1,0:T(8,128)S(1)}, s32[256,128]{1,0:T(8,128)S(1)}, bf16...) custom-call(bf16[136,768]{1,0:T(8,128)(2,1)S(1)} %collective-permute-done.refs_0_, ...), custom_call_target="tpu_custom_call" | custom-call | flops 1811939328 | bytes 8388608 | tf_op jit(solution)/shard_map/pair_work/pallas_call | solution.py:186
  36.7 4.1 %pair_work.7 = (bf16[128,768]{1,0:T(8,128)(2,1)S(1)}, bf16[128,768]{1,0:T(8,128)(2,1)S(1)}, f32[256,128]{1,0:T(8,128)S(1)}, s32[256,128]{1,0:T(8,128)S(1)}, bf16...) custom-call(bf16[136,768]{1,0:T(8,128)(2,1)S(1)} %collective-permute-done.8.refs_0_, ...), custom_call_target="tpu_custom_call" | custom-call | flops 1811939328 | bytes 8388608 | tf_op jit(solution)/shard_map/pair_work/pallas_call | solution.py:186
  41.7 1.2 %collective-permute-done.12.got_ref = bf16[2,192,768]{2,1,0:T(8,128)(2,1)S(1)} collective-permute-done((bf16[2,192,768]{2,1,0:T(8,128)(2,1)S(1)}, bf16[2,192,768]{2,1,0:T(8,128)(2,1)S(1)}, u32[]{:S(2)}, u32[]{:S(2)}) %collective-permute-start.12) | collective-permute-done | bytes 589856 | tf_op jit(solution)/shard_map/ppermute | solution.py:272
  43.8 4.4 %collective-permute-done.11 = bf16[128,768]{1,0:T(8,128)(2,1)S(1)} collective-permute-done((bf16[128,768]{1,0:T(8,128)(2,1)S(1)}, bf16[128,768]{1,0:T(8,128)(2,1)S(1)}, u32[]{:S(2)}, u32[]{:S(2)}) %collective-permute-start.11) | collective-permute-done | bytes 196640 | tf_op jit(solution)/shard_map/ppermute | solution.py:272
  48.2 1.2 %grad_label_work.2 = bf16[1024,768]{1,0:T(8,128)(2,1)S(1)} custom-call(f32[256,128]{1,0:T(8,128)S(1)} %get-tuple-element.63.refs_0_, f32[256,128]{1,0:T(8,128)S(1)} %get-tuple-element.82.refs_1_, f32[256,128]{1,0:T(8,128)S(1)} %get-tuple-element.83.refs_2_, f32[256,128]{1,0:T(8,128)S(1)} %get-tuple-element.84.refs_3_, ...), custom_call_target="tpu_custom_call" | custom-call | flops 805306368 | bytes 4194304 | tf_op jit(solution)/shard_map/grad_label_work/pallas_call | solution.py:186
  50.3 1.8 %collective-permute-done.13.refs_0_ = bf16[192,768]{1,0:T(8,128)(2,1)S(1)} collective-permute-done((bf16[192,768]{1,0:T(8,128)(2,1)S(1)}, bf16[192,768]{1,0:T(8,128)(2,1)S(1)}, u32[]{:S(2)}, u32[]{:S(2)}) %collective-permute-start.13) | collective-permute-done | bytes 294944 | tf_op jit(solution)/shard_map/ppermute | solution.py:272
  53.2 1.5 %collective-permute-start.14 = (bf16[128,768]{1,0:T(8,128)(2,1)S(1)}, bf16[128,768]{1,0:T(8,128)(2,1)S(1)}, u32[]{:S(2)}, u32[]{:S(2)}) collective-permute-start(bf16[128,768]{1,0:T(8,128)(2,1)S(1)} %add_convert_fusion.4), channel_id=1, source_target_pairs={{0,2},{1,3},{2,0},{3,1},{4,6},{5,7},{6,4},{7,5},{8,10},{9,11},{10,... | collective-permute-start | bytes 589832 | tf_op jit(solution)/shard_map/ppermute | solution.py:272
  55.3 4.7 %collective-permute-done.17 = bf16[96,768]{1,0:T(8,128)(2,1)S(1)} collective-permute-done((bf16[96,768]{1,0:T(8,128)(2,1)S(1)}, bf16[96,768]{1,0:T(8,128)(2,1)S(1)}, u32[]{:S(2)}, u32[]{:S(2)}) %collective-permute-start.17) | collective-permute-done | bytes 147488 | tf_op jit(solution)/shard_map/ppermute | solution.py:272
  60.0 2.4 %collective-permute-start.22 = (bf16[96,768]{1,0:T(8,128)(2,1)S(1)}, bf16[96,768]{1,0:T(8,128)(2,1)S(1)}, u32[]{:S(2)}, u32[]{:S(2)}) collective-permute-start(bf16[96,768]{1,0:T(8,128)(2,1)S(1)} %add_convert_fusion.6), channel_id=1, source_target_pairs={{0,8},{4,12},{8,0},{12,4},{1,9},{5,13},{9,1},{13,5},{2,10},{6,14},... | collective-permute-start | bytes 442376 | tf_op jit(solution)/shard_map/ppermute | solution.py:272
  63.2 2.0 %collective-permute-start.20 = (bf16[128,768]{1,0:T(8,128)(2,1)S(1)}, bf16[128,768]{1,0:T(8,128)(2,1)S(1)}, u32[]{:S(2)}, u32[]{:S(2)}) collective-permute-start(bf16[128,768]{1,0:T(8,128)(2,1)S(1)} %add_convert_fusion.2), channel_id=1, source_target_pairs={{0,8},{4,12},{8,0},{12,4},{1,9},{5,13},{9,1},{13,5},{2,10},{6,14},... | collective-permute-start | bytes 589832 | tf_op jit(solution)/shard_map/ppermute | solution.py:272
  65.6 8.5 %collective-permute-done.22 = bf16[96,768]{1,0:T(8,128)(2,1)S(1)} collective-permute-done((bf16[96,768]{1,0:T(8,128)(2,1)S(1)}, bf16[96,768]{1,0:T(8,128)(2,1)S(1)}, u32[]{:S(2)}, u32[]{:S(2)}) %collective-permute-start.22) | collective-permute-done | bytes 147488 | tf_op jit(solution)/shard_map/ppermute | solution.py:272
  74.5 3.6 %collective-permute-done.20 = bf16[128,768]{1,0:T(8,128)(2,1)S(1)} collective-permute-done((bf16[128,768]{1,0:T(8,128)(2,1)S(1)}, bf16[128,768]{1,0:T(8,128)(2,1)S(1)}, u32[]{:S(2)}, u32[]{:S(2)}) %collective-permute-start.20) | collective-permute-done | bytes 196640 | tf_op jit(solution)/shard_map/ppermute | solution.py:272
  78.9 2.4 %grad_label_work.3 = bf16[1024,768]{1,0:T(8,128)(2,1)} custom-call(f32[256,128]{1,0:T(8,128)S(1)} %get-tuple-element.63.refs_0_, f32[256,128]{1,0:T(8,128)S(1)} %get-tuple-element.82.refs_1_, f32[256,128]{1,0:T(8,128)S(1)} %get-tuple-element.83.refs_2_, f32[256,128]{1,0:T(8,128)S(1)} %get-tuple-element.84.refs_3_, s32[256,128]{1,0:T(8,128)S(1)} %get-tuple-element.85.refs_4_, ...), custom_call_target="tpu_custom_call" | custom-call | flops 805306368 | bytes 4194304 | tf_op jit(solution)/shard_map/grad_label_work/pallas_call | solution.py:186
  (47 shorter events, 12.5 us)
Async XLA Ops:
  0.6 9.5 %collective-permute-start.3 = (bf16[1024,768]{1,0:T(8,128)(2,1)}, bf16[1024,768]{1,0:T(8,128)(2,1)S(1)}, u32[]{:S(2)}, u32[]{:S(2)}) collective-permute-start(bf16[1024,768]{1,0:T(8,128)(2,1)} %label_ref), channel_id=1, source_target_pairs={{0,1},{1,0},{2,3},{3,2},{4,5},{5,4},{6,7},{7,6},{8,9},{9,8},{10,11... | collective-permute-start | bytes 4718600 | tf_op jit(solution)/shard_map/ppermute | solution.py:272
  1.1 17.6 %collective-permute-start.4 = (bf16[192,768]{1,0:T(8,128)(2,1)}, bf16[192,768]{1,0:T(8,128)(2,1)S(1)}, u32[]{:S(2)}, u32[]{:S(2)}) collective-permute-start(bf16[192,768]{1,0:T(8,128)(2,1)} %shard_ref.1), channel_id=1, source_target_pairs={{0,2},{1,3},{2,0},{3,1},{4,6},{5,7},{6,4},{7,5},{8,10},{9,11},{10,... | collective-permute-start | bytes 884744 | tf_op jit(solution)/shard_map/ppermute | solution.py:272
  5.4 10.6 %collective-permute-start.2 = (bf16[136,768]{1,0:T(8,128)(2,1)}, bf16[136,768]{1,0:T(8,128)(2,1)S(1)}, u32[]{:S(2)}, u32[]{:S(2)}) collective-permute-start(bf16[136,768]{1,0:T(8,128)(2,1)} %own_block.1.refs_0_), channel_id=1, source_target_pairs={{0,2},{1,3},{2,0},{3,1},{4,6},{5,7},{6,4},{7,5},{8,10},{9,11},{10,... | collective-permute-start | bytes 626696 | tf_op jit(solution)/shard_map/ppermute | solution.py:272
  5.4 13.1 %collective-permute-start.1 = (bf16[136,768]{1,0:T(8,128)(2,1)}, bf16[136,768]{1,0:T(8,128)(2,1)S(1)}, u32[]{:S(2)}, u32[]{:S(2)}) collective-permute-start(bf16[136,768]{1,0:T(8,128)(2,1)} %own_block.1.refs_0_), channel_id=1, source_target_pairs={{0,8},{4,12},{8,0},{12,4},{1,9},{5,13},{9,1},{13,5},{2,10},{6,14},... | collective-permute-start | bytes 626696 | tf_op jit(solution)/shard_map/ppermute | solution.py:272
  8.6 10.2 %collective-permute-start = (bf16[136,768]{1,0:T(8,128)(2,1)}, bf16[136,768]{1,0:T(8,128)(2,1)S(1)}, u32[]{:S(2)}, u32[]{:S(2)}) collective-permute-start(bf16[136,768]{1,0:T(8,128)(2,1)} %own_block.1.refs_0_), channel_id=1, source_target_pairs={{0,4},{4,0},{8,12},{12,8},{1,5},{5,1},{9,13},{13,9},{2,6},{6,2},{1... | collective-permute-start | bytes 626696 | tf_op jit(solution)/shard_map/ppermute | solution.py:272
  18.8 3.5 %collective-permute-start.5 = (bf16[192,768]{1,0:T(8,128)(2,1)S(1)}, bf16[192,768]{1,0:T(8,128)(2,1)S(1)}, u32[]{:S(2)}, u32[]{:S(2)}) collective-permute-start(bf16[192,768]{1,0:T(8,128)(2,1)S(1)} %copy-done.1), channel_id=1, source_target_pairs={{0,1},{1,0},{2,3},{3,2},{4,5},{5,4},{6,7},{7,6},{8,9},{9,8},{10,11... | collective-permute-start | bytes 884744 | tf_op jit(solution)/shard_map/ppermute | solution.py:272
  18.8 3.5 %collective-permute-start.6 = (bf16[192,768]{1,0:T(8,128)(2,1)S(1)}, bf16[192,768]{1,0:T(8,128)(2,1)S(1)}, u32[]{:S(2)}, u32[]{:S(2)}) collective-permute-start(bf16[192,768]{1,0:T(8,128)(2,1)S(1)} %collective-permute-done.4.refs_6_), channel_id=1, source_target_pairs={{0,1},{1,0},{2,3},{3,2},{4,5},{5,4},{6,7},{7,6},{8,9},{9,8},{10,11... | collective-permute-start | bytes 884744 | tf_op jit(solution)/shard_map/ppermute | solution.py:272
  19.3 7.6 %collective-permute-start.7 = (bf16[136,768]{1,0:T(8,128)(2,1)S(1)}, bf16[136,768]{1,0:T(8,128)(2,1)S(1)}, u32[]{:S(2)}, u32[]{:S(2)}) collective-permute-start(bf16[136,768]{1,0:T(8,128)(2,1)S(1)} %collective-permute-done.1.refs_0_), channel_id=1, source_target_pairs={{0,2},{1,3},{2,0},{3,1},{4,6},{5,7},{6,4},{7,5},{8,10},{9,11},{10,... | collective-permute-start | bytes 626696 | tf_op jit(solution)/shard_map/ppermute | solution.py:272
  20.8 6.8 %collective-permute-start.8 = (bf16[136,768]{1,0:T(8,128)(2,1)S(1)}, bf16[136,768]{1,0:T(8,128)(2,1)S(1)}, u32[]{:S(2)}, u32[]{:S(2)}) collective-permute-start(bf16[136,768]{1,0:T(8,128)(2,1)S(1)} %collective-permute-done.1.refs_0_), channel_id=1, source_target_pairs={{0,4},{4,0},{8,12},{12,8},{1,5},{5,1},{9,13},{13,9},{2,6},{6,2},{1... | collective-permute-start | bytes 626696 | tf_op jit(solution)/shard_map/ppermute | solution.py:272
  26.2 6.6 %collective-permute-start.10 = (bf16[136,768]{1,0:T(8,128)(2,1)S(1)}, bf16[136,768]{1,0:T(8,128)(2,1)S(1)}, u32[]{:S(2)}, u32[]{:S(2)}) collective-permute-start(bf16[136,768]{1,0:T(8,128)(2,1)S(1)} %collective-permute-done.2.refs_1_), channel_id=1, source_target_pairs={{0,4},{4,0},{8,12},{12,8},{1,5},{5,1},{9,13},{13,9},{2,6},{6,2},{1... | collective-permute-start | bytes 626696 | tf_op jit(solution)/shard_map/ppermute | solution.py:272
  27.6 9.1 %collective-permute-start.9 = (bf16[136,768]{1,0:T(8,128)(2,1)S(1)}, bf16[136,768]{1,0:T(8,128)(2,1)S(1)}, u32[]{:S(2)}, u32[]{:S(2)}) collective-permute-start(bf16[136,768]{1,0:T(8,128)(2,1)S(1)} %collective-permute-done.8.refs_0_), channel_id=1, source_target_pairs={{0,2},{1,3},{2,0},{3,1},{4,6},{5,7},{6,4},{7,5},{8,10},{9,11},{10,... | collective-permute-start | bytes 626696 | tf_op jit(solution)/shard_map/ppermute | solution.py:272
  40.8 2.1 %collective-permute-start.12 = (bf16[2,192,768]{2,1,0:T(8,128)(2,1)S(1)}, bf16[2,192,768]{2,1,0:T(8,128)(2,1)S(1)}, u32[]{:S(2)}, u32[]{:S(2)}) collective-permute-start(bf16[2,192,768]{2,1,0:T(8,128)(2,1)S(1)} %get-tuple-element.69), channel_id=1, source_target_pairs={{0,1},{1,0},{2,3},{3,2},{4,5},{5,4},{6,7},{7,6},{8,9},{9,8},{10,11... | collective-permute-start | bytes 1769480 | tf_op jit(solution)/shard_map/ppermute | solution.py:272
  40.9 7.3 %collective-permute-start.11 = (bf16[128,768]{1,0:T(8,128)(2,1)S(1)}, bf16[128,768]{1,0:T(8,128)(2,1)S(1)}, u32[]{:S(2)}, u32[]{:S(2)}) collective-permute-start(bf16[128,768]{1,0:T(8,128)(2,1)S(1)} %get-tuple-element.67), channel_id=1, source_target_pairs={{0,4},{4,0},{8,12},{12,8},{1,5},{5,1},{9,13},{13,9},{2,6},{6,2},{1... | collective-permute-start | bytes 589832 | tf_op jit(solution)/shard_map/ppermute | solution.py:272
  43.0 9.1 %collective-permute-start.13 = (bf16[192,768]{1,0:T(8,128)(2,1)S(1)}, bf16[192,768]{1,0:T(8,128)(2,1)S(1)}, u32[]{:S(2)}, u32[]{:S(2)}) collective-permute-start(bf16[192,768]{1,0:T(8,128)(2,1)S(1)} %fusion), channel_id=1, source_target_pairs={{0,2},{1,3},{2,0},{3,1},{4,6},{5,7},{6,4},{7,5},{8,10},{9,11},{10,... | collective-permute-start | bytes 884744 | tf_op jit(solution)/shard_map/ppermute | solution.py:272
  49.4 29.5 %collective-permute-start.21 = (bf16[1024,768]{1,0:T(8,128)(2,1)S(1)}, bf16[1024,768]{1,0:T(8,128)(2,1)S(1)}, u32[]{:S(2)}, u32[]{:S(2)}) collective-permute-start(bf16[1024,768]{1,0:T(8,128)(2,1)S(1)} %grad_label_work.2), channel_id=1, source_target_pairs={{0,1},{1,0},{2,3},{3,2},{4,5},{5,4},{6,7},{7,6},{8,9},{9,8},{10,11... | collective-permute-start | bytes 4718600 | tf_op jit(solution)/shard_map/ppermute | solution.py:272
  49.5 13.0 %collective-permute-start.19 = (bf16[128,768]{1,0:T(8,128)(2,1)S(1)}, bf16[128,768]{1,0:T(8,128)(2,1)S(1)}, u32[]{:S(2)}, u32[]{:S(2)}) collective-permute-start(bf16[128,768]{1,0:T(8,128)(2,1)S(1)} %get-tuple-element.80), channel_id=1, source_target_pairs={{0,4},{4,0},{8,12},{12,8},{1,5},{5,1},{9,13},{13,9},{2,6},{6,2},{1... | collective-permute-start | bytes 589832 | tf_op jit(solution)/shard_map/ppermute | solution.py:272
  52.3 7.7 %collective-permute-start.17 = (bf16[96,768]{1,0:T(8,128)(2,1)S(1)}, bf16[96,768]{1,0:T(8,128)(2,1)S(1)}, u32[]{:S(2)}, u32[]{:S(2)}) collective-permute-start(bf16[96,768]{1,0:T(8,128)(2,1)S(1)} %get-tuple-element.77), channel_id=1, source_target_pairs={{0,4},{4,0},{8,12},{12,8},{1,5},{5,1},{9,13},{13,9},{2,6},{6,2},{1... | collective-permute-start | bytes 442376 | tf_op jit(solution)/shard_map/ppermute | solution.py:272
  53.2 9.3 %collective-permute-start.14 = (bf16[128,768]{1,0:T(8,128)(2,1)S(1)}, bf16[128,768]{1,0:T(8,128)(2,1)S(1)}, u32[]{:S(2)}, u32[]{:S(2)}) collective-permute-start(bf16[128,768]{1,0:T(8,128)(2,1)S(1)} %add_convert_fusion.4), channel_id=1, source_target_pairs={{0,2},{1,3},{2,0},{3,1},{4,6},{5,7},{6,4},{7,5},{8,10},{9,11},{10,... | collective-permute-start | bytes 589832 | tf_op jit(solution)/shard_map/ppermute | solution.py:272
  54.7 10.5 %collective-permute-start.16 = (bf16[128,768]{1,0:T(8,128)(2,1)S(1)}, bf16[128,768]{1,0:T(8,128)(2,1)S(1)}, u32[]{:S(2)}, u32[]{:S(2)}) collective-permute-start(bf16[128,768]{1,0:T(8,128)(2,1)S(1)} %get-tuple-element.76), channel_id=1, source_target_pairs={{0,2},{1,3},{2,0},{3,1},{4,6},{5,7},{6,4},{7,5},{8,10},{9,11},{10,... | collective-permute-start | bytes 589832 | tf_op jit(solution)/shard_map/ppermute | solution.py:272
  60.0 14.0 %collective-permute-start.22 = (bf16[96,768]{1,0:T(8,128)(2,1)S(1)}, bf16[96,768]{1,0:T(8,128)(2,1)S(1)}, u32[]{:S(2)}, u32[]{:S(2)}) collective-permute-start(bf16[96,768]{1,0:T(8,128)(2,1)S(1)} %add_convert_fusion.6), channel_id=1, source_target_pairs={{0,8},{4,12},{8,0},{12,4},{1,9},{5,13},{9,1},{13,5},{2,10},{6,14},... | collective-permute-start | bytes 442376 | tf_op jit(solution)/shard_map/ppermute | solution.py:272
  62.6 11.9 %collective-permute-start.15 = (bf16[128,768]{1,0:T(8,128)(2,1)S(1)}, bf16[128,768]{1,0:T(8,128)(2,1)S(1)}, u32[]{:S(2)}, u32[]{:S(2)}) collective-permute-start(bf16[128,768]{1,0:T(8,128)(2,1)S(1)} %get-tuple-element.73), channel_id=1, source_target_pairs={{0,2},{1,3},{2,0},{3,1},{4,6},{5,7},{6,4},{7,5},{8,10},{9,11},{10,... | collective-permute-start | bytes 589832 | tf_op jit(solution)/shard_map/ppermute | solution.py:272
  63.2 14.9 %collective-permute-start.20 = (bf16[128,768]{1,0:T(8,128)(2,1)S(1)}, bf16[128,768]{1,0:T(8,128)(2,1)S(1)}, u32[]{:S(2)}, u32[]{:S(2)}) collective-permute-start(bf16[128,768]{1,0:T(8,128)(2,1)S(1)} %add_convert_fusion.2), channel_id=1, source_target_pairs={{0,8},{4,12},{8,0},{12,4},{1,9},{5,13},{9,1},{13,5},{2,10},{6,14},... | collective-permute-start | bytes 589832 | tf_op jit(solution)/shard_map/ppermute | solution.py:272
  65.2 12.9 %collective-permute-start.18 = (bf16[128,768]{1,0:T(8,128)(2,1)S(1)}, bf16[128,768]{1,0:T(8,128)(2,1)S(1)}, u32[]{:S(2)}, u32[]{:S(2)}) collective-permute-start(bf16[128,768]{1,0:T(8,128)(2,1)S(1)} %add_convert_fusion.3), channel_id=1, source_target_pairs={{0,4},{4,0},{8,12},{12,8},{1,5},{5,1},{9,13},{13,9},{2,6},{6,2},{1... | collective-permute-start | bytes 589832 | tf_op jit(solution)/shard_map/ppermute | solution.py:272
  74.1 7.2 %collective-permute-start.23 = (bf16[96,768]{1,0:T(8,128)(2,1)S(1)}, bf16[96,768]{1,0:T(8,128)(2,1)S(1)}, u32[]{:S(2)}, u32[]{:S(2)}) collective-permute-start(bf16[96,768]{1,0:T(8,128)(2,1)S(1)} %add_convert_fusion.5.mine_ref), channel_id=1, source_target_pairs={{0,4},{4,0},{8,12},{12,8},{1,5},{5,1},{9,13},{13,9},{2,6},{6,2},{1... | collective-permute-start | bytes 442376 | tf_op jit(solution)/shard_map/ppermute | solution.py:272
  (3 other events, 12.1 us)

commit v13 on v12

--- a/solution.py
+++ b/solution.py
@@ -122,19 +122,23 @@
 
 def grad_label_kernel(*refs, calls, n_sets, j):
     grad_scores, blocks, embeddings = refs[:calls], refs[calls : 2 * calls], refs[2 * calls : 3 * calls]
-    more, out_ref = refs[3 * calls : -1], refs[-1]
-    part = blocks[0].shape[0] // n_sets
-    at = slice(j * part, (j + 1) * part)
-    grad_scores_t = jnp.concatenate([r[at, :].T for r in grad_scores], axis=1)
-    block_t = jnp.concatenate([r[at, :].T for r in blocks], axis=1)
-    embedding = jnp.concatenate([r[at, :] for r in embeddings], axis=0)
+    *more, out_ref, result, sem = refs[3 * calls :]
+    rows_of = [slice(j * r.shape[0] // n_sets, (j + 1) * r.shape[0] // n_sets) for r in blocks]
+    grad_scores_t = jnp.concatenate([r[at, :].T for r, at in zip(grad_scores, rows_of)], axis=1)
+    block_t = jnp.concatenate([r[at, :].T for r, at in zip(blocks, rows_of)], axis=1)
+    embedding = jnp.concatenate([r[at, :] for r, at in zip(embeddings, rows_of)], axis=0)
+    copies = []
     for b in range(out_ref.shape[0] // BLK):
-        rows = slice(b * BLK, (b + 1) * BLK)
+        rows = pl.ds(b * BLK, BLK)
         spread_t = jnp.where(block_t == b, grad_scores_t, 0.0).astype(BF16)
         total = dot(spread_t, embedding)
         for ref in more:
             total = total + ref[rows, :].astype(F32)
-        out_ref[rows, :] = total.astype(BF16)
+        result[rows, :] = total.astype(BF16)
+        copies.append(pltpu.make_async_copy(result.at[rows], out_ref.at[rows], sem.at[b]))
+        copies[b].start()
+    for copy in copies:
+        copy.wait()
 
 
 def own_block_kernel(feats_ref, owners_ref, blocks_ref, positives_ref, out_ref, ints, sem):
@@ -182,11 +186,11 @@
     out_ref[half_at(False, half), :] = other_ref[...].astype(F32)
 
 
-def call(kernel, name, out_shape, scratch, flops, megabytes, *args, space=VMEM, limit=24):
+def call(kernel, name, out_shape, scratch, flops, megabytes, *args, space=VMEM, out_space=VMEM, limit=24):
     return pl.pallas_call(
         kernel,
         in_specs=[space] * len(args),
-        out_specs=jax.tree.map(lambda _: VMEM, out_shape),
+        out_specs=jax.tree.map(lambda _: out_space, out_shape),
         out_shape=out_shape,
         scratch_shapes=scratch,
         compiler_params=pltpu.CompilerParams(vmem_limit_bytes=limit << 20),
@@ -253,13 +257,14 @@
         functools.partial(grad_label_kernel, calls=len(works), n_sets=n_sets, j=j),
         "grad_label_work",
         shaped(labels_shape),
-        [],
+        [pltpu.VMEM(labels_shape, BF16), pltpu.SemaphoreType.DMA((labels_shape[0] // BLK,))],
         2 * sum(x.shape[0] for x in slots[0]) // n_sets * labels_shape[0] * labels_shape[1],
         4,
         *slots[0],
         *slots[1],
         *slots[2],
         *more,
+        out_space=pl.BlockSpec(memory_space=pl.ANY),
     )
 
 
@@ -409,24 +414,31 @@
         )
         near = gather_labels(own, labels[0])
         far = {0: gather_far(near[0])}
-        shards = gather_near(gather_far(enc_weight), *far[0][1:], *near[1:3], labels[0])
+        shards = gather_near(
+            gather_far(enc_weight), *far[0][1:], *near[1:3], labels[0]
+        )
         shards[0] = own_shard
         works, backs = [], {}
-        for run in [*range(0, n_labels, 2), *range(1, n_labels, 2)]:
-            last = run == n_labels - 1
-            if last:
-                far[run] = gather_far(after(near[run], *far[run - 1][1:]))
-            elif run % 2:
-                sent = [after(x, works[0]["slots"][0]) for x in far[run - 1][1:]]
-                far[run] = near[run : run + 1] + [partner(x, "labels", 1) for x in sent]
-            elif run:
-                far[run] = gather_far(after(near[run], *far[0][1:]))
-            sources = [after(near[run], *([] if run else near[1:3]))] + far[run][1:]
-            before = works[-1] if works else None
+        last_call = list(range(1, n_labels, 2))
+        for call_runs in [[run] for run in range(0, n_labels, 2)] + [last_call]:
+            sources = []
+            for run in call_runs:
+                if run == n_labels - 1:
+                    held = far[run - 1][1:] + works[0]["slots"][:1]
+                    far[run] = gather_far(after(near[run], *held))
+                elif run % 2:
+                    sent = [after(x, *shards[1:]) for x in far[run - 1][1:]]
+                    far[run] = near[run : run + 1] + [partner(x, "labels", 1) for x in sent]
+                elif run:
+                    far[run] = gather_far(after(near[run], *far[0][1:]))
+                sources += [after(near[run], *([] if run else near[1:3]))] + far[run][1:]
+            before, last = works[-1] if works else None, call_runs is last_call
             works.append(pair_work(sources, labels, shards, cap, pick_count, before, last))
-            backs[run] = works[-1]["back"]
-        got_last = [partner(x, "labels", 1) for x in works[-1]["back"]]
-        keep, first, share = sum_shares(*works[-1]["shares"], *got_last[1:])
+            parts = len(sources) // len(call_runs)
+            for i, run in enumerate(call_runs):
+                backs[run] = works[-1]["back"][i * parts : (i + 1) * parts]
+        got_last = [partner(x, "labels", 1) for x in backs[n_labels - 1]]
+        keep, first, share = sum_shares(*works[-1]["shares"], *got_last)
         terms = reduce_runs(backs, got_last, keep, first)
         works[0]["slots"][2] = after(works[0]["slots"][2], *got_last[1:])
         other = partner(grad_label_work(works, 2, 1, label_weight.shape), "dp", 1)

time: 82.3 us -> 83.6 us (1.016)
  starting transfers between devices: 23.8 us -> 25.4 us
  waiting for transfers between devices: 31.9 us -> 30.9 us
    ppermute x24, starting transfers between devices: 23.8 us -> 25.4 us  [partner(): lax.ppermute(x, axis, [(i, i ^ mask) for i in range(lax.axis_size(axis))])]
    ppermute x24, waiting for transfers between devices: 31.9 us -> 30.9 us  [partner(): lax.ppermute(x, axis, [(i, i ^ mask) for i in range(lax.axis_size(axis))])]
    pallas_call x10 -> x9, Pallas kernels: 22.2 us -> 22.8 us  [call(): pl.pallas_call(kernel, in_specs=[space] * len(args), out_specs=jax.tree.m...]
  transfers between devices with their start and end apart: 24 -> 24, of which waited for: 11 -> 13; matrix products, arithmetic and copies ran while one was open for 1% -> 1% of each run, Pallas kernels for 21% -> 20%
where the time goes in v13:
time: 83.6 us; the launch traced here: 83.4 us
  waiting for transfers between devices  30.9 us (37%)
  starting transfers between devices  25.4 us (30%)
  Pallas kernels  22.8 us (27%)
  local copies, waits for them, and re-layouts  2.37 us (3%)
  other arithmetic  1.09 us (1%)
    ppermute x24, waiting for transfers between devices, partner(): lax.ppermute(x, axis, [(i, i ^ mask) for i in range(lax.axis_size(axis))])  30.9 us
    ppermute x24, starting transfers between devices, partner(): lax.ppermute(x, axis, [(i, i ^ mask) for i in range(lax.axis_size(axis))])  25.4 us
    pallas_call x9, Pallas kernels, call(): pl.pallas_call(kernel, in_specs=[space] * len(args), out_specs=jax.tree.m...  22.8 us
    unnamed x6, local copies, waits for them, and re-layouts  2.37 us
  transfers between devices with their start and end apart: 24, of which 13 were waited for; matrix products, arithmetic and copies ran while one was open for 1% of the time, Pallas kernels for 20%

profile of v13, /device:TPU:0, one launch (start us, length us, event | category | flops | bytes accessed | tf_op | source)
XLA Modules:
  0.0 83.4 jit_solution(7027740240634338411)
XLA Ops:
  1.1 2.6 %collective-permute-start.4 = (bf16[192,768]{1,0:T(8,128)(2,1)}, bf16[192,768]{1,0:T(8,128)(2,1)S(1)}, u32[]{:S(2)}, u32[]{:S(2)}) collective-permute-start(bf16[192,768]{1,0:T(8,128)(2,1)} %shard_ref.1), channel_id=1, source_target_pairs={{0,2},{1,3},{2,0},{3,1},{4,6},{5,7},{6,4},{7,5},{8,10},{9,11},{10,... | collective-permute-start | bytes 884744 | tf_op jit(solution)/shard_map/ppermute | solution.py:277
  3.7 1.6 %own_block.1.refs_0_ = bf16[136,768]{1,0:T(8,128)(2,1)} custom-call(bf16[128,768]{1,0:T(8,128)(2,1)} %feats_ref.1, s32[4,128]{1,0:T(4,128)} %bitcast.5, s32[4,128]{1,0:T(4,128)} %bitcast.6, s32[4,128]{1,0:T(4,128)} %bitcast.7), custom_call_target="tpu_custom_call" | custom-call | bytes 1048576 | tf_op jit(solution)/shard_map/own_block/pallas_call | solution.py:190
  5.4 3.1 %collective-permute-start.1 = (bf16[136,768]{1,0:T(8,128)(2,1)}, bf16[136,768]{1,0:T(8,128)(2,1)S(1)}, u32[]{:S(2)}, u32[]{:S(2)}) collective-permute-start(bf16[136,768]{1,0:T(8,128)(2,1)} %own_block.1.refs_0_), channel_id=1, source_target_pairs={{0,8},{4,12},{8,0},{12,4},{1,9},{5,13},{9,1},{13,5},{2,10},{6,14},... | collective-permute-start | bytes 626696 | tf_op jit(solution)/shard_map/ppermute | solution.py:277
  8.6 1.6 %collective-permute-start = (bf16[136,768]{1,0:T(8,128)(2,1)}, bf16[136,768]{1,0:T(8,128)(2,1)S(1)}, u32[]{:S(2)}, u32[]{:S(2)}) collective-permute-start(bf16[136,768]{1,0:T(8,128)(2,1)} %own_block.1.refs_0_), channel_id=1, source_target_pairs={{0,4},{4,0},{8,12},{12,8},{1,5},{5,1},{9,13},{13,9},{2,6},{6,2},{1... | collective-permute-start | bytes 626696 | tf_op jit(solution)/shard_map/ppermute | solution.py:277
  12.6 3.4 %collective-permute-done.2.refs_1_ = bf16[136,768]{1,0:T(8,128)(2,1)S(1)} collective-permute-done((bf16[136,768]{1,0:T(8,128)(2,1)}, bf16[136,768]{1,0:T(8,128)(2,1)S(1)}, u32[]{:S(2)}, u32[]{:S(2)}) %collective-permute-start.2) | collective-permute-done | bytes 208928 | tf_op jit(solution)/shard_map/ppermute | solution.py:277
  16.0 2.6 %collective-permute-done.1.refs_0_ = bf16[136,768]{1,0:T(8,128)(2,1)S(1)} collective-permute-done((bf16[136,768]{1,0:T(8,128)(2,1)}, bf16[136,768]{1,0:T(8,128)(2,1)S(1)}, u32[]{:S(2)}, u32[]{:S(2)}) %collective-permute-start.1) | collective-permute-done | bytes 208928 | tf_op jit(solution)/shard_map/ppermute | solution.py:277
  19.3 1.5 %collective-permute-start.7 = (bf16[136,768]{1,0:T(8,128)(2,1)S(1)}, bf16[136,768]{1,0:T(8,128)(2,1)S(1)}, u32[]{:S(2)}, u32[]{:S(2)}) collective-permute-start(bf16[136,768]{1,0:T(8,128)(2,1)S(1)} %collective-permute-done.1.refs_0_), channel_id=1, source_target_pairs={{0,2},{1,3},{2,0},{3,1},{4,6},{5,7},{6,4},{7,5},{8,10},{9,11},{10,... | collective-permute-start | bytes 626696 | tf_op jit(solution)/shard_map/ppermute | solution.py:277
  22.8 3.9 %pair_work.3 = (bf16[128,768]{1,0:T(8,128)(2,1)S(1)}, bf16[128,768]{1,0:T(8,128)(2,1)S(1)}, f32[256,128]{1,0:T(8,128)S(1)}, s32[256,128]{1,0:T(8,128)S(1)}, bf16...) custom-call(bf16[136,768]{1,0:T(8,128)(2,1)S(1)} %copy-done.2, ...), custom_call_target="tpu_custom_call" | custom-call | flops 1811939328 | bytes 8388608 | tf_op jit(solution)/shard_map/pair_work/pallas_call | solution.py:190
  26.8 2.1 %collective-permute-done.9.refs_2_ = bf16[136,768]{1,0:T(8,128)(2,1)S(1)} collective-permute-done((bf16[136,768]{1,0:T(8,128)(2,1)S(1)}, bf16[136,768]{1,0:T(8,128)(2,1)S(1)}, u32[]{:S(2)}, u32[]{:S(2)}) %collective-permute-start.9) | collective-permute-done | bytes 208928 | tf_op jit(solution)/shard_map/ppermute | solution.py:277
  29.4 3.8 %pair_work.4 = (bf16[128,768]{1,0:T(8,128)(2,1)S(1)}, bf16[128,768]{1,0:T(8,128)(2,1)S(1)}, f32[256,128]{1,0:T(8,128)S(1)}, s32[256,128]{1,0:T(8,128)S(1)}, bf16...) custom-call(bf16[136,768]{1,0:T(8,128)(2,1)S(1)} %collective-permute-done.1.refs_0_, ...), custom_call_target="tpu_custom_call" | custom-call | flops 1811939328 | bytes 8388608 | tf_op jit(solution)/shard_map/pair_work/pallas_call | solution.py:190
  34.7 5.6 %pair_work.5 = (bf16[128,768]{1,0:T(8,128)(2,1)S(1)}, bf16[128,768]{1,0:T(8,128)(2,1)S(1)}, bf16[128,768]{1,0:T(8,128)(2,1)S(1)}, bf16[128,768]{1,0:T(8,128)(2,1...) custom-call(bf16[136,768]{1,0:T(8,128)(2,1)S(1)} %collective-permute, ...), custom_call_target="tpu_custom_call" | custom-call | flops 3623878656 | bytes 8388608 | tf_op jit(solution)/shard_map/pair_work/pallas_call | solution.py:190
  40.4 1.5 %collective-permute-start.11 = (bf16[128,768]{1,0:T(8,128)(2,1)S(1)}, bf16[128,768]{1,0:T(8,128)(2,1)S(1)}, u32[]{:S(2)}, u32[]{:S(2)}) collective-permute-start(bf16[128,768]{1,0:T(8,128)(2,1)S(1)} %get-tuple-element.62), channel_id=1, source_target_pairs={{0,4},{4,0},{8,12},{12,8},{1,5},{5,1},{9,13},{13,9},{2,6},{6,2},{1... | collective-permute-start | bytes 589832 | tf_op jit(solution)/shard_map/ppermute | solution.py:277
  43.0 1.5 %collective-permute-start.13 = (bf16[128,768]{1,0:T(8,128)(2,1)S(1)}, bf16[128,768]{1,0:T(8,128)(2,1)S(1)}, u32[]{:S(2)}, u32[]{:S(2)}) collective-permute-start(bf16[128,768]{1,0:T(8,128)(2,1)S(1)} %get-tuple-element.65), channel_id=1, source_target_pairs={{0,4},{4,0},{8,12},{12,8},{1,5},{5,1},{9,13},{13,9},{2,6},{6,2},{1... | collective-permute-start | bytes 589832 | tf_op jit(solution)/shard_map/ppermute | solution.py:277
  44.5 3.7 %collective-permute-done.11 = bf16[128,768]{1,0:T(8,128)(2,1)S(1)} collective-permute-done((bf16[128,768]{1,0:T(8,128)(2,1)S(1)}, bf16[128,768]{1,0:T(8,128)(2,1)S(1)}, u32[]{:S(2)}, u32[]{:S(2)}) %collective-permute-start.11) | collective-permute-done | bytes 196640 | tf_op jit(solution)/shard_map/ppermute | solution.py:277
  48.2 4.8 %grad_label_work.2 = bf16[1024,768]{1,0:T(8,128)(2,1)S(1)} custom-call(f32[256,128]{1,0:T(8,128)S(1)} %get-tuple-element.59.refs_0_, f32[256,128]{1,0:T(8,128)S(1)} %get-tuple-element.77.refs_1_, f32[512,128]{1,0:T(8,128)S(1)} %get-tuple-element.78.refs_2_, s32[256,128]{1,0:T(8,128)S(1)} %get-tuple-element.79.refs_3_, ...), custom_call_target="tpu_custom_call" | custom-call | flops 805306368 | bytes 4194304 | tf_op jit(solution)/shard_map/grad_label_work/pallas_call | solution.py:190
  53.2 1.5 %collective-permute-start.18 = (bf16[96,768]{1,0:T(8,128)(2,1)S(1)}, bf16[96,768]{1,0:T(8,128)(2,1)S(1)}, u32[]{:S(2)}, u32[]{:S(2)}) collective-permute-start(bf16[96,768]{1,0:T(8,128)(2,1)S(1)} %get-tuple-element.73), channel_id=1, source_target_pairs={{0,4},{4,0},{8,12},{12,8},{1,5},{5,1},{9,13},{13,9},{2,6},{6,2},{1... | collective-permute-start | bytes 442376 | tf_op jit(solution)/shard_map/ppermute | solution.py:277
  55.4 1.5 %collective-permute-start.17 = (bf16[128,768]{1,0:T(8,128)(2,1)S(1)}, bf16[128,768]{1,0:T(8,128)(2,1)S(1)}, u32[]{:S(2)}, u32[]{:S(2)}) collective-permute-start(bf16[128,768]{1,0:T(8,128)(2,1)S(1)} %get-tuple-element.72), channel_id=1, source_target_pairs={{0,2},{1,3},{2,0},{3,1},{4,6},{5,7},{6,4},{7,5},{8,10},{9,11},{10,... | collective-permute-start | bytes 589832 | tf_op jit(solution)/shard_map/ppermute | solution.py:277
  56.9 2.7 %collective-permute-done.18 = bf16[96,768]{1,0:T(8,128)(2,1)S(1)} collective-permute-done((bf16[96,768]{1,0:T(8,128)(2,1)S(1)}, bf16[96,768]{1,0:T(8,128)(2,1)S(1)}, u32[]{:S(2)}, u32[]{:S(2)}) %collective-permute-start.18) | collective-permute-done | bytes 147488 | tf_op jit(solution)/shard_map/ppermute | solution.py:277
  59.6 2.1 %collective-permute-start.22 = (bf16[96,768]{1,0:T(8,128)(2,1)S(1)}, bf16[96,768]{1,0:T(8,128)(2,1)S(1)}, u32[]{:S(2)}, u32[]{:S(2)}) collective-permute-start(bf16[96,768]{1,0:T(8,128)(2,1)S(1)} %add_convert_fusion.6), channel_id=1, source_target_pairs={{0,8},{4,12},{8,0},{12,4},{1,9},{5,13},{9,1},{13,5},{2,10},{6,14},... | collective-permute-start | bytes 442376 | tf_op jit(solution)/shard_map/ppermute | solution.py:277
  63.3 2.3 %collective-permute-start.20 = (bf16[128,768]{1,0:T(8,128)(2,1)S(1)}, bf16[128,768]{1,0:T(8,128)(2,1)S(1)}, u32[]{:S(2)}, u32[]{:S(2)}) collective-permute-start(bf16[128,768]{1,0:T(8,128)(2,1)S(1)} %add_convert_fusion.2), channel_id=1, source_target_pairs={{0,8},{4,12},{8,0},{12,4},{1,9},{5,13},{9,1},{13,5},{2,10},{6,14},... | collective-permute-start | bytes 589832 | tf_op jit(solution)/shard_map/ppermute | solution.py:277
  67.5 6.9 %collective-permute-done.22 = bf16[96,768]{1,0:T(8,128)(2,1)S(1)} collective-permute-done((bf16[96,768]{1,0:T(8,128)(2,1)S(1)}, bf16[96,768]{1,0:T(8,128)(2,1)S(1)}, u32[]{:S(2)}, u32[]{:S(2)}) %collective-permute-start.22) | collective-permute-done | bytes 147488 | tf_op jit(solution)/shard_map/ppermute | solution.py:277
  74.6 3.1 %collective-permute-done.20 = bf16[128,768]{1,0:T(8,128)(2,1)S(1)} collective-permute-done((bf16[128,768]{1,0:T(8,128)(2,1)S(1)}, bf16[128,768]{1,0:T(8,128)(2,1)S(1)}, u32[]{:S(2)}, u32[]{:S(2)}) %collective-permute-start.20) | collective-permute-done | bytes 196640 | tf_op jit(solution)/shard_map/ppermute | solution.py:277
  77.7 2.2 %collective-permute-done.19 = bf16[128,768]{1,0:T(8,128)(2,1)S(1)} collective-permute-done((bf16[128,768]{1,0:T(8,128)(2,1)S(1)}, bf16[128,768]{1,0:T(8,128)(2,1)S(1)}, u32[]{:S(2)}, u32[]{:S(2)}) %collective-permute-start.19) | collective-permute-done | bytes 196640 | tf_op jit(solution)/shard_map/ppermute | solution.py:277
  80.7 1.8 %grad_label_work.3 = bf16[1024,768]{1,0:T(8,128)(2,1)} custom-call(f32[256,128]{1,0:T(8,128)S(1)} %get-tuple-element.59.refs_0_, f32[256,128]{1,0:T(8,128)S(1)} %get-tuple-element.77.refs_1_, f32[512,128]{1,0:T(8,128)S(1)} %get-tuple-element.78.refs_2_, s32[256,128]{1,0:T(8,128)S(1)} %get-tuple-element.79.refs_3_, s32[256,128]{1,0:T(8,128)S(1)} %get-tuple-element.80.refs_4_, ...), custom_call_target="tpu_custom_call" | custom-call | flops 805306368 | bytes 4194304 | tf_op jit(solution)/shard_map/grad_label_work/pallas_call | solution.py:190
  (46 shorter events, 15.2 us)
Async XLA Ops:
  0.6 9.5 %collective-permute-start.3 = (bf16[1024,768]{1,0:T(8,128)(2,1)}, bf16[1024,768]{1,0:T(8,128)(2,1)S(1)}, u32[]{:S(2)}, u32[]{:S(2)}) collective-permute-start(bf16[1024,768]{1,0:T(8,128)(2,1)} %label_ref), channel_id=1, source_target_pairs={{0,1},{1,0},{2,3},{3,2},{4,5},{5,4},{6,7},{7,6},{8,9},{9,8},{10,11... | collective-permute-start | bytes 4718600 | tf_op jit(solution)/shard_map/ppermute | solution.py:277
  1.1 17.6 %collective-permute-start.4 = (bf16[192,768]{1,0:T(8,128)(2,1)}, bf16[192,768]{1,0:T(8,128)(2,1)S(1)}, u32[]{:S(2)}, u32[]{:S(2)}) collective-permute-start(bf16[192,768]{1,0:T(8,128)(2,1)} %shard_ref.1), channel_id=1, source_target_pairs={{0,2},{1,3},{2,0},{3,1},{4,6},{5,7},{6,4},{7,5},{8,10},{9,11},{10,... | collective-permute-start | bytes 884744 | tf_op jit(solution)/shard_map/ppermute | solution.py:277
  5.4 10.6 %collective-permute-start.2 = (bf16[136,768]{1,0:T(8,128)(2,1)}, bf16[136,768]{1,0:T(8,128)(2,1)S(1)}, u32[]{:S(2)}, u32[]{:S(2)}) collective-permute-start(bf16[136,768]{1,0:T(8,128)(2,1)} %own_block.1.refs_0_), channel_id=1, source_target_pairs={{0,2},{1,3},{2,0},{3,1},{4,6},{5,7},{6,4},{7,5},{8,10},{9,11},{10,... | collective-permute-start | bytes 626696 | tf_op jit(solution)/shard_map/ppermute | solution.py:277
  5.4 13.1 %collective-permute-start.1 = (bf16[136,768]{1,0:T(8,128)(2,1)}, bf16[136,768]{1,0:T(8,128)(2,1)S(1)}, u32[]{:S(2)}, u32[]{:S(2)}) collective-permute-start(bf16[136,768]{1,0:T(8,128)(2,1)} %own_block.1.refs_0_), channel_id=1, source_target_pairs={{0,8},{4,12},{8,0},{12,4},{1,9},{5,13},{9,1},{13,5},{2,10},{6,14},... | collective-permute-start | bytes 626696 | tf_op jit(solution)/shard_map/ppermute | solution.py:277
  8.6 10.2 %collective-permute-start = (bf16[136,768]{1,0:T(8,128)(2,1)}, bf16[136,768]{1,0:T(8,128)(2,1)S(1)}, u32[]{:S(2)}, u32[]{:S(2)}) collective-permute-start(bf16[136,768]{1,0:T(8,128)(2,1)} %own_block.1.refs_0_), channel_id=1, source_target_pairs={{0,4},{4,0},{8,12},{12,8},{1,5},{5,1},{9,13},{13,9},{2,6},{6,2},{1... | collective-permute-start | bytes 626696 | tf_op jit(solution)/shard_map/ppermute | solution.py:277
  18.8 3.5 %collective-permute-start.5 = (bf16[192,768]{1,0:T(8,128)(2,1)S(1)}, bf16[192,768]{1,0:T(8,128)(2,1)S(1)}, u32[]{:S(2)}, u32[]{:S(2)}) collective-permute-start(bf16[192,768]{1,0:T(8,128)(2,1)S(1)} %copy-done.1), channel_id=1, source_target_pairs={{0,1},{1,0},{2,3},{3,2},{4,5},{5,4},{6,7},{7,6},{8,9},{9,8},{10,11... | collective-permute-start | bytes 884744 | tf_op jit(solution)/shard_map/ppermute | solution.py:277
  18.8 3.5 %collective-permute-start.6 = (bf16[192,768]{1,0:T(8,128)(2,1)S(1)}, bf16[192,768]{1,0:T(8,128)(2,1)S(1)}, u32[]{:S(2)}, u32[]{:S(2)}) collective-permute-start(bf16[192,768]{1,0:T(8,128)(2,1)S(1)} %collective-permute-done.4.refs_6_), channel_id=1, source_target_pairs={{0,1},{1,0},{2,3},{3,2},{4,5},{5,4},{6,7},{7,6},{8,9},{9,8},{10,11... | collective-permute-start | bytes 884744 | tf_op jit(solution)/shard_map/ppermute | solution.py:277
  19.3 7.5 %collective-permute-start.7 = (bf16[136,768]{1,0:T(8,128)(2,1)S(1)}, bf16[136,768]{1,0:T(8,128)(2,1)S(1)}, u32[]{:S(2)}, u32[]{:S(2)}) collective-permute-start(bf16[136,768]{1,0:T(8,128)(2,1)S(1)} %collective-permute-done.1.refs_0_), channel_id=1, source_target_pairs={{0,2},{1,3},{2,0},{3,1},{4,6},{5,7},{6,4},{7,5},{8,10},{9,11},{10,... | collective-permute-start | bytes 626696 | tf_op jit(solution)/shard_map/ppermute | solution.py:277
  20.8 8.1 %collective-permute-start.9 = (bf16[136,768]{1,0:T(8,128)(2,1)S(1)}, bf16[136,768]{1,0:T(8,128)(2,1)S(1)}, u32[]{:S(2)}, u32[]{:S(2)}) collective-permute-start(bf16[136,768]{1,0:T(8,128)(2,1)S(1)} %collective-permute-done.1.refs_0_), channel_id=1, source_target_pairs={{0,4},{4,0},{8,12},{12,8},{1,5},{5,1},{9,13},{13,9},{2,6},{6,2},{1... | collective-permute-start | bytes 626696 | tf_op jit(solution)/shard_map/ppermute | solution.py:277
  22.3 11.0 %collective-permute-start.8 = (bf16[136,768]{1,0:T(8,128)(2,1)S(1)}, bf16[136,768]{1,0:T(8,128)(2,1)S(1)}, u32[]{:S(2)}, u32[]{:S(2)}) collective-permute-start(bf16[136,768]{1,0:T(8,128)(2,1)S(1)} %collective-permute-done.2.refs_1_), channel_id=1, source_target_pairs={{0,4},{4,0},{8,12},{12,8},{1,5},{5,1},{9,13},{13,9},{2,6},{6,2},{1... | collective-permute-start | bytes 626696 | tf_op jit(solution)/shard_map/ppermute | solution.py:277
  28.9 5.8 %collective-permute-start.10 = (bf16[136,768]{1,0:T(8,128)(2,1)S(1)}, bf16[136,768]{1,0:T(8,128)(2,1)S(1)}, u32[]{:S(2)}, u32[]{:S(2)}) collective-permute-start(bf16[136,768]{1,0:T(8,128)(2,1)S(1)} %collective-permute-done.9.refs_2_), channel_id=1, source_target_pairs={{0,2},{1,3},{2,0},{3,1},{4,6},{5,7},{6,4},{7,5},{8,10},{9,11},{10,... | collective-permute-start | bytes 626696 | tf_op jit(solution)/shard_map/ppermute | solution.py:277
  40.3 2.1 %collective-permute-start.12 = (bf16[2,192,768]{2,1,0:T(8,128)(2,1)S(1)}, bf16[2,192,768]{2,1,0:T(8,128)(2,1)S(1)}, u32[]{:S(2)}, u32[]{:S(2)}) collective-permute-start(bf16[2,192,768]{2,1,0:T(8,128)(2,1)S(1)} %get-tuple-element.64), channel_id=1, source_target_pairs={{0,1},{1,0},{2,3},{3,2},{4,5},{5,4},{6,7},{7,6},{8,9},{9,8},{10,11... | collective-permute-start | bytes 1769480 | tf_op jit(solution)/shard_map/ppermute | solution.py:277
  40.4 7.8 %collective-permute-start.11 = (bf16[128,768]{1,0:T(8,128)(2,1)S(1)}, bf16[128,768]{1,0:T(8,128)(2,1)S(1)}, u32[]{:S(2)}, u32[]{:S(2)}) collective-permute-start(bf16[128,768]{1,0:T(8,128)(2,1)S(1)} %get-tuple-element.62), channel_id=1, source_target_pairs={{0,4},{4,0},{8,12},{12,8},{1,5},{5,1},{9,13},{13,9},{2,6},{6,2},{1... | collective-permute-start | bytes 589832 | tf_op jit(solution)/shard_map/ppermute | solution.py:277
  42.5 10.6 %collective-permute-start.14 = (bf16[192,768]{1,0:T(8,128)(2,1)S(1)}, bf16[192,768]{1,0:T(8,128)(2,1)S(1)}, u32[]{:S(2)}, u32[]{:S(2)}) collective-permute-start(bf16[192,768]{1,0:T(8,128)(2,1)S(1)} %fusion), channel_id=1, source_target_pairs={{0,2},{1,3},{2,0},{3,1},{4,6},{5,7},{6,4},{7,5},{8,10},{9,11},{10,... | collective-permute-start | bytes 884744 | tf_op jit(solution)/shard_map/ppermute | solution.py:277
  43.0 10.0 %collective-permute-start.13 = (bf16[128,768]{1,0:T(8,128)(2,1)S(1)}, bf16[128,768]{1,0:T(8,128)(2,1)S(1)}, u32[]{:S(2)}, u32[]{:S(2)}) collective-permute-start(bf16[128,768]{1,0:T(8,128)(2,1)S(1)} %get-tuple-element.65), channel_id=1, source_target_pairs={{0,4},{4,0},{8,12},{12,8},{1,5},{5,1},{9,13},{13,9},{2,6},{6,2},{1... | collective-permute-start | bytes 589832 | tf_op jit(solution)/shard_map/ppermute | solution.py:277
  52.9 27.7 %collective-permute-start.21 = (bf16[1024,768]{1,0:T(8,128)(2,1)S(1)}, bf16[1024,768]{1,0:T(8,128)(2,1)S(1)}, u32[]{:S(2)}, u32[]{:S(2)}) collective-permute-start(bf16[1024,768]{1,0:T(8,128)(2,1)S(1)} %grad_label_work.2), channel_id=1, source_target_pairs={{0,1},{1,0},{2,3},{3,2},{4,5},{5,4},{6,7},{7,6},{8,9},{9,8},{10,11... | collective-permute-start | bytes 4718600 | tf_op jit(solution)/shard_map/ppermute | solution.py:277
  53.2 6.3 %collective-permute-start.18 = (bf16[96,768]{1,0:T(8,128)(2,1)S(1)}, bf16[96,768]{1,0:T(8,128)(2,1)S(1)}, u32[]{:S(2)}, u32[]{:S(2)}) collective-permute-start(bf16[96,768]{1,0:T(8,128)(2,1)S(1)} %get-tuple-element.73), channel_id=1, source_target_pairs={{0,4},{4,0},{8,12},{12,8},{1,5},{5,1},{9,13},{13,9},{2,6},{6,2},{1... | collective-permute-start | bytes 442376 | tf_op jit(solution)/shard_map/ppermute | solution.py:277
  54.8 7.8 %collective-permute-start.15 = (bf16[128,768]{1,0:T(8,128)(2,1)S(1)}, bf16[128,768]{1,0:T(8,128)(2,1)S(1)}, u32[]{:S(2)}, u32[]{:S(2)}) collective-permute-start(bf16[128,768]{1,0:T(8,128)(2,1)S(1)} %add_convert_fusion.4), channel_id=1, source_target_pairs={{0,2},{1,3},{2,0},{3,1},{4,6},{5,7},{6,4},{7,5},{8,10},{9,11},{10,... | collective-permute-start | bytes 589832 | tf_op jit(solution)/shard_map/ppermute | solution.py:277
  55.4 11.4 %collective-permute-start.17 = (bf16[128,768]{1,0:T(8,128)(2,1)S(1)}, bf16[128,768]{1,0:T(8,128)(2,1)S(1)}, u32[]{:S(2)}, u32[]{:S(2)}) collective-permute-start(bf16[128,768]{1,0:T(8,128)(2,1)S(1)} %get-tuple-element.72), channel_id=1, source_target_pairs={{0,2},{1,3},{2,0},{3,1},{4,6},{5,7},{6,4},{7,5},{8,10},{9,11},{10,... | collective-permute-start | bytes 589832 | tf_op jit(solution)/shard_map/ppermute | solution.py:277
  59.6 14.9 %collective-permute-start.22 = (bf16[96,768]{1,0:T(8,128)(2,1)S(1)}, bf16[96,768]{1,0:T(8,128)(2,1)S(1)}, u32[]{:S(2)}, u32[]{:S(2)}) collective-permute-start(bf16[96,768]{1,0:T(8,128)(2,1)S(1)} %add_convert_fusion.6), channel_id=1, source_target_pairs={{0,8},{4,12},{8,0},{12,4},{1,9},{5,13},{9,1},{13,5},{2,10},{6,14},... | collective-permute-start | bytes 442376 | tf_op jit(solution)/shard_map/ppermute | solution.py:277
  62.7 11.9 %collective-permute-start.16 = (bf16[128,768]{1,0:T(8,128)(2,1)S(1)}, bf16[128,768]{1,0:T(8,128)(2,1)S(1)}, u32[]{:S(2)}, u32[]{:S(2)}) collective-permute-start(bf16[128,768]{1,0:T(8,128)(2,1)S(1)} %get-tuple-element.69), channel_id=1, source_target_pairs={{0,2},{1,3},{2,0},{3,1},{4,6},{5,7},{6,4},{7,5},{8,10},{9,11},{10,... | collective-permute-start | bytes 589832 | tf_op jit(solution)/shard_map/ppermute | solution.py:277
  63.3 14.4 %collective-permute-start.20 = (bf16[128,768]{1,0:T(8,128)(2,1)S(1)}, bf16[128,768]{1,0:T(8,128)(2,1)S(1)}, u32[]{:S(2)}, u32[]{:S(2)}) collective-permute-start(bf16[128,768]{1,0:T(8,128)(2,1)S(1)} %add_convert_fusion.2), channel_id=1, source_target_pairs={{0,8},{4,12},{8,0},{12,4},{1,9},{5,13},{9,1},{13,5},{2,10},{6,14},... | collective-permute-start | bytes 589832 | tf_op jit(solution)/shard_map/ppermute | solution.py:277
  66.9 13.0 %collective-permute-start.19 = (bf16[128,768]{1,0:T(8,128)(2,1)S(1)}, bf16[128,768]{1,0:T(8,128)(2,1)S(1)}, u32[]{:S(2)}, u32[]{:S(2)}) collective-permute-start(bf16[128,768]{1,0:T(8,128)(2,1)S(1)} %add_convert_fusion.3), channel_id=1, source_target_pairs={{0,4},{4,0},{8,12},{12,8},{1,5},{5,1},{9,13},{13,9},{2,6},{6,2},{1... | collective-permute-start | bytes 589832 | tf_op jit(solution)/shard_map/ppermute | solution.py:277
  74.5 8.0 %collective-permute-start.23 = (bf16[96,768]{1,0:T(8,128)(2,1)S(1)}, bf16[96,768]{1,0:T(8,128)(2,1)S(1)}, u32[]{:S(2)}, u32[]{:S(2)}) collective-permute-start(bf16[96,768]{1,0:T(8,128)(2,1)S(1)} %add_convert_fusion.5.mine_ref), channel_id=1, source_target_pairs={{0,4},{4,0},{8,12},{12,8},{1,5},{5,1},{9,13},{13,9},{2,6},{6,2},{1... | collective-permute-start | bytes 442376 | tf_op jit(solution)/shard_map/ppermute | solution.py:277
  (3 other events, 12.7 us)

commit v14 on v13

--- a/solution.py
+++ b/solution.py
@@ -120,9 +120,10 @@
         backs[s][...] = dot(picks[s], jnp.concatenate(parts, axis=0), 0, 0).astype(BF16)
 
 
-def grad_label_kernel(*refs, calls, n_sets, j):
+def grad_label_kernel(*refs, calls, n_sets, j, n_more):
     grad_scores, blocks, embeddings = refs[:calls], refs[calls : 2 * calls], refs[2 * calls : 3 * calls]
-    *more, out_ref, result, sem = refs[3 * calls :]
+    more, rest = refs[3 * calls : 3 * calls + n_more], refs[3 * calls + n_more :]
+    out_ref, (result, *sem) = rest[0], rest[-2:] if len(rest) > 1 else rest
     rows_of = [slice(j * r.shape[0] // n_sets, (j + 1) * r.shape[0] // n_sets) for r in blocks]
     grad_scores_t = jnp.concatenate([r[at, :].T for r, at in zip(grad_scores, rows_of)], axis=1)
     block_t = jnp.concatenate([r[at, :].T for r, at in zip(blocks, rows_of)], axis=1)
@@ -135,8 +136,9 @@
         for ref in more:
             total = total + ref[rows, :].astype(F32)
         result[rows, :] = total.astype(BF16)
-        copies.append(pltpu.make_async_copy(result.at[rows], out_ref.at[rows], sem.at[b]))
-        copies[b].start()
+        if sem:
+            copies.append(pltpu.make_async_copy(result.at[rows], out_ref.at[rows], sem[0].at[b]))
+            copies[b].start()
     for copy in copies:
         copy.wait()
 
@@ -253,18 +255,24 @@
 
 def grad_label_work(works, n_sets, j, labels_shape, *more):
     slots = list(zip(*(work["slots"] for work in works)))
+    scratch = []
+    if j == 0:
+        sem = pltpu.SemaphoreType.DMA((labels_shape[0] // BLK,))
+        scratch = [pltpu.VMEM(labels_shape, BF16), sem]
     return call(
-        functools.partial(grad_label_kernel, calls=len(works), n_sets=n_sets, j=j),
+        functools.partial(
+            grad_label_kernel, calls=len(works), n_sets=n_sets, j=j, n_more=len(more)
+        ),
         "grad_label_work",
         shaped(labels_shape),
-        [pltpu.VMEM(labels_shape, BF16), pltpu.SemaphoreType.DMA((labels_shape[0] // BLK,))],
+        scratch,
         2 * sum(x.shape[0] for x in slots[0]) // n_sets * labels_shape[0] * labels_shape[1],
         4,
         *slots[0],
         *slots[1],
         *slots[2],
         *more,
-        out_space=pl.BlockSpec(memory_space=pl.ANY),
+        out_space=pl.BlockSpec(memory_space=pl.ANY) if scratch else VMEM,
     )
 
 
@@ -310,17 +318,17 @@
 
 
 def dp_terms(even, odd):
-    got = partner(odd, "dp", 1)
+    got = sent = partner(odd, "dp", 1)
     terms = [[even[i], got[i]] for i in range(even.shape[0])]
     for mask in masks(len(terms)):
         for i in range(len(terms)):
             if i & mask == 0 and i % mask == 0:
-                terms[i].append(partner(add(*terms[i | mask]).astype(BF16), "dp", 2 * mask))
-    return got, terms[0]
-
-
-def sum_shares(even, odd, *first):
-    got, terms = dp_terms(even, odd)
+                sent = add(*terms[i | mask]).astype(BF16)
+                terms[i].append(partner(sent, "dp", 2 * mask))
+    return got, terms[0], sent
+
+
+def sum_shares(even, got, terms, *first):
     rows, width = even.shape[1:]
     half = rows // 2
     keep, send = call(
@@ -347,7 +355,7 @@
     return call(merge_kernel, "merge_share", out, [], 0, 1, after(x, *first), other)
 
 
-def reduce_runs(runs, got_last, keep, first):
+def reduce_runs(runs, got_last, ahead, keep, first):
     def over_dp(parts, *hold):
         parts = [list(part) for part in parts]
         for mask in masks(len(parts)):
@@ -357,11 +365,10 @@
         return parts[0]
 
     n = len(runs)
-    sums = {n - 2: over_dp(list(zip(runs[n - 2], got_last)), keep)}
-    held = sums[n - 2][-1:]
+    sums = {n - 2: over_dp(list(zip(runs[n - 2], got_last)), ahead)}
     for i in reversed(range(0, n - 2, 2)):
         near = after(add(*over_dp([[x] for x in runs[i + 1]], keep)).astype(BF16), first)
-        sums[i] = over_dp([[x] for x in runs[i]], *held) + [partner(near, "labels", 1)]
+        sums[i] = over_dp([[x] for x in runs[i]], keep) + [partner(near, "labels", 1)]
     for mask in masks(n)[1:]:
         for i in range(0, n, 2 * mask):
             sent = after(add(*sums[i + mask]).astype(BF16), first)
@@ -420,12 +427,11 @@
         shards[0] = own_shard
         works, backs = [], {}
         last_call = list(range(1, n_labels, 2))
-        for call_runs in [[run] for run in range(0, n_labels, 2)] + [last_call]:
+        for call_runs in (list(range(0, n_labels, 2)), last_call):
             sources = []
             for run in call_runs:
                 if run == n_labels - 1:
-                    held = far[run - 1][1:] + works[0]["slots"][:1]
-                    far[run] = gather_far(after(near[run], *held))
+                    far[run] = gather_far(after(near[run], *far[run - 1][1:]))
                 elif run % 2:
                     sent = [after(x, *shards[1:]) for x in far[run - 1][1:]]
                     far[run] = near[run : run + 1] + [partner(x, "labels", 1) for x in sent]
@@ -437,10 +443,13 @@
             parts = len(sources) // len(call_runs)
             for i, run in enumerate(call_runs):
                 backs[run] = works[-1]["back"][i * parts : (i + 1) * parts]
-        got_last = [partner(x, "labels", 1) for x in backs[n_labels - 1]]
-        keep, first, share = sum_shares(*works[-1]["shares"], *got_last)
-        terms = reduce_runs(backs, got_last, keep, first)
-        works[0]["slots"][2] = after(works[0]["slots"][2], *got_last[1:])
+        even, odd = works[-1]["shares"]
+        got, share_terms, sent = dp_terms(even, odd)
+        near_last, *far_last = backs[n_labels - 1]
+        got_last = [partner(x, "labels", 1) for x in (after(near_last, sent), *far_last)]
+        keep, first, share = sum_shares(even, got, share_terms, *got_last)
+        terms = reduce_runs(backs, got_last, sent, keep, first)
+        works[0]["slots"][2] = after(works[0]["slots"][2], sent)
         other = partner(grad_label_work(works, 2, 1, label_weight.shape), "dp", 1)
         grad_label = grad_label_work(works, 2, 0, label_weight.shape, other)
         grad_feats = add(*terms).astype(BF16)
@@ -476,7 +485,9 @@
         back = jnp.concatenate([back for work in works for back in work["back"]], axis=0)
         back = swap(back.reshape(n_labels, n_data, cap, width)).reshape(slot_total, width)
         grad_feats = dot(pick, back, 0, 0).astype(BF16)
-        *_, share = sum_shares(*works[-1]["shares"])
+        even, odd = works[-1]["shares"]
+        got, share_terms, _ = dp_terms(even, odd)
+        *_, share = sum_shares(even, got, share_terms)
         grad_label = grad_label_work(works, 1, 0, label_weight.shape)
         grad_enc = join_halves(share, grad_label, grad_feats)
 

time: 83.6 us -> 83.4 us (level)
  waiting for transfers between devices: 30.9 us -> 38 us
  Pallas kernels: 22.8 us -> 16.8 us
  starting transfers between devices: 25.4 us -> 24.3 us
    ppermute x24, waiting for transfers between devices: 30.9 us -> 38 us  [partner(): lax.ppermute(x, axis, [(i, i ^ mask) for i in range(lax.axis_size(axis))])]
    pallas_call x9 -> x8, Pallas kernels: 22.8 us -> 16.8 us  [call(): pl.pallas_call(kernel, in_specs=[space] * len(args), out_specs=jax.tree.m...]
    ppermute x24, starting transfers between devices: 25.4 us -> 24.3 us  [partner(): lax.ppermute(x, axis, [(i, i ^ mask) for i in range(lax.axis_size(axis))])]
  transfers between devices with their start and end apart: 24 -> 24, of which waited for: 13 -> 14; matrix products, arithmetic and copies ran while one was open for 1% -> 1% of each run, Pallas kernels for 20% -> 12%
where the time goes in v14:
time: 83.4 us; the launch traced here: 83.2 us
  waiting for transfers between devices  38 us (46%)
  starting transfers between devices  24.3 us (29%)
  Pallas kernels  16.8 us (20%)
  local copies, waits for them, and re-layouts  2.37 us (3%)
  other arithmetic  1.09 us (1%)
    ppermute x24, waiting for transfers between devices, partner(): lax.ppermute(x, axis, [(i, i ^ mask) for i in range(lax.axis_size(axis))])  38 us
    ppermute x24, starting transfers between devices, partner(): lax.ppermute(x, axis, [(i, i ^ mask) for i in range(lax.axis_size(axis))])  24.3 us
    pallas_call x8, Pallas kernels, call(): pl.pallas_call(kernel, in_specs=[space] * len(args), out_specs=jax.tree.m...  16.8 us
    unnamed x6, local copies, waits for them, and re-layouts  2.37 us
  transfers between devices with their start and end apart: 24, of which 14 were waited for; matrix products, arithmetic and copies ran while one was open for 1% of the time, Pallas kernels for 12%

profile of v14, /device:TPU:0, one launch (start us, length us, event | category | flops | bytes accessed | tf_op | source)
XLA Modules:
  0.0 83.2 jit_solution(5729971499189496289)
XLA Ops:
  1.1 2.6 %collective-permute-start.5 = (bf16[192,768]{1,0:T(8,128)(2,1)}, bf16[192,768]{1,0:T(8,128)(2,1)S(1)}, u32[]{:S(2)}, u32[]{:S(2)}) collective-permute-start(bf16[192,768]{1,0:T(8,128)(2,1)} %shard_ref.1), channel_id=1, source_target_pairs={{0,2},{1,3},{2,0},{3,1},{4,6},{5,7},{6,4},{7,5},{8,10},{9,11},{10,... | collective-permute-start | bytes 884744 | tf_op jit(solution)/shard_map/ppermute | solution.py:285
  3.7 1.6 %own_block.1.refs_0_ = bf16[136,768]{1,0:T(8,128)(2,1)} custom-call(bf16[128,768]{1,0:T(8,128)(2,1)} %feats_ref.1, s32[4,128]{1,0:T(4,128)} %bitcast.5, s32[4,128]{1,0:T(4,128)} %bitcast.6, s32[4,128]{1,0:T(4,128)} %bitcast.7), custom_call_target="tpu_custom_call" | custom-call | bytes 1048576 | tf_op jit(solution)/shard_map/own_block/pallas_call | solution.py:192
  5.4 3.1 %collective-permute-start.1 = (bf16[136,768]{1,0:T(8,128)(2,1)}, bf16[136,768]{1,0:T(8,128)(2,1)S(1)}, u32[]{:S(2)}, u32[]{:S(2)}) collective-permute-start(bf16[136,768]{1,0:T(8,128)(2,1)} %own_block.1.refs_0_), channel_id=1, source_target_pairs={{0,8},{4,12},{8,0},{12,4},{1,9},{5,13},{9,1},{13,5},{2,10},{6,14},... | collective-permute-start | bytes 626696 | tf_op jit(solution)/shard_map/ppermute | solution.py:285
  8.6 1.6 %collective-permute-start = (bf16[136,768]{1,0:T(8,128)(2,1)}, bf16[136,768]{1,0:T(8,128)(2,1)S(1)}, u32[]{:S(2)}, u32[]{:S(2)}) collective-permute-start(bf16[136,768]{1,0:T(8,128)(2,1)} %own_block.1.refs_0_), channel_id=1, source_target_pairs={{0,4},{4,0},{8,12},{12,8},{1,5},{5,1},{9,13},{13,9},{2,6},{6,2},{1... | collective-permute-start | bytes 626696 | tf_op jit(solution)/shard_map/ppermute | solution.py:285
  12.6 3.4 %collective-permute-done.2.refs_1_ = bf16[136,768]{1,0:T(8,128)(2,1)S(1)} collective-permute-done((bf16[136,768]{1,0:T(8,128)(2,1)}, bf16[136,768]{1,0:T(8,128)(2,1)S(1)}, u32[]{:S(2)}, u32[]{:S(2)}) %collective-permute-start.2) | collective-permute-done | bytes 208928 | tf_op jit(solution)/shard_map/ppermute | solution.py:285
  16.0 2.6 %collective-permute-done.1.refs_2_ = bf16[136,768]{1,0:T(8,128)(2,1)S(1)} collective-permute-done((bf16[136,768]{1,0:T(8,128)(2,1)}, bf16[136,768]{1,0:T(8,128)(2,1)S(1)}, u32[]{:S(2)}, u32[]{:S(2)}) %collective-permute-start.1) | collective-permute-done | bytes 208928 | tf_op jit(solution)/shard_map/ppermute | solution.py:285
  19.3 1.5 %collective-permute-start.3 = (bf16[136,768]{1,0:T(8,128)(2,1)S(1)}, bf16[136,768]{1,0:T(8,128)(2,1)S(1)}, u32[]{:S(2)}, u32[]{:S(2)}) collective-permute-start(bf16[136,768]{1,0:T(8,128)(2,1)S(1)} %collective-permute-done.1.refs_2_), channel_id=1, source_target_pairs={{0,2},{1,3},{2,0},{3,1},{4,6},{5,7},{6,4},{7,5},{8,10},{9,11},{10,... | collective-permute-start | bytes 626696 | tf_op jit(solution)/shard_map/ppermute | solution.py:285
  20.8 1.4 %collective-permute-start.9 = (bf16[136,768]{1,0:T(8,128)(2,1)S(1)}, bf16[136,768]{1,0:T(8,128)(2,1)S(1)}, u32[]{:S(2)}, u32[]{:S(2)}) collective-permute-start(bf16[136,768]{1,0:T(8,128)(2,1)S(1)} %collective-permute-done.1.refs_2_), channel_id=1, source_target_pairs={{0,4},{4,0},{8,12},{12,8},{1,5},{5,1},{9,13},{13,9},{2,6},{6,2},{1... | collective-permute-start | bytes 626696 | tf_op jit(solution)/shard_map/ppermute | solution.py:285
  22.2 4.1 %collective-permute-done.3.refs_3_ = bf16[136,768]{1,0:T(8,128)(2,1)S(1)} collective-permute-done((bf16[136,768]{1,0:T(8,128)(2,1)S(1)}, bf16[136,768]{1,0:T(8,128)(2,1)S(1)}, u32[]{:S(2)}, u32[]{:S(2)}) %collective-permute-start.3) | collective-permute-done | bytes 208928 | tf_op jit(solution)/shard_map/ppermute | solution.py:285
  28.1 1.5 %collective-permute-start.8 = (bf16[136,768]{1,0:T(8,128)(2,1)S(1)}, bf16[136,768]{1,0:T(8,128)(2,1)S(1)}, u32[]{:S(2)}, u32[]{:S(2)}) collective-permute-start(bf16[136,768]{1,0:T(8,128)(2,1)S(1)} %collective-permute-done.2.refs_1_), channel_id=1, source_target_pairs={{0,4},{4,0},{8,12},{12,8},{1,5},{5,1},{9,13},{13,9},{2,6},{6,2},{1... | collective-permute-start | bytes 626696 | tf_op jit(solution)/shard_map/ppermute | solution.py:285
  29.6 5.4 %pair_work.2 = (bf16[128,768]{1,0:T(8,128)(2,1)S(1)}, bf16[128,768]{1,0:T(8,128)(2,1)S(1)}, bf16[128,768]{1,0:T(8,128)(2,1)S(1)}, bf16[128,768]{1,0:T(8,128)(2,1...) custom-call(bf16[136,768]{1,0:T(8,128)(2,1)S(1)} %copy-done.2, ...), custom_call_target="tpu_custom_call" | custom-call | flops 3623878656 | bytes 8388608 | tf_op jit(solution)/shard_map/pair_work/pallas_call | solution.py:192
  35.0 5.6 %pair_work.3 = (bf16[128,768]{1,0:T(8,128)(2,1)S(1)}, bf16[128,768]{1,0:T(8,128)(2,1)S(1)}, bf16[128,768]{1,0:T(8,128)(2,1)S(1)}, bf16[128,768]{1,0:T(8,128)(2,1...) custom-call(bf16[136,768]{1,0:T(8,128)(2,1)S(1)} %collective-permute, ...), custom_call_target="tpu_custom_call" | custom-call | flops 3623878656 | bytes 8388608 | tf_op jit(solution)/shard_map/pair_work/pallas_call | solution.py:192
  42.8 1.5 %collective-permute-start.14 = (bf16[192,768]{1,0:T(8,128)(2,1)S(1)}, bf16[192,768]{1,0:T(8,128)(2,1)S(1)}, u32[]{:S(2)}, u32[]{:S(2)}) collective-permute-start(bf16[192,768]{1,0:T(8,128)(2,1)S(1)} %fusion), channel_id=1, source_target_pairs={{0,2},{1,3},{2,0},{3,1},{4,6},{5,7},{6,4},{7,5},{8,10},{9,11},{10,... | collective-permute-start | bytes 884744 | tf_op jit(solution)/shard_map/ppermute | solution.py:285
  46.1 2.4 %collective-permute-done.13 = bf16[128,768]{1,0:T(8,128)(2,1)S(1)} collective-permute-done((bf16[128,768]{1,0:T(8,128)(2,1)S(1)}, bf16[128,768]{1,0:T(8,128)(2,1)S(1)}, u32[]{:S(2)}, u32[]{:S(2)}) %collective-permute-start.13) | collective-permute-done | bytes 196640 | tf_op jit(solution)/shard_map/ppermute | solution.py:285
  48.5 1.5 %collective-permute-start.19 = (bf16[128,768]{1,0:T(8,128)(2,1)S(1)}, bf16[128,768]{1,0:T(8,128)(2,1)S(1)}, u32[]{:S(2)}, u32[]{:S(2)}) collective-permute-start(bf16[128,768]{1,0:T(8,128)(2,1)S(1)} %add_convert_fusion.3), channel_id=1, source_target_pairs={{0,2},{1,3},{2,0},{3,1},{4,6},{5,7},{6,4},{7,5},{8,10},{9,11},{10,... | collective-permute-start | bytes 589832 | tf_op jit(solution)/shard_map/ppermute | solution.py:285
  50.1 2.2 %collective-permute-done.12 = bf16[128,768]{1,0:T(8,128)(2,1)S(1)} collective-permute-done((bf16[128,768]{1,0:T(8,128)(2,1)S(1)}, bf16[128,768]{1,0:T(8,128)(2,1)S(1)}, u32[]{:S(2)}, u32[]{:S(2)}) %collective-permute-start.12) | collective-permute-done | bytes 196640 | tf_op jit(solution)/shard_map/ppermute | solution.py:285
  53.5 2.6 %collective-permute-done.19 = bf16[128,768]{1,0:T(8,128)(2,1)S(1)} collective-permute-done((bf16[128,768]{1,0:T(8,128)(2,1)S(1)}, bf16[128,768]{1,0:T(8,128)(2,1)S(1)}, u32[]{:S(2)}, u32[]{:S(2)}) %collective-permute-start.19) | collective-permute-done | bytes 196640 | tf_op jit(solution)/shard_map/ppermute | solution.py:285
  56.2 1.5 %collective-permute-start.15 = (bf16[128,768]{1,0:T(8,128)(2,1)S(1)}, bf16[128,768]{1,0:T(8,128)(2,1)S(1)}, u32[]{:S(2)}, u32[]{:S(2)}) collective-permute-start(bf16[128,768]{1,0:T(8,128)(2,1)S(1)} %get-tuple-element.63), channel_id=1, source_target_pairs={{0,2},{1,3},{2,0},{3,1},{4,6},{5,7},{6,4},{7,5},{8,10},{9,11},{10,... | collective-permute-start | bytes 589832 | tf_op jit(solution)/shard_map/ppermute | solution.py:285
  58.3 2.5 %collective-permute-start.22 = (bf16[96,768]{1,0:T(8,128)(2,1)S(1)}, bf16[96,768]{1,0:T(8,128)(2,1)S(1)}, u32[]{:S(2)}, u32[]{:S(2)}) collective-permute-start(bf16[96,768]{1,0:T(8,128)(2,1)S(1)} %add_convert_fusion.6), channel_id=1, source_target_pairs={{0,8},{4,12},{8,0},{12,4},{1,9},{5,13},{9,1},{13,5},{2,10},{6,14},... | collective-permute-start | bytes 442376 | tf_op jit(solution)/shard_map/ppermute | solution.py:285
  61.3 5.3 %collective-permute-done.16 = bf16[128,768]{1,0:T(8,128)(2,1)S(1)} collective-permute-done((bf16[128,768]{1,0:T(8,128)(2,1)S(1)}, bf16[128,768]{1,0:T(8,128)(2,1)S(1)}, u32[]{:S(2)}, u32[]{:S(2)}) %collective-permute-start.16) | collective-permute-done | bytes 196640 | tf_op jit(solution)/shard_map/ppermute | solution.py:285
  67.2 4.4 %collective-permute-done.22 = bf16[96,768]{1,0:T(8,128)(2,1)S(1)} collective-permute-done((bf16[96,768]{1,0:T(8,128)(2,1)S(1)}, bf16[96,768]{1,0:T(8,128)(2,1)S(1)}, u32[]{:S(2)}, u32[]{:S(2)}) %collective-permute-start.22) | collective-permute-done | bytes 147488 | tf_op jit(solution)/shard_map/ppermute | solution.py:285
  72.0 3.5 %collective-permute-done.20 = bf16[128,768]{1,0:T(8,128)(2,1)S(1)} collective-permute-done((bf16[128,768]{1,0:T(8,128)(2,1)S(1)}, bf16[128,768]{1,0:T(8,128)(2,1)S(1)}, u32[]{:S(2)}, u32[]{:S(2)}) %collective-permute-start.20) | collective-permute-done | bytes 196640 | tf_op jit(solution)/shard_map/ppermute | solution.py:285
  75.5 4.3 %collective-permute-done.18 = bf16[128,768]{1,0:T(8,128)(2,1)S(1)} collective-permute-done((bf16[128,768]{1,0:T(8,128)(2,1)S(1)}, bf16[128,768]{1,0:T(8,128)(2,1)S(1)}, u32[]{:S(2)}, u32[]{:S(2)}) %collective-permute-start.18) | collective-permute-done | bytes 196640 | tf_op jit(solution)/shard_map/ppermute | solution.py:285
  80.5 1.8 %grad_label_work.3 = bf16[1024,768]{1,0:T(8,128)(2,1)} custom-call(f32[512,128]{1,0:T(8,128)S(1)} %get-tuple-element.73.refs_0_, f32[512,128]{1,0:T(8,128)S(1)} %get-tuple-element.74.refs_1_, s32[512,128]{1,0:T(8,128)S(1)} %get-tuple-element.75.refs_2_, s32[512,128]{1,0:T(8,128)S(1)} %get-tuple-element.76.refs_3_, ...), custom_call_target="tpu_custom_call" | custom-call | flops 805306368 | bytes 4194304 | tf_op jit(solution)/shard_map/grad_label_work/pallas_call | solution.py:192
  (45 shorter events, 14.5 us)
Async XLA Ops:
  0.6 9.5 %collective-permute-start.4 = (bf16[1024,768]{1,0:T(8,128)(2,1)}, bf16[1024,768]{1,0:T(8,128)(2,1)S(1)}, u32[]{:S(2)}, u32[]{:S(2)}) collective-permute-start(bf16[1024,768]{1,0:T(8,128)(2,1)} %label_ref), channel_id=1, source_target_pairs={{0,1},{1,0},{2,3},{3,2},{4,5},{5,4},{6,7},{7,6},{8,9},{9,8},{10,11... | collective-permute-start | bytes 4718600 | tf_op jit(solution)/shard_map/ppermute | solution.py:285
  1.1 17.6 %collective-permute-start.5 = (bf16[192,768]{1,0:T(8,128)(2,1)}, bf16[192,768]{1,0:T(8,128)(2,1)S(1)}, u32[]{:S(2)}, u32[]{:S(2)}) collective-permute-start(bf16[192,768]{1,0:T(8,128)(2,1)} %shard_ref.1), channel_id=1, source_target_pairs={{0,2},{1,3},{2,0},{3,1},{4,6},{5,7},{6,4},{7,5},{8,10},{9,11},{10,... | collective-permute-start | bytes 884744 | tf_op jit(solution)/shard_map/ppermute | solution.py:285
  5.4 10.6 %collective-permute-start.2 = (bf16[136,768]{1,0:T(8,128)(2,1)}, bf16[136,768]{1,0:T(8,128)(2,1)S(1)}, u32[]{:S(2)}, u32[]{:S(2)}) collective-permute-start(bf16[136,768]{1,0:T(8,128)(2,1)} %own_block.1.refs_0_), channel_id=1, source_target_pairs={{0,2},{1,3},{2,0},{3,1},{4,6},{5,7},{6,4},{7,5},{8,10},{9,11},{10,... | collective-permute-start | bytes 626696 | tf_op jit(solution)/shard_map/ppermute | solution.py:285
  5.4 13.1 %collective-permute-start.1 = (bf16[136,768]{1,0:T(8,128)(2,1)}, bf16[136,768]{1,0:T(8,128)(2,1)S(1)}, u32[]{:S(2)}, u32[]{:S(2)}) collective-permute-start(bf16[136,768]{1,0:T(8,128)(2,1)} %own_block.1.refs_0_), channel_id=1, source_target_pairs={{0,8},{4,12},{8,0},{12,4},{1,9},{5,13},{9,1},{13,5},{2,10},{6,14},... | collective-permute-start | bytes 626696 | tf_op jit(solution)/shard_map/ppermute | solution.py:285
  8.6 10.2 %collective-permute-start = (bf16[136,768]{1,0:T(8,128)(2,1)}, bf16[136,768]{1,0:T(8,128)(2,1)S(1)}, u32[]{:S(2)}, u32[]{:S(2)}) collective-permute-start(bf16[136,768]{1,0:T(8,128)(2,1)} %own_block.1.refs_0_), channel_id=1, source_target_pairs={{0,4},{4,0},{8,12},{12,8},{1,5},{5,1},{9,13},{13,9},{2,6},{6,2},{1... | collective-permute-start | bytes 626696 | tf_op jit(solution)/shard_map/ppermute | solution.py:285
  18.8 9.3 %collective-permute-start.6 = (bf16[192,768]{1,0:T(8,128)(2,1)S(1)}, bf16[192,768]{1,0:T(8,128)(2,1)S(1)}, u32[]{:S(2)}, u32[]{:S(2)}) collective-permute-start(bf16[192,768]{1,0:T(8,128)(2,1)S(1)} %copy-done.1), channel_id=1, source_target_pairs={{0,1},{1,0},{2,3},{3,2},{4,5},{5,4},{6,7},{7,6},{8,9},{9,8},{10,11... | collective-permute-start | bytes 884744 | tf_op jit(solution)/shard_map/ppermute | solution.py:285
  18.8 9.3 %collective-permute-start.7 = (bf16[192,768]{1,0:T(8,128)(2,1)S(1)}, bf16[192,768]{1,0:T(8,128)(2,1)S(1)}, u32[]{:S(2)}, u32[]{:S(2)}) collective-permute-start(bf16[192,768]{1,0:T(8,128)(2,1)S(1)} %collective-permute-done.5.refs_8_), channel_id=1, source_target_pairs={{0,1},{1,0},{2,3},{3,2},{4,5},{5,4},{6,7},{7,6},{8,9},{9,8},{10,11... | collective-permute-start | bytes 884744 | tf_op jit(solution)/shard_map/ppermute | solution.py:285
  19.3 7.1 %collective-permute-start.3 = (bf16[136,768]{1,0:T(8,128)(2,1)S(1)}, bf16[136,768]{1,0:T(8,128)(2,1)S(1)}, u32[]{:S(2)}, u32[]{:S(2)}) collective-permute-start(bf16[136,768]{1,0:T(8,128)(2,1)S(1)} %collective-permute-done.1.refs_2_), channel_id=1, source_target_pairs={{0,2},{1,3},{2,0},{3,1},{4,6},{5,7},{6,4},{7,5},{8,10},{9,11},{10,... | collective-permute-start | bytes 626696 | tf_op jit(solution)/shard_map/ppermute | solution.py:285
  20.8 6.8 %collective-permute-start.9 = (bf16[136,768]{1,0:T(8,128)(2,1)S(1)}, bf16[136,768]{1,0:T(8,128)(2,1)S(1)}, u32[]{:S(2)}, u32[]{:S(2)}) collective-permute-start(bf16[136,768]{1,0:T(8,128)(2,1)S(1)} %collective-permute-done.1.refs_2_), channel_id=1, source_target_pairs={{0,4},{4,0},{8,12},{12,8},{1,5},{5,1},{9,13},{13,9},{2,6},{6,2},{1... | collective-permute-start | bytes 626696 | tf_op jit(solution)/shard_map/ppermute | solution.py:285
  27.6 7.4 %collective-permute-start.10 = (bf16[136,768]{1,0:T(8,128)(2,1)S(1)}, bf16[136,768]{1,0:T(8,128)(2,1)S(1)}, u32[]{:S(2)}, u32[]{:S(2)}) collective-permute-start(bf16[136,768]{1,0:T(8,128)(2,1)S(1)} %collective-permute-done.9.refs_2_), channel_id=1, source_target_pairs={{0,2},{1,3},{2,0},{3,1},{4,6},{5,7},{6,4},{7,5},{8,10},{9,11},{10,... | collective-permute-start | bytes 626696 | tf_op jit(solution)/shard_map/ppermute | solution.py:285
  28.1 6.9 %collective-permute-start.8 = (bf16[136,768]{1,0:T(8,128)(2,1)S(1)}, bf16[136,768]{1,0:T(8,128)(2,1)S(1)}, u32[]{:S(2)}, u32[]{:S(2)}) collective-permute-start(bf16[136,768]{1,0:T(8,128)(2,1)S(1)} %collective-permute-done.2.refs_1_), channel_id=1, source_target_pairs={{0,4},{4,0},{8,12},{12,8},{1,5},{5,1},{9,13},{13,9},{2,6},{6,2},{1... | collective-permute-start | bytes 626696 | tf_op jit(solution)/shard_map/ppermute | solution.py:285
  40.6 2.1 %collective-permute-start.11 = (bf16[2,192,768]{2,1,0:T(8,128)(2,1)S(1)}, bf16[2,192,768]{2,1,0:T(8,128)(2,1)S(1)}, u32[]{:S(2)}, u32[]{:S(2)}) collective-permute-start(bf16[2,192,768]{2,1,0:T(8,128)(2,1)S(1)} %get-tuple-element.57), channel_id=1, source_target_pairs={{0,1},{1,0},{2,3},{3,2},{4,5},{5,4},{6,7},{7,6},{8,9},{9,8},{10,11... | collective-permute-start | bytes 1769480 | tf_op jit(solution)/shard_map/ppermute | solution.py:285
  40.7 7.8 %collective-permute-start.13 = (bf16[128,768]{1,0:T(8,128)(2,1)S(1)}, bf16[128,768]{1,0:T(8,128)(2,1)S(1)}, u32[]{:S(2)}, u32[]{:S(2)}) collective-permute-start(bf16[128,768]{1,0:T(8,128)(2,1)S(1)} %get-tuple-element.60), channel_id=1, source_target_pairs={{0,4},{4,0},{8,12},{12,8},{1,5},{5,1},{9,13},{13,9},{2,6},{6,2},{1... | collective-permute-start | bytes 589832 | tf_op jit(solution)/shard_map/ppermute | solution.py:285
  42.8 9.9 %collective-permute-start.14 = (bf16[192,768]{1,0:T(8,128)(2,1)S(1)}, bf16[192,768]{1,0:T(8,128)(2,1)S(1)}, u32[]{:S(2)}, u32[]{:S(2)}) collective-permute-start(bf16[192,768]{1,0:T(8,128)(2,1)S(1)} %fusion), channel_id=1, source_target_pairs={{0,2},{1,3},{2,0},{3,1},{4,6},{5,7},{6,4},{7,5},{8,10},{9,11},{10,... | collective-permute-start | bytes 884744 | tf_op jit(solution)/shard_map/ppermute | solution.py:285
  44.3 7.9 %collective-permute-start.12 = (bf16[128,768]{1,0:T(8,128)(2,1)S(1)}, bf16[128,768]{1,0:T(8,128)(2,1)S(1)}, u32[]{:S(2)}, u32[]{:S(2)}) collective-permute-start(bf16[128,768]{1,0:T(8,128)(2,1)S(1)} %get-tuple-element.59), channel_id=1, source_target_pairs={{0,4},{4,0},{8,12},{12,8},{1,5},{5,1},{9,13},{13,9},{2,6},{6,2},{1... | collective-permute-start | bytes 589832 | tf_op jit(solution)/shard_map/ppermute | solution.py:285
  46.0 34.5 %collective-permute-start.21 = (bf16[1024,768]{1,0:T(8,128)(2,1)S(1)}, bf16[1024,768]{1,0:T(8,128)(2,1)S(1)}, u32[]{:S(2)}, u32[]{:S(2)}) collective-permute-start(bf16[1024,768]{1,0:T(8,128)(2,1)S(1)} %grad_label_work.2), channel_id=1, source_target_pairs={{0,1},{1,0},{2,3},{3,2},{4,5},{5,4},{6,7},{7,6},{8,9},{9,8},{10,11... | collective-permute-start | bytes 4718600 | tf_op jit(solution)/shard_map/ppermute | solution.py:285
  48.5 7.6 %collective-permute-start.19 = (bf16[128,768]{1,0:T(8,128)(2,1)S(1)}, bf16[128,768]{1,0:T(8,128)(2,1)S(1)}, u32[]{:S(2)}, u32[]{:S(2)}) collective-permute-start(bf16[128,768]{1,0:T(8,128)(2,1)S(1)} %add_convert_fusion.3), channel_id=1, source_target_pairs={{0,2},{1,3},{2,0},{3,1},{4,6},{5,7},{6,4},{7,5},{8,10},{9,11},{10,... | collective-permute-start | bytes 589832 | tf_op jit(solution)/shard_map/ppermute | solution.py:285
  52.9 5.4 %collective-permute-start.17 = (bf16[96,768]{1,0:T(8,128)(2,1)S(1)}, bf16[96,768]{1,0:T(8,128)(2,1)S(1)}, u32[]{:S(2)}, u32[]{:S(2)}) collective-permute-start(bf16[96,768]{1,0:T(8,128)(2,1)S(1)} %get-tuple-element.67), channel_id=1, source_target_pairs={{0,4},{4,0},{8,12},{12,8},{1,5},{5,1},{9,13},{13,9},{2,6},{6,2},{1... | collective-permute-start | bytes 442376 | tf_op jit(solution)/shard_map/ppermute | solution.py:285
  56.2 15.8 %collective-permute-start.15 = (bf16[128,768]{1,0:T(8,128)(2,1)S(1)}, bf16[128,768]{1,0:T(8,128)(2,1)S(1)}, u32[]{:S(2)}, u32[]{:S(2)}) collective-permute-start(bf16[128,768]{1,0:T(8,128)(2,1)S(1)} %get-tuple-element.63), channel_id=1, source_target_pairs={{0,2},{1,3},{2,0},{3,1},{4,6},{5,7},{6,4},{7,5},{8,10},{9,11},{10,... | collective-permute-start | bytes 589832 | tf_op jit(solution)/shard_map/ppermute | solution.py:285
  57.7 8.9 %collective-permute-start.16 = (bf16[128,768]{1,0:T(8,128)(2,1)S(1)}, bf16[128,768]{1,0:T(8,128)(2,1)S(1)}, u32[]{:S(2)}, u32[]{:S(2)}) collective-permute-start(bf16[128,768]{1,0:T(8,128)(2,1)S(1)} %get-tuple-element.66), channel_id=1, source_target_pairs={{0,2},{1,3},{2,0},{3,1},{4,6},{5,7},{6,4},{7,5},{8,10},{9,11},{10,... | collective-permute-start | bytes 589832 | tf_op jit(solution)/shard_map/ppermute | solution.py:285
  58.3 13.3 %collective-permute-start.22 = (bf16[96,768]{1,0:T(8,128)(2,1)S(1)}, bf16[96,768]{1,0:T(8,128)(2,1)S(1)}, u32[]{:S(2)}, u32[]{:S(2)}) collective-permute-start(bf16[96,768]{1,0:T(8,128)(2,1)S(1)} %add_convert_fusion.6), channel_id=1, source_target_pairs={{0,8},{4,12},{8,0},{12,4},{1,9},{5,13},{9,1},{13,5},{2,10},{6,14},... | collective-permute-start | bytes 442376 | tf_op jit(solution)/shard_map/ppermute | solution.py:285
  60.8 14.7 %collective-permute-start.20 = (bf16[128,768]{1,0:T(8,128)(2,1)S(1)}, bf16[128,768]{1,0:T(8,128)(2,1)S(1)}, u32[]{:S(2)}, u32[]{:S(2)}) collective-permute-start(bf16[128,768]{1,0:T(8,128)(2,1)S(1)} %add_convert_fusion.2), channel_id=1, source_target_pairs={{0,8},{4,12},{8,0},{12,4},{1,9},{5,13},{9,1},{13,5},{2,10},{6,14},... | collective-permute-start | bytes 589832 | tf_op jit(solution)/shard_map/ppermute | solution.py:285
  66.6 13.1 %collective-permute-start.18 = (bf16[128,768]{1,0:T(8,128)(2,1)S(1)}, bf16[128,768]{1,0:T(8,128)(2,1)S(1)}, u32[]{:S(2)}, u32[]{:S(2)}) collective-permute-start(bf16[128,768]{1,0:T(8,128)(2,1)S(1)} %add_convert_fusion.4), channel_id=1, source_target_pairs={{0,4},{4,0},{8,12},{12,8},{1,5},{5,1},{9,13},{13,9},{2,6},{6,2},{1... | collective-permute-start | bytes 589832 | tf_op jit(solution)/shard_map/ppermute | solution.py:285
  71.7 10.7 %collective-permute-start.23 = (bf16[96,768]{1,0:T(8,128)(2,1)S(1)}, bf16[96,768]{1,0:T(8,128)(2,1)S(1)}, u32[]{:S(2)}, u32[]{:S(2)}) collective-permute-start(bf16[96,768]{1,0:T(8,128)(2,1)S(1)} %add_convert_fusion.5.mine_ref), channel_id=1, source_target_pairs={{0,4},{4,0},{8,12},{12,8},{1,5},{5,1},{9,13},{13,9},{2,6},{6,2},{1... | collective-permute-start | bytes 442376 | tf_op jit(solution)/shard_map/ppermute | solution.py:285
  (3 other events, 19.4 us)

commit v15 on v14

--- a/solution.py
+++ b/solution.py
@@ -365,13 +365,14 @@
         return parts[0]
 
     n = len(runs)
-    sums = {n - 2: over_dp(list(zip(runs[n - 2], got_last)), ahead)}
+    sums, sent_near = {n - 2: over_dp(list(zip(runs[n - 2], got_last)), ahead)}, []
     for i in reversed(range(0, n - 2, 2)):
-        near = after(add(*over_dp([[x] for x in runs[i + 1]], keep)).astype(BF16), first)
-        sums[i] = over_dp([[x] for x in runs[i]], keep) + [partner(near, "labels", 1)]
+        near = add(*over_dp([[x] for x in runs[i + 1]], ahead)).astype(BF16)
+        sent_near.append(partner(near, "labels", 1))
+        sums[i] = over_dp([[x] for x in runs[i]], keep) + sent_near[-1:]
     for mask in masks(n)[1:]:
         for i in range(0, n, 2 * mask):
-            sent = after(add(*sums[i + mask]).astype(BF16), first)
+            sent = after(add(*sums[i + mask]).astype(BF16), first, *sent_near)
             sums[i].append(partner(sent, "labels", mask))
     return sums[0]
 
@@ -420,10 +421,8 @@
             enc_weight,
         )
         near = gather_labels(own, labels[0])
-        far = {0: gather_far(near[0])}
-        shards = gather_near(
-            gather_far(enc_weight), *far[0][1:], *near[1:3], labels[0]
-        )
+        far = {0: gather_far(own)}
+        shards = gather_near(gather_far(enc_weight))
         shards[0] = own_shard
         works, backs = [], {}
         last_call = list(range(1, n_labels, 2))
@@ -436,7 +435,7 @@
                     sent = [after(x, *shards[1:]) for x in far[run - 1][1:]]
                     far[run] = near[run : run + 1] + [partner(x, "labels", 1) for x in sent]
                 elif run:
-                    far[run] = gather_far(after(near[run], *far[0][1:]))
+                    far[run] = gather_far(after(near[run], *far[0][1:], *near[1:3], labels[0]))
                 sources += [after(near[run], *([] if run else near[1:3]))] + far[run][1:]
             before, last = works[-1] if works else None, call_runs is last_call
             works.append(pair_work(sources, labels, shards, cap, pick_count, before, last))
@@ -449,7 +448,6 @@
         got_last = [partner(x, "labels", 1) for x in (after(near_last, sent), *far_last)]
         keep, first, share = sum_shares(even, got, share_terms, *got_last)
         terms = reduce_runs(backs, got_last, sent, keep, first)
-        works[0]["slots"][2] = after(works[0]["slots"][2], sent)
         other = partner(grad_label_work(works, 2, 1, label_weight.shape), "dp", 1)
         grad_label = grad_label_work(works, 2, 0, label_weight.shape, other)
         grad_feats = add(*terms).astype(BF16)

time: 83.4 us -> 79.8 us (0.957)
  waiting for transfers between devices: 38 us -> 31 us
  starting transfers between devices: 24.3 us -> 27.6 us
    ppermute x24, waiting for transfers between devices: 38 us -> 31 us  [partner(): lax.ppermute(x, axis, [(i, i ^ mask) for i in range(lax.axis_size(axis))])]
    ppermute x24, starting transfers between devices: 24.3 us -> 27.6 us  [partner(): lax.ppermute(x, axis, [(i, i ^ mask) for i in range(lax.axis_size(axis))])]
  transfers between devices with their start and end apart: 24 -> 24, of which waited for: 14 -> 13; matrix products, arithmetic and copies ran while one was open for 1% -> 1% of each run, Pallas kernels for 12% -> 13%
where the time goes in v15:
time: 79.8 us; the launch traced here: 79.6 us
  waiting for transfers between devices  31 us (39%)
  starting transfers between devices  27.6 us (35%)
  Pallas kernels  16.7 us (21%)
  local copies, waits for them, and re-layouts  2.37 us (3%)
  other arithmetic  1.1 us (1%)
    ppermute x24, waiting for transfers between devices, partner(): lax.ppermute(x, axis, [(i, i ^ mask) for i in range(lax.axis_size(axis))])  31 us
    ppermute x24, starting transfers between devices, partner(): lax.ppermute(x, axis, [(i, i ^ mask) for i in range(lax.axis_size(axis))])  27.6 us
    pallas_call x8, Pallas kernels, call(): pl.pallas_call(kernel, in_specs=[space] * len(args), out_specs=jax.tree.m...  16.7 us
    unnamed x6, local copies, waits for them, and re-layouts  2.37 us
  transfers between devices with their start and end apart: 24, of which 13 were waited for; matrix products, arithmetic and copies ran while one was open for 1% of the time, Pallas kernels for 13%

profile of v15, /device:TPU:0, one launch (start us, length us, event | category | flops | bytes accessed | tf_op | source)
XLA Modules:
  0.0 79.6 jit_solution(1087998239197058817)
XLA Ops:
  1.1 2.6 %collective-permute-start.5 = (bf16[192,768]{1,0:T(8,128)(2,1)}, bf16[192,768]{1,0:T(8,128)(2,1)S(1)}, u32[]{:S(2)}, u32[]{:S(2)}) collective-permute-start(bf16[192,768]{1,0:T(8,128)(2,1)} %shard_ref.1), channel_id=1, source_target_pairs={{0,2},{1,3},{2,0},{3,1},{4,6},{5,7},{6,4},{7,5},{8,10},{9,11},{10,... | collective-permute-start | bytes 884744 | tf_op jit(solution)/shard_map/ppermute | solution.py:285
  3.7 1.6 %own_block.1.refs_0_ = bf16[136,768]{1,0:T(8,128)(2,1)} custom-call(bf16[128,768]{1,0:T(8,128)(2,1)} %feats_ref.1, s32[4,128]{1,0:T(4,128)} %bitcast.5, s32[4,128]{1,0:T(4,128)} %bitcast.6, s32[4,128]{1,0:T(4,128)} %bitcast.7), custom_call_target="tpu_custom_call" | custom-call | bytes 1048576 | tf_op jit(solution)/shard_map/own_block/pallas_call | solution.py:192
  5.4 2.7 %collective-permute-start.1 = (bf16[136,768]{1,0:T(8,128)(2,1)}, bf16[136,768]{1,0:T(8,128)(2,1)S(1)}, u32[]{:S(2)}, u32[]{:S(2)}) collective-permute-start(bf16[136,768]{1,0:T(8,128)(2,1)} %own_block.1.refs_0_), channel_id=1, source_target_pairs={{0,8},{4,12},{8,0},{12,4},{1,9},{5,13},{9,1},{13,5},{2,10},{6,14},... | collective-permute-start | bytes 626696 | tf_op jit(solution)/shard_map/ppermute | solution.py:285
  8.6 1.6 %collective-permute-start = (bf16[136,768]{1,0:T(8,128)(2,1)}, bf16[136,768]{1,0:T(8,128)(2,1)S(1)}, u32[]{:S(2)}, u32[]{:S(2)}) collective-permute-start(bf16[136,768]{1,0:T(8,128)(2,1)} %own_block.1.refs_0_), channel_id=1, source_target_pairs={{0,4},{4,0},{8,12},{12,8},{1,5},{5,1},{9,13},{13,9},{2,6},{6,2},{1... | collective-permute-start | bytes 626696 | tf_op jit(solution)/shard_map/ppermute | solution.py:285
  10.1 1.7 %collective-permute-done.5.refs_8_ = bf16[192,768]{1,0:T(8,128)(2,1)S(1)} collective-permute-done((bf16[192,768]{1,0:T(8,128)(2,1)}, bf16[192,768]{1,0:T(8,128)(2,1)S(1)}, u32[]{:S(2)}, u32[]{:S(2)}) %collective-permute-start.5) | collective-permute-done | bytes 294944 | tf_op jit(solution)/shard_map/ppermute | solution.py:285
  12.3 1.4 %copy-done = bf16[1024,768]{1,0:T(8,128)(2,1)S(1)} copy-done((bf16[1024,768]{1,0:T(8,128)(2,1)S(1)}, bf16[1024,768]{1,0:T(8,128)(2,1)}, u32[]{:S(2)}) %copy-start) | copy-done | bytes 1572888
  14.8 3.6 %collective-permute-done.1.refs_2_ = bf16[136,768]{1,0:T(8,128)(2,1)S(1)} collective-permute-done((bf16[136,768]{1,0:T(8,128)(2,1)}, bf16[136,768]{1,0:T(8,128)(2,1)S(1)}, u32[]{:S(2)}, u32[]{:S(2)}) %collective-permute-start.1) | collective-permute-done | bytes 208928 | tf_op jit(solution)/shard_map/ppermute | solution.py:285
  18.8 1.4 %collective-permute-start.4 = (bf16[136,768]{1,0:T(8,128)(2,1)S(1)}, bf16[136,768]{1,0:T(8,128)(2,1)S(1)}, u32[]{:S(2)}, u32[]{:S(2)}) collective-permute-start(bf16[136,768]{1,0:T(8,128)(2,1)S(1)} %collective-permute-done.1.refs_2_), channel_id=1, source_target_pairs={{0,2},{1,3},{2,0},{3,1},{4,6},{5,7},{6,4},{7,5},{8,10},{9,11},{10,... | collective-permute-start | bytes 626696 | tf_op jit(solution)/shard_map/ppermute | solution.py:285
  20.5 1.8 %collective-permute-start.8 = (bf16[136,768]{1,0:T(8,128)(2,1)S(1)}, bf16[136,768]{1,0:T(8,128)(2,1)S(1)}, u32[]{:S(2)}, u32[]{:S(2)}) collective-permute-start(bf16[136,768]{1,0:T(8,128)(2,1)S(1)} %collective-permute-done.2.refs_1_), channel_id=1, source_target_pairs={{0,4},{4,0},{8,12},{12,8},{1,5},{5,1},{9,13},{13,9},{2,6},{6,2},{1... | collective-permute-start | bytes 626696 | tf_op jit(solution)/shard_map/ppermute | solution.py:285
  22.3 2.4 %collective-permute-done.4.refs_3_ = bf16[136,768]{1,0:T(8,128)(2,1)S(1)} collective-permute-done((bf16[136,768]{1,0:T(8,128)(2,1)S(1)}, bf16[136,768]{1,0:T(8,128)(2,1)S(1)}, u32[]{:S(2)}, u32[]{:S(2)}) %collective-permute-start.4) | collective-permute-done | bytes 208928 | tf_op jit(solution)/shard_map/ppermute | solution.py:285
  24.7 2.8 %collective-permute-done.9.refs_2_ = bf16[136,768]{1,0:T(8,128)(2,1)S(1)} collective-permute-done((bf16[136,768]{1,0:T(8,128)(2,1)S(1)}, bf16[136,768]{1,0:T(8,128)(2,1)S(1)}, u32[]{:S(2)}, u32[]{:S(2)}) %collective-permute-start.9) | collective-permute-done | bytes 208928 | tf_op jit(solution)/shard_map/ppermute | solution.py:285
  28.7 5.4 %pair_work.2 = (bf16[128,768]{1,0:T(8,128)(2,1)S(1)}, bf16[128,768]{1,0:T(8,128)(2,1)S(1)}, bf16[128,768]{1,0:T(8,128)(2,1)S(1)}, bf16[128,768]{1,0:T(8,128)(2,1...) custom-call(bf16[136,768]{1,0:T(8,128)(2,1)S(1)} %copy-done.2, ...), custom_call_target="tpu_custom_call" | custom-call | flops 3623878656 | bytes 8388608 | tf_op jit(solution)/shard_map/pair_work/pallas_call | solution.py:192
  34.1 5.6 %pair_work.3 = (bf16[128,768]{1,0:T(8,128)(2,1)S(1)}, bf16[128,768]{1,0:T(8,128)(2,1)S(1)}, bf16[128,768]{1,0:T(8,128)(2,1)S(1)}, bf16[128,768]{1,0:T(8,128)(2,1...) custom-call(bf16[136,768]{1,0:T(8,128)(2,1)S(1)} %collective-permute, ...), custom_call_target="tpu_custom_call" | custom-call | flops 3623878656 | bytes 8388608 | tf_op jit(solution)/shard_map/pair_work/pallas_call | solution.py:192
  39.8 1.5 %collective-permute-start.13 = (bf16[128,768]{1,0:T(8,128)(2,1)S(1)}, bf16[128,768]{1,0:T(8,128)(2,1)S(1)}, u32[]{:S(2)}, u32[]{:S(2)}) collective-permute-start(bf16[128,768]{1,0:T(8,128)(2,1)S(1)} %get-tuple-element.58), channel_id=1, source_target_pairs={{0,4},{4,0},{8,12},{12,8},{1,5},{5,1},{9,13},{13,9},{2,6},{6,2},{1... | collective-permute-start | bytes 589832 | tf_op jit(solution)/shard_map/ppermute | solution.py:285
  44.2 1.2 %collective-permute-start.16 = (bf16[128,768]{1,0:T(8,128)(2,1)S(1)}, bf16[128,768]{1,0:T(8,128)(2,1)S(1)}, u32[]{:S(2)}, u32[]{:S(2)}) collective-permute-start(bf16[128,768]{1,0:T(8,128)(2,1)S(1)} %get-tuple-element.64), channel_id=1, source_target_pairs={{0,2},{1,3},{2,0},{3,1},{4,6},{5,7},{6,4},{7,5},{8,10},{9,11},{10,... | collective-permute-start | bytes 589832 | tf_op jit(solution)/shard_map/ppermute | solution.py:285
  45.4 2.2 %collective-permute-done.13 = bf16[128,768]{1,0:T(8,128)(2,1)S(1)} collective-permute-done((bf16[128,768]{1,0:T(8,128)(2,1)S(1)}, bf16[128,768]{1,0:T(8,128)(2,1)S(1)}, u32[]{:S(2)}, u32[]{:S(2)}) %collective-permute-start.13) | collective-permute-done | bytes 196640 | tf_op jit(solution)/shard_map/ppermute | solution.py:285
  48.5 2.9 %collective-permute-done.12 = bf16[128,768]{1,0:T(8,128)(2,1)S(1)} collective-permute-done((bf16[128,768]{1,0:T(8,128)(2,1)S(1)}, bf16[128,768]{1,0:T(8,128)(2,1)S(1)}, u32[]{:S(2)}, u32[]{:S(2)}) %collective-permute-start.12) | collective-permute-done | bytes 196640 | tf_op jit(solution)/shard_map/ppermute | solution.py:285
  51.4 1.2 %collective-permute-done.14.refs_0_ = bf16[192,768]{1,0:T(8,128)(2,1)S(1)} collective-permute-done((bf16[192,768]{1,0:T(8,128)(2,1)S(1)}, bf16[192,768]{1,0:T(8,128)(2,1)S(1)}, u32[]{:S(2)}, u32[]{:S(2)}) %collective-permute-start.14) | collective-permute-done | bytes 294944 | tf_op jit(solution)/shard_map/ppermute | solution.py:285
  53.5 3.3 %collective-permute-done.16 = bf16[128,768]{1,0:T(8,128)(2,1)S(1)} collective-permute-done((bf16[128,768]{1,0:T(8,128)(2,1)S(1)}, bf16[128,768]{1,0:T(8,128)(2,1)S(1)}, u32[]{:S(2)}, u32[]{:S(2)}) %collective-permute-start.16) | collective-permute-done | bytes 196640 | tf_op jit(solution)/shard_map/ppermute | solution.py:285
  58.0 2.3 %collective-permute-start.22 = (bf16[96,768]{1,0:T(8,128)(2,1)S(1)}, bf16[96,768]{1,0:T(8,128)(2,1)S(1)}, u32[]{:S(2)}, u32[]{:S(2)}) collective-permute-start(bf16[96,768]{1,0:T(8,128)(2,1)S(1)} %add_convert_fusion.6), channel_id=1, source_target_pairs={{0,8},{4,12},{8,0},{12,4},{1,9},{5,13},{9,1},{13,5},{2,10},{6,14},... | collective-permute-start | bytes 442376 | tf_op jit(solution)/shard_map/ppermute | solution.py:285
  61.6 4.3 %collective-permute-done.17 = bf16[128,768]{1,0:T(8,128)(2,1)S(1)} collective-permute-done((bf16[128,768]{1,0:T(8,128)(2,1)S(1)}, bf16[128,768]{1,0:T(8,128)(2,1)S(1)}, u32[]{:S(2)}, u32[]{:S(2)}) %collective-permute-start.17) | collective-permute-done | bytes 196640 | tf_op jit(solution)/shard_map/ppermute | solution.py:285
  67.1 3.3 %collective-permute-start.23 = (bf16[96,768]{1,0:T(8,128)(2,1)S(1)}, bf16[96,768]{1,0:T(8,128)(2,1)S(1)}, u32[]{:S(2)}, u32[]{:S(2)}) collective-permute-start(bf16[96,768]{1,0:T(8,128)(2,1)S(1)} %add_convert_fusion.5.mine_ref), channel_id=1, source_target_pairs={{0,4},{4,0},{8,12},{12,8},{1,5},{5,1},{9,13},{13,9},{2,6},{6,2},{1... | collective-permute-start | bytes 442376 | tf_op jit(solution)/shard_map/ppermute | solution.py:285
  70.4 5.7 %collective-permute-done.20 = bf16[128,768]{1,0:T(8,128)(2,1)S(1)} collective-permute-done((bf16[128,768]{1,0:T(8,128)(2,1)S(1)}, bf16[128,768]{1,0:T(8,128)(2,1)S(1)}, u32[]{:S(2)}, u32[]{:S(2)}) %collective-permute-start.20) | collective-permute-done | bytes 196640 | tf_op jit(solution)/shard_map/ppermute | solution.py:285
  76.9 1.8 %grad_label_work.3 = bf16[1024,768]{1,0:T(8,128)(2,1)} custom-call(f32[512,128]{1,0:T(8,128)S(1)} %get-tuple-element.70.refs_0_, f32[512,128]{1,0:T(8,128)S(1)} %get-tuple-element.71.refs_1_, s32[512,128]{1,0:T(8,128)S(1)} %get-tuple-element.72.refs_2_, s32[512,128]{1,0:T(8,128)S(1)} %get-tuple-element.73.refs_3_, ...), custom_call_target="tpu_custom_call" | custom-call | flops 805306368 | bytes 4194304 | tf_op jit(solution)/shard_map/grad_label_work/pallas_call | solution.py:192
  (45 shorter events, 14.6 us)
Async XLA Ops:
  0.6 11.2 %collective-permute-start.3 = (bf16[1024,768]{1,0:T(8,128)(2,1)}, bf16[1024,768]{1,0:T(8,128)(2,1)S(1)}, u32[]{:S(2)}, u32[]{:S(2)}) collective-permute-start(bf16[1024,768]{1,0:T(8,128)(2,1)} %label_ref), channel_id=1, source_target_pairs={{0,1},{1,0},{2,3},{3,2},{4,5},{5,4},{6,7},{7,6},{8,9},{9,8},{10,11... | collective-permute-start | bytes 4718600 | tf_op jit(solution)/shard_map/ppermute | solution.py:285
  1.1 10.6 %collective-permute-start.5 = (bf16[192,768]{1,0:T(8,128)(2,1)}, bf16[192,768]{1,0:T(8,128)(2,1)S(1)}, u32[]{:S(2)}, u32[]{:S(2)}) collective-permute-start(bf16[192,768]{1,0:T(8,128)(2,1)} %shard_ref.1), channel_id=1, source_target_pairs={{0,2},{1,3},{2,0},{3,1},{4,6},{5,7},{6,4},{7,5},{8,10},{9,11},{10,... | collective-permute-start | bytes 884744 | tf_op jit(solution)/shard_map/ppermute | solution.py:285
  5.4 13.0 %collective-permute-start.1 = (bf16[136,768]{1,0:T(8,128)(2,1)}, bf16[136,768]{1,0:T(8,128)(2,1)S(1)}, u32[]{:S(2)}, u32[]{:S(2)}) collective-permute-start(bf16[136,768]{1,0:T(8,128)(2,1)} %own_block.1.refs_0_), channel_id=1, source_target_pairs={{0,8},{4,12},{8,0},{12,4},{1,9},{5,13},{9,1},{13,5},{2,10},{6,14},... | collective-permute-start | bytes 626696 | tf_op jit(solution)/shard_map/ppermute | solution.py:285
  8.0 10.3 %collective-permute-start.2 = (bf16[136,768]{1,0:T(8,128)(2,1)}, bf16[136,768]{1,0:T(8,128)(2,1)S(1)}, u32[]{:S(2)}, u32[]{:S(2)}) collective-permute-start(bf16[136,768]{1,0:T(8,128)(2,1)} %own_block.1.refs_0_), channel_id=1, source_target_pairs={{0,2},{1,3},{2,0},{3,1},{4,6},{5,7},{6,4},{7,5},{8,10},{9,11},{10,... | collective-permute-start | bytes 626696 | tf_op jit(solution)/shard_map/ppermute | solution.py:285
  8.6 10.2 %collective-permute-start = (bf16[136,768]{1,0:T(8,128)(2,1)}, bf16[136,768]{1,0:T(8,128)(2,1)S(1)}, u32[]{:S(2)}, u32[]{:S(2)}) collective-permute-start(bf16[136,768]{1,0:T(8,128)(2,1)} %own_block.1.refs_0_), channel_id=1, source_target_pairs={{0,4},{4,0},{8,12},{12,8},{1,5},{5,1},{9,13},{13,9},{2,6},{6,2},{1... | collective-permute-start | bytes 626696 | tf_op jit(solution)/shard_map/ppermute | solution.py:285
  11.8 8.7 %collective-permute-start.6 = (bf16[192,768]{1,0:T(8,128)(2,1)}, bf16[192,768]{1,0:T(8,128)(2,1)S(1)}, u32[]{:S(2)}, u32[]{:S(2)}) collective-permute-start(bf16[192,768]{1,0:T(8,128)(2,1)} %shard_ref.1), channel_id=1, source_target_pairs={{0,1},{1,0},{2,3},{3,2},{4,5},{5,4},{6,7},{7,6},{8,9},{9,8},{10,11... | collective-permute-start | bytes 884744 | tf_op jit(solution)/shard_map/ppermute | solution.py:285
  11.8 8.7 %collective-permute-start.7 = (bf16[192,768]{1,0:T(8,128)(2,1)S(1)}, bf16[192,768]{1,0:T(8,128)(2,1)S(1)}, u32[]{:S(2)}, u32[]{:S(2)}) collective-permute-start(bf16[192,768]{1,0:T(8,128)(2,1)S(1)} %collective-permute-done.5.refs_8_), channel_id=1, source_target_pairs={{0,1},{1,0},{2,3},{3,2},{4,5},{5,4},{6,7},{7,6},{8,9},{9,8},{10,11... | collective-permute-start | bytes 884744 | tf_op jit(solution)/shard_map/ppermute | solution.py:285
  18.8 5.9 %collective-permute-start.4 = (bf16[136,768]{1,0:T(8,128)(2,1)S(1)}, bf16[136,768]{1,0:T(8,128)(2,1)S(1)}, u32[]{:S(2)}, u32[]{:S(2)}) collective-permute-start(bf16[136,768]{1,0:T(8,128)(2,1)S(1)} %collective-permute-done.1.refs_2_), channel_id=1, source_target_pairs={{0,2},{1,3},{2,0},{3,1},{4,6},{5,7},{6,4},{7,5},{8,10},{9,11},{10,... | collective-permute-start | bytes 626696 | tf_op jit(solution)/shard_map/ppermute | solution.py:285
  20.2 7.2 %collective-permute-start.9 = (bf16[136,768]{1,0:T(8,128)(2,1)S(1)}, bf16[136,768]{1,0:T(8,128)(2,1)S(1)}, u32[]{:S(2)}, u32[]{:S(2)}) collective-permute-start(bf16[136,768]{1,0:T(8,128)(2,1)S(1)} %collective-permute-done.1.refs_2_), channel_id=1, source_target_pairs={{0,4},{4,0},{8,12},{12,8},{1,5},{5,1},{9,13},{13,9},{2,6},{6,2},{1... | collective-permute-start | bytes 626696 | tf_op jit(solution)/shard_map/ppermute | solution.py:285
  20.5 13.6 %collective-permute-start.8 = (bf16[136,768]{1,0:T(8,128)(2,1)S(1)}, bf16[136,768]{1,0:T(8,128)(2,1)S(1)}, u32[]{:S(2)}, u32[]{:S(2)}) collective-permute-start(bf16[136,768]{1,0:T(8,128)(2,1)S(1)} %collective-permute-done.2.refs_1_), channel_id=1, source_target_pairs={{0,4},{4,0},{8,12},{12,8},{1,5},{5,1},{9,13},{13,9},{2,6},{6,2},{1... | collective-permute-start | bytes 626696 | tf_op jit(solution)/shard_map/ppermute | solution.py:285
  27.5 6.6 %collective-permute-start.10 = (bf16[136,768]{1,0:T(8,128)(2,1)S(1)}, bf16[136,768]{1,0:T(8,128)(2,1)S(1)}, u32[]{:S(2)}, u32[]{:S(2)}) collective-permute-start(bf16[136,768]{1,0:T(8,128)(2,1)S(1)} %collective-permute-done.9.refs_2_), channel_id=1, source_target_pairs={{0,2},{1,3},{2,0},{3,1},{4,6},{5,7},{6,4},{7,5},{8,10},{9,11},{10,... | collective-permute-start | bytes 626696 | tf_op jit(solution)/shard_map/ppermute | solution.py:285
  39.7 2.9 %collective-permute-start.11 = (bf16[2,192,768]{2,1,0:T(8,128)(2,1)S(1)}, bf16[2,192,768]{2,1,0:T(8,128)(2,1)S(1)}, u32[]{:S(2)}, u32[]{:S(2)}) collective-permute-start(bf16[2,192,768]{2,1,0:T(8,128)(2,1)S(1)} %get-tuple-element.55), channel_id=1, source_target_pairs={{0,1},{1,0},{2,3},{3,2},{4,5},{5,4},{6,7},{7,6},{8,9},{9,8},{10,11... | collective-permute-start | bytes 1769480 | tf_op jit(solution)/shard_map/ppermute | solution.py:285
  39.8 7.8 %collective-permute-start.13 = (bf16[128,768]{1,0:T(8,128)(2,1)S(1)}, bf16[128,768]{1,0:T(8,128)(2,1)S(1)}, u32[]{:S(2)}, u32[]{:S(2)}) collective-permute-start(bf16[128,768]{1,0:T(8,128)(2,1)S(1)} %get-tuple-element.58), channel_id=1, source_target_pairs={{0,4},{4,0},{8,12},{12,8},{1,5},{5,1},{9,13},{13,9},{2,6},{6,2},{1... | collective-permute-start | bytes 589832 | tf_op jit(solution)/shard_map/ppermute | solution.py:285
  42.4 34.5 %collective-permute-start.21 = (bf16[1024,768]{1,0:T(8,128)(2,1)S(1)}, bf16[1024,768]{1,0:T(8,128)(2,1)S(1)}, u32[]{:S(2)}, u32[]{:S(2)}) collective-permute-start(bf16[1024,768]{1,0:T(8,128)(2,1)S(1)} %grad_label_work.2), channel_id=1, source_target_pairs={{0,1},{1,0},{2,3},{3,2},{4,5},{5,4},{6,7},{7,6},{8,9},{9,8},{10,11... | collective-permute-start | bytes 4718600 | tf_op jit(solution)/shard_map/ppermute | solution.py:285
  42.7 9.9 %collective-permute-start.14 = (bf16[192,768]{1,0:T(8,128)(2,1)S(1)}, bf16[192,768]{1,0:T(8,128)(2,1)S(1)}, u32[]{:S(2)}, u32[]{:S(2)}) collective-permute-start(bf16[192,768]{1,0:T(8,128)(2,1)S(1)} %fusion), channel_id=1, source_target_pairs={{0,2},{1,3},{2,0},{3,1},{4,6},{5,7},{6,4},{7,5},{8,10},{9,11},{10,... | collective-permute-start | bytes 884744 | tf_op jit(solution)/shard_map/ppermute | solution.py:285
  43.3 8.1 %collective-permute-start.12 = (bf16[128,768]{1,0:T(8,128)(2,1)S(1)}, bf16[128,768]{1,0:T(8,128)(2,1)S(1)}, u32[]{:S(2)}, u32[]{:S(2)}) collective-permute-start(bf16[128,768]{1,0:T(8,128)(2,1)S(1)} %get-tuple-element.57), channel_id=1, source_target_pairs={{0,4},{4,0},{8,12},{12,8},{1,5},{5,1},{9,13},{13,9},{2,6},{6,2},{1... | collective-permute-start | bytes 589832 | tf_op jit(solution)/shard_map/ppermute | solution.py:285
  44.2 12.6 %collective-permute-start.16 = (bf16[128,768]{1,0:T(8,128)(2,1)S(1)}, bf16[128,768]{1,0:T(8,128)(2,1)S(1)}, u32[]{:S(2)}, u32[]{:S(2)}) collective-permute-start(bf16[128,768]{1,0:T(8,128)(2,1)S(1)} %get-tuple-element.64), channel_id=1, source_target_pairs={{0,2},{1,3},{2,0},{3,1},{4,6},{5,7},{6,4},{7,5},{8,10},{9,11},{10,... | collective-permute-start | bytes 589832 | tf_op jit(solution)/shard_map/ppermute | solution.py:285
  47.6 12.8 %collective-permute-start.18 = (bf16[128,768]{1,0:T(8,128)(2,1)S(1)}, bf16[128,768]{1,0:T(8,128)(2,1)S(1)}, u32[]{:S(2)}, u32[]{:S(2)}) collective-permute-start(bf16[128,768]{1,0:T(8,128)(2,1)S(1)} %add_convert_fusion.3), channel_id=1, source_target_pairs={{0,2},{1,3},{2,0},{3,1},{4,6},{5,7},{6,4},{7,5},{8,10},{9,11},{10,... | collective-permute-start | bytes 589832 | tf_op jit(solution)/shard_map/ppermute | solution.py:285
  52.8 5.2 %collective-permute-start.19 = (bf16[96,768]{1,0:T(8,128)(2,1)S(1)}, bf16[96,768]{1,0:T(8,128)(2,1)S(1)}, u32[]{:S(2)}, u32[]{:S(2)}) collective-permute-start(bf16[96,768]{1,0:T(8,128)(2,1)S(1)} %get-tuple-element.68), channel_id=1, source_target_pairs={{0,4},{4,0},{8,12},{12,8},{1,5},{5,1},{9,13},{13,9},{2,6},{6,2},{1... | collective-permute-start | bytes 442376 | tf_op jit(solution)/shard_map/ppermute | solution.py:285
  56.9 9.0 %collective-permute-start.17 = (bf16[128,768]{1,0:T(8,128)(2,1)S(1)}, bf16[128,768]{1,0:T(8,128)(2,1)S(1)}, u32[]{:S(2)}, u32[]{:S(2)}) collective-permute-start(bf16[128,768]{1,0:T(8,128)(2,1)S(1)} %add_convert_fusion.4), channel_id=1, source_target_pairs={{0,4},{4,0},{8,12},{12,8},{1,5},{5,1},{9,13},{13,9},{2,6},{6,2},{1... | collective-permute-start | bytes 589832 | tf_op jit(solution)/shard_map/ppermute | solution.py:285
  58.0 9.0 %collective-permute-start.22 = (bf16[96,768]{1,0:T(8,128)(2,1)S(1)}, bf16[96,768]{1,0:T(8,128)(2,1)S(1)}, u32[]{:S(2)}, u32[]{:S(2)}) collective-permute-start(bf16[96,768]{1,0:T(8,128)(2,1)S(1)} %add_convert_fusion.6), channel_id=1, source_target_pairs={{0,8},{4,12},{8,0},{12,4},{1,9},{5,13},{9,1},{13,5},{2,10},{6,14},... | collective-permute-start | bytes 442376 | tf_op jit(solution)/shard_map/ppermute | solution.py:285
  60.5 9.9 %collective-permute-start.15 = (bf16[128,768]{1,0:T(8,128)(2,1)S(1)}, bf16[128,768]{1,0:T(8,128)(2,1)S(1)}, u32[]{:S(2)}, u32[]{:S(2)}) collective-permute-start(bf16[128,768]{1,0:T(8,128)(2,1)S(1)} %get-tuple-element.61), channel_id=1, source_target_pairs={{0,2},{1,3},{2,0},{3,1},{4,6},{5,7},{6,4},{7,5},{8,10},{9,11},{10,... | collective-permute-start | bytes 589832 | tf_op jit(solution)/shard_map/ppermute | solution.py:285
  65.9 10.2 %collective-permute-start.20 = (bf16[128,768]{1,0:T(8,128)(2,1)S(1)}, bf16[128,768]{1,0:T(8,128)(2,1)S(1)}, u32[]{:S(2)}, u32[]{:S(2)}) collective-permute-start(bf16[128,768]{1,0:T(8,128)(2,1)S(1)} %add_convert_fusion.2), channel_id=1, source_target_pairs={{0,8},{4,12},{8,0},{12,4},{1,9},{5,13},{9,1},{13,5},{2,10},{6,14},... | collective-permute-start | bytes 589832 | tf_op jit(solution)/shard_map/ppermute | solution.py:285
  67.1 11.6 %collective-permute-start.23 = (bf16[96,768]{1,0:T(8,128)(2,1)S(1)}, bf16[96,768]{1,0:T(8,128)(2,1)S(1)}, u32[]{:S(2)}, u32[]{:S(2)}) collective-permute-start(bf16[96,768]{1,0:T(8,128)(2,1)S(1)} %add_convert_fusion.5.mine_ref), channel_id=1, source_target_pairs={{0,4},{4,0},{8,12},{12,8},{1,5},{5,1},{9,13},{13,9},{2,6},{6,2},{1... | collective-permute-start | bytes 442376 | tf_op jit(solution)/shard_map/ppermute | solution.py:285
  (3 other events, 16.4 us)

commit v16 on v15

--- a/solution.py
+++ b/solution.py
@@ -450,8 +450,8 @@
         terms = reduce_runs(backs, got_last, sent, keep, first)
         other = partner(grad_label_work(works, 2, 1, label_weight.shape), "dp", 1)
         grad_label = grad_label_work(works, 2, 0, label_weight.shape, other)
-        grad_feats = add(*terms).astype(BF16)
-        grad_enc = join_halves(share, grad_label, grad_feats)
+        grad_enc = join_halves(share, grad_label)
+        grad_feats = add(after(terms[0], grad_enc), *terms[1:]).astype(BF16)
     else:
         shards = gather_near(gather_far(enc_weight))
         flat = owners.reshape(-1)

time: 79.8 us -> 79.3 us (level)
  local copies, waits for them, and re-layouts: 2.37 us -> 3.52 us
  starting transfers between devices: 27.6 us -> 26.8 us
  waiting for transfers between devices: 31 us -> 30.2 us
    unnamed x6 -> x10, local copies, waits for them, and re-layouts: 2.37 us -> 3.52 us
    ppermute x24, starting transfers between devices: 27.6 us -> 26.8 us  [partner(): lax.ppermute(x, axis, [(i, i ^ mask) for i in range(lax.axis_size(axis))])]
  transfers between devices with their start and end apart: 24 -> 24, of which waited for: 13 -> 13; matrix products, arithmetic and copies ran while one was open for 1% -> 0% of each run, Pallas kernels for 13% -> 14%
where the time goes in v16:
time: 79.3 us; the launch traced here: 79.1 us
  waiting for transfers between devices  30.2 us (38%)
  starting transfers between devices  26.8 us (34%)
  Pallas kernels  16.7 us (21%)
  local copies, waits for them, and re-layouts  3.52 us (4%)
  other arithmetic  1.08 us (1%)
    ppermute x24, waiting for transfers between devices, partner(): lax.ppermute(x, axis, [(i, i ^ mask) for i in range(lax.axis_size(axis))])  30.2 us
    ppermute x24, starting transfers between devices, partner(): lax.ppermute(x, axis, [(i, i ^ mask) for i in range(lax.axis_size(axis))])  26.8 us
    pallas_call x8, Pallas kernels, call(): pl.pallas_call(kernel, in_specs=[space] * len(args), out_specs=jax.tree.m...  16.7 us
    unnamed x10, local copies, waits for them, and re-layouts  3.52 us
  transfers between devices with their start and end apart: 24, of which 13 were waited for; matrix products, arithmetic and copies ran while one was open for 0% of the time, Pallas kernels for 14%

profile of v16, /device:TPU:0, one launch (start us, length us, event | category | flops | bytes accessed | tf_op | source)
XLA Modules:
  0.0 79.1 jit_solution(10645880370533286829)
XLA Ops:
  1.1 2.6 %collective-permute-start.5 = (bf16[192,768]{1,0:T(8,128)(2,1)}, bf16[192,768]{1,0:T(8,128)(2,1)S(1)}, u32[]{:S(2)}, u32[]{:S(2)}) collective-permute-start(bf16[192,768]{1,0:T(8,128)(2,1)} %shard_ref.1), channel_id=1, source_target_pairs={{0,2},{1,3},{2,0},{3,1},{4,6},{5,7},{6,4},{7,5},{8,10},{9,11},{10,... | collective-permute-start | bytes 884744 | tf_op jit(solution)/shard_map/ppermute | solution.py:285
  3.7 1.6 %own_block.1.refs_0_ = bf16[136,768]{1,0:T(8,128)(2,1)} custom-call(bf16[128,768]{1,0:T(8,128)(2,1)} %feats_ref.1, s32[4,128]{1,0:T(4,128)} %bitcast.5, s32[4,128]{1,0:T(4,128)} %bitcast.6, s32[4,128]{1,0:T(4,128)} %bitcast.7), custom_call_target="tpu_custom_call" | custom-call | bytes 1048576 | tf_op jit(solution)/shard_map/own_block/pallas_call | solution.py:192
  5.4 2.7 %collective-permute-start.1 = (bf16[136,768]{1,0:T(8,128)(2,1)}, bf16[136,768]{1,0:T(8,128)(2,1)S(1)}, u32[]{:S(2)}, u32[]{:S(2)}) collective-permute-start(bf16[136,768]{1,0:T(8,128)(2,1)} %own_block.1.refs_0_), channel_id=1, source_target_pairs={{0,8},{4,12},{8,0},{12,4},{1,9},{5,13},{9,1},{13,5},{2,10},{6,14},... | collective-permute-start | bytes 626696 | tf_op jit(solution)/shard_map/ppermute | solution.py:285
  8.6 1.6 %collective-permute-start = (bf16[136,768]{1,0:T(8,128)(2,1)}, bf16[136,768]{1,0:T(8,128)(2,1)S(1)}, u32[]{:S(2)}, u32[]{:S(2)}) collective-permute-start(bf16[136,768]{1,0:T(8,128)(2,1)} %own_block.1.refs_0_), channel_id=1, source_target_pairs={{0,4},{4,0},{8,12},{12,8},{1,5},{5,1},{9,13},{13,9},{2,6},{6,2},{1... | collective-permute-start | bytes 626696 | tf_op jit(solution)/shard_map/ppermute | solution.py:285
  10.1 1.7 %collective-permute-done.5.refs_8_ = bf16[192,768]{1,0:T(8,128)(2,1)S(1)} collective-permute-done((bf16[192,768]{1,0:T(8,128)(2,1)}, bf16[192,768]{1,0:T(8,128)(2,1)S(1)}, u32[]{:S(2)}, u32[]{:S(2)}) %collective-permute-start.5) | collective-permute-done | bytes 294944 | tf_op jit(solution)/shard_map/ppermute | solution.py:285
  13.4 1.4 %copy-done = bf16[1024,768]{1,0:T(8,128)(2,1)S(1)} copy-done((bf16[1024,768]{1,0:T(8,128)(2,1)S(1)}, bf16[1024,768]{1,0:T(8,128)(2,1)}, u32[]{:S(2)}) %copy-start) | copy-done | bytes 1572888
  15.9 2.4 %collective-permute-done.1.refs_2_ = bf16[136,768]{1,0:T(8,128)(2,1)S(1)} collective-permute-done((bf16[136,768]{1,0:T(8,128)(2,1)}, bf16[136,768]{1,0:T(8,128)(2,1)S(1)}, u32[]{:S(2)}, u32[]{:S(2)}) %collective-permute-start.1) | collective-permute-done | bytes 208928 | tf_op jit(solution)/shard_map/ppermute | solution.py:285
  18.8 1.4 %collective-permute-start.4 = (bf16[136,768]{1,0:T(8,128)(2,1)S(1)}, bf16[136,768]{1,0:T(8,128)(2,1)S(1)}, u32[]{:S(2)}, u32[]{:S(2)}) collective-permute-start(bf16[136,768]{1,0:T(8,128)(2,1)S(1)} %collective-permute-done.1.refs_2_), channel_id=1, source_target_pairs={{0,2},{1,3},{2,0},{3,1},{4,6},{5,7},{6,4},{7,5},{8,10},{9,11},{10,... | collective-permute-start | bytes 626696 | tf_op jit(solution)/shard_map/ppermute | solution.py:285
  20.5 1.8 %collective-permute-start.8 = (bf16[136,768]{1,0:T(8,128)(2,1)S(1)}, bf16[136,768]{1,0:T(8,128)(2,1)S(1)}, u32[]{:S(2)}, u32[]{:S(2)}) collective-permute-start(bf16[136,768]{1,0:T(8,128)(2,1)S(1)} %collective-permute-done.2.refs_1_), channel_id=1, source_target_pairs={{0,4},{4,0},{8,12},{12,8},{1,5},{5,1},{9,13},{13,9},{2,6},{6,2},{1... | collective-permute-start | bytes 626696 | tf_op jit(solution)/shard_map/ppermute | solution.py:285
  22.3 2.4 %collective-permute-done.4.refs_3_ = bf16[136,768]{1,0:T(8,128)(2,1)S(1)} collective-permute-done((bf16[136,768]{1,0:T(8,128)(2,1)S(1)}, bf16[136,768]{1,0:T(8,128)(2,1)S(1)}, u32[]{:S(2)}, u32[]{:S(2)}) %collective-permute-start.4) | collective-permute-done | bytes 208928 | tf_op jit(solution)/shard_map/ppermute | solution.py:285
  24.7 2.8 %collective-permute-done.9.refs_2_ = bf16[136,768]{1,0:T(8,128)(2,1)S(1)} collective-permute-done((bf16[136,768]{1,0:T(8,128)(2,1)S(1)}, bf16[136,768]{1,0:T(8,128)(2,1)S(1)}, u32[]{:S(2)}, u32[]{:S(2)}) %collective-permute-start.9) | collective-permute-done | bytes 208928 | tf_op jit(solution)/shard_map/ppermute | solution.py:285
  28.7 5.4 %pair_work.2 = (bf16[128,768]{1,0:T(8,128)(2,1)S(1)}, bf16[128,768]{1,0:T(8,128)(2,1)S(1)}, bf16[128,768]{1,0:T(8,128)(2,1)S(1)}, bf16[128,768]{1,0:T(8,128)(2,1...) custom-call(bf16[136,768]{1,0:T(8,128)(2,1)S(1)} %copy-done.2, ...), custom_call_target="tpu_custom_call" | custom-call | flops 3623878656 | bytes 8388608 | tf_op jit(solution)/shard_map/pair_work/pallas_call | solution.py:192
  34.1 5.6 %pair_work.3 = (bf16[128,768]{1,0:T(8,128)(2,1)S(1)}, bf16[128,768]{1,0:T(8,128)(2,1)S(1)}, bf16[128,768]{1,0:T(8,128)(2,1)S(1)}, bf16[128,768]{1,0:T(8,128)(2,1...) custom-call(bf16[136,768]{1,0:T(8,128)(2,1)S(1)} %collective-permute, ...), custom_call_target="tpu_custom_call" | custom-call | flops 3623878656 | bytes 8388608 | tf_op jit(solution)/shard_map/pair_work/pallas_call | solution.py:192
  41.5 1.4 %collective-permute-start.13 = (bf16[128,768]{1,0:T(8,128)(2,1)S(1)}, bf16[128,768]{1,0:T(8,128)(2,1)S(1)}, u32[]{:S(2)}, u32[]{:S(2)}) collective-permute-start(bf16[128,768]{1,0:T(8,128)(2,1)S(1)} %get-tuple-element.58), channel_id=1, source_target_pairs={{0,4},{4,0},{8,12},{12,8},{1,5},{5,1},{9,13},{13,9},{2,6},{6,2},{1... | collective-permute-start | bytes 589832 | tf_op jit(solution)/shard_map/ppermute | solution.py:285
  45.7 3.6 %collective-permute-done.13 = bf16[128,768]{1,0:T(8,128)(2,1)S(1)} collective-permute-done((bf16[128,768]{1,0:T(8,128)(2,1)S(1)}, bf16[128,768]{1,0:T(8,128)(2,1)S(1)}, u32[]{:S(2)}, u32[]{:S(2)}) %collective-permute-start.13) | collective-permute-done | bytes 196640 | tf_op jit(solution)/shard_map/ppermute | solution.py:285
  50.1 2.4 %collective-permute-done.12 = bf16[128,768]{1,0:T(8,128)(2,1)S(1)} collective-permute-done((bf16[128,768]{1,0:T(8,128)(2,1)S(1)}, bf16[128,768]{1,0:T(8,128)(2,1)S(1)}, u32[]{:S(2)}, u32[]{:S(2)}) %collective-permute-start.12) | collective-permute-done | bytes 196640 | tf_op jit(solution)/shard_map/ppermute | solution.py:285
  54.3 2.9 %collective-permute-done.20 = bf16[128,768]{1,0:T(8,128)(2,1)S(1)} collective-permute-done((bf16[128,768]{1,0:T(8,128)(2,1)S(1)}, bf16[128,768]{1,0:T(8,128)(2,1)S(1)}, u32[]{:S(2)}, u32[]{:S(2)}) %collective-permute-start.20) | collective-permute-done | bytes 196640 | tf_op jit(solution)/shard_map/ppermute | solution.py:285
  57.9 1.3 %collective-permute-done.15 = bf16[96,768]{1,0:T(8,128)(2,1)S(1)} collective-permute-done((bf16[96,768]{1,0:T(8,128)(2,1)S(1)}, bf16[96,768]{1,0:T(8,128)(2,1)S(1)}, u32[]{:S(2)}, u32[]{:S(2)}) %collective-permute-start.15) | collective-permute-done | bytes 147488 | tf_op jit(solution)/shard_map/ppermute | solution.py:285
  59.2 2.4 %collective-permute-start.16 = (bf16[96,768]{1,0:T(8,128)(2,1)S(1)}, bf16[96,768]{1,0:T(8,128)(2,1)S(1)}, u32[]{:S(2)}, u32[]{:S(2)}) collective-permute-start(bf16[96,768]{1,0:T(8,128)(2,1)S(1)} %add_convert_fusion.6), channel_id=1, source_target_pairs={{0,8},{4,12},{8,0},{12,4},{1,9},{5,13},{9,1},{13,5},{2,10},{6,14},... | collective-permute-start | bytes 442376 | tf_op jit(solution)/shard_map/ppermute | solution.py:285
  62.7 1.9 %collective-permute-done.21 = bf16[128,768]{1,0:T(8,128)(2,1)S(1)} collective-permute-done((bf16[128,768]{1,0:T(8,128)(2,1)S(1)}, bf16[128,768]{1,0:T(8,128)(2,1)S(1)}, u32[]{:S(2)}, u32[]{:S(2)}) %collective-permute-start.21) | collective-permute-done | bytes 196640 | tf_op jit(solution)/shard_map/ppermute | solution.py:285
  64.6 2.4 %collective-permute-start.23 = (bf16[128,768]{1,0:T(8,128)(2,1)S(1)}, bf16[128,768]{1,0:T(8,128)(2,1)S(1)}, u32[]{:S(2)}, u32[]{:S(2)}) collective-permute-start(bf16[128,768]{1,0:T(8,128)(2,1)S(1)} %add_convert_fusion.2), channel_id=1, source_target_pairs={{0,8},{4,12},{8,0},{12,4},{1,9},{5,13},{9,1},{13,5},{2,10},{6,14},... | collective-permute-start | bytes 589832 | tf_op jit(solution)/shard_map/ppermute | solution.py:285
  67.0 2.8 %collective-permute-done.16 = bf16[96,768]{1,0:T(8,128)(2,1)S(1)} collective-permute-done((bf16[96,768]{1,0:T(8,128)(2,1)S(1)}, bf16[96,768]{1,0:T(8,128)(2,1)S(1)}, u32[]{:S(2)}, u32[]{:S(2)}) %collective-permute-start.16) | collective-permute-done | bytes 147488 | tf_op jit(solution)/shard_map/ppermute | solution.py:285
  70.3 1.8 %grad_label_work.3 = bf16[1024,768]{1,0:T(8,128)(2,1)} custom-call(f32[512,128]{1,0:T(8,128)S(1)} %get-tuple-element.62.refs_0_, f32[512,128]{1,0:T(8,128)S(1)} %get-tuple-element.63.refs_1_, s32[512,128]{1,0:T(8,128)S(1)} %get-tuple-element.64.refs_2_, s32[512,128]{1,0:T(8,128)S(1)} %get-tuple-element.65.refs_3_, ...), custom_call_target="tpu_custom_call" | custom-call | flops 805306368 | bytes 4194304 | tf_op jit(solution)/shard_map/grad_label_work/pallas_call | solution.py:192
  72.2 5.3 %collective-permute-done.18.other_ref = bf16[96,768]{1,0:T(8,128)(2,1)S(1)} collective-permute-done((bf16[96,768]{1,0:T(8,128)(2,1)S(1)}, bf16[96,768]{1,0:T(8,128)(2,1)S(1)}, u32[]{:S(2)}, u32[]{:S(2)}) %collective-permute-start.18) | collective-permute-done | bytes 147488 | tf_op jit(solution)/shard_map/ppermute | solution.py:285
  (49 shorter events, 16.9 us)
Async XLA Ops:
  0.6 11.2 %collective-permute-start.3 = (bf16[1024,768]{1,0:T(8,128)(2,1)}, bf16[1024,768]{1,0:T(8,128)(2,1)S(1)}, u32[]{:S(2)}, u32[]{:S(2)}) collective-permute-start(bf16[1024,768]{1,0:T(8,128)(2,1)} %label_ref), channel_id=1, source_target_pairs={{0,1},{1,0},{2,3},{3,2},{4,5},{5,4},{6,7},{7,6},{8,9},{9,8},{10,11... | collective-permute-start | bytes 4718600 | tf_op jit(solution)/shard_map/ppermute | solution.py:285
  1.1 10.6 %collective-permute-start.5 = (bf16[192,768]{1,0:T(8,128)(2,1)}, bf16[192,768]{1,0:T(8,128)(2,1)S(1)}, u32[]{:S(2)}, u32[]{:S(2)}) collective-permute-start(bf16[192,768]{1,0:T(8,128)(2,1)} %shard_ref.1), channel_id=1, source_target_pairs={{0,2},{1,3},{2,0},{3,1},{4,6},{5,7},{6,4},{7,5},{8,10},{9,11},{10,... | collective-permute-start | bytes 884744 | tf_op jit(solution)/shard_map/ppermute | solution.py:285
  5.4 13.0 %collective-permute-start.1 = (bf16[136,768]{1,0:T(8,128)(2,1)}, bf16[136,768]{1,0:T(8,128)(2,1)S(1)}, u32[]{:S(2)}, u32[]{:S(2)}) collective-permute-start(bf16[136,768]{1,0:T(8,128)(2,1)} %own_block.1.refs_0_), channel_id=1, source_target_pairs={{0,8},{4,12},{8,0},{12,4},{1,9},{5,13},{9,1},{13,5},{2,10},{6,14},... | collective-permute-start | bytes 626696 | tf_op jit(solution)/shard_map/ppermute | solution.py:285
  8.0 10.3 %collective-permute-start.2 = (bf16[136,768]{1,0:T(8,128)(2,1)}, bf16[136,768]{1,0:T(8,128)(2,1)S(1)}, u32[]{:S(2)}, u32[]{:S(2)}) collective-permute-start(bf16[136,768]{1,0:T(8,128)(2,1)} %own_block.1.refs_0_), channel_id=1, source_target_pairs={{0,2},{1,3},{2,0},{3,1},{4,6},{5,7},{6,4},{7,5},{8,10},{9,11},{10,... | collective-permute-start | bytes 626696 | tf_op jit(solution)/shard_map/ppermute | solution.py:285
  8.6 10.2 %collective-permute-start = (bf16[136,768]{1,0:T(8,128)(2,1)}, bf16[136,768]{1,0:T(8,128)(2,1)S(1)}, u32[]{:S(2)}, u32[]{:S(2)}) collective-permute-start(bf16[136,768]{1,0:T(8,128)(2,1)} %own_block.1.refs_0_), channel_id=1, source_target_pairs={{0,4},{4,0},{8,12},{12,8},{1,5},{5,1},{9,13},{13,9},{2,6},{6,2},{1... | collective-permute-start | bytes 626696 | tf_op jit(solution)/shard_map/ppermute | solution.py:285
  11.8 8.7 %collective-permute-start.6 = (bf16[192,768]{1,0:T(8,128)(2,1)}, bf16[192,768]{1,0:T(8,128)(2,1)S(1)}, u32[]{:S(2)}, u32[]{:S(2)}) collective-permute-start(bf16[192,768]{1,0:T(8,128)(2,1)} %shard_ref.1), channel_id=1, source_target_pairs={{0,1},{1,0},{2,3},{3,2},{4,5},{5,4},{6,7},{7,6},{8,9},{9,8},{10,11... | collective-permute-start | bytes 884744 | tf_op jit(solution)/shard_map/ppermute | solution.py:285
  12.9 7.6 %collective-permute-start.7 = (bf16[192,768]{1,0:T(8,128)(2,1)S(1)}, bf16[192,768]{1,0:T(8,128)(2,1)S(1)}, u32[]{:S(2)}, u32[]{:S(2)}) collective-permute-start(bf16[192,768]{1,0:T(8,128)(2,1)S(1)} %collective-permute-done.5.refs_8_), channel_id=1, source_target_pairs={{0,1},{1,0},{2,3},{3,2},{4,5},{5,4},{6,7},{7,6},{8,9},{9,8},{10,11... | collective-permute-start | bytes 884744 | tf_op jit(solution)/shard_map/ppermute | solution.py:285
  18.8 5.9 %collective-permute-start.4 = (bf16[136,768]{1,0:T(8,128)(2,1)S(1)}, bf16[136,768]{1,0:T(8,128)(2,1)S(1)}, u32[]{:S(2)}, u32[]{:S(2)}) collective-permute-start(bf16[136,768]{1,0:T(8,128)(2,1)S(1)} %collective-permute-done.1.refs_2_), channel_id=1, source_target_pairs={{0,2},{1,3},{2,0},{3,1},{4,6},{5,7},{6,4},{7,5},{8,10},{9,11},{10,... | collective-permute-start | bytes 626696 | tf_op jit(solution)/shard_map/ppermute | solution.py:285
  20.2 7.2 %collective-permute-start.9 = (bf16[136,768]{1,0:T(8,128)(2,1)S(1)}, bf16[136,768]{1,0:T(8,128)(2,1)S(1)}, u32[]{:S(2)}, u32[]{:S(2)}) collective-permute-start(bf16[136,768]{1,0:T(8,128)(2,1)S(1)} %collective-permute-done.1.refs_2_), channel_id=1, source_target_pairs={{0,4},{4,0},{8,12},{12,8},{1,5},{5,1},{9,13},{13,9},{2,6},{6,2},{1... | collective-permute-start | bytes 626696 | tf_op jit(solution)/shard_map/ppermute | solution.py:285
  20.5 13.6 %collective-permute-start.8 = (bf16[136,768]{1,0:T(8,128)(2,1)S(1)}, bf16[136,768]{1,0:T(8,128)(2,1)S(1)}, u32[]{:S(2)}, u32[]{:S(2)}) collective-permute-start(bf16[136,768]{1,0:T(8,128)(2,1)S(1)} %collective-permute-done.2.refs_1_), channel_id=1, source_target_pairs={{0,4},{4,0},{8,12},{12,8},{1,5},{5,1},{9,13},{13,9},{2,6},{6,2},{1... | collective-permute-start | bytes 626696 | tf_op jit(solution)/shard_map/ppermute | solution.py:285
  27.5 6.6 %collective-permute-start.10 = (bf16[136,768]{1,0:T(8,128)(2,1)S(1)}, bf16[136,768]{1,0:T(8,128)(2,1)S(1)}, u32[]{:S(2)}, u32[]{:S(2)}) collective-permute-start(bf16[136,768]{1,0:T(8,128)(2,1)S(1)} %collective-permute-done.9.refs_2_), channel_id=1, source_target_pairs={{0,2},{1,3},{2,0},{3,1},{4,6},{5,7},{6,4},{7,5},{8,10},{9,11},{10,... | collective-permute-start | bytes 626696 | tf_op jit(solution)/shard_map/ppermute | solution.py:285
  39.7 3.1 %collective-permute-start.11 = (bf16[2,192,768]{2,1,0:T(8,128)(2,1)S(1)}, bf16[2,192,768]{2,1,0:T(8,128)(2,1)S(1)}, u32[]{:S(2)}, u32[]{:S(2)}) collective-permute-start(bf16[2,192,768]{2,1,0:T(8,128)(2,1)S(1)} %get-tuple-element.55), channel_id=1, source_target_pairs={{0,1},{1,0},{2,3},{3,2},{4,5},{5,4},{6,7},{7,6},{8,9},{9,8},{10,11... | collective-permute-start | bytes 1769480 | tf_op jit(solution)/shard_map/ppermute | solution.py:285
  40.9 29.4 %collective-permute-start.17 = (bf16[1024,768]{1,0:T(8,128)(2,1)S(1)}, bf16[1024,768]{1,0:T(8,128)(2,1)S(1)}, u32[]{:S(2)}, u32[]{:S(2)}) collective-permute-start(bf16[1024,768]{1,0:T(8,128)(2,1)S(1)} %grad_label_work.2), channel_id=1, source_target_pairs={{0,1},{1,0},{2,3},{3,2},{4,5},{5,4},{6,7},{7,6},{8,9},{9,8},{10,11... | collective-permute-start | bytes 4718600 | tf_op jit(solution)/shard_map/ppermute | solution.py:285
  41.5 7.8 %collective-permute-start.13 = (bf16[128,768]{1,0:T(8,128)(2,1)S(1)}, bf16[128,768]{1,0:T(8,128)(2,1)S(1)}, u32[]{:S(2)}, u32[]{:S(2)}) collective-permute-start(bf16[128,768]{1,0:T(8,128)(2,1)S(1)} %get-tuple-element.58), channel_id=1, source_target_pairs={{0,4},{4,0},{8,12},{12,8},{1,5},{5,1},{9,13},{13,9},{2,6},{6,2},{1... | collective-permute-start | bytes 589832 | tf_op jit(solution)/shard_map/ppermute | solution.py:285
  43.0 10.0 %collective-permute-start.14 = (bf16[192,768]{1,0:T(8,128)(2,1)S(1)}, bf16[192,768]{1,0:T(8,128)(2,1)S(1)}, u32[]{:S(2)}, u32[]{:S(2)}) collective-permute-start(bf16[192,768]{1,0:T(8,128)(2,1)S(1)} %fusion), channel_id=1, source_target_pairs={{0,2},{1,3},{2,0},{3,1},{4,6},{5,7},{6,4},{7,5},{8,10},{9,11},{10,... | collective-permute-start | bytes 884744 | tf_op jit(solution)/shard_map/ppermute | solution.py:285
  43.5 9.0 %collective-permute-start.12 = (bf16[128,768]{1,0:T(8,128)(2,1)S(1)}, bf16[128,768]{1,0:T(8,128)(2,1)S(1)}, u32[]{:S(2)}, u32[]{:S(2)}) collective-permute-start(bf16[128,768]{1,0:T(8,128)(2,1)S(1)} %get-tuple-element.57), channel_id=1, source_target_pairs={{0,4},{4,0},{8,12},{12,8},{1,5},{5,1},{9,13},{13,9},{2,6},{6,2},{1... | collective-permute-start | bytes 589832 | tf_op jit(solution)/shard_map/ppermute | solution.py:285
  44.4 12.7 %collective-permute-start.20 = (bf16[128,768]{1,0:T(8,128)(2,1)S(1)}, bf16[128,768]{1,0:T(8,128)(2,1)S(1)}, u32[]{:S(2)}, u32[]{:S(2)}) collective-permute-start(bf16[128,768]{1,0:T(8,128)(2,1)S(1)} %get-tuple-element.74), channel_id=1, source_target_pairs={{0,2},{1,3},{2,0},{3,1},{4,6},{5,7},{6,4},{7,5},{8,10},{9,11},{10,... | collective-permute-start | bytes 589832 | tf_op jit(solution)/shard_map/ppermute | solution.py:285
  49.3 12.2 %collective-permute-start.22 = (bf16[128,768]{1,0:T(8,128)(2,1)S(1)}, bf16[128,768]{1,0:T(8,128)(2,1)S(1)}, u32[]{:S(2)}, u32[]{:S(2)}) collective-permute-start(bf16[128,768]{1,0:T(8,128)(2,1)S(1)} %add_convert_fusion.3), channel_id=1, source_target_pairs={{0,2},{1,3},{2,0},{3,1},{4,6},{5,7},{6,4},{7,5},{8,10},{9,11},{10,... | collective-permute-start | bytes 589832 | tf_op jit(solution)/shard_map/ppermute | solution.py:285
  53.1 6.0 %collective-permute-start.15 = (bf16[96,768]{1,0:T(8,128)(2,1)S(1)}, bf16[96,768]{1,0:T(8,128)(2,1)S(1)}, u32[]{:S(2)}, u32[]{:S(2)}) collective-permute-start(bf16[96,768]{1,0:T(8,128)(2,1)S(1)} %get-tuple-element.61), channel_id=1, source_target_pairs={{0,4},{4,0},{8,12},{12,8},{1,5},{5,1},{9,13},{13,9},{2,6},{6,2},{1... | collective-permute-start | bytes 442376 | tf_op jit(solution)/shard_map/ppermute | solution.py:285
  57.2 7.4 %collective-permute-start.21 = (bf16[128,768]{1,0:T(8,128)(2,1)S(1)}, bf16[128,768]{1,0:T(8,128)(2,1)S(1)}, u32[]{:S(2)}, u32[]{:S(2)}) collective-permute-start(bf16[128,768]{1,0:T(8,128)(2,1)S(1)} %add_convert_fusion.4), channel_id=1, source_target_pairs={{0,4},{4,0},{8,12},{12,8},{1,5},{5,1},{9,13},{13,9},{2,6},{6,2},{1... | collective-permute-start | bytes 589832 | tf_op jit(solution)/shard_map/ppermute | solution.py:285
  59.2 10.7 %collective-permute-start.16 = (bf16[96,768]{1,0:T(8,128)(2,1)S(1)}, bf16[96,768]{1,0:T(8,128)(2,1)S(1)}, u32[]{:S(2)}, u32[]{:S(2)}) collective-permute-start(bf16[96,768]{1,0:T(8,128)(2,1)S(1)} %add_convert_fusion.6), channel_id=1, source_target_pairs={{0,8},{4,12},{8,0},{12,4},{1,9},{5,13},{9,1},{13,5},{2,10},{6,14},... | collective-permute-start | bytes 442376 | tf_op jit(solution)/shard_map/ppermute | solution.py:285
  61.6 16.7 %collective-permute-start.19 = (bf16[128,768]{1,0:T(8,128)(2,1)S(1)}, bf16[128,768]{1,0:T(8,128)(2,1)S(1)}, u32[]{:S(2)}, u32[]{:S(2)}) collective-permute-start(bf16[128,768]{1,0:T(8,128)(2,1)S(1)} %get-tuple-element.71), channel_id=1, source_target_pairs={{0,2},{1,3},{2,0},{3,1},{4,6},{5,7},{6,4},{7,5},{8,10},{9,11},{10,... | collective-permute-start | bytes 589832 | tf_op jit(solution)/shard_map/ppermute | solution.py:285
  64.6 13.8 %collective-permute-start.23 = (bf16[128,768]{1,0:T(8,128)(2,1)S(1)}, bf16[128,768]{1,0:T(8,128)(2,1)S(1)}, u32[]{:S(2)}, u32[]{:S(2)}) collective-permute-start(bf16[128,768]{1,0:T(8,128)(2,1)S(1)} %add_convert_fusion.2), channel_id=1, source_target_pairs={{0,8},{4,12},{8,0},{12,4},{1,9},{5,13},{9,1},{13,5},{2,10},{6,14},... | collective-permute-start | bytes 589832 | tf_op jit(solution)/shard_map/ppermute | solution.py:285
  69.9 7.6 %collective-permute-start.18 = (bf16[96,768]{1,0:T(8,128)(2,1)S(1)}, bf16[96,768]{1,0:T(8,128)(2,1)S(1)}, u32[]{:S(2)}, u32[]{:S(2)}) collective-permute-start(bf16[96,768]{1,0:T(8,128)(2,1)S(1)} %add_convert_fusion.5.mine_ref), channel_id=1, source_target_pairs={{0,4},{4,0},{8,12},{12,8},{1,5},{5,1},{9,13},{13,9},{2,6},{6,2},{1... | collective-permute-start | bytes 442376 | tf_op jit(solution)/shard_map/ppermute | solution.py:285
  (5 other events, 29.3 us)

commit v17 on v16

--- a/solution.py
+++ b/solution.py
@@ -367,9 +367,10 @@
     n = len(runs)
     sums, sent_near = {n - 2: over_dp(list(zip(runs[n - 2], got_last)), ahead)}, []
     for i in reversed(range(0, n - 2, 2)):
-        near = add(*over_dp([[x] for x in runs[i + 1]], ahead)).astype(BF16)
-        sent_near.append(partner(near, "labels", 1))
-        sums[i] = over_dp([[x] for x in runs[i]], keep) + sent_near[-1:]
+        odd = over_dp([[x] for x in runs[i + 1]], keep)
+        sent_near.append(odd[-1])
+        got = partner(add(*odd).astype(BF16), "labels", 1)
+        sums[i] = over_dp([[x] for x in runs[i]], odd[-1]) + [got]
     for mask in masks(n)[1:]:
         for i in range(0, n, 2 * mask):
             sent = after(add(*sums[i + mask]).astype(BF16), first, *sent_near)

time: 79.3 us -> 81 us (1.021)
  waiting for transfers between devices: 30.2 us -> 35.4 us
  starting transfers between devices: 26.8 us -> 24.4 us
  local copies, waits for them, and re-layouts: 3.52 us -> 2.37 us
    ppermute x24, waiting for transfers between devices: 30.2 us -> 35.4 us  [partner(): lax.ppermute(x, axis, [(i, i ^ mask) for i in range(lax.axis_size(axis))])]
    ppermute x24, starting transfers between devices: 26.8 us -> 24.4 us  [partner(): lax.ppermute(x, axis, [(i, i ^ mask) for i in range(lax.axis_size(axis))])]
    unnamed x10 -> x6, local copies, waits for them, and re-layouts: 3.52 us -> 2.37 us
where the time goes in v17:
time: 81 us; the launch traced here: 80.8 us
  waiting for transfers between devices  35.4 us (44%)
  starting transfers between devices  24.4 us (30%)
  Pallas kernels  16.7 us (21%)
  local copies, waits for them, and re-layouts  2.37 us (3%)
  other arithmetic  1.11 us (1%)
    ppermute x24, waiting for transfers between devices, partner(): lax.ppermute(x, axis, [(i, i ^ mask) for i in range(lax.axis_size(axis))])  35.4 us
    ppermute x24, starting transfers between devices, partner(): lax.ppermute(x, axis, [(i, i ^ mask) for i in range(lax.axis_size(axis))])  24.4 us
    pallas_call x8, Pallas kernels, call(): pl.pallas_call(kernel, in_specs=[space] * len(args), out_specs=jax.tree.m...  16.7 us
    unnamed x6, local copies, waits for them, and re-layouts  2.37 us
  transfers between devices with their start and end apart: 24, of which 13 were waited for; matrix products, arithmetic and copies ran while one was open for 0% of the time, Pallas kernels for 14%

profile of v17, /device:TPU:0, one launch (start us, length us, event | category | flops | bytes accessed | tf_op | source)
XLA Modules:
  0.0 80.8 jit_solution(5345026954204872074)
XLA Ops:
  1.1 2.6 %collective-permute-start.5 = (bf16[192,768]{1,0:T(8,128)(2,1)}, bf16[192,768]{1,0:T(8,128)(2,1)S(1)}, u32[]{:S(2)}, u32[]{:S(2)}) collective-permute-start(bf16[192,768]{1,0:T(8,128)(2,1)} %shard_ref.1), channel_id=1, source_target_pairs={{0,2},{1,3},{2,0},{3,1},{4,6},{5,7},{6,4},{7,5},{8,10},{9,11},{10,... | collective-permute-start | bytes 884744 | tf_op jit(solution)/shard_map/ppermute | solution.py:285
  3.7 1.6 %own_block.1.refs_0_ = bf16[136,768]{1,0:T(8,128)(2,1)} custom-call(bf16[128,768]{1,0:T(8,128)(2,1)} %feats_ref.1, s32[4,128]{1,0:T(4,128)} %bitcast.5, s32[4,128]{1,0:T(4,128)} %bitcast.6, s32[4,128]{1,0:T(4,128)} %bitcast.7), custom_call_target="tpu_custom_call" | custom-call | bytes 1048576 | tf_op jit(solution)/shard_map/own_block/pallas_call | solution.py:192
  5.4 2.7 %collective-permute-start.1 = (bf16[136,768]{1,0:T(8,128)(2,1)}, bf16[136,768]{1,0:T(8,128)(2,1)S(1)}, u32[]{:S(2)}, u32[]{:S(2)}) collective-permute-start(bf16[136,768]{1,0:T(8,128)(2,1)} %own_block.1.refs_0_), channel_id=1, source_target_pairs={{0,8},{4,12},{8,0},{12,4},{1,9},{5,13},{9,1},{13,5},{2,10},{6,14},... | collective-permute-start | bytes 626696 | tf_op jit(solution)/shard_map/ppermute | solution.py:285
  8.6 1.6 %collective-permute-start = (bf16[136,768]{1,0:T(8,128)(2,1)}, bf16[136,768]{1,0:T(8,128)(2,1)S(1)}, u32[]{:S(2)}, u32[]{:S(2)}) collective-permute-start(bf16[136,768]{1,0:T(8,128)(2,1)} %own_block.1.refs_0_), channel_id=1, source_target_pairs={{0,4},{4,0},{8,12},{12,8},{1,5},{5,1},{9,13},{13,9},{2,6},{6,2},{1... | collective-permute-start | bytes 626696 | tf_op jit(solution)/shard_map/ppermute | solution.py:285
  10.1 1.7 %collective-permute-done.5.refs_8_ = bf16[192,768]{1,0:T(8,128)(2,1)S(1)} collective-permute-done((bf16[192,768]{1,0:T(8,128)(2,1)}, bf16[192,768]{1,0:T(8,128)(2,1)S(1)}, u32[]{:S(2)}, u32[]{:S(2)}) %collective-permute-start.5) | collective-permute-done | bytes 294944 | tf_op jit(solution)/shard_map/ppermute | solution.py:285
  12.3 1.4 %copy-done = bf16[1024,768]{1,0:T(8,128)(2,1)S(1)} copy-done((bf16[1024,768]{1,0:T(8,128)(2,1)S(1)}, bf16[1024,768]{1,0:T(8,128)(2,1)}, u32[]{:S(2)}) %copy-start) | copy-done | bytes 1572888
  14.8 3.6 %collective-permute-done.1.refs_2_ = bf16[136,768]{1,0:T(8,128)(2,1)S(1)} collective-permute-done((bf16[136,768]{1,0:T(8,128)(2,1)}, bf16[136,768]{1,0:T(8,128)(2,1)S(1)}, u32[]{:S(2)}, u32[]{:S(2)}) %collective-permute-start.1) | collective-permute-done | bytes 208928 | tf_op jit(solution)/shard_map/ppermute | solution.py:285
  18.8 1.4 %collective-permute-start.4 = (bf16[136,768]{1,0:T(8,128)(2,1)S(1)}, bf16[136,768]{1,0:T(8,128)(2,1)S(1)}, u32[]{:S(2)}, u32[]{:S(2)}) collective-permute-start(bf16[136,768]{1,0:T(8,128)(2,1)S(1)} %collective-permute-done.1.refs_2_), channel_id=1, source_target_pairs={{0,2},{1,3},{2,0},{3,1},{4,6},{5,7},{6,4},{7,5},{8,10},{9,11},{10,... | collective-permute-start | bytes 626696 | tf_op jit(solution)/shard_map/ppermute | solution.py:285
  20.5 1.8 %collective-permute-start.8 = (bf16[136,768]{1,0:T(8,128)(2,1)S(1)}, bf16[136,768]{1,0:T(8,128)(2,1)S(1)}, u32[]{:S(2)}, u32[]{:S(2)}) collective-permute-start(bf16[136,768]{1,0:T(8,128)(2,1)S(1)} %collective-permute-done.2.refs_1_), channel_id=1, source_target_pairs={{0,4},{4,0},{8,12},{12,8},{1,5},{5,1},{9,13},{13,9},{2,6},{6,2},{1... | collective-permute-start | bytes 626696 | tf_op jit(solution)/shard_map/ppermute | solution.py:285
  22.3 2.4 %collective-permute-done.4.refs_3_ = bf16[136,768]{1,0:T(8,128)(2,1)S(1)} collective-permute-done((bf16[136,768]{1,0:T(8,128)(2,1)S(1)}, bf16[136,768]{1,0:T(8,128)(2,1)S(1)}, u32[]{:S(2)}, u32[]{:S(2)}) %collective-permute-start.4) | collective-permute-done | bytes 208928 | tf_op jit(solution)/shard_map/ppermute | solution.py:285
  24.7 2.8 %collective-permute-done.9.refs_2_ = bf16[136,768]{1,0:T(8,128)(2,1)S(1)} collective-permute-done((bf16[136,768]{1,0:T(8,128)(2,1)S(1)}, bf16[136,768]{1,0:T(8,128)(2,1)S(1)}, u32[]{:S(2)}, u32[]{:S(2)}) %collective-permute-start.9) | collective-permute-done | bytes 208928 | tf_op jit(solution)/shard_map/ppermute | solution.py:285
  28.7 5.4 %pair_work.2 = (bf16[128,768]{1,0:T(8,128)(2,1)S(1)}, bf16[128,768]{1,0:T(8,128)(2,1)S(1)}, bf16[128,768]{1,0:T(8,128)(2,1)S(1)}, bf16[128,768]{1,0:T(8,128)(2,1...) custom-call(bf16[136,768]{1,0:T(8,128)(2,1)S(1)} %copy-done.2, ...), custom_call_target="tpu_custom_call" | custom-call | flops 3623878656 | bytes 8388608 | tf_op jit(solution)/shard_map/pair_work/pallas_call | solution.py:192
  34.1 5.6 %pair_work.3 = (bf16[128,768]{1,0:T(8,128)(2,1)S(1)}, bf16[128,768]{1,0:T(8,128)(2,1)S(1)}, bf16[128,768]{1,0:T(8,128)(2,1)S(1)}, bf16[128,768]{1,0:T(8,128)(2,1...) custom-call(bf16[136,768]{1,0:T(8,128)(2,1)S(1)} %collective-permute, ...), custom_call_target="tpu_custom_call" | custom-call | flops 3623878656 | bytes 8388608 | tf_op jit(solution)/shard_map/pair_work/pallas_call | solution.py:192
  39.8 1.5 %collective-permute-start.13 = (bf16[128,768]{1,0:T(8,128)(2,1)S(1)}, bf16[128,768]{1,0:T(8,128)(2,1)S(1)}, u32[]{:S(2)}, u32[]{:S(2)}) collective-permute-start(bf16[128,768]{1,0:T(8,128)(2,1)S(1)} %get-tuple-element.58), channel_id=1, source_target_pairs={{0,4},{4,0},{8,12},{12,8},{1,5},{5,1},{9,13},{13,9},{2,6},{6,2},{1... | collective-permute-start | bytes 589832 | tf_op jit(solution)/shard_map/ppermute | solution.py:285
  44.2 3.4 %collective-permute-done.13 = bf16[128,768]{1,0:T(8,128)(2,1)S(1)} collective-permute-done((bf16[128,768]{1,0:T(8,128)(2,1)S(1)}, bf16[128,768]{1,0:T(8,128)(2,1)S(1)}, u32[]{:S(2)}, u32[]{:S(2)}) %collective-permute-start.13) | collective-permute-done | bytes 196640 | tf_op jit(solution)/shard_map/ppermute | solution.py:285
  48.5 2.9 %collective-permute-done.12 = bf16[128,768]{1,0:T(8,128)(2,1)S(1)} collective-permute-done((bf16[128,768]{1,0:T(8,128)(2,1)S(1)}, bf16[128,768]{1,0:T(8,128)(2,1)S(1)}, u32[]{:S(2)}, u32[]{:S(2)}) %collective-permute-start.12) | collective-permute-done | bytes 196640 | tf_op jit(solution)/shard_map/ppermute | solution.py:285
  51.4 1.2 %collective-permute-done.14.refs_0_ = bf16[192,768]{1,0:T(8,128)(2,1)S(1)} collective-permute-done((bf16[192,768]{1,0:T(8,128)(2,1)S(1)}, bf16[192,768]{1,0:T(8,128)(2,1)S(1)}, u32[]{:S(2)}, u32[]{:S(2)}) %collective-permute-start.14) | collective-permute-done | bytes 294944 | tf_op jit(solution)/shard_map/ppermute | solution.py:285
  53.5 2.8 %collective-permute-done.22 = bf16[128,768]{1,0:T(8,128)(2,1)S(1)} collective-permute-done((bf16[128,768]{1,0:T(8,128)(2,1)S(1)}, bf16[128,768]{1,0:T(8,128)(2,1)S(1)}, u32[]{:S(2)}, u32[]{:S(2)}) %collective-permute-start.22) | collective-permute-done | bytes 196640 | tf_op jit(solution)/shard_map/ppermute | solution.py:285
  58.0 2.3 %collective-permute-start.16 = (bf16[96,768]{1,0:T(8,128)(2,1)S(1)}, bf16[96,768]{1,0:T(8,128)(2,1)S(1)}, u32[]{:S(2)}, u32[]{:S(2)}) collective-permute-start(bf16[96,768]{1,0:T(8,128)(2,1)S(1)} %add_convert_fusion.6), channel_id=1, source_target_pairs={{0,8},{4,12},{8,0},{12,4},{1,9},{5,13},{9,1},{13,5},{2,10},{6,14},... | collective-permute-start | bytes 442376 | tf_op jit(solution)/shard_map/ppermute | solution.py:285
  60.4 2.3 %collective-permute-done.19 = bf16[128,768]{1,0:T(8,128)(2,1)S(1)} collective-permute-done((bf16[128,768]{1,0:T(8,128)(2,1)S(1)}, bf16[128,768]{1,0:T(8,128)(2,1)S(1)}, u32[]{:S(2)}, u32[]{:S(2)}) %collective-permute-start.19) | collective-permute-done | bytes 196640 | tf_op jit(solution)/shard_map/ppermute | solution.py:285
  63.3 2.8 %collective-permute-start.23 = (bf16[128,768]{1,0:T(8,128)(2,1)S(1)}, bf16[128,768]{1,0:T(8,128)(2,1)S(1)}, u32[]{:S(2)}, u32[]{:S(2)}) collective-permute-start(bf16[128,768]{1,0:T(8,128)(2,1)S(1)} %add_convert_fusion.2), channel_id=1, source_target_pairs={{0,8},{4,12},{8,0},{12,4},{1,9},{5,13},{9,1},{13,5},{2,10},{6,14},... | collective-permute-start | bytes 589832 | tf_op jit(solution)/shard_map/ppermute | solution.py:285
  66.3 4.1 %collective-permute-done.16 = bf16[96,768]{1,0:T(8,128)(2,1)S(1)} collective-permute-done((bf16[96,768]{1,0:T(8,128)(2,1)S(1)}, bf16[96,768]{1,0:T(8,128)(2,1)S(1)}, u32[]{:S(2)}, u32[]{:S(2)}) %collective-permute-start.16) | collective-permute-done | bytes 147488 | tf_op jit(solution)/shard_map/ppermute | solution.py:285
  70.6 1.8 %grad_label_work.3 = bf16[1024,768]{1,0:T(8,128)(2,1)} custom-call(f32[512,128]{1,0:T(8,128)S(1)} %get-tuple-element.62.refs_0_, f32[512,128]{1,0:T(8,128)S(1)} %get-tuple-element.63.refs_1_, s32[512,128]{1,0:T(8,128)S(1)} %get-tuple-element.64.refs_2_, s32[512,128]{1,0:T(8,128)S(1)} %get-tuple-element.65.refs_3_, ...), custom_call_target="tpu_custom_call" | custom-call | flops 805306368 | bytes 4194304 | tf_op jit(solution)/shard_map/grad_label_work/pallas_call | solution.py:192
  72.5 6.7 %collective-permute-done.18.other_ref = bf16[96,768]{1,0:T(8,128)(2,1)S(1)} collective-permute-done((bf16[96,768]{1,0:T(8,128)(2,1)S(1)}, bf16[96,768]{1,0:T(8,128)(2,1)S(1)}, u32[]{:S(2)}, u32[]{:S(2)}) %collective-permute-start.18) | collective-permute-done | bytes 147488 | tf_op jit(solution)/shard_map/ppermute | solution.py:285
  (45 shorter events, 13.7 us)
Async XLA Ops:
  0.6 11.2 %collective-permute-start.3 = (bf16[1024,768]{1,0:T(8,128)(2,1)}, bf16[1024,768]{1,0:T(8,128)(2,1)S(1)}, u32[]{:S(2)}, u32[]{:S(2)}) collective-permute-start(bf16[1024,768]{1,0:T(8,128)(2,1)} %label_ref), channel_id=1, source_target_pairs={{0,1},{1,0},{2,3},{3,2},{4,5},{5,4},{6,7},{7,6},{8,9},{9,8},{10,11... | collective-permute-start | bytes 4718600 | tf_op jit(solution)/shard_map/ppermute | solution.py:285
  1.1 10.6 %collective-permute-start.5 = (bf16[192,768]{1,0:T(8,128)(2,1)}, bf16[192,768]{1,0:T(8,128)(2,1)S(1)}, u32[]{:S(2)}, u32[]{:S(2)}) collective-permute-start(bf16[192,768]{1,0:T(8,128)(2,1)} %shard_ref.1), channel_id=1, source_target_pairs={{0,2},{1,3},{2,0},{3,1},{4,6},{5,7},{6,4},{7,5},{8,10},{9,11},{10,... | collective-permute-start | bytes 884744 | tf_op jit(solution)/shard_map/ppermute | solution.py:285
  5.4 13.0 %collective-permute-start.1 = (bf16[136,768]{1,0:T(8,128)(2,1)}, bf16[136,768]{1,0:T(8,128)(2,1)S(1)}, u32[]{:S(2)}, u32[]{:S(2)}) collective-permute-start(bf16[136,768]{1,0:T(8,128)(2,1)} %own_block.1.refs_0_), channel_id=1, source_target_pairs={{0,8},{4,12},{8,0},{12,4},{1,9},{5,13},{9,1},{13,5},{2,10},{6,14},... | collective-permute-start | bytes 626696 | tf_op jit(solution)/shard_map/ppermute | solution.py:285
  8.0 10.3 %collective-permute-start.2 = (bf16[136,768]{1,0:T(8,128)(2,1)}, bf16[136,768]{1,0:T(8,128)(2,1)S(1)}, u32[]{:S(2)}, u32[]{:S(2)}) collective-permute-start(bf16[136,768]{1,0:T(8,128)(2,1)} %own_block.1.refs_0_), channel_id=1, source_target_pairs={{0,2},{1,3},{2,0},{3,1},{4,6},{5,7},{6,4},{7,5},{8,10},{9,11},{10,... | collective-permute-start | bytes 626696 | tf_op jit(solution)/shard_map/ppermute | solution.py:285
  8.6 10.2 %collective-permute-start = (bf16[136,768]{1,0:T(8,128)(2,1)}, bf16[136,768]{1,0:T(8,128)(2,1)S(1)}, u32[]{:S(2)}, u32[]{:S(2)}) collective-permute-start(bf16[136,768]{1,0:T(8,128)(2,1)} %own_block.1.refs_0_), channel_id=1, source_target_pairs={{0,4},{4,0},{8,12},{12,8},{1,5},{5,1},{9,13},{13,9},{2,6},{6,2},{1... | collective-permute-start | bytes 626696 | tf_op jit(solution)/shard_map/ppermute | solution.py:285
  11.8 8.7 %collective-permute-start.6 = (bf16[192,768]{1,0:T(8,128)(2,1)}, bf16[192,768]{1,0:T(8,128)(2,1)S(1)}, u32[]{:S(2)}, u32[]{:S(2)}) collective-permute-start(bf16[192,768]{1,0:T(8,128)(2,1)} %shard_ref.1), channel_id=1, source_target_pairs={{0,1},{1,0},{2,3},{3,2},{4,5},{5,4},{6,7},{7,6},{8,9},{9,8},{10,11... | collective-permute-start | bytes 884744 | tf_op jit(solution)/shard_map/ppermute | solution.py:285
  11.8 8.7 %collective-permute-start.7 = (bf16[192,768]{1,0:T(8,128)(2,1)S(1)}, bf16[192,768]{1,0:T(8,128)(2,1)S(1)}, u32[]{:S(2)}, u32[]{:S(2)}) collective-permute-start(bf16[192,768]{1,0:T(8,128)(2,1)S(1)} %collective-permute-done.5.refs_8_), channel_id=1, source_target_pairs={{0,1},{1,0},{2,3},{3,2},{4,5},{5,4},{6,7},{7,6},{8,9},{9,8},{10,11... | collective-permute-start | bytes 884744 | tf_op jit(solution)/shard_map/ppermute | solution.py:285
  18.8 5.9 %collective-permute-start.4 = (bf16[136,768]{1,0:T(8,128)(2,1)S(1)}, bf16[136,768]{1,0:T(8,128)(2,1)S(1)}, u32[]{:S(2)}, u32[]{:S(2)}) collective-permute-start(bf16[136,768]{1,0:T(8,128)(2,1)S(1)} %collective-permute-done.1.refs_2_), channel_id=1, source_target_pairs={{0,2},{1,3},{2,0},{3,1},{4,6},{5,7},{6,4},{7,5},{8,10},{9,11},{10,... | collective-permute-start | bytes 626696 | tf_op jit(solution)/shard_map/ppermute | solution.py:285
  20.2 7.2 %collective-permute-start.9 = (bf16[136,768]{1,0:T(8,128)(2,1)S(1)}, bf16[136,768]{1,0:T(8,128)(2,1)S(1)}, u32[]{:S(2)}, u32[]{:S(2)}) collective-permute-start(bf16[136,768]{1,0:T(8,128)(2,1)S(1)} %collective-permute-done.1.refs_2_), channel_id=1, source_target_pairs={{0,4},{4,0},{8,12},{12,8},{1,5},{5,1},{9,13},{13,9},{2,6},{6,2},{1... | collective-permute-start | bytes 626696 | tf_op jit(solution)/shard_map/ppermute | solution.py:285
  20.5 13.6 %collective-permute-start.8 = (bf16[136,768]{1,0:T(8,128)(2,1)S(1)}, bf16[136,768]{1,0:T(8,128)(2,1)S(1)}, u32[]{:S(2)}, u32[]{:S(2)}) collective-permute-start(bf16[136,768]{1,0:T(8,128)(2,1)S(1)} %collective-permute-done.2.refs_1_), channel_id=1, source_target_pairs={{0,4},{4,0},{8,12},{12,8},{1,5},{5,1},{9,13},{13,9},{2,6},{6,2},{1... | collective-permute-start | bytes 626696 | tf_op jit(solution)/shard_map/ppermute | solution.py:285
  27.5 6.6 %collective-permute-start.10 = (bf16[136,768]{1,0:T(8,128)(2,1)S(1)}, bf16[136,768]{1,0:T(8,128)(2,1)S(1)}, u32[]{:S(2)}, u32[]{:S(2)}) collective-permute-start(bf16[136,768]{1,0:T(8,128)(2,1)S(1)} %collective-permute-done.9.refs_2_), channel_id=1, source_target_pairs={{0,2},{1,3},{2,0},{3,1},{4,6},{5,7},{6,4},{7,5},{8,10},{9,11},{10,... | collective-permute-start | bytes 626696 | tf_op jit(solution)/shard_map/ppermute | solution.py:285
  39.7 2.9 %collective-permute-start.11 = (bf16[2,192,768]{2,1,0:T(8,128)(2,1)S(1)}, bf16[2,192,768]{2,1,0:T(8,128)(2,1)S(1)}, u32[]{:S(2)}, u32[]{:S(2)}) collective-permute-start(bf16[2,192,768]{2,1,0:T(8,128)(2,1)S(1)} %get-tuple-element.55), channel_id=1, source_target_pairs={{0,1},{1,0},{2,3},{3,2},{4,5},{5,4},{6,7},{7,6},{8,9},{9,8},{10,11... | collective-permute-start | bytes 1769480 | tf_op jit(solution)/shard_map/ppermute | solution.py:285
  39.8 7.8 %collective-permute-start.13 = (bf16[128,768]{1,0:T(8,128)(2,1)S(1)}, bf16[128,768]{1,0:T(8,128)(2,1)S(1)}, u32[]{:S(2)}, u32[]{:S(2)}) collective-permute-start(bf16[128,768]{1,0:T(8,128)(2,1)S(1)} %get-tuple-element.58), channel_id=1, source_target_pairs={{0,4},{4,0},{8,12},{12,8},{1,5},{5,1},{9,13},{13,9},{2,6},{6,2},{1... | collective-permute-start | bytes 589832 | tf_op jit(solution)/shard_map/ppermute | solution.py:285
  42.4 28.2 %collective-permute-start.17 = (bf16[1024,768]{1,0:T(8,128)(2,1)S(1)}, bf16[1024,768]{1,0:T(8,128)(2,1)S(1)}, u32[]{:S(2)}, u32[]{:S(2)}) collective-permute-start(bf16[1024,768]{1,0:T(8,128)(2,1)S(1)} %grad_label_work.2), channel_id=1, source_target_pairs={{0,1},{1,0},{2,3},{3,2},{4,5},{5,4},{6,7},{7,6},{8,9},{9,8},{10,11... | collective-permute-start | bytes 4718600 | tf_op jit(solution)/shard_map/ppermute | solution.py:285
  42.7 9.9 %collective-permute-start.14 = (bf16[192,768]{1,0:T(8,128)(2,1)S(1)}, bf16[192,768]{1,0:T(8,128)(2,1)S(1)}, u32[]{:S(2)}, u32[]{:S(2)}) collective-permute-start(bf16[192,768]{1,0:T(8,128)(2,1)S(1)} %fusion), channel_id=1, source_target_pairs={{0,2},{1,3},{2,0},{3,1},{4,6},{5,7},{6,4},{7,5},{8,10},{9,11},{10,... | collective-permute-start | bytes 884744 | tf_op jit(solution)/shard_map/ppermute | solution.py:285
  43.3 8.1 %collective-permute-start.12 = (bf16[128,768]{1,0:T(8,128)(2,1)S(1)}, bf16[128,768]{1,0:T(8,128)(2,1)S(1)}, u32[]{:S(2)}, u32[]{:S(2)}) collective-permute-start(bf16[128,768]{1,0:T(8,128)(2,1)S(1)} %get-tuple-element.57), channel_id=1, source_target_pairs={{0,4},{4,0},{8,12},{12,8},{1,5},{5,1},{9,13},{13,9},{2,6},{6,2},{1... | collective-permute-start | bytes 589832 | tf_op jit(solution)/shard_map/ppermute | solution.py:285
  47.6 8.6 %collective-permute-start.22 = (bf16[128,768]{1,0:T(8,128)(2,1)S(1)}, bf16[128,768]{1,0:T(8,128)(2,1)S(1)}, u32[]{:S(2)}, u32[]{:S(2)}) collective-permute-start(bf16[128,768]{1,0:T(8,128)(2,1)S(1)} %add_convert_fusion.3), channel_id=1, source_target_pairs={{0,2},{1,3},{2,0},{3,1},{4,6},{5,7},{6,4},{7,5},{8,10},{9,11},{10,... | collective-permute-start | bytes 589832 | tf_op jit(solution)/shard_map/ppermute | solution.py:285
  52.8 5.2 %collective-permute-start.15 = (bf16[96,768]{1,0:T(8,128)(2,1)S(1)}, bf16[96,768]{1,0:T(8,128)(2,1)S(1)}, u32[]{:S(2)}, u32[]{:S(2)}) collective-permute-start(bf16[96,768]{1,0:T(8,128)(2,1)S(1)} %get-tuple-element.61), channel_id=1, source_target_pairs={{0,4},{4,0},{8,12},{12,8},{1,5},{5,1},{9,13},{13,9},{2,6},{6,2},{1... | collective-permute-start | bytes 442376 | tf_op jit(solution)/shard_map/ppermute | solution.py:285
  56.3 6.4 %collective-permute-start.19 = (bf16[128,768]{1,0:T(8,128)(2,1)S(1)}, bf16[128,768]{1,0:T(8,128)(2,1)S(1)}, u32[]{:S(2)}, u32[]{:S(2)}) collective-permute-start(bf16[128,768]{1,0:T(8,128)(2,1)S(1)} %get-tuple-element.72), channel_id=1, source_target_pairs={{0,2},{1,3},{2,0},{3,1},{4,6},{5,7},{6,4},{7,5},{8,10},{9,11},{10,... | collective-permute-start | bytes 589832 | tf_op jit(solution)/shard_map/ppermute | solution.py:285
  58.0 12.4 %collective-permute-start.16 = (bf16[96,768]{1,0:T(8,128)(2,1)S(1)}, bf16[96,768]{1,0:T(8,128)(2,1)S(1)}, u32[]{:S(2)}, u32[]{:S(2)}) collective-permute-start(bf16[96,768]{1,0:T(8,128)(2,1)S(1)} %add_convert_fusion.6), channel_id=1, source_target_pairs={{0,8},{4,12},{8,0},{12,4},{1,9},{5,13},{9,1},{13,5},{2,10},{6,14},... | collective-permute-start | bytes 442376 | tf_op jit(solution)/shard_map/ppermute | solution.py:285
  62.7 17.3 %collective-permute-start.20 = (bf16[128,768]{1,0:T(8,128)(2,1)S(1)}, bf16[128,768]{1,0:T(8,128)(2,1)S(1)}, u32[]{:S(2)}, u32[]{:S(2)}) collective-permute-start(bf16[128,768]{1,0:T(8,128)(2,1)S(1)} %get-tuple-element.73), channel_id=1, source_target_pairs={{0,2},{1,3},{2,0},{3,1},{4,6},{5,7},{6,4},{7,5},{8,10},{9,11},{10,... | collective-permute-start | bytes 589832 | tf_op jit(solution)/shard_map/ppermute | solution.py:285
  63.3 16.8 %collective-permute-start.23 = (bf16[128,768]{1,0:T(8,128)(2,1)S(1)}, bf16[128,768]{1,0:T(8,128)(2,1)S(1)}, u32[]{:S(2)}, u32[]{:S(2)}) collective-permute-start(bf16[128,768]{1,0:T(8,128)(2,1)S(1)} %add_convert_fusion.2), channel_id=1, source_target_pairs={{0,8},{4,12},{8,0},{12,4},{1,9},{5,13},{9,1},{13,5},{2,10},{6,14},... | collective-permute-start | bytes 589832 | tf_op jit(solution)/shard_map/ppermute | solution.py:285
  66.1 13.9 %collective-permute-start.21 = (bf16[128,768]{1,0:T(8,128)(2,1)S(1)}, bf16[128,768]{1,0:T(8,128)(2,1)S(1)}, u32[]{:S(2)}, u32[]{:S(2)}) collective-permute-start(bf16[128,768]{1,0:T(8,128)(2,1)S(1)} %add_convert_fusion.4), channel_id=1, source_target_pairs={{0,4},{4,0},{8,12},{12,8},{1,5},{5,1},{9,13},{13,9},{2,6},{6,2},{1... | collective-permute-start | bytes 589832 | tf_op jit(solution)/shard_map/ppermute | solution.py:285
  70.5 8.6 %collective-permute-start.18 = (bf16[96,768]{1,0:T(8,128)(2,1)S(1)}, bf16[96,768]{1,0:T(8,128)(2,1)S(1)}, u32[]{:S(2)}, u32[]{:S(2)}) collective-permute-start(bf16[96,768]{1,0:T(8,128)(2,1)S(1)} %add_convert_fusion.5.mine_ref), channel_id=1, source_target_pairs={{0,4},{4,0},{8,12},{12,8},{1,5},{5,1},{9,13},{13,9},{2,6},{6,2},{1... | collective-permute-start | bytes 442376 | tf_op jit(solution)/shard_map/ppermute | solution.py:285
  (3 other events, 16.4 us)

commit v18 on v16

--- a/solution.py
+++ b/solution.py
@@ -33,6 +33,7 @@
     shards = take(n_data if first else 0)
     enc, total_in = (None, None) if first else take(2)
     backs, grad_scores_ref, block_ref, embedding_ref = take(n_sources), *take(3)
+    grad_hidden_ref = next(it) if last else None
     enc = next(it) if first else enc
     shares = take(2 if last else 0)
     total_ref = next(it)
@@ -111,13 +112,32 @@
     for m in range(n_data if last else 0):
         shares[m % 2][m // 2] = total_ref[shard_at(m, shard_rows), :].astype(BF16)
 
-    grad_feats = dot(grad_hidden, enc[...], 1, 1).astype(BF16)
-    for s in range(n_sources):
-        parts = [
-            grad_feats[(j * n_sources + s) * cap : (j * n_sources + s + 1) * cap]
-            for j in range(n_sets)
-        ]
-        backs[s][...] = dot(picks[s], jnp.concatenate(parts, axis=0), 0, 0).astype(BF16)
+    if last:
+        grad_hidden_ref[...] = grad_hidden
+        for pick, ref in zip(picks, backs):
+            ref[...] = pick
+        return
+    for ref, back in zip(backs, back_rows(picks, grad_hidden, enc[...], cap, n_sets)):
+        ref[...] = back
+
+
+def back_rows(picks, grad_hidden, enc, cap, n_sets):
+    grad_feats = dot(grad_hidden, enc, 1, 1).astype(BF16)
+    for s, pick in enumerate(picks):
+        parts = []
+        for j in range(n_sets):
+            at = (j * len(picks) + s) * cap
+            parts.append(grad_feats[at : at + cap])
+        yield dot(pick, jnp.concatenate(parts, axis=0), 0, 0).astype(BF16)
+
+
+def back_kernel(*refs, cap, n_sets):
+    sources = (len(refs) - 2) // 2
+    picks = [r[...] for r in refs[:sources]]
+    grad_hidden, enc = refs[sources][...], refs[sources + 1][...]
+    backs = back_rows(picks, grad_hidden, enc, cap, n_sets)
+    for ref, back in zip(refs[sources + 2 :], backs):
+        ref[...] = back
 
 
 def grad_label_kernel(*refs, calls, n_sets, j, n_more):
@@ -215,8 +235,10 @@
     shard_rows = shards[0].shape[0]
     full = (n_data * shard_rows, width)
     backs = len(sources)
-    shapes = [shaped((rows, width))] * backs
+    shapes = [shaped((n_sets * cap, rows) if last else (rows, width))] * backs
     shapes += [shaped((slots, BLK), F32), shaped((slots, BLK), jnp.int32), shaped((slots, width))]
+    if last:
+        shapes += [shaped((slots, width))]
     more = [before["enc"], before["total"]] if before else shards
     scratch = []
     if not before:
@@ -248,8 +270,21 @@
     )
     result = {"back": list(out[:backs]), "slots": list(out[backs : backs + 3])}
     rest = list(out[backs + 3 :])
+    grad_hidden = rest.pop(0) if last else None
     result["enc"] = before["enc"] if before else rest.pop(0)
     result["shares" if last else "total"] = rest if last else rest[0]
+    if last:
+        result["back"] = call(
+            functools.partial(back_kernel, cap=cap, n_sets=n_sets),
+            "back_work",
+            [shaped((rows, width))] * backs,
+            [],
+            2 * slots * width * (width + rows),
+            3,
+            *result["back"],
+            grad_hidden,
+            result["enc"],
+        )
     return result
 
 

time: 79.3 us -> 80.1 us (1.010)
  starting transfers between devices: 26.8 us -> 32.3 us
  waiting for transfers between devices: 30.2 us -> 26 us
  local copies, waits for them, and re-layouts: 3.52 us -> 2.37 us
    ppermute x24, starting transfers between devices: 26.8 us -> 32.3 us  [partner(): lax.ppermute(x, axis, [(i, i ^ mask) for i in range(lax.axis_size(axis))])]
    ppermute x24, waiting for transfers between devices: 30.2 us -> 26 us  [partner(): lax.ppermute(x, axis, [(i, i ^ mask) for i in range(lax.axis_size(axis))])]
    unnamed x10 -> x6, local copies, waits for them, and re-layouts: 3.52 us -> 2.37 us
    pallas_call x8 -> x9, Pallas kernels: 16.7 us -> 17.4 us  [call(): pl.pallas_call(kernel, in_specs=[space] * len(args), out_specs=jax.tree.m...]
  transfers between devices with their start and end apart: 24 -> 24, of which waited for: 13 -> 12; matrix products, arithmetic and copies ran while one was open for 0% -> 0% of each run, Pallas kernels for 14% -> 16%
where the time goes in v18:
time: 80.1 us; the launch traced here: 79.9 us
  starting transfers between devices  32.3 us (40%)
  waiting for transfers between devices  26 us (32%)
  Pallas kernels  17.4 us (22%)
  local copies, waits for them, and re-layouts  2.37 us (3%)
  other arithmetic  1.09 us (1%)
    ppermute x24, starting transfers between devices, partner(): lax.ppermute(x, axis, [(i, i ^ mask) for i in range(lax.axis_size(axis))])  32.3 us
    ppermute x24, waiting for transfers between devices, partner(): lax.ppermute(x, axis, [(i, i ^ mask) for i in range(lax.axis_size(axis))])  26 us
    pallas_call x9, Pallas kernels, call(): pl.pallas_call(kernel, in_specs=[space] * len(args), out_specs=jax.tree.m...  17.4 us
    unnamed x6, local copies, waits for them, and re-layouts  2.37 us
  transfers between devices with their start and end apart: 24, of which 12 were waited for; matrix products, arithmetic and copies ran while one was open for 0% of the time, Pallas kernels for 16%

profile of v18, /device:TPU:0, one launch (start us, length us, event | category | flops | bytes accessed | tf_op | source)
XLA Modules:
  0.0 79.9 jit_solution(13066974712549151118)
XLA Ops:
  1.1 2.6 %collective-permute-start.5 = (bf16[192,768]{1,0:T(8,128)(2,1)}, bf16[192,768]{1,0:T(8,128)(2,1)S(1)}, u32[]{:S(2)}, u32[]{:S(2)}) collective-permute-start(bf16[192,768]{1,0:T(8,128)(2,1)} %shard_ref.1), channel_id=1, source_target_pairs={{0,2},{1,3},{2,0},{3,1},{4,6},{5,7},{6,4},{7,5},{8,10},{9,11},{10,... | collective-permute-start | bytes 884744 | tf_op jit(solution)/shard_map/ppermute | solution.py:320
  3.7 1.6 %own_block.1.refs_0_ = bf16[136,768]{1,0:T(8,128)(2,1)} custom-call(bf16[128,768]{1,0:T(8,128)(2,1)} %feats_ref.1, s32[4,128]{1,0:T(4,128)} %bitcast.5, s32[4,128]{1,0:T(4,128)} %bitcast.6, s32[4,128]{1,0:T(4,128)} %bitcast.7), custom_call_target="tpu_custom_call" | custom-call | bytes 1048576 | tf_op jit(solution)/shard_map/own_block/pallas_call | solution.py:212
  5.4 2.7 %collective-permute-start.1 = (bf16[136,768]{1,0:T(8,128)(2,1)}, bf16[136,768]{1,0:T(8,128)(2,1)S(1)}, u32[]{:S(2)}, u32[]{:S(2)}) collective-permute-start(bf16[136,768]{1,0:T(8,128)(2,1)} %own_block.1.refs_0_), channel_id=1, source_target_pairs={{0,8},{4,12},{8,0},{12,4},{1,9},{5,13},{9,1},{13,5},{2,10},{6,14},... | collective-permute-start | bytes 626696 | tf_op jit(solution)/shard_map/ppermute | solution.py:320
  8.6 1.6 %collective-permute-start = (bf16[136,768]{1,0:T(8,128)(2,1)}, bf16[136,768]{1,0:T(8,128)(2,1)S(1)}, u32[]{:S(2)}, u32[]{:S(2)}) collective-permute-start(bf16[136,768]{1,0:T(8,128)(2,1)} %own_block.1.refs_0_), channel_id=1, source_target_pairs={{0,4},{4,0},{8,12},{12,8},{1,5},{5,1},{9,13},{13,9},{2,6},{6,2},{1... | collective-permute-start | bytes 626696 | tf_op jit(solution)/shard_map/ppermute | solution.py:320
  10.1 1.7 %collective-permute-done.5.refs_8_ = bf16[192,768]{1,0:T(8,128)(2,1)S(1)} collective-permute-done((bf16[192,768]{1,0:T(8,128)(2,1)}, bf16[192,768]{1,0:T(8,128)(2,1)S(1)}, u32[]{:S(2)}, u32[]{:S(2)}) %collective-permute-start.5) | collective-permute-done | bytes 294944 | tf_op jit(solution)/shard_map/ppermute | solution.py:320
  14.8 3.6 %collective-permute-done.1.refs_2_ = bf16[136,768]{1,0:T(8,128)(2,1)S(1)} collective-permute-done((bf16[136,768]{1,0:T(8,128)(2,1)}, bf16[136,768]{1,0:T(8,128)(2,1)S(1)}, u32[]{:S(2)}, u32[]{:S(2)}) %collective-permute-start.1) | collective-permute-done | bytes 208928 | tf_op jit(solution)/shard_map/ppermute | solution.py:320
  18.8 1.4 %collective-permute-start.4 = (bf16[136,768]{1,0:T(8,128)(2,1)S(1)}, bf16[136,768]{1,0:T(8,128)(2,1)S(1)}, u32[]{:S(2)}, u32[]{:S(2)}) collective-permute-start(bf16[136,768]{1,0:T(8,128)(2,1)S(1)} %collective-permute-done.1.refs_2_), channel_id=1, source_target_pairs={{0,2},{1,3},{2,0},{3,1},{4,6},{5,7},{6,4},{7,5},{8,10},{9,11},{10,... | collective-permute-start | bytes 626696 | tf_op jit(solution)/shard_map/ppermute | solution.py:320
  20.5 1.8 %collective-permute-start.8 = (bf16[136,768]{1,0:T(8,128)(2,1)S(1)}, bf16[136,768]{1,0:T(8,128)(2,1)S(1)}, u32[]{:S(2)}, u32[]{:S(2)}) collective-permute-start(bf16[136,768]{1,0:T(8,128)(2,1)S(1)} %collective-permute-done.2.refs_1_), channel_id=1, source_target_pairs={{0,4},{4,0},{8,12},{12,8},{1,5},{5,1},{9,13},{13,9},{2,6},{6,2},{1... | collective-permute-start | bytes 626696 | tf_op jit(solution)/shard_map/ppermute | solution.py:320
  22.3 2.4 %collective-permute-done.4.refs_3_ = bf16[136,768]{1,0:T(8,128)(2,1)S(1)} collective-permute-done((bf16[136,768]{1,0:T(8,128)(2,1)S(1)}, bf16[136,768]{1,0:T(8,128)(2,1)S(1)}, u32[]{:S(2)}, u32[]{:S(2)}) %collective-permute-start.4) | collective-permute-done | bytes 208928 | tf_op jit(solution)/shard_map/ppermute | solution.py:320
  24.7 2.8 %collective-permute-done.9.refs_2_ = bf16[136,768]{1,0:T(8,128)(2,1)S(1)} collective-permute-done((bf16[136,768]{1,0:T(8,128)(2,1)S(1)}, bf16[136,768]{1,0:T(8,128)(2,1)S(1)}, u32[]{:S(2)}, u32[]{:S(2)}) %collective-permute-start.9) | collective-permute-done | bytes 208928 | tf_op jit(solution)/shard_map/ppermute | solution.py:320
  28.7 5.4 %pair_work.2 = (bf16[128,768]{1,0:T(8,128)(2,1)S(1)}, bf16[128,768]{1,0:T(8,128)(2,1)S(1)}, bf16[128,768]{1,0:T(8,128)(2,1)S(1)}, bf16[128,768]{1,0:T(8,128)(2,1...) custom-call(bf16[136,768]{1,0:T(8,128)(2,1)S(1)} %copy-done.2, ...), custom_call_target="tpu_custom_call" | custom-call | flops 3623878656 | bytes 8388608 | tf_op jit(solution)/shard_map/pair_work/pallas_call | solution.py:212
  34.1 4.9 %pair_work.3 = (bf16[128,128]{1,0:T(8,128)(2,1)S(1)}, bf16[128,128]{1,0:T(8,128)(2,1)S(1)}, bf16[128,128]{1,0:T(8,128)(2,1)S(1)}, bf16[128,128]{1,0:T(8,128)(2,1...) custom-call(bf16[136,768]{1,0:T(8,128)(2,1)S(1)} %collective-permute, ...), custom_call_target="tpu_custom_call" | custom-call | flops 3623878656 | bytes 8388608 | tf_op jit(solution)/shard_map/pair_work/pallas_call | solution.py:212
  40.7 1.4 %back_work.1 = (bf16[128,768]{1,0:T(8,128)(2,1)S(1)}, bf16[128,768]{1,0:T(8,128)(2,1)S(1)}, bf16[128,768]{1,0:T(8,128)(2,1)S(1)}, bf16[128,768]{1,0:T(8,128)(2,1)S(1)}) custom-call(bf16[128,128]{1,0:T(8,128)(2,1)S(1)} %get-tuple-element.61.refs_0_, bf16[128,128]{1,0:T(8,128)(2,1)S(1)} %get-tuple-element.62.refs_1_, ...), custom_call_target="tpu_custom_call" | custom-call | flops 704643072 | bytes 3145728 | tf_op jit(solution)/shard_map/back_work/pallas_call | solution.py:212
  42.1 1.5 %collective-permute-start.13 = (bf16[128,768]{1,0:T(8,128)(2,1)S(1)}, bf16[128,768]{1,0:T(8,128)(2,1)S(1)}, u32[]{:S(2)}, u32[]{:S(2)}) collective-permute-start(bf16[128,768]{1,0:T(8,128)(2,1)S(1)} %get-tuple-element.68), channel_id=1, source_target_pairs={{0,4},{4,0},{8,12},{12,8},{1,5},{5,1},{9,13},{13,9},{2,6},{6,2},{1... | collective-permute-start | bytes 589832 | tf_op jit(solution)/shard_map/ppermute | solution.py:320
  46.4 3.6 %collective-permute-done.13 = bf16[128,768]{1,0:T(8,128)(2,1)S(1)} collective-permute-done((bf16[128,768]{1,0:T(8,128)(2,1)S(1)}, bf16[128,768]{1,0:T(8,128)(2,1)S(1)}, u32[]{:S(2)}, u32[]{:S(2)}) %collective-permute-start.13) | collective-permute-done | bytes 196640 | tf_op jit(solution)/shard_map/ppermute | solution.py:320
  50.9 2.4 %collective-permute-done.12 = bf16[128,768]{1,0:T(8,128)(2,1)S(1)} collective-permute-done((bf16[128,768]{1,0:T(8,128)(2,1)S(1)}, bf16[128,768]{1,0:T(8,128)(2,1)S(1)}, u32[]{:S(2)}, u32[]{:S(2)}) %collective-permute-start.12) | collective-permute-done | bytes 196640 | tf_op jit(solution)/shard_map/ppermute | solution.py:320
  54.9 3.0 %collective-permute-done.20 = bf16[128,768]{1,0:T(8,128)(2,1)S(1)} collective-permute-done((bf16[128,768]{1,0:T(8,128)(2,1)S(1)}, bf16[128,768]{1,0:T(8,128)(2,1)S(1)}, u32[]{:S(2)}, u32[]{:S(2)}) %collective-permute-start.20) | collective-permute-done | bytes 196640 | tf_op jit(solution)/shard_map/ppermute | solution.py:320
  58.6 1.4 %collective-permute-done.15 = bf16[96,768]{1,0:T(8,128)(2,1)S(1)} collective-permute-done((bf16[96,768]{1,0:T(8,128)(2,1)S(1)}, bf16[96,768]{1,0:T(8,128)(2,1)S(1)}, u32[]{:S(2)}, u32[]{:S(2)}) %collective-permute-start.15) | collective-permute-done | bytes 147488 | tf_op jit(solution)/shard_map/ppermute | solution.py:320
  60.1 2.3 %collective-permute-start.16 = (bf16[96,768]{1,0:T(8,128)(2,1)S(1)}, bf16[96,768]{1,0:T(8,128)(2,1)S(1)}, u32[]{:S(2)}, u32[]{:S(2)}) collective-permute-start(bf16[96,768]{1,0:T(8,128)(2,1)S(1)} %add_convert_fusion.6), channel_id=1, source_target_pairs={{0,8},{4,12},{8,0},{12,4},{1,9},{5,13},{9,1},{13,5},{2,10},{6,14},... | collective-permute-start | bytes 442376 | tf_op jit(solution)/shard_map/ppermute | solution.py:320
  63.6 1.5 %collective-permute-done.21 = bf16[128,768]{1,0:T(8,128)(2,1)S(1)} collective-permute-done((bf16[128,768]{1,0:T(8,128)(2,1)S(1)}, bf16[128,768]{1,0:T(8,128)(2,1)S(1)}, u32[]{:S(2)}, u32[]{:S(2)}) %collective-permute-start.21) | collective-permute-done | bytes 196640 | tf_op jit(solution)/shard_map/ppermute | solution.py:320
  65.2 2.2 %collective-permute-start.23 = (bf16[128,768]{1,0:T(8,128)(2,1)S(1)}, bf16[128,768]{1,0:T(8,128)(2,1)S(1)}, u32[]{:S(2)}, u32[]{:S(2)}) collective-permute-start(bf16[128,768]{1,0:T(8,128)(2,1)S(1)} %add_convert_fusion.2), channel_id=1, source_target_pairs={{0,8},{4,12},{8,0},{12,4},{1,9},{5,13},{9,1},{13,5},{2,10},{6,14},... | collective-permute-start | bytes 589832 | tf_op jit(solution)/shard_map/ppermute | solution.py:320
  67.4 6.2 %collective-permute-start.18 = (bf16[96,768]{1,0:T(8,128)(2,1)S(1)}, bf16[96,768]{1,0:T(8,128)(2,1)S(1)}, u32[]{:S(2)}, u32[]{:S(2)}) collective-permute-start(bf16[96,768]{1,0:T(8,128)(2,1)S(1)} %add_convert_fusion.5.mine_ref), channel_id=1, source_target_pairs={{0,4},{4,0},{8,12},{12,8},{1,5},{5,1},{9,13},{13,9},{2,6},{6,2},{1... | collective-permute-start | bytes 442376 | tf_op jit(solution)/shard_map/ppermute | solution.py:320
  73.6 1.8 %grad_label_work.3 = bf16[1024,768]{1,0:T(8,128)(2,1)} custom-call(f32[512,128]{1,0:T(8,128)S(1)} %get-tuple-element.72.refs_0_, f32[512,128]{1,0:T(8,128)S(1)} %get-tuple-element.73.refs_1_, s32[512,128]{1,0:T(8,128)S(1)} %get-tuple-element.74.refs_2_, s32[512,128]{1,0:T(8,128)S(1)} %get-tuple-element.75.refs_3_, ...), custom_call_target="tpu_custom_call" | custom-call | flops 805306368 | bytes 4194304 | tf_op jit(solution)/shard_map/grad_label_work/pallas_call | solution.py:212
  75.4 2.9 %collective-permute-done.18.other_ref = bf16[96,768]{1,0:T(8,128)(2,1)S(1)} collective-permute-done((bf16[96,768]{1,0:T(8,128)(2,1)S(1)}, bf16[96,768]{1,0:T(8,128)(2,1)S(1)}, u32[]{:S(2)}, u32[]{:S(2)}) %collective-permute-start.18) | collective-permute-done | bytes 147488 | tf_op jit(solution)/shard_map/ppermute | solution.py:320
  (46 shorter events, 16.7 us)
Async XLA Ops:
  0.6 11.2 %collective-permute-start.3 = (bf16[1024,768]{1,0:T(8,128)(2,1)}, bf16[1024,768]{1,0:T(8,128)(2,1)S(1)}, u32[]{:S(2)}, u32[]{:S(2)}) collective-permute-start(bf16[1024,768]{1,0:T(8,128)(2,1)} %label_ref), channel_id=1, source_target_pairs={{0,1},{1,0},{2,3},{3,2},{4,5},{5,4},{6,7},{7,6},{8,9},{9,8},{10,11... | collective-permute-start | bytes 4718600 | tf_op jit(solution)/shard_map/ppermute | solution.py:320
  1.1 10.6 %collective-permute-start.5 = (bf16[192,768]{1,0:T(8,128)(2,1)}, bf16[192,768]{1,0:T(8,128)(2,1)S(1)}, u32[]{:S(2)}, u32[]{:S(2)}) collective-permute-start(bf16[192,768]{1,0:T(8,128)(2,1)} %shard_ref.1), channel_id=1, source_target_pairs={{0,2},{1,3},{2,0},{3,1},{4,6},{5,7},{6,4},{7,5},{8,10},{9,11},{10,... | collective-permute-start | bytes 884744 | tf_op jit(solution)/shard_map/ppermute | solution.py:320
  5.4 13.0 %collective-permute-start.1 = (bf16[136,768]{1,0:T(8,128)(2,1)}, bf16[136,768]{1,0:T(8,128)(2,1)S(1)}, u32[]{:S(2)}, u32[]{:S(2)}) collective-permute-start(bf16[136,768]{1,0:T(8,128)(2,1)} %own_block.1.refs_0_), channel_id=1, source_target_pairs={{0,8},{4,12},{8,0},{12,4},{1,9},{5,13},{9,1},{13,5},{2,10},{6,14},... | collective-permute-start | bytes 626696 | tf_op jit(solution)/shard_map/ppermute | solution.py:320
  8.0 10.3 %collective-permute-start.2 = (bf16[136,768]{1,0:T(8,128)(2,1)}, bf16[136,768]{1,0:T(8,128)(2,1)S(1)}, u32[]{:S(2)}, u32[]{:S(2)}) collective-permute-start(bf16[136,768]{1,0:T(8,128)(2,1)} %own_block.1.refs_0_), channel_id=1, source_target_pairs={{0,2},{1,3},{2,0},{3,1},{4,6},{5,7},{6,4},{7,5},{8,10},{9,11},{10,... | collective-permute-start | bytes 626696 | tf_op jit(solution)/shard_map/ppermute | solution.py:320
  8.6 10.2 %collective-permute-start = (bf16[136,768]{1,0:T(8,128)(2,1)}, bf16[136,768]{1,0:T(8,128)(2,1)S(1)}, u32[]{:S(2)}, u32[]{:S(2)}) collective-permute-start(bf16[136,768]{1,0:T(8,128)(2,1)} %own_block.1.refs_0_), channel_id=1, source_target_pairs={{0,4},{4,0},{8,12},{12,8},{1,5},{5,1},{9,13},{13,9},{2,6},{6,2},{1... | collective-permute-start | bytes 626696 | tf_op jit(solution)/shard_map/ppermute | solution.py:320
  11.8 8.7 %collective-permute-start.6 = (bf16[192,768]{1,0:T(8,128)(2,1)}, bf16[192,768]{1,0:T(8,128)(2,1)S(1)}, u32[]{:S(2)}, u32[]{:S(2)}) collective-permute-start(bf16[192,768]{1,0:T(8,128)(2,1)} %shard_ref.1), channel_id=1, source_target_pairs={{0,1},{1,0},{2,3},{3,2},{4,5},{5,4},{6,7},{7,6},{8,9},{9,8},{10,11... | collective-permute-start | bytes 884744 | tf_op jit(solution)/shard_map/ppermute | solution.py:320
  11.8 8.7 %collective-permute-start.7 = (bf16[192,768]{1,0:T(8,128)(2,1)S(1)}, bf16[192,768]{1,0:T(8,128)(2,1)S(1)}, u32[]{:S(2)}, u32[]{:S(2)}) collective-permute-start(bf16[192,768]{1,0:T(8,128)(2,1)S(1)} %collective-permute-done.5.refs_8_), channel_id=1, source_target_pairs={{0,1},{1,0},{2,3},{3,2},{4,5},{5,4},{6,7},{7,6},{8,9},{9,8},{10,11... | collective-permute-start | bytes 884744 | tf_op jit(solution)/shard_map/ppermute | solution.py:320
  18.8 5.9 %collective-permute-start.4 = (bf16[136,768]{1,0:T(8,128)(2,1)S(1)}, bf16[136,768]{1,0:T(8,128)(2,1)S(1)}, u32[]{:S(2)}, u32[]{:S(2)}) collective-permute-start(bf16[136,768]{1,0:T(8,128)(2,1)S(1)} %collective-permute-done.1.refs_2_), channel_id=1, source_target_pairs={{0,2},{1,3},{2,0},{3,1},{4,6},{5,7},{6,4},{7,5},{8,10},{9,11},{10,... | collective-permute-start | bytes 626696 | tf_op jit(solution)/shard_map/ppermute | solution.py:320
  20.2 7.2 %collective-permute-start.9 = (bf16[136,768]{1,0:T(8,128)(2,1)S(1)}, bf16[136,768]{1,0:T(8,128)(2,1)S(1)}, u32[]{:S(2)}, u32[]{:S(2)}) collective-permute-start(bf16[136,768]{1,0:T(8,128)(2,1)S(1)} %collective-permute-done.1.refs_2_), channel_id=1, source_target_pairs={{0,4},{4,0},{8,12},{12,8},{1,5},{5,1},{9,13},{13,9},{2,6},{6,2},{1... | collective-permute-start | bytes 626696 | tf_op jit(solution)/shard_map/ppermute | solution.py:320
  20.5 13.6 %collective-permute-start.8 = (bf16[136,768]{1,0:T(8,128)(2,1)S(1)}, bf16[136,768]{1,0:T(8,128)(2,1)S(1)}, u32[]{:S(2)}, u32[]{:S(2)}) collective-permute-start(bf16[136,768]{1,0:T(8,128)(2,1)S(1)} %collective-permute-done.2.refs_1_), channel_id=1, source_target_pairs={{0,4},{4,0},{8,12},{12,8},{1,5},{5,1},{9,13},{13,9},{2,6},{6,2},{1... | collective-permute-start | bytes 626696 | tf_op jit(solution)/shard_map/ppermute | solution.py:320
  27.5 6.6 %collective-permute-start.10 = (bf16[136,768]{1,0:T(8,128)(2,1)S(1)}, bf16[136,768]{1,0:T(8,128)(2,1)S(1)}, u32[]{:S(2)}, u32[]{:S(2)}) collective-permute-start(bf16[136,768]{1,0:T(8,128)(2,1)S(1)} %collective-permute-done.9.refs_2_), channel_id=1, source_target_pairs={{0,2},{1,3},{2,0},{3,1},{4,6},{5,7},{6,4},{7,5},{8,10},{9,11},{10,... | collective-permute-start | bytes 626696 | tf_op jit(solution)/shard_map/ppermute | solution.py:320
  39.0 4.6 %collective-permute-start.11 = (bf16[2,192,768]{2,1,0:T(8,128)(2,1)S(1)}, bf16[2,192,768]{2,1,0:T(8,128)(2,1)S(1)}, u32[]{:S(2)}, u32[]{:S(2)}) collective-permute-start(bf16[2,192,768]{2,1,0:T(8,128)(2,1)S(1)} %get-tuple-element.60), channel_id=1, source_target_pairs={{0,1},{1,0},{2,3},{3,2},{4,5},{5,4},{6,7},{7,6},{8,9},{9,8},{10,11... | collective-permute-start | bytes 1769480 | tf_op jit(solution)/shard_map/ppermute | solution.py:320
  40.2 33.4 %collective-permute-start.17 = (bf16[1024,768]{1,0:T(8,128)(2,1)S(1)}, bf16[1024,768]{1,0:T(8,128)(2,1)S(1)}, u32[]{:S(2)}, u32[]{:S(2)}) collective-permute-start(bf16[1024,768]{1,0:T(8,128)(2,1)S(1)} %grad_label_work.2), channel_id=1, source_target_pairs={{0,1},{1,0},{2,3},{3,2},{4,5},{5,4},{6,7},{7,6},{8,9},{9,8},{10,11... | collective-permute-start | bytes 4718600 | tf_op jit(solution)/shard_map/ppermute | solution.py:320
  42.1 7.8 %collective-permute-start.13 = (bf16[128,768]{1,0:T(8,128)(2,1)S(1)}, bf16[128,768]{1,0:T(8,128)(2,1)S(1)}, u32[]{:S(2)}, u32[]{:S(2)}) collective-permute-start(bf16[128,768]{1,0:T(8,128)(2,1)S(1)} %get-tuple-element.68), channel_id=1, source_target_pairs={{0,4},{4,0},{8,12},{12,8},{1,5},{5,1},{9,13},{13,9},{2,6},{6,2},{1... | collective-permute-start | bytes 589832 | tf_op jit(solution)/shard_map/ppermute | solution.py:320
  43.7 10.0 %collective-permute-start.14 = (bf16[192,768]{1,0:T(8,128)(2,1)S(1)}, bf16[192,768]{1,0:T(8,128)(2,1)S(1)}, u32[]{:S(2)}, u32[]{:S(2)}) collective-permute-start(bf16[192,768]{1,0:T(8,128)(2,1)S(1)} %fusion), channel_id=1, source_target_pairs={{0,2},{1,3},{2,0},{3,1},{4,6},{5,7},{6,4},{7,5},{8,10},{9,11},{10,... | collective-permute-start | bytes 884744 | tf_op jit(solution)/shard_map/ppermute | solution.py:320
  44.3 8.9 %collective-permute-start.12 = (bf16[128,768]{1,0:T(8,128)(2,1)S(1)}, bf16[128,768]{1,0:T(8,128)(2,1)S(1)}, u32[]{:S(2)}, u32[]{:S(2)}) collective-permute-start(bf16[128,768]{1,0:T(8,128)(2,1)S(1)} %get-tuple-element.67), channel_id=1, source_target_pairs={{0,4},{4,0},{8,12},{12,8},{1,5},{5,1},{9,13},{13,9},{2,6},{6,2},{1... | collective-permute-start | bytes 589832 | tf_op jit(solution)/shard_map/ppermute | solution.py:320
  45.2 12.7 %collective-permute-start.20 = (bf16[128,768]{1,0:T(8,128)(2,1)S(1)}, bf16[128,768]{1,0:T(8,128)(2,1)S(1)}, u32[]{:S(2)}, u32[]{:S(2)}) collective-permute-start(bf16[128,768]{1,0:T(8,128)(2,1)S(1)} %get-tuple-element.84), channel_id=1, source_target_pairs={{0,2},{1,3},{2,0},{3,1},{4,6},{5,7},{6,4},{7,5},{8,10},{9,11},{10,... | collective-permute-start | bytes 589832 | tf_op jit(solution)/shard_map/ppermute | solution.py:320
  50.0 12.4 %collective-permute-start.22 = (bf16[128,768]{1,0:T(8,128)(2,1)S(1)}, bf16[128,768]{1,0:T(8,128)(2,1)S(1)}, u32[]{:S(2)}, u32[]{:S(2)}) collective-permute-start(bf16[128,768]{1,0:T(8,128)(2,1)S(1)} %add_convert_fusion.3), channel_id=1, source_target_pairs={{0,2},{1,3},{2,0},{3,1},{4,6},{5,7},{6,4},{7,5},{8,10},{9,11},{10,... | collective-permute-start | bytes 589832 | tf_op jit(solution)/shard_map/ppermute | solution.py:320
  53.9 6.2 %collective-permute-start.15 = (bf16[96,768]{1,0:T(8,128)(2,1)S(1)}, bf16[96,768]{1,0:T(8,128)(2,1)S(1)}, u32[]{:S(2)}, u32[]{:S(2)}) collective-permute-start(bf16[96,768]{1,0:T(8,128)(2,1)S(1)} %get-tuple-element.71), channel_id=1, source_target_pairs={{0,4},{4,0},{8,12},{12,8},{1,5},{5,1},{9,13},{13,9},{2,6},{6,2},{1... | collective-permute-start | bytes 442376 | tf_op jit(solution)/shard_map/ppermute | solution.py:320
  57.9 7.2 %collective-permute-start.21 = (bf16[128,768]{1,0:T(8,128)(2,1)S(1)}, bf16[128,768]{1,0:T(8,128)(2,1)S(1)}, u32[]{:S(2)}, u32[]{:S(2)}) collective-permute-start(bf16[128,768]{1,0:T(8,128)(2,1)S(1)} %add_convert_fusion.4), channel_id=1, source_target_pairs={{0,4},{4,0},{8,12},{12,8},{1,5},{5,1},{9,13},{13,9},{2,6},{6,2},{1... | collective-permute-start | bytes 589832 | tf_op jit(solution)/shard_map/ppermute | solution.py:320
  60.1 7.2 %collective-permute-start.16 = (bf16[96,768]{1,0:T(8,128)(2,1)S(1)}, bf16[96,768]{1,0:T(8,128)(2,1)S(1)}, u32[]{:S(2)}, u32[]{:S(2)}) collective-permute-start(bf16[96,768]{1,0:T(8,128)(2,1)S(1)} %add_convert_fusion.6), channel_id=1, source_target_pairs={{0,8},{4,12},{8,0},{12,4},{1,9},{5,13},{9,1},{13,5},{2,10},{6,14},... | collective-permute-start | bytes 442376 | tf_op jit(solution)/shard_map/ppermute | solution.py:320
  62.5 16.6 %collective-permute-start.19 = (bf16[128,768]{1,0:T(8,128)(2,1)S(1)}, bf16[128,768]{1,0:T(8,128)(2,1)S(1)}, u32[]{:S(2)}, u32[]{:S(2)}) collective-permute-start(bf16[128,768]{1,0:T(8,128)(2,1)S(1)} %get-tuple-element.81), channel_id=1, source_target_pairs={{0,2},{1,3},{2,0},{3,1},{4,6},{5,7},{6,4},{7,5},{8,10},{9,11},{10,... | collective-permute-start | bytes 589832 | tf_op jit(solution)/shard_map/ppermute | solution.py:320
  65.2 14.0 %collective-permute-start.23 = (bf16[128,768]{1,0:T(8,128)(2,1)S(1)}, bf16[128,768]{1,0:T(8,128)(2,1)S(1)}, u32[]{:S(2)}, u32[]{:S(2)}) collective-permute-start(bf16[128,768]{1,0:T(8,128)(2,1)S(1)} %add_convert_fusion.2), channel_id=1, source_target_pairs={{0,8},{4,12},{8,0},{12,4},{1,9},{5,13},{9,1},{13,5},{2,10},{6,14},... | collective-permute-start | bytes 589832 | tf_op jit(solution)/shard_map/ppermute | solution.py:320
  67.4 10.9 %collective-permute-start.18 = (bf16[96,768]{1,0:T(8,128)(2,1)S(1)}, bf16[96,768]{1,0:T(8,128)(2,1)S(1)}, u32[]{:S(2)}, u32[]{:S(2)}) collective-permute-start(bf16[96,768]{1,0:T(8,128)(2,1)S(1)} %add_convert_fusion.5.mine_ref), channel_id=1, source_target_pairs={{0,4},{4,0},{8,12},{12,8},{1,5},{5,1},{9,13},{13,9},{2,6},{6,2},{1... | collective-permute-start | bytes 442376 | tf_op jit(solution)/shard_map/ppermute | solution.py:320
  (3 other events, 16.4 us)

commit v19 on v16

--- a/solution.py
+++ b/solution.py
@@ -450,8 +450,8 @@
         terms = reduce_runs(backs, got_last, sent, keep, first)
         other = partner(grad_label_work(works, 2, 1, label_weight.shape), "dp", 1)
         grad_label = grad_label_work(works, 2, 0, label_weight.shape, other)
-        grad_enc = join_halves(share, grad_label)
-        grad_feats = add(after(terms[0], grad_enc), *terms[1:]).astype(BF16)
+        grad_feats = add(after(terms[0], grad_label), *terms[1:]).astype(BF16)
+        grad_enc = join_halves(share, grad_feats)
     else:
         shards = gather_near(gather_far(enc_weight))
         flat = owners.reshape(-1)

time: 79.3 us -> 78.5 us (0.990)
  transfers between devices with their start and end apart: 24 -> 24, of which waited for: 13 -> 14; matrix products, arithmetic and copies ran while one was open for 0% -> 1% of each run, Pallas kernels for 14% -> 13%
where the time goes in v19:
time: 78.5 us; the launch traced here: 78.3 us
  waiting for transfers between devices  29.5 us (38%)
  starting transfers between devices  26.8 us (34%)
  Pallas kernels  16.7 us (21%)
  local copies, waits for them, and re-layouts  3.52 us (4%)
  other arithmetic  1.08 us (1%)
    ppermute x24, waiting for transfers between devices, partner(): lax.ppermute(x, axis, [(i, i ^ mask) for i in range(lax.axis_size(axis))])  29.5 us
    ppermute x24, starting transfers between devices, partner(): lax.ppermute(x, axis, [(i, i ^ mask) for i in range(lax.axis_size(axis))])  26.8 us
    pallas_call x8, Pallas kernels, call(): pl.pallas_call(kernel, in_specs=[space] * len(args), out_specs=jax.tree.m...  16.7 us
    unnamed x10, local copies, waits for them, and re-layouts  3.52 us
  transfers between devices with their start and end apart: 24, of which 14 were waited for; matrix products, arithmetic and copies ran while one was open for 1% of the time, Pallas kernels for 13%

profile of v19, /device:TPU:0, one launch (start us, length us, event | category | flops | bytes accessed | tf_op | source)
XLA Modules:
  0.0 78.3 jit_solution(17988903771186938427)
XLA Ops:
  1.1 2.6 %collective-permute-start.5 = (bf16[192,768]{1,0:T(8,128)(2,1)}, bf16[192,768]{1,0:T(8,128)(2,1)S(1)}, u32[]{:S(2)}, u32[]{:S(2)}) collective-permute-start(bf16[192,768]{1,0:T(8,128)(2,1)} %shard_ref.1), channel_id=1, source_target_pairs={{0,2},{1,3},{2,0},{3,1},{4,6},{5,7},{6,4},{7,5},{8,10},{9,11},{10,... | collective-permute-start | bytes 884744 | tf_op jit(solution)/shard_map/ppermute | solution.py:285
  3.7 1.6 %own_block.1.refs_0_ = bf16[136,768]{1,0:T(8,128)(2,1)} custom-call(bf16[128,768]{1,0:T(8,128)(2,1)} %feats_ref.1, s32[4,128]{1,0:T(4,128)} %bitcast.5, s32[4,128]{1,0:T(4,128)} %bitcast.6, s32[4,128]{1,0:T(4,128)} %bitcast.7), custom_call_target="tpu_custom_call" | custom-call | bytes 1048576 | tf_op jit(solution)/shard_map/own_block/pallas_call | solution.py:192
  5.4 2.7 %collective-permute-start.1 = (bf16[136,768]{1,0:T(8,128)(2,1)}, bf16[136,768]{1,0:T(8,128)(2,1)S(1)}, u32[]{:S(2)}, u32[]{:S(2)}) collective-permute-start(bf16[136,768]{1,0:T(8,128)(2,1)} %own_block.1.refs_0_), channel_id=1, source_target_pairs={{0,8},{4,12},{8,0},{12,4},{1,9},{5,13},{9,1},{13,5},{2,10},{6,14},... | collective-permute-start | bytes 626696 | tf_op jit(solution)/shard_map/ppermute | solution.py:285
  8.6 1.6 %collective-permute-start = (bf16[136,768]{1,0:T(8,128)(2,1)}, bf16[136,768]{1,0:T(8,128)(2,1)S(1)}, u32[]{:S(2)}, u32[]{:S(2)}) collective-permute-start(bf16[136,768]{1,0:T(8,128)(2,1)} %own_block.1.refs_0_), channel_id=1, source_target_pairs={{0,4},{4,0},{8,12},{12,8},{1,5},{5,1},{9,13},{13,9},{2,6},{6,2},{1... | collective-permute-start | bytes 626696 | tf_op jit(solution)/shard_map/ppermute | solution.py:285
  10.1 1.7 %collective-permute-done.5.refs_8_ = bf16[192,768]{1,0:T(8,128)(2,1)S(1)} collective-permute-done((bf16[192,768]{1,0:T(8,128)(2,1)}, bf16[192,768]{1,0:T(8,128)(2,1)S(1)}, u32[]{:S(2)}, u32[]{:S(2)}) %collective-permute-start.5) | collective-permute-done | bytes 294944 | tf_op jit(solution)/shard_map/ppermute | solution.py:285
  13.4 1.4 %copy-done = bf16[1024,768]{1,0:T(8,128)(2,1)S(1)} copy-done((bf16[1024,768]{1,0:T(8,128)(2,1)S(1)}, bf16[1024,768]{1,0:T(8,128)(2,1)}, u32[]{:S(2)}) %copy-start) | copy-done | bytes 1572888
  15.9 2.4 %collective-permute-done.1.refs_2_ = bf16[136,768]{1,0:T(8,128)(2,1)S(1)} collective-permute-done((bf16[136,768]{1,0:T(8,128)(2,1)}, bf16[136,768]{1,0:T(8,128)(2,1)S(1)}, u32[]{:S(2)}, u32[]{:S(2)}) %collective-permute-start.1) | collective-permute-done | bytes 208928 | tf_op jit(solution)/shard_map/ppermute | solution.py:285
  18.8 1.4 %collective-permute-start.4 = (bf16[136,768]{1,0:T(8,128)(2,1)S(1)}, bf16[136,768]{1,0:T(8,128)(2,1)S(1)}, u32[]{:S(2)}, u32[]{:S(2)}) collective-permute-start(bf16[136,768]{1,0:T(8,128)(2,1)S(1)} %collective-permute-done.1.refs_2_), channel_id=1, source_target_pairs={{0,2},{1,3},{2,0},{3,1},{4,6},{5,7},{6,4},{7,5},{8,10},{9,11},{10,... | collective-permute-start | bytes 626696 | tf_op jit(solution)/shard_map/ppermute | solution.py:285
  20.5 1.8 %collective-permute-start.8 = (bf16[136,768]{1,0:T(8,128)(2,1)S(1)}, bf16[136,768]{1,0:T(8,128)(2,1)S(1)}, u32[]{:S(2)}, u32[]{:S(2)}) collective-permute-start(bf16[136,768]{1,0:T(8,128)(2,1)S(1)} %collective-permute-done.2.refs_1_), channel_id=1, source_target_pairs={{0,4},{4,0},{8,12},{12,8},{1,5},{5,1},{9,13},{13,9},{2,6},{6,2},{1... | collective-permute-start | bytes 626696 | tf_op jit(solution)/shard_map/ppermute | solution.py:285
  22.3 2.4 %collective-permute-done.4.refs_3_ = bf16[136,768]{1,0:T(8,128)(2,1)S(1)} collective-permute-done((bf16[136,768]{1,0:T(8,128)(2,1)S(1)}, bf16[136,768]{1,0:T(8,128)(2,1)S(1)}, u32[]{:S(2)}, u32[]{:S(2)}) %collective-permute-start.4) | collective-permute-done | bytes 208928 | tf_op jit(solution)/shard_map/ppermute | solution.py:285
  24.7 2.8 %collective-permute-done.9.refs_2_ = bf16[136,768]{1,0:T(8,128)(2,1)S(1)} collective-permute-done((bf16[136,768]{1,0:T(8,128)(2,1)S(1)}, bf16[136,768]{1,0:T(8,128)(2,1)S(1)}, u32[]{:S(2)}, u32[]{:S(2)}) %collective-permute-start.9) | collective-permute-done | bytes 208928 | tf_op jit(solution)/shard_map/ppermute | solution.py:285
  28.7 5.4 %pair_work.2 = (bf16[128,768]{1,0:T(8,128)(2,1)S(1)}, bf16[128,768]{1,0:T(8,128)(2,1)S(1)}, bf16[128,768]{1,0:T(8,128)(2,1)S(1)}, bf16[128,768]{1,0:T(8,128)(2,1...) custom-call(bf16[136,768]{1,0:T(8,128)(2,1)S(1)} %copy-done.2, ...), custom_call_target="tpu_custom_call" | custom-call | flops 3623878656 | bytes 8388608 | tf_op jit(solution)/shard_map/pair_work/pallas_call | solution.py:192
  34.1 5.6 %pair_work.3 = (bf16[128,768]{1,0:T(8,128)(2,1)S(1)}, bf16[128,768]{1,0:T(8,128)(2,1)S(1)}, bf16[128,768]{1,0:T(8,128)(2,1)S(1)}, bf16[128,768]{1,0:T(8,128)(2,1...) custom-call(bf16[136,768]{1,0:T(8,128)(2,1)S(1)} %collective-permute, ...), custom_call_target="tpu_custom_call" | custom-call | flops 3623878656 | bytes 8388608 | tf_op jit(solution)/shard_map/pair_work/pallas_call | solution.py:192
  41.5 1.4 %collective-permute-start.14 = (bf16[128,768]{1,0:T(8,128)(2,1)S(1)}, bf16[128,768]{1,0:T(8,128)(2,1)S(1)}, u32[]{:S(2)}, u32[]{:S(2)}) collective-permute-start(bf16[128,768]{1,0:T(8,128)(2,1)S(1)} %get-tuple-element.66), channel_id=1, source_target_pairs={{0,4},{4,0},{8,12},{12,8},{1,5},{5,1},{9,13},{13,9},{2,6},{6,2},{1... | collective-permute-start | bytes 589832 | tf_op jit(solution)/shard_map/ppermute | solution.py:285
  45.7 3.6 %collective-permute-done.14 = bf16[128,768]{1,0:T(8,128)(2,1)S(1)} collective-permute-done((bf16[128,768]{1,0:T(8,128)(2,1)S(1)}, bf16[128,768]{1,0:T(8,128)(2,1)S(1)}, u32[]{:S(2)}, u32[]{:S(2)}) %collective-permute-start.14) | collective-permute-done | bytes 196640 | tf_op jit(solution)/shard_map/ppermute | solution.py:285
  50.1 2.4 %collective-permute-done.13 = bf16[128,768]{1,0:T(8,128)(2,1)S(1)} collective-permute-done((bf16[128,768]{1,0:T(8,128)(2,1)S(1)}, bf16[128,768]{1,0:T(8,128)(2,1)S(1)}, u32[]{:S(2)}, u32[]{:S(2)}) %collective-permute-start.13) | collective-permute-done | bytes 196640 | tf_op jit(solution)/shard_map/ppermute | solution.py:285
  54.3 2.9 %collective-permute-done.17 = bf16[128,768]{1,0:T(8,128)(2,1)S(1)} collective-permute-done((bf16[128,768]{1,0:T(8,128)(2,1)S(1)}, bf16[128,768]{1,0:T(8,128)(2,1)S(1)}, u32[]{:S(2)}, u32[]{:S(2)}) %collective-permute-start.17) | collective-permute-done | bytes 196640 | tf_op jit(solution)/shard_map/ppermute | solution.py:285
  57.9 1.3 %collective-permute-done.20 = bf16[96,768]{1,0:T(8,128)(2,1)S(1)} collective-permute-done((bf16[96,768]{1,0:T(8,128)(2,1)S(1)}, bf16[96,768]{1,0:T(8,128)(2,1)S(1)}, u32[]{:S(2)}, u32[]{:S(2)}) %collective-permute-start.20) | collective-permute-done | bytes 147488 | tf_op jit(solution)/shard_map/ppermute | solution.py:285
  59.2 2.4 %collective-permute-start.22 = (bf16[96,768]{1,0:T(8,128)(2,1)S(1)}, bf16[96,768]{1,0:T(8,128)(2,1)S(1)}, u32[]{:S(2)}, u32[]{:S(2)}) collective-permute-start(bf16[96,768]{1,0:T(8,128)(2,1)S(1)} %add_convert_fusion.6), channel_id=1, source_target_pairs={{0,8},{4,12},{8,0},{12,4},{1,9},{5,13},{9,1},{13,5},{2,10},{6,14},... | collective-permute-start | bytes 442376 | tf_op jit(solution)/shard_map/ppermute | solution.py:285
  62.7 1.9 %collective-permute-done.18 = bf16[128,768]{1,0:T(8,128)(2,1)S(1)} collective-permute-done((bf16[128,768]{1,0:T(8,128)(2,1)S(1)}, bf16[128,768]{1,0:T(8,128)(2,1)S(1)}, u32[]{:S(2)}, u32[]{:S(2)}) %collective-permute-start.18) | collective-permute-done | bytes 196640 | tf_op jit(solution)/shard_map/ppermute | solution.py:285
  64.6 2.4 %collective-permute-start.21 = (bf16[128,768]{1,0:T(8,128)(2,1)S(1)}, bf16[128,768]{1,0:T(8,128)(2,1)S(1)}, u32[]{:S(2)}, u32[]{:S(2)}) collective-permute-start(bf16[128,768]{1,0:T(8,128)(2,1)S(1)} %add_convert_fusion.2), channel_id=1, source_target_pairs={{0,8},{4,12},{8,0},{12,4},{1,9},{5,13},{9,1},{13,5},{2,10},{6,14},... | collective-permute-start | bytes 589832 | tf_op jit(solution)/shard_map/ppermute | solution.py:285
  67.0 2.8 %collective-permute-done.22 = bf16[96,768]{1,0:T(8,128)(2,1)S(1)} collective-permute-done((bf16[96,768]{1,0:T(8,128)(2,1)S(1)}, bf16[96,768]{1,0:T(8,128)(2,1)S(1)}, u32[]{:S(2)}, u32[]{:S(2)}) %collective-permute-start.22) | collective-permute-done | bytes 147488 | tf_op jit(solution)/shard_map/ppermute | solution.py:285
  70.3 1.8 %grad_label_work.3 = bf16[1024,768]{1,0:T(8,128)(2,1)} custom-call(f32[512,128]{1,0:T(8,128)S(1)} %get-tuple-element.49.refs_0_, f32[512,128]{1,0:T(8,128)S(1)} %get-tuple-element.55.refs_1_, s32[512,128]{1,0:T(8,128)S(1)} %get-tuple-element.56.refs_2_, s32[512,128]{1,0:T(8,128)S(1)} %get-tuple-element.57.refs_3_, ...), custom_call_target="tpu_custom_call" | custom-call | flops 805306368 | bytes 4194304 | tf_op jit(solution)/shard_map/grad_label_work/pallas_call | solution.py:192
  72.2 3.8 %collective-permute-done.21 = bf16[128,768]{1,0:T(8,128)(2,1)S(1)} collective-permute-done((bf16[128,768]{1,0:T(8,128)(2,1)S(1)}, bf16[128,768]{1,0:T(8,128)(2,1)S(1)}, u32[]{:S(2)}, u32[]{:S(2)}) %collective-permute-start.21) | collective-permute-done | bytes 196640 | tf_op jit(solution)/shard_map/ppermute | solution.py:285
  (49 shorter events, 17.6 us)
Async XLA Ops:
  0.6 11.2 %collective-permute-start.3 = (bf16[1024,768]{1,0:T(8,128)(2,1)}, bf16[1024,768]{1,0:T(8,128)(2,1)S(1)}, u32[]{:S(2)}, u32[]{:S(2)}) collective-permute-start(bf16[1024,768]{1,0:T(8,128)(2,1)} %label_ref), channel_id=1, source_target_pairs={{0,1},{1,0},{2,3},{3,2},{4,5},{5,4},{6,7},{7,6},{8,9},{9,8},{10,11... | collective-permute-start | bytes 4718600 | tf_op jit(solution)/shard_map/ppermute | solution.py:285
  1.1 10.6 %collective-permute-start.5 = (bf16[192,768]{1,0:T(8,128)(2,1)}, bf16[192,768]{1,0:T(8,128)(2,1)S(1)}, u32[]{:S(2)}, u32[]{:S(2)}) collective-permute-start(bf16[192,768]{1,0:T(8,128)(2,1)} %shard_ref.1), channel_id=1, source_target_pairs={{0,2},{1,3},{2,0},{3,1},{4,6},{5,7},{6,4},{7,5},{8,10},{9,11},{10,... | collective-permute-start | bytes 884744 | tf_op jit(solution)/shard_map/ppermute | solution.py:285
  5.4 13.0 %collective-permute-start.1 = (bf16[136,768]{1,0:T(8,128)(2,1)}, bf16[136,768]{1,0:T(8,128)(2,1)S(1)}, u32[]{:S(2)}, u32[]{:S(2)}) collective-permute-start(bf16[136,768]{1,0:T(8,128)(2,1)} %own_block.1.refs_0_), channel_id=1, source_target_pairs={{0,8},{4,12},{8,0},{12,4},{1,9},{5,13},{9,1},{13,5},{2,10},{6,14},... | collective-permute-start | bytes 626696 | tf_op jit(solution)/shard_map/ppermute | solution.py:285
  8.0 10.3 %collective-permute-start.2 = (bf16[136,768]{1,0:T(8,128)(2,1)}, bf16[136,768]{1,0:T(8,128)(2,1)S(1)}, u32[]{:S(2)}, u32[]{:S(2)}) collective-permute-start(bf16[136,768]{1,0:T(8,128)(2,1)} %own_block.1.refs_0_), channel_id=1, source_target_pairs={{0,2},{1,3},{2,0},{3,1},{4,6},{5,7},{6,4},{7,5},{8,10},{9,11},{10,... | collective-permute-start | bytes 626696 | tf_op jit(solution)/shard_map/ppermute | solution.py:285
  8.6 10.2 %collective-permute-start = (bf16[136,768]{1,0:T(8,128)(2,1)}, bf16[136,768]{1,0:T(8,128)(2,1)S(1)}, u32[]{:S(2)}, u32[]{:S(2)}) collective-permute-start(bf16[136,768]{1,0:T(8,128)(2,1)} %own_block.1.refs_0_), channel_id=1, source_target_pairs={{0,4},{4,0},{8,12},{12,8},{1,5},{5,1},{9,13},{13,9},{2,6},{6,2},{1... | collective-permute-start | bytes 626696 | tf_op jit(solution)/shard_map/ppermute | solution.py:285
  11.8 8.7 %collective-permute-start.6 = (bf16[192,768]{1,0:T(8,128)(2,1)}, bf16[192,768]{1,0:T(8,128)(2,1)S(1)}, u32[]{:S(2)}, u32[]{:S(2)}) collective-permute-start(bf16[192,768]{1,0:T(8,128)(2,1)} %shard_ref.1), channel_id=1, source_target_pairs={{0,1},{1,0},{2,3},{3,2},{4,5},{5,4},{6,7},{7,6},{8,9},{9,8},{10,11... | collective-permute-start | bytes 884744 | tf_op jit(solution)/shard_map/ppermute | solution.py:285
  12.9 7.6 %collective-permute-start.7 = (bf16[192,768]{1,0:T(8,128)(2,1)S(1)}, bf16[192,768]{1,0:T(8,128)(2,1)S(1)}, u32[]{:S(2)}, u32[]{:S(2)}) collective-permute-start(bf16[192,768]{1,0:T(8,128)(2,1)S(1)} %collective-permute-done.5.refs_8_), channel_id=1, source_target_pairs={{0,1},{1,0},{2,3},{3,2},{4,5},{5,4},{6,7},{7,6},{8,9},{9,8},{10,11... | collective-permute-start | bytes 884744 | tf_op jit(solution)/shard_map/ppermute | solution.py:285
  18.8 5.9 %collective-permute-start.4 = (bf16[136,768]{1,0:T(8,128)(2,1)S(1)}, bf16[136,768]{1,0:T(8,128)(2,1)S(1)}, u32[]{:S(2)}, u32[]{:S(2)}) collective-permute-start(bf16[136,768]{1,0:T(8,128)(2,1)S(1)} %collective-permute-done.1.refs_2_), channel_id=1, source_target_pairs={{0,2},{1,3},{2,0},{3,1},{4,6},{5,7},{6,4},{7,5},{8,10},{9,11},{10,... | collective-permute-start | bytes 626696 | tf_op jit(solution)/shard_map/ppermute | solution.py:285
  20.2 7.2 %collective-permute-start.9 = (bf16[136,768]{1,0:T(8,128)(2,1)S(1)}, bf16[136,768]{1,0:T(8,128)(2,1)S(1)}, u32[]{:S(2)}, u32[]{:S(2)}) collective-permute-start(bf16[136,768]{1,0:T(8,128)(2,1)S(1)} %collective-permute-done.1.refs_2_), channel_id=1, source_target_pairs={{0,4},{4,0},{8,12},{12,8},{1,5},{5,1},{9,13},{13,9},{2,6},{6,2},{1... | collective-permute-start | bytes 626696 | tf_op jit(solution)/shard_map/ppermute | solution.py:285
  20.5 13.6 %collective-permute-start.8 = (bf16[136,768]{1,0:T(8,128)(2,1)S(1)}, bf16[136,768]{1,0:T(8,128)(2,1)S(1)}, u32[]{:S(2)}, u32[]{:S(2)}) collective-permute-start(bf16[136,768]{1,0:T(8,128)(2,1)S(1)} %collective-permute-done.2.refs_1_), channel_id=1, source_target_pairs={{0,4},{4,0},{8,12},{12,8},{1,5},{5,1},{9,13},{13,9},{2,6},{6,2},{1... | collective-permute-start | bytes 626696 | tf_op jit(solution)/shard_map/ppermute | solution.py:285
  27.5 6.6 %collective-permute-start.10 = (bf16[136,768]{1,0:T(8,128)(2,1)S(1)}, bf16[136,768]{1,0:T(8,128)(2,1)S(1)}, u32[]{:S(2)}, u32[]{:S(2)}) collective-permute-start(bf16[136,768]{1,0:T(8,128)(2,1)S(1)} %collective-permute-done.9.refs_2_), channel_id=1, source_target_pairs={{0,2},{1,3},{2,0},{3,1},{4,6},{5,7},{6,4},{7,5},{8,10},{9,11},{10,... | collective-permute-start | bytes 626696 | tf_op jit(solution)/shard_map/ppermute | solution.py:285
  39.7 3.1 %collective-permute-start.12 = (bf16[2,192,768]{2,1,0:T(8,128)(2,1)S(1)}, bf16[2,192,768]{2,1,0:T(8,128)(2,1)S(1)}, u32[]{:S(2)}, u32[]{:S(2)}) collective-permute-start(bf16[2,192,768]{2,1,0:T(8,128)(2,1)S(1)} %get-tuple-element.63), channel_id=1, source_target_pairs={{0,1},{1,0},{2,3},{3,2},{4,5},{5,4},{6,7},{7,6},{8,9},{9,8},{10,11... | collective-permute-start | bytes 1769480 | tf_op jit(solution)/shard_map/ppermute | solution.py:285
  40.9 29.4 %collective-permute-start.11 = (bf16[1024,768]{1,0:T(8,128)(2,1)S(1)}, bf16[1024,768]{1,0:T(8,128)(2,1)S(1)}, u32[]{:S(2)}, u32[]{:S(2)}) collective-permute-start(bf16[1024,768]{1,0:T(8,128)(2,1)S(1)} %grad_label_work.2), channel_id=1, source_target_pairs={{0,1},{1,0},{2,3},{3,2},{4,5},{5,4},{6,7},{7,6},{8,9},{9,8},{10,11... | collective-permute-start | bytes 4718600 | tf_op jit(solution)/shard_map/ppermute | solution.py:285
  41.5 7.8 %collective-permute-start.14 = (bf16[128,768]{1,0:T(8,128)(2,1)S(1)}, bf16[128,768]{1,0:T(8,128)(2,1)S(1)}, u32[]{:S(2)}, u32[]{:S(2)}) collective-permute-start(bf16[128,768]{1,0:T(8,128)(2,1)S(1)} %get-tuple-element.66), channel_id=1, source_target_pairs={{0,4},{4,0},{8,12},{12,8},{1,5},{5,1},{9,13},{13,9},{2,6},{6,2},{1... | collective-permute-start | bytes 589832 | tf_op jit(solution)/shard_map/ppermute | solution.py:285
  43.0 10.0 %collective-permute-start.15 = (bf16[192,768]{1,0:T(8,128)(2,1)S(1)}, bf16[192,768]{1,0:T(8,128)(2,1)S(1)}, u32[]{:S(2)}, u32[]{:S(2)}) collective-permute-start(bf16[192,768]{1,0:T(8,128)(2,1)S(1)} %fusion), channel_id=1, source_target_pairs={{0,2},{1,3},{2,0},{3,1},{4,6},{5,7},{6,4},{7,5},{8,10},{9,11},{10,... | collective-permute-start | bytes 884744 | tf_op jit(solution)/shard_map/ppermute | solution.py:285
  43.5 9.0 %collective-permute-start.13 = (bf16[128,768]{1,0:T(8,128)(2,1)S(1)}, bf16[128,768]{1,0:T(8,128)(2,1)S(1)}, u32[]{:S(2)}, u32[]{:S(2)}) collective-permute-start(bf16[128,768]{1,0:T(8,128)(2,1)S(1)} %get-tuple-element.65), channel_id=1, source_target_pairs={{0,4},{4,0},{8,12},{12,8},{1,5},{5,1},{9,13},{13,9},{2,6},{6,2},{1... | collective-permute-start | bytes 589832 | tf_op jit(solution)/shard_map/ppermute | solution.py:285
  44.4 12.7 %collective-permute-start.17 = (bf16[128,768]{1,0:T(8,128)(2,1)S(1)}, bf16[128,768]{1,0:T(8,128)(2,1)S(1)}, u32[]{:S(2)}, u32[]{:S(2)}) collective-permute-start(bf16[128,768]{1,0:T(8,128)(2,1)S(1)} %get-tuple-element.72), channel_id=1, source_target_pairs={{0,2},{1,3},{2,0},{3,1},{4,6},{5,7},{6,4},{7,5},{8,10},{9,11},{10,... | collective-permute-start | bytes 589832 | tf_op jit(solution)/shard_map/ppermute | solution.py:285
  49.3 12.2 %collective-permute-start.19 = (bf16[128,768]{1,0:T(8,128)(2,1)S(1)}, bf16[128,768]{1,0:T(8,128)(2,1)S(1)}, u32[]{:S(2)}, u32[]{:S(2)}) collective-permute-start(bf16[128,768]{1,0:T(8,128)(2,1)S(1)} %add_convert_fusion.3), channel_id=1, source_target_pairs={{0,2},{1,3},{2,0},{3,1},{4,6},{5,7},{6,4},{7,5},{8,10},{9,11},{10,... | collective-permute-start | bytes 589832 | tf_op jit(solution)/shard_map/ppermute | solution.py:285
  53.1 6.0 %collective-permute-start.20 = (bf16[96,768]{1,0:T(8,128)(2,1)S(1)}, bf16[96,768]{1,0:T(8,128)(2,1)S(1)}, u32[]{:S(2)}, u32[]{:S(2)}) collective-permute-start(bf16[96,768]{1,0:T(8,128)(2,1)S(1)} %get-tuple-element.76), channel_id=1, source_target_pairs={{0,4},{4,0},{8,12},{12,8},{1,5},{5,1},{9,13},{13,9},{2,6},{6,2},{1... | collective-permute-start | bytes 442376 | tf_op jit(solution)/shard_map/ppermute | solution.py:285
  57.2 7.4 %collective-permute-start.18 = (bf16[128,768]{1,0:T(8,128)(2,1)S(1)}, bf16[128,768]{1,0:T(8,128)(2,1)S(1)}, u32[]{:S(2)}, u32[]{:S(2)}) collective-permute-start(bf16[128,768]{1,0:T(8,128)(2,1)S(1)} %add_convert_fusion.4), channel_id=1, source_target_pairs={{0,4},{4,0},{8,12},{12,8},{1,5},{5,1},{9,13},{13,9},{2,6},{6,2},{1... | collective-permute-start | bytes 589832 | tf_op jit(solution)/shard_map/ppermute | solution.py:285
  59.2 10.7 %collective-permute-start.22 = (bf16[96,768]{1,0:T(8,128)(2,1)S(1)}, bf16[96,768]{1,0:T(8,128)(2,1)S(1)}, u32[]{:S(2)}, u32[]{:S(2)}) collective-permute-start(bf16[96,768]{1,0:T(8,128)(2,1)S(1)} %add_convert_fusion.6), channel_id=1, source_target_pairs={{0,8},{4,12},{8,0},{12,4},{1,9},{5,13},{9,1},{13,5},{2,10},{6,14},... | collective-permute-start | bytes 442376 | tf_op jit(solution)/shard_map/ppermute | solution.py:285
  61.6 10.6 %collective-permute-start.16 = (bf16[128,768]{1,0:T(8,128)(2,1)S(1)}, bf16[128,768]{1,0:T(8,128)(2,1)S(1)}, u32[]{:S(2)}, u32[]{:S(2)}) collective-permute-start(bf16[128,768]{1,0:T(8,128)(2,1)S(1)} %get-tuple-element.69), channel_id=1, source_target_pairs={{0,2},{1,3},{2,0},{3,1},{4,6},{5,7},{6,4},{7,5},{8,10},{9,11},{10,... | collective-permute-start | bytes 589832 | tf_op jit(solution)/shard_map/ppermute | solution.py:285
  64.6 11.4 %collective-permute-start.21 = (bf16[128,768]{1,0:T(8,128)(2,1)S(1)}, bf16[128,768]{1,0:T(8,128)(2,1)S(1)}, u32[]{:S(2)}, u32[]{:S(2)}) collective-permute-start(bf16[128,768]{1,0:T(8,128)(2,1)S(1)} %add_convert_fusion.2), channel_id=1, source_target_pairs={{0,8},{4,12},{8,0},{12,4},{1,9},{5,13},{9,1},{13,5},{2,10},{6,14},... | collective-permute-start | bytes 589832 | tf_op jit(solution)/shard_map/ppermute | solution.py:285
  69.9 7.6 %collective-permute-start.23 = (bf16[96,768]{1,0:T(8,128)(2,1)S(1)}, bf16[96,768]{1,0:T(8,128)(2,1)S(1)}, u32[]{:S(2)}, u32[]{:S(2)}) collective-permute-start(bf16[96,768]{1,0:T(8,128)(2,1)S(1)} %add_convert_fusion.5.mine_ref), channel_id=1, source_target_pairs={{0,4},{4,0},{8,12},{12,8},{1,5},{5,1},{9,13},{13,9},{2,6},{6,2},{1... | collective-permute-start | bytes 442376 | tf_op jit(solution)/shard_map/ppermute | solution.py:285
  (5 other events, 29.3 us)

commit v20 on v19

--- a/solution.py
+++ b/solution.py
@@ -372,7 +372,7 @@
         sums[i] = over_dp([[x] for x in runs[i]], keep) + sent_near[-1:]
     for mask in masks(n)[1:]:
         for i in range(0, n, 2 * mask):
-            sent = after(add(*sums[i + mask]).astype(BF16), first, *sent_near)
+            sent = after(add(*sums[i + mask]).astype(BF16), first)
             sums[i].append(partner(sent, "labels", mask))
     return sums[0]
 

time: 78.5 us -> 78.5 us (level)
  starting transfers between devices: 26.8 us -> 25.3 us
  waiting for transfers between devices: 29.5 us -> 31 us
    ppermute x24, waiting for transfers between devices: 29.5 us -> 31 us  [partner(): lax.ppermute(x, axis, [(i, i ^ mask) for i in range(lax.axis_size(axis))])]
    ppermute x24, starting transfers between devices: 26.8 us -> 25.3 us  [partner(): lax.ppermute(x, axis, [(i, i ^ mask) for i in range(lax.axis_size(axis))])]
  transfers between devices with their start and end apart: 24 -> 24, of which waited for: 14 -> 13; matrix products, arithmetic and copies ran while one was open for 1% -> 1% of each run, Pallas kernels for 13% -> 13%
where the time goes in v20:
time: 78.5 us; the launch traced here: 78.4 us
  waiting for transfers between devices  31 us (39%)
  starting transfers between devices  25.3 us (32%)
  Pallas kernels  16.7 us (21%)
  local copies, waits for them, and re-layouts  3.52 us (4%)
  other arithmetic  1.09 us (1%)
    ppermute x24, waiting for transfers between devices, partner(): lax.ppermute(x, axis, [(i, i ^ mask) for i in range(lax.axis_size(axis))])  31 us
    ppermute x24, starting transfers between devices, partner(): lax.ppermute(x, axis, [(i, i ^ mask) for i in range(lax.axis_size(axis))])  25.3 us
    pallas_call x8, Pallas kernels, call(): pl.pallas_call(kernel, in_specs=[space] * len(args), out_specs=jax.tree.m...  16.7 us
    unnamed x10, local copies, waits for them, and re-layouts  3.52 us
  transfers between devices with their start and end apart: 24, of which 13 were waited for; matrix products, arithmetic and copies ran while one was open for 1% of the time, Pallas kernels for 13%

profile of v20, /device:TPU:0, one launch (start us, length us, event | category | flops | bytes accessed | tf_op | source)
XLA Modules:
  0.0 78.4 jit_solution(12694147042601506427)
XLA Ops:
  1.1 2.6 %collective-permute-start.5 = (bf16[192,768]{1,0:T(8,128)(2,1)}, bf16[192,768]{1,0:T(8,128)(2,1)S(1)}, u32[]{:S(2)}, u32[]{:S(2)}) collective-permute-start(bf16[192,768]{1,0:T(8,128)(2,1)} %shard_ref.1), channel_id=1, source_target_pairs={{0,2},{1,3},{2,0},{3,1},{4,6},{5,7},{6,4},{7,5},{8,10},{9,11},{10,... | collective-permute-start | bytes 884744 | tf_op jit(solution)/shard_map/ppermute | solution.py:285
  3.7 1.6 %own_block.1.refs_0_ = bf16[136,768]{1,0:T(8,128)(2,1)} custom-call(bf16[128,768]{1,0:T(8,128)(2,1)} %feats_ref.1, s32[4,128]{1,0:T(4,128)} %bitcast.5, s32[4,128]{1,0:T(4,128)} %bitcast.6, s32[4,128]{1,0:T(4,128)} %bitcast.7), custom_call_target="tpu_custom_call" | custom-call | bytes 1048576 | tf_op jit(solution)/shard_map/own_block/pallas_call | solution.py:192
  5.4 2.7 %collective-permute-start.1 = (bf16[136,768]{1,0:T(8,128)(2,1)}, bf16[136,768]{1,0:T(8,128)(2,1)S(1)}, u32[]{:S(2)}, u32[]{:S(2)}) collective-permute-start(bf16[136,768]{1,0:T(8,128)(2,1)} %own_block.1.refs_0_), channel_id=1, source_target_pairs={{0,8},{4,12},{8,0},{12,4},{1,9},{5,13},{9,1},{13,5},{2,10},{6,14},... | collective-permute-start | bytes 626696 | tf_op jit(solution)/shard_map/ppermute | solution.py:285
  8.6 1.6 %collective-permute-start = (bf16[136,768]{1,0:T(8,128)(2,1)}, bf16[136,768]{1,0:T(8,128)(2,1)S(1)}, u32[]{:S(2)}, u32[]{:S(2)}) collective-permute-start(bf16[136,768]{1,0:T(8,128)(2,1)} %own_block.1.refs_0_), channel_id=1, source_target_pairs={{0,4},{4,0},{8,12},{12,8},{1,5},{5,1},{9,13},{13,9},{2,6},{6,2},{1... | collective-permute-start | bytes 626696 | tf_op jit(solution)/shard_map/ppermute | solution.py:285
  10.1 1.7 %collective-permute-done.5.refs_8_ = bf16[192,768]{1,0:T(8,128)(2,1)S(1)} collective-permute-done((bf16[192,768]{1,0:T(8,128)(2,1)}, bf16[192,768]{1,0:T(8,128)(2,1)S(1)}, u32[]{:S(2)}, u32[]{:S(2)}) %collective-permute-start.5) | collective-permute-done | bytes 294944 | tf_op jit(solution)/shard_map/ppermute | solution.py:285
  11.8 1.1 %copy-done.3 = bf16[1024,768]{1,0:T(8,128)(2,1)} copy-done((bf16[1024,768]{1,0:T(8,128)(2,1)}, bf16[1024,768]{1,0:T(8,128)(2,1)S(1)}, u32[]{:S(2)}) %copy-start.3) | copy-done | bytes 1572888
  13.4 1.4 %copy-done = bf16[1024,768]{1,0:T(8,128)(2,1)S(1)} copy-done((bf16[1024,768]{1,0:T(8,128)(2,1)S(1)}, bf16[1024,768]{1,0:T(8,128)(2,1)}, u32[]{:S(2)}) %copy-start) | copy-done | bytes 1572888
  15.9 2.4 %collective-permute-done.1.refs_2_ = bf16[136,768]{1,0:T(8,128)(2,1)S(1)} collective-permute-done((bf16[136,768]{1,0:T(8,128)(2,1)}, bf16[136,768]{1,0:T(8,128)(2,1)S(1)}, u32[]{:S(2)}, u32[]{:S(2)}) %collective-permute-start.1) | collective-permute-done | bytes 208928 | tf_op jit(solution)/shard_map/ppermute | solution.py:285
  18.8 1.4 %collective-permute-start.4 = (bf16[136,768]{1,0:T(8,128)(2,1)S(1)}, bf16[136,768]{1,0:T(8,128)(2,1)S(1)}, u32[]{:S(2)}, u32[]{:S(2)}) collective-permute-start(bf16[136,768]{1,0:T(8,128)(2,1)S(1)} %collective-permute-done.1.refs_2_), channel_id=1, source_target_pairs={{0,2},{1,3},{2,0},{3,1},{4,6},{5,7},{6,4},{7,5},{8,10},{9,11},{10,... | collective-permute-start | bytes 626696 | tf_op jit(solution)/shard_map/ppermute | solution.py:285
  20.5 1.8 %collective-permute-start.8 = (bf16[136,768]{1,0:T(8,128)(2,1)S(1)}, bf16[136,768]{1,0:T(8,128)(2,1)S(1)}, u32[]{:S(2)}, u32[]{:S(2)}) collective-permute-start(bf16[136,768]{1,0:T(8,128)(2,1)S(1)} %collective-permute-done.2.refs_1_), channel_id=1, source_target_pairs={{0,4},{4,0},{8,12},{12,8},{1,5},{5,1},{9,13},{13,9},{2,6},{6,2},{1... | collective-permute-start | bytes 626696 | tf_op jit(solution)/shard_map/ppermute | solution.py:285
  22.3 2.4 %collective-permute-done.4.refs_3_ = bf16[136,768]{1,0:T(8,128)(2,1)S(1)} collective-permute-done((bf16[136,768]{1,0:T(8,128)(2,1)S(1)}, bf16[136,768]{1,0:T(8,128)(2,1)S(1)}, u32[]{:S(2)}, u32[]{:S(2)}) %collective-permute-start.4) | collective-permute-done | bytes 208928 | tf_op jit(solution)/shard_map/ppermute | solution.py:285
  24.7 2.8 %collective-permute-done.9.refs_2_ = bf16[136,768]{1,0:T(8,128)(2,1)S(1)} collective-permute-done((bf16[136,768]{1,0:T(8,128)(2,1)S(1)}, bf16[136,768]{1,0:T(8,128)(2,1)S(1)}, u32[]{:S(2)}, u32[]{:S(2)}) %collective-permute-start.9) | collective-permute-done | bytes 208928 | tf_op jit(solution)/shard_map/ppermute | solution.py:285
  27.5 1.2 %collective-permute-start.10 = (bf16[136,768]{1,0:T(8,128)(2,1)S(1)}, bf16[136,768]{1,0:T(8,128)(2,1)S(1)}, u32[]{:S(2)}, u32[]{:S(2)}) collective-permute-start(bf16[136,768]{1,0:T(8,128)(2,1)S(1)} %collective-permute-done.9.refs_2_), channel_id=1, source_target_pairs={{0,2},{1,3},{2,0},{3,1},{4,6},{5,7},{6,4},{7,5},{8,10},{9,11},{10,... | collective-permute-start | bytes 626696 | tf_op jit(solution)/shard_map/ppermute | solution.py:285
  28.7 5.4 %pair_work.2 = (bf16[128,768]{1,0:T(8,128)(2,1)S(1)}, bf16[128,768]{1,0:T(8,128)(2,1)S(1)}, bf16[128,768]{1,0:T(8,128)(2,1)S(1)}, bf16[128,768]{1,0:T(8,128)(2,1...) custom-call(bf16[136,768]{1,0:T(8,128)(2,1)S(1)} %copy-done.2, ...), custom_call_target="tpu_custom_call" | custom-call | flops 3623878656 | bytes 8388608 | tf_op jit(solution)/shard_map/pair_work/pallas_call | solution.py:192
  34.1 5.6 %pair_work.3 = (bf16[128,768]{1,0:T(8,128)(2,1)S(1)}, bf16[128,768]{1,0:T(8,128)(2,1)S(1)}, bf16[128,768]{1,0:T(8,128)(2,1)S(1)}, bf16[128,768]{1,0:T(8,128)(2,1...) custom-call(bf16[136,768]{1,0:T(8,128)(2,1)S(1)} %collective-permute, ...), custom_call_target="tpu_custom_call" | custom-call | flops 3623878656 | bytes 8388608 | tf_op jit(solution)/shard_map/pair_work/pallas_call | solution.py:192
  41.5 1.4 %collective-permute-start.14 = (bf16[128,768]{1,0:T(8,128)(2,1)S(1)}, bf16[128,768]{1,0:T(8,128)(2,1)S(1)}, u32[]{:S(2)}, u32[]{:S(2)}) collective-permute-start(bf16[128,768]{1,0:T(8,128)(2,1)S(1)} %get-tuple-element.66), channel_id=1, source_target_pairs={{0,4},{4,0},{8,12},{12,8},{1,5},{5,1},{9,13},{13,9},{2,6},{6,2},{1... | collective-permute-start | bytes 589832 | tf_op jit(solution)/shard_map/ppermute | solution.py:285
  44.4 1.2 %collective-permute-start.17 = (bf16[128,768]{1,0:T(8,128)(2,1)S(1)}, bf16[128,768]{1,0:T(8,128)(2,1)S(1)}, u32[]{:S(2)}, u32[]{:S(2)}) collective-permute-start(bf16[128,768]{1,0:T(8,128)(2,1)S(1)} %get-tuple-element.72), channel_id=1, source_target_pairs={{0,2},{1,3},{2,0},{3,1},{4,6},{5,7},{6,4},{7,5},{8,10},{9,11},{10,... | collective-permute-start | bytes 589832 | tf_op jit(solution)/shard_map/ppermute | solution.py:285
  45.7 3.6 %collective-permute-done.14 = bf16[128,768]{1,0:T(8,128)(2,1)S(1)} collective-permute-done((bf16[128,768]{1,0:T(8,128)(2,1)S(1)}, bf16[128,768]{1,0:T(8,128)(2,1)S(1)}, u32[]{:S(2)}, u32[]{:S(2)}) %collective-permute-start.14) | collective-permute-done | bytes 196640 | tf_op jit(solution)/shard_map/ppermute | solution.py:285
  50.1 2.4 %collective-permute-done.13 = bf16[128,768]{1,0:T(8,128)(2,1)S(1)} collective-permute-done((bf16[128,768]{1,0:T(8,128)(2,1)S(1)}, bf16[128,768]{1,0:T(8,128)(2,1)S(1)}, u32[]{:S(2)}, u32[]{:S(2)}) %collective-permute-start.13) | collective-permute-done | bytes 196640 | tf_op jit(solution)/shard_map/ppermute | solution.py:285
  54.3 2.9 %collective-permute-done.17 = bf16[128,768]{1,0:T(8,128)(2,1)S(1)} collective-permute-done((bf16[128,768]{1,0:T(8,128)(2,1)S(1)}, bf16[128,768]{1,0:T(8,128)(2,1)S(1)}, u32[]{:S(2)}, u32[]{:S(2)}) %collective-permute-start.17) | collective-permute-done | bytes 196640 | tf_op jit(solution)/shard_map/ppermute | solution.py:285
  57.9 1.3 %collective-permute-done.20 = bf16[96,768]{1,0:T(8,128)(2,1)S(1)} collective-permute-done((bf16[96,768]{1,0:T(8,128)(2,1)S(1)}, bf16[96,768]{1,0:T(8,128)(2,1)S(1)}, u32[]{:S(2)}, u32[]{:S(2)}) %collective-permute-start.20) | collective-permute-done | bytes 147488 | tf_op jit(solution)/shard_map/ppermute | solution.py:285
  59.2 2.4 %collective-permute-start.22 = (bf16[96,768]{1,0:T(8,128)(2,1)S(1)}, bf16[96,768]{1,0:T(8,128)(2,1)S(1)}, u32[]{:S(2)}, u32[]{:S(2)}) collective-permute-start(bf16[96,768]{1,0:T(8,128)(2,1)S(1)} %add_convert_fusion.6), channel_id=1, source_target_pairs={{0,8},{4,12},{8,0},{12,4},{1,9},{5,13},{9,1},{13,5},{2,10},{6,14},... | collective-permute-start | bytes 442376 | tf_op jit(solution)/shard_map/ppermute | solution.py:285
  63.6 8.6 %collective-permute-done.22 = bf16[96,768]{1,0:T(8,128)(2,1)S(1)} collective-permute-done((bf16[96,768]{1,0:T(8,128)(2,1)S(1)}, bf16[96,768]{1,0:T(8,128)(2,1)S(1)}, u32[]{:S(2)}, u32[]{:S(2)}) %collective-permute-start.22) | collective-permute-done | bytes 147488 | tf_op jit(solution)/shard_map/ppermute | solution.py:285
  72.7 1.8 %grad_label_work.3 = bf16[1024,768]{1,0:T(8,128)(2,1)} custom-call(f32[512,128]{1,0:T(8,128)S(1)} %get-tuple-element.49.refs_0_, f32[512,128]{1,0:T(8,128)S(1)} %get-tuple-element.55.refs_1_, s32[512,128]{1,0:T(8,128)S(1)} %get-tuple-element.56.refs_2_, s32[512,128]{1,0:T(8,128)S(1)} %get-tuple-element.57.refs_3_, ...), custom_call_target="tpu_custom_call" | custom-call | flops 805306368 | bytes 4194304 | tf_op jit(solution)/shard_map/grad_label_work/pallas_call | solution.py:192
  (49 shorter events, 16.4 us)
Async XLA Ops:
  0.6 11.2 %collective-permute-start.3 = (bf16[1024,768]{1,0:T(8,128)(2,1)}, bf16[1024,768]{1,0:T(8,128)(2,1)S(1)}, u32[]{:S(2)}, u32[]{:S(2)}) collective-permute-start(bf16[1024,768]{1,0:T(8,128)(2,1)} %label_ref), channel_id=1, source_target_pairs={{0,1},{1,0},{2,3},{3,2},{4,5},{5,4},{6,7},{7,6},{8,9},{9,8},{10,11... | collective-permute-start | bytes 4718600 | tf_op jit(solution)/shard_map/ppermute | solution.py:285
  1.1 10.6 %collective-permute-start.5 = (bf16[192,768]{1,0:T(8,128)(2,1)}, bf16[192,768]{1,0:T(8,128)(2,1)S(1)}, u32[]{:S(2)}, u32[]{:S(2)}) collective-permute-start(bf16[192,768]{1,0:T(8,128)(2,1)} %shard_ref.1), channel_id=1, source_target_pairs={{0,2},{1,3},{2,0},{3,1},{4,6},{5,7},{6,4},{7,5},{8,10},{9,11},{10,... | collective-permute-start | bytes 884744 | tf_op jit(solution)/shard_map/ppermute | solution.py:285
  5.4 13.0 %collective-permute-start.1 = (bf16[136,768]{1,0:T(8,128)(2,1)}, bf16[136,768]{1,0:T(8,128)(2,1)S(1)}, u32[]{:S(2)}, u32[]{:S(2)}) collective-permute-start(bf16[136,768]{1,0:T(8,128)(2,1)} %own_block.1.refs_0_), channel_id=1, source_target_pairs={{0,8},{4,12},{8,0},{12,4},{1,9},{5,13},{9,1},{13,5},{2,10},{6,14},... | collective-permute-start | bytes 626696 | tf_op jit(solution)/shard_map/ppermute | solution.py:285
  8.0 10.3 %collective-permute-start.2 = (bf16[136,768]{1,0:T(8,128)(2,1)}, bf16[136,768]{1,0:T(8,128)(2,1)S(1)}, u32[]{:S(2)}, u32[]{:S(2)}) collective-permute-start(bf16[136,768]{1,0:T(8,128)(2,1)} %own_block.1.refs_0_), channel_id=1, source_target_pairs={{0,2},{1,3},{2,0},{3,1},{4,6},{5,7},{6,4},{7,5},{8,10},{9,11},{10,... | collective-permute-start | bytes 626696 | tf_op jit(solution)/shard_map/ppermute | solution.py:285
  8.6 10.2 %collective-permute-start = (bf16[136,768]{1,0:T(8,128)(2,1)}, bf16[136,768]{1,0:T(8,128)(2,1)S(1)}, u32[]{:S(2)}, u32[]{:S(2)}) collective-permute-start(bf16[136,768]{1,0:T(8,128)(2,1)} %own_block.1.refs_0_), channel_id=1, source_target_pairs={{0,4},{4,0},{8,12},{12,8},{1,5},{5,1},{9,13},{13,9},{2,6},{6,2},{1... | collective-permute-start | bytes 626696 | tf_op jit(solution)/shard_map/ppermute | solution.py:285
  11.8 8.7 %collective-permute-start.6 = (bf16[192,768]{1,0:T(8,128)(2,1)}, bf16[192,768]{1,0:T(8,128)(2,1)S(1)}, u32[]{:S(2)}, u32[]{:S(2)}) collective-permute-start(bf16[192,768]{1,0:T(8,128)(2,1)} %shard_ref.1), channel_id=1, source_target_pairs={{0,1},{1,0},{2,3},{3,2},{4,5},{5,4},{6,7},{7,6},{8,9},{9,8},{10,11... | collective-permute-start | bytes 884744 | tf_op jit(solution)/shard_map/ppermute | solution.py:285
  12.9 7.6 %collective-permute-start.7 = (bf16[192,768]{1,0:T(8,128)(2,1)S(1)}, bf16[192,768]{1,0:T(8,128)(2,1)S(1)}, u32[]{:S(2)}, u32[]{:S(2)}) collective-permute-start(bf16[192,768]{1,0:T(8,128)(2,1)S(1)} %collective-permute-done.5.refs_8_), channel_id=1, source_target_pairs={{0,1},{1,0},{2,3},{3,2},{4,5},{5,4},{6,7},{7,6},{8,9},{9,8},{10,11... | collective-permute-start | bytes 884744 | tf_op jit(solution)/shard_map/ppermute | solution.py:285
  18.8 5.9 %collective-permute-start.4 = (bf16[136,768]{1,0:T(8,128)(2,1)S(1)}, bf16[136,768]{1,0:T(8,128)(2,1)S(1)}, u32[]{:S(2)}, u32[]{:S(2)}) collective-permute-start(bf16[136,768]{1,0:T(8,128)(2,1)S(1)} %collective-permute-done.1.refs_2_), channel_id=1, source_target_pairs={{0,2},{1,3},{2,0},{3,1},{4,6},{5,7},{6,4},{7,5},{8,10},{9,11},{10,... | collective-permute-start | bytes 626696 | tf_op jit(solution)/shard_map/ppermute | solution.py:285
  20.2 7.2 %collective-permute-start.9 = (bf16[136,768]{1,0:T(8,128)(2,1)S(1)}, bf16[136,768]{1,0:T(8,128)(2,1)S(1)}, u32[]{:S(2)}, u32[]{:S(2)}) collective-permute-start(bf16[136,768]{1,0:T(8,128)(2,1)S(1)} %collective-permute-done.1.refs_2_), channel_id=1, source_target_pairs={{0,4},{4,0},{8,12},{12,8},{1,5},{5,1},{9,13},{13,9},{2,6},{6,2},{1... | collective-permute-start | bytes 626696 | tf_op jit(solution)/shard_map/ppermute | solution.py:285
  20.5 13.6 %collective-permute-start.8 = (bf16[136,768]{1,0:T(8,128)(2,1)S(1)}, bf16[136,768]{1,0:T(8,128)(2,1)S(1)}, u32[]{:S(2)}, u32[]{:S(2)}) collective-permute-start(bf16[136,768]{1,0:T(8,128)(2,1)S(1)} %collective-permute-done.2.refs_1_), channel_id=1, source_target_pairs={{0,4},{4,0},{8,12},{12,8},{1,5},{5,1},{9,13},{13,9},{2,6},{6,2},{1... | collective-permute-start | bytes 626696 | tf_op jit(solution)/shard_map/ppermute | solution.py:285
  27.5 6.6 %collective-permute-start.10 = (bf16[136,768]{1,0:T(8,128)(2,1)S(1)}, bf16[136,768]{1,0:T(8,128)(2,1)S(1)}, u32[]{:S(2)}, u32[]{:S(2)}) collective-permute-start(bf16[136,768]{1,0:T(8,128)(2,1)S(1)} %collective-permute-done.9.refs_2_), channel_id=1, source_target_pairs={{0,2},{1,3},{2,0},{3,1},{4,6},{5,7},{6,4},{7,5},{8,10},{9,11},{10,... | collective-permute-start | bytes 626696 | tf_op jit(solution)/shard_map/ppermute | solution.py:285
  39.7 3.1 %collective-permute-start.12 = (bf16[2,192,768]{2,1,0:T(8,128)(2,1)S(1)}, bf16[2,192,768]{2,1,0:T(8,128)(2,1)S(1)}, u32[]{:S(2)}, u32[]{:S(2)}) collective-permute-start(bf16[2,192,768]{2,1,0:T(8,128)(2,1)S(1)} %get-tuple-element.63), channel_id=1, source_target_pairs={{0,1},{1,0},{2,3},{3,2},{4,5},{5,4},{6,7},{7,6},{8,9},{9,8},{10,11... | collective-permute-start | bytes 1769480 | tf_op jit(solution)/shard_map/ppermute | solution.py:285
  40.9 31.8 %collective-permute-start.11 = (bf16[1024,768]{1,0:T(8,128)(2,1)S(1)}, bf16[1024,768]{1,0:T(8,128)(2,1)S(1)}, u32[]{:S(2)}, u32[]{:S(2)}) collective-permute-start(bf16[1024,768]{1,0:T(8,128)(2,1)S(1)} %grad_label_work.2), channel_id=1, source_target_pairs={{0,1},{1,0},{2,3},{3,2},{4,5},{5,4},{6,7},{7,6},{8,9},{9,8},{10,11... | collective-permute-start | bytes 4718600 | tf_op jit(solution)/shard_map/ppermute | solution.py:285
  41.5 7.8 %collective-permute-start.14 = (bf16[128,768]{1,0:T(8,128)(2,1)S(1)}, bf16[128,768]{1,0:T(8,128)(2,1)S(1)}, u32[]{:S(2)}, u32[]{:S(2)}) collective-permute-start(bf16[128,768]{1,0:T(8,128)(2,1)S(1)} %get-tuple-element.66), channel_id=1, source_target_pairs={{0,4},{4,0},{8,12},{12,8},{1,5},{5,1},{9,13},{13,9},{2,6},{6,2},{1... | collective-permute-start | bytes 589832 | tf_op jit(solution)/shard_map/ppermute | solution.py:285
  43.0 10.0 %collective-permute-start.15 = (bf16[192,768]{1,0:T(8,128)(2,1)S(1)}, bf16[192,768]{1,0:T(8,128)(2,1)S(1)}, u32[]{:S(2)}, u32[]{:S(2)}) collective-permute-start(bf16[192,768]{1,0:T(8,128)(2,1)S(1)} %fusion), channel_id=1, source_target_pairs={{0,2},{1,3},{2,0},{3,1},{4,6},{5,7},{6,4},{7,5},{8,10},{9,11},{10,... | collective-permute-start | bytes 884744 | tf_op jit(solution)/shard_map/ppermute | solution.py:285
  43.5 9.0 %collective-permute-start.13 = (bf16[128,768]{1,0:T(8,128)(2,1)S(1)}, bf16[128,768]{1,0:T(8,128)(2,1)S(1)}, u32[]{:S(2)}, u32[]{:S(2)}) collective-permute-start(bf16[128,768]{1,0:T(8,128)(2,1)S(1)} %get-tuple-element.65), channel_id=1, source_target_pairs={{0,4},{4,0},{8,12},{12,8},{1,5},{5,1},{9,13},{13,9},{2,6},{6,2},{1... | collective-permute-start | bytes 589832 | tf_op jit(solution)/shard_map/ppermute | solution.py:285
  44.4 12.7 %collective-permute-start.17 = (bf16[128,768]{1,0:T(8,128)(2,1)S(1)}, bf16[128,768]{1,0:T(8,128)(2,1)S(1)}, u32[]{:S(2)}, u32[]{:S(2)}) collective-permute-start(bf16[128,768]{1,0:T(8,128)(2,1)S(1)} %get-tuple-element.72), channel_id=1, source_target_pairs={{0,2},{1,3},{2,0},{3,1},{4,6},{5,7},{6,4},{7,5},{8,10},{9,11},{10,... | collective-permute-start | bytes 589832 | tf_op jit(solution)/shard_map/ppermute | solution.py:285
  49.3 12.3 %collective-permute-start.19 = (bf16[128,768]{1,0:T(8,128)(2,1)S(1)}, bf16[128,768]{1,0:T(8,128)(2,1)S(1)}, u32[]{:S(2)}, u32[]{:S(2)}) collective-permute-start(bf16[128,768]{1,0:T(8,128)(2,1)S(1)} %add_convert_fusion.3), channel_id=1, source_target_pairs={{0,2},{1,3},{2,0},{3,1},{4,6},{5,7},{6,4},{7,5},{8,10},{9,11},{10,... | collective-permute-start | bytes 589832 | tf_op jit(solution)/shard_map/ppermute | solution.py:285
  53.1 6.0 %collective-permute-start.20 = (bf16[96,768]{1,0:T(8,128)(2,1)S(1)}, bf16[96,768]{1,0:T(8,128)(2,1)S(1)}, u32[]{:S(2)}, u32[]{:S(2)}) collective-permute-start(bf16[96,768]{1,0:T(8,128)(2,1)S(1)} %get-tuple-element.76), channel_id=1, source_target_pairs={{0,4},{4,0},{8,12},{12,8},{1,5},{5,1},{9,13},{13,9},{2,6},{6,2},{1... | collective-permute-start | bytes 442376 | tf_op jit(solution)/shard_map/ppermute | solution.py:285
  57.2 17.4 %collective-permute-start.18 = (bf16[128,768]{1,0:T(8,128)(2,1)S(1)}, bf16[128,768]{1,0:T(8,128)(2,1)S(1)}, u32[]{:S(2)}, u32[]{:S(2)}) collective-permute-start(bf16[128,768]{1,0:T(8,128)(2,1)S(1)} %add_convert_fusion.4), channel_id=1, source_target_pairs={{0,4},{4,0},{8,12},{12,8},{1,5},{5,1},{9,13},{13,9},{2,6},{6,2},{1... | collective-permute-start | bytes 589832 | tf_op jit(solution)/shard_map/ppermute | solution.py:285
  59.2 13.1 %collective-permute-start.22 = (bf16[96,768]{1,0:T(8,128)(2,1)S(1)}, bf16[96,768]{1,0:T(8,128)(2,1)S(1)}, u32[]{:S(2)}, u32[]{:S(2)}) collective-permute-start(bf16[96,768]{1,0:T(8,128)(2,1)S(1)} %add_convert_fusion.6), channel_id=1, source_target_pairs={{0,8},{4,12},{8,0},{12,4},{1,9},{5,13},{9,1},{13,5},{2,10},{6,14},... | collective-permute-start | bytes 442376 | tf_op jit(solution)/shard_map/ppermute | solution.py:285
  61.6 13.0 %collective-permute-start.16 = (bf16[128,768]{1,0:T(8,128)(2,1)S(1)}, bf16[128,768]{1,0:T(8,128)(2,1)S(1)}, u32[]{:S(2)}, u32[]{:S(2)}) collective-permute-start(bf16[128,768]{1,0:T(8,128)(2,1)S(1)} %get-tuple-element.69), channel_id=1, source_target_pairs={{0,2},{1,3},{2,0},{3,1},{4,6},{5,7},{6,4},{7,5},{8,10},{9,11},{10,... | collective-permute-start | bytes 589832 | tf_op jit(solution)/shard_map/ppermute | solution.py:285
  62.7 12.9 %collective-permute-start.21 = (bf16[128,768]{1,0:T(8,128)(2,1)S(1)}, bf16[128,768]{1,0:T(8,128)(2,1)S(1)}, u32[]{:S(2)}, u32[]{:S(2)}) collective-permute-start(bf16[128,768]{1,0:T(8,128)(2,1)S(1)} %add_convert_fusion.2), channel_id=1, source_target_pairs={{0,8},{4,12},{8,0},{12,4},{1,9},{5,13},{9,1},{13,5},{2,10},{6,14},... | collective-permute-start | bytes 589832 | tf_op jit(solution)/shard_map/ppermute | solution.py:285
  72.3 5.2 %collective-permute-start.23 = (bf16[96,768]{1,0:T(8,128)(2,1)S(1)}, bf16[96,768]{1,0:T(8,128)(2,1)S(1)}, u32[]{:S(2)}, u32[]{:S(2)}) collective-permute-start(bf16[96,768]{1,0:T(8,128)(2,1)S(1)} %add_convert_fusion.5.mine_ref), channel_id=1, source_target_pairs={{0,4},{4,0},{8,12},{12,8},{1,5},{5,1},{9,13},{13,9},{2,6},{6,2},{1... | collective-permute-start | bytes 442376 | tf_op jit(solution)/shard_map/ppermute | solution.py:285
  (5 other events, 29.3 us)

commit v21 on v20

--- a/solution.py
+++ b/solution.py
@@ -445,7 +445,7 @@
         even, odd = works[-1]["shares"]
         got, share_terms, sent = dp_terms(even, odd)
         near_last, *far_last = backs[n_labels - 1]
-        got_last = [partner(x, "labels", 1) for x in (after(near_last, sent), *far_last)]
+        got_last = [partner(after(x, sent), "labels", 1) for x in (near_last, *far_last)]
         keep, first, share = sum_shares(even, got, share_terms, *got_last)
         terms = reduce_runs(backs, got_last, sent, keep, first)
         other = partner(grad_label_work(works, 2, 1, label_weight.shape), "dp", 1)

time: 78.5 us -> 80.7 us (1.028)
  waiting for transfers between devices: 31 us -> 34 us
  starting transfers between devices: 25.3 us -> 24.4 us
    ppermute x24, waiting for transfers between devices: 31 us -> 34 us  [partner(): lax.ppermute(x, axis, [(i, i ^ mask) for i in range(lax.axis_size(axis))])]
    ppermute x24, starting transfers between devices: 25.3 us -> 24.4 us  [partner(): lax.ppermute(x, axis, [(i, i ^ mask) for i in range(lax.axis_size(axis))])]
where the time goes in v21:
time: 80.7 us; the launch traced here: 80.5 us
  waiting for transfers between devices  34 us (42%)
  starting transfers between devices  24.4 us (30%)
  Pallas kernels  16.7 us (21%)
  local copies, waits for them, and re-layouts  3.52 us (4%)
  other arithmetic  1.08 us (1%)
    ppermute x24, waiting for transfers between devices, partner(): lax.ppermute(x, axis, [(i, i ^ mask) for i in range(lax.axis_size(axis))])  34 us
    ppermute x24, starting transfers between devices, partner(): lax.ppermute(x, axis, [(i, i ^ mask) for i in range(lax.axis_size(axis))])  24.4 us
    pallas_call x8, Pallas kernels, call(): pl.pallas_call(kernel, in_specs=[space] * len(args), out_specs=jax.tree.m...  16.7 us
    unnamed x10, local copies, waits for them, and re-layouts  3.52 us
  transfers between devices with their start and end apart: 24, of which 13 were waited for; matrix products, arithmetic and copies ran while one was open for 1% of the time, Pallas kernels for 13%

profile of v21, /device:TPU:0, one launch (start us, length us, event | category | flops | bytes accessed | tf_op | source)
XLA Modules:
  0.0 80.5 jit_solution(631360102812463819)
XLA Ops:
  1.1 2.6 %collective-permute-start.5 = (bf16[192,768]{1,0:T(8,128)(2,1)}, bf16[192,768]{1,0:T(8,128)(2,1)S(1)}, u32[]{:S(2)}, u32[]{:S(2)}) collective-permute-start(bf16[192,768]{1,0:T(8,128)(2,1)} %shard_ref.1), channel_id=1, source_target_pairs={{0,2},{1,3},{2,0},{3,1},{4,6},{5,7},{6,4},{7,5},{8,10},{9,11},{10,... | collective-permute-start | bytes 884744 | tf_op jit(solution)/shard_map/ppermute | solution.py:285
  3.7 1.6 %own_block.1.refs_0_ = bf16[136,768]{1,0:T(8,128)(2,1)} custom-call(bf16[128,768]{1,0:T(8,128)(2,1)} %feats_ref.1, s32[4,128]{1,0:T(4,128)} %bitcast.5, s32[4,128]{1,0:T(4,128)} %bitcast.6, s32[4,128]{1,0:T(4,128)} %bitcast.7), custom_call_target="tpu_custom_call" | custom-call | bytes 1048576 | tf_op jit(solution)/shard_map/own_block/pallas_call | solution.py:192
  5.4 2.7 %collective-permute-start.1 = (bf16[136,768]{1,0:T(8,128)(2,1)}, bf16[136,768]{1,0:T(8,128)(2,1)S(1)}, u32[]{:S(2)}, u32[]{:S(2)}) collective-permute-start(bf16[136,768]{1,0:T(8,128)(2,1)} %own_block.1.refs_0_), channel_id=1, source_target_pairs={{0,8},{4,12},{8,0},{12,4},{1,9},{5,13},{9,1},{13,5},{2,10},{6,14},... | collective-permute-start | bytes 626696 | tf_op jit(solution)/shard_map/ppermute | solution.py:285
  8.6 1.6 %collective-permute-start = (bf16[136,768]{1,0:T(8,128)(2,1)}, bf16[136,768]{1,0:T(8,128)(2,1)S(1)}, u32[]{:S(2)}, u32[]{:S(2)}) collective-permute-start(bf16[136,768]{1,0:T(8,128)(2,1)} %own_block.1.refs_0_), channel_id=1, source_target_pairs={{0,4},{4,0},{8,12},{12,8},{1,5},{5,1},{9,13},{13,9},{2,6},{6,2},{1... | collective-permute-start | bytes 626696 | tf_op jit(solution)/shard_map/ppermute | solution.py:285
  10.1 1.7 %collective-permute-done.5.refs_8_ = bf16[192,768]{1,0:T(8,128)(2,1)S(1)} collective-permute-done((bf16[192,768]{1,0:T(8,128)(2,1)}, bf16[192,768]{1,0:T(8,128)(2,1)S(1)}, u32[]{:S(2)}, u32[]{:S(2)}) %collective-permute-start.5) | collective-permute-done | bytes 294944 | tf_op jit(solution)/shard_map/ppermute | solution.py:285
  13.4 1.4 %copy-done = bf16[1024,768]{1,0:T(8,128)(2,1)S(1)} copy-done((bf16[1024,768]{1,0:T(8,128)(2,1)S(1)}, bf16[1024,768]{1,0:T(8,128)(2,1)}, u32[]{:S(2)}) %copy-start) | copy-done | bytes 1572888
  15.9 2.4 %collective-permute-done.1.refs_2_ = bf16[136,768]{1,0:T(8,128)(2,1)S(1)} collective-permute-done((bf16[136,768]{1,0:T(8,128)(2,1)}, bf16[136,768]{1,0:T(8,128)(2,1)S(1)}, u32[]{:S(2)}, u32[]{:S(2)}) %collective-permute-start.1) | collective-permute-done | bytes 208928 | tf_op jit(solution)/shard_map/ppermute | solution.py:285
  18.8 1.4 %collective-permute-start.4 = (bf16[136,768]{1,0:T(8,128)(2,1)S(1)}, bf16[136,768]{1,0:T(8,128)(2,1)S(1)}, u32[]{:S(2)}, u32[]{:S(2)}) collective-permute-start(bf16[136,768]{1,0:T(8,128)(2,1)S(1)} %collective-permute-done.1.refs_2_), channel_id=1, source_target_pairs={{0,2},{1,3},{2,0},{3,1},{4,6},{5,7},{6,4},{7,5},{8,10},{9,11},{10,... | collective-permute-start | bytes 626696 | tf_op jit(solution)/shard_map/ppermute | solution.py:285
  20.5 1.8 %collective-permute-start.8 = (bf16[136,768]{1,0:T(8,128)(2,1)S(1)}, bf16[136,768]{1,0:T(8,128)(2,1)S(1)}, u32[]{:S(2)}, u32[]{:S(2)}) collective-permute-start(bf16[136,768]{1,0:T(8,128)(2,1)S(1)} %collective-permute-done.2.refs_1_), channel_id=1, source_target_pairs={{0,4},{4,0},{8,12},{12,8},{1,5},{5,1},{9,13},{13,9},{2,6},{6,2},{1... | collective-permute-start | bytes 626696 | tf_op jit(solution)/shard_map/ppermute | solution.py:285
  22.3 2.4 %collective-permute-done.4.refs_3_ = bf16[136,768]{1,0:T(8,128)(2,1)S(1)} collective-permute-done((bf16[136,768]{1,0:T(8,128)(2,1)S(1)}, bf16[136,768]{1,0:T(8,128)(2,1)S(1)}, u32[]{:S(2)}, u32[]{:S(2)}) %collective-permute-start.4) | collective-permute-done | bytes 208928 | tf_op jit(solution)/shard_map/ppermute | solution.py:285
  24.7 2.8 %collective-permute-done.9.refs_2_ = bf16[136,768]{1,0:T(8,128)(2,1)S(1)} collective-permute-done((bf16[136,768]{1,0:T(8,128)(2,1)S(1)}, bf16[136,768]{1,0:T(8,128)(2,1)S(1)}, u32[]{:S(2)}, u32[]{:S(2)}) %collective-permute-start.9) | collective-permute-done | bytes 208928 | tf_op jit(solution)/shard_map/ppermute | solution.py:285
  27.5 1.2 %collective-permute-start.10 = (bf16[136,768]{1,0:T(8,128)(2,1)S(1)}, bf16[136,768]{1,0:T(8,128)(2,1)S(1)}, u32[]{:S(2)}, u32[]{:S(2)}) collective-permute-start(bf16[136,768]{1,0:T(8,128)(2,1)S(1)} %collective-permute-done.9.refs_2_), channel_id=1, source_target_pairs={{0,2},{1,3},{2,0},{3,1},{4,6},{5,7},{6,4},{7,5},{8,10},{9,11},{10,... | collective-permute-start | bytes 626696 | tf_op jit(solution)/shard_map/ppermute | solution.py:285
  28.7 5.4 %pair_work.2 = (bf16[128,768]{1,0:T(8,128)(2,1)S(1)}, bf16[128,768]{1,0:T(8,128)(2,1)S(1)}, bf16[128,768]{1,0:T(8,128)(2,1)S(1)}, bf16[128,768]{1,0:T(8,128)(2,1...) custom-call(bf16[136,768]{1,0:T(8,128)(2,1)S(1)} %copy-done.2, ...), custom_call_target="tpu_custom_call" | custom-call | flops 3623878656 | bytes 8388608 | tf_op jit(solution)/shard_map/pair_work/pallas_call | solution.py:192
  34.1 5.6 %pair_work.3 = (bf16[128,768]{1,0:T(8,128)(2,1)S(1)}, bf16[128,768]{1,0:T(8,128)(2,1)S(1)}, bf16[128,768]{1,0:T(8,128)(2,1)S(1)}, bf16[128,768]{1,0:T(8,128)(2,1...) custom-call(bf16[136,768]{1,0:T(8,128)(2,1)S(1)} %collective-permute, ...), custom_call_target="tpu_custom_call" | custom-call | flops 3623878656 | bytes 8388608 | tf_op jit(solution)/shard_map/pair_work/pallas_call | solution.py:192
  41.9 1.5 %collective-permute-start.14 = (bf16[128,768]{1,0:T(8,128)(2,1)S(1)}, bf16[128,768]{1,0:T(8,128)(2,1)S(1)}, u32[]{:S(2)}, u32[]{:S(2)}) collective-permute-start(bf16[128,768]{1,0:T(8,128)(2,1)S(1)} %get-tuple-element.68), channel_id=1, source_target_pairs={{0,4},{4,0},{8,12},{12,8},{1,5},{5,1},{9,13},{13,9},{2,6},{6,2},{1... | collective-permute-start | bytes 589832 | tf_op jit(solution)/shard_map/ppermute | solution.py:285
  44.8 1.2 %collective-permute-start.17 = (bf16[128,768]{1,0:T(8,128)(2,1)S(1)}, bf16[128,768]{1,0:T(8,128)(2,1)S(1)}, u32[]{:S(2)}, u32[]{:S(2)}) collective-permute-start(bf16[128,768]{1,0:T(8,128)(2,1)S(1)} %get-tuple-element.74), channel_id=1, source_target_pairs={{0,2},{1,3},{2,0},{3,1},{4,6},{5,7},{6,4},{7,5},{8,10},{9,11},{10,... | collective-permute-start | bytes 589832 | tf_op jit(solution)/shard_map/ppermute | solution.py:285
  46.0 3.7 %collective-permute-done.14 = bf16[128,768]{1,0:T(8,128)(2,1)S(1)} collective-permute-done((bf16[128,768]{1,0:T(8,128)(2,1)S(1)}, bf16[128,768]{1,0:T(8,128)(2,1)S(1)}, u32[]{:S(2)}, u32[]{:S(2)}) %collective-permute-start.14) | collective-permute-done | bytes 196640 | tf_op jit(solution)/shard_map/ppermute | solution.py:285
  49.7 3.4 %collective-permute-done.13 = bf16[128,768]{1,0:T(8,128)(2,1)S(1)} collective-permute-done((bf16[128,768]{1,0:T(8,128)(2,1)S(1)}, bf16[128,768]{1,0:T(8,128)(2,1)S(1)}, u32[]{:S(2)}, u32[]{:S(2)}) %collective-permute-start.13) | collective-permute-done | bytes 196640 | tf_op jit(solution)/shard_map/ppermute | solution.py:285
  55.3 2.1 %collective-permute-done.17 = bf16[128,768]{1,0:T(8,128)(2,1)S(1)} collective-permute-done((bf16[128,768]{1,0:T(8,128)(2,1)S(1)}, bf16[128,768]{1,0:T(8,128)(2,1)S(1)}, u32[]{:S(2)}, u32[]{:S(2)}) %collective-permute-start.17) | collective-permute-done | bytes 196640 | tf_op jit(solution)/shard_map/ppermute | solution.py:285
  58.6 2.0 %collective-permute-done.20 = bf16[96,768]{1,0:T(8,128)(2,1)S(1)} collective-permute-done((bf16[96,768]{1,0:T(8,128)(2,1)S(1)}, bf16[96,768]{1,0:T(8,128)(2,1)S(1)}, u32[]{:S(2)}, u32[]{:S(2)}) %collective-permute-start.20) | collective-permute-done | bytes 147488 | tf_op jit(solution)/shard_map/ppermute | solution.py:285
  60.6 2.3 %collective-permute-start.22 = (bf16[96,768]{1,0:T(8,128)(2,1)S(1)}, bf16[96,768]{1,0:T(8,128)(2,1)S(1)}, u32[]{:S(2)}, u32[]{:S(2)}) collective-permute-start(bf16[96,768]{1,0:T(8,128)(2,1)S(1)} %add_convert_fusion.6), channel_id=1, source_target_pairs={{0,8},{4,12},{8,0},{12,4},{1,9},{5,13},{9,1},{13,5},{2,10},{6,14},... | collective-permute-start | bytes 442376 | tf_op jit(solution)/shard_map/ppermute | solution.py:285
  64.1 10.3 %collective-permute-done.22 = bf16[96,768]{1,0:T(8,128)(2,1)S(1)} collective-permute-done((bf16[96,768]{1,0:T(8,128)(2,1)S(1)}, bf16[96,768]{1,0:T(8,128)(2,1)S(1)}, u32[]{:S(2)}, u32[]{:S(2)}) %collective-permute-start.22) | collective-permute-done | bytes 147488 | tf_op jit(solution)/shard_map/ppermute | solution.py:285
  74.5 1.8 %grad_label_work.3 = bf16[1024,768]{1,0:T(8,128)(2,1)} custom-call(f32[512,128]{1,0:T(8,128)S(1)} %get-tuple-element.50.refs_0_, f32[512,128]{1,0:T(8,128)S(1)} %get-tuple-element.56.refs_1_, s32[512,128]{1,0:T(8,128)S(1)} %get-tuple-element.57.refs_2_, s32[512,128]{1,0:T(8,128)S(1)} %get-tuple-element.58.refs_3_, ...), custom_call_target="tpu_custom_call" | custom-call | flops 805306368 | bytes 4194304 | tf_op jit(solution)/shard_map/grad_label_work/pallas_call | solution.py:192
  77.3 2.4 %collective-permute-done.23.other_ref = bf16[96,768]{1,0:T(8,128)(2,1)S(1)} collective-permute-done((bf16[96,768]{1,0:T(8,128)(2,1)S(1)}, bf16[96,768]{1,0:T(8,128)(2,1)S(1)}, u32[]{:S(2)}, u32[]{:S(2)}) %collective-permute-start.23) | collective-permute-done | bytes 147488 | tf_op jit(solution)/shard_map/ppermute | solution.py:285
  (49 shorter events, 14.6 us)
Async XLA Ops:
  0.6 11.2 %collective-permute-start.3 = (bf16[1024,768]{1,0:T(8,128)(2,1)}, bf16[1024,768]{1,0:T(8,128)(2,1)S(1)}, u32[]{:S(2)}, u32[]{:S(2)}) collective-permute-start(bf16[1024,768]{1,0:T(8,128)(2,1)} %label_ref), channel_id=1, source_target_pairs={{0,1},{1,0},{2,3},{3,2},{4,5},{5,4},{6,7},{7,6},{8,9},{9,8},{10,11... | collective-permute-start | bytes 4718600 | tf_op jit(solution)/shard_map/ppermute | solution.py:285
  1.1 10.6 %collective-permute-start.5 = (bf16[192,768]{1,0:T(8,128)(2,1)}, bf16[192,768]{1,0:T(8,128)(2,1)S(1)}, u32[]{:S(2)}, u32[]{:S(2)}) collective-permute-start(bf16[192,768]{1,0:T(8,128)(2,1)} %shard_ref.1), channel_id=1, source_target_pairs={{0,2},{1,3},{2,0},{3,1},{4,6},{5,7},{6,4},{7,5},{8,10},{9,11},{10,... | collective-permute-start | bytes 884744 | tf_op jit(solution)/shard_map/ppermute | solution.py:285
  5.4 13.0 %collective-permute-start.1 = (bf16[136,768]{1,0:T(8,128)(2,1)}, bf16[136,768]{1,0:T(8,128)(2,1)S(1)}, u32[]{:S(2)}, u32[]{:S(2)}) collective-permute-start(bf16[136,768]{1,0:T(8,128)(2,1)} %own_block.1.refs_0_), channel_id=1, source_target_pairs={{0,8},{4,12},{8,0},{12,4},{1,9},{5,13},{9,1},{13,5},{2,10},{6,14},... | collective-permute-start | bytes 626696 | tf_op jit(solution)/shard_map/ppermute | solution.py:285
  8.0 10.3 %collective-permute-start.2 = (bf16[136,768]{1,0:T(8,128)(2,1)}, bf16[136,768]{1,0:T(8,128)(2,1)S(1)}, u32[]{:S(2)}, u32[]{:S(2)}) collective-permute-start(bf16[136,768]{1,0:T(8,128)(2,1)} %own_block.1.refs_0_), channel_id=1, source_target_pairs={{0,2},{1,3},{2,0},{3,1},{4,6},{5,7},{6,4},{7,5},{8,10},{9,11},{10,... | collective-permute-start | bytes 626696 | tf_op jit(solution)/shard_map/ppermute | solution.py:285
  8.6 10.2 %collective-permute-start = (bf16[136,768]{1,0:T(8,128)(2,1)}, bf16[136,768]{1,0:T(8,128)(2,1)S(1)}, u32[]{:S(2)}, u32[]{:S(2)}) collective-permute-start(bf16[136,768]{1,0:T(8,128)(2,1)} %own_block.1.refs_0_), channel_id=1, source_target_pairs={{0,4},{4,0},{8,12},{12,8},{1,5},{5,1},{9,13},{13,9},{2,6},{6,2},{1... | collective-permute-start | bytes 626696 | tf_op jit(solution)/shard_map/ppermute | solution.py:285
  11.8 8.7 %collective-permute-start.6 = (bf16[192,768]{1,0:T(8,128)(2,1)}, bf16[192,768]{1,0:T(8,128)(2,1)S(1)}, u32[]{:S(2)}, u32[]{:S(2)}) collective-permute-start(bf16[192,768]{1,0:T(8,128)(2,1)} %shard_ref.1), channel_id=1, source_target_pairs={{0,1},{1,0},{2,3},{3,2},{4,5},{5,4},{6,7},{7,6},{8,9},{9,8},{10,11... | collective-permute-start | bytes 884744 | tf_op jit(solution)/shard_map/ppermute | solution.py:285
  12.9 7.6 %collective-permute-start.7 = (bf16[192,768]{1,0:T(8,128)(2,1)S(1)}, bf16[192,768]{1,0:T(8,128)(2,1)S(1)}, u32[]{:S(2)}, u32[]{:S(2)}) collective-permute-start(bf16[192,768]{1,0:T(8,128)(2,1)S(1)} %collective-permute-done.5.refs_8_), channel_id=1, source_target_pairs={{0,1},{1,0},{2,3},{3,2},{4,5},{5,4},{6,7},{7,6},{8,9},{9,8},{10,11... | collective-permute-start | bytes 884744 | tf_op jit(solution)/shard_map/ppermute | solution.py:285
  18.8 5.9 %collective-permute-start.4 = (bf16[136,768]{1,0:T(8,128)(2,1)S(1)}, bf16[136,768]{1,0:T(8,128)(2,1)S(1)}, u32[]{:S(2)}, u32[]{:S(2)}) collective-permute-start(bf16[136,768]{1,0:T(8,128)(2,1)S(1)} %collective-permute-done.1.refs_2_), channel_id=1, source_target_pairs={{0,2},{1,3},{2,0},{3,1},{4,6},{5,7},{6,4},{7,5},{8,10},{9,11},{10,... | collective-permute-start | bytes 626696 | tf_op jit(solution)/shard_map/ppermute | solution.py:285
  20.2 7.2 %collective-permute-start.9 = (bf16[136,768]{1,0:T(8,128)(2,1)S(1)}, bf16[136,768]{1,0:T(8,128)(2,1)S(1)}, u32[]{:S(2)}, u32[]{:S(2)}) collective-permute-start(bf16[136,768]{1,0:T(8,128)(2,1)S(1)} %collective-permute-done.1.refs_2_), channel_id=1, source_target_pairs={{0,4},{4,0},{8,12},{12,8},{1,5},{5,1},{9,13},{13,9},{2,6},{6,2},{1... | collective-permute-start | bytes 626696 | tf_op jit(solution)/shard_map/ppermute | solution.py:285
  20.5 13.6 %collective-permute-start.8 = (bf16[136,768]{1,0:T(8,128)(2,1)S(1)}, bf16[136,768]{1,0:T(8,128)(2,1)S(1)}, u32[]{:S(2)}, u32[]{:S(2)}) collective-permute-start(bf16[136,768]{1,0:T(8,128)(2,1)S(1)} %collective-permute-done.2.refs_1_), channel_id=1, source_target_pairs={{0,4},{4,0},{8,12},{12,8},{1,5},{5,1},{9,13},{13,9},{2,6},{6,2},{1... | collective-permute-start | bytes 626696 | tf_op jit(solution)/shard_map/ppermute | solution.py:285
  27.5 6.6 %collective-permute-start.10 = (bf16[136,768]{1,0:T(8,128)(2,1)S(1)}, bf16[136,768]{1,0:T(8,128)(2,1)S(1)}, u32[]{:S(2)}, u32[]{:S(2)}) collective-permute-start(bf16[136,768]{1,0:T(8,128)(2,1)S(1)} %collective-permute-done.9.refs_2_), channel_id=1, source_target_pairs={{0,2},{1,3},{2,0},{3,1},{4,6},{5,7},{6,4},{7,5},{8,10},{9,11},{10,... | collective-permute-start | bytes 626696 | tf_op jit(solution)/shard_map/ppermute | solution.py:285
  39.7 2.1 %collective-permute-start.12 = (bf16[2,192,768]{2,1,0:T(8,128)(2,1)S(1)}, bf16[2,192,768]{2,1,0:T(8,128)(2,1)S(1)}, u32[]{:S(2)}, u32[]{:S(2)}) collective-permute-start(bf16[2,192,768]{2,1,0:T(8,128)(2,1)S(1)} %get-tuple-element.64), channel_id=1, source_target_pairs={{0,1},{1,0},{2,3},{3,2},{4,5},{5,4},{6,7},{7,6},{8,9},{9,8},{10,11... | collective-permute-start | bytes 1769480 | tf_op jit(solution)/shard_map/ppermute | solution.py:285
  40.9 33.6 %collective-permute-start.11 = (bf16[1024,768]{1,0:T(8,128)(2,1)S(1)}, bf16[1024,768]{1,0:T(8,128)(2,1)S(1)}, u32[]{:S(2)}, u32[]{:S(2)}) collective-permute-start(bf16[1024,768]{1,0:T(8,128)(2,1)S(1)} %grad_label_work.2), channel_id=1, source_target_pairs={{0,1},{1,0},{2,3},{3,2},{4,5},{5,4},{6,7},{7,6},{8,9},{9,8},{10,11... | collective-permute-start | bytes 4718600 | tf_op jit(solution)/shard_map/ppermute | solution.py:285
  41.9 7.8 %collective-permute-start.14 = (bf16[128,768]{1,0:T(8,128)(2,1)S(1)}, bf16[128,768]{1,0:T(8,128)(2,1)S(1)}, u32[]{:S(2)}, u32[]{:S(2)}) collective-permute-start(bf16[128,768]{1,0:T(8,128)(2,1)S(1)} %get-tuple-element.68), channel_id=1, source_target_pairs={{0,4},{4,0},{8,12},{12,8},{1,5},{5,1},{9,13},{13,9},{2,6},{6,2},{1... | collective-permute-start | bytes 589832 | tf_op jit(solution)/shard_map/ppermute | solution.py:285
  43.4 10.5 %collective-permute-start.15 = (bf16[192,768]{1,0:T(8,128)(2,1)S(1)}, bf16[192,768]{1,0:T(8,128)(2,1)S(1)}, u32[]{:S(2)}, u32[]{:S(2)}) collective-permute-start(bf16[192,768]{1,0:T(8,128)(2,1)S(1)} %fusion), channel_id=1, source_target_pairs={{0,2},{1,3},{2,0},{3,1},{4,6},{5,7},{6,4},{7,5},{8,10},{9,11},{10,... | collective-permute-start | bytes 884744 | tf_op jit(solution)/shard_map/ppermute | solution.py:285
  43.9 9.2 %collective-permute-start.13 = (bf16[128,768]{1,0:T(8,128)(2,1)S(1)}, bf16[128,768]{1,0:T(8,128)(2,1)S(1)}, u32[]{:S(2)}, u32[]{:S(2)}) collective-permute-start(bf16[128,768]{1,0:T(8,128)(2,1)S(1)} %get-tuple-element.66), channel_id=1, source_target_pairs={{0,4},{4,0},{8,12},{12,8},{1,5},{5,1},{9,13},{13,9},{2,6},{6,2},{1... | collective-permute-start | bytes 589832 | tf_op jit(solution)/shard_map/ppermute | solution.py:285
  44.8 12.7 %collective-permute-start.17 = (bf16[128,768]{1,0:T(8,128)(2,1)S(1)}, bf16[128,768]{1,0:T(8,128)(2,1)S(1)}, u32[]{:S(2)}, u32[]{:S(2)}) collective-permute-start(bf16[128,768]{1,0:T(8,128)(2,1)S(1)} %get-tuple-element.74), channel_id=1, source_target_pairs={{0,2},{1,3},{2,0},{3,1},{4,6},{5,7},{6,4},{7,5},{8,10},{9,11},{10,... | collective-permute-start | bytes 589832 | tf_op jit(solution)/shard_map/ppermute | solution.py:285
  53.1 9.8 %collective-permute-start.19 = (bf16[128,768]{1,0:T(8,128)(2,1)S(1)}, bf16[128,768]{1,0:T(8,128)(2,1)S(1)}, u32[]{:S(2)}, u32[]{:S(2)}) collective-permute-start(bf16[128,768]{1,0:T(8,128)(2,1)S(1)} %add_convert_fusion.3), channel_id=1, source_target_pairs={{0,2},{1,3},{2,0},{3,1},{4,6},{5,7},{6,4},{7,5},{8,10},{9,11},{10,... | collective-permute-start | bytes 589832 | tf_op jit(solution)/shard_map/ppermute | solution.py:285
  54.1 6.5 %collective-permute-start.20 = (bf16[96,768]{1,0:T(8,128)(2,1)S(1)}, bf16[96,768]{1,0:T(8,128)(2,1)S(1)}, u32[]{:S(2)}, u32[]{:S(2)}) collective-permute-start(bf16[96,768]{1,0:T(8,128)(2,1)S(1)} %get-tuple-element.78), channel_id=1, source_target_pairs={{0,4},{4,0},{8,12},{12,8},{1,5},{5,1},{9,13},{13,9},{2,6},{6,2},{1... | collective-permute-start | bytes 442376 | tf_op jit(solution)/shard_map/ppermute | solution.py:285
  57.5 18.8 %collective-permute-start.18 = (bf16[128,768]{1,0:T(8,128)(2,1)S(1)}, bf16[128,768]{1,0:T(8,128)(2,1)S(1)}, u32[]{:S(2)}, u32[]{:S(2)}) collective-permute-start(bf16[128,768]{1,0:T(8,128)(2,1)S(1)} %add_convert_fusion.4), channel_id=1, source_target_pairs={{0,4},{4,0},{8,12},{12,8},{1,5},{5,1},{9,13},{13,9},{2,6},{6,2},{1... | collective-permute-start | bytes 589832 | tf_op jit(solution)/shard_map/ppermute | solution.py:285
  57.6 18.8 %collective-permute-start.16 = (bf16[128,768]{1,0:T(8,128)(2,1)S(1)}, bf16[128,768]{1,0:T(8,128)(2,1)S(1)}, u32[]{:S(2)}, u32[]{:S(2)}) collective-permute-start(bf16[128,768]{1,0:T(8,128)(2,1)S(1)} %get-tuple-element.71), channel_id=1, source_target_pairs={{0,2},{1,3},{2,0},{3,1},{4,6},{5,7},{6,4},{7,5},{8,10},{9,11},{10,... | collective-permute-start | bytes 589832 | tf_op jit(solution)/shard_map/ppermute | solution.py:285
  60.6 13.7 %collective-permute-start.22 = (bf16[96,768]{1,0:T(8,128)(2,1)S(1)}, bf16[96,768]{1,0:T(8,128)(2,1)S(1)}, u32[]{:S(2)}, u32[]{:S(2)}) collective-permute-start(bf16[96,768]{1,0:T(8,128)(2,1)S(1)} %add_convert_fusion.6), channel_id=1, source_target_pairs={{0,8},{4,12},{8,0},{12,4},{1,9},{5,13},{9,1},{13,5},{2,10},{6,14},... | collective-permute-start | bytes 442376 | tf_op jit(solution)/shard_map/ppermute | solution.py:285
  63.0 13.5 %collective-permute-start.21 = (bf16[128,768]{1,0:T(8,128)(2,1)S(1)}, bf16[128,768]{1,0:T(8,128)(2,1)S(1)}, u32[]{:S(2)}, u32[]{:S(2)}) collective-permute-start(bf16[128,768]{1,0:T(8,128)(2,1)S(1)} %add_convert_fusion.2), channel_id=1, source_target_pairs={{0,8},{4,12},{8,0},{12,4},{1,9},{5,13},{9,1},{13,5},{2,10},{6,14},... | collective-permute-start | bytes 589832 | tf_op jit(solution)/shard_map/ppermute | solution.py:285
  74.4 5.2 %collective-permute-start.23 = (bf16[96,768]{1,0:T(8,128)(2,1)S(1)}, bf16[96,768]{1,0:T(8,128)(2,1)S(1)}, u32[]{:S(2)}, u32[]{:S(2)}) collective-permute-start(bf16[96,768]{1,0:T(8,128)(2,1)S(1)} %add_convert_fusion.5.mine_ref), channel_id=1, source_target_pairs={{0,4},{4,0},{8,12},{12,8},{1,5},{5,1},{9,13},{13,9},{2,6},{6,2},{1... | collective-permute-start | bytes 442376 | tf_op jit(solution)/shard_map/ppermute | solution.py:285
  (5 other events, 29.3 us)

commit v22 on v20

--- a/solution.py
+++ b/solution.py
@@ -369,7 +369,7 @@
     for i in reversed(range(0, n - 2, 2)):
         near = add(*over_dp([[x] for x in runs[i + 1]], ahead)).astype(BF16)
         sent_near.append(partner(near, "labels", 1))
-        sums[i] = over_dp([[x] for x in runs[i]], keep) + sent_near[-1:]
+        sums[i] = over_dp([[x] for x in runs[i]], sent_near[-1]) + sent_near[-1:]
     for mask in masks(n)[1:]:
         for i in range(0, n, 2 * mask):
             sent = after(add(*sums[i + mask]).astype(BF16), first)

time: 78.5 us -> 77.8 us (level)
  waiting for transfers between devices: 31 us -> 27.4 us
  starting transfers between devices: 25.3 us -> 28.1 us
    ppermute x24, waiting for transfers between devices: 31 us -> 27.4 us  [partner(): lax.ppermute(x, axis, [(i, i ^ mask) for i in range(lax.axis_size(axis))])]
    ppermute x24, starting transfers between devices: 25.3 us -> 28.1 us  [partner(): lax.ppermute(x, axis, [(i, i ^ mask) for i in range(lax.axis_size(axis))])]
  transfers between devices with their start and end apart: 24 -> 24, of which waited for: 13 -> 12; matrix products, arithmetic and copies ran while one was open for 1% -> 1% of each run, Pallas kernels for 13% -> 13%
where the time goes in v22:
time: 77.8 us; the launch traced here: 77.6 us
  starting transfers between devices  28.1 us (36%)
  waiting for transfers between devices  27.4 us (35%)
  Pallas kernels  16.7 us (21%)
  local copies, waits for them, and re-layouts  3.52 us (5%)
  other arithmetic  1.08 us (1%)
    ppermute x24, starting transfers between devices, partner(): lax.ppermute(x, axis, [(i, i ^ mask) for i in range(lax.axis_size(axis))])  28.1 us
    ppermute x24, waiting for transfers between devices, partner(): lax.ppermute(x, axis, [(i, i ^ mask) for i in range(lax.axis_size(axis))])  27.4 us
    pallas_call x8, Pallas kernels, call(): pl.pallas_call(kernel, in_specs=[space] * len(args), out_specs=jax.tree.m...  16.7 us
    unnamed x10, local copies, waits for them, and re-layouts  3.52 us
  transfers between devices with their start and end apart: 24, of which 12 were waited for; matrix products, arithmetic and copies ran while one was open for 1% of the time, Pallas kernels for 13%

profile of v22, /device:TPU:0, one launch (start us, length us, event | category | flops | bytes accessed | tf_op | source)
XLA Modules:
  0.0 77.6 jit_solution(5815818824763406417)
XLA Ops:
  1.1 2.6 %collective-permute-start.5 = (bf16[192,768]{1,0:T(8,128)(2,1)}, bf16[192,768]{1,0:T(8,128)(2,1)S(1)}, u32[]{:S(2)}, u32[]{:S(2)}) collective-permute-start(bf16[192,768]{1,0:T(8,128)(2,1)} %shard_ref.1), channel_id=1, source_target_pairs={{0,2},{1,3},{2,0},{3,1},{4,6},{5,7},{6,4},{7,5},{8,10},{9,11},{10,... | collective-permute-start | bytes 884744 | tf_op jit(solution)/shard_map/ppermute | solution.py:285
  3.7 1.6 %own_block.1.refs_0_ = bf16[136,768]{1,0:T(8,128)(2,1)} custom-call(bf16[128,768]{1,0:T(8,128)(2,1)} %feats_ref.1, s32[4,128]{1,0:T(4,128)} %bitcast.5, s32[4,128]{1,0:T(4,128)} %bitcast.6, s32[4,128]{1,0:T(4,128)} %bitcast.7), custom_call_target="tpu_custom_call" | custom-call | bytes 1048576 | tf_op jit(solution)/shard_map/own_block/pallas_call | solution.py:192
  5.4 2.7 %collective-permute-start.1 = (bf16[136,768]{1,0:T(8,128)(2,1)}, bf16[136,768]{1,0:T(8,128)(2,1)S(1)}, u32[]{:S(2)}, u32[]{:S(2)}) collective-permute-start(bf16[136,768]{1,0:T(8,128)(2,1)} %own_block.1.refs_0_), channel_id=1, source_target_pairs={{0,8},{4,12},{8,0},{12,4},{1,9},{5,13},{9,1},{13,5},{2,10},{6,14},... | collective-permute-start | bytes 626696 | tf_op jit(solution)/shard_map/ppermute | solution.py:285
  8.6 1.6 %collective-permute-start = (bf16[136,768]{1,0:T(8,128)(2,1)}, bf16[136,768]{1,0:T(8,128)(2,1)S(1)}, u32[]{:S(2)}, u32[]{:S(2)}) collective-permute-start(bf16[136,768]{1,0:T(8,128)(2,1)} %own_block.1.refs_0_), channel_id=1, source_target_pairs={{0,4},{4,0},{8,12},{12,8},{1,5},{5,1},{9,13},{13,9},{2,6},{6,2},{1... | collective-permute-start | bytes 626696 | tf_op jit(solution)/shard_map/ppermute | solution.py:285
  10.1 1.7 %collective-permute-done.5.refs_8_ = bf16[192,768]{1,0:T(8,128)(2,1)S(1)} collective-permute-done((bf16[192,768]{1,0:T(8,128)(2,1)}, bf16[192,768]{1,0:T(8,128)(2,1)S(1)}, u32[]{:S(2)}, u32[]{:S(2)}) %collective-permute-start.5) | collective-permute-done | bytes 294944 | tf_op jit(solution)/shard_map/ppermute | solution.py:285
  13.4 1.4 %copy-done = bf16[1024,768]{1,0:T(8,128)(2,1)S(1)} copy-done((bf16[1024,768]{1,0:T(8,128)(2,1)S(1)}, bf16[1024,768]{1,0:T(8,128)(2,1)}, u32[]{:S(2)}) %copy-start) | copy-done | bytes 1572888
  15.9 2.4 %collective-permute-done.1.refs_2_ = bf16[136,768]{1,0:T(8,128)(2,1)S(1)} collective-permute-done((bf16[136,768]{1,0:T(8,128)(2,1)}, bf16[136,768]{1,0:T(8,128)(2,1)S(1)}, u32[]{:S(2)}, u32[]{:S(2)}) %collective-permute-start.1) | collective-permute-done | bytes 208928 | tf_op jit(solution)/shard_map/ppermute | solution.py:285
  18.8 1.4 %collective-permute-start.4 = (bf16[136,768]{1,0:T(8,128)(2,1)S(1)}, bf16[136,768]{1,0:T(8,128)(2,1)S(1)}, u32[]{:S(2)}, u32[]{:S(2)}) collective-permute-start(bf16[136,768]{1,0:T(8,128)(2,1)S(1)} %collective-permute-done.1.refs_2_), channel_id=1, source_target_pairs={{0,2},{1,3},{2,0},{3,1},{4,6},{5,7},{6,4},{7,5},{8,10},{9,11},{10,... | collective-permute-start | bytes 626696 | tf_op jit(solution)/shard_map/ppermute | solution.py:285
  20.5 1.8 %collective-permute-start.8 = (bf16[136,768]{1,0:T(8,128)(2,1)S(1)}, bf16[136,768]{1,0:T(8,128)(2,1)S(1)}, u32[]{:S(2)}, u32[]{:S(2)}) collective-permute-start(bf16[136,768]{1,0:T(8,128)(2,1)S(1)} %collective-permute-done.2.refs_1_), channel_id=1, source_target_pairs={{0,4},{4,0},{8,12},{12,8},{1,5},{5,1},{9,13},{13,9},{2,6},{6,2},{1... | collective-permute-start | bytes 626696 | tf_op jit(solution)/shard_map/ppermute | solution.py:285
  22.3 2.4 %collective-permute-done.4.refs_3_ = bf16[136,768]{1,0:T(8,128)(2,1)S(1)} collective-permute-done((bf16[136,768]{1,0:T(8,128)(2,1)S(1)}, bf16[136,768]{1,0:T(8,128)(2,1)S(1)}, u32[]{:S(2)}, u32[]{:S(2)}) %collective-permute-start.4) | collective-permute-done | bytes 208928 | tf_op jit(solution)/shard_map/ppermute | solution.py:285
  24.7 2.8 %collective-permute-done.9.refs_2_ = bf16[136,768]{1,0:T(8,128)(2,1)S(1)} collective-permute-done((bf16[136,768]{1,0:T(8,128)(2,1)S(1)}, bf16[136,768]{1,0:T(8,128)(2,1)S(1)}, u32[]{:S(2)}, u32[]{:S(2)}) %collective-permute-start.9) | collective-permute-done | bytes 208928 | tf_op jit(solution)/shard_map/ppermute | solution.py:285
  28.7 5.4 %pair_work.2 = (bf16[128,768]{1,0:T(8,128)(2,1)S(1)}, bf16[128,768]{1,0:T(8,128)(2,1)S(1)}, bf16[128,768]{1,0:T(8,128)(2,1)S(1)}, bf16[128,768]{1,0:T(8,128)(2,1...) custom-call(bf16[136,768]{1,0:T(8,128)(2,1)S(1)} %copy-done.2, ...), custom_call_target="tpu_custom_call" | custom-call | flops 3623878656 | bytes 8388608 | tf_op jit(solution)/shard_map/pair_work/pallas_call | solution.py:192
  34.1 5.6 %pair_work.3 = (bf16[128,768]{1,0:T(8,128)(2,1)S(1)}, bf16[128,768]{1,0:T(8,128)(2,1)S(1)}, bf16[128,768]{1,0:T(8,128)(2,1)S(1)}, bf16[128,768]{1,0:T(8,128)(2,1...) custom-call(bf16[136,768]{1,0:T(8,128)(2,1)S(1)} %collective-permute, ...), custom_call_target="tpu_custom_call" | custom-call | flops 3623878656 | bytes 8388608 | tf_op jit(solution)/shard_map/pair_work/pallas_call | solution.py:192
  41.5 1.4 %collective-permute-start.17 = (bf16[128,768]{1,0:T(8,128)(2,1)S(1)}, bf16[128,768]{1,0:T(8,128)(2,1)S(1)}, u32[]{:S(2)}, u32[]{:S(2)}) collective-permute-start(bf16[128,768]{1,0:T(8,128)(2,1)S(1)} %get-tuple-element.72), channel_id=1, source_target_pairs={{0,4},{4,0},{8,12},{12,8},{1,5},{5,1},{9,13},{13,9},{2,6},{6,2},{1... | collective-permute-start | bytes 589832 | tf_op jit(solution)/shard_map/ppermute | solution.py:285
  43.5 1.5 %collective-permute-start.13 = (bf16[128,768]{1,0:T(8,128)(2,1)S(1)}, bf16[128,768]{1,0:T(8,128)(2,1)S(1)}, u32[]{:S(2)}, u32[]{:S(2)}) collective-permute-start(bf16[128,768]{1,0:T(8,128)(2,1)S(1)} %get-tuple-element.66), channel_id=1, source_target_pairs={{0,2},{1,3},{2,0},{3,1},{4,6},{5,7},{6,4},{7,5},{8,10},{9,11},{10,... | collective-permute-start | bytes 589832 | tf_op jit(solution)/shard_map/ppermute | solution.py:285
  45.7 3.6 %collective-permute-done.17 = bf16[128,768]{1,0:T(8,128)(2,1)S(1)} collective-permute-done((bf16[128,768]{1,0:T(8,128)(2,1)S(1)}, bf16[128,768]{1,0:T(8,128)(2,1)S(1)}, u32[]{:S(2)}, u32[]{:S(2)}) %collective-permute-start.17) | collective-permute-done | bytes 196640 | tf_op jit(solution)/shard_map/ppermute | solution.py:285
  50.1 2.4 %collective-permute-done.16 = bf16[128,768]{1,0:T(8,128)(2,1)S(1)} collective-permute-done((bf16[128,768]{1,0:T(8,128)(2,1)S(1)}, bf16[128,768]{1,0:T(8,128)(2,1)S(1)}, u32[]{:S(2)}, u32[]{:S(2)}) %collective-permute-start.16) | collective-permute-done | bytes 196640 | tf_op jit(solution)/shard_map/ppermute | solution.py:285
  54.3 2.9 %collective-permute-done.13 = bf16[128,768]{1,0:T(8,128)(2,1)S(1)} collective-permute-done((bf16[128,768]{1,0:T(8,128)(2,1)S(1)}, bf16[128,768]{1,0:T(8,128)(2,1)S(1)}, u32[]{:S(2)}, u32[]{:S(2)}) %collective-permute-start.13) | collective-permute-done | bytes 196640 | tf_op jit(solution)/shard_map/ppermute | solution.py:285
  59.2 2.4 %collective-permute-start.22 = (bf16[96,768]{1,0:T(8,128)(2,1)S(1)}, bf16[96,768]{1,0:T(8,128)(2,1)S(1)}, u32[]{:S(2)}, u32[]{:S(2)}) collective-permute-start(bf16[96,768]{1,0:T(8,128)(2,1)S(1)} %add_convert_fusion.6), channel_id=1, source_target_pairs={{0,8},{4,12},{8,0},{12,4},{1,9},{5,13},{9,1},{13,5},{2,10},{6,14},... | collective-permute-start | bytes 442376 | tf_op jit(solution)/shard_map/ppermute | solution.py:285
  61.6 3.0 %collective-permute-done.14 = bf16[128,768]{1,0:T(8,128)(2,1)S(1)} collective-permute-done((bf16[128,768]{1,0:T(8,128)(2,1)S(1)}, bf16[128,768]{1,0:T(8,128)(2,1)S(1)}, u32[]{:S(2)}, u32[]{:S(2)}) %collective-permute-start.14) | collective-permute-done | bytes 196640 | tf_op jit(solution)/shard_map/ppermute | solution.py:285
  65.1 2.4 %collective-permute-start.21 = (bf16[128,768]{1,0:T(8,128)(2,1)S(1)}, bf16[128,768]{1,0:T(8,128)(2,1)S(1)}, u32[]{:S(2)}, u32[]{:S(2)}) collective-permute-start(bf16[128,768]{1,0:T(8,128)(2,1)S(1)} %add_convert_fusion.2), channel_id=1, source_target_pairs={{0,8},{4,12},{8,0},{12,4},{1,9},{5,13},{9,1},{13,5},{2,10},{6,14},... | collective-permute-start | bytes 589832 | tf_op jit(solution)/shard_map/ppermute | solution.py:285
  67.5 2.4 %collective-permute-start.23 = (bf16[96,768]{1,0:T(8,128)(2,1)S(1)}, bf16[96,768]{1,0:T(8,128)(2,1)S(1)}, u32[]{:S(2)}, u32[]{:S(2)}) collective-permute-start(bf16[96,768]{1,0:T(8,128)(2,1)S(1)} %add_convert_fusion.5.mine_ref), channel_id=1, source_target_pairs={{0,4},{4,0},{8,12},{12,8},{1,5},{5,1},{9,13},{13,9},{2,6},{6,2},{1... | collective-permute-start | bytes 442376 | tf_op jit(solution)/shard_map/ppermute | solution.py:285
  69.9 1.8 %grad_label_work.3 = bf16[1024,768]{1,0:T(8,128)(2,1)} custom-call(f32[512,128]{1,0:T(8,128)S(1)} %get-tuple-element.49.refs_0_, f32[512,128]{1,0:T(8,128)S(1)} %get-tuple-element.55.refs_1_, s32[512,128]{1,0:T(8,128)S(1)} %get-tuple-element.56.refs_2_, s32[512,128]{1,0:T(8,128)S(1)} %get-tuple-element.57.refs_3_, ...), custom_call_target="tpu_custom_call" | custom-call | flops 805306368 | bytes 4194304 | tf_op jit(solution)/shard_map/grad_label_work/pallas_call | solution.py:192
  71.8 4.2 %collective-permute-done.21 = bf16[128,768]{1,0:T(8,128)(2,1)S(1)} collective-permute-done((bf16[128,768]{1,0:T(8,128)(2,1)S(1)}, bf16[128,768]{1,0:T(8,128)(2,1)S(1)}, u32[]{:S(2)}, u32[]{:S(2)}) %collective-permute-start.21) | collective-permute-done | bytes 196640 | tf_op jit(solution)/shard_map/ppermute | solution.py:285
  (49 shorter events, 15.6 us)
Async XLA Ops:
  0.6 11.2 %collective-permute-start.3 = (bf16[1024,768]{1,0:T(8,128)(2,1)}, bf16[1024,768]{1,0:T(8,128)(2,1)S(1)}, u32[]{:S(2)}, u32[]{:S(2)}) collective-permute-start(bf16[1024,768]{1,0:T(8,128)(2,1)} %label_ref), channel_id=1, source_target_pairs={{0,1},{1,0},{2,3},{3,2},{4,5},{5,4},{6,7},{7,6},{8,9},{9,8},{10,11... | collective-permute-start | bytes 4718600 | tf_op jit(solution)/shard_map/ppermute | solution.py:285
  1.1 10.6 %collective-permute-start.5 = (bf16[192,768]{1,0:T(8,128)(2,1)}, bf16[192,768]{1,0:T(8,128)(2,1)S(1)}, u32[]{:S(2)}, u32[]{:S(2)}) collective-permute-start(bf16[192,768]{1,0:T(8,128)(2,1)} %shard_ref.1), channel_id=1, source_target_pairs={{0,2},{1,3},{2,0},{3,1},{4,6},{5,7},{6,4},{7,5},{8,10},{9,11},{10,... | collective-permute-start | bytes 884744 | tf_op jit(solution)/shard_map/ppermute | solution.py:285
  5.4 13.0 %collective-permute-start.1 = (bf16[136,768]{1,0:T(8,128)(2,1)}, bf16[136,768]{1,0:T(8,128)(2,1)S(1)}, u32[]{:S(2)}, u32[]{:S(2)}) collective-permute-start(bf16[136,768]{1,0:T(8,128)(2,1)} %own_block.1.refs_0_), channel_id=1, source_target_pairs={{0,8},{4,12},{8,0},{12,4},{1,9},{5,13},{9,1},{13,5},{2,10},{6,14},... | collective-permute-start | bytes 626696 | tf_op jit(solution)/shard_map/ppermute | solution.py:285
  8.0 10.3 %collective-permute-start.2 = (bf16[136,768]{1,0:T(8,128)(2,1)}, bf16[136,768]{1,0:T(8,128)(2,1)S(1)}, u32[]{:S(2)}, u32[]{:S(2)}) collective-permute-start(bf16[136,768]{1,0:T(8,128)(2,1)} %own_block.1.refs_0_), channel_id=1, source_target_pairs={{0,2},{1,3},{2,0},{3,1},{4,6},{5,7},{6,4},{7,5},{8,10},{9,11},{10,... | collective-permute-start | bytes 626696 | tf_op jit(solution)/shard_map/ppermute | solution.py:285
  8.6 10.2 %collective-permute-start = (bf16[136,768]{1,0:T(8,128)(2,1)}, bf16[136,768]{1,0:T(8,128)(2,1)S(1)}, u32[]{:S(2)}, u32[]{:S(2)}) collective-permute-start(bf16[136,768]{1,0:T(8,128)(2,1)} %own_block.1.refs_0_), channel_id=1, source_target_pairs={{0,4},{4,0},{8,12},{12,8},{1,5},{5,1},{9,13},{13,9},{2,6},{6,2},{1... | collective-permute-start | bytes 626696 | tf_op jit(solution)/shard_map/ppermute | solution.py:285
  11.8 8.7 %collective-permute-start.6 = (bf16[192,768]{1,0:T(8,128)(2,1)}, bf16[192,768]{1,0:T(8,128)(2,1)S(1)}, u32[]{:S(2)}, u32[]{:S(2)}) collective-permute-start(bf16[192,768]{1,0:T(8,128)(2,1)} %shard_ref.1), channel_id=1, source_target_pairs={{0,1},{1,0},{2,3},{3,2},{4,5},{5,4},{6,7},{7,6},{8,9},{9,8},{10,11... | collective-permute-start | bytes 884744 | tf_op jit(solution)/shard_map/ppermute | solution.py:285
  12.9 7.6 %collective-permute-start.7 = (bf16[192,768]{1,0:T(8,128)(2,1)S(1)}, bf16[192,768]{1,0:T(8,128)(2,1)S(1)}, u32[]{:S(2)}, u32[]{:S(2)}) collective-permute-start(bf16[192,768]{1,0:T(8,128)(2,1)S(1)} %collective-permute-done.5.refs_8_), channel_id=1, source_target_pairs={{0,1},{1,0},{2,3},{3,2},{4,5},{5,4},{6,7},{7,6},{8,9},{9,8},{10,11... | collective-permute-start | bytes 884744 | tf_op jit(solution)/shard_map/ppermute | solution.py:285
  18.8 5.9 %collective-permute-start.4 = (bf16[136,768]{1,0:T(8,128)(2,1)S(1)}, bf16[136,768]{1,0:T(8,128)(2,1)S(1)}, u32[]{:S(2)}, u32[]{:S(2)}) collective-permute-start(bf16[136,768]{1,0:T(8,128)(2,1)S(1)} %collective-permute-done.1.refs_2_), channel_id=1, source_target_pairs={{0,2},{1,3},{2,0},{3,1},{4,6},{5,7},{6,4},{7,5},{8,10},{9,11},{10,... | collective-permute-start | bytes 626696 | tf_op jit(solution)/shard_map/ppermute | solution.py:285
  20.2 7.2 %collective-permute-start.9 = (bf16[136,768]{1,0:T(8,128)(2,1)S(1)}, bf16[136,768]{1,0:T(8,128)(2,1)S(1)}, u32[]{:S(2)}, u32[]{:S(2)}) collective-permute-start(bf16[136,768]{1,0:T(8,128)(2,1)S(1)} %collective-permute-done.1.refs_2_), channel_id=1, source_target_pairs={{0,4},{4,0},{8,12},{12,8},{1,5},{5,1},{9,13},{13,9},{2,6},{6,2},{1... | collective-permute-start | bytes 626696 | tf_op jit(solution)/shard_map/ppermute | solution.py:285
  20.5 13.6 %collective-permute-start.8 = (bf16[136,768]{1,0:T(8,128)(2,1)S(1)}, bf16[136,768]{1,0:T(8,128)(2,1)S(1)}, u32[]{:S(2)}, u32[]{:S(2)}) collective-permute-start(bf16[136,768]{1,0:T(8,128)(2,1)S(1)} %collective-permute-done.2.refs_1_), channel_id=1, source_target_pairs={{0,4},{4,0},{8,12},{12,8},{1,5},{5,1},{9,13},{13,9},{2,6},{6,2},{1... | collective-permute-start | bytes 626696 | tf_op jit(solution)/shard_map/ppermute | solution.py:285
  27.5 6.6 %collective-permute-start.10 = (bf16[136,768]{1,0:T(8,128)(2,1)S(1)}, bf16[136,768]{1,0:T(8,128)(2,1)S(1)}, u32[]{:S(2)}, u32[]{:S(2)}) collective-permute-start(bf16[136,768]{1,0:T(8,128)(2,1)S(1)} %collective-permute-done.9.refs_2_), channel_id=1, source_target_pairs={{0,2},{1,3},{2,0},{3,1},{4,6},{5,7},{6,4},{7,5},{8,10},{9,11},{10,... | collective-permute-start | bytes 626696 | tf_op jit(solution)/shard_map/ppermute | solution.py:285
  39.7 3.1 %collective-permute-start.12 = (bf16[2,192,768]{2,1,0:T(8,128)(2,1)S(1)}, bf16[2,192,768]{2,1,0:T(8,128)(2,1)S(1)}, u32[]{:S(2)}, u32[]{:S(2)}) collective-permute-start(bf16[2,192,768]{2,1,0:T(8,128)(2,1)S(1)} %get-tuple-element.65), channel_id=1, source_target_pairs={{0,1},{1,0},{2,3},{3,2},{4,5},{5,4},{6,7},{7,6},{8,9},{9,8},{10,11... | collective-permute-start | bytes 1769480 | tf_op jit(solution)/shard_map/ppermute | solution.py:285
  40.9 29.0 %collective-permute-start.11 = (bf16[1024,768]{1,0:T(8,128)(2,1)S(1)}, bf16[1024,768]{1,0:T(8,128)(2,1)S(1)}, u32[]{:S(2)}, u32[]{:S(2)}) collective-permute-start(bf16[1024,768]{1,0:T(8,128)(2,1)S(1)} %grad_label_work.2), channel_id=1, source_target_pairs={{0,1},{1,0},{2,3},{3,2},{4,5},{5,4},{6,7},{7,6},{8,9},{9,8},{10,11... | collective-permute-start | bytes 4718600 | tf_op jit(solution)/shard_map/ppermute | solution.py:285
  41.5 7.8 %collective-permute-start.17 = (bf16[128,768]{1,0:T(8,128)(2,1)S(1)}, bf16[128,768]{1,0:T(8,128)(2,1)S(1)}, u32[]{:S(2)}, u32[]{:S(2)}) collective-permute-start(bf16[128,768]{1,0:T(8,128)(2,1)S(1)} %get-tuple-element.72), channel_id=1, source_target_pairs={{0,4},{4,0},{8,12},{12,8},{1,5},{5,1},{9,13},{13,9},{2,6},{6,2},{1... | collective-permute-start | bytes 589832 | tf_op jit(solution)/shard_map/ppermute | solution.py:285
  43.0 10.0 %collective-permute-start.19 = (bf16[192,768]{1,0:T(8,128)(2,1)S(1)}, bf16[192,768]{1,0:T(8,128)(2,1)S(1)}, u32[]{:S(2)}, u32[]{:S(2)}) collective-permute-start(bf16[192,768]{1,0:T(8,128)(2,1)S(1)} %fusion), channel_id=1, source_target_pairs={{0,2},{1,3},{2,0},{3,1},{4,6},{5,7},{6,4},{7,5},{8,10},{9,11},{10,... | collective-permute-start | bytes 884744 | tf_op jit(solution)/shard_map/ppermute | solution.py:285
  43.5 13.6 %collective-permute-start.13 = (bf16[128,768]{1,0:T(8,128)(2,1)S(1)}, bf16[128,768]{1,0:T(8,128)(2,1)S(1)}, u32[]{:S(2)}, u32[]{:S(2)}) collective-permute-start(bf16[128,768]{1,0:T(8,128)(2,1)S(1)} %get-tuple-element.66), channel_id=1, source_target_pairs={{0,2},{1,3},{2,0},{3,1},{4,6},{5,7},{6,4},{7,5},{8,10},{9,11},{10,... | collective-permute-start | bytes 589832 | tf_op jit(solution)/shard_map/ppermute | solution.py:285
  45.0 7.5 %collective-permute-start.16 = (bf16[128,768]{1,0:T(8,128)(2,1)S(1)}, bf16[128,768]{1,0:T(8,128)(2,1)S(1)}, u32[]{:S(2)}, u32[]{:S(2)}) collective-permute-start(bf16[128,768]{1,0:T(8,128)(2,1)S(1)} %get-tuple-element.70), channel_id=1, source_target_pairs={{0,4},{4,0},{8,12},{12,8},{1,5},{5,1},{9,13},{13,9},{2,6},{6,2},{1... | collective-permute-start | bytes 589832 | tf_op jit(solution)/shard_map/ppermute | solution.py:285
  49.3 12.2 %collective-permute-start.18 = (bf16[128,768]{1,0:T(8,128)(2,1)S(1)}, bf16[128,768]{1,0:T(8,128)(2,1)S(1)}, u32[]{:S(2)}, u32[]{:S(2)}) collective-permute-start(bf16[128,768]{1,0:T(8,128)(2,1)S(1)} %add_convert_fusion.3), channel_id=1, source_target_pairs={{0,2},{1,3},{2,0},{3,1},{4,6},{5,7},{6,4},{7,5},{8,10},{9,11},{10,... | collective-permute-start | bytes 589832 | tf_op jit(solution)/shard_map/ppermute | solution.py:285
  53.1 6.0 %collective-permute-start.20 = (bf16[96,768]{1,0:T(8,128)(2,1)S(1)}, bf16[96,768]{1,0:T(8,128)(2,1)S(1)}, u32[]{:S(2)}, u32[]{:S(2)}) collective-permute-start(bf16[96,768]{1,0:T(8,128)(2,1)S(1)} %get-tuple-element.76), channel_id=1, source_target_pairs={{0,4},{4,0},{8,12},{12,8},{1,5},{5,1},{9,13},{13,9},{2,6},{6,2},{1... | collective-permute-start | bytes 442376 | tf_op jit(solution)/shard_map/ppermute | solution.py:285
  57.2 7.4 %collective-permute-start.14 = (bf16[128,768]{1,0:T(8,128)(2,1)S(1)}, bf16[128,768]{1,0:T(8,128)(2,1)S(1)}, u32[]{:S(2)}, u32[]{:S(2)}) collective-permute-start(bf16[128,768]{1,0:T(8,128)(2,1)S(1)} %add_convert_fusion.4), channel_id=1, source_target_pairs={{0,4},{4,0},{8,12},{12,8},{1,5},{5,1},{9,13},{13,9},{2,6},{6,2},{1... | collective-permute-start | bytes 589832 | tf_op jit(solution)/shard_map/ppermute | solution.py:285
  59.2 8.3 %collective-permute-start.22 = (bf16[96,768]{1,0:T(8,128)(2,1)S(1)}, bf16[96,768]{1,0:T(8,128)(2,1)S(1)}, u32[]{:S(2)}, u32[]{:S(2)}) collective-permute-start(bf16[96,768]{1,0:T(8,128)(2,1)S(1)} %add_convert_fusion.6), channel_id=1, source_target_pairs={{0,8},{4,12},{8,0},{12,4},{1,9},{5,13},{9,1},{13,5},{2,10},{6,14},... | collective-permute-start | bytes 442376 | tf_op jit(solution)/shard_map/ppermute | solution.py:285
  64.6 7.2 %collective-permute-start.15 = (bf16[128,768]{1,0:T(8,128)(2,1)S(1)}, bf16[128,768]{1,0:T(8,128)(2,1)S(1)}, u32[]{:S(2)}, u32[]{:S(2)}) collective-permute-start(bf16[128,768]{1,0:T(8,128)(2,1)S(1)} %get-tuple-element.67), channel_id=1, source_target_pairs={{0,2},{1,3},{2,0},{3,1},{4,6},{5,7},{6,4},{7,5},{8,10},{9,11},{10,... | collective-permute-start | bytes 589832 | tf_op jit(solution)/shard_map/ppermute | solution.py:285
  65.1 10.9 %collective-permute-start.21 = (bf16[128,768]{1,0:T(8,128)(2,1)S(1)}, bf16[128,768]{1,0:T(8,128)(2,1)S(1)}, u32[]{:S(2)}, u32[]{:S(2)}) collective-permute-start(bf16[128,768]{1,0:T(8,128)(2,1)S(1)} %add_convert_fusion.2), channel_id=1, source_target_pairs={{0,8},{4,12},{8,0},{12,4},{1,9},{5,13},{9,1},{13,5},{2,10},{6,14},... | collective-permute-start | bytes 589832 | tf_op jit(solution)/shard_map/ppermute | solution.py:285
  67.5 9.3 %collective-permute-start.23 = (bf16[96,768]{1,0:T(8,128)(2,1)S(1)}, bf16[96,768]{1,0:T(8,128)(2,1)S(1)}, u32[]{:S(2)}, u32[]{:S(2)}) collective-permute-start(bf16[96,768]{1,0:T(8,128)(2,1)S(1)} %add_convert_fusion.5.mine_ref), channel_id=1, source_target_pairs={{0,4},{4,0},{8,12},{12,8},{1,5},{5,1},{9,13},{13,9},{2,6},{6,2},{1... | collective-permute-start | bytes 442376 | tf_op jit(solution)/shard_map/ppermute | solution.py:285
  (5 other events, 29.3 us)
